TPU v7x, 32 devices: a whole 2x2x4 slice. The times are simulated.
32 devices in a mesh: outer: 4 (over x, core), vocab: 8 (over z, y).
Axes of the slice: x: 2, y: 2, z: 4, core: 2. Of those that a mesh axis runs over, the one named last changes fastest.
Arguments:
- hidden: bfloat16 [512, 4096], P(('outer', 'vocab')), parts along dimension 0, may hold values from -96 to 96
- targets: int32 [512], P(('outer', 'vocab')), parts along dimension 0, may hold values from 0 to 16383
- head: bfloat16 [16384, 16384], P('outer', 'vocab'), parts along dimension 0, may hold values from -1 to 1
- global_frag: float32 [128, 16384], P(None, 'vocab'), may hold values from -6 to 6
- momentum: float32 [128, 16384], P(None, 'vocab'), may hold values from -6 to 6
- peer_delta: float32 [512, 16384], P('outer', 'vocab'), parts along dimension 0, may hold values from -6 to 6
Outputs:
- loss: float32 [4], P('outer'), parts along dimension 0
- hidden_grad: bfloat16 [512, 4096], P(('outer', 'vocab')), parts along dimension 0
- new_global: float32 [512, 16384], P('outer', 'vocab'), parts along dimension 0
- new_momentum: float32 [512, 16384], P('outer', 'vocab'), parts along dimension 0
There are 4 independent parts, one for each index of `outer`. A program takes and returns all parts, laid end to end along the dimension named above; an argument that names none is the same for every part. Nothing has to cross between parts.
All inputs are finite; a program needn't handle non-finite values.
Results may differ from a plain program's by a relative error of at most 0.0031.
Values may be sent and summed in bfloat16 or wider, within the bound.
No kernel may reach another device: no remote copies, remote signals or barrier semaphores. Data moves between devices by JAX's collectives and lax.ppermute only.
A program may use at most 128 MiB of HBM per device.

v0:
```python
import jax
import jax.numpy as jnp
from jax import lax
from jax.sharding import PartitionSpec as P

FRAG = 128
REPLICAS = 4


def body(hidden, targets, head, global_frag, momentum, peer_delta):
    rows_all, ids_all = (
        lax.all_gather(hidden, "vocab", axis=0, tiled=True),
        lax.all_gather(targets, "vocab", axis=0, tiled=True),
    )
    row_count = rows_all.shape[0]
    width = head.shape[1]
    logits = jnp.dot(rows_all, head, preferred_element_type=jnp.float32)
    offset = lax.axis_index("vocab") * width
    columns = offset + jnp.arange(width, dtype=jnp.int32)
    onehot = (columns[None, :] == ids_all[:, None]).astype(jnp.float32)
    local_max = jnp.max(logits, axis=1)
    local_pick = jnp.sum(logits * onehot, axis=1)
    top = lax.pmax(local_max, "vocab")
    total, picked = lax.psum((jnp.sum(jnp.exp(logits - top[:, None]), axis=1), local_pick), "vocab")
    loss = jnp.mean(top + jnp.log(total) - picked).reshape((1,))
    dlogits = ((jnp.exp(logits - top[:, None]) / total[:, None] - onehot) / row_count).astype(
        jnp.bfloat16
    )
    own_rows = hidden.shape[0]
    partial_grad = lax.dot_general(
        dlogits, head, (((1,), (1,)), ((), ())), preferred_element_type=jnp.float32
    )
    summed = lax.psum(partial_grad, "vocab")
    hidden_grad = lax.dynamic_slice_in_dim(
        summed, lax.axis_index("vocab") * own_rows, own_rows, 0
    ).astype(jnp.bfloat16)
    frag_grad = lax.dot_general(
        rows_all[:, :FRAG], dlogits, (((0,), (0,)), ((), ())), preferred_element_type=jnp.float32
    )
    local_frag = head[:FRAG].astype(jnp.float32) - 1.0 * frag_grad
    pseudo = (global_frag - local_frag + peer_delta) / REPLICAS
    new_momentum = 0.9 * momentum + pseudo
    new_global = global_frag - 0.7 * (pseudo + 0.9 * new_momentum)
    return (loss, hidden_grad, new_global, new_momentum)


def solution(mesh):
    in_specs = (
        P(("outer", "vocab"), None),
        P(("outer", "vocab")),
        P("outer", "vocab"),
        P(None, "vocab"),
        P(None, "vocab"),
        P("outer", "vocab"),
    )
    out_specs = (P("outer"), P(("outer", "vocab"), None), P("outer", "vocab"), P("outer", "vocab"))
    return jax.shard_map(body, mesh=mesh, in_specs=in_specs, out_specs=out_specs, check_vma=False)
```

profile of v0, /device:TPU:0, one launch (start us, length us, event | category | flops | bytes accessed | tf_op | source)
XLA Modules:
  0.0 218.9 jit_solution(4428422526723672996)
XLA Ops:
  7.2 0.0 all-gather.2.cloned.1.call-start
  7.2 0.7 all-gather.2.cloned.1.call-update
  7.9 1.1 slice.6
  9.0 1.0 copy.17
  10.0 2.5 %copy.14 = f32[128,2048]{0,1:T(8,128)} copy(f32[128,2048]{1,0:T(8,128)} %param.9) | data formatting | bytes 2097152 | tf_op args[3]
  12.5 2.5 %copy.13 = f32[128,2048]{0,1:T(8,128)} copy(f32[128,2048]{1,0:T(8,128)} %param.10) | data formatting | bytes 2097152 | tf_op args[4]
  15.1 2.6 %copy.12 = f32[128,2048]{0,1:T(8,128)} copy(f32[128,2048]{1,0:T(8,128)} %param.11) | data formatting | bytes 2097152 | tf_op args[5]
  17.6 1.2 dynamic-slice
  19.5 0.9 dynamic-update-slice
  20.4 13.1 %all-reduce = s32[128]{0:T(128)S(1)} all-reduce(s32[128]{0:T(128)S(1)} %dynamic-update-slice), channel_id=1, replica_groups=mesh['outer'=4,'vocab'=8] {'vocab'}, use_global_device_ids=true, to_apply=%add | all-reduce | flops 128 | bytes 1024
  33.5 19.7 %all-gather.2.cloned.1.call-done = bf16[128,4096]{1,0:T(8,128)(2,1)} async-done(((bf16[16,4096]{1,0:T(8,128)(2,1)}), bf16[128,4096]{1,0:T(8,128)(2,1)}) %all-gather.2.cloned.1.call-update) | async-done | bytes 1048592 | tf_op jit(solution)/shard_map/all_gather | solution.py:12
  53.1 8.5 %fusion.13 = (f32[128]{0:T(128)S(1)}, f32[128,2048]{1,0:T(8,128)S(1)}) fusion(bf16[128,4096]{1,0:T(8,128)(2,1)} %all-gather.2.cloned.1.call-done, bf16[4096,2048]{1,0:T(8,128)(2,1)} %param.8), kind=kOutput, calls=%fused_computation.20 | convolution fusion | flops 2147745792 | bytes 18874880 | tf_op jit(solution)/shard_map/dot_general | solution.py:17
  61.7 19.2 %pmax.7 = f32[128]{0:T(128)S(1)} all-reduce(f32[128]{0:T(128)S(1)} %get-tuple-element.14), channel_id=1, replica_groups=mesh['outer'=4,'vocab'=8] {'vocab'}, use_global_device_ids=true, to_apply=%region_1.0 | all-reduce | flops 128 | bytes 1024 | tf_op jit(solution)/shard_map/pmax | solution.py:23
  80.9 0.4 fusion.8
  81.2 17.1 %psum.21 = f32[128]{0:T(128)S(1)} all-reduce(f32[128]{0:T(128)S(1)} %get-tuple-element.8), channel_id=1, replica_groups=mesh['outer'=4,'vocab'=8] {'vocab'}, use_global_device_ids=true, to_apply=%region_3.0 | all-reduce | flops 128 | bytes 1024 | tf_op jit(solution)/shard_map/psum | solution.py:24
  98.4 11.7 %fusion.11 = f32[128,4096]{1,0:T(8,128)S(1)} fusion(bf16[4096,2048]{1,0:T(8,128)(2,1)} %param.8, f32[128,2048]{1,0:T(8,128)S(1)} %get-tuple-element.15, f32[128]{0:T(128)S(1)} %psum.21, s32[2048]{0:T(1024)S(1)} %iota_add_fusion, f32[128]{0:T(128)S(1)} %pmax.7, s32[128]{0:T(128)S(1)} %all-reduce), kind=kOutput, calls=%fused_computation.19 | convolution fusion | flops 2149318656 | bytes 19932672 | tf_op jit(solution)/shard_map/dot_general | solution.py:30
  110.0 4.2 %multiply_add_fusion = (f32[128,2048]{0,1:T(8,128)}, f32[128,2048]{0,1:T(8,128)}) fusion(f32[128,2048]{0,1:T(8,128)} %copy.13, f32[128,2048]{0,1:T(8,128)} %copy.14, f32[128,2048]{0,1:T(8,128)} %copy.12, bf16[128,4096]{1,0:T(8,128)(2,1)} %all-gather.2.cloned.1.call-done, f32[128,2048]{1,0:T(8,128)S(1)} %get-tuple-element.15, f32[128]{0:T(128)S(1)} %psum.21, ...), kind=kOutput, calls=%fused_computation.12 | convolution fusion | flops 71827456 | bytes 6858240 | tf_op jit(solution)/shard_map/dot_general | solution.py:37
  114.3 2.5 %copy.16 = f32[128,2048]{1,0:T(8,128)} copy(f32[128,2048]{0,1:T(8,128)} %get-tuple-element.12) | data formatting | bytes 2097152
  116.8 89.6 %all-reduce.3 = (f32[128]{0:T(128)S(1)}, bf16[128,4096]{1,0:T(8,128)(2,1)S(1)}) all-reduce(f32[128]{0:T(128)S(1)} %get-tuple-element.9, f32[128,4096]{1,0:T(8,128)S(1)} %fusion.11), channel_id=1, replica_groups=mesh['outer'=4,'vocab'=8] {'vocab'}, use_global_device_ids=true, to_apply=%region_5.0 | all-reduce | flops 524416 | bytes 3146752 | tf_op jit(solution)/shard_map/psum | solution.py:24
  206.4 0.6 subtract_reduce_fusion
  207.0 2.5 %copy.15 = f32[128,2048]{1,0:T(8,128)} copy(f32[128,2048]{0,1:T(8,128)} %get-tuple-element.13) | data formatting | bytes 2097152
  210.2 0.7 dynamic-slice_convert_fusion
  (2 shorter events, 0.0 us)
Async XLA Ops:
  7.2 46.0 %all-gather.2.cloned.1.call-start = ((), (), s32[]{:S(2)}) async-start(), calls=%async_computation | async-start | bytes 1179648 | tf_op jit(solution)/shard_map/all_gather | solution.py:12
Sparse Core Ops, SparseCore 0:
  10.1 42.9 all-gather.1
where the time goes:
time: 219 us
  blocking collectives  139 us (63%)
  matrix products  24.4 us (11%)
  waiting for transfers between devices  20.3 us (9%)
  local copies, waits for them, and re-layouts  17.6 us (8%)
  between operations  16.5 us (8%)
    psum x2, blocking collectives, body(): lax.psum((jnp.sum(jnp.exp(logits - top[:, None]), axis=1), local_pick), '...  107 us
    all_gather x1, waiting for transfers between devices, body(): lax.all_gather(hidden, 'vocab', axis=0, tiled=True)  19.7 us
    pmax x1, blocking collectives, body(): top = lax.pmax(local_max, 'vocab')  19.2 us
    unnamed x9, local copies, waits for them, and re-layouts  15.8 us
    unnamed x1, blocking collectives  13.1 us
    dot_general x1, matrix products, body(): lax.dot_general(dlogits, head, (((1,), (1,)), ((), ())), preferred_elemen...  11.7 us
    dot_general x1, matrix products, body(): logits = jnp.dot(rows_all, head, preferred_element_type=jnp.float32)  8.53 us
  transfers between devices with their start and end apart: 1, of which 1 were waited for; matrix products, arithmetic and copies ran while one was open for 5% of the time, Pallas kernels for 0%

commit v1 on v0

v1 whole, which is shorter than its diff:
```python
import jax
import jax.numpy as jnp
from jax import lax
from jax.sharding import PartitionSpec as P

FRAG = 128
REPLICAS = 4
AXIS = "vocab"


def swap(value, members, step):
    return lax.ppermute(value, AXIS, [(i, i ^ step) for i in range(members)])


def gather(value, members):
    return [value] + [swap(value, members, step) for step in range(1, members)]


def body(hidden, targets, head, global_frag, momentum, peer_delta):
    members = lax.axis_size(AXIS)
    own = hidden.shape[0]
    rows = own * members
    width = head.shape[1]

    rows_all = jnp.concatenate(gather(hidden, members), axis=0)
    ids_all = jnp.concatenate(gather(targets, members), axis=0)

    logits = jnp.dot(rows_all, head, preferred_element_type=jnp.float32)
    columns = lax.axis_index(AXIS) * width + jnp.arange(width, dtype=jnp.int32)
    hit = columns[None, :] == ids_all[:, None]
    local_max = jnp.max(logits, axis=1)
    local_sum = jnp.sum(jnp.exp(logits - local_max[:, None]), axis=1)
    local_pick = jnp.sum(jnp.where(hit, logits, 0.0), axis=1)

    stats = jnp.stack([local_max, local_sum, local_pick]).reshape(3, members, own)
    seen = [stats]
    for step in range(1, members):
        there = swap(stats, members, step)
        seen.append(there[:, jnp.array([i ^ step for i in range(members)])])
    seen = jnp.stack(seen).reshape(members, 3, rows)
    top = jnp.max(seen[:, 0], axis=0)
    total = jnp.sum(seen[:, 1] * jnp.exp(seen[:, 0] - top), axis=0)
    picked = jnp.sum(seen[:, 2], axis=0)
    loss = jnp.mean(top + jnp.log(total) - picked).reshape((1,))

    onehot = hit.astype(jnp.float32)
    dlogits = ((jnp.exp(logits - top[:, None]) / total[:, None] - onehot) / rows).astype(jnp.bfloat16)
    partial_grad = lax.dot_general(
        dlogits, head, (((1,), (1,)), ((), ())), preferred_element_type=jnp.float32
    )
    summed = partial_grad[:own]
    for step in range(1, members):
        block = partial_grad[step * own : (step + 1) * own].astype(jnp.bfloat16)
        summed = summed + swap(block, members, step).astype(jnp.float32)
    hidden_grad = summed.astype(jnp.bfloat16)

    frag_grad = lax.dot_general(
        rows_all[:, :FRAG], dlogits, (((0,), (0,)), ((), ())), preferred_element_type=jnp.float32
    )
    local_frag = head[:FRAG].astype(jnp.float32) - 1.0 * frag_grad
    pseudo = (global_frag - local_frag + peer_delta) / REPLICAS
    new_momentum = 0.9 * momentum + pseudo
    new_global = global_frag - 0.7 * (pseudo + 0.9 * new_momentum)
    return (loss, hidden_grad, new_global, new_momentum)


def solution(mesh):
    in_specs = (
        P(("outer", "vocab"), None),
        P(("outer", "vocab")),
        P("outer", "vocab"),
        P(None, "vocab"),
        P(None, "vocab"),
        P("outer", "vocab"),
    )
    out_specs = (P("outer"), P(("outer", "vocab"), None), P("outer", "vocab"), P("outer", "vocab"))
    return jax.shard_map(body, mesh=mesh, in_specs=in_specs, out_specs=out_specs, check_vma=False)
```

time: 219 us -> 113 us (0.52)
  blocking collectives: 139 us -> 0 us
  starting transfers between devices: 0.04 us -> 50.4 us
  between operations: 16.5 us -> 2.71 us
  local copies, waits for them, and re-layouts: 17.6 us -> 7.4 us
  other arithmetic: 1 us -> 8.09 us
  waiting for transfers between devices: 20.3 us -> 17.9 us
    psum x2 -> x0, blocking collectives: 107 us -> none  [body(): lax.psum((jnp.sum(jnp.exp(logits - top[:, None]), axis=1), local_pick), '...]
    ppermute x0 -> x28, starting transfers between devices: none -> 50.4 us  [swap(): return lax.ppermute(value, AXIS, [(i, i ^ step) for i in range(members)])]
    all_gather x1 -> x0, waiting for transfers between devices: 19.7 us -> none  [body(): lax.all_gather(hidden, 'vocab', axis=0, tiled=True)]
    pmax x1 -> x0, blocking collectives: 19.2 us -> none  [body(): top = lax.pmax(local_max, 'vocab')]
    ppermute x0 -> x28, waiting for transfers between devices: none -> 17.9 us  [swap(): return lax.ppermute(value, AXIS, [(i, i ^ step) for i in range(members)])]
    unnamed x9 -> x17, local copies, waits for them, and re-layouts: 15.8 us -> 1.03 us
    unnamed x1 -> x0, blocking collectives: 13.1 us -> none
    gather x0 -> x14, local copies, waits for them, and re-layouts: none -> 4.08 us  [body(): seen.append(there[:, jnp.array([i ^ step for i in range(members)])])]
  transfers between devices with their start and end apart: 1 -> 28, of which waited for: 1 -> 7; matrix products, arithmetic and copies ran while one was open for 5% -> 14% of each run, Pallas kernels for 0% -> 0%
where the time goes in v1:
time: 113 us; the launch traced here: 112 us
  starting transfers between devices  50.4 us (45%)
  matrix products  25.3 us (22%)
  waiting for transfers between devices  17.9 us (16%)
  other arithmetic  8.09 us (7%)
  local copies, waits for them, and re-layouts  7.4 us (7%)
  between operations  2.71 us (2%)
    ppermute x28, starting transfers between devices, swap(): return lax.ppermute(value, AXIS, [(i, i ^ step) for i in range(members)])  50.4 us
    ppermute x28, waiting for transfers between devices, swap(): return lax.ppermute(value, AXIS, [(i, i ^ step) for i in range(members)])  17.9 us
    dot_general x1, matrix products, body(): lax.dot_general(dlogits, head, (((1,), (1,)), ((), ())), preferred_elemen...  13 us
    dot_general x1, matrix products, body(): logits = jnp.dot(rows_all, head, preferred_element_type=jnp.float32)  8.19 us
    dot_general x1, matrix products, body(): lax.dot_general(rows_all[:, :FRAG], dlogits, (((0,), (0,)), ((), ())), pr...  4.12 us
    gather x14, local copies, waits for them, and re-layouts, body(): seen.append(there[:, jnp.array([i ^ step for i in range(members)])])  4.08 us
    gather x7, other arithmetic, body(): seen.append(there[:, jnp.array([i ^ step for i in range(members)])])  3.97 us
  transfers between devices with their start and end apart: 28, of which 7 were waited for; matrix products, arithmetic and copies ran while one was open for 14% of the time, Pallas kernels for 0%

profile of v1, /device:TPU:0, one launch (start us, length us, event | category | flops | bytes accessed | tf_op | source)
XLA Modules:
  0.0 111.9 jit_solution(6841414529957532633)
XLA Ops:
  0.6 3.0 %collective-permute-start = (bf16[16,4096]{1,0:T(8,128)(2,1)}, bf16[16,4096]{1,0:T(8,128)(2,1)S(1)}, u32[]{:S(2)}, u32[]{:S(2)}) collective-permute-start(bf16[16,4096]{1,0:T(8,128)(2,1)} %param.13), channel_id=1, source_target_pairs={{0,1},{1,0},{2,3},{3,2},{4,5},{5,4},{6,7},{7,6},{8,9},{9,8},{10,11... | collective-permute-start | bytes 393224 | tf_op jit(solution)/shard_map/ppermute | solution.py:12
  3.7 1.6 %collective-permute-start.1 = (bf16[16,4096]{1,0:T(8,128)(2,1)}, bf16[16,4096]{1,0:T(8,128)(2,1)S(1)}, u32[]{:S(2)}, u32[]{:S(2)}) collective-permute-start(bf16[16,4096]{1,0:T(8,128)(2,1)} %param.13), channel_id=1, source_target_pairs={{0,2},{1,3},{2,0},{3,1},{4,6},{5,7},{6,4},{7,5},{8,10},{9,11},{10,... | collective-permute-start | bytes 393224 | tf_op jit(solution)/shard_map/ppermute | solution.py:12
  5.3 1.9 %collective-permute-start.7 = (s32[16]{0:T(128)}, s32[16]{0:T(128)S(1)}, u32[]{:S(2)}, u32[]{:S(2)}) collective-permute-start(s32[16]{0:T(128)} %param.14), channel_id=1, source_target_pairs={{0,1},{1,0},{2,3},{3,2},{4,5},{5,4},{6,7},{7,6},{8,9},{9,8},{10,11... | collective-permute-start | bytes 200 | tf_op jit(solution)/shard_map/ppermute | solution.py:12
  13.7 3.0 %collective-permute-start.10 = (s32[16]{0:T(128)}, s32[16]{0:T(128)S(1)}, u32[]{:S(2)}, u32[]{:S(2)}) collective-permute-start(s32[16]{0:T(128)} %param.14), channel_id=1, source_target_pairs={{0,4},{1,5},{2,6},{3,7},{4,0},{5,1},{6,2},{7,3},{8,12},{9,13},{10,... | collective-permute-start | bytes 200 | tf_op jit(solution)/shard_map/ppermute | solution.py:12
  16.6 1.6 %collective-permute-done.9 = s32[16]{0:T(128)S(1)} collective-permute-done((s32[16]{0:T(128)}, s32[16]{0:T(128)S(1)}, u32[]{:S(2)}, u32[]{:S(2)}) %collective-permute-start.9) | collective-permute-done | bytes 96 | tf_op jit(solution)/shard_map/ppermute | solution.py:12
  18.2 2.5 %collective-permute-start.11 = (s32[16]{0:T(128)}, s32[16]{0:T(128)S(1)}, u32[]{:S(2)}, u32[]{:S(2)}) collective-permute-start(s32[16]{0:T(128)} %param.14), channel_id=1, source_target_pairs={{0,5},{1,4},{2,7},{3,6},{4,1},{5,0},{6,3},{7,2},{8,13},{9,12},{10,... | collective-permute-start | bytes 200 | tf_op jit(solution)/shard_map/ppermute | solution.py:12
  23.7 2.4 %collective-permute-start.13 = (s32[16]{0:T(128)}, s32[16]{0:T(128)S(1)}, u32[]{:S(2)}, u32[]{:S(2)}) collective-permute-start(s32[16]{0:T(128)} %param.14), channel_id=1, source_target_pairs={{0,7},{1,6},{2,5},{3,4},{4,3},{5,2},{6,1},{7,0},{8,15},{9,14},{10,... | collective-permute-start | bytes 200 | tf_op jit(solution)/shard_map/ppermute | solution.py:12
  26.3 3.8 %collective-permute-done.13 = s32[16]{0:T(128)S(1)} collective-permute-done((s32[16]{0:T(128)}, s32[16]{0:T(128)S(1)}, u32[]{:S(2)}, u32[]{:S(2)}) %collective-permute-start.13) | collective-permute-done | bytes 96 | tf_op jit(solution)/shard_map/ppermute | solution.py:12
  31.6 1.8 %collective-permute-start.5 = (bf16[16,4096]{1,0:T(8,128)(2,1)}, bf16[16,4096]{1,0:T(8,128)(2,1)S(1)}, u32[]{:S(2)}, u32[]{:S(2)}) collective-permute-start(bf16[16,4096]{1,0:T(8,128)(2,1)} %param.13), channel_id=1, source_target_pairs={{0,6},{1,7},{2,4},{3,5},{4,2},{5,3},{6,0},{7,1},{8,14},{9,15},{10,... | collective-permute-start | bytes 393224 | tf_op jit(solution)/shard_map/ppermute | solution.py:12
  33.5 3.1 %collective-permute-start.6 = (bf16[16,4096]{1,0:T(8,128)(2,1)}, bf16[16,4096]{1,0:T(8,128)(2,1)S(1)}, u32[]{:S(2)}, u32[]{:S(2)}) collective-permute-start(bf16[16,4096]{1,0:T(8,128)(2,1)} %param.13), channel_id=1, source_target_pairs={{0,7},{1,6},{2,5},{3,4},{4,3},{5,2},{6,1},{7,0},{8,15},{9,14},{10,... | collective-permute-start | bytes 393224 | tf_op jit(solution)/shard_map/ppermute | solution.py:12
  36.6 5.7 %collective-permute-done.3 = bf16[16,4096]{1,0:T(8,128)(2,1)S(1)} collective-permute-done((bf16[16,4096]{1,0:T(8,128)(2,1)}, bf16[16,4096]{1,0:T(8,128)(2,1)S(1)}, u32[]{:S(2)}, u32[]{:S(2)}) %collective-permute-start.3) | collective-permute-done | bytes 131104 | tf_op jit(solution)/shard_map/ppermute | solution.py:12
  42.2 3.8 %collective-permute-done.4 = bf16[16,4096]{1,0:T(8,128)(2,1)S(1)} collective-permute-done((bf16[16,4096]{1,0:T(8,128)(2,1)}, bf16[16,4096]{1,0:T(8,128)(2,1)S(1)}, u32[]{:S(2)}, u32[]{:S(2)}) %collective-permute-start.4) | collective-permute-done | bytes 131104 | tf_op jit(solution)/shard_map/ppermute | solution.py:12
  46.1 8.2 %fusion.20 = (f32[128]{0:T(128)S(1)}, f32[128,2048]{1,0:T(8,128)S(1)}) fusion(bf16[128,4096]{1,0:T(8,128)(2,1)S(1)} %constant_dynamic-update-slice_fusion, bf16[4096,2048]{1,0:T(8,128)(2,1)} %param.15), kind=kOutput, calls=%fused_computation.60 | convolution fusion | flops 2147745792 | bytes 18874880 | tf_op jit(solution)/shard_map/dot_general | solution.py:28
  55.5 3.7 %collective-permute-start.15 = (f32[3,8,16]{2,0,1:T(4,128)S(1)}, f32[3,8,16]{2,0,1:T(4,128)S(1)}, u32[]{:S(2)}, u32[]{:S(2)}) collective-permute-start(f32[3,8,16]{2,0,1:T(4,128)S(1)} %pad_maximum_fusion), channel_id=1, source_target_pairs={{0,2},{1,3},{2,0},{3,1},{4,6},{5,7},{6,4},{7,5},{8,10},{9,11},{10,... | collective-permute-start | bytes 4616 | tf_op jit(solution)/shard_map/ppermute | solution.py:12
  60.3 2.3 %collective-permute-start.17 = (f32[3,8,16]{2,0,1:T(4,128)S(1)}, f32[3,8,16]{2,0,1:T(4,128)S(1)}, u32[]{:S(2)}, u32[]{:S(2)}) collective-permute-start(f32[3,8,16]{2,0,1:T(4,128)S(1)} %pad_maximum_fusion), channel_id=1, source_target_pairs={{0,4},{1,5},{2,6},{3,7},{4,0},{5,1},{6,2},{7,3},{8,12},{9,13},{10,... | collective-permute-start | bytes 4616 | tf_op jit(solution)/shard_map/ppermute | solution.py:12
  63.3 1.8 %collective-permute-start.19 = (f32[3,8,16]{2,0,1:T(4,128)S(1)}, f32[3,8,16]{2,0,1:T(4,128)S(1)}, u32[]{:S(2)}, u32[]{:S(2)}) collective-permute-start(f32[3,8,16]{2,0,1:T(4,128)S(1)} %pad_maximum_fusion), channel_id=1, source_target_pairs={{0,6},{1,7},{2,4},{3,5},{4,2},{5,3},{6,0},{7,1},{8,14},{9,15},{10,... | collective-permute-start | bytes 4616 | tf_op jit(solution)/shard_map/ppermute | solution.py:12
  65.1 2.9 %collective-permute-start.20 = (f32[3,8,16]{2,0,1:T(4,128)S(1)}, f32[3,8,16]{2,0,1:T(4,128)S(1)}, u32[]{:S(2)}, u32[]{:S(2)}) collective-permute-start(f32[3,8,16]{2,0,1:T(4,128)S(1)} %pad_maximum_fusion), channel_id=1, source_target_pairs={{0,7},{1,6},{2,5},{3,4},{4,3},{5,2},{6,1},{7,0},{8,15},{9,14},{10,... | collective-permute-start | bytes 4616 | tf_op jit(solution)/shard_map/ppermute | solution.py:12
  73.3 13.0 %fusion.21 = (bf16[128,4096]{1,0:T(8,128)(2,1)S(1)}, f32[128,4096]{1,0:T(8,128)}) fusion(bf16[4096,2048]{1,0:T(8,128)(2,1)} %param.15, f32[128,2048]{1,0:T(8,128)S(1)} %get-tuple-element.19, f32[128]{0:T(128)S(1)} %multiply_reduce_fusion, f32[128]{0:T(128)S(1)} %reduce_max.19, s32[2048]{0:T(1024)S(1)} %iota_add_fusion, s32[128]{0:T(128)S(1)} %concatenate.11), kind=kOutput, calls=%fused_computation.61 | convolution fusion | flops 2149842944 | bytes 20981248 | tf_op jit(solution)/shard_map/dot_general | solution.py:48
  87.1 2.4 %collective-permute-start.27 = (bf16[16,4096]{1,0:T(8,128)(2,1)S(1)}, bf16[16,4096]{1,0:T(8,128)(2,1)S(1)}, u32[]{:S(2)}, u32[]{:S(2)}) collective-permute-start(bf16[16,4096]{1,0:T(8,128)(2,1)S(1)} %get-tuple-element.9), channel_id=1, source_target_pairs={{0,7},{1,6},{2,5},{3,4},{4,3},{5,2},{6,1},{7,0},{8,15},{9,14},{10,... | collective-permute-start | bytes 393224 | tf_op jit(solution)/shard_map/ppermute | solution.py:12
  89.5 1.8 %collective-permute-start.26 = (bf16[16,4096]{1,0:T(8,128)(2,1)S(1)}, bf16[16,4096]{1,0:T(8,128)(2,1)S(1)}, u32[]{:S(2)}, u32[]{:S(2)}) collective-permute-start(bf16[16,4096]{1,0:T(8,128)(2,1)S(1)} %get-tuple-element.10), channel_id=1, source_target_pairs={{0,6},{1,7},{2,4},{3,5},{4,2},{5,3},{6,0},{7,1},{8,14},{9,15},{10,... | collective-permute-start | bytes 393224 | tf_op jit(solution)/shard_map/ppermute | solution.py:12
  91.2 3.5 %collective-permute-start.24 = (bf16[16,4096]{1,0:T(8,128)(2,1)}, bf16[16,4096]{1,0:T(8,128)(2,1)S(1)}, u32[]{:S(2)}, u32[]{:S(2)}) collective-permute-start(bf16[16,4096]{1,0:T(8,128)(2,1)} %get-tuple-element.12), channel_id=1, source_target_pairs={{0,4},{1,5},{2,6},{3,7},{4,0},{5,1},{6,2},{7,3},{8,12},{9,13},{10,... | collective-permute-start | bytes 393224 | tf_op jit(solution)/shard_map/ppermute | solution.py:12
  96.2 6.0 %collective-permute-start.22 = (bf16[16,4096]{1,0:T(8,128)(2,1)S(1)}, bf16[16,4096]{1,0:T(8,128)(2,1)S(1)}, u32[]{:S(2)}, u32[]{:S(2)}) collective-permute-start(bf16[16,4096]{1,0:T(8,128)(2,1)S(1)} %get-tuple-element.14), channel_id=1, source_target_pairs={{0,2},{1,3},{2,0},{3,1},{4,6},{5,7},{6,4},{7,5},{8,10},{9,11},{10,... | collective-permute-start | bytes 393224 | tf_op jit(solution)/shard_map/ppermute | solution.py:12
  102.8 4.1 %multiply_subtract_fusion = (f32[128,2048]{1,0:T(8,128)}, f32[128,2048]{1,0:T(8,128)}) fusion(f32[128,2048]{1,0:T(8,128)} %param.16, f32[128,2048]{1,0:T(8,128)} %param.17, f32[128,2048]{1,0:T(8,128)} %param.18, f32[128,2048]{1,0:T(8,128)S(1)} %get-tuple-element.19, f32[128]{0:T(128)} %copy-done, f32[128]{0:T(128)S(1)} %reduce_max.19, ...), kind=kOutput, calls=%fused_computation.17 | convolution fusion | flops 71827456 | bytes 6858240 | tf_op jit(solution)/shard_map/dot_general | solution.py:57
  109.0 1.7 %fusion.13 = bf16[16,4096]{1,0:T(8,128)(2,1)} fusion(f32[128,4096]{1,0:T(8,128)} %get-tuple-element.21, bf16[16,4096]{1,0:T(8,128)(2,1)S(1)} %collective-permute-done.27, bf16[16,4096]{1,0:T(8,128)(2,1)S(1)} %collective-permute-done.26, bf16[16,4096]{1,0:T(8,128)(2,1)S(1)} %collective-permute-done.25, bf16[16,4096]{1,0:T(8,128)(2,1)S(1)} %collective-permute-done.24, ...), kind=kLoop, calls=%fused_computation.27 | loop fusion | flops 983040 | bytes 1310720 | tf_op jit(solution)/shard_map/convert_element_type | solution.py:55
  (96 shorter events, 23.6 us)
Async XLA Ops:
  0.6 30.9 %collective-permute-start = (bf16[16,4096]{1,0:T(8,128)(2,1)}, bf16[16,4096]{1,0:T(8,128)(2,1)S(1)}, u32[]{:S(2)}, u32[]{:S(2)}) collective-permute-start(bf16[16,4096]{1,0:T(8,128)(2,1)} %param.13), channel_id=1, source_target_pairs={{0,1},{1,0},{2,3},{3,2},{4,5},{5,4},{6,7},{7,6},{8,9},{9,8},{10,11... | collective-permute-start | bytes 393224 | tf_op jit(solution)/shard_map/ppermute | solution.py:12
  3.7 29.8 %collective-permute-start.1 = (bf16[16,4096]{1,0:T(8,128)(2,1)}, bf16[16,4096]{1,0:T(8,128)(2,1)S(1)}, u32[]{:S(2)}, u32[]{:S(2)}) collective-permute-start(bf16[16,4096]{1,0:T(8,128)(2,1)} %param.13), channel_id=1, source_target_pairs={{0,2},{1,3},{2,0},{3,1},{4,6},{5,7},{6,4},{7,5},{8,10},{9,11},{10,... | collective-permute-start | bytes 393224 | tf_op jit(solution)/shard_map/ppermute | solution.py:12
  5.3 31.3 %collective-permute-start.2 = (bf16[16,4096]{1,0:T(8,128)(2,1)}, bf16[16,4096]{1,0:T(8,128)(2,1)S(1)}, u32[]{:S(2)}, u32[]{:S(2)}) collective-permute-start(bf16[16,4096]{1,0:T(8,128)(2,1)} %param.13), channel_id=1, source_target_pairs={{0,3},{1,2},{2,1},{3,0},{4,7},{5,6},{6,5},{7,4},{8,11},{9,10},{10,... | collective-permute-start | bytes 393224 | tf_op jit(solution)/shard_map/ppermute | solution.py:12
  5.3 8.4 %collective-permute-start.7 = (s32[16]{0:T(128)}, s32[16]{0:T(128)S(1)}, u32[]{:S(2)}, u32[]{:S(2)}) collective-permute-start(s32[16]{0:T(128)} %param.14), channel_id=1, source_target_pairs={{0,1},{1,0},{2,3},{3,2},{4,5},{5,4},{6,7},{7,6},{8,9},{9,8},{10,11... | collective-permute-start | bytes 200 | tf_op jit(solution)/shard_map/ppermute | solution.py:12
  7.2 6.5 %collective-permute-start.8 = (s32[16]{0:T(128)}, s32[16]{0:T(128)S(1)}, u32[]{:S(2)}, u32[]{:S(2)}) collective-permute-start(s32[16]{0:T(128)} %param.14), channel_id=1, source_target_pairs={{0,2},{1,3},{2,0},{3,1},{4,6},{5,7},{6,4},{7,5},{8,10},{9,11},{10,... | collective-permute-start | bytes 200 | tf_op jit(solution)/shard_map/ppermute | solution.py:12
  13.7 7.1 %collective-permute-start.10 = (s32[16]{0:T(128)}, s32[16]{0:T(128)S(1)}, u32[]{:S(2)}, u32[]{:S(2)}) collective-permute-start(s32[16]{0:T(128)} %param.14), channel_id=1, source_target_pairs={{0,4},{1,5},{2,6},{3,7},{4,0},{5,1},{6,2},{7,3},{8,12},{9,13},{10,... | collective-permute-start | bytes 200 | tf_op jit(solution)/shard_map/ppermute | solution.py:12
  26.3 16.0 %collective-permute-start.3 = (bf16[16,4096]{1,0:T(8,128)(2,1)}, bf16[16,4096]{1,0:T(8,128)(2,1)S(1)}, u32[]{:S(2)}, u32[]{:S(2)}) collective-permute-start(bf16[16,4096]{1,0:T(8,128)(2,1)} %param.13), channel_id=1, source_target_pairs={{0,4},{1,5},{2,6},{3,7},{4,0},{5,1},{6,2},{7,3},{8,12},{9,13},{10,... | collective-permute-start | bytes 393224 | tf_op jit(solution)/shard_map/ppermute | solution.py:12
  30.1 15.9 %collective-permute-start.4 = (bf16[16,4096]{1,0:T(8,128)(2,1)}, bf16[16,4096]{1,0:T(8,128)(2,1)S(1)}, u32[]{:S(2)}, u32[]{:S(2)}) collective-permute-start(bf16[16,4096]{1,0:T(8,128)(2,1)} %param.13), channel_id=1, source_target_pairs={{0,5},{1,4},{2,7},{3,6},{4,1},{5,0},{6,3},{7,2},{8,13},{9,12},{10,... | collective-permute-start | bytes 393224 | tf_op jit(solution)/shard_map/ppermute | solution.py:12
  31.6 14.4 %collective-permute-start.5 = (bf16[16,4096]{1,0:T(8,128)(2,1)}, bf16[16,4096]{1,0:T(8,128)(2,1)S(1)}, u32[]{:S(2)}, u32[]{:S(2)}) collective-permute-start(bf16[16,4096]{1,0:T(8,128)(2,1)} %param.13), channel_id=1, source_target_pairs={{0,6},{1,7},{2,4},{3,5},{4,2},{5,3},{6,0},{7,1},{8,14},{9,15},{10,... | collective-permute-start | bytes 393224 | tf_op jit(solution)/shard_map/ppermute | solution.py:12
  33.5 12.6 %collective-permute-start.6 = (bf16[16,4096]{1,0:T(8,128)(2,1)}, bf16[16,4096]{1,0:T(8,128)(2,1)S(1)}, u32[]{:S(2)}, u32[]{:S(2)}) collective-permute-start(bf16[16,4096]{1,0:T(8,128)(2,1)} %param.13), channel_id=1, source_target_pairs={{0,7},{1,6},{2,5},{3,4},{4,3},{5,2},{6,1},{7,0},{8,15},{9,14},{10,... | collective-permute-start | bytes 393224 | tf_op jit(solution)/shard_map/ppermute | solution.py:12
  54.9 8.3 %collective-permute-start.14 = (f32[3,8,16]{2,0,1:T(4,128)S(1)}, f32[3,8,16]{2,0,1:T(4,128)S(1)}, u32[]{:S(2)}, u32[]{:S(2)}) collective-permute-start(f32[3,8,16]{2,0,1:T(4,128)S(1)} %pad_maximum_fusion), channel_id=1, source_target_pairs={{0,1},{1,0},{2,3},{3,2},{4,5},{5,4},{6,7},{7,6},{8,9},{9,8},{10,11... | collective-permute-start | bytes 4616 | tf_op jit(solution)/shard_map/ppermute | solution.py:12
  55.5 9.6 %collective-permute-start.15 = (f32[3,8,16]{2,0,1:T(4,128)S(1)}, f32[3,8,16]{2,0,1:T(4,128)S(1)}, u32[]{:S(2)}, u32[]{:S(2)}) collective-permute-start(f32[3,8,16]{2,0,1:T(4,128)S(1)} %pad_maximum_fusion), channel_id=1, source_target_pairs={{0,2},{1,3},{2,0},{3,1},{4,6},{5,7},{6,4},{7,5},{8,10},{9,11},{10,... | collective-permute-start | bytes 4616 | tf_op jit(solution)/shard_map/ppermute | solution.py:12
  59.3 10.0 %collective-permute-start.16 = (f32[3,8,16]{2,0,1:T(4,128)S(1)}, f32[3,8,16]{2,0,1:T(4,128)S(1)}, u32[]{:S(2)}, u32[]{:S(2)}) collective-permute-start(f32[3,8,16]{2,0,1:T(4,128)S(1)} %pad_maximum_fusion), channel_id=1, source_target_pairs={{0,3},{1,2},{2,1},{3,0},{4,7},{5,6},{6,5},{7,4},{8,11},{9,10},{10,... | collective-permute-start | bytes 4616 | tf_op jit(solution)/shard_map/ppermute | solution.py:12
  60.3 9.7 %collective-permute-start.17 = (f32[3,8,16]{2,0,1:T(4,128)S(1)}, f32[3,8,16]{2,0,1:T(4,128)S(1)}, u32[]{:S(2)}, u32[]{:S(2)}) collective-permute-start(f32[3,8,16]{2,0,1:T(4,128)S(1)} %pad_maximum_fusion), channel_id=1, source_target_pairs={{0,4},{1,5},{2,6},{3,7},{4,0},{5,1},{6,2},{7,3},{8,12},{9,13},{10,... | collective-permute-start | bytes 4616 | tf_op jit(solution)/shard_map/ppermute | solution.py:12
  62.6 8.0 %collective-permute-start.18 = (f32[3,8,16]{2,0,1:T(4,128)S(1)}, f32[3,8,16]{2,0,1:T(4,128)S(1)}, u32[]{:S(2)}, u32[]{:S(2)}) collective-permute-start(f32[3,8,16]{2,0,1:T(4,128)S(1)} %pad_maximum_fusion), channel_id=1, source_target_pairs={{0,5},{1,4},{2,7},{3,6},{4,1},{5,0},{6,3},{7,2},{8,13},{9,12},{10,... | collective-permute-start | bytes 4616 | tf_op jit(solution)/shard_map/ppermute | solution.py:12
  63.3 8.0 %collective-permute-start.19 = (f32[3,8,16]{2,0,1:T(4,128)S(1)}, f32[3,8,16]{2,0,1:T(4,128)S(1)}, u32[]{:S(2)}, u32[]{:S(2)}) collective-permute-start(f32[3,8,16]{2,0,1:T(4,128)S(1)} %pad_maximum_fusion), channel_id=1, source_target_pairs={{0,6},{1,7},{2,4},{3,5},{4,2},{5,3},{6,0},{7,1},{8,14},{9,15},{10,... | collective-permute-start | bytes 4616 | tf_op jit(solution)/shard_map/ppermute | solution.py:12
  65.1 6.9 %collective-permute-start.20 = (f32[3,8,16]{2,0,1:T(4,128)S(1)}, f32[3,8,16]{2,0,1:T(4,128)S(1)}, u32[]{:S(2)}, u32[]{:S(2)}) collective-permute-start(f32[3,8,16]{2,0,1:T(4,128)S(1)} %pad_maximum_fusion), channel_id=1, source_target_pairs={{0,7},{1,6},{2,5},{3,4},{4,3},{5,2},{6,1},{7,0},{8,15},{9,14},{10,... | collective-permute-start | bytes 4616 | tf_op jit(solution)/shard_map/ppermute | solution.py:12
  87.1 9.2 %collective-permute-start.27 = (bf16[16,4096]{1,0:T(8,128)(2,1)S(1)}, bf16[16,4096]{1,0:T(8,128)(2,1)S(1)}, u32[]{:S(2)}, u32[]{:S(2)}) collective-permute-start(bf16[16,4096]{1,0:T(8,128)(2,1)S(1)} %get-tuple-element.9), channel_id=1, source_target_pairs={{0,7},{1,6},{2,5},{3,4},{4,3},{5,2},{6,1},{7,0},{8,15},{9,14},{10,... | collective-permute-start | bytes 393224 | tf_op jit(solution)/shard_map/ppermute | solution.py:12
  89.5 12.8 %collective-permute-start.26 = (bf16[16,4096]{1,0:T(8,128)(2,1)S(1)}, bf16[16,4096]{1,0:T(8,128)(2,1)S(1)}, u32[]{:S(2)}, u32[]{:S(2)}) collective-permute-start(bf16[16,4096]{1,0:T(8,128)(2,1)S(1)} %get-tuple-element.10), channel_id=1, source_target_pairs={{0,6},{1,7},{2,4},{3,5},{4,2},{5,3},{6,0},{7,1},{8,14},{9,15},{10,... | collective-permute-start | bytes 393224 | tf_op jit(solution)/shard_map/ppermute | solution.py:12
  91.2 17.7 %collective-permute-start.25 = (bf16[16,4096]{1,0:T(8,128)(2,1)}, bf16[16,4096]{1,0:T(8,128)(2,1)S(1)}, u32[]{:S(2)}, u32[]{:S(2)}) collective-permute-start(bf16[16,4096]{1,0:T(8,128)(2,1)} %get-tuple-element.11), channel_id=1, source_target_pairs={{0,5},{1,4},{2,7},{3,6},{4,1},{5,0},{6,3},{7,2},{8,13},{9,12},{10,... | collective-permute-start | bytes 393224 | tf_op jit(solution)/shard_map/ppermute | solution.py:12
  91.2 17.7 %collective-permute-start.24 = (bf16[16,4096]{1,0:T(8,128)(2,1)}, bf16[16,4096]{1,0:T(8,128)(2,1)S(1)}, u32[]{:S(2)}, u32[]{:S(2)}) collective-permute-start(bf16[16,4096]{1,0:T(8,128)(2,1)} %get-tuple-element.12), channel_id=1, source_target_pairs={{0,4},{1,5},{2,6},{3,7},{4,0},{5,1},{6,2},{7,3},{8,12},{9,13},{10,... | collective-permute-start | bytes 393224 | tf_op jit(solution)/shard_map/ppermute | solution.py:12
  94.7 14.3 %collective-permute-start.23 = (bf16[16,4096]{1,0:T(8,128)(2,1)S(1)}, bf16[16,4096]{1,0:T(8,128)(2,1)S(1)}, u32[]{:S(2)}, u32[]{:S(2)}) collective-permute-start(bf16[16,4096]{1,0:T(8,128)(2,1)S(1)} %get-tuple-element.13), channel_id=1, source_target_pairs={{0,3},{1,2},{2,1},{3,0},{4,7},{5,6},{6,5},{7,4},{8,11},{9,10},{10,... | collective-permute-start | bytes 393224 | tf_op jit(solution)/shard_map/ppermute | solution.py:12
  96.2 12.8 %collective-permute-start.22 = (bf16[16,4096]{1,0:T(8,128)(2,1)S(1)}, bf16[16,4096]{1,0:T(8,128)(2,1)S(1)}, u32[]{:S(2)}, u32[]{:S(2)}) collective-permute-start(bf16[16,4096]{1,0:T(8,128)(2,1)S(1)} %get-tuple-element.14), channel_id=1, source_target_pairs={{0,2},{1,3},{2,0},{3,1},{4,6},{5,7},{6,4},{7,5},{8,10},{9,11},{10,... | collective-permute-start | bytes 393224 | tf_op jit(solution)/shard_map/ppermute | solution.py:12
  102.2 6.8 %collective-permute-start.21 = (bf16[16,4096]{1,0:T(8,128)(2,1)S(1)}, bf16[16,4096]{1,0:T(8,128)(2,1)S(1)}, u32[]{:S(2)}, u32[]{:S(2)}) collective-permute-start(bf16[16,4096]{1,0:T(8,128)(2,1)S(1)} %get-tuple-element.8), channel_id=1, source_target_pairs={{0,1},{1,0},{2,3},{3,2},{4,5},{5,4},{6,7},{7,6},{8,9},{9,8},{10,11... | collective-permute-start | bytes 393224 | tf_op jit(solution)/shard_map/ppermute | solution.py:12
  (6 other events, 93.6 us)

commit v2 on v1

--- a/solution.py
+++ b/solution.py
@@ -8,22 +8,24 @@
 AXIS = "vocab"
 
 
-def swap(value, members, step):
-    return lax.ppermute(value, AXIS, [(i, i ^ step) for i in range(members)])
-
-
-def gather(value, members):
-    return [value] + [swap(value, members, step) for step in range(1, members)]
+def gather(value):
+    members = lax.axis_size(AXIS)
+    copies = jnp.broadcast_to(value[None], (members,) + value.shape)
+    return lax.all_to_all(copies, AXIS, split_axis=0, concat_axis=0)
 
 
 def body(hidden, targets, head, global_frag, momentum, peer_delta):
     members = lax.axis_size(AXIS)
-    own = hidden.shape[0]
+    own, depth = hidden.shape
     rows = own * members
     width = head.shape[1]
 
-    rows_all = jnp.concatenate(gather(hidden, members), axis=0)
-    ids_all = jnp.concatenate(gather(targets, members), axis=0)
+    digits = jnp.stack([targets // 256, targets % 256], axis=1).astype(jnp.bfloat16)
+    packed = jnp.concatenate([hidden, jnp.pad(digits, ((0, 0), (0, 126)))], axis=1)
+    packed = gather(packed).reshape(rows, depth + 128)
+    rows_all = packed[:, :depth]
+    digits = packed[:, depth : depth + 2].astype(jnp.int32)
+    ids_all = digits[:, 0] * 256 + digits[:, 1]
 
     logits = jnp.dot(rows_all, head, preferred_element_type=jnp.float32)
     columns = lax.axis_index(AXIS) * width + jnp.arange(width, dtype=jnp.int32)
@@ -32,12 +34,7 @@
     local_sum = jnp.sum(jnp.exp(logits - local_max[:, None]), axis=1)
     local_pick = jnp.sum(jnp.where(hit, logits, 0.0), axis=1)
 
-    stats = jnp.stack([local_max, local_sum, local_pick]).reshape(3, members, own)
-    seen = [stats]
-    for step in range(1, members):
-        there = swap(stats, members, step)
-        seen.append(there[:, jnp.array([i ^ step for i in range(members)])])
-    seen = jnp.stack(seen).reshape(members, 3, rows)
+    seen = gather(jnp.stack([local_max, local_sum, local_pick]))
     top = jnp.max(seen[:, 0], axis=0)
     total = jnp.sum(seen[:, 1] * jnp.exp(seen[:, 0] - top), axis=0)
     picked = jnp.sum(seen[:, 2], axis=0)
@@ -48,11 +45,9 @@
     partial_grad = lax.dot_general(
         dlogits, head, (((1,), (1,)), ((), ())), preferred_element_type=jnp.float32
     )
-    summed = partial_grad[:own]
-    for step in range(1, members):
-        block = partial_grad[step * own : (step + 1) * own].astype(jnp.bfloat16)
-        summed = summed + swap(block, members, step).astype(jnp.float32)
-    hidden_grad = summed.astype(jnp.bfloat16)
+    blocks = partial_grad.astype(jnp.bfloat16).reshape(members, own, depth)
+    blocks = lax.all_to_all(blocks, AXIS, split_axis=0, concat_axis=0)
+    hidden_grad = jnp.sum(blocks.astype(jnp.float32), axis=0).astype(jnp.bfloat16)
 
     frag_grad = lax.dot_general(
         rows_all[:, :FRAG], dlogits, (((0,), (0,)), ((), ())), preferred_element_type=jnp.float32

time: 113 us -> 99.5 us (0.88)
  starting transfers between devices: 50.4 us -> 10.8 us
  waiting for transfers between devices: 17.9 us -> 46 us
  blocking collectives: 0 us -> 9.97 us
  local copies, waits for them, and re-layouts: 7.4 us -> 1.18 us
  other arithmetic: 8.09 us -> 3.68 us
    ppermute x28 -> x0, starting transfers between devices: 50.4 us -> none  [swap(): return lax.ppermute(value, AXIS, [(i, i ^ step) for i in range(members)])]
    all_to_all x0 -> x2, waiting for transfers between devices: none -> 46 us  [the longest x1 26.5 us: gather(): return lax.all_to_all(copies, AXIS, split_axis=0, concat_axis=0)]
    ppermute x28 -> x0, waiting for transfers between devices: 17.9 us -> none  [swap(): return lax.ppermute(value, AXIS, [(i, i ^ step) for i in range(members)])]
    all_to_all x0 -> x2, starting transfers between devices: none -> 10.8 us  [the longest x1 7.28 us: gather(): return lax.all_to_all(copies, AXIS, split_axis=0, concat_axis=0)]
    all_to_all x0 -> x1, blocking collectives: none -> 9.97 us  [gather(): return lax.all_to_all(copies, AXIS, split_axis=0, concat_axis=0)]
    gather x14 -> x0, local copies, waits for them, and re-layouts: 4.08 us -> none  [body(): seen.append(there[:, jnp.array([i ^ step for i in range(members)])])]
    gather x7 -> x0, other arithmetic: 3.97 us -> none  [body(): seen.append(there[:, jnp.array([i ^ step for i in range(members)])])]
    convert_element_type x1, other arithmetic: 1.74 us -> 0.01 us  [body(): digits = packed[:, depth:depth + 2].astype(jnp.int32)]
  transfers between devices with their start and end apart: 28 -> 2, of which waited for: 7 -> 2; matrix products, arithmetic and copies ran while one was open for 14% -> 5% of each run, Pallas kernels for 0% -> 0%
where the time goes in v2:
time: 99.5 us; the launch traced here: 99.1 us
  waiting for transfers between devices  46 us (46%)
  matrix products  25 us (25%)
  starting transfers between devices  10.8 us (11%)
  blocking collectives  9.97 us (10%)
  other arithmetic  3.68 us (4%)
  between operations  2.46 us (2%)
  local copies, waits for them, and re-layouts  1.18 us (1%)
    all_to_all x1, waiting for transfers between devices, gather(): return lax.all_to_all(copies, AXIS, split_axis=0, concat_axis=0)  26.5 us
    all_to_all x1, waiting for transfers between devices, body(): blocks = lax.all_to_all(blocks, AXIS, split_axis=0, concat_axis=0)  19.5 us
    dot_general x1, matrix products, body(): lax.dot_general(dlogits, head, (((1,), (1,)), ((), ())), preferred_elemen...  12.7 us
    all_to_all x1, blocking collectives, gather(): return lax.all_to_all(copies, AXIS, split_axis=0, concat_axis=0)  9.97 us
    dot_general x1, matrix products, body(): logits = jnp.dot(rows_all, head, preferred_element_type=jnp.float32)  8.19 us
    all_to_all x1, starting transfers between devices, gather(): return lax.all_to_all(copies, AXIS, split_axis=0, concat_axis=0)  7.28 us
    dot_general x1, matrix products, body(): lax.dot_general(rows_all[:, :FRAG], dlogits, (((0,), (0,)), ((), ())), pr...  4.12 us
    all_to_all x1, starting transfers between devices, body(): blocks = lax.all_to_all(blocks, AXIS, split_axis=0, concat_axis=0)  3.56 us
  transfers between devices with their start and end apart: 2, of which 2 were waited for; matrix products, arithmetic and copies ran while one was open for 5% of the time, Pallas kernels for 0%

profile of v2, /device:TPU:0, one launch (start us, length us, event | category | flops | bytes accessed | tf_op | source)
XLA Modules:
  0.0 99.1 jit_solution(6984310976179146777)
XLA Ops:
  0.6 0.7 convert_bitcast_fusion
  1.3 0.1 copy.22
  1.4 0.9 fusion.10
  2.3 1.1 %broadcast_in_dim.7 = bf16[8,16,4224]{2,1,0:T(8,128)(2,1)} broadcast(bf16[16,4224]{1,0:T(8,128)(2,1)S(1)} %fusion.10), dimensions={1,2} | broadcast | bytes 1216512 | tf_op jit(solution)/shard_map/broadcast_in_dim | solution.py:13
  3.4 7.3 %all-to-all-start = ((bf16[8,16,4224]{2,1,0:T(8,128)(2,1)}), bf16[8,16,4224]{2,1,0:T(8,128)(2,1)S(1)}, u32[]{:S(2)}, u32[]{:S(2)}) async-start(bf16[8,16,4224]{2,1,0:T(8,128)(2,1)} %broadcast_in_dim.7), calls=%async_computation | async-start | bytes 2162688 | tf_op jit(solution)/shard_map/all_to_all | solution.py:14
  10.7 26.5 %all-to-all-done = bf16[8,16,4224]{2,1,0:T(8,128)(2,1)S(1)} async-done(((bf16[8,16,4224]{2,1,0:T(8,128)(2,1)}), bf16[8,16,4224]{2,1,0:T(8,128)(2,1)S(1)}, u32[]{:S(2)}, u32[]{:S(2)}) %all-to-all-start) | async-done | bytes 1081376 | tf_op jit(solution)/shard_map/all_to_all | solution.py:14
  37.2 0.2 fusion.11
  37.3 8.2 %fusion.18 = (f32[128]{0:T(128)S(1)}, f32[128,2048]{1,0:T(8,128)S(1)}) fusion(bf16[4096,2048]{1,0:T(8,128)(2,1)} %param.8, bf16[128,4224]{1,0:T(8,128)(2,1)S(1)} %bitcast.18), kind=kOutput, calls=%fused_computation.38 | convolution fusion | flops 2147745792 | bytes 18874880 | tf_op jit(solution)/shard_map/dot_general | solution.py:30
  45.5 0.4 exponential_reduce_fusion
  46.0 10.0 %all_to_all.15 = f32[8,3,128]{2,1,0:T(4,128)S(1)} all-to-all(f32[8,3,128]{2,1,0:T(4,128)S(1)} %broadcast_in_dim.10), channel_id=1, replica_groups=mesh['outer'=4,'vocab'=8] {'vocab'}, dimensions={0} | all-to-all | bytes 24576 | tf_op jit(solution)/shard_map/all_to_all | solution.py:14
  56.0 12.7 %convolution_convert_fusion = bf16[128,4096]{1,0:T(8,128)(2,1)} fusion(bf16[4096,2048]{1,0:T(8,128)(2,1)} %param.8, f32[128,2048]{1,0:T(8,128)S(1)} %get-tuple-element.14, f32[128]{0:T(128)S(1)} %multiply_reduce_fusion, f32[128]{0:T(128)S(1)} %reduce_max.19, s32[2048]{0:T(1024)S(1)} %iota_add_fusion, s32[128]{0:T(128)S(1)} %fusion.11), kind=kOutput, calls=%fused_computation | convolution fusion | flops 2149842944 | bytes 18884096 | tf_op jit(solution)/shard_map/dot_general | solution.py:45
  68.7 3.6 %all-to-all-start.2 = ((bf16[8,16,4096]{2,1,0:T(8,128)(2,1)}), bf16[8,16,4096]{2,1,0:T(8,128)(2,1)S(1)}, u32[]{:S(2)}, u32[]{:S(2)}) async-start(bf16[8,16,4096]{2,1,0:T(8,128)(2,1)} %bitcast.20), calls=%async_computation.2 | async-start | bytes 2097152 | tf_op jit(solution)/shard_map/all_to_all | solution.py:49
  72.2 0.6 subtract_reduce_fusion
  73.5 4.1 %multiply_subtract_fusion = (f32[128,2048]{1,0:T(8,128)}, f32[128,2048]{1,0:T(8,128)}) fusion(f32[128,2048]{1,0:T(8,128)} %param.9, f32[128,2048]{1,0:T(8,128)} %param.10, f32[128,2048]{1,0:T(8,128)} %param.11, f32[128,2048]{1,0:T(8,128)S(1)} %get-tuple-element.14, f32[128]{0:T(128)S(1)} %multiply_reduce_fusion, f32[128]{0:T(128)S(1)} %reduce_max.19, ...), kind=kOutput, calls=%fused_computation.13 | convolution fusion | flops 71827456 | bytes 6858240 | tf_op jit(solution)/shard_map/dot_general | solution.py:52
  77.6 19.5 %all-to-all-done.2 = bf16[8,16,4096]{2,1,0:T(8,128)(2,1)S(1)} async-done(((bf16[8,16,4096]{2,1,0:T(8,128)(2,1)}), bf16[8,16,4096]{2,1,0:T(8,128)(2,1)S(1)}, u32[]{:S(2)}, u32[]{:S(2)}) %all-to-all-start.2) | async-done | bytes 1048608 | tf_op jit(solution)/shard_map/all_to_all | solution.py:49
  97.1 0.8 reduce_sum.62
  (9 shorter events, 0.1 us)
Async XLA Ops:
  3.4 33.8 %all-to-all-start = ((bf16[8,16,4224]{2,1,0:T(8,128)(2,1)}), bf16[8,16,4224]{2,1,0:T(8,128)(2,1)S(1)}, u32[]{:S(2)}, u32[]{:S(2)}) async-start(bf16[8,16,4224]{2,1,0:T(8,128)(2,1)} %broadcast_in_dim.7), calls=%async_computation | async-start | bytes 2162688 | tf_op jit(solution)/shard_map/all_to_all | solution.py:14
  68.7 28.5 %all-to-all-start.2 = ((bf16[8,16,4096]{2,1,0:T(8,128)(2,1)}), bf16[8,16,4096]{2,1,0:T(8,128)(2,1)S(1)}, u32[]{:S(2)}, u32[]{:S(2)}) async-start(bf16[8,16,4096]{2,1,0:T(8,128)(2,1)} %bitcast.20), calls=%async_computation.2 | async-start | bytes 2097152 | tf_op jit(solution)/shard_map/all_to_all | solution.py:49

commit v3 on v2

v3 whole, which is shorter than its diff:
```python
import jax
import jax.numpy as jnp
from jax import lax
from jax.sharding import PartitionSpec as P

FRAG = 128
REPLICAS = 4
AXIS = "vocab"
SEND = jnp.float16


def swap(value, step):
    return lax.ppermute(value, AXIS, [(i, i ^ step) for i in range(lax.axis_size(AXIS))])


def doubled(value, step):
    return jnp.concatenate([value, swap(value, step)], axis=0)


def far_steps():
    step = lax.axis_size(AXIS) // 2
    steps = []
    while step > 2:
        steps.append(step)
        step //= 2
    return steps


def flip_blocks(value, own):
    members = lax.axis_size(AXIS)
    me = lax.axis_index(AXIS)
    lead = value.shape[:-1]
    bits = [1, 2] + far_steps()[::-1]
    value = value.reshape(lead + (2,) * len(bits) + (own,))
    for place, bit in enumerate(bits):
        value = jnp.where((me & bit) != 0, jnp.flip(value, len(lead) + place), value)
    return value.reshape(lead + (members * own,))


def to_device_order(value, own):
    value = flip_blocks(value, own)
    return reverse_bits(value, own)


def to_xor_order(value, own):
    return flip_blocks(reverse_bits(value, own), own)


def reverse_bits(value, own):
    lead = value.shape[:-1]
    count = len(far_steps()) + 2
    value = value.reshape(lead + (2,) * count + (own,))
    first = len(lead)
    order = list(range(first)) + list(range(first + count - 1, first - 1, -1)) + [first + count]
    return value.transpose(order).reshape(lead + (-1,))


def gather_rows(hidden, digits):
    half = hidden.shape[1] // 2
    for step in far_steps():
        hidden, digits = doubled(hidden, step), doubled(digits, step)
    left = jnp.concatenate([hidden[:, :half], digits], axis=1)
    right = hidden[:, half:]
    near = right.shape[0]
    left = doubled(left, 2)
    right = doubled(right, 1)
    left = doubled(left, 1)
    other = swap(right, 2)
    right = jnp.concatenate([right[:near], other[:near], right[near:], other[near:]], axis=0)
    return left[:, :half], right, left[:, half:]


def scatter_sums(left, right, scale):
    rows = left.shape[0]
    quarter = rows // 4

    def code(value):
        return (value * scale).astype(SEND)

    def decode(value):
        return value.astype(jnp.float32) * (1.0 / scale)

    left = left[: rows // 2] + decode(swap(code(left[rows // 2 :]), 1))
    right = right.reshape(2, 2, quarter, -1)
    right = right[:, 0] + decode(swap(code(right[:, 1]), 2))
    left = left[:quarter] + decode(swap(code(left[quarter:]), 2))
    right = right[0] + decode(swap(code(right[1]), 1))
    both = jnp.concatenate([left, right], axis=1)
    for step in far_steps()[::-1]:
        keep = both.shape[0] // 2
        both = both[:keep] + decode(swap(code(both[keep:]), step))
    return both


def body(hidden, targets, head, global_frag, momentum, peer_delta):
    members = lax.axis_size(AXIS)
    own, depth = hidden.shape
    half = depth // 2
    rows = own * members
    width = head.shape[1]

    digits = jnp.stack([targets // 256, targets % 256], axis=1).astype(jnp.bfloat16)
    digits = jnp.pad(digits, ((0, 0), (0, 126)))
    left, right, digits = gather_rows(hidden, digits)
    digits = digits[:, :2].astype(jnp.int32)
    ids_all = digits[:, 0] * 256 + digits[:, 1]

    logits = jnp.dot(left, head[:half], preferred_element_type=jnp.float32)
    logits = logits + jnp.dot(right, head[half:], preferred_element_type=jnp.float32)
    columns = lax.axis_index(AXIS) * width + jnp.arange(width, dtype=jnp.int32)
    hit = columns[None, :] == ids_all[:, None]
    local_max = jnp.max(logits, axis=1)
    local_sum = jnp.sum(jnp.exp(logits - local_max[:, None]), axis=1)
    local_pick = jnp.sum(jnp.where(hit, logits, 0.0), axis=1)

    stats = to_device_order(jnp.stack([local_max, local_sum, local_pick]), own)
    seen = lax.all_to_all(
        jnp.broadcast_to(stats[None], (members,) + stats.shape), AXIS, split_axis=0, concat_axis=0
    )
    top = jnp.max(seen[:, 0], axis=0)
    total = jnp.sum(seen[:, 1] * jnp.exp(seen[:, 0] - top), axis=0)
    picked = jnp.sum(seen[:, 2], axis=0)
    loss = jnp.mean(top + jnp.log(total) - picked).reshape((1,))
    top, total = to_xor_order(jnp.stack([top, total]), own)

    onehot = hit.astype(jnp.float32)
    dlogits = ((jnp.exp(logits - top[:, None]) / total[:, None] - onehot) / rows).astype(jnp.bfloat16)

    def grad(part):
        return lax.dot_general(
            dlogits, part, (((1,), (1,)), ((), ())), preferred_element_type=jnp.float32
        )

    hidden_grad = scatter_sums(grad(head[:half]), grad(head[half:]), 2.0**14 * rows).astype(jnp.bfloat16)

    frag_grad = lax.dot_general(
        left[:, :FRAG], dlogits, (((0,), (0,)), ((), ())), preferred_element_type=jnp.float32
    )
    local_frag = head[:FRAG].astype(jnp.float32) - 1.0 * frag_grad
    pseudo = (global_frag - local_frag + peer_delta) / REPLICAS
    new_momentum = 0.9 * momentum + pseudo
    new_global = global_frag - 0.7 * (pseudo + 0.9 * new_momentum)
    return (loss, hidden_grad, new_global, new_momentum)


def solution(mesh):
    in_specs = (
        P(("outer", "vocab"), None),
        P(("outer", "vocab")),
        P("outer", "vocab"),
        P(None, "vocab"),
        P(None, "vocab"),
        P("outer", "vocab"),
    )
    out_specs = (P("outer"), P(("outer", "vocab"), None), P("outer", "vocab"), P("outer", "vocab"))
    return jax.shard_map(body, mesh=mesh, in_specs=in_specs, out_specs=out_specs, check_vma=False)
```

time: 99.5 us -> 82.2 us (0.83)
  waiting for transfers between devices: 46 us -> 31.3 us
  matrix products: 25 us -> 22 us
  blocking collectives: 9.97 us -> 11.6 us
  starting transfers between devices: 10.8 us -> 9.19 us
    all_to_all x2 -> x0, waiting for transfers between devices: 46 us -> none  [the longest x1 26.5 us: gather(): return lax.all_to_all(copies, AXIS, split_axis=0, concat_axis=0)]
    ppermute x0 -> x11, waiting for transfers between devices: none -> 31.3 us  [swap(): lax.ppermute(value, AXIS, [(i, i ^ step) for i in range(lax.axis_size(AXI...]
    all_to_all x2 -> x0, starting transfers between devices: 10.8 us -> none  [the longest x1 7.28 us: gather(): return lax.all_to_all(copies, AXIS, split_axis=0, concat_axis=0)]
    ppermute x0 -> x11, starting transfers between devices: none -> 9.19 us  [swap(): lax.ppermute(value, AXIS, [(i, i ^ step) for i in range(lax.axis_size(AXI...]
    dot_general x3 -> x5, matrix products: 25 us -> 22 us  [the longest x2 12.8 us: grad(): lax.dot_general(dlogits, part, (((1,), (1,)), ((), ())), preferred_elemen...]
    all_to_all x1, blocking collectives: 9.97 us -> 11.6 us  [body(): lax.all_to_all(jnp.broadcast_to(stats[None], (members,) + stats.shape), A...]
  transfers between devices with their start and end apart: 2 -> 11, of which waited for: 2 -> 9; matrix products, arithmetic and copies ran while one was open for 5% -> 12% of each run, Pallas kernels for 0% -> 0%
where the time goes in v3:
time: 82.2 us; the launch traced here: 81.9 us
  waiting for transfers between devices  31.3 us (38%)
  matrix products  22 us (27%)
  blocking collectives  11.6 us (14%)
  starting transfers between devices  9.19 us (11%)
  other arithmetic  3.16 us (4%)
  between operations  2.75 us (3%)
  local copies, waits for them, and re-layouts  1.95 us (2%)
    ppermute x11, waiting for transfers between devices, swap(): lax.ppermute(value, AXIS, [(i, i ^ step) for i in range(lax.axis_size(AXI...  31.3 us
    dot_general x2, matrix products, grad(): lax.dot_general(dlogits, part, (((1,), (1,)), ((), ())), preferred_elemen...  12.8 us
    all_to_all x1, blocking collectives, body(): lax.all_to_all(jnp.broadcast_to(stats[None], (members,) + stats.shape), A...  11.6 us
    ppermute x11, starting transfers between devices, swap(): lax.ppermute(value, AXIS, [(i, i ^ step) for i in range(lax.axis_size(AXI...  9.19 us
    dot_general x1, matrix products, body(): jnp.dot(right, head[half:], preferred_element_type=jnp.float32)  4.67 us
    dot_general x1, matrix products, body(): lax.dot_general(left[:, :FRAG], dlogits, (((0,), (0,)), ((), ())), prefer...  3.17 us
  transfers between devices with their start and end apart: 11, of which 9 were waited for; matrix products, arithmetic and copies ran while one was open for 12% of the time, Pallas kernels for 0%

profile of v3, /device:TPU:0, one launch (start us, length us, event | category | flops | bytes accessed | tf_op | source)
XLA Modules:
  0.0 81.9 jit_solution(2642902006934110325)
XLA Ops:
  0.6 0.7 convert_bitcast_fusion
  1.3 4.1 %collective-permute-start.1 = (bf16[16,128]{0,1:T(8,128)(2,1)S(1)}, bf16[16,128]{0,1:T(8,128)(2,1)S(1)}, u32[]{:S(2)}, u32[]{:S(2)}) collective-permute-start(bf16[16,128]{0,1:T(8,128)(2,1)S(1)} %fusion.43), channel_id=1, source_target_pairs={{0,4},{1,5},{2,6},{3,7},{4,0},{5,1},{6,2},{7,3},{8,12},{9,13},{10,... | collective-permute-start | bytes 12296 | tf_op jit(solution)/shard_map/ppermute | solution.py:13
  5.5 0.9 %constant_dynamic-update-slice_fusion.1 = bf16[32,4096]{1,0:T(8,128)(2,1)S(1)} fusion(bf16[16,4096]{1,0:T(8,128)(2,1)} %param.6), kind=kLoop, calls=%fused_computation.82 | loop fusion | bytes 262144
  6.5 1.1 %collective-permute-done.1 = bf16[16,128]{0,1:T(8,128)(2,1)S(1)} collective-permute-done((bf16[16,128]{0,1:T(8,128)(2,1)S(1)}, bf16[16,128]{0,1:T(8,128)(2,1)S(1)}, u32[]{:S(2)}, u32[]{:S(2)}) %collective-permute-start.1) | collective-permute-done | bytes 4128 | tf_op jit(solution)/shard_map/ppermute | solution.py:13
  7.7 6.6 %collective-permute-done = bf16[16,4096]{1,0:T(8,128)(2,1)S(1)} collective-permute-done((bf16[16,4096]{1,0:T(8,128)(2,1)}, bf16[16,4096]{1,0:T(8,128)(2,1)S(1)}, u32[]{:S(2)}, u32[]{:S(2)}) %collective-permute-start) | collective-permute-done | bytes 131104 | tf_op jit(solution)/shard_map/ppermute | solution.py:13
  14.3 1.6 %collective-permute-start.4 = (bf16[32,2048]{1,0:T(8,128)(2,1)S(1)}, bf16[32,2048]{1,0:T(8,128)(2,1)S(1)}, u32[]{:S(2)}, u32[]{:S(2)}) collective-permute-start(bf16[32,2048]{1,0:T(8,128)(2,1)S(1)} %get-tuple-element.9), channel_id=1, source_target_pairs={{0,1},{1,0},{2,3},{3,2},{4,5},{5,4},{6,7},{7,6},{8,9},{9,8},{10,11... | collective-permute-start | bytes 393224 | tf_op jit(solution)/shard_map/ppermute | solution.py:13
  16.0 3.3 %collective-permute-done.4 = bf16[32,2048]{1,0:T(8,128)(2,1)S(1)} collective-permute-done((bf16[32,2048]{1,0:T(8,128)(2,1)S(1)}, bf16[32,2048]{1,0:T(8,128)(2,1)S(1)}, u32[]{:S(2)}, u32[]{:S(2)}) %collective-permute-start.4) | collective-permute-done | bytes 131104 | tf_op jit(solution)/shard_map/ppermute | solution.py:13
  19.6 2.7 %collective-permute-done.2 = bf16[32,2176]{1,0:T(8,128)(2,1)S(1)} collective-permute-done((bf16[32,2176]{1,0:T(8,128)(2,1)S(1)}, bf16[32,2176]{1,0:T(8,128)(2,1)S(1)}, u32[]{:S(2)}, u32[]{:S(2)}) %collective-permute-start.2) | collective-permute-done | bytes 139296 | tf_op jit(solution)/shard_map/ppermute | solution.py:13
  22.4 4.3 %collective-permute-done.5 = bf16[64,2048]{1,0:T(8,128)(2,1)S(1)} collective-permute-done((bf16[64,2048]{1,0:T(8,128)(2,1)S(1)}, bf16[64,2048]{1,0:T(8,128)(2,1)S(1)}, u32[]{:S(2)}, u32[]{:S(2)}) %collective-permute-start.5) | collective-permute-done | bytes 262176 | tf_op jit(solution)/shard_map/ppermute | solution.py:13
  26.7 4.7 %fusion.2 = f32[128,2048]{1,0:T(8,128)S(1)} fusion(bf16[4096,2048]{1,0:T(8,128)(2,1)} %param.8, bf16[32,2048]{1,0:T(8,128)(2,1)S(1)} %get-tuple-element.11, bf16[32,2048]{1,0:T(8,128)(2,1)S(1)} %collective-permute-done.4, bf16[32,2048]{1,0:T(8,128)(2,1)S(1)} %get-tuple-element.10, bf16[32,2048]{1,0:T(8,128)(2,1)S(1)} %get-tuple-element.9), kind=kOutput, calls=%fused_computation.2 | convolution fusion | flops 1075838976 | bytes 9961472 | tf_op jit(solution)/shard_map/dot_general | solution.py:109
  31.7 1.4 %fusion.64 = (f32[128]{0:T(128)S(1)}, f32[128,2048]{1,0:T(8,128)S(1)}) fusion(f32[128,2048]{1,0:T(8,128)S(1)} %fusion.2, bf16[4096,2048]{1,0:T(8,128)(2,1)S(1)} %copy-done, bf16[128,2176]{1,0:T(8,128)(2,1)S(1)} %pad_maximum_fusion), kind=kOutput, calls=%fused_computation.105 | convolution fusion | flops 1074265984 | bytes 11010560 | tf_op jit(solution)/shard_map/dot_general | solution.py:108
  33.9 11.6 %all_to_all.5 = f32[8,3,128]{2,1,0:T(4,128)S(1)} all-to-all(f32[8,3,128]{2,1,0:T(4,128)S(1)} %broadcast_in_dim.17), channel_id=1, replica_groups=mesh['outer'=4,'vocab'=8] {'vocab'}, dimensions={0} | all-to-all | bytes 24576 | tf_op jit(solution)/shard_map/all_to_all | solution.py:117
  46.0 6.3 %fusion.4 = f32[128,2048]{1,0:T(8,128)S(1)} fusion(bf16[4096,2048]{1,0:T(8,128)(2,1)} %param.8, f32[128,2048]{1,0:T(8,128)S(1)} %get-tuple-element.20, f32[128]{0:T(128)S(1)} %div.42, f32[128]{0:T(128)S(1)} %sub.51, s32[2048]{0:T(1024)S(1)} %iota_add_fusion, s32[128]{0:T(128)S(1)} %fusion.40), kind=kOutput, calls=%fused_computation.4 | convolution fusion | flops 1075576832 | bytes 10495488 | tf_op jit(solution)/shard_map/dot_general | solution.py:130
  52.4 6.5 %fusion = f32[128,2048]{1,0:T(8,128)S(1)} fusion(bf16[4096,2048]{1,0:T(8,128)(2,1)} %param.8, f32[128,2048]{1,0:T(8,128)S(1)} %get-tuple-element.20, f32[128]{0:T(128)S(1)} %div.42, f32[128]{0:T(128)S(1)} %sub.51, s32[2048]{0:T(1024)S(1)} %iota_add_fusion, s32[128]{0:T(128)S(1)} %fusion.40), kind=kOutput, calls=%fused_computation | convolution fusion | flops 1075576832 | bytes 10495488 | tf_op jit(solution)/shard_map/dot_general | solution.py:130
  58.9 0.6 collective-permute-start.6
  59.5 0.7 collective-permute-start.8
  60.2 6.2 %collective-permute-done.6 = f16[64,2048]{1,0:T(8,128)(2,1)S(1)} collective-permute-done((f16[64,2048]{1,0:T(8,128)(2,1)S(1)}, f16[64,2048]{1,0:T(8,128)(2,1)S(1)}, u32[]{:S(2)}, u32[]{:S(2)}) %collective-permute-start.6) | collective-permute-done | bytes 262176 | tf_op jit(solution)/shard_map/ppermute | solution.py:13
  66.6 0.8 collective-permute-done.8
  67.5 1.2 %collective-permute-start.9 = (f16[32,2048]{1,0:T(8,128)(2,1)S(1)}, f16[32,2048]{1,0:T(8,128)(2,1)S(1)}, u32[]{:S(2)}, u32[]{:S(2)}) collective-permute-start(f16[32,2048]{1,0:T(8,128)(2,1)S(1)} %fusion.39), channel_id=1, source_target_pairs={{0,1},{1,0},{2,3},{3,2},{4,5},{5,4},{6,7},{7,6},{8,9},{9,8},{10,11... | collective-permute-start | bytes 393224 | tf_op jit(solution)/shard_map/ppermute | solution.py:13
  68.7 3.9 %collective-permute-done.7 = f16[32,2048]{1,0:T(8,128)(2,1)S(1)} collective-permute-done((f16[32,2048]{1,0:T(8,128)(2,1)S(1)}, f16[32,2048]{1,0:T(8,128)(2,1)S(1)}, u32[]{:S(2)}, u32[]{:S(2)}) %collective-permute-start.7) | collective-permute-done | bytes 131104 | tf_op jit(solution)/shard_map/ppermute | solution.py:13
  73.3 3.2 %multiply_subtract_fusion = (f32[128,2048]{1,0:T(8,128)}, f32[128,2048]{1,0:T(8,128)}) fusion(f32[128,2048]{1,0:T(8,128)S(1)} %copy-done.1, f32[128,2048]{1,0:T(8,128)S(1)} %copy-done.2, f32[128,2048]{1,0:T(8,128)S(1)} %copy-done.3, f32[128,2048]{1,0:T(8,128)S(1)} %get-tuple-element.20, f32[128]{0:T(128)S(1)} %div.42, f32[128]{0:T(128)S(1)} %sub.51, ...), kind=kOutput, calls=%fused_computation.19 | convolution fusion | flops 71991296 | bytes 7382528 | tf_op jit(solution)/shard_map/dot_general | solution.py:136
  76.5 0.6 subtract_reduce_fusion
  77.7 2.3 %collective-permute-done.10 = f16[16,4096]{1,0:T(8,128)(2,1)S(1)} collective-permute-done((f16[16,4096]{1,0:T(8,128)(2,1)S(1)}, f16[16,4096]{1,0:T(8,128)(2,1)S(1)}, u32[]{:S(2)}, u32[]{:S(2)}) %collective-permute-start.10) | collective-permute-done | bytes 131104 | tf_op jit(solution)/shard_map/ppermute | solution.py:13
  80.0 0.7 fusion.32
  (68 shorter events, 3.2 us)
Async XLA Ops:
  1.3 6.3 %collective-permute-start.1 = (bf16[16,128]{0,1:T(8,128)(2,1)S(1)}, bf16[16,128]{0,1:T(8,128)(2,1)S(1)}, u32[]{:S(2)}, u32[]{:S(2)}) collective-permute-start(bf16[16,128]{0,1:T(8,128)(2,1)S(1)} %fusion.43), channel_id=1, source_target_pairs={{0,4},{1,5},{2,6},{3,7},{4,0},{5,1},{6,2},{7,3},{8,12},{9,13},{10,... | collective-permute-start | bytes 12296 | tf_op jit(solution)/shard_map/ppermute | solution.py:13
  5.4 8.9 %collective-permute-start = (bf16[16,4096]{1,0:T(8,128)(2,1)}, bf16[16,4096]{1,0:T(8,128)(2,1)S(1)}, u32[]{:S(2)}, u32[]{:S(2)}) collective-permute-start(bf16[16,4096]{1,0:T(8,128)(2,1)} %param.6), channel_id=1, source_target_pairs={{0,4},{1,5},{2,6},{3,7},{4,0},{5,1},{6,2},{7,3},{8,12},{9,13},{10,... | collective-permute-start | bytes 393224 | tf_op jit(solution)/shard_map/ppermute | solution.py:13
  14.3 5.0 %collective-permute-start.4 = (bf16[32,2048]{1,0:T(8,128)(2,1)S(1)}, bf16[32,2048]{1,0:T(8,128)(2,1)S(1)}, u32[]{:S(2)}, u32[]{:S(2)}) collective-permute-start(bf16[32,2048]{1,0:T(8,128)(2,1)S(1)} %get-tuple-element.9), channel_id=1, source_target_pairs={{0,1},{1,0},{2,3},{3,2},{4,5},{5,4},{6,7},{7,6},{8,9},{9,8},{10,11... | collective-permute-start | bytes 393224 | tf_op jit(solution)/shard_map/ppermute | solution.py:13
  15.9 15.7 %copy-start = (bf16[4096,2048]{1,0:T(8,128)(2,1)S(1)}, bf16[4096,2048]{1,0:T(8,128)(2,1)}, u32[]{:S(2)}) copy-start(bf16[4096,2048]{1,0:T(8,128)(2,1)} %param.8) | copy-start | bytes 50331652
  15.9 6.3 %collective-permute-start.2 = (bf16[32,2176]{1,0:T(8,128)(2,1)S(1)}, bf16[32,2176]{1,0:T(8,128)(2,1)S(1)}, u32[]{:S(2)}, u32[]{:S(2)}) collective-permute-start(bf16[32,2176]{1,0:T(8,128)(2,1)S(1)} %maximum_maximum_fusion), channel_id=1, source_target_pairs={{0,2},{1,3},{2,0},{3,1},{4,6},{5,7},{6,4},{7,5},{8,10},{9,11},{10,... | collective-permute-start | bytes 417800 | tf_op jit(solution)/shard_map/ppermute | solution.py:13
  19.4 7.3 %collective-permute-start.5 = (bf16[64,2048]{1,0:T(8,128)(2,1)S(1)}, bf16[64,2048]{1,0:T(8,128)(2,1)S(1)}, u32[]{:S(2)}, u32[]{:S(2)}) collective-permute-start(bf16[64,2048]{1,0:T(8,128)(2,1)S(1)} %pad_maximum_fusion.3), channel_id=1, source_target_pairs={{0,2},{1,3},{2,0},{3,1},{4,6},{5,7},{6,4},{7,5},{8,10},{9,11},{10,... | collective-permute-start | bytes 786440 | tf_op jit(solution)/shard_map/ppermute | solution.py:13
  22.3 9.1 %collective-permute-start.3 = (bf16[64,2176]{1,0:T(8,128)(2,1)S(1)}, bf16[64,2176]{1,0:T(8,128)(2,1)S(1)}, u32[]{:S(2)}, u32[]{:S(2)}) collective-permute-start(bf16[64,2176]{1,0:T(8,128)(2,1)S(1)} %pad_maximum_fusion.1), channel_id=1, source_target_pairs={{0,1},{1,0},{2,3},{3,2},{4,5},{5,4},{6,7},{7,6},{8,9},{9,8},{10,11... | collective-permute-start | bytes 835592 | tf_op jit(solution)/shard_map/ppermute | solution.py:13
  52.3 20.9 %copy-start.1 = (f32[128,2048]{1,0:T(8,128)S(1)}, f32[128,2048]{1,0:T(8,128)}, u32[]{:S(2)}) copy-start(f32[128,2048]{1,0:T(8,128)} %param.9) | copy-start | bytes 3145732
  52.4 20.9 %copy-start.2 = (f32[128,2048]{1,0:T(8,128)S(1)}, f32[128,2048]{1,0:T(8,128)}, u32[]{:S(2)}) copy-start(f32[128,2048]{1,0:T(8,128)} %param.10) | copy-start | bytes 3145732
  52.4 20.9 %copy-start.3 = (f32[128,2048]{1,0:T(8,128)S(1)}, f32[128,2048]{1,0:T(8,128)}, u32[]{:S(2)}) copy-start(f32[128,2048]{1,0:T(8,128)} %param.11) | copy-start | bytes 3145732
  58.9 7.5 %collective-permute-start.6 = (f16[64,2048]{1,0:T(8,128)(2,1)S(1)}, f16[64,2048]{1,0:T(8,128)(2,1)S(1)}, u32[]{:S(2)}, u32[]{:S(2)}) collective-permute-start(f16[64,2048]{1,0:T(8,128)(2,1)S(1)} %fusion.21), channel_id=1, source_target_pairs={{0,1},{1,0},{2,3},{3,2},{4,5},{5,4},{6,7},{7,6},{8,9},{9,8},{10,11... | collective-permute-start | bytes 786440 | tf_op jit(solution)/shard_map/ppermute | solution.py:13
  59.5 7.8 %collective-permute-start.8 = (f16[2,32,2048]{2,1,0:T(8,128)(2,1)S(1)}, f16[2,32,2048]{2,1,0:T(8,128)(2,1)S(1)}, u32[]{:S(2)}, u32[]{:S(2)}) collective-permute-start(f16[2,32,2048]{2,1,0:T(8,128)(2,1)S(1)} %fusion.33), channel_id=1, source_target_pairs={{0,2},{1,3},{2,0},{3,1},{4,6},{5,7},{6,4},{7,5},{8,10},{9,11},{10,... | collective-permute-start | bytes 786440 | tf_op jit(solution)/shard_map/ppermute | solution.py:13
  66.5 6.1 %collective-permute-start.7 = (f16[32,2048]{1,0:T(8,128)(2,1)S(1)}, f16[32,2048]{1,0:T(8,128)(2,1)S(1)}, u32[]{:S(2)}, u32[]{:S(2)}) collective-permute-start(f16[32,2048]{1,0:T(8,128)(2,1)S(1)} %fusion.38), channel_id=1, source_target_pairs={{0,2},{1,3},{2,0},{3,1},{4,6},{5,7},{6,4},{7,5},{8,10},{9,11},{10,... | collective-permute-start | bytes 393224 | tf_op jit(solution)/shard_map/ppermute | solution.py:13
  67.5 5.2 %collective-permute-start.9 = (f16[32,2048]{1,0:T(8,128)(2,1)S(1)}, f16[32,2048]{1,0:T(8,128)(2,1)S(1)}, u32[]{:S(2)}, u32[]{:S(2)}) collective-permute-start(f16[32,2048]{1,0:T(8,128)(2,1)S(1)} %fusion.39), channel_id=1, source_target_pairs={{0,1},{1,0},{2,3},{3,2},{4,5},{5,4},{6,7},{7,6},{8,9},{9,8},{10,11... | collective-permute-start | bytes 393224 | tf_op jit(solution)/shard_map/ppermute | solution.py:13
  72.7 7.3 %collective-permute-start.10 = (f16[16,4096]{1,0:T(8,128)(2,1)S(1)}, f16[16,4096]{1,0:T(8,128)(2,1)S(1)}, u32[]{:S(2)}, u32[]{:S(2)}) collective-permute-start(f16[16,4096]{1,0:T(8,128)(2,1)S(1)} %fusion.35), channel_id=1, source_target_pairs={{0,4},{1,5},{2,6},{3,7},{4,0},{5,1},{6,2},{7,3},{8,12},{9,13},{10,... | collective-permute-start | bytes 393224 | tf_op jit(solution)/shard_map/ppermute | solution.py:13

commit v4 on v3

--- a/solution.py
+++ b/solution.py
@@ -1,12 +1,40 @@
 import jax
 import jax.numpy as jnp
 from jax import lax
+from jax.experimental import pallas as pl
+from jax.experimental.pallas import tpu as pltpu
 from jax.sharding import PartitionSpec as P
 
 FRAG = 128
 REPLICAS = 4
 AXIS = "vocab"
 SEND = jnp.float16
+
+
+def resident(head):
+    cuts = 4
+    block = head.shape[0] // cuts
+
+    def kernel(source, target, sems):
+        copies = []
+        for i in range(cuts):
+            part = pl.ds(i * block, block)
+            copies.append(pltpu.make_async_copy(source.at[part], target.at[part], sems.at[i]))
+        for copy in copies:
+            copy.start()
+        for copy in copies:
+            copy.wait()
+
+    size = head.size * head.dtype.itemsize
+    return pl.pallas_call(
+        kernel,
+        out_shape=pltpu.VMEM(head.shape, head.dtype),
+        in_specs=[pl.BlockSpec(memory_space=pltpu.HBM)],
+        out_specs=pl.BlockSpec(memory_space=pltpu.VMEM),
+        scratch_shapes=[pltpu.SemaphoreType.DMA((cuts,))],
+        compiler_params=pltpu.CompilerParams(vmem_limit_bytes=size + 2**20),
+        cost_estimate=pl.CostEstimate(flops=0, bytes_accessed=size, transcendentals=0),
+    )(head)
 
 
 def swap(value, step):
@@ -105,12 +133,14 @@
     digits = digits[:, :2].astype(jnp.int32)
     ids_all = digits[:, 0] * 256 + digits[:, 1]
 
-    logits = jnp.dot(left, head[:half], preferred_element_type=jnp.float32)
-    logits = logits + jnp.dot(right, head[half:], preferred_element_type=jnp.float32)
+    near = resident(head)
+    logits = jnp.dot(left, near[:half], preferred_element_type=jnp.float32)
+    logits = logits + jnp.dot(right, near[half:], preferred_element_type=jnp.float32)
     columns = lax.axis_index(AXIS) * width + jnp.arange(width, dtype=jnp.int32)
     hit = columns[None, :] == ids_all[:, None]
     local_max = jnp.max(logits, axis=1)
-    local_sum = jnp.sum(jnp.exp(logits - local_max[:, None]), axis=1)
+    raised = jnp.exp(logits - local_max[:, None])
+    local_sum = jnp.sum(raised, axis=1)
     local_pick = jnp.sum(jnp.where(hit, logits, 0.0), axis=1)
 
     stats = to_device_order(jnp.stack([local_max, local_sum, local_pick]), own)
@@ -123,16 +153,23 @@
     loss = jnp.mean(top + jnp.log(total) - picked).reshape((1,))
     top, total = to_xor_order(jnp.stack([top, total]), own)
 
+    both = jnp.concatenate([jnp.where(hit, 0.0, raised), hit.astype(jnp.float32)]).astype(jnp.bfloat16)
+    both = lax.optimization_barrier(both)
+
+    soft = jnp.exp(local_max - top) / (total * rows)
+    hard = ((jnp.exp(local_pick - top) / total - 1.0) / rows).astype(jnp.bfloat16).astype(jnp.float32)
+
+    def grad(part):
+        terms = lax.dot_general(
+            both, part, (((1,), (1,)), ((), ())), preferred_element_type=jnp.float32
+        )
+        terms = lax.optimization_barrier(terms)
+        return soft[:, None] * terms[:rows] + hard[:, None] * terms[rows:]
+
+    hidden_grad = scatter_sums(grad(near[:half]), grad(near[half:]), 2.0**14 * rows).astype(jnp.bfloat16)
+
     onehot = hit.astype(jnp.float32)
     dlogits = ((jnp.exp(logits - top[:, None]) / total[:, None] - onehot) / rows).astype(jnp.bfloat16)
-
-    def grad(part):
-        return lax.dot_general(
-            dlogits, part, (((1,), (1,)), ((), ())), preferred_element_type=jnp.float32
-        )
-
-    hidden_grad = scatter_sums(grad(head[:half]), grad(head[half:]), 2.0**14 * rows).astype(jnp.bfloat16)
-
     frag_grad = lax.dot_general(
         left[:, :FRAG], dlogits, (((0,), (0,)), ((), ())), preferred_element_type=jnp.float32
     )

time: 82.2 us -> 85.4 us (1.039)
  waiting for transfers between devices: 31.3 us -> 15.4 us
  starting transfers between devices: 9.19 us -> 24 us
  local copies, waits for them, and re-layouts: 1.95 us -> 14.1 us
  blocking collectives: 11.6 us -> 0 us
  other arithmetic: 3.16 us -> 5.59 us
  Pallas kernels: 0 us -> 1.16 us
    ppermute x11, waiting for transfers between devices: 31.3 us -> 15.4 us  [swap(): lax.ppermute(value, AXIS, [(i, i ^ step) for i in range(lax.axis_size(AXI...]
    all_to_all x1 -> x0, blocking collectives: 11.6 us -> none  [body(): lax.all_to_all(jnp.broadcast_to(stats[None], (members,) + stats.shape), A...]
    unnamed x11 -> x19, local copies, waits for them, and re-layouts: 0.98 us -> 12.5 us
    ppermute x11, starting transfers between devices: 9.19 us -> 19 us  [swap(): lax.ppermute(value, AXIS, [(i, i ^ step) for i in range(lax.axis_size(AXI...]
    all_to_all x0 -> x1, starting transfers between devices: none -> 4.99 us  [body(): lax.all_to_all(jnp.broadcast_to(stats[None], (members,) + stats.shape), A...]
    add x0 -> x1, other arithmetic: none -> 2.14 us  [grad(): return soft[:, None] * terms[:rows] + hard[:, None] * terms[rows:]]
    pallas_call x0 -> x1, Pallas kernels: none -> 1.16 us  [resident(): pl.pallas_call(kernel, out_shape=pltpu.VMEM(head.shape, head.dtype), in_s...]
  transfers between devices with their start and end apart: 11 -> 12, of which waited for: 9 -> 8; matrix products, arithmetic and copies ran while one was open for 12% -> 28% of each run, Pallas kernels for 0% -> 1%
where the time goes in v4:
time: 85.4 us; the launch traced here: 85 us
  starting transfers between devices  24 us (28%)
  matrix products  22.1 us (26%)
  waiting for transfers between devices  15.4 us (18%)
  local copies, waits for them, and re-layouts  14.1 us (17%)
  other arithmetic  5.59 us (7%)
  between operations  2.77 us (3%)
  Pallas kernels  1.16 us (1%)
    ppermute x11, starting transfers between devices, swap(): lax.ppermute(value, AXIS, [(i, i ^ step) for i in range(lax.axis_size(AXI...  19 us
    ppermute x11, waiting for transfers between devices, swap(): lax.ppermute(value, AXIS, [(i, i ^ step) for i in range(lax.axis_size(AXI...  15.4 us
    dot_general x2, matrix products, grad(): lax.dot_general(both, part, (((1,), (1,)), ((), ())), preferred_element_t...  12.8 us
    unnamed x19, local copies, waits for them, and re-layouts  12.5 us
    all_to_all x1, starting transfers between devices, body(): lax.all_to_all(jnp.broadcast_to(stats[None], (members,) + stats.shape), A...  4.99 us
    dot_general x1, matrix products, body(): jnp.dot(right, near[half:], preferred_element_type=jnp.float32)  4.63 us
    dot_general x1, matrix products, body(): lax.dot_general(left[:, :FRAG], dlogits, (((0,), (0,)), ((), ())), prefer...  3.23 us
    add x1, other arithmetic, grad(): return soft[:, None] * terms[:rows] + hard[:, None] * terms[rows:]  2.14 us
  transfers between devices with their start and end apart: 12, of which 8 were waited for; matrix products, arithmetic and copies ran while one was open for 28% of the time, Pallas kernels for 1%

profile of v4, /device:TPU:0, one launch (start us, length us, event | category | flops | bytes accessed | tf_op | source)
XLA Modules:
  0.0 85.0 jit_solution(11397656466347953404)
XLA Ops:
  0.6 4.1 %collective-permute-start = (bf16[16,4096]{1,0:T(8,128)(2,1)}, bf16[16,4096]{1,0:T(8,128)(2,1)S(1)}, u32[]{:S(2)}, u32[]{:S(2)}) collective-permute-start(bf16[16,4096]{1,0:T(8,128)(2,1)} %param.6), channel_id=1, source_target_pairs={{0,4},{1,5},{2,6},{3,7},{4,0},{5,1},{6,2},{7,3},{8,12},{9,13},{10,... | collective-permute-start | bytes 393224 | tf_op jit(solution)/shard_map/ppermute | solution.py:41
  6.5 5.8 %copy-done = bf16[4096,2048]{1,0:T(8,128)(2,1)S(1)} copy-done((bf16[4096,2048]{1,0:T(8,128)(2,1)S(1)}, bf16[4096,2048]{1,0:T(8,128)(2,1)}, u32[]{:S(2)}) %copy-start) | copy-done | bytes 16777240
  12.3 1.2 %shard_map.93 = bf16[4096,2048]{1,0:T(8,128)(2,1)S(1)} custom-call(bf16[4096,2048]{1,0:T(8,128)(2,1)S(1)} %copy-done), custom_call_target="tpu_custom_call" | custom-call | bytes 16777216 | tf_op jit(solution)/shard_map/pallas_call | solution.py:29
  13.5 5.7 %copy-done.1 = bf16[4096,2048]{1,0:T(8,128)(2,1)} copy-done((bf16[4096,2048]{1,0:T(8,128)(2,1)}, bf16[4096,2048]{1,0:T(8,128)(2,1)S(1)}, u32[]{:S(2)}) %copy-start.1) | copy-done | bytes 16777240
  19.3 1.9 %collective-permute-start.4 = (bf16[32,2048]{1,0:T(8,128)(2,1)S(1)}, bf16[32,2048]{1,0:T(8,128)(2,1)S(1)}, u32[]{:S(2)}, u32[]{:S(2)}) collective-permute-start(bf16[32,2048]{1,0:T(8,128)(2,1)S(1)} %get-tuple-element.10), channel_id=1, source_target_pairs={{0,1},{1,0},{2,3},{3,2},{4,5},{5,4},{6,7},{7,6},{8,9},{9,8},{10,11... | collective-permute-start | bytes 393224 | tf_op jit(solution)/shard_map/ppermute | solution.py:41
  21.2 1.6 %collective-permute-start.2 = (bf16[32,2176]{1,0:T(8,128)(2,1)S(1)}, bf16[32,2176]{1,0:T(8,128)(2,1)S(1)}, u32[]{:S(2)}, u32[]{:S(2)}) collective-permute-start(bf16[32,2176]{1,0:T(8,128)(2,1)S(1)} %maximum_maximum_fusion), channel_id=1, source_target_pairs={{0,2},{1,3},{2,0},{3,1},{4,6},{5,7},{6,4},{7,5},{8,10},{9,11},{10,... | collective-permute-start | bytes 417800 | tf_op jit(solution)/shard_map/ppermute | solution.py:41
  22.9 1.5 %collective-permute-done.4 = bf16[32,2048]{1,0:T(8,128)(2,1)S(1)} collective-permute-done((bf16[32,2048]{1,0:T(8,128)(2,1)S(1)}, bf16[32,2048]{1,0:T(8,128)(2,1)S(1)}, u32[]{:S(2)}, u32[]{:S(2)}) %collective-permute-start.4) | collective-permute-done | bytes 131104 | tf_op jit(solution)/shard_map/ppermute | solution.py:41
  24.4 2.0 %collective-permute-start.5 = (bf16[64,2048]{1,0:T(8,128)(2,1)S(1)}, bf16[64,2048]{1,0:T(8,128)(2,1)S(1)}, u32[]{:S(2)}, u32[]{:S(2)}) collective-permute-start(bf16[64,2048]{1,0:T(8,128)(2,1)S(1)} %pad_maximum_fusion.4), channel_id=1, source_target_pairs={{0,2},{1,3},{2,0},{3,1},{4,6},{5,7},{6,4},{7,5},{8,10},{9,11},{10,... | collective-permute-start | bytes 786440 | tf_op jit(solution)/shard_map/ppermute | solution.py:41
  26.3 1.0 %collective-permute-done.2 = bf16[32,2176]{1,0:T(8,128)(2,1)S(1)} collective-permute-done((bf16[32,2176]{1,0:T(8,128)(2,1)S(1)}, bf16[32,2176]{1,0:T(8,128)(2,1)S(1)}, u32[]{:S(2)}, u32[]{:S(2)}) %collective-permute-start.2) | collective-permute-done | bytes 139296 | tf_op jit(solution)/shard_map/ppermute | solution.py:41
  27.9 4.0 %collective-permute-done.5 = bf16[64,2048]{1,0:T(8,128)(2,1)S(1)} collective-permute-done((bf16[64,2048]{1,0:T(8,128)(2,1)S(1)}, bf16[64,2048]{1,0:T(8,128)(2,1)S(1)}, u32[]{:S(2)}, u32[]{:S(2)}) %collective-permute-start.5) | collective-permute-done | bytes 262176 | tf_op jit(solution)/shard_map/ppermute | solution.py:41
  32.0 4.6 %fusion.2 = f32[128,2048]{1,0:T(8,128)S(1)} fusion(bf16[4096,2048]{1,0:T(8,128)(2,1)} %copy-done.1, bf16[32,2048]{1,0:T(8,128)(2,1)S(1)} %get-tuple-element.12, bf16[32,2048]{1,0:T(8,128)(2,1)S(1)} %collective-permute-done.4, bf16[32,2048]{1,0:T(8,128)(2,1)S(1)} %get-tuple-element.11, bf16[32,2048]{1,0:T(8,128)(2,1)S(1)} %get-tuple-element.10), kind=kOutput, calls=%fused_computation.2 | convolution fusion | flops 1075838976 | bytes 9961472 | tf_op jit(solution)/shard_map/dot_general | solution.py:138
  36.7 1.4 %fusion.73 = (f32[128]{0:T(128)S(1)}, f32[128,2048]{1,0:T(8,128)S(1)}) fusion(f32[128,2048]{1,0:T(8,128)S(1)} %fusion.2, bf16[4096,2048]{1,0:T(8,128)(2,1)S(1)} %copy-done.2, bf16[128,2176]{1,0:T(8,128)(2,1)S(1)} %pad_maximum_fusion.1), kind=kOutput, calls=%fused_computation.125 | convolution fusion | flops 1074265984 | bytes 11010560 | tf_op jit(solution)/shard_map/dot_general | solution.py:137
  40.0 5.0 %all-to-all-start = ((f32[8,3,128]{2,1,0:T(4,128)}), f32[8,3,128]{2,1,0:T(4,128)S(1)}, u32[]{:S(2)}, u32[]{:S(2)}) async-start(f32[8,3,128]{2,1,0:T(4,128)} %broadcast_in_dim.12), calls=%async_computation | async-start | bytes 32768 | tf_op jit(solution)/shard_map/all_to_all | solution.py:147
  45.1 5.7 %fusion = f32[256,2048]{1,0:T(8,128)S(1)} fusion(bf16[256,2048]{1,0:T(8,128)(2,1)S(1)} %pad_maximum_fusion, bf16[4096,2048]{1,0:T(8,128)(2,1)} %copy-done.1), kind=kOutput, calls=%fused_computation | convolution fusion | flops 2147483648 | bytes 11534336 | tf_op jit(solution)/shard_map/dot_general | solution.py:163
  50.8 7.1 %fusion.4 = f32[256,2048]{1,0:T(8,128)} fusion(bf16[256,2048]{1,0:T(8,128)(2,1)S(1)} %pad_maximum_fusion, bf16[4096,2048]{1,0:T(8,128)(2,1)} %copy-done.1), kind=kOutput, calls=%fused_computation.4 | convolution fusion | flops 2147483648 | bytes 11534336 | tf_op jit(solution)/shard_map/dot_general | solution.py:163
  58.5 2.1 %fusion.20 = (f32[128,2048]{1,0:T(8,128)S(1)}, f32[128,2048]{1,0:T(8,128)S(1)}) fusion(f32[256,2048]{1,0:T(8,128)S(1)} %fusion, f32[128]{0:T(128)S(1)} %get-tuple-element.21, f32[128]{0:T(128)S(1)} %get-tuple-element.20, f32[256,2048]{1,0:T(8,128)} %fusion.4), kind=kLoop, calls=%fused_computation.23 | loop fusion | flops 1572864 | bytes 6292480 | tf_op jit(solution)/shard_map/add | solution.py:167
  60.7 2.1 %collective-permute-start.6 = (f16[64,2048]{1,0:T(8,128)(2,1)S(1)}, f16[64,2048]{1,0:T(8,128)(2,1)S(1)}, u32[]{:S(2)}, u32[]{:S(2)}) collective-permute-start(f16[64,2048]{1,0:T(8,128)(2,1)S(1)} %fusion.27), channel_id=1, source_target_pairs={{0,1},{1,0},{2,3},{3,2},{4,5},{5,4},{6,7},{7,6},{8,9},{9,8},{10,11... | collective-permute-start | bytes 786440 | tf_op jit(solution)/shard_map/ppermute | solution.py:41
  62.8 1.5 %collective-permute-start.8 = (f16[2,32,2048]{2,1,0:T(8,128)(2,1)S(1)}, f16[2,32,2048]{2,1,0:T(8,128)(2,1)S(1)}, u32[]{:S(2)}, u32[]{:S(2)}) collective-permute-start(f16[2,32,2048]{2,1,0:T(8,128)(2,1)S(1)} %fusion.44), channel_id=1, source_target_pairs={{0,2},{1,3},{2,0},{3,1},{4,6},{5,7},{6,4},{7,5},{8,10},{9,11},{10,... | collective-permute-start | bytes 786440 | tf_op jit(solution)/shard_map/ppermute | solution.py:41
  64.4 2.8 %collective-permute-done.6 = f16[64,2048]{1,0:T(8,128)(2,1)S(1)} collective-permute-done((f16[64,2048]{1,0:T(8,128)(2,1)S(1)}, f16[64,2048]{1,0:T(8,128)(2,1)S(1)}, u32[]{:S(2)}, u32[]{:S(2)}) %collective-permute-start.6) | collective-permute-done | bytes 262176 | tf_op jit(solution)/shard_map/ppermute | solution.py:41
  67.2 2.1 %collective-permute-start.7 = (f16[32,2048]{1,0:T(8,128)(2,1)S(1)}, f16[32,2048]{1,0:T(8,128)(2,1)S(1)}, u32[]{:S(2)}, u32[]{:S(2)}) collective-permute-start(f16[32,2048]{1,0:T(8,128)(2,1)S(1)} %fusion.49), channel_id=1, source_target_pairs={{0,2},{1,3},{2,0},{3,1},{4,6},{5,7},{6,4},{7,5},{8,10},{9,11},{10,... | collective-permute-start | bytes 393224 | tf_op jit(solution)/shard_map/ppermute | solution.py:41
  69.3 1.3 %collective-permute-done.8 = f16[2,32,2048]{2,1,0:T(8,128)(2,1)S(1)} collective-permute-done((f16[2,32,2048]{2,1,0:T(8,128)(2,1)S(1)}, f16[2,32,2048]{2,1,0:T(8,128)(2,1)S(1)}, u32[]{:S(2)}, u32[]{:S(2)}) %collective-permute-start.8) | collective-permute-done | bytes 262176 | tf_op jit(solution)/shard_map/ppermute | solution.py:41
  72.3 3.5 %collective-permute-done.9 = f16[32,2048]{1,0:T(8,128)(2,1)S(1)} collective-permute-done((f16[32,2048]{1,0:T(8,128)(2,1)S(1)}, f16[32,2048]{1,0:T(8,128)(2,1)S(1)}, u32[]{:S(2)}, u32[]{:S(2)}) %collective-permute-start.9) | collective-permute-done | bytes 131104 | tf_op jit(solution)/shard_map/ppermute | solution.py:41
  75.9 2.4 %collective-permute-start.10 = (f16[16,4096]{1,0:T(8,128)(2,1)S(1)}, f16[16,4096]{1,0:T(8,128)(2,1)S(1)}, u32[]{:S(2)}, u32[]{:S(2)}) collective-permute-start(f16[16,4096]{1,0:T(8,128)(2,1)S(1)} %fusion.46), channel_id=1, source_target_pairs={{0,4},{1,5},{2,6},{3,7},{4,0},{5,1},{6,2},{7,3},{8,12},{9,13},{10,... | collective-permute-start | bytes 393224 | tf_op jit(solution)/shard_map/ppermute | solution.py:41
  78.3 3.2 %multiply_subtract_fusion = (f32[128,2048]{1,0:T(8,128)}, f32[128,2048]{1,0:T(8,128)}) fusion(f32[128,2048]{1,0:T(8,128)S(1)} %copy-done.5, f32[128,2048]{1,0:T(8,128)S(1)} %copy-done.6, f32[128,2048]{1,0:T(8,128)S(1)} %copy-done.7, f32[128,2048]{1,0:T(8,128)S(1)} %copy-done.4, f32[128]{0:T(128)S(1)} %unstack.15, f32[128]{0:T(128)S(1)} %unstack.13, ...), kind=kOutput, calls=%fused_computation.29 | convolution fusion | flops 71991296 | bytes 7382528 | tf_op jit(solution)/shard_map/dot_general | solution.py:173
  (82 shorter events, 8.6 us)
Async XLA Ops:
  0.6 18.6 %collective-permute-start = (bf16[16,4096]{1,0:T(8,128)(2,1)}, bf16[16,4096]{1,0:T(8,128)(2,1)S(1)}, u32[]{:S(2)}, u32[]{:S(2)}) collective-permute-start(bf16[16,4096]{1,0:T(8,128)(2,1)} %param.6), channel_id=1, source_target_pairs={{0,4},{1,5},{2,6},{3,7},{4,0},{5,1},{6,2},{7,3},{8,12},{9,13},{10,... | collective-permute-start | bytes 393224 | tf_op jit(solution)/shard_map/ppermute | solution.py:41
  5.4 13.8 %collective-permute-start.1 = (bf16[16,128]{0,1:T(8,128)(2,1)S(1)}, bf16[16,128]{0,1:T(8,128)(2,1)S(1)}, u32[]{:S(2)}, u32[]{:S(2)}) collective-permute-start(bf16[16,128]{0,1:T(8,128)(2,1)S(1)} %fusion.54), channel_id=1, source_target_pairs={{0,4},{1,5},{2,6},{3,7},{4,0},{5,1},{6,2},{7,3},{8,12},{9,13},{10,... | collective-permute-start | bytes 12296 | tf_op jit(solution)/shard_map/ppermute | solution.py:41
  6.5 5.8 %copy-start = (bf16[4096,2048]{1,0:T(8,128)(2,1)S(1)}, bf16[4096,2048]{1,0:T(8,128)(2,1)}, u32[]{:S(2)}) copy-start(bf16[4096,2048]{1,0:T(8,128)(2,1)} %source.1) | copy-start | bytes 50331652
  13.4 5.7 %copy-start.1 = (bf16[4096,2048]{1,0:T(8,128)(2,1)}, bf16[4096,2048]{1,0:T(8,128)(2,1)S(1)}, u32[]{:S(2)}) copy-start(bf16[4096,2048]{1,0:T(8,128)(2,1)S(1)} %shard_map.93) | copy-start | bytes 50331652
  19.3 17.4 %copy-start.2 = (bf16[4096,2048]{1,0:T(8,128)(2,1)S(1)}, bf16[4096,2048]{1,0:T(8,128)(2,1)}, u32[]{:S(2)}) copy-start(bf16[4096,2048]{1,0:T(8,128)(2,1)} %copy-done.1) | copy-start | bytes 50331652
  19.3 5.0 %collective-permute-start.4 = (bf16[32,2048]{1,0:T(8,128)(2,1)S(1)}, bf16[32,2048]{1,0:T(8,128)(2,1)S(1)}, u32[]{:S(2)}, u32[]{:S(2)}) collective-permute-start(bf16[32,2048]{1,0:T(8,128)(2,1)S(1)} %get-tuple-element.10), channel_id=1, source_target_pairs={{0,1},{1,0},{2,3},{3,2},{4,5},{5,4},{6,7},{7,6},{8,9},{9,8},{10,11... | collective-permute-start | bytes 393224 | tf_op jit(solution)/shard_map/ppermute | solution.py:41
  21.2 6.1 %collective-permute-start.2 = (bf16[32,2176]{1,0:T(8,128)(2,1)S(1)}, bf16[32,2176]{1,0:T(8,128)(2,1)S(1)}, u32[]{:S(2)}, u32[]{:S(2)}) collective-permute-start(bf16[32,2176]{1,0:T(8,128)(2,1)S(1)} %maximum_maximum_fusion), channel_id=1, source_target_pairs={{0,2},{1,3},{2,0},{3,1},{4,6},{5,7},{6,4},{7,5},{8,10},{9,11},{10,... | collective-permute-start | bytes 417800 | tf_op jit(solution)/shard_map/ppermute | solution.py:41
  24.4 7.6 %collective-permute-start.5 = (bf16[64,2048]{1,0:T(8,128)(2,1)S(1)}, bf16[64,2048]{1,0:T(8,128)(2,1)S(1)}, u32[]{:S(2)}, u32[]{:S(2)}) collective-permute-start(bf16[64,2048]{1,0:T(8,128)(2,1)S(1)} %pad_maximum_fusion.4), channel_id=1, source_target_pairs={{0,2},{1,3},{2,0},{3,1},{4,6},{5,7},{6,4},{7,5},{8,10},{9,11},{10,... | collective-permute-start | bytes 786440 | tf_op jit(solution)/shard_map/ppermute | solution.py:41
  27.4 9.3 %collective-permute-start.3 = (bf16[64,2176]{1,0:T(8,128)(2,1)S(1)}, bf16[64,2176]{1,0:T(8,128)(2,1)S(1)}, u32[]{:S(2)}, u32[]{:S(2)}) collective-permute-start(bf16[64,2176]{1,0:T(8,128)(2,1)S(1)} %pad_maximum_fusion.2), channel_id=1, source_target_pairs={{0,1},{1,0},{2,3},{3,2},{4,5},{5,4},{6,7},{7,6},{8,9},{9,8},{10,11... | collective-permute-start | bytes 835592 | tf_op jit(solution)/shard_map/ppermute | solution.py:41
  38.1 6.9 %copy-start.3 = (f32[128,2048]{1,0:T(8,128)}, f32[128,2048]{1,0:T(8,128)S(1)}, u32[]{:S(2)}) copy-start(f32[128,2048]{1,0:T(8,128)S(1)} %get-tuple-element.25) | copy-start | bytes 3145732
  40.0 17.9 %all-to-all-start = ((f32[8,3,128]{2,1,0:T(4,128)}), f32[8,3,128]{2,1,0:T(4,128)S(1)}, u32[]{:S(2)}, u32[]{:S(2)}) async-start(f32[8,3,128]{2,1,0:T(4,128)} %broadcast_in_dim.12), calls=%async_computation | async-start | bytes 32768 | tf_op jit(solution)/shard_map/all_to_all | solution.py:147
  58.4 19.9 %copy-start.4 = (f32[128,2048]{1,0:T(8,128)S(1)}, f32[128,2048]{1,0:T(8,128)}, u32[]{:S(2)}) copy-start(f32[128,2048]{1,0:T(8,128)} %copy-done.3) | copy-start | bytes 3145732
  58.4 19.9 %copy-start.5 = (f32[128,2048]{1,0:T(8,128)S(1)}, f32[128,2048]{1,0:T(8,128)}, u32[]{:S(2)}) copy-start(f32[128,2048]{1,0:T(8,128)} %param.9) | copy-start | bytes 3145732
  58.5 19.9 %copy-start.6 = (f32[128,2048]{1,0:T(8,128)S(1)}, f32[128,2048]{1,0:T(8,128)}, u32[]{:S(2)}) copy-start(f32[128,2048]{1,0:T(8,128)} %param.10) | copy-start | bytes 3145732
  58.5 19.9 %copy-start.7 = (f32[128,2048]{1,0:T(8,128)S(1)}, f32[128,2048]{1,0:T(8,128)}, u32[]{:S(2)}) copy-start(f32[128,2048]{1,0:T(8,128)} %param.11) | copy-start | bytes 3145732
  60.7 6.4 %collective-permute-start.6 = (f16[64,2048]{1,0:T(8,128)(2,1)S(1)}, f16[64,2048]{1,0:T(8,128)(2,1)S(1)}, u32[]{:S(2)}, u32[]{:S(2)}) collective-permute-start(f16[64,2048]{1,0:T(8,128)(2,1)S(1)} %fusion.27), channel_id=1, source_target_pairs={{0,1},{1,0},{2,3},{3,2},{4,5},{5,4},{6,7},{7,6},{8,9},{9,8},{10,11... | collective-permute-start | bytes 786440 | tf_op jit(solution)/shard_map/ppermute | solution.py:41
  62.8 7.8 %collective-permute-start.8 = (f16[2,32,2048]{2,1,0:T(8,128)(2,1)S(1)}, f16[2,32,2048]{2,1,0:T(8,128)(2,1)S(1)}, u32[]{:S(2)}, u32[]{:S(2)}) collective-permute-start(f16[2,32,2048]{2,1,0:T(8,128)(2,1)S(1)} %fusion.44), channel_id=1, source_target_pairs={{0,2},{1,3},{2,0},{3,1},{4,6},{5,7},{6,4},{7,5},{8,10},{9,11},{10,... | collective-permute-start | bytes 786440 | tf_op jit(solution)/shard_map/ppermute | solution.py:41
  67.2 5.0 %collective-permute-start.7 = (f16[32,2048]{1,0:T(8,128)(2,1)S(1)}, f16[32,2048]{1,0:T(8,128)(2,1)S(1)}, u32[]{:S(2)}, u32[]{:S(2)}) collective-permute-start(f16[32,2048]{1,0:T(8,128)(2,1)S(1)} %fusion.49), channel_id=1, source_target_pairs={{0,2},{1,3},{2,0},{3,1},{4,6},{5,7},{6,4},{7,5},{8,10},{9,11},{10,... | collective-permute-start | bytes 393224 | tf_op jit(solution)/shard_map/ppermute | solution.py:41
  70.8 5.0 %collective-permute-start.9 = (f16[32,2048]{1,0:T(8,128)(2,1)S(1)}, f16[32,2048]{1,0:T(8,128)(2,1)S(1)}, u32[]{:S(2)}, u32[]{:S(2)}) collective-permute-start(f16[32,2048]{1,0:T(8,128)(2,1)S(1)} %fusion.50), channel_id=1, source_target_pairs={{0,1},{1,0},{2,3},{3,2},{4,5},{5,4},{6,7},{7,6},{8,9},{9,8},{10,11... | collective-permute-start | bytes 393224 | tf_op jit(solution)/shard_map/ppermute | solution.py:41
  75.9 7.3 %collective-permute-start.10 = (f16[16,4096]{1,0:T(8,128)(2,1)S(1)}, f16[16,4096]{1,0:T(8,128)(2,1)S(1)}, u32[]{:S(2)}, u32[]{:S(2)}) collective-permute-start(f16[16,4096]{1,0:T(8,128)(2,1)S(1)} %fusion.46), channel_id=1, source_target_pairs={{0,4},{1,5},{2,6},{3,7},{4,0},{5,1},{6,2},{7,3},{8,12},{9,13},{10,... | collective-permute-start | bytes 393224 | tf_op jit(solution)/shard_map/ppermute | solution.py:41

commit v5 on v3

v5 whole, which is shorter than its diff:
```python
import functools

import jax
import jax.numpy as jnp
from jax import lax
from jax.experimental import pallas as pl
from jax.experimental.pallas import tpu as pltpu
from jax.sharding import PartitionSpec as P

FRAG = 128
REPLICAS = 4
AXIS = "vocab"
SEND = jnp.float16
LANES = 128
VMEM = pl.BlockSpec(memory_space=pltpu.VMEM)


def call(kernel, outs, operands, flops=0, scratch=(), sources=None, vmem=16 * 2**20):
    outs = [pltpu.VMEM(shape, dtype) for shape, dtype in outs]
    places = sources or [pltpu.VMEM] * len(operands)
    moved = sum(x.size * x.dtype.itemsize for x in operands)
    return pl.pallas_call(
        kernel,
        out_shape=outs,
        in_specs=[pl.BlockSpec(memory_space=place) for place in places],
        out_specs=[VMEM] * len(outs),
        scratch_shapes=list(scratch),
        compiler_params=pltpu.CompilerParams(vmem_limit_bytes=vmem),
        cost_estimate=pl.CostEstimate(flops=flops, bytes_accessed=moved, transcendentals=0),
    )(*[pltpu.with_memory_space_constraint(x, place) for x, place in zip(operands, places)])


def load_kernel(source, target, sems):
    block = source.shape[0] // sems.shape[0]
    copies = []
    for i in range(sems.shape[0]):
        part = pl.ds(i * block, block)
        copies.append(pltpu.make_async_copy(source.at[part], target.at[part], sems.at[i]))
    for copy in copies:
        copy.start()
    for copy in copies:
        copy.wait()


def resident(head):
    return call(
        load_kernel, [(head.shape, head.dtype)], [head],
        scratch=[pltpu.SemaphoreType.DMA((4,))], sources=[pltpu.HBM],
    )[0]


TILE = 512


def first_kernel(rows_ref, near_ref, out_ref):
    depth = rows_ref.shape[1]

    @pl.loop(0, out_ref.shape[1] // TILE)
    def _(i):
        part = pl.ds(pl.multiple_of(i * TILE, TILE), TILE)
        out_ref[:, part] = jnp.dot(
            rows_ref[...], near_ref[:depth, part], preferred_element_type=jnp.float32
        )


def xor_blocks(value, own):
    me = lax.axis_index(AXIS)
    lane = lax.broadcasted_iota(jnp.int32, value.shape, 1)
    size = value.shape[1]
    group, bit = size // 2, 1
    while group >= own:
        up, down = pltpu.roll(value, group, 1), pltpu.roll(value, size - group, 1)
        swapped = jnp.where((lane & group) != 0, up, down)
        value = jnp.where((me & bit) != 0, swapped, value)
        group, bit = group // 2, bit * 2
    return value


def second_kernel(own, rows_ref, before_ref, digits_ref, near_ref,
                  logits_ref, both_ref, mine_ref, shared_ref, columns_ref):
    rows, depth = rows_ref.shape
    width = logits_ref.shape[1]
    first = near_ref.shape[0] - depth

    @pl.loop(0, width // TILE)
    def _(i):
        part = pl.ds(pl.multiple_of(i * TILE, TILE), TILE)
        logits_ref[:, part] = before_ref[:, part] + jnp.dot(
            rows_ref[...], near_ref[first:, part], preferred_element_type=jnp.float32
        )

    chunk = 32
    offset = lax.axis_index(AXIS) * width

    @pl.loop(0, rows // chunk)
    def _(i):
        part = pl.ds(pl.multiple_of(i * chunk, chunk), chunk)
        logits = logits_ref[part, :]
        digits = digits_ref[part, :].astype(jnp.float32)
        ids = (digits[:, 0:1] * 256.0 + digits[:, 1:2]).astype(jnp.int32) - offset
        hit = lax.broadcasted_iota(jnp.int32, logits.shape, 1) == ids
        top = jnp.max(logits, axis=1, keepdims=True)
        raised = jnp.exp(logits - top)
        total = jnp.sum(raised, axis=1, keepdims=True)
        pick = jnp.sum(jnp.where(hit, logits, 0.0), axis=1, keepdims=True)
        both_ref[part, :] = jnp.where(hit, 0.0, raised).astype(jnp.bfloat16)
        other = pl.ds(pl.multiple_of(rows + i * chunk, chunk), chunk)
        both_ref[other, :] = jnp.where(hit, 1.0, 0.0).astype(jnp.bfloat16)
        place = lax.broadcasted_iota(jnp.int32, (chunk, LANES), 1)
        columns_ref[part, :] = jnp.where(place == 0, top, jnp.where(place == 1, total, pick))

    mine = columns_ref[...].T[:8]
    mine_ref[...] = mine
    shared_ref[...] = xor_blocks(mine, own)


def grad_kernel(both_ref, near_ref, terms_ref):
    tile = 1024

    @pl.loop(0, near_ref.shape[0] // tile)
    def _(i):
        part = pl.ds(pl.multiple_of(i * tile, tile), tile)
        turned = lax.dot_general(
            near_ref[part, :], both_ref[...], (((1,), (1,)), ((), ())),
            preferred_element_type=jnp.float32,
        )
        terms_ref[:, part] = turned.T


def join_kernel(own, scale, seen_ref, mine_ref, terms_ref,
                left_send_ref, right_send_ref, left_ref, right_ref, lines_ref, loss_ref):
    rows = mine_ref.shape[1]
    half = terms_ref.shape[1] // 2
    seen = seen_ref[...]
    top = jnp.max(seen[:, 0], axis=0, keepdims=True)
    total = jnp.sum(seen[:, 1] * jnp.exp(seen[:, 0] - top), axis=0, keepdims=True)
    picked = jnp.sum(seen[:, 2], axis=0, keepdims=True)
    loss = jnp.sum(top + jnp.log(total) - picked, axis=1, keepdims=True) / rows
    loss_ref[...] = jnp.broadcast_to(loss, loss_ref.shape)

    place = lax.broadcasted_iota(jnp.int32, (8, rows), 0)
    lines = xor_blocks(jnp.where(place == 0, top, total), own)
    lines_ref[...] = lines
    top, total = lines[0:1], lines[1:2]
    soft = jnp.exp(mine_ref[0:1, :] - top) / (total * rows)
    hard = (jnp.exp(mine_ref[2:3, :] - top) / total - 1.0) / rows
    hard = hard.astype(jnp.bfloat16).astype(jnp.float32)
    soft = jnp.broadcast_to(soft, (LANES, rows)).T[:, 0:1]
    hard = jnp.broadcast_to(hard, (LANES, rows)).T[:, 0:1]

    def joined(first, count, columns):
        part, other = pl.ds(first, count), pl.ds(rows + first, count)
        return (
            soft[first : first + count] * terms_ref[part, columns]
            + hard[first : first + count] * terms_ref[other, columns]
        )

    quarter = rows // 4
    for cut in range(4):
        first = cut * quarter
        value = joined(first, quarter, pl.ds(0, half))
        if cut >= 2:
            left_send_ref[pl.ds(first - 2 * quarter, quarter), :] = value * scale
        else:
            left_ref[pl.ds(first, quarter), :] = value
        value = joined(first, quarter, pl.ds(half, half))
        slot = pl.ds((cut // 2) * quarter, quarter)
        if cut % 2:
            right_send_ref[slot, :] = value * scale
        else:
            right_ref[slot, :] = value


def swap(value, step):
    return lax.ppermute(value, AXIS, [(i, i ^ step) for i in range(lax.axis_size(AXIS))])


def doubled(value, step):
    return jnp.concatenate([value, swap(value, step)], axis=0)


def far_steps():
    step = lax.axis_size(AXIS) // 2
    steps = []
    while step > 2:
        steps.append(step)
        step //= 2
    return steps


def gather_rows(hidden, digits):
    half = hidden.shape[1] // 2
    for step in far_steps():
        hidden, digits = doubled(hidden, step), doubled(digits, step)
    left = jnp.concatenate([hidden[:, :half], digits], axis=1)
    right = hidden[:, half:]
    near = right.shape[0]
    left = doubled(left, 2)
    right = doubled(right, 1)
    left = doubled(left, 1)
    other = swap(right, 2)
    right = jnp.concatenate([right[:near], other[:near], right[near:], other[near:]], axis=0)
    return left[:, :half], right, left[:, half:]


def scatter_sums(left_send, right_send, left, right, scale):
    quarter = left.shape[0] // 2

    def code(value):
        return (value * scale).astype(SEND)

    def decode(value):
        return value.astype(jnp.float32) * (1.0 / scale)

    left = left + decode(swap(left_send.astype(SEND), 1))
    right = right + decode(swap(right_send.astype(SEND), 2))
    left = left[:quarter] + decode(swap(code(left[quarter:]), 2))
    right = right[:quarter] + decode(swap(code(right[quarter:]), 1))
    both = jnp.concatenate([left, right], axis=1)
    for step in far_steps()[::-1]:
        keep = both.shape[0] // 2
        both = both[:keep] + decode(swap(code(both[keep:]), step))
    return both


def body(hidden, targets, head, global_frag, momentum, peer_delta):
    members = lax.axis_size(AXIS)
    own, depth = hidden.shape
    half = depth // 2
    rows = own * members
    width = head.shape[1]

    digits = jnp.stack([targets // 256, targets % 256], axis=1).astype(jnp.bfloat16)
    digits = jnp.pad(digits, ((0, 0), (0, 126)))
    left, right, digits = gather_rows(hidden, digits)

    near = resident(head)
    work = 2 * rows * half * width
    logits = call(first_kernel, [((rows, width), jnp.float32)], [left, near], work)[0]
    logits, both, mine, shared = call(
        functools.partial(second_kernel, own),
        [((rows, width), jnp.float32), ((2 * rows, width), jnp.bfloat16),
         ((8, rows), jnp.float32), ((8, rows), jnp.float32)],
        [right, logits, digits, near], work,
        scratch=[pltpu.VMEM((rows, LANES), jnp.float32)],
    )

    seen = lax.all_to_all(
        jnp.broadcast_to(shared[None], (members,) + shared.shape), AXIS, split_axis=0, concat_axis=0
    )

    terms = call(grad_kernel, [((2 * rows, depth), jnp.float32)], [both, near], 8 * work)[0]

    scale = 2.0**14 * rows
    cut = (rows // 2, half)
    left_send, right_send, left_keep, right_keep, lines, loss = call(
        functools.partial(join_kernel, own, scale),
        [(cut, jnp.float32)] * 4
        + [((8, rows), jnp.float32), ((8, LANES), jnp.float32)],
        [seen, mine, terms],
    )
    hidden_grad = scatter_sums(left_send, right_send, left_keep, right_keep, scale).astype(jnp.bfloat16)
    loss = loss[0, :1]

    top, total = lines[0], lines[1]
    digits = digits[:, :2].astype(jnp.int32)
    ids_all = digits[:, 0] * 256 + digits[:, 1]
    columns = lax.axis_index(AXIS) * width + jnp.arange(width, dtype=jnp.int32)
    onehot = (columns[None, :] == ids_all[:, None]).astype(jnp.float32)
    dlogits = ((jnp.exp(logits - top[:, None]) / total[:, None] - onehot) / rows).astype(jnp.bfloat16)
    frag_grad = lax.dot_general(
        left[:, :FRAG], dlogits, (((0,), (0,)), ((), ())), preferred_element_type=jnp.float32
    )
    local_frag = head[:FRAG].astype(jnp.float32) - 1.0 * frag_grad
    pseudo = (global_frag - local_frag + peer_delta) / REPLICAS
    new_momentum = 0.9 * momentum + pseudo
    new_global = global_frag - 0.7 * (pseudo + 0.9 * new_momentum)
    return (loss, hidden_grad, new_global, new_momentum)


def solution(mesh):
    in_specs = (
        P(("outer", "vocab"), None),
        P(("outer", "vocab")),
        P("outer", "vocab"),
        P(None, "vocab"),
        P(None, "vocab"),
        P("outer", "vocab"),
    )
    out_specs = (P("outer"), P(("outer", "vocab"), None), P("outer", "vocab"), P("outer", "vocab"))
    return jax.shard_map(body, mesh=mesh, in_specs=in_specs, out_specs=out_specs, check_vma=False)
```

time: 82.2 us -> 88.4 us (1.075)
  matrix products: 22 us -> 3.17 us
  Pallas kernels: 0 us -> 17.2 us
  local copies, waits for them, and re-layouts: 1.95 us -> 17.9 us
  blocking collectives: 11.6 us -> 0 us
  starting transfers between devices: 9.19 us -> 18.7 us
  waiting for transfers between devices: 31.3 us -> 28.2 us
  between operations: 2.75 us -> 0.84 us
  other arithmetic: 3.16 us -> 2.06 us
    dot_general x4 -> x0, matrix products: 18.8 us -> none  [the longest x2 12.8 us: grad(): lax.dot_general(dlogits, part, (((1,), (1,)), ((), ())), preferred_elemen...]
    pallas_call x0 -> x5, Pallas kernels: none -> 17.2 us  [call(): pl.pallas_call(kernel, out_shape=outs, in_specs=[pl.BlockSpec(memory_spac...]
    unnamed x11 -> x15, local copies, waits for them, and re-layouts: 0.98 us -> 16.6 us
    all_to_all x1 -> x0, blocking collectives: 11.6 us -> none  [body(): lax.all_to_all(jnp.broadcast_to(stats[None], (members,) + stats.shape), A...]
    ppermute x11, waiting for transfers between devices: 31.3 us -> 21.5 us  [swap(): lax.ppermute(value, AXIS, [(i, i ^ step) for i in range(lax.axis_size(AXI...]
    all_to_all x0 -> x1, waiting for transfers between devices: none -> 6.67 us  [body(): lax.all_to_all(jnp.broadcast_to(shared[None], (members,) + shared.shape),...]
    all_to_all x0 -> x1, starting transfers between devices: none -> 4.89 us  [body(): lax.all_to_all(jnp.broadcast_to(shared[None], (members,) + shared.shape),...]
    ppermute x11, starting transfers between devices: 9.19 us -> 13.8 us  [swap(): lax.ppermute(value, AXIS, [(i, i ^ step) for i in range(lax.axis_size(AXI...]
  transfers between devices with their start and end apart: 11 -> 12, of which waited for: 9 -> 9; matrix products, arithmetic and copies ran while one was open for 12% -> 6% of each run, Pallas kernels for 0% -> 7%
where the time goes in v5:
time: 88.4 us; the launch traced here: 88 us
  waiting for transfers between devices  28.2 us (32%)
  starting transfers between devices  18.7 us (21%)
  local copies, waits for them, and re-layouts  17.9 us (20%)
  Pallas kernels  17.2 us (19%)
  matrix products  3.17 us (4%)
  other arithmetic  2.06 us (2%)
    ppermute x11, waiting for transfers between devices, swap(): lax.ppermute(value, AXIS, [(i, i ^ step) for i in range(lax.axis_size(AXI...  21.5 us
    pallas_call x5, Pallas kernels, call(): pl.pallas_call(kernel, out_shape=outs, in_specs=[pl.BlockSpec(memory_spac...  17.2 us
    unnamed x15, local copies, waits for them, and re-layouts  16.6 us
    ppermute x11, starting transfers between devices, swap(): lax.ppermute(value, AXIS, [(i, i ^ step) for i in range(lax.axis_size(AXI...  13.8 us
    all_to_all x1, waiting for transfers between devices, body(): lax.all_to_all(jnp.broadcast_to(shared[None], (members,) + shared.shape),...  6.67 us
    all_to_all x1, starting transfers between devices, body(): lax.all_to_all(jnp.broadcast_to(shared[None], (members,) + shared.shape),...  4.89 us
    dot_general x1, matrix products, body(): lax.dot_general(left[:, :FRAG], dlogits, (((0,), (0,)), ((), ())), prefer...  3.17 us
  transfers between devices with their start and end apart: 12, of which 9 were waited for; matrix products, arithmetic and copies ran while one was open for 6% of the time, Pallas kernels for 7%

profile of v5, /device:TPU:0, one launch (start us, length us, event | category | flops | bytes accessed | tf_op | source)
XLA Modules:
  0.0 88.0 jit_solution(9828412755924034803)
XLA Ops:
  1.4 4.0 %collective-permute-start.3 = (bf16[16,128]{1,0:T(8,128)(2,1)S(1)}, bf16[16,128]{1,0:T(8,128)(2,1)S(1)}, u32[]{:S(2)}, u32[]{:S(2)}) collective-permute-start(bf16[16,128]{1,0:T(8,128)(2,1)S(1)} %pad.4), channel_id=1, source_target_pairs={{0,4},{1,5},{2,6},{3,7},{4,0},{5,1},{6,2},{7,3},{8,12},{9,13},{10,... | collective-permute-start | bytes 12296 | tf_op jit(solution)/shard_map/ppermute | solution.py:175
  5.5 0.9 %constant_dynamic-update-slice_fusion.1 = bf16[32,4096]{1,0:T(8,128)(2,1)S(1)} fusion(bf16[16,4096]{1,0:T(8,128)(2,1)} %param.6), kind=kLoop, calls=%fused_computation.49 | loop fusion | bytes 262144
  6.5 5.9 %shard_map.93.near_ref = bf16[4096,2048]{1,0:T(8,128)(2,1)S(1)} custom-call(bf16[4096,2048]{1,0:T(8,128)(2,1)} %source.1), custom_call_target="tpu_custom_call" | custom-call | bytes 16777216 | tf_op jit(solution)/shard_map/pallas_call | solution.py:22
  12.4 5.7 %copy-done = bf16[4096,2048]{1,0:T(8,128)(2,1)} copy-done((bf16[4096,2048]{1,0:T(8,128)(2,1)}, bf16[4096,2048]{1,0:T(8,128)(2,1)S(1)}, u32[]{:S(2)}) %copy-start) | copy-done | bytes 16777240
  18.2 1.8 %collective-permute-start.1 = (bf16[32,2048]{1,0:T(8,128)(2,1)S(1)}, bf16[32,2048]{1,0:T(8,128)(2,1)S(1)}, u32[]{:S(2)}, u32[]{:S(2)}) collective-permute-start(bf16[32,2048]{1,0:T(8,128)(2,1)S(1)} %get-tuple-element.27), channel_id=1, source_target_pairs={{0,1},{1,0},{2,3},{3,2},{4,5},{5,4},{6,7},{7,6},{8,9},{9,8},{10,11... | collective-permute-start | bytes 393224 | tf_op jit(solution)/shard_map/ppermute | solution.py:175
  20.0 1.6 %collective-permute-start.4 = (bf16[32,2176]{1,0:T(8,128)(2,1)S(1)}, bf16[32,2176]{1,0:T(8,128)(2,1)S(1)}, u32[]{:S(2)}, u32[]{:S(2)}) collective-permute-start(bf16[32,2176]{1,0:T(8,128)(2,1)S(1)} %maximum_maximum_fusion), channel_id=1, source_target_pairs={{0,2},{1,3},{2,0},{3,1},{4,6},{5,7},{6,4},{7,5},{8,10},{9,11},{10,... | collective-permute-start | bytes 417800 | tf_op jit(solution)/shard_map/ppermute | solution.py:175
  21.7 1.5 %collective-permute-done.1 = bf16[32,2048]{1,0:T(8,128)(2,1)S(1)} collective-permute-done((bf16[32,2048]{1,0:T(8,128)(2,1)S(1)}, bf16[32,2048]{1,0:T(8,128)(2,1)S(1)}, u32[]{:S(2)}, u32[]{:S(2)}) %collective-permute-start.1) | collective-permute-done | bytes 131104 | tf_op jit(solution)/shard_map/ppermute | solution.py:175
  23.2 1.9 %collective-permute-start.2 = (bf16[64,2048]{1,0:T(8,128)(2,1)S(1)}, bf16[64,2048]{1,0:T(8,128)(2,1)S(1)}, u32[]{:S(2)}, u32[]{:S(2)}) collective-permute-start(bf16[64,2048]{1,0:T(8,128)(2,1)S(1)} %pad_maximum_fusion.4), channel_id=1, source_target_pairs={{0,2},{1,3},{2,0},{3,1},{4,6},{5,7},{6,4},{7,5},{8,10},{9,11},{10,... | collective-permute-start | bytes 786440 | tf_op jit(solution)/shard_map/ppermute | solution.py:175
  25.1 0.9 %collective-permute-done.4 = bf16[32,2176]{1,0:T(8,128)(2,1)S(1)} collective-permute-done((bf16[32,2176]{1,0:T(8,128)(2,1)S(1)}, bf16[32,2176]{1,0:T(8,128)(2,1)S(1)}, u32[]{:S(2)}, u32[]{:S(2)}) %collective-permute-start.4) | collective-permute-done | bytes 139296 | tf_op jit(solution)/shard_map/ppermute | solution.py:175
  26.7 4.0 %collective-permute-done.2 = bf16[64,2048]{1,0:T(8,128)(2,1)S(1)} collective-permute-done((bf16[64,2048]{1,0:T(8,128)(2,1)S(1)}, bf16[64,2048]{1,0:T(8,128)(2,1)S(1)}, u32[]{:S(2)}, u32[]{:S(2)}) %collective-permute-start.2) | collective-permute-done | bytes 262176 | tf_op jit(solution)/shard_map/ppermute | solution.py:175
  30.8 1.9 %collective-permute-done.5 = bf16[64,2176]{1,0:T(8,128)(2,1)S(1)} collective-permute-done((bf16[64,2176]{1,0:T(8,128)(2,1)S(1)}, bf16[64,2176]{1,0:T(8,128)(2,1)S(1)}, u32[]{:S(2)}, u32[]{:S(2)}) %collective-permute-start.5) | collective-permute-done | bytes 278560 | tf_op jit(solution)/shard_map/ppermute | solution.py:175
  32.8 5.8 %copy-done.1 = bf16[4096,2048]{1,0:T(8,128)(2,1)S(1)} copy-done((bf16[4096,2048]{1,0:T(8,128)(2,1)S(1)}, bf16[4096,2048]{1,0:T(8,128)(2,1)}, u32[]{:S(2)}) %copy-start.1) | copy-done | bytes 16777240
  38.6 1.9 %shard_map.94.before_ref = f32[128,2048]{1,0:T(8,128)S(1)} custom-call(bf16[128,2048]{1,0:T(8,128)(2,1)S(1)} %slice.86.rows_ref, bf16[4096,2048]{1,0:T(8,128)(2,1)S(1)} %copy-done.1), custom_call_target="tpu_custom_call" | custom-call | flops 1073741824 | bytes 17301504 | tf_op jit(solution)/shard_map/pallas_call | solution.py:22
  40.5 3.3 %shard_map.95 = (f32[128,2048]{1,0:T(8,128)S(1)}, bf16[256,2048]{1,0:T(8,128)(2,1)S(1)}, f32[8,128]{1,0:T(8,128)S(1)}, f32[8,128]{1,0:T(8,128)S(1)}) custom-call(bf16[128,2048]{1,0:T(8,128)(2,1)S(1)} %pad_maximum_fusion.1.rows_ref, f32[128,2048]{1,0:T(8,128)S(1)} %shard_map.94.before_ref, bf16[128,128]{1,0:T(8,128)(2,1)S(1)} %pad_maximum_fusion.5.digits_ref, ...), custom_call_target="tpu_custom_call" | custom-call | flops 1073741824 | bytes 18382848 | tf_op jit(solution)/shard_map/pallas_call | solution.py:22
  43.7 5.5 %shard_map.96.terms_ref = f32[256,4096]{1,0:T(8,128)S(1)} custom-call(bf16[256,2048]{1,0:T(8,128)(2,1)S(1)} %get-tuple-element.16.both_ref, bf16[4096,2048]{1,0:T(8,128)(2,1)S(1)} %copy-done.1), custom_call_target="tpu_custom_call" | custom-call | flops 8589934592 | bytes 17825792 | tf_op jit(solution)/shard_map/pallas_call | solution.py:22
  49.2 1.9 %copy-done.2 = f32[256,4096]{1,0:T(8,128)} copy-done((f32[256,4096]{1,0:T(8,128)}, f32[256,4096]{1,0:T(8,128)S(1)}, u32[]{:S(2)}) %copy-start.2) | copy-done | bytes 4194328
  51.8 4.9 %all-to-all-start = ((f32[8,8,128]{2,1,0:T(8,128)}), f32[8,8,128]{2,1,0:T(8,128)S(1)}, u32[]{:S(2)}, u32[]{:S(2)}) async-start(f32[8,8,128]{2,1,0:T(8,128)} %broadcast_in_dim.2), calls=%async_computation | async-start | bytes 65536 | tf_op jit(solution)/shard_map/all_to_all | solution.py:248
  56.7 6.7 %all-to-all-done.seen_ref = f32[8,8,128]{2,1,0:T(8,128)S(1)} async-done(((f32[8,8,128]{2,1,0:T(8,128)}), f32[8,8,128]{2,1,0:T(8,128)S(1)}, u32[]{:S(2)}, u32[]{:S(2)}) %all-to-all-start) | async-done | bytes 32800 | tf_op jit(solution)/shard_map/all_to_all | solution.py:248
  63.3 2.2 %copy-done.3 = f32[256,4096]{1,0:T(8,128)S(1)} copy-done((f32[256,4096]{1,0:T(8,128)S(1)}, f32[256,4096]{1,0:T(8,128)}, u32[]{:S(2)}) %copy-start.3) | copy-done | bytes 4194328
  67.8 6.1 %collective-permute-done.8 = f16[64,2048]{1,0:T(8,128)(2,1)S(1)} collective-permute-done((f16[64,2048]{1,0:T(8,128)(2,1)S(1)}, f16[64,2048]{1,0:T(8,128)(2,1)S(1)}, u32[]{:S(2)}, u32[]{:S(2)}) %collective-permute-start.8) | collective-permute-done | bytes 262176 | tf_op jit(solution)/shard_map/ppermute | solution.py:175
  75.7 3.4 %collective-permute-done.9 = f16[32,2048]{1,0:T(8,128)(2,1)S(1)} collective-permute-done((f16[32,2048]{1,0:T(8,128)(2,1)S(1)}, f16[32,2048]{1,0:T(8,128)(2,1)S(1)}, u32[]{:S(2)}, u32[]{:S(2)}) %collective-permute-start.9) | collective-permute-done | bytes 131104 | tf_op jit(solution)/shard_map/ppermute | solution.py:175
  79.1 0.9 collective-permute-done.7
  80.8 3.2 %multiply_subtract_fusion = (f32[128,2048]{1,0:T(8,128)}, f32[128,2048]{1,0:T(8,128)}) fusion(f32[128,2048]{1,0:T(8,128)S(1)} %copy-done.4, f32[128,2048]{1,0:T(8,128)S(1)} %copy-done.5, f32[128,2048]{1,0:T(8,128)S(1)} %copy-done.6, f32[128,2048]{1,0:T(8,128)S(1)} %get-tuple-element.22, s32[2048]{0:T(1024)S(1)} %iota_add_fusion, ...), kind=kOutput, calls=%fused_computation.4 | convolution fusion | flops 71991296 | bytes 7382528 | tf_op jit(solution)/shard_map/dot_general | solution.py:271
  84.5 2.8 %collective-permute-done.10 = f16[16,4096]{1,0:T(8,128)(2,1)S(1)} collective-permute-done((f16[16,4096]{1,0:T(8,128)(2,1)S(1)}, f16[16,4096]{1,0:T(8,128)(2,1)S(1)}, u32[]{:S(2)}, u32[]{:S(2)}) %collective-permute-start.10) | collective-permute-done | bytes 131104 | tf_op jit(solution)/shard_map/ppermute | solution.py:175
  (51 shorter events, 8.5 us)
Async XLA Ops:
  1.4 18.6 %collective-permute-start.3 = (bf16[16,128]{1,0:T(8,128)(2,1)S(1)}, bf16[16,128]{1,0:T(8,128)(2,1)S(1)}, u32[]{:S(2)}, u32[]{:S(2)}) collective-permute-start(bf16[16,128]{1,0:T(8,128)(2,1)S(1)} %pad.4), channel_id=1, source_target_pairs={{0,4},{1,5},{2,6},{3,7},{4,0},{5,1},{6,2},{7,3},{8,12},{9,13},{10,... | collective-permute-start | bytes 12296 | tf_op jit(solution)/shard_map/ppermute | solution.py:175
  5.5 12.7 %collective-permute-start = (bf16[16,4096]{1,0:T(8,128)(2,1)}, bf16[16,4096]{1,0:T(8,128)(2,1)S(1)}, u32[]{:S(2)}, u32[]{:S(2)}) collective-permute-start(bf16[16,4096]{1,0:T(8,128)(2,1)} %param.6), channel_id=1, source_target_pairs={{0,4},{1,5},{2,6},{3,7},{4,0},{5,1},{6,2},{7,3},{8,12},{9,13},{10,... | collective-permute-start | bytes 393224 | tf_op jit(solution)/shard_map/ppermute | solution.py:175
  12.4 5.7 %copy-start = (bf16[4096,2048]{1,0:T(8,128)(2,1)}, bf16[4096,2048]{1,0:T(8,128)(2,1)S(1)}, u32[]{:S(2)}) copy-start(bf16[4096,2048]{1,0:T(8,128)(2,1)S(1)} %shard_map.93.near_ref) | copy-start | bytes 50331652
  18.2 5.0 %collective-permute-start.1 = (bf16[32,2048]{1,0:T(8,128)(2,1)S(1)}, bf16[32,2048]{1,0:T(8,128)(2,1)S(1)}, u32[]{:S(2)}, u32[]{:S(2)}) collective-permute-start(bf16[32,2048]{1,0:T(8,128)(2,1)S(1)} %get-tuple-element.27), channel_id=1, source_target_pairs={{0,1},{1,0},{2,3},{3,2},{4,5},{5,4},{6,7},{7,6},{8,9},{9,8},{10,11... | collective-permute-start | bytes 393224 | tf_op jit(solution)/shard_map/ppermute | solution.py:175
  20.0 6.0 %collective-permute-start.4 = (bf16[32,2176]{1,0:T(8,128)(2,1)S(1)}, bf16[32,2176]{1,0:T(8,128)(2,1)S(1)}, u32[]{:S(2)}, u32[]{:S(2)}) collective-permute-start(bf16[32,2176]{1,0:T(8,128)(2,1)S(1)} %maximum_maximum_fusion), channel_id=1, source_target_pairs={{0,2},{1,3},{2,0},{3,1},{4,6},{5,7},{6,4},{7,5},{8,10},{9,11},{10,... | collective-permute-start | bytes 417800 | tf_op jit(solution)/shard_map/ppermute | solution.py:175
  23.2 7.5 %collective-permute-start.2 = (bf16[64,2048]{1,0:T(8,128)(2,1)S(1)}, bf16[64,2048]{1,0:T(8,128)(2,1)S(1)}, u32[]{:S(2)}, u32[]{:S(2)}) collective-permute-start(bf16[64,2048]{1,0:T(8,128)(2,1)S(1)} %pad_maximum_fusion.4), channel_id=1, source_target_pairs={{0,2},{1,3},{2,0},{3,1},{4,6},{5,7},{6,4},{7,5},{8,10},{9,11},{10,... | collective-permute-start | bytes 786440 | tf_op jit(solution)/shard_map/ppermute | solution.py:175
  26.1 6.6 %collective-permute-start.5 = (bf16[64,2176]{1,0:T(8,128)(2,1)S(1)}, bf16[64,2176]{1,0:T(8,128)(2,1)S(1)}, u32[]{:S(2)}, u32[]{:S(2)}) collective-permute-start(bf16[64,2176]{1,0:T(8,128)(2,1)S(1)} %pad_maximum_fusion.2), channel_id=1, source_target_pairs={{0,1},{1,0},{2,3},{3,2},{4,5},{5,4},{6,7},{7,6},{8,9},{9,8},{10,11... | collective-permute-start | bytes 835592 | tf_op jit(solution)/shard_map/ppermute | solution.py:175
  32.8 5.8 %copy-start.1 = (bf16[4096,2048]{1,0:T(8,128)(2,1)S(1)}, bf16[4096,2048]{1,0:T(8,128)(2,1)}, u32[]{:S(2)}) copy-start(bf16[4096,2048]{1,0:T(8,128)(2,1)} %copy-done) | copy-start | bytes 50331652
  49.2 1.9 %copy-start.2 = (f32[256,4096]{1,0:T(8,128)}, f32[256,4096]{1,0:T(8,128)S(1)}, u32[]{:S(2)}) copy-start(f32[256,4096]{1,0:T(8,128)S(1)} %shard_map.96.terms_ref) | copy-start | bytes 12582916
  51.8 11.6 %all-to-all-start = ((f32[8,8,128]{2,1,0:T(8,128)}), f32[8,8,128]{2,1,0:T(8,128)S(1)}, u32[]{:S(2)}, u32[]{:S(2)}) async-start(f32[8,8,128]{2,1,0:T(8,128)} %broadcast_in_dim.2), calls=%async_computation | async-start | bytes 65536 | tf_op jit(solution)/shard_map/all_to_all | solution.py:248
  63.3 2.2 %copy-start.3 = (f32[256,4096]{1,0:T(8,128)S(1)}, f32[256,4096]{1,0:T(8,128)}, u32[]{:S(2)}) copy-start(f32[256,4096]{1,0:T(8,128)} %copy-done.2) | copy-start | bytes 12582916
  66.3 7.6 %collective-permute-start.8 = (f16[64,2048]{1,0:T(8,128)(2,1)S(1)}, f16[64,2048]{1,0:T(8,128)(2,1)S(1)}, u32[]{:S(2)}, u32[]{:S(2)}) collective-permute-start(f16[64,2048]{1,0:T(8,128)(2,1)S(1)} %convert_element_type.52), channel_id=1, source_target_pairs={{0,2},{1,3},{2,0},{3,1},{4,6},{5,7},{6,4},{7,5},{8,10},{9,11},{10,... | collective-permute-start | bytes 786440 | tf_op jit(solution)/shard_map/ppermute | solution.py:175
  66.9 7.8 %collective-permute-start.6 = (f16[64,2048]{1,0:T(8,128)(2,1)S(1)}, f16[64,2048]{1,0:T(8,128)(2,1)S(1)}, u32[]{:S(2)}, u32[]{:S(2)}) collective-permute-start(f16[64,2048]{1,0:T(8,128)(2,1)S(1)} %convert_element_type.48), channel_id=1, source_target_pairs={{0,1},{1,0},{2,3},{3,2},{4,5},{5,4},{6,7},{7,6},{8,9},{9,8},{10,11... | collective-permute-start | bytes 786440 | tf_op jit(solution)/shard_map/ppermute | solution.py:175
  74.0 5.0 %collective-permute-start.9 = (f16[32,2048]{1,0:T(8,128)(2,1)S(1)}, f16[32,2048]{1,0:T(8,128)(2,1)S(1)}, u32[]{:S(2)}, u32[]{:S(2)}) collective-permute-start(f16[32,2048]{1,0:T(8,128)(2,1)S(1)} %fusion.13), channel_id=1, source_target_pairs={{0,1},{1,0},{2,3},{3,2},{4,5},{5,4},{6,7},{7,6},{8,9},{9,8},{10,11... | collective-permute-start | bytes 393224 | tf_op jit(solution)/shard_map/ppermute | solution.py:175
  74.8 6.1 %copy-start.6 = (f32[128,2048]{1,0:T(8,128)S(1)}, f32[128,2048]{1,0:T(8,128)}, u32[]{:S(2)}) copy-start(f32[128,2048]{1,0:T(8,128)} %param.11) | copy-start | bytes 3145732
  74.8 6.0 %copy-start.4 = (f32[128,2048]{1,0:T(8,128)S(1)}, f32[128,2048]{1,0:T(8,128)}, u32[]{:S(2)}) copy-start(f32[128,2048]{1,0:T(8,128)} %param.9) | copy-start | bytes 3145732
  74.8 6.0 %copy-start.5 = (f32[128,2048]{1,0:T(8,128)S(1)}, f32[128,2048]{1,0:T(8,128)}, u32[]{:S(2)}) copy-start(f32[128,2048]{1,0:T(8,128)} %param.10) | copy-start | bytes 3145732
  74.9 5.0 %collective-permute-start.7 = (f16[32,2048]{1,0:T(8,128)(2,1)S(1)}, f16[32,2048]{1,0:T(8,128)(2,1)S(1)}, u32[]{:S(2)}, u32[]{:S(2)}) collective-permute-start(f16[32,2048]{1,0:T(8,128)(2,1)S(1)} %fusion.14), channel_id=1, source_target_pairs={{0,2},{1,3},{2,0},{3,1},{4,6},{5,7},{6,4},{7,5},{8,10},{9,11},{10,... | collective-permute-start | bytes 393224 | tf_op jit(solution)/shard_map/ppermute | solution.py:175
  80.0 7.3 %collective-permute-start.10 = (f16[16,4096]{1,0:T(8,128)(2,1)S(1)}, f16[16,4096]{1,0:T(8,128)(2,1)S(1)}, u32[]{:S(2)}, u32[]{:S(2)}) collective-permute-start(f16[16,4096]{1,0:T(8,128)(2,1)S(1)} %fusion.12), channel_id=1, source_target_pairs={{0,4},{1,5},{2,6},{3,7},{4,0},{5,1},{6,2},{7,3},{8,12},{9,13},{10,... | collective-permute-start | bytes 393224 | tf_op jit(solution)/shard_map/ppermute | solution.py:175

commit v6 on v5

v6 whole, which is shorter than its diff:
```python
import functools

import jax
import jax.numpy as jnp
from jax import lax
from jax.experimental import pallas as pl
from jax.experimental.pallas import tpu as pltpu
from jax.sharding import PartitionSpec as P

FRAG = 128
REPLICAS = 4
AXIS = "vocab"
SEND = jnp.float16
LANES = 128
VMEM = pl.BlockSpec(memory_space=pltpu.VMEM)


def call(kernel, outs, operands, flops=0, scratch=(), sources=None, vmem=16 * 2**20):
    outs = [pltpu.VMEM(shape, dtype) for shape, dtype in outs]
    places = sources or [pltpu.VMEM] * len(operands)
    moved = sum(x.size * x.dtype.itemsize for x in operands)
    return pl.pallas_call(
        kernel,
        out_shape=outs,
        in_specs=[pl.BlockSpec(memory_space=place) for place in places],
        out_specs=[VMEM] * len(outs),
        scratch_shapes=list(scratch),
        compiler_params=pltpu.CompilerParams(vmem_limit_bytes=vmem),
        cost_estimate=pl.CostEstimate(flops=flops, bytes_accessed=moved, transcendentals=0),
    )(*[pltpu.with_memory_space_constraint(x, place) for x, place in zip(operands, places)])


def load_kernel(source, target, sems):
    block = source.shape[0] // sems.shape[0]
    copies = []
    for i in range(sems.shape[0]):
        part = pl.ds(i * block, block)
        copies.append(pltpu.make_async_copy(source.at[part], target.at[part], sems.at[i]))
    for copy in copies:
        copy.start()
    for copy in copies:
        copy.wait()


def resident(head):
    return call(
        load_kernel, [(head.shape, head.dtype)], [head],
        scratch=[pltpu.SemaphoreType.DMA((4,))], sources=[pltpu.HBM],
    )[0]


TILE = 512


def first_kernel(rows_ref, near_ref, out_ref):
    depth = rows_ref.shape[1]

    @pl.loop(0, out_ref.shape[1] // TILE)
    def _(i):
        part = pl.ds(pl.multiple_of(i * TILE, TILE), TILE)
        out_ref[:, part] = jnp.dot(
            rows_ref[...], near_ref[:depth, part], preferred_element_type=jnp.float32
        )


def ids_of(digits):
    digits = digits.astype(jnp.float32)
    return (digits[:, 0:1] * 256.0 + digits[:, 1:2]).astype(jnp.int32)


def block_group(step, size):
    return size // (2 * step)


def swap_blocks(value, group):
    size = value.shape[1]
    lane = lax.broadcasted_iota(jnp.int32, value.shape, 1)
    up, down = pltpu.roll(value, group, 1), pltpu.roll(value, size - group, 1)
    return jnp.where((lane & group) != 0, up, down)


def shared_order(value, members):
    me = lax.axis_index(AXIS)
    step = 1
    while step < members:
        swapped = swap_blocks(value, block_group(step, value.shape[1]))
        value = jnp.where((me & step) != 0, swapped, value)
        step *= 2
    return value


def as_columns(line):
    return jnp.broadcast_to(line, (LANES, line.shape[1])).T[:, 0:1]


def second_kernel(rows_ref, before_ref, near_ref, logits_ref, both_ref, mine_ref, columns_ref):
    rows = rows_ref.shape[0]
    depth = rows_ref.shape[1] - LANES
    width = logits_ref.shape[1]
    first = near_ref.shape[0] - depth

    @pl.loop(0, width // TILE)
    def _(i):
        part = pl.ds(pl.multiple_of(i * TILE, TILE), TILE)
        logits_ref[:, part] = before_ref[:, part] + jnp.dot(
            rows_ref[:, :depth], near_ref[first:, part], preferred_element_type=jnp.float32
        )

    chunk = 32
    offset = lax.axis_index(AXIS) * width

    @pl.loop(0, rows // chunk)
    def _(i):
        part = pl.ds(pl.multiple_of(i * chunk, chunk), chunk)
        logits = logits_ref[part, :]
        ids = ids_of(rows_ref[part, depth:]) - offset
        hit = lax.broadcasted_iota(jnp.int32, logits.shape, 1) == ids
        top = jnp.max(logits, axis=1, keepdims=True)
        raised = jnp.exp(logits - top)
        total = jnp.sum(raised, axis=1, keepdims=True)
        pick = jnp.sum(jnp.where(hit, logits, 0.0), axis=1, keepdims=True)
        both_ref[part, :] = jnp.where(hit, 0.0, raised).astype(jnp.bfloat16)
        other = pl.ds(pl.multiple_of(rows + i * chunk, chunk), chunk)
        both_ref[other, :] = jnp.where(hit, 1.0, 0.0).astype(jnp.bfloat16)
        place = lax.broadcasted_iota(jnp.int32, (chunk, LANES), 1)
        columns_ref[part, :] = jnp.where(place == 0, top, jnp.where(place == 1, total, pick))

    mine_ref[...] = columns_ref[...].T[:8]


def merge_kernel(step, mine_ref, other_ref, out_ref):
    size = mine_ref.shape[1]
    mine, other = mine_ref[...], swap_blocks(other_ref[...], block_group(step, size))
    upper = (lax.axis_index(AXIS) & step) != 0
    one, two = jnp.where(upper, other, mine), jnp.where(upper, mine, other)
    top = jnp.maximum(one[0:1], two[0:1])
    total = one[1:2] * jnp.exp(one[0:1] - top) + two[1:2] * jnp.exp(two[0:1] - top)
    pick = one[2:3] + two[2:3]
    place = lax.broadcasted_iota(jnp.int32, mine.shape, 0)
    out_ref[...] = jnp.where(place == 0, top, jnp.where(place == 1, total, pick))


def grad_kernel(first, both_ref, near_ref, terms_ref):
    turned = lax.dot_general(
        near_ref[pl.ds(first, terms_ref.shape[1]), :], both_ref[...], (((1,), (1,)), ((), ())),
        preferred_element_type=jnp.float32,
    )
    terms_ref[...] = turned.T


def join_kernel(members, scale, lines_ref, mine_ref, *refs):
    *terms_refs, left_send_ref, right_send_ref, left_ref, right_ref, loss_ref = refs
    rows = mine_ref.shape[1]
    lines = lines_ref[...]
    same = shared_order(lines, members)
    loss = jnp.sum(same[0:1] + jnp.log(same[1:2]) - same[2:3], axis=1, keepdims=True) / rows
    loss_ref[...] = jnp.broadcast_to(loss, loss_ref.shape)

    top, total = lines[0:1], lines[1:2]
    soft = as_columns(jnp.exp(mine_ref[0:1, :] - top) / (total * rows))
    hard = (jnp.exp(mine_ref[2:3, :] - top) / total - 1.0) / rows
    hard = as_columns(hard.astype(jnp.bfloat16).astype(jnp.float32))

    quarter = rows // 4
    for place, terms_ref in enumerate(terms_refs):
        width = terms_ref.shape[1]
        in_left = place < len(terms_refs) // 2
        columns = pl.ds(place % (len(terms_refs) // 2) * width, width)
        for cut in range(4):
            first = cut * quarter
            value = (
                soft[first : first + quarter] * terms_ref[pl.ds(first, quarter), :]
                + hard[first : first + quarter] * terms_ref[pl.ds(rows + first, quarter), :]
            )
            near, far = (cut % 2, cut // 2) if in_left else (cut // 2, cut % 2)
            slot = pl.ds(near * quarter, quarter)
            if far:
                (left_send_ref if in_left else right_send_ref)[slot, columns] = value * scale
            else:
                (left_ref if in_left else right_ref)[slot, columns] = value


def frag_kernel(rows_ref, digits_ref, lines_ref, logits_ref, head_ref, global_ref, momentum_ref,
                peer_ref, new_global_ref, new_momentum_ref):
    rows, tile = logits_ref.shape
    top, total = as_columns(lines_ref[0:1, :]), as_columns(lines_ref[1:2, :])
    offset = (lax.axis_index(AXIS) * pl.num_programs(0) + pl.program_id(0)) * tile
    hit = lax.broadcasted_iota(jnp.int32, (rows, tile), 1) == ids_of(digits_ref[...]) - offset
    shares = jnp.exp(logits_ref[...] - top) / total
    dlogits = ((shares - jnp.where(hit, 1.0, 0.0)) / rows).astype(jnp.bfloat16)
    turned = rows_ref[...].astype(jnp.float32).T.astype(jnp.bfloat16)
    frag_grad = jnp.dot(turned, dlogits, preferred_element_type=jnp.float32)
    local_frag = head_ref[...].astype(jnp.float32) - 1.0 * frag_grad
    pseudo = (global_ref[...] - local_frag + peer_ref[...]) / REPLICAS
    new_momentum = 0.9 * momentum_ref[...] + pseudo
    new_momentum_ref[...] = new_momentum
    new_global_ref[...] = global_ref[...] - 0.7 * (pseudo + 0.9 * new_momentum)


def frag_update(left, right, lines, logits, near, global_frag, momentum, peer_delta):
    rows, width = logits.shape
    last = right.shape[1] // LANES - 1
    tile = pl.BlockSpec((FRAG, TILE), lambda i: (0, i))
    return pl.pallas_call(
        frag_kernel,
        grid=(width // TILE,),
        out_shape=[jax.ShapeDtypeStruct((FRAG, width), jnp.float32)] * 2,
        in_specs=[
            pl.BlockSpec((rows, FRAG), lambda i: (0, 0)),
            pl.BlockSpec((rows, LANES), lambda i: (0, last)),
            pl.BlockSpec((8, rows), lambda i: (0, 0)),
            pl.BlockSpec((rows, TILE), lambda i: (0, i)),
            tile, tile, tile, tile,
        ],
        out_specs=[tile, tile],
        compiler_params=pltpu.CompilerParams(vmem_limit_bytes=16 * 2**20),
        cost_estimate=pl.CostEstimate(
            flops=2 * rows * FRAG * width, bytes_accessed=24 * FRAG * width, transcendentals=0
        ),
    )(
        left, right, lines, pltpu.with_memory_space_constraint(logits, pltpu.VMEM),
        pltpu.with_memory_space_constraint(near, pltpu.VMEM), global_frag, momentum, peer_delta,
    )


def swap(value, step):
    return lax.ppermute(value, AXIS, [(i, i ^ step) for i in range(lax.axis_size(AXIS))])


def doubled(value, step):
    return jnp.concatenate([value, swap(value, step)], axis=0)


def far_steps():
    step = lax.axis_size(AXIS) // 2
    steps = []
    while step > 2:
        steps.append(step)
        step //= 2
    return steps


def gather_rows(hidden, digits):
    half = hidden.shape[1] // 2
    for step in far_steps():
        hidden, digits = doubled(hidden, step), doubled(digits, step)
    left = doubled(doubled(hidden[:, :half], 2), 1)
    right = doubled(jnp.concatenate([hidden[:, half:], digits], axis=1), 1)
    near = right.shape[0] // 2
    other = swap(right, 2)
    right = jnp.concatenate([right[:near], other[:near], right[near:], other[near:]], axis=0)
    return left, right


def scatter_sums(left_send, right_send, left, right, scale):
    quarter = left.shape[0] // 2

    def code(value):
        return (value * scale).astype(SEND)

    def decode(value):
        return value.astype(jnp.float32) * (1.0 / scale)

    left = left + decode(swap(left_send.astype(SEND), 1))
    right = right + decode(swap(right_send.astype(SEND), 2))
    left = left[:quarter] + decode(swap(code(left[quarter:]), 2))
    right = right[:quarter] + decode(swap(code(right[quarter:]), 1))
    both = jnp.concatenate([left, right], axis=1)
    for step in far_steps()[::-1]:
        keep = both.shape[0] // 2
        both = both[:keep] + decode(swap(code(both[keep:]), step))
    return both


def body(hidden, targets, head, global_frag, momentum, peer_delta):
    members = lax.axis_size(AXIS)
    own, depth = hidden.shape
    half = depth // 2
    rows = own * members
    width = head.shape[1]

    digits = jnp.stack([targets // 256, targets % 256], axis=1).astype(jnp.bfloat16)
    digits = jnp.pad(digits, ((0, 0), (0, 126)))
    left, right = gather_rows(hidden, digits)

    near = resident(head)
    work = 2 * rows * half * width
    logits = call(first_kernel, [((rows, width), jnp.float32)], [left, near], work)[0]
    logits, both, mine = call(
        second_kernel,
        [((rows, width), jnp.float32), ((2 * rows, width), jnp.bfloat16), ((8, rows), jnp.float32)],
        [right, logits, near], work,
        scratch=[pltpu.VMEM((rows, LANES), jnp.float32)],
    )

    lines = mine
    for step in far_steps() + [2, 1]:
        lines = call(
            functools.partial(merge_kernel, step), [((8, rows), jnp.float32)], [lines, swap(lines, step)]
        )[0]

    cuts = 4
    terms = [
        call(
            functools.partial(grad_kernel, i * depth // cuts),
            [((2 * rows, depth // cuts), jnp.float32)], [both, near], 8 * work // cuts,
        )[0]
        for i in range(cuts)
    ]

    scale = 2.0**14 * rows
    *parts, loss = call(
        functools.partial(join_kernel, members, scale),
        [((rows // 2, half), jnp.float32)] * 4 + [((8, LANES), jnp.float32)],
        [lines, mine] + terms,
    )
    hidden_grad = scatter_sums(*parts, scale).astype(jnp.bfloat16)
    new_global, new_momentum = frag_update(
        left, right, lines, logits, near, global_frag, momentum, peer_delta
    )
    return (loss[0, :1], hidden_grad, new_global, new_momentum)


def solution(mesh):
    in_specs = (
        P(("outer", "vocab"), None),
        P(("outer", "vocab")),
        P("outer", "vocab"),
        P(None, "vocab"),
        P(None, "vocab"),
        P("outer", "vocab"),
    )
    out_specs = (P("outer"), P(("outer", "vocab"), None), P("outer", "vocab"), P("outer", "vocab"))
    return jax.shard_map(body, mesh=mesh, in_specs=in_specs, out_specs=out_specs, check_vma=False)
```

time: 88.4 us -> 67.8 us (0.77)
  local copies, waits for them, and re-layouts: 17.9 us -> 1.63 us
  waiting for transfers between devices: 28.2 us -> 20.2 us
  starting transfers between devices: 18.7 us -> 22.5 us
  Pallas kernels: 17.2 us -> 20.5 us
  matrix products: 3.17 us -> 0 us
    unnamed x15 -> x7, local copies, waits for them, and re-layouts: 16.6 us -> 0.96 us
    ppermute x11 -> x14, starting transfers between devices: 13.8 us -> 22.5 us  [swap(): lax.ppermute(value, AXIS, [(i, i ^ step) for i in range(lax.axis_size(AXI...]
    all_to_all x1 -> x0, waiting for transfers between devices: 6.67 us -> none  [body(): lax.all_to_all(jnp.broadcast_to(shared[None], (members,) + shared.shape),...]
    all_to_all x1 -> x0, starting transfers between devices: 4.89 us -> none  [body(): lax.all_to_all(jnp.broadcast_to(shared[None], (members,) + shared.shape),...]
    pallas_call x0 -> x1, Pallas kernels: none -> 3.36 us  [frag_update(): pl.pallas_call(frag_kernel, grid=(width // TILE,), out_shape=[jax.ShapeDt...]
    dot_general x1 -> x0, matrix products: 3.17 us -> none  [body(): lax.dot_general(left[:, :FRAG], dlogits, (((0,), (0,)), ((), ())), prefer...]
    ppermute x11 -> x14, waiting for transfers between devices: 21.5 us -> 20.2 us  [swap(): lax.ppermute(value, AXIS, [(i, i ^ step) for i in range(lax.axis_size(AXI...]
    pallas_call x5 -> x11, Pallas kernels: 17.2 us -> 17.1 us  [call(): pl.pallas_call(kernel, out_shape=outs, in_specs=[pl.BlockSpec(memory_spac...]
  transfers between devices with their start and end apart: 12 -> 14, of which waited for: 9 -> 9; matrix products, arithmetic and copies ran while one was open for 6% -> 3% of each run, Pallas kernels for 7% -> 25%
where the time goes in v6:
time: 67.8 us; the launch traced here: 67.6 us
  starting transfers between devices  22.5 us (33%)
  Pallas kernels  20.5 us (30%)
  waiting for transfers between devices  20.2 us (30%)
  other arithmetic  1.86 us (3%)
  local copies, waits for them, and re-layouts  1.63 us (2%)
  between operations  0.84 us (1%)
    ppermute x14, starting transfers between devices, swap(): lax.ppermute(value, AXIS, [(i, i ^ step) for i in range(lax.axis_size(AXI...  22.5 us
    ppermute x14, waiting for transfers between devices, swap(): lax.ppermute(value, AXIS, [(i, i ^ step) for i in range(lax.axis_size(AXI...  20.2 us
    pallas_call x11, Pallas kernels, call(): pl.pallas_call(kernel, out_shape=outs, in_specs=[pl.BlockSpec(memory_spac...  17.1 us
    pallas_call x1, Pallas kernels, frag_update(): pl.pallas_call(frag_kernel, grid=(width // TILE,), out_shape=[jax.ShapeDt...  3.36 us
  transfers between devices with their start and end apart: 14, of which 9 were waited for; matrix products, arithmetic and copies ran while one was open for 3% of the time, Pallas kernels for 25%

profile of v6, /device:TPU:0, one launch (start us, length us, event | category | flops | bytes accessed | tf_op | source)
XLA Modules:
  0.0 67.6 jit_solution(13966879046062475453)
XLA Ops:
  1.4 4.0 %collective-permute-start.1 = (bf16[16,128]{1,0:T(8,128)(2,1)S(1)}, bf16[16,128]{1,0:T(8,128)(2,1)S(1)}, u32[]{:S(2)}, u32[]{:S(2)}) collective-permute-start(bf16[16,128]{1,0:T(8,128)(2,1)S(1)} %pad.4), channel_id=1, source_target_pairs={{0,4},{1,5},{2,6},{3,7},{4,0},{5,1},{6,2},{7,3},{8,12},{9,13},{10,... | collective-permute-start | bytes 12296 | tf_op jit(solution)/shard_map/ppermute | solution.py:227
  6.5 5.9 %shard_map.93.near_ref.head_ref = bf16[4096,2048]{1,0:T(8,128)(2,1)S(1)} custom-call(bf16[4096,2048]{1,0:T(8,128)(2,1)} %source.1), custom_call_target="tpu_custom_call" | custom-call | bytes 16777216 | tf_op jit(solution)/shard_map/pallas_call | solution.py:22
  12.4 1.9 %collective-permute-done = bf16[16,4096]{1,0:T(8,128)(2,1)S(1)} collective-permute-done((bf16[16,4096]{1,0:T(8,128)(2,1)}, bf16[16,4096]{1,0:T(8,128)(2,1)S(1)}, u32[]{:S(2)}, u32[]{:S(2)}) %collective-permute-start) | collective-permute-done | bytes 131104 | tf_op jit(solution)/shard_map/ppermute | solution.py:227
  14.5 1.6 %collective-permute-start.2 = (bf16[32,2176]{1,0:T(8,128)(2,1)S(1)}, bf16[32,2176]{1,0:T(8,128)(2,1)S(1)}, u32[]{:S(2)}, u32[]{:S(2)}) collective-permute-start(bf16[32,2176]{1,0:T(8,128)(2,1)S(1)} %maximum_maximum_fusion), channel_id=1, source_target_pairs={{0,1},{1,0},{2,3},{3,2},{4,5},{5,4},{6,7},{7,6},{8,9},{9,8},{10,11... | collective-permute-start | bytes 417800 | tf_op jit(solution)/shard_map/ppermute | solution.py:227
  16.1 3.3 %collective-permute-done.4 = bf16[32,2048]{1,0:T(8,128)(2,1)S(1)} collective-permute-done((bf16[32,2048]{1,0:T(8,128)(2,1)S(1)}, bf16[32,2048]{1,0:T(8,128)(2,1)S(1)}, u32[]{:S(2)}, u32[]{:S(2)}) %collective-permute-start.4) | collective-permute-done | bytes 131104 | tf_op jit(solution)/shard_map/ppermute | solution.py:227
  19.4 1.6 %collective-permute-start.5 = (bf16[64,2048]{1,0:T(8,128)(2,1)S(1)}, bf16[64,2048]{1,0:T(8,128)(2,1)S(1)}, u32[]{:S(2)}, u32[]{:S(2)}) collective-permute-start(bf16[64,2048]{1,0:T(8,128)(2,1)S(1)} %pad_maximum_fusion.4), channel_id=1, source_target_pairs={{0,1},{1,0},{2,3},{3,2},{4,5},{5,4},{6,7},{7,6},{8,9},{9,8},{10,11... | collective-permute-start | bytes 786440 | tf_op jit(solution)/shard_map/ppermute | solution.py:227
  21.0 2.1 %collective-permute-start.3 = (bf16[64,2176]{1,0:T(8,128)(2,1)S(1)}, bf16[64,2176]{1,0:T(8,128)(2,1)S(1)}, u32[]{:S(2)}, u32[]{:S(2)}) collective-permute-start(bf16[64,2176]{1,0:T(8,128)(2,1)S(1)} %pad_maximum_fusion.2), channel_id=1, source_target_pairs={{0,2},{1,3},{2,0},{3,1},{4,6},{5,7},{6,4},{7,5},{8,10},{9,11},{10,... | collective-permute-start | bytes 835592 | tf_op jit(solution)/shard_map/ppermute | solution.py:227
  23.1 2.7 %collective-permute-done.5 = bf16[64,2048]{1,0:T(8,128)(2,1)S(1)} collective-permute-done((bf16[64,2048]{1,0:T(8,128)(2,1)S(1)}, bf16[64,2048]{1,0:T(8,128)(2,1)S(1)}, u32[]{:S(2)}, u32[]{:S(2)}) %collective-permute-start.5) | collective-permute-done | bytes 262176 | tf_op jit(solution)/shard_map/ppermute | solution.py:227
  25.9 1.8 %shard_map.94.before_ref = f32[128,2048]{1,0:T(8,128)S(1)} custom-call(bf16[128,2048]{1,0:T(8,128)(2,1)S(1)} %pad_maximum_fusion.1.rows_ref, bf16[4096,2048]{1,0:T(8,128)(2,1)S(1)} %shard_map.93.near_ref.head_ref), custom_call_target="tpu_custom_call" | custom-call | flops 1073741824 | bytes 17301504 | tf_op jit(solution)/shard_map/pallas_call | solution.py:22
  27.8 3.1 %shard_map.95 = (f32[128,2048]{1,0:T(8,128)S(1)}, bf16[256,2048]{1,0:T(8,128)(2,1)S(1)}, f32[8,128]{1,0:T(8,128)S(1)}) custom-call(bf16[128,2176]{1,0:T(8,128)(2,1)S(1)} %pad_maximum_fusion.rows_ref.digits_ref, f32[128,2048]{1,0:T(8,128)S(1)} %shard_map.94.before_ref, bf16[4096,2048]{1,0:T(8,128)(2,1)S(1)} %shard_map.93.near_ref.head_ref), custom_call_target="tpu_custom_call" | custom-call | flops 1073741824 | bytes 18382848 | tf_op jit(solution)/shard_map/pallas_call | solution.py:22
  30.9 2.0 %collective-permute-start.6 = (f32[8,128]{1,0:T(8,128)S(1)}, f32[8,128]{1,0:T(8,128)S(1)}, u32[]{:S(2)}, u32[]{:S(2)}) collective-permute-start(f32[8,128]{1,0:T(8,128)S(1)} %get-tuple-element.14.mine_ref), channel_id=1, source_target_pairs={{0,4},{1,5},{2,6},{3,7},{4,0},{5,1},{6,2},{7,3},{8,12},{9,13},{10,... | collective-permute-start | bytes 12296 | tf_op jit(solution)/shard_map/ppermute | solution.py:227
  34.3 1.4 %shard_map.101.refs_2_ = f32[256,1024]{1,0:T(8,128)S(1)} custom-call(bf16[256,2048]{1,0:T(8,128)(2,1)S(1)} %get-tuple-element.15.both_ref, bf16[4096,2048]{1,0:T(8,128)(2,1)S(1)} %shard_map.93.near_ref.head_ref), custom_call_target="tpu_custom_call" | custom-call | flops 2147483648 | bytes 17825792 | tf_op jit(solution)/shard_map/pallas_call | solution.py:22
  35.8 1.8 %collective-permute-start.7 = (f32[8,128]{1,0:T(8,128)S(1)}, f32[8,128]{1,0:T(8,128)S(1)}, u32[]{:S(2)}, u32[]{:S(2)}) collective-permute-start(f32[8,128]{1,0:T(8,128)S(1)} %shard_map.96.mine_ref), channel_id=1, source_target_pairs={{0,2},{1,3},{2,0},{3,1},{4,6},{5,7},{6,4},{7,5},{8,10},{9,11},{10,... | collective-permute-start | bytes 12296 | tf_op jit(solution)/shard_map/ppermute | solution.py:227
  37.6 1.4 %shard_map.100.refs_1_ = f32[256,1024]{1,0:T(8,128)S(1)} custom-call(bf16[256,2048]{1,0:T(8,128)(2,1)S(1)} %get-tuple-element.15.both_ref, bf16[4096,2048]{1,0:T(8,128)(2,1)S(1)} %shard_map.93.near_ref.head_ref), custom_call_target="tpu_custom_call" | custom-call | flops 2147483648 | bytes 17825792 | tf_op jit(solution)/shard_map/pallas_call | solution.py:22
  39.5 1.6 %collective-permute-start.8 = (f32[8,128]{1,0:T(8,128)S(1)}, f32[8,128]{1,0:T(8,128)S(1)}, u32[]{:S(2)}, u32[]{:S(2)}) collective-permute-start(f32[8,128]{1,0:T(8,128)S(1)} %shard_map.97.mine_ref), channel_id=1, source_target_pairs={{0,1},{1,0},{2,3},{3,2},{4,5},{5,4},{6,7},{7,6},{8,9},{9,8},{10,11... | collective-permute-start | bytes 12296 | tf_op jit(solution)/shard_map/ppermute | solution.py:227
  44.0 1.7 %collective-permute-start.11 = (f16[64,2048]{1,0:T(8,128)(2,1)S(1)}, f16[64,2048]{1,0:T(8,128)(2,1)S(1)}, u32[]{:S(2)}, u32[]{:S(2)}) collective-permute-start(f16[64,2048]{1,0:T(8,128)(2,1)S(1)} %convert_element_type.40), channel_id=1, source_target_pairs={{0,2},{1,3},{2,0},{3,1},{4,6},{5,7},{6,4},{7,5},{8,10},{9,11},{10,... | collective-permute-start | bytes 786440 | tf_op jit(solution)/shard_map/ppermute | solution.py:227
  45.8 1.6 %collective-permute-start.9 = (f16[64,2048]{1,0:T(8,128)(2,1)S(1)}, f16[64,2048]{1,0:T(8,128)(2,1)S(1)}, u32[]{:S(2)}, u32[]{:S(2)}) collective-permute-start(f16[64,2048]{1,0:T(8,128)(2,1)S(1)} %convert_element_type.36), channel_id=1, source_target_pairs={{0,1},{1,0},{2,3},{3,2},{4,5},{5,4},{6,7},{7,6},{8,9},{9,8},{10,11... | collective-permute-start | bytes 786440 | tf_op jit(solution)/shard_map/ppermute | solution.py:227
  47.4 4.4 %collective-permute-done.11 = f16[64,2048]{1,0:T(8,128)(2,1)S(1)} collective-permute-done((f16[64,2048]{1,0:T(8,128)(2,1)S(1)}, f16[64,2048]{1,0:T(8,128)(2,1)S(1)}, u32[]{:S(2)}, u32[]{:S(2)}) %collective-permute-start.11) | collective-permute-done | bytes 262176 | tf_op jit(solution)/shard_map/ppermute | solution.py:227
  51.9 1.6 %collective-permute-start.12 = (f16[32,2048]{1,0:T(8,128)(2,1)S(1)}, f16[32,2048]{1,0:T(8,128)(2,1)S(1)}, u32[]{:S(2)}, u32[]{:S(2)}) collective-permute-start(f16[32,2048]{1,0:T(8,128)(2,1)S(1)} %fusion.5), channel_id=1, source_target_pairs={{0,1},{1,0},{2,3},{3,2},{4,5},{5,4},{6,7},{7,6},{8,9},{9,8},{10,11... | collective-permute-start | bytes 393224 | tf_op jit(solution)/shard_map/ppermute | solution.py:227
  53.7 1.8 %collective-permute-start.10 = (f16[32,2048]{1,0:T(8,128)(2,1)S(1)}, f16[32,2048]{1,0:T(8,128)(2,1)S(1)}, u32[]{:S(2)}, u32[]{:S(2)}) collective-permute-start(f16[32,2048]{1,0:T(8,128)(2,1)S(1)} %fusion.6), channel_id=1, source_target_pairs={{0,2},{1,3},{2,0},{3,1},{4,6},{5,7},{6,4},{7,5},{8,10},{9,11},{10,... | collective-permute-start | bytes 393224 | tf_op jit(solution)/shard_map/ppermute | solution.py:227
  55.4 1.5 %collective-permute-done.12 = f16[32,2048]{1,0:T(8,128)(2,1)S(1)} collective-permute-done((f16[32,2048]{1,0:T(8,128)(2,1)S(1)}, f16[32,2048]{1,0:T(8,128)(2,1)S(1)}, u32[]{:S(2)}, u32[]{:S(2)}) %collective-permute-start.12) | collective-permute-done | bytes 131104 | tf_op jit(solution)/shard_map/ppermute | solution.py:227
  57.0 2.5 %collective-permute-done.10 = f16[32,2048]{1,0:T(8,128)(2,1)S(1)} collective-permute-done((f16[32,2048]{1,0:T(8,128)(2,1)S(1)}, f16[32,2048]{1,0:T(8,128)(2,1)S(1)}, u32[]{:S(2)}, u32[]{:S(2)}) %collective-permute-start.10) | collective-permute-done | bytes 131104 | tf_op jit(solution)/shard_map/ppermute | solution.py:227
  61.1 3.4 %shard_map.104 = (f32[128,2048]{1,0:T(8,128)}, f32[128,2048]{1,0:T(8,128)}) custom-call(bf16[128,2048]{1,0:T(8,128)(2,1)S(1)} %pad_maximum_fusion.1.rows_ref, bf16[128,2176]{1,0:T(8,128)(2,1)S(1)} %pad_maximum_fusion.rows_ref.digits_ref, f32[8,128]{1,0:T(8,128)S(1)} %shard_map.98.lines_ref, f32[128,2048]{1,0:T(8,128)S(1)} %get-tuple-element.21.logits_ref, ...), custom_call_target="tpu_custom_call" | custom-call | flops 67108864 | bytes 6291456 | tf_op jit(solution)/shard_map/pallas_call | solution.py:204
  64.4 2.5 %collective-permute-done.13 = f16[16,4096]{1,0:T(8,128)(2,1)S(1)} collective-permute-done((f16[16,4096]{1,0:T(8,128)(2,1)S(1)}, f16[16,4096]{1,0:T(8,128)(2,1)S(1)}, u32[]{:S(2)}, u32[]{:S(2)}) %collective-permute-start.13) | collective-permute-done | bytes 131104 | tf_op jit(solution)/shard_map/ppermute | solution.py:227
  (46 shorter events, 9.5 us)
Async XLA Ops:
  1.4 13.0 %collective-permute-start.1 = (bf16[16,128]{1,0:T(8,128)(2,1)S(1)}, bf16[16,128]{1,0:T(8,128)(2,1)S(1)}, u32[]{:S(2)}, u32[]{:S(2)}) collective-permute-start(bf16[16,128]{1,0:T(8,128)(2,1)S(1)} %pad.4), channel_id=1, source_target_pairs={{0,4},{1,5},{2,6},{3,7},{4,0},{5,1},{6,2},{7,3},{8,12},{9,13},{10,... | collective-permute-start | bytes 12296 | tf_op jit(solution)/shard_map/ppermute | solution.py:227
  5.5 8.9 %collective-permute-start = (bf16[16,4096]{1,0:T(8,128)(2,1)}, bf16[16,4096]{1,0:T(8,128)(2,1)S(1)}, u32[]{:S(2)}, u32[]{:S(2)}) collective-permute-start(bf16[16,4096]{1,0:T(8,128)(2,1)} %param.6), channel_id=1, source_target_pairs={{0,4},{1,5},{2,6},{3,7},{4,0},{5,1},{6,2},{7,3},{8,12},{9,13},{10,... | collective-permute-start | bytes 393224 | tf_op jit(solution)/shard_map/ppermute | solution.py:227
  14.4 5.0 %collective-permute-start.4 = (bf16[32,2048]{1,0:T(8,128)(2,1)S(1)}, bf16[32,2048]{1,0:T(8,128)(2,1)S(1)}, u32[]{:S(2)}, u32[]{:S(2)}) collective-permute-start(bf16[32,2048]{1,0:T(8,128)(2,1)S(1)} %get-tuple-element.26), channel_id=1, source_target_pairs={{0,2},{1,3},{2,0},{3,1},{4,6},{5,7},{6,4},{7,5},{8,10},{9,11},{10,... | collective-permute-start | bytes 393224 | tf_op jit(solution)/shard_map/ppermute | solution.py:227
  14.5 6.5 %collective-permute-start.2 = (bf16[32,2176]{1,0:T(8,128)(2,1)S(1)}, bf16[32,2176]{1,0:T(8,128)(2,1)S(1)}, u32[]{:S(2)}, u32[]{:S(2)}) collective-permute-start(bf16[32,2176]{1,0:T(8,128)(2,1)S(1)} %maximum_maximum_fusion), channel_id=1, source_target_pairs={{0,1},{1,0},{2,3},{3,2},{4,5},{5,4},{6,7},{7,6},{8,9},{9,8},{10,11... | collective-permute-start | bytes 417800 | tf_op jit(solution)/shard_map/ppermute | solution.py:227
  19.4 6.4 %collective-permute-start.5 = (bf16[64,2048]{1,0:T(8,128)(2,1)S(1)}, bf16[64,2048]{1,0:T(8,128)(2,1)S(1)}, u32[]{:S(2)}, u32[]{:S(2)}) collective-permute-start(bf16[64,2048]{1,0:T(8,128)(2,1)S(1)} %pad_maximum_fusion.4), channel_id=1, source_target_pairs={{0,1},{1,0},{2,3},{3,2},{4,5},{5,4},{6,7},{7,6},{8,9},{9,8},{10,11... | collective-permute-start | bytes 786440 | tf_op jit(solution)/shard_map/ppermute | solution.py:227
  21.0 6.7 %collective-permute-start.3 = (bf16[64,2176]{1,0:T(8,128)(2,1)S(1)}, bf16[64,2176]{1,0:T(8,128)(2,1)S(1)}, u32[]{:S(2)}, u32[]{:S(2)}) collective-permute-start(bf16[64,2176]{1,0:T(8,128)(2,1)S(1)} %pad_maximum_fusion.2), channel_id=1, source_target_pairs={{0,2},{1,3},{2,0},{3,1},{4,6},{5,7},{6,4},{7,5},{8,10},{9,11},{10,... | collective-permute-start | bytes 835592 | tf_op jit(solution)/shard_map/ppermute | solution.py:227
  30.9 4.8 %collective-permute-start.6 = (f32[8,128]{1,0:T(8,128)S(1)}, f32[8,128]{1,0:T(8,128)S(1)}, u32[]{:S(2)}, u32[]{:S(2)}) collective-permute-start(f32[8,128]{1,0:T(8,128)S(1)} %get-tuple-element.14.mine_ref), channel_id=1, source_target_pairs={{0,4},{1,5},{2,6},{3,7},{4,0},{5,1},{6,2},{7,3},{8,12},{9,13},{10,... | collective-permute-start | bytes 12296 | tf_op jit(solution)/shard_map/ppermute | solution.py:227
  35.8 3.7 %collective-permute-start.7 = (f32[8,128]{1,0:T(8,128)S(1)}, f32[8,128]{1,0:T(8,128)S(1)}, u32[]{:S(2)}, u32[]{:S(2)}) collective-permute-start(f32[8,128]{1,0:T(8,128)S(1)} %shard_map.96.mine_ref), channel_id=1, source_target_pairs={{0,2},{1,3},{2,0},{3,1},{4,6},{5,7},{6,4},{7,5},{8,10},{9,11},{10,... | collective-permute-start | bytes 12296 | tf_op jit(solution)/shard_map/ppermute | solution.py:227
  39.5 3.7 %collective-permute-start.8 = (f32[8,128]{1,0:T(8,128)S(1)}, f32[8,128]{1,0:T(8,128)S(1)}, u32[]{:S(2)}, u32[]{:S(2)}) collective-permute-start(f32[8,128]{1,0:T(8,128)S(1)} %shard_map.97.mine_ref), channel_id=1, source_target_pairs={{0,1},{1,0},{2,3},{3,2},{4,5},{5,4},{6,7},{7,6},{8,9},{9,8},{10,11... | collective-permute-start | bytes 12296 | tf_op jit(solution)/shard_map/ppermute | solution.py:227
  44.0 7.8 %collective-permute-start.11 = (f16[64,2048]{1,0:T(8,128)(2,1)S(1)}, f16[64,2048]{1,0:T(8,128)(2,1)S(1)}, u32[]{:S(2)}, u32[]{:S(2)}) collective-permute-start(f16[64,2048]{1,0:T(8,128)(2,1)S(1)} %convert_element_type.40), channel_id=1, source_target_pairs={{0,2},{1,3},{2,0},{3,1},{4,6},{5,7},{6,4},{7,5},{8,10},{9,11},{10,... | collective-permute-start | bytes 786440 | tf_op jit(solution)/shard_map/ppermute | solution.py:227
  45.8 7.7 %collective-permute-start.9 = (f16[64,2048]{1,0:T(8,128)(2,1)S(1)}, f16[64,2048]{1,0:T(8,128)(2,1)S(1)}, u32[]{:S(2)}, u32[]{:S(2)}) collective-permute-start(f16[64,2048]{1,0:T(8,128)(2,1)S(1)} %convert_element_type.36), channel_id=1, source_target_pairs={{0,1},{1,0},{2,3},{3,2},{4,5},{5,4},{6,7},{7,6},{8,9},{9,8},{10,11... | collective-permute-start | bytes 786440 | tf_op jit(solution)/shard_map/ppermute | solution.py:227
  51.9 5.0 %collective-permute-start.12 = (f16[32,2048]{1,0:T(8,128)(2,1)S(1)}, f16[32,2048]{1,0:T(8,128)(2,1)S(1)}, u32[]{:S(2)}, u32[]{:S(2)}) collective-permute-start(f16[32,2048]{1,0:T(8,128)(2,1)S(1)} %fusion.5), channel_id=1, source_target_pairs={{0,1},{1,0},{2,3},{3,2},{4,5},{5,4},{6,7},{7,6},{8,9},{9,8},{10,11... | collective-permute-start | bytes 393224 | tf_op jit(solution)/shard_map/ppermute | solution.py:227
  53.5 7.6 %copy-start.2 = (f32[128,2048]{1,0:T(8,128)S(1)}, f32[128,2048]{1,0:T(8,128)}, u32[]{:S(2)}) copy-start(f32[128,2048]{1,0:T(8,128)} %peer_ref.1) | copy-start | bytes 3145732
  53.6 7.5 %copy-start = (f32[128,2048]{1,0:T(8,128)S(1)}, f32[128,2048]{1,0:T(8,128)}, u32[]{:S(2)}) copy-start(f32[128,2048]{1,0:T(8,128)} %global_ref.1) | copy-start | bytes 3145732
  53.6 7.5 %copy-start.1 = (f32[128,2048]{1,0:T(8,128)S(1)}, f32[128,2048]{1,0:T(8,128)}, u32[]{:S(2)}) copy-start(f32[128,2048]{1,0:T(8,128)} %momentum_ref.1) | copy-start | bytes 3145732
  53.7 5.8 %collective-permute-start.10 = (f16[32,2048]{1,0:T(8,128)(2,1)S(1)}, f16[32,2048]{1,0:T(8,128)(2,1)S(1)}, u32[]{:S(2)}, u32[]{:S(2)}) collective-permute-start(f16[32,2048]{1,0:T(8,128)(2,1)S(1)} %fusion.6), channel_id=1, source_target_pairs={{0,2},{1,3},{2,0},{3,1},{4,6},{5,7},{6,4},{7,5},{8,10},{9,11},{10,... | collective-permute-start | bytes 393224 | tf_op jit(solution)/shard_map/ppermute | solution.py:227
  59.6 7.3 %collective-permute-start.13 = (f16[16,4096]{1,0:T(8,128)(2,1)S(1)}, f16[16,4096]{1,0:T(8,128)(2,1)S(1)}, u32[]{:S(2)}, u32[]{:S(2)}) collective-permute-start(f16[16,4096]{1,0:T(8,128)(2,1)S(1)} %fusion.4), channel_id=1, source_target_pairs={{0,4},{1,5},{2,6},{3,7},{4,0},{5,1},{6,2},{7,3},{8,12},{9,13},{10,... | collective-permute-start | bytes 393224 | tf_op jit(solution)/shard_map/ppermute | solution.py:227

commit v7 on v6

v7 whole, which is shorter than its diff:
```python
import functools

import jax
import jax.numpy as jnp
from jax import lax
from jax.experimental import pallas as pl
from jax.experimental.pallas import tpu as pltpu
from jax.sharding import PartitionSpec as P

FRAG = 128
REPLICAS = 4
AXIS = "vocab"
SEND = jnp.float16
LANES = 128
VMEM = pl.BlockSpec(memory_space=pltpu.VMEM)


def call(kernel, outs, operands, flops=0, scratch=(), sources=None, vmem=16 * 2**20):
    outs = [pltpu.VMEM(shape, dtype) for shape, dtype in outs]
    places = sources or [pltpu.VMEM] * len(operands)
    moved = sum(x.size * x.dtype.itemsize for x in operands)
    return pl.pallas_call(
        kernel,
        out_shape=outs,
        in_specs=[pl.BlockSpec(memory_space=place) for place in places],
        out_specs=[VMEM] * len(outs),
        scratch_shapes=list(scratch),
        compiler_params=pltpu.CompilerParams(vmem_limit_bytes=vmem),
        cost_estimate=pl.CostEstimate(flops=flops, bytes_accessed=moved, transcendentals=0),
    )(*[pltpu.with_memory_space_constraint(x, place) for x, place in zip(operands, places)])


def load_kernel(source, target, token_ref, sems):
    block = source.shape[0] // sems.shape[0]
    copies = []
    for i in range(sems.shape[0]):
        part = pl.ds(i * block, block)
        copies.append(pltpu.make_async_copy(source.at[part], target.at[part], sems.at[i]))
    for copy in copies:
        copy.start()
    for copy in copies:
        copy.wait()
    token_ref[...] = jnp.zeros_like(token_ref)


def resident(head):
    return call(
        load_kernel, [(head.shape, head.dtype), ((8, LANES), jnp.float32)], [head],
        scratch=[pltpu.SemaphoreType.DMA((4,))], sources=[pltpu.HBM],
    )


TILE = 512


def pack_kernel(targets_ref, rows_ref, out_ref):
    own, depth = rows_ref.shape
    place = lax.broadcasted_iota(jnp.int32, (own, LANES), 0)
    ids = jnp.zeros((own, LANES), jnp.int32)
    for i in range(own):
        ids = jnp.where(place == i, targets_ref[i], ids)
    lane = lax.broadcasted_iota(jnp.int32, (own, LANES), 1)
    digits = jnp.where(lane == 0, ids // 256, ids % 256)
    out_ref[:, :depth] = rows_ref[...]
    out_ref[:, depth:] = digits.astype(jnp.float32).astype(jnp.bfloat16)


def ids_of(digits):
    digits = digits.astype(jnp.float32)
    return (digits[:, 0:1] * 256.0 + digits[:, 1:2]).astype(jnp.int32)


def swap_blocks(value, group):
    size = value.shape[1]
    lane = lax.broadcasted_iota(jnp.int32, value.shape, 1)
    up, down = pltpu.roll(value, group, 1), pltpu.roll(value, size - group, 1)
    return jnp.where((lane & group) != 0, up, down)


def shared_order(value, members):
    me = lax.axis_index(AXIS)
    step = 1
    while step < members:
        swapped = swap_blocks(value, value.shape[1] // members * step)
        value = jnp.where((me & step) != 0, swapped, value)
        step *= 2
    return value


def as_columns(line):
    return jnp.broadcast_to(line, (LANES, line.shape[1])).T[:, 0:1]


def rows_kernel(rows_ref, near_ref, *refs):
    before_ref, (logits_ref, both_ref, stats_ref) = (None, refs) if len(refs) == 3 else (refs[0], refs[1:4])
    rows = rows_ref.shape[0]
    depth, width = near_ref.shape

    @pl.loop(0, width // TILE)
    def _(i):
        part = pl.ds(pl.multiple_of(i * TILE, TILE), TILE)
        logits_ref[:, part] = jnp.dot(
            rows_ref[:, :depth], near_ref[:, part], preferred_element_type=jnp.float32
        )

    chunk = 32
    offset = lax.axis_index(AXIS) * width
    columns_ref = stats_ref if before_ref is None else refs[4]
    first = 0 if before_ref is None else before_ref.shape[0]

    @pl.loop(0, rows // chunk)
    def _(i):
        part = pl.ds(pl.multiple_of(i * chunk, chunk), chunk)
        logits = logits_ref[part, :]
        ids = ids_of(rows_ref[part, depth:]) - offset
        hit = lax.broadcasted_iota(jnp.int32, logits.shape, 1) == ids
        top = jnp.max(logits, axis=1, keepdims=True)
        raised = jnp.exp(logits - top)
        total = jnp.sum(raised, axis=1, keepdims=True)
        pick = jnp.sum(jnp.where(hit, logits, 0.0), axis=1, keepdims=True)
        both_ref[part, :] = jnp.where(hit, 0.0, raised).astype(jnp.bfloat16)
        other = pl.ds(pl.multiple_of(rows + i * chunk, chunk), chunk)
        both_ref[other, :] = jnp.where(hit, 1.0, 0.0).astype(jnp.bfloat16)
        place = lax.broadcasted_iota(jnp.int32, (chunk, LANES), 1)
        slot = pl.ds(pl.multiple_of(first + i * chunk, chunk), chunk)
        columns_ref[slot, :] = jnp.where(place == 0, top, jnp.where(place == 1, total, pick))

    if before_ref is not None:
        columns_ref[pl.ds(0, first), :] = before_ref[...]
        stats_ref[...] = columns_ref[...].T[:8]


def merge_kernel(step, members, mine_ref, other_ref, out_ref):
    mine = mine_ref[...]
    other = swap_blocks(other_ref[...], mine.shape[1] // members * step)
    upper = (lax.axis_index(AXIS) & step) != 0
    one, two = jnp.where(upper, other, mine), jnp.where(upper, mine, other)
    top = jnp.maximum(one[0:1], two[0:1])
    total = one[1:2] * jnp.exp(one[0:1] - top) + two[1:2] * jnp.exp(two[0:1] - top)
    pick = one[2:3] + two[2:3]
    place = lax.broadcasted_iota(jnp.int32, mine.shape, 0)
    out_ref[...] = jnp.where(place == 0, top, jnp.where(place == 1, total, pick))


def grad_kernel(first, one_ref, two_ref, near_ref, terms_ref):
    both = jnp.concatenate([one_ref[...], two_ref[...]], axis=0)
    turned = lax.dot_general(
        near_ref[pl.ds(first, terms_ref.shape[1]), :], both, (((1,), (1,)), ((), ())),
        preferred_element_type=jnp.float32,
    )
    terms_ref[...] = turned.T


def join_kernel(members, scale, lines_ref, mine_ref, *refs):
    *terms_refs, out_ref, loss_ref = refs
    rows = mine_ref.shape[1]
    lines = lines_ref[...]
    same = shared_order(lines, members)
    loss = jnp.sum(same[0:1] + jnp.log(same[1:2]) - same[2:3], axis=1, keepdims=True) / rows
    loss_ref[...] = jnp.broadcast_to(loss, loss_ref.shape)

    top, total = lines[0:1], lines[1:2]
    soft = as_columns(jnp.exp(mine_ref[0:1, :] - top) / (total * rows)) * scale
    hard = (jnp.exp(mine_ref[2:3, :] - top) / total - 1.0) / rows
    hard = as_columns(hard.astype(jnp.bfloat16).astype(jnp.float32)) * scale

    near = rows // members * 4
    chunk = min(near, rows - near, 64)
    for place, terms_ref in enumerate(terms_refs):
        columns = pl.ds(place * terms_ref.shape[1], terms_ref.shape[1])
        for first in range(0, rows, chunk):
            at, other = (first, near) if first < near else (near + first, rows - near)
            out_ref[pl.ds(first, chunk), columns] = (
                soft[first : first + chunk] * terms_ref[pl.ds(at, chunk), :]
                + hard[first : first + chunk] * terms_ref[pl.ds(at + other, chunk), :]
            )


def frag_kernel(rows_ref, digits_ref, lines_ref, one_ref, two_ref, head_ref, global_ref, momentum_ref,
                peer_ref, new_global_ref, new_momentum_ref):
    logits = jnp.concatenate([one_ref[...], two_ref[...]], axis=0)
    rows, tile = logits.shape
    top, total = as_columns(lines_ref[0:1, :]), as_columns(lines_ref[1:2, :])
    offset = (lax.axis_index(AXIS) * pl.num_programs(0) + pl.program_id(0)) * tile
    hit = lax.broadcasted_iota(jnp.int32, (rows, tile), 1) == ids_of(digits_ref[...]) - offset
    shares = jnp.exp(logits - top) / total
    dlogits = ((shares - jnp.where(hit, 1.0, 0.0)) / rows).astype(jnp.bfloat16)
    turned = rows_ref[...].astype(jnp.float32).T.astype(jnp.bfloat16)
    frag_grad = jnp.dot(turned, dlogits, preferred_element_type=jnp.float32)
    local_frag = head_ref[...].astype(jnp.float32) - 1.0 * frag_grad
    pseudo = (global_ref[...] - local_frag + peer_ref[...]) / REPLICAS
    new_momentum = 0.9 * momentum_ref[...] + pseudo
    new_momentum_ref[...] = new_momentum
    new_global_ref[...] = global_ref[...] - 0.7 * (pseudo + 0.9 * new_momentum)


def frag_update(rows_all, lines, logits, near, global_frag, momentum, peer_delta):
    rows = rows_all.shape[0]
    width = near.shape[1]
    last = rows_all.shape[1] // LANES - 1
    tile = pl.BlockSpec((FRAG, TILE), lambda i: (0, i))
    return pl.pallas_call(
        frag_kernel,
        grid=(width // TILE,),
        out_shape=[jax.ShapeDtypeStruct((FRAG, width), jnp.float32)] * 2,
        in_specs=[
            pl.BlockSpec((rows, FRAG), lambda i: (0, 0)),
            pl.BlockSpec((rows, LANES), lambda i: (0, last)),
            pl.BlockSpec((8, rows), lambda i: (0, 0)),
        ]
        + [pl.BlockSpec((x.shape[0], TILE), lambda i: (0, i)) for x in logits]
        + [tile] * 4,
        out_specs=[tile, tile],
        compiler_params=pltpu.CompilerParams(vmem_limit_bytes=16 * 2**20),
        cost_estimate=pl.CostEstimate(
            flops=2 * rows * FRAG * width, bytes_accessed=24 * FRAG * width, transcendentals=0
        ),
    )(
        rows_all, rows_all, lines,
        *[pltpu.with_memory_space_constraint(x, pltpu.VMEM) for x in logits],
        pltpu.with_memory_space_constraint(near, pltpu.VMEM), global_frag, momentum, peer_delta,
    )


def swap(value, step):
    return lax.ppermute(value, AXIS, [(i, i ^ step) for i in range(lax.axis_size(AXIS))])


def far_steps():
    step = 4
    steps = []
    while step < lax.axis_size(AXIS):
        steps.append(step)
        step *= 2
    return steps


def gather_rows(packed, token):
    own = packed.shape[0]
    held = packed
    for step in far_steps()[:1]:
        held = jnp.concatenate([held, swap(held, step)], axis=0)
    packed, _ = lax.optimization_barrier((packed, token))
    near = [packed] + [swap(packed, step) for step in (3, 2, 1)][::-1]
    for step in far_steps()[1:]:
        held = jnp.concatenate([held, swap(held, step)], axis=0)
    far = held[own:]
    far = jnp.stack([far] + [swap(far, step) for step in (3, 2, 1)][::-1])
    count = far.shape[1] // own
    far = far.reshape(4, count, own, -1).swapaxes(0, 1).reshape(4 * count * own, -1)
    return jnp.concatenate(near, axis=0), far


def scatter_sums(grads, own):
    members = grads.shape[0] // own
    blocks = [grads[i * own : (i + 1) * own] for i in range(members)]

    def moved(parts, step):
        value = jnp.concatenate([part.astype(SEND) for part in parts], axis=0)
        value = swap(value, step).astype(jnp.float32)
        return [value[i * own : (i + 1) * own] for i in range(len(parts))]

    sums = blocks[::4]
    for part in (list(range(1, members // 4)), [0]):
        for step in (3, 2, 1):
            for i, value in zip(part, moved([blocks[4 * i + step] for i in part], step)):
                sums[i] = sums[i] + value
    for step in far_steps()[::-1]:
        keep = len(sums) // 2
        sums = [a + b for a, b in zip(sums[:keep], moved(sums[keep:], step))]
    return sums[0]


def body(hidden, targets, head, global_frag, momentum, peer_delta):
    members = lax.axis_size(AXIS)
    own, depth = hidden.shape
    rows = own * members
    width = head.shape[1]

    packed = call(
        pack_kernel, [((own, depth + LANES), hidden.dtype)], [targets, hidden],
        sources=[pltpu.SMEM, pltpu.VMEM],
    )[0]
    near, token = resident(head)
    rows_near, rows_far = gather_rows(packed, token)

    def part(held, *before):
        count = held.shape[0]
        stats = (8, rows) if before else (count, LANES)
        return call(
            rows_kernel,
            [((count, width), jnp.float32), ((2 * count, width), jnp.bfloat16), (stats, jnp.float32)],
            [held, near, *before], 2 * count * depth * width,
            scratch=[pltpu.VMEM((rows, LANES), jnp.float32)] if before else [],
        )

    logits_near, both_near, columns = part(rows_near)
    logits_far, both_far, mine = part(rows_far, columns)

    lines = mine
    for step in far_steps()[::-1] + [2, 1]:
        lines = call(
            functools.partial(merge_kernel, step, members),
            [((8, rows), jnp.float32)], [lines, swap(lines, step)],
        )[0]

    cuts = 4
    terms = [
        call(
            functools.partial(grad_kernel, i * depth // cuts),
            [((2 * rows, depth // cuts), jnp.float32)], [both_near, both_far, near],
            4 * rows * depth * width // cuts,
        )[0]
        for i in range(cuts)
    ]

    scale = 2.0**14 * rows
    grads, loss = call(
        functools.partial(join_kernel, members, scale),
        [((rows, depth), jnp.float32), ((8, LANES), jnp.float32)],
        [lines, mine] + terms,
    )
    hidden_grad = (scatter_sums(grads, own) * (1.0 / scale)).astype(jnp.bfloat16)
    new_global, new_momentum = frag_update(
        jnp.concatenate([rows_near, rows_far], axis=0), lines, [logits_near, logits_far], near,
        global_frag, momentum, peer_delta,
    )
    return (loss[0, :1], hidden_grad, new_global, new_momentum)


def solution(mesh):
    in_specs = (
        P(("outer", "vocab"), None),
        P(("outer", "vocab")),
        P("outer", "vocab"),
        P(None, "vocab"),
        P(None, "vocab"),
        P("outer", "vocab"),
    )
    out_specs = (P("outer"), P(("outer", "vocab"), None), P("outer", "vocab"), P("outer", "vocab"))
    return jax.shard_map(body, mesh=mesh, in_specs=in_specs, out_specs=out_specs, check_vma=False)
```

time: 67.8 us -> 58.8 us (0.87)
  waiting for transfers between devices: 20.2 us -> 4.23 us
  Pallas kernels: 20.5 us -> 24.8 us
  starting transfers between devices: 22.5 us -> 25.4 us
  other arithmetic: 1.86 us -> 1.07 us
  local copies, waits for them, and re-layouts: 1.63 us -> 2.32 us
    ppermute x14 -> x17, waiting for transfers between devices: 20.2 us -> 4.23 us  [swap(): lax.ppermute(value, AXIS, [(i, i ^ step) for i in range(lax.axis_size(AXI...]
    pallas_call x11 -> x12, Pallas kernels: 17.1 us -> 21.4 us  [call(): pl.pallas_call(kernel, out_shape=outs, in_specs=[pl.BlockSpec(memory_spac...]
    ppermute x14 -> x17, starting transfers between devices: 22.5 us -> 25.4 us  [swap(): lax.ppermute(value, AXIS, [(i, i ^ step) for i in range(lax.axis_size(AXI...]
    unnamed x7 -> x14, local copies, waits for them, and re-layouts: 0.96 us -> 1.63 us
  transfers between devices with their start and end apart: 14 -> 17, of which waited for: 9 -> 6; matrix products, arithmetic and copies ran while one was open for 3% -> 1% of each run, Pallas kernels for 25% -> 33%
where the time goes in v7:
time: 58.8 us; the launch traced here: 58.6 us
  starting transfers between devices  25.4 us (43%)
  Pallas kernels  24.8 us (42%)
  waiting for transfers between devices  4.23 us (7%)
  local copies, waits for them, and re-layouts  2.32 us (4%)
  other arithmetic  1.07 us (2%)
  between operations  0.8 us (1%)
    ppermute x17, starting transfers between devices, swap(): lax.ppermute(value, AXIS, [(i, i ^ step) for i in range(lax.axis_size(AXI...  25.4 us
    pallas_call x12, Pallas kernels, call(): pl.pallas_call(kernel, out_shape=outs, in_specs=[pl.BlockSpec(memory_spac...  21.4 us
    ppermute x17, waiting for transfers between devices, swap(): lax.ppermute(value, AXIS, [(i, i ^ step) for i in range(lax.axis_size(AXI...  4.23 us
    pallas_call x1, Pallas kernels, frag_update(): pl.pallas_call(frag_kernel, grid=(width // TILE,), out_shape=[jax.ShapeDt...  3.36 us
    unnamed x14, local copies, waits for them, and re-layouts  1.63 us
  transfers between devices with their start and end apart: 17, of which 6 were waited for; matrix products, arithmetic and copies ran while one was open for 1% of the time, Pallas kernels for 33%

profile of v7, /device:TPU:0, one launch (start us, length us, event | category | flops | bytes accessed | tf_op | source)
XLA Modules:
  0.0 58.6 jit_solution(10498724592172348814)
XLA Ops:
  0.6 0.9 %copy-done.3 = bf16[16,4096]{1,0:T(8,128)(2,1)S(1)} copy-done((bf16[16,4096]{1,0:T(8,128)(2,1)S(1)}, bf16[16,4096]{1,0:T(8,128)(2,1)}, u32[]{:S(2)}) %copy-start.3) | copy-done | bytes 131096
  2.8 4.0 %collective-permute-start.6 = (bf16[16,4224]{1,0:T(8,128)(2,1)S(1)}, bf16[16,4224]{1,0:T(8,128)(2,1)S(1)}, u32[]{:S(2)}, u32[]{:S(2)}) collective-permute-start(bf16[16,4224]{1,0:T(8,128)(2,1)S(1)} %shard_map.93), channel_id=1, source_target_pairs={{0,3},{1,2},{2,1},{3,0},{4,7},{5,6},{6,5},{7,4},{8,11},{9,10},{10,... | collective-permute-start | bytes 405512 | tf_op jit(solution)/shard_map/ppermute | solution.py:226
  7.5 2.9 %collective-permute-start = (bf16[16,4224]{1,0:T(8,128)(2,1)S(1)}, bf16[16,4224]{1,0:T(8,128)(2,1)S(1)}, u32[]{:S(2)}, u32[]{:S(2)}) collective-permute-start(bf16[16,4224]{1,0:T(8,128)(2,1)S(1)} %shard_map.93), channel_id=1, source_target_pairs={{0,4},{1,5},{2,6},{3,7},{4,0},{5,1},{6,2},{7,3},{8,12},{9,13},{10,... | collective-permute-start | bytes 405512 | tf_op jit(solution)/shard_map/ppermute | solution.py:226
  10.4 6.5 %shard_map.94 = (bf16[4096,2048]{1,0:T(8,128)(2,1)S(1)}, f32[8,128]{1,0:T(8,128)}) custom-call(bf16[4096,2048]{1,0:T(8,128)(2,1)} %source.1), custom_call_target="tpu_custom_call" | custom-call | bytes 16777216 | tf_op jit(solution)/shard_map/pallas_call | solution.py:22
  16.9 2.6 %collective-permute-start.3 = (bf16[16,4224]{1,0:T(8,128)(2,1)S(1)}, bf16[16,4224]{1,0:T(8,128)(2,1)S(1)}, u32[]{:S(2)}, u32[]{:S(2)}) collective-permute-start(bf16[16,4224]{1,0:T(8,128)(2,1)S(1)} %collective-permute-done), channel_id=1, source_target_pairs={{0,3},{1,2},{2,1},{3,0},{4,7},{5,6},{6,5},{7,4},{8,11},{9,10},{10,... | collective-permute-start | bytes 405512 | tf_op jit(solution)/shard_map/ppermute | solution.py:226
  20.5 4.0 %shard_map.95 = (f32[64,2048]{1,0:T(8,128)S(1)}, bf16[128,2048]{1,0:T(8,128)(2,1)S(1)}, f32[64,128]{1,0:T(8,128)S(1)}) custom-call(bf16[64,4224]{1,0:T(8,128)(2,1)S(1)} %pad_maximum_fusion.1.rows_ref, bf16[4096,2048]{1,0:T(8,128)(2,1)S(1)} %get-tuple-element.15.near_ref.head_ref), custom_call_target="tpu_custom_call" | custom-call | flops 1073741824 | bytes 17317888 | tf_op jit(solution)/shard_map/pallas_call | solution.py:22
  25.4 4.0 %shard_map.96 = (f32[64,2048]{1,0:T(8,128)S(1)}, bf16[128,2048]{1,0:T(8,128)(2,1)S(1)}, f32[8,128]{1,0:T(8,128)S(1)}) custom-call(bf16[64,4224]{1,0:T(8,128)(2,1)S(1)} %bitcast.6, bf16[4096,2048]{1,0:T(8,128)(2,1)S(1)} %get-tuple-element.15.near_ref.head_ref, f32[64,128]{1,0:T(8,128)S(1)} %get-tuple-element.16.refs_0_), custom_call_target="tpu_custom_call" | custom-call | flops 1073741824 | bytes 17350656 | tf_op jit(solution)/shard_map/pallas_call | solution.py:22
  29.5 1.8 %collective-permute-start.7 = (f32[8,128]{1,0:T(8,128)S(1)}, f32[8,128]{1,0:T(8,128)S(1)}, u32[]{:S(2)}, u32[]{:S(2)}) collective-permute-start(f32[8,128]{1,0:T(8,128)S(1)} %get-tuple-element.17.mine_ref), channel_id=1, source_target_pairs={{0,4},{1,5},{2,6},{3,7},{4,0},{5,1},{6,2},{7,3},{8,12},{9,13},{10,... | collective-permute-start | bytes 12296 | tf_op jit(solution)/shard_map/ppermute | solution.py:226
  31.2 1.4 %shard_map.103.refs_3_ = f32[256,1024]{1,0:T(8,128)S(1)} custom-call(bf16[128,2048]{1,0:T(8,128)(2,1)S(1)} %get-tuple-element.18.one_ref, bf16[128,2048]{1,0:T(8,128)(2,1)S(1)} %get-tuple-element.19.two_ref, bf16[4096,2048]{1,0:T(8,128)(2,1)S(1)} %get-tuple-element.15.near_ref.head_ref), custom_call_target="tpu_custom_call" | custom-call | flops 1073741824 | bytes 17825792 | tf_op jit(solution)/shard_map/pallas_call | solution.py:22
  32.6 1.4 %shard_map.102.refs_2_ = f32[256,1024]{1,0:T(8,128)S(1)} custom-call(bf16[128,2048]{1,0:T(8,128)(2,1)S(1)} %get-tuple-element.18.one_ref, bf16[128,2048]{1,0:T(8,128)(2,1)S(1)} %get-tuple-element.19.two_ref, bf16[4096,2048]{1,0:T(8,128)(2,1)S(1)} %get-tuple-element.15.near_ref.head_ref), custom_call_target="tpu_custom_call" | custom-call | flops 1073741824 | bytes 17825792 | tf_op jit(solution)/shard_map/pallas_call | solution.py:22
  34.1 1.9 %collective-permute-start.8 = (f32[8,128]{1,0:T(8,128)S(1)}, f32[8,128]{1,0:T(8,128)S(1)}, u32[]{:S(2)}, u32[]{:S(2)}) collective-permute-start(f32[8,128]{1,0:T(8,128)S(1)} %shard_map.97.mine_ref), channel_id=1, source_target_pairs={{0,2},{1,3},{2,0},{3,1},{4,6},{5,7},{6,4},{7,5},{8,10},{9,11},{10,... | collective-permute-start | bytes 12296 | tf_op jit(solution)/shard_map/ppermute | solution.py:226
  36.0 1.4 %shard_map.101.refs_1_ = f32[256,1024]{1,0:T(8,128)S(1)} custom-call(bf16[128,2048]{1,0:T(8,128)(2,1)S(1)} %get-tuple-element.18.one_ref, bf16[128,2048]{1,0:T(8,128)(2,1)S(1)} %get-tuple-element.19.two_ref, bf16[4096,2048]{1,0:T(8,128)(2,1)S(1)} %get-tuple-element.15.near_ref.head_ref), custom_call_target="tpu_custom_call" | custom-call | flops 1073741824 | bytes 17825792 | tf_op jit(solution)/shard_map/pallas_call | solution.py:22
  37.8 1.2 %collective-permute-start.9 = (f32[8,128]{1,0:T(8,128)S(1)}, f32[8,128]{1,0:T(8,128)S(1)}, u32[]{:S(2)}, u32[]{:S(2)}) collective-permute-start(f32[8,128]{1,0:T(8,128)S(1)} %shard_map.98.mine_ref), channel_id=1, source_target_pairs={{0,1},{1,0},{2,3},{3,2},{4,5},{5,4},{6,7},{7,6},{8,9},{9,8},{10,11... | collective-permute-start | bytes 12296 | tf_op jit(solution)/shard_map/ppermute | solution.py:226
  39.0 1.4 %shard_map.100.refs_0_ = f32[256,1024]{1,0:T(8,128)S(1)} custom-call(bf16[128,2048]{1,0:T(8,128)(2,1)S(1)} %get-tuple-element.18.one_ref, bf16[128,2048]{1,0:T(8,128)(2,1)S(1)} %get-tuple-element.19.two_ref, bf16[4096,2048]{1,0:T(8,128)(2,1)S(1)} %get-tuple-element.15.near_ref.head_ref), custom_call_target="tpu_custom_call" | custom-call | flops 1073741824 | bytes 17825792 | tf_op jit(solution)/shard_map/pallas_call | solution.py:22
  40.4 1.1 %collective-permute-done.9.other_ref = f32[8,128]{1,0:T(8,128)S(1)} collective-permute-done((f32[8,128]{1,0:T(8,128)S(1)}, f32[8,128]{1,0:T(8,128)S(1)}, u32[]{:S(2)}, u32[]{:S(2)}) %collective-permute-start.9) | collective-permute-done | bytes 4128 | tf_op jit(solution)/shard_map/ppermute | solution.py:226
  42.5 1.2 %collective-permute-start.15 = (f16[16,4096]{1,0:T(8,128)(2,1)S(1)}, f16[16,4096]{1,0:T(8,128)(2,1)S(1)}, u32[]{:S(2)}, u32[]{:S(2)}) collective-permute-start(f16[16,4096]{1,0:T(8,128)(2,1)S(1)} %get-tuple-element.27), channel_id=1, source_target_pairs={{0,1},{1,0},{2,3},{3,2},{4,5},{5,4},{6,7},{7,6},{8,9},{9,8},{10,11... | collective-permute-start | bytes 393224 | tf_op jit(solution)/shard_map/ppermute | solution.py:226
  43.7 1.5 %collective-permute-start.14 = (f16[16,4096]{1,0:T(8,128)(2,1)S(1)}, f16[16,4096]{1,0:T(8,128)(2,1)S(1)}, u32[]{:S(2)}, u32[]{:S(2)}) collective-permute-start(f16[16,4096]{1,0:T(8,128)(2,1)S(1)} %get-tuple-element.28), channel_id=1, source_target_pairs={{0,2},{1,3},{2,0},{3,1},{4,6},{5,7},{6,4},{7,5},{8,10},{9,11},{10,... | collective-permute-start | bytes 393224 | tf_op jit(solution)/shard_map/ppermute | solution.py:226
  45.3 0.8 %collective-permute-start.13 = (f16[16,4096]{1,0:T(8,128)(2,1)S(1)}, f16[16,4096]{1,0:T(8,128)(2,1)S(1)}, u32[]{:S(2)}, u32[]{:S(2)}) collective-permute-start(f16[16,4096]{1,0:T(8,128)(2,1)S(1)} %get-tuple-element.29), channel_id=1, source_target_pairs={{0,3},{1,2},{2,1},{3,0},{4,7},{5,6},{6,5},{7,4},{8,11},{9,10},{10,... | collective-permute-start | bytes 393224 | tf_op jit(solution)/shard_map/ppermute | solution.py:226
  46.1 2.2 %collective-permute-start.10 = (f16[16,4096]{1,0:T(8,128)(2,1)S(1)}, f16[16,4096]{1,0:T(8,128)(2,1)S(1)}, u32[]{:S(2)}, u32[]{:S(2)}) collective-permute-start(f16[16,4096]{1,0:T(8,128)(2,1)S(1)} %get-tuple-element.26), channel_id=1, source_target_pairs={{0,3},{1,2},{2,1},{3,0},{4,7},{5,6},{6,5},{7,4},{8,11},{9,10},{10,... | collective-permute-start | bytes 393224 | tf_op jit(solution)/shard_map/ppermute | solution.py:226
  48.3 1.2 %collective-permute-start.12 = (f16[16,4096]{1,0:T(8,128)(2,1)S(1)}, f16[16,4096]{1,0:T(8,128)(2,1)S(1)}, u32[]{:S(2)}, u32[]{:S(2)}) collective-permute-start(f16[16,4096]{1,0:T(8,128)(2,1)S(1)} %get-tuple-element.30), channel_id=1, source_target_pairs={{0,1},{1,0},{2,3},{3,2},{4,5},{5,4},{6,7},{7,6},{8,9},{9,8},{10,11... | collective-permute-start | bytes 393224 | tf_op jit(solution)/shard_map/ppermute | solution.py:226
  50.1 1.7 %collective-permute-done.13 = f16[16,4096]{1,0:T(8,128)(2,1)S(1)} collective-permute-done((f16[16,4096]{1,0:T(8,128)(2,1)S(1)}, f16[16,4096]{1,0:T(8,128)(2,1)S(1)}, u32[]{:S(2)}, u32[]{:S(2)}) %collective-permute-start.13) | collective-permute-done | bytes 131104 | tf_op jit(solution)/shard_map/ppermute | solution.py:226
  51.9 1.8 %collective-permute-start.16 = (f16[16,4096]{1,0:T(8,128)(2,1)S(1)}, f16[16,4096]{1,0:T(8,128)(2,1)S(1)}, u32[]{:S(2)}, u32[]{:S(2)}) collective-permute-start(f16[16,4096]{1,0:T(8,128)(2,1)S(1)} %add_convert_fusion), channel_id=1, source_target_pairs={{0,4},{1,5},{2,6},{3,7},{4,0},{5,1},{6,2},{7,3},{8,12},{9,13},{10,... | collective-permute-start | bytes 393224 | tf_op jit(solution)/shard_map/ppermute | solution.py:226
  54.3 3.4 %shard_map.105 = (f32[128,2048]{1,0:T(8,128)}, f32[128,2048]{1,0:T(8,128)}) custom-call(bf16[128,4224]{1,0:T(8,128)(2,1)S(1)} %constant_dynamic-update-slice_fusion.rows_ref.digits_ref, bf16[128,4224]{1,0:T(8,128)(2,1)S(1)} %constant_dynamic-update-slice_fusion.rows_ref.digits_ref, f32[8,128]{1,0:T(8,128)S(1)} %shard_map.99.lines_ref, ...), custom_call_target="tpu_custom_call" | custom-call | flops 67108864 | bytes 6291456 | tf_op jit(solution)/shard_map/pallas_call | solution.py:202
  57.9 0.8 %multiply_convert_fusion = bf16[16,4096]{1,0:T(8,128)(2,1)} fusion(f16[16,4096]{1,0:T(8,128)(2,1)S(1)} %collective-permute-done.16, f16[16,4096]{1,0:T(8,128)(2,1)S(1)} %collective-permute-done.12, f16[16,4096]{1,0:T(8,128)(2,1)S(1)} %collective-permute-done.11, f16[16,4096]{1,0:T(8,128)(2,1)S(1)} %collective-permute-done.10, ...), kind=kLoop, calls=%fused_computation.2 | loop fusion | flops 655360 | bytes 917504 | tf_op jit(solution)/shard_map/convert_element_type | solution.py:323
  (45 shorter events, 6.8 us)
Async XLA Ops:
  0.6 0.9 %copy-start.3 = (bf16[16,4096]{1,0:T(8,128)(2,1)S(1)}, bf16[16,4096]{1,0:T(8,128)(2,1)}, u32[]{:S(2)}) copy-start(bf16[16,4096]{1,0:T(8,128)(2,1)} %rows_ref.1) | copy-start | bytes 393220
  1.5 0.7 %copy-start.4 = (s32[16]{0:T(128)S(1)}, s32[16]{0:T(128)}, u32[]{:S(2)}) copy-start(s32[16]{0:T(128)} %targets_ref.1) | copy-start | bytes 196
  2.8 17.7 %collective-permute-start.6 = (bf16[16,4224]{1,0:T(8,128)(2,1)S(1)}, bf16[16,4224]{1,0:T(8,128)(2,1)S(1)}, u32[]{:S(2)}, u32[]{:S(2)}) collective-permute-start(bf16[16,4224]{1,0:T(8,128)(2,1)S(1)} %shard_map.93), channel_id=1, source_target_pairs={{0,3},{1,2},{2,1},{3,0},{4,7},{5,6},{6,5},{7,4},{8,11},{9,10},{10,... | collective-permute-start | bytes 405512 | tf_op jit(solution)/shard_map/ppermute | solution.py:226
  6.8 13.6 %collective-permute-start.5 = (bf16[16,4224]{1,0:T(8,128)(2,1)S(1)}, bf16[16,4224]{1,0:T(8,128)(2,1)S(1)}, u32[]{:S(2)}, u32[]{:S(2)}) collective-permute-start(bf16[16,4224]{1,0:T(8,128)(2,1)S(1)} %shard_map.93), channel_id=1, source_target_pairs={{0,2},{1,3},{2,0},{3,1},{4,6},{5,7},{6,4},{7,5},{8,10},{9,11},{10,... | collective-permute-start | bytes 405512 | tf_op jit(solution)/shard_map/ppermute | solution.py:226
  7.3 12.7 %collective-permute-start.4 = (bf16[16,4224]{1,0:T(8,128)(2,1)S(1)}, bf16[16,4224]{1,0:T(8,128)(2,1)S(1)}, u32[]{:S(2)}, u32[]{:S(2)}) collective-permute-start(bf16[16,4224]{1,0:T(8,128)(2,1)S(1)} %shard_map.93), channel_id=1, source_target_pairs={{0,1},{1,0},{2,3},{3,2},{4,5},{5,4},{6,7},{7,6},{8,9},{9,8},{10,11... | collective-permute-start | bytes 405512 | tf_op jit(solution)/shard_map/ppermute | solution.py:226
  7.5 9.4 %collective-permute-start = (bf16[16,4224]{1,0:T(8,128)(2,1)S(1)}, bf16[16,4224]{1,0:T(8,128)(2,1)S(1)}, u32[]{:S(2)}, u32[]{:S(2)}) collective-permute-start(bf16[16,4224]{1,0:T(8,128)(2,1)S(1)} %shard_map.93), channel_id=1, source_target_pairs={{0,4},{1,5},{2,6},{3,7},{4,0},{5,1},{6,2},{7,3},{8,12},{9,13},{10,... | collective-permute-start | bytes 405512 | tf_op jit(solution)/shard_map/ppermute | solution.py:226
  16.9 7.7 %collective-permute-start.3 = (bf16[16,4224]{1,0:T(8,128)(2,1)S(1)}, bf16[16,4224]{1,0:T(8,128)(2,1)S(1)}, u32[]{:S(2)}, u32[]{:S(2)}) collective-permute-start(bf16[16,4224]{1,0:T(8,128)(2,1)S(1)} %collective-permute-done), channel_id=1, source_target_pairs={{0,3},{1,2},{2,1},{3,0},{4,7},{5,6},{6,5},{7,4},{8,11},{9,10},{10,... | collective-permute-start | bytes 405512 | tf_op jit(solution)/shard_map/ppermute | solution.py:226
  19.5 5.5 %collective-permute-start.2 = (bf16[16,4224]{1,0:T(8,128)(2,1)S(1)}, bf16[16,4224]{1,0:T(8,128)(2,1)S(1)}, u32[]{:S(2)}, u32[]{:S(2)}) collective-permute-start(bf16[16,4224]{1,0:T(8,128)(2,1)S(1)} %collective-permute-done), channel_id=1, source_target_pairs={{0,2},{1,3},{2,0},{3,1},{4,6},{5,7},{6,4},{7,5},{8,10},{9,11},{10,... | collective-permute-start | bytes 405512 | tf_op jit(solution)/shard_map/ppermute | solution.py:226
  19.9 5.4 %collective-permute-start.1 = (bf16[16,4224]{1,0:T(8,128)(2,1)S(1)}, bf16[16,4224]{1,0:T(8,128)(2,1)S(1)}, u32[]{:S(2)}, u32[]{:S(2)}) collective-permute-start(bf16[16,4224]{1,0:T(8,128)(2,1)S(1)} %collective-permute-done), channel_id=1, source_target_pairs={{0,1},{1,0},{2,3},{3,2},{4,5},{5,4},{6,7},{7,6},{8,9},{9,8},{10,11... | collective-permute-start | bytes 405512 | tf_op jit(solution)/shard_map/ppermute | solution.py:226
  29.5 4.5 %collective-permute-start.7 = (f32[8,128]{1,0:T(8,128)S(1)}, f32[8,128]{1,0:T(8,128)S(1)}, u32[]{:S(2)}, u32[]{:S(2)}) collective-permute-start(f32[8,128]{1,0:T(8,128)S(1)} %get-tuple-element.17.mine_ref), channel_id=1, source_target_pairs={{0,4},{1,5},{2,6},{3,7},{4,0},{5,1},{6,2},{7,3},{8,12},{9,13},{10,... | collective-permute-start | bytes 12296 | tf_op jit(solution)/shard_map/ppermute | solution.py:226
  34.1 3.7 %collective-permute-start.8 = (f32[8,128]{1,0:T(8,128)S(1)}, f32[8,128]{1,0:T(8,128)S(1)}, u32[]{:S(2)}, u32[]{:S(2)}) collective-permute-start(f32[8,128]{1,0:T(8,128)S(1)} %shard_map.97.mine_ref), channel_id=1, source_target_pairs={{0,2},{1,3},{2,0},{3,1},{4,6},{5,7},{6,4},{7,5},{8,10},{9,11},{10,... | collective-permute-start | bytes 12296 | tf_op jit(solution)/shard_map/ppermute | solution.py:226
  37.8 3.7 %collective-permute-start.9 = (f32[8,128]{1,0:T(8,128)S(1)}, f32[8,128]{1,0:T(8,128)S(1)}, u32[]{:S(2)}, u32[]{:S(2)}) collective-permute-start(f32[8,128]{1,0:T(8,128)S(1)} %shard_map.98.mine_ref), channel_id=1, source_target_pairs={{0,1},{1,0},{2,3},{3,2},{4,5},{5,4},{6,7},{7,6},{8,9},{9,8},{10,11... | collective-permute-start | bytes 12296 | tf_op jit(solution)/shard_map/ppermute | solution.py:226
  42.4 12.0 %copy-start.2 = (f32[128,2048]{1,0:T(8,128)S(1)}, f32[128,2048]{1,0:T(8,128)}, u32[]{:S(2)}) copy-start(f32[128,2048]{1,0:T(8,128)} %peer_ref.1) | copy-start | bytes 3145732
  42.5 11.8 %copy-start = (f32[128,2048]{1,0:T(8,128)S(1)}, f32[128,2048]{1,0:T(8,128)}, u32[]{:S(2)}) copy-start(f32[128,2048]{1,0:T(8,128)} %global_ref.1) | copy-start | bytes 3145732
  42.5 11.8 %copy-start.1 = (f32[128,2048]{1,0:T(8,128)S(1)}, f32[128,2048]{1,0:T(8,128)}, u32[]{:S(2)}) copy-start(f32[128,2048]{1,0:T(8,128)} %momentum_ref.1) | copy-start | bytes 3145732
  42.5 6.9 %collective-permute-start.15 = (f16[16,4096]{1,0:T(8,128)(2,1)S(1)}, f16[16,4096]{1,0:T(8,128)(2,1)S(1)}, u32[]{:S(2)}, u32[]{:S(2)}) collective-permute-start(f16[16,4096]{1,0:T(8,128)(2,1)S(1)} %get-tuple-element.27), channel_id=1, source_target_pairs={{0,1},{1,0},{2,3},{3,2},{4,5},{5,4},{6,7},{7,6},{8,9},{9,8},{10,11... | collective-permute-start | bytes 393224 | tf_op jit(solution)/shard_map/ppermute | solution.py:226
  43.7 6.4 %collective-permute-start.14 = (f16[16,4096]{1,0:T(8,128)(2,1)S(1)}, f16[16,4096]{1,0:T(8,128)(2,1)S(1)}, u32[]{:S(2)}, u32[]{:S(2)}) collective-permute-start(f16[16,4096]{1,0:T(8,128)(2,1)S(1)} %get-tuple-element.28), channel_id=1, source_target_pairs={{0,2},{1,3},{2,0},{3,1},{4,6},{5,7},{6,4},{7,5},{8,10},{9,11},{10,... | collective-permute-start | bytes 393224 | tf_op jit(solution)/shard_map/ppermute | solution.py:226
  45.3 6.6 %collective-permute-start.13 = (f16[16,4096]{1,0:T(8,128)(2,1)S(1)}, f16[16,4096]{1,0:T(8,128)(2,1)S(1)}, u32[]{:S(2)}, u32[]{:S(2)}) collective-permute-start(f16[16,4096]{1,0:T(8,128)(2,1)S(1)} %get-tuple-element.29), channel_id=1, source_target_pairs={{0,3},{1,2},{2,1},{3,0},{4,7},{5,6},{6,5},{7,4},{8,11},{9,10},{10,... | collective-permute-start | bytes 393224 | tf_op jit(solution)/shard_map/ppermute | solution.py:226
  46.1 11.6 %collective-permute-start.10 = (f16[16,4096]{1,0:T(8,128)(2,1)S(1)}, f16[16,4096]{1,0:T(8,128)(2,1)S(1)}, u32[]{:S(2)}, u32[]{:S(2)}) collective-permute-start(f16[16,4096]{1,0:T(8,128)(2,1)S(1)} %get-tuple-element.26), channel_id=1, source_target_pairs={{0,3},{1,2},{2,1},{3,0},{4,7},{5,6},{6,5},{7,4},{8,11},{9,10},{10,... | collective-permute-start | bytes 393224 | tf_op jit(solution)/shard_map/ppermute | solution.py:226
  48.3 9.4 %collective-permute-start.12 = (f16[16,4096]{1,0:T(8,128)(2,1)S(1)}, f16[16,4096]{1,0:T(8,128)(2,1)S(1)}, u32[]{:S(2)}, u32[]{:S(2)}) collective-permute-start(f16[16,4096]{1,0:T(8,128)(2,1)S(1)} %get-tuple-element.30), channel_id=1, source_target_pairs={{0,1},{1,0},{2,3},{3,2},{4,5},{5,4},{6,7},{7,6},{8,9},{9,8},{10,11... | collective-permute-start | bytes 393224 | tf_op jit(solution)/shard_map/ppermute | solution.py:226
  49.5 8.2 %collective-permute-start.11 = (f16[16,4096]{1,0:T(8,128)(2,1)S(1)}, f16[16,4096]{1,0:T(8,128)(2,1)S(1)}, u32[]{:S(2)}, u32[]{:S(2)}) collective-permute-start(f16[16,4096]{1,0:T(8,128)(2,1)S(1)} %get-tuple-element.31), channel_id=1, source_target_pairs={{0,2},{1,3},{2,0},{3,1},{4,6},{5,7},{6,4},{7,5},{8,10},{9,11},{10,... | collective-permute-start | bytes 393224 | tf_op jit(solution)/shard_map/ppermute | solution.py:226
  51.9 5.9 %collective-permute-start.16 = (f16[16,4096]{1,0:T(8,128)(2,1)S(1)}, f16[16,4096]{1,0:T(8,128)(2,1)S(1)}, u32[]{:S(2)}, u32[]{:S(2)}) collective-permute-start(f16[16,4096]{1,0:T(8,128)(2,1)S(1)} %add_convert_fusion), channel_id=1, source_target_pairs={{0,4},{1,5},{2,6},{3,7},{4,0},{5,1},{6,2},{7,3},{8,12},{9,13},{10,... | collective-permute-start | bytes 393224 | tf_op jit(solution)/shard_map/ppermute | solution.py:226

commit v8 on v7

--- a/solution.py
+++ b/solution.py
@@ -30,7 +30,7 @@
     )(*[pltpu.with_memory_space_constraint(x, place) for x, place in zip(operands, places)])
 
 
-def load_kernel(source, target, token_ref, sems):
+def load_kernel(source, target, sems):
     block = source.shape[0] // sems.shape[0]
     copies = []
     for i in range(sems.shape[0]):
@@ -40,29 +40,34 @@
         copy.start()
     for copy in copies:
         copy.wait()
-    token_ref[...] = jnp.zeros_like(token_ref)
 
 
 def resident(head):
     return call(
-        load_kernel, [(head.shape, head.dtype), ((8, LANES), jnp.float32)], [head],
+        load_kernel, [(head.shape, head.dtype)], [head],
         scratch=[pltpu.SemaphoreType.DMA((4,))], sources=[pltpu.HBM],
-    )
+    )[0]
 
 
 TILE = 512
-
-
-def pack_kernel(targets_ref, rows_ref, out_ref):
-    own, depth = rows_ref.shape
+WIDE = 1024
+
+
+def pack_kernel(targets, rows, out_ref, targets_ref, sems):
+    own, depth = rows.shape
+    ids_copy = pltpu.make_async_copy(targets, targets_ref, sems.at[0])
+    rows_copy = pltpu.make_async_copy(rows, out_ref.at[:, pl.ds(0, depth)], sems.at[1])
+    ids_copy.start()
+    rows_copy.start()
+    ids_copy.wait()
     place = lax.broadcasted_iota(jnp.int32, (own, LANES), 0)
     ids = jnp.zeros((own, LANES), jnp.int32)
     for i in range(own):
         ids = jnp.where(place == i, targets_ref[i], ids)
     lane = lax.broadcasted_iota(jnp.int32, (own, LANES), 1)
     digits = jnp.where(lane == 0, ids // 256, ids % 256)
-    out_ref[:, :depth] = rows_ref[...]
     out_ref[:, depth:] = digits.astype(jnp.float32).astype(jnp.bfloat16)
+    rows_copy.wait()
 
 
 def ids_of(digits):
@@ -96,9 +101,9 @@
     rows = rows_ref.shape[0]
     depth, width = near_ref.shape
 
-    @pl.loop(0, width // TILE)
+    @pl.loop(0, width // WIDE)
     def _(i):
-        part = pl.ds(pl.multiple_of(i * TILE, TILE), TILE)
+        part = pl.ds(pl.multiple_of(i * WIDE, WIDE), WIDE)
         logits_ref[:, part] = jnp.dot(
             rows_ref[:, :depth], near_ref[:, part], preferred_element_type=jnp.float32
         )
@@ -130,15 +135,27 @@
         stats_ref[...] = columns_ref[...].T[:8]
 
 
-def merge_kernel(step, members, mine_ref, other_ref, out_ref):
-    mine = mine_ref[...]
-    other = swap_blocks(other_ref[...], mine.shape[1] // members * step)
-    upper = (lax.axis_index(AXIS) & step) != 0
-    one, two = jnp.where(upper, other, mine), jnp.where(upper, mine, other)
-    top = jnp.maximum(one[0:1], two[0:1])
-    total = one[1:2] * jnp.exp(one[0:1] - top) + two[1:2] * jnp.exp(two[0:1] - top)
-    pick = one[2:3] + two[2:3]
-    place = lax.broadcasted_iota(jnp.int32, mine.shape, 0)
+def merge_kernel(steps, members, mine_ref, *refs):
+    *other_refs, out_ref = refs
+    block = mine_ref.shape[1] // members
+    me = lax.axis_index(AXIS)
+    groups = [mine_ref[...]]
+    for step, other_ref in zip(steps, other_refs):
+        other, bit = other_ref[...], 1
+        while bit <= step:
+            if step & bit:
+                other = swap_blocks(other, block * bit)
+            bit *= 2
+        groups.append(other)
+    unit, bit = steps[0], 1
+    while bit < len(groups):
+        upper = (me & (unit * bit)) != 0
+        groups = [jnp.where(upper, groups[i ^ bit], group) for i, group in enumerate(groups)]
+        bit *= 2
+    top = functools.reduce(jnp.maximum, [group[0:1] for group in groups])
+    total = sum(group[1:2] * jnp.exp(group[0:1] - top) for group in groups)
+    pick = sum(group[2:3] for group in groups)
+    place = lax.broadcasted_iota(jnp.int32, out_ref.shape, 0)
     out_ref[...] = jnp.where(place == 0, top, jnp.where(place == 1, total, pick))
 
 
@@ -235,12 +252,11 @@
     return steps
 
 
-def gather_rows(packed, token):
+def gather_rows(packed):
     own = packed.shape[0]
     held = packed
     for step in far_steps()[:1]:
         held = jnp.concatenate([held, swap(held, step)], axis=0)
-    packed, _ = lax.optimization_barrier((packed, token))
     near = [packed] + [swap(packed, step) for step in (3, 2, 1)][::-1]
     for step in far_steps()[1:]:
         held = jnp.concatenate([held, swap(held, step)], axis=0)
@@ -279,10 +295,11 @@
 
     packed = call(
         pack_kernel, [((own, depth + LANES), hidden.dtype)], [targets, hidden],
-        sources=[pltpu.SMEM, pltpu.VMEM],
+        scratch=[pltpu.SMEM(targets.shape, targets.dtype), pltpu.SemaphoreType.DMA((2,))],
+        sources=[pltpu.HBM, pltpu.HBM],
     )[0]
-    near, token = resident(head)
-    rows_near, rows_far = gather_rows(packed, token)
+    rows_near, rows_far = gather_rows(packed)
+    near = resident(head)
 
     def part(held, *before):
         count = held.shape[0]
@@ -298,10 +315,10 @@
     logits_far, both_far, mine = part(rows_far, columns)
 
     lines = mine
-    for step in far_steps()[::-1] + [2, 1]:
+    for steps in [[step] for step in far_steps()] + [[1, 2, 3]]:
         lines = call(
-            functools.partial(merge_kernel, step, members),
-            [((8, rows), jnp.float32)], [lines, swap(lines, step)],
+            functools.partial(merge_kernel, steps, members),
+            [((8, rows), jnp.float32)], [lines] + [swap(lines, step) for step in steps],
         )[0]
 
     cuts = 4

time: 58.8 us -> 61.4 us (1.044)
  waiting for transfers between devices: 4.23 us -> 7.74 us
  local copies, waits for them, and re-layouts: 2.32 us -> 0.77 us
  starting transfers between devices: 25.4 us -> 26.8 us
  Pallas kernels: 24.8 us -> 24.1 us
    ppermute x17 -> x18, waiting for transfers between devices: 4.23 us -> 7.74 us  [swap(): lax.ppermute(value, AXIS, [(i, i ^ step) for i in range(lax.axis_size(AXI...]
    unnamed x14 -> x10, local copies, waits for them, and re-layouts: 1.63 us -> 0.08 us
    ppermute x17 -> x18, starting transfers between devices: 25.4 us -> 26.8 us  [swap(): lax.ppermute(value, AXIS, [(i, i ^ step) for i in range(lax.axis_size(AXI...]
    pallas_call x12 -> x11, Pallas kernels: 21.4 us -> 20.7 us  [call(): pl.pallas_call(kernel, out_shape=outs, in_specs=[pl.BlockSpec(memory_spac...]
  transfers between devices with their start and end apart: 17 -> 18, of which waited for: 6 -> 7; matrix products, arithmetic and copies ran while one was open for 1% -> 1% of each run, Pallas kernels for 33% -> 26%
where the time goes in v8:
time: 61.4 us; the launch traced here: 61.3 us
  starting transfers between devices  26.8 us (44%)
  Pallas kernels  24.1 us (39%)
  waiting for transfers between devices  7.74 us (13%)
  other arithmetic  1.07 us (2%)
  between operations  0.81 us (1%)
  local copies, waits for them, and re-layouts  0.77 us (1%)
    ppermute x18, starting transfers between devices, swap(): lax.ppermute(value, AXIS, [(i, i ^ step) for i in range(lax.axis_size(AXI...  26.8 us
    pallas_call x11, Pallas kernels, call(): pl.pallas_call(kernel, out_shape=outs, in_specs=[pl.BlockSpec(memory_spac...  20.7 us
    ppermute x18, waiting for transfers between devices, swap(): lax.ppermute(value, AXIS, [(i, i ^ step) for i in range(lax.axis_size(AXI...  7.74 us
    pallas_call x1, Pallas kernels, frag_update(): pl.pallas_call(frag_kernel, grid=(width // TILE,), out_shape=[jax.ShapeDt...  3.36 us
  transfers between devices with their start and end apart: 18, of which 7 were waited for; matrix products, arithmetic and copies ran while one was open for 1% of the time, Pallas kernels for 26%

profile of v8, /device:TPU:0, one launch (start us, length us, event | category | flops | bytes accessed | tf_op | source)
XLA Modules:
  0.0 61.3 jit_solution(7735969697394917461)
XLA Ops:
  0.6 0.9 %shard_map.93 = bf16[16,4224]{1,0:T(8,128)(2,1)S(1)} custom-call(s32[16]{0:T(128)} %targets.1, bf16[16,4096]{1,0:T(8,128)(2,1)} %rows.1), custom_call_target="tpu_custom_call" | custom-call | bytes 131136 | tf_op jit(solution)/shard_map/pallas_call | solution.py:22
  1.6 4.0 %collective-permute-start.6 = (bf16[16,4224]{1,0:T(8,128)(2,1)S(1)}, bf16[16,4224]{1,0:T(8,128)(2,1)S(1)}, u32[]{:S(2)}, u32[]{:S(2)}) collective-permute-start(bf16[16,4224]{1,0:T(8,128)(2,1)S(1)} %shard_map.93), channel_id=1, source_target_pairs={{0,3},{1,2},{2,1},{3,0},{4,7},{5,6},{6,5},{7,4},{8,11},{9,10},{10,... | collective-permute-start | bytes 405512 | tf_op jit(solution)/shard_map/ppermute | solution.py:243
  6.3 2.9 %collective-permute-start = (bf16[16,4224]{1,0:T(8,128)(2,1)S(1)}, bf16[16,4224]{1,0:T(8,128)(2,1)S(1)}, u32[]{:S(2)}, u32[]{:S(2)}) collective-permute-start(bf16[16,4224]{1,0:T(8,128)(2,1)S(1)} %shard_map.93), channel_id=1, source_target_pairs={{0,4},{1,5},{2,6},{3,7},{4,0},{5,1},{6,2},{7,3},{8,12},{9,13},{10,... | collective-permute-start | bytes 405512 | tf_op jit(solution)/shard_map/ppermute | solution.py:243
  9.2 5.9 %shard_map.94.near_ref.head_ref = bf16[4096,2048]{1,0:T(8,128)(2,1)S(1)} custom-call(bf16[4096,2048]{1,0:T(8,128)(2,1)} %source.1), custom_call_target="tpu_custom_call" | custom-call | bytes 16777216 | tf_op jit(solution)/shard_map/pallas_call | solution.py:22
  15.1 2.6 %collective-permute-start.3 = (bf16[16,4224]{1,0:T(8,128)(2,1)S(1)}, bf16[16,4224]{1,0:T(8,128)(2,1)S(1)}, u32[]{:S(2)}, u32[]{:S(2)}) collective-permute-start(bf16[16,4224]{1,0:T(8,128)(2,1)S(1)} %collective-permute-done), channel_id=1, source_target_pairs={{0,3},{1,2},{2,1},{3,0},{4,7},{5,6},{6,5},{7,4},{8,11},{9,10},{10,... | collective-permute-start | bytes 405512 | tf_op jit(solution)/shard_map/ppermute | solution.py:243
  18.1 1.1 %collective-permute-start.1 = (bf16[16,4224]{1,0:T(8,128)(2,1)S(1)}, bf16[16,4224]{1,0:T(8,128)(2,1)S(1)}, u32[]{:S(2)}, u32[]{:S(2)}) collective-permute-start(bf16[16,4224]{1,0:T(8,128)(2,1)S(1)} %collective-permute-done), channel_id=1, source_target_pairs={{0,1},{1,0},{2,3},{3,2},{4,5},{5,4},{6,7},{7,6},{8,9},{9,8},{10,11... | collective-permute-start | bytes 405512 | tf_op jit(solution)/shard_map/ppermute | solution.py:243
  19.3 3.8 %shard_map.95 = (f32[64,2048]{1,0:T(8,128)S(1)}, bf16[128,2048]{1,0:T(8,128)(2,1)S(1)}, f32[64,128]{1,0:T(8,128)S(1)}) custom-call(bf16[64,4224]{1,0:T(8,128)(2,1)S(1)} %pad_maximum_fusion.1.rows_ref, bf16[4096,2048]{1,0:T(8,128)(2,1)S(1)} %shard_map.94.near_ref.head_ref), custom_call_target="tpu_custom_call" | custom-call | flops 1073741824 | bytes 17317888 | tf_op jit(solution)/shard_map/pallas_call | solution.py:22
  23.5 3.8 %shard_map.96 = (f32[64,2048]{1,0:T(8,128)S(1)}, bf16[128,2048]{1,0:T(8,128)(2,1)S(1)}, f32[8,128]{1,0:T(8,128)S(1)}) custom-call(bf16[64,4224]{1,0:T(8,128)(2,1)S(1)} %bitcast.6, bf16[4096,2048]{1,0:T(8,128)(2,1)S(1)} %shard_map.94.near_ref.head_ref, f32[64,128]{1,0:T(8,128)S(1)} %get-tuple-element.14.refs_0_), custom_call_target="tpu_custom_call" | custom-call | flops 1073741824 | bytes 17350656 | tf_op jit(solution)/shard_map/pallas_call | solution.py:22
  27.3 1.4 %shard_map.102.refs_3_ = f32[256,1024]{1,0:T(8,128)S(1)} custom-call(bf16[128,2048]{1,0:T(8,128)(2,1)S(1)} %get-tuple-element.16.one_ref, bf16[128,2048]{1,0:T(8,128)(2,1)S(1)} %get-tuple-element.17.two_ref, bf16[4096,2048]{1,0:T(8,128)(2,1)S(1)} %shard_map.94.near_ref.head_ref), custom_call_target="tpu_custom_call" | custom-call | flops 1073741824 | bytes 17825792 | tf_op jit(solution)/shard_map/pallas_call | solution.py:22
  28.7 1.4 %shard_map.101.refs_2_ = f32[256,1024]{1,0:T(8,128)S(1)} custom-call(bf16[128,2048]{1,0:T(8,128)(2,1)S(1)} %get-tuple-element.16.one_ref, bf16[128,2048]{1,0:T(8,128)(2,1)S(1)} %get-tuple-element.17.two_ref, bf16[4096,2048]{1,0:T(8,128)(2,1)S(1)} %shard_map.94.near_ref.head_ref), custom_call_target="tpu_custom_call" | custom-call | flops 1073741824 | bytes 17825792 | tf_op jit(solution)/shard_map/pallas_call | solution.py:22
  30.0 2.5 %collective-permute-start.7 = (f32[8,128]{1,0:T(8,128)S(1)}, f32[8,128]{1,0:T(8,128)S(1)}, u32[]{:S(2)}, u32[]{:S(2)}) collective-permute-start(f32[8,128]{1,0:T(8,128)S(1)} %get-tuple-element.15.mine_ref), channel_id=1, source_target_pairs={{0,4},{1,5},{2,6},{3,7},{4,0},{5,1},{6,2},{7,3},{8,12},{9,13},{10,... | collective-permute-start | bytes 12296 | tf_op jit(solution)/shard_map/ppermute | solution.py:243
  32.6 1.4 %shard_map.100.refs_1_ = f32[256,1024]{1,0:T(8,128)S(1)} custom-call(bf16[128,2048]{1,0:T(8,128)(2,1)S(1)} %get-tuple-element.16.one_ref, bf16[128,2048]{1,0:T(8,128)(2,1)S(1)} %get-tuple-element.17.two_ref, bf16[4096,2048]{1,0:T(8,128)(2,1)S(1)} %shard_map.94.near_ref.head_ref), custom_call_target="tpu_custom_call" | custom-call | flops 1073741824 | bytes 17825792 | tf_op jit(solution)/shard_map/pallas_call | solution.py:22
  34.7 2.6 %collective-permute-start.10 = (f32[8,128]{1,0:T(8,128)S(1)}, f32[8,128]{1,0:T(8,128)S(1)}, u32[]{:S(2)}, u32[]{:S(2)}) collective-permute-start(f32[8,128]{1,0:T(8,128)S(1)} %shard_map.97.mine_ref), channel_id=1, source_target_pairs={{0,3},{1,2},{2,1},{3,0},{4,7},{5,6},{6,5},{7,4},{8,11},{9,10},{10,... | collective-permute-start | bytes 12296 | tf_op jit(solution)/shard_map/ppermute | solution.py:243
  37.7 1.1 %collective-permute-start.8 = (f32[8,128]{1,0:T(8,128)S(1)}, f32[8,128]{1,0:T(8,128)S(1)}, u32[]{:S(2)}, u32[]{:S(2)}) collective-permute-start(f32[8,128]{1,0:T(8,128)S(1)} %shard_map.97.mine_ref), channel_id=1, source_target_pairs={{0,1},{1,0},{2,3},{3,2},{4,5},{5,4},{6,7},{7,6},{8,9},{9,8},{10,11... | collective-permute-start | bytes 12296 | tf_op jit(solution)/shard_map/ppermute | solution.py:243
  38.8 1.4 %shard_map.99.refs_0_ = f32[256,1024]{1,0:T(8,128)S(1)} custom-call(bf16[128,2048]{1,0:T(8,128)(2,1)S(1)} %get-tuple-element.16.one_ref, bf16[128,2048]{1,0:T(8,128)(2,1)S(1)} %get-tuple-element.17.two_ref, bf16[4096,2048]{1,0:T(8,128)(2,1)S(1)} %shard_map.94.near_ref.head_ref), custom_call_target="tpu_custom_call" | custom-call | flops 1073741824 | bytes 17825792 | tf_op jit(solution)/shard_map/pallas_call | solution.py:22
  40.2 0.8 %collective-permute-done.9.refs_1_ = f32[8,128]{1,0:T(8,128)S(1)} collective-permute-done((f32[8,128]{1,0:T(8,128)S(1)}, f32[8,128]{1,0:T(8,128)S(1)}, u32[]{:S(2)}, u32[]{:S(2)}) %collective-permute-start.9) | collective-permute-done | bytes 4128 | tf_op jit(solution)/shard_map/ppermute | solution.py:243
  42.4 1.1 %collective-permute-start.16 = (f16[16,4096]{1,0:T(8,128)(2,1)S(1)}, f16[16,4096]{1,0:T(8,128)(2,1)S(1)}, u32[]{:S(2)}, u32[]{:S(2)}) collective-permute-start(f16[16,4096]{1,0:T(8,128)(2,1)S(1)} %get-tuple-element.25), channel_id=1, source_target_pairs={{0,1},{1,0},{2,3},{3,2},{4,5},{5,4},{6,7},{7,6},{8,9},{9,8},{10,11... | collective-permute-start | bytes 393224 | tf_op jit(solution)/shard_map/ppermute | solution.py:243
  43.6 2.1 %collective-permute-start.15 = (f16[16,4096]{1,0:T(8,128)(2,1)S(1)}, f16[16,4096]{1,0:T(8,128)(2,1)S(1)}, u32[]{:S(2)}, u32[]{:S(2)}) collective-permute-start(f16[16,4096]{1,0:T(8,128)(2,1)S(1)} %get-tuple-element.26), channel_id=1, source_target_pairs={{0,2},{1,3},{2,0},{3,1},{4,6},{5,7},{6,4},{7,5},{8,10},{9,11},{10,... | collective-permute-start | bytes 393224 | tf_op jit(solution)/shard_map/ppermute | solution.py:243
  46.0 2.6 %collective-permute-start.11 = (f16[16,4096]{1,0:T(8,128)(2,1)S(1)}, f16[16,4096]{1,0:T(8,128)(2,1)S(1)}, u32[]{:S(2)}, u32[]{:S(2)}) collective-permute-start(f16[16,4096]{1,0:T(8,128)(2,1)S(1)} %get-tuple-element.24), channel_id=1, source_target_pairs={{0,3},{1,2},{2,1},{3,0},{4,7},{5,6},{6,5},{7,4},{8,11},{9,10},{10,... | collective-permute-start | bytes 393224 | tf_op jit(solution)/shard_map/ppermute | solution.py:243
  49.2 1.0 %collective-permute-done.16 = f16[16,4096]{1,0:T(8,128)(2,1)S(1)} collective-permute-done((f16[16,4096]{1,0:T(8,128)(2,1)S(1)}, f16[16,4096]{1,0:T(8,128)(2,1)S(1)}, u32[]{:S(2)}, u32[]{:S(2)}) %collective-permute-start.16) | collective-permute-done | bytes 131104 | tf_op jit(solution)/shard_map/ppermute | solution.py:243
  50.2 0.9 %collective-permute-start.12 = (f16[16,4096]{1,0:T(8,128)(2,1)S(1)}, f16[16,4096]{1,0:T(8,128)(2,1)S(1)}, u32[]{:S(2)}, u32[]{:S(2)}) collective-permute-start(f16[16,4096]{1,0:T(8,128)(2,1)S(1)} %get-tuple-element.29), channel_id=1, source_target_pairs={{0,2},{1,3},{2,0},{3,1},{4,6},{5,7},{6,4},{7,5},{8,10},{9,11},{10,... | collective-permute-start | bytes 393224 | tf_op jit(solution)/shard_map/ppermute | solution.py:243
  51.1 2.0 %collective-permute-done.14 = f16[16,4096]{1,0:T(8,128)(2,1)S(1)} collective-permute-done((f16[16,4096]{1,0:T(8,128)(2,1)S(1)}, f16[16,4096]{1,0:T(8,128)(2,1)S(1)}, u32[]{:S(2)}, u32[]{:S(2)}) %collective-permute-start.14) | collective-permute-done | bytes 131104 | tf_op jit(solution)/shard_map/ppermute | solution.py:243
  54.5 3.4 %shard_map.104 = (f32[128,2048]{1,0:T(8,128)}, f32[128,2048]{1,0:T(8,128)}) custom-call(bf16[128,4224]{1,0:T(8,128)(2,1)S(1)} %constant_dynamic-update-slice_fusion.rows_ref.digits_ref, bf16[128,4224]{1,0:T(8,128)(2,1)S(1)} %constant_dynamic-update-slice_fusion.rows_ref.digits_ref, f32[8,128]{1,0:T(8,128)S(1)} %shard_map.98.lines_ref, ...), custom_call_target="tpu_custom_call" | custom-call | flops 67108864 | bytes 6291456 | tf_op jit(solution)/shard_map/pallas_call | solution.py:219
  57.9 2.6 %collective-permute-done.17 = f16[16,4096]{1,0:T(8,128)(2,1)S(1)} collective-permute-done((f16[16,4096]{1,0:T(8,128)(2,1)S(1)}, f16[16,4096]{1,0:T(8,128)(2,1)S(1)}, u32[]{:S(2)}, u32[]{:S(2)}) %collective-permute-start.17) | collective-permute-done | bytes 131104 | tf_op jit(solution)/shard_map/ppermute | solution.py:243
  (42 shorter events, 7.2 us)
Async XLA Ops:
  1.6 17.7 %collective-permute-start.6 = (bf16[16,4224]{1,0:T(8,128)(2,1)S(1)}, bf16[16,4224]{1,0:T(8,128)(2,1)S(1)}, u32[]{:S(2)}, u32[]{:S(2)}) collective-permute-start(bf16[16,4224]{1,0:T(8,128)(2,1)S(1)} %shard_map.93), channel_id=1, source_target_pairs={{0,3},{1,2},{2,1},{3,0},{4,7},{5,6},{6,5},{7,4},{8,11},{9,10},{10,... | collective-permute-start | bytes 405512 | tf_op jit(solution)/shard_map/ppermute | solution.py:243
  5.6 13.6 %collective-permute-start.5 = (bf16[16,4224]{1,0:T(8,128)(2,1)S(1)}, bf16[16,4224]{1,0:T(8,128)(2,1)S(1)}, u32[]{:S(2)}, u32[]{:S(2)}) collective-permute-start(bf16[16,4224]{1,0:T(8,128)(2,1)S(1)} %shard_map.93), channel_id=1, source_target_pairs={{0,2},{1,3},{2,0},{3,1},{4,6},{5,7},{6,4},{7,5},{8,10},{9,11},{10,... | collective-permute-start | bytes 405512 | tf_op jit(solution)/shard_map/ppermute | solution.py:243
  6.1 12.1 %collective-permute-start.4 = (bf16[16,4224]{1,0:T(8,128)(2,1)S(1)}, bf16[16,4224]{1,0:T(8,128)(2,1)S(1)}, u32[]{:S(2)}, u32[]{:S(2)}) collective-permute-start(bf16[16,4224]{1,0:T(8,128)(2,1)S(1)} %shard_map.93), channel_id=1, source_target_pairs={{0,1},{1,0},{2,3},{3,2},{4,5},{5,4},{6,7},{7,6},{8,9},{9,8},{10,11... | collective-permute-start | bytes 405512 | tf_op jit(solution)/shard_map/ppermute | solution.py:243
  6.3 8.8 %collective-permute-start = (bf16[16,4224]{1,0:T(8,128)(2,1)S(1)}, bf16[16,4224]{1,0:T(8,128)(2,1)S(1)}, u32[]{:S(2)}, u32[]{:S(2)}) collective-permute-start(bf16[16,4224]{1,0:T(8,128)(2,1)S(1)} %shard_map.93), channel_id=1, source_target_pairs={{0,4},{1,5},{2,6},{3,7},{4,0},{5,1},{6,2},{7,3},{8,12},{9,13},{10,... | collective-permute-start | bytes 405512 | tf_op jit(solution)/shard_map/ppermute | solution.py:243
  15.1 8.0 %collective-permute-start.3 = (bf16[16,4224]{1,0:T(8,128)(2,1)S(1)}, bf16[16,4224]{1,0:T(8,128)(2,1)S(1)}, u32[]{:S(2)}, u32[]{:S(2)}) collective-permute-start(bf16[16,4224]{1,0:T(8,128)(2,1)S(1)} %collective-permute-done), channel_id=1, source_target_pairs={{0,3},{1,2},{2,1},{3,0},{4,7},{5,6},{6,5},{7,4},{8,11},{9,10},{10,... | collective-permute-start | bytes 405512 | tf_op jit(solution)/shard_map/ppermute | solution.py:243
  17.7 5.7 %collective-permute-start.2 = (bf16[16,4224]{1,0:T(8,128)(2,1)S(1)}, bf16[16,4224]{1,0:T(8,128)(2,1)S(1)}, u32[]{:S(2)}, u32[]{:S(2)}) collective-permute-start(bf16[16,4224]{1,0:T(8,128)(2,1)S(1)} %collective-permute-done), channel_id=1, source_target_pairs={{0,2},{1,3},{2,0},{3,1},{4,6},{5,7},{6,4},{7,5},{8,10},{9,11},{10,... | collective-permute-start | bytes 405512 | tf_op jit(solution)/shard_map/ppermute | solution.py:243
  18.1 5.3 %collective-permute-start.1 = (bf16[16,4224]{1,0:T(8,128)(2,1)S(1)}, bf16[16,4224]{1,0:T(8,128)(2,1)S(1)}, u32[]{:S(2)}, u32[]{:S(2)}) collective-permute-start(bf16[16,4224]{1,0:T(8,128)(2,1)S(1)} %collective-permute-done), channel_id=1, source_target_pairs={{0,1},{1,0},{2,3},{3,2},{4,5},{5,4},{6,7},{7,6},{8,9},{9,8},{10,11... | collective-permute-start | bytes 405512 | tf_op jit(solution)/shard_map/ppermute | solution.py:243
  30.0 4.6 %collective-permute-start.7 = (f32[8,128]{1,0:T(8,128)S(1)}, f32[8,128]{1,0:T(8,128)S(1)}, u32[]{:S(2)}, u32[]{:S(2)}) collective-permute-start(f32[8,128]{1,0:T(8,128)S(1)} %get-tuple-element.15.mine_ref), channel_id=1, source_target_pairs={{0,4},{1,5},{2,6},{3,7},{4,0},{5,1},{6,2},{7,3},{8,12},{9,13},{10,... | collective-permute-start | bytes 12296 | tf_op jit(solution)/shard_map/ppermute | solution.py:243
  34.7 5.5 %collective-permute-start.10 = (f32[8,128]{1,0:T(8,128)S(1)}, f32[8,128]{1,0:T(8,128)S(1)}, u32[]{:S(2)}, u32[]{:S(2)}) collective-permute-start(f32[8,128]{1,0:T(8,128)S(1)} %shard_map.97.mine_ref), channel_id=1, source_target_pairs={{0,3},{1,2},{2,1},{3,0},{4,7},{5,6},{6,5},{7,4},{8,11},{9,10},{10,... | collective-permute-start | bytes 12296 | tf_op jit(solution)/shard_map/ppermute | solution.py:243
  37.4 3.6 %collective-permute-start.9 = (f32[8,128]{1,0:T(8,128)S(1)}, f32[8,128]{1,0:T(8,128)S(1)}, u32[]{:S(2)}, u32[]{:S(2)}) collective-permute-start(f32[8,128]{1,0:T(8,128)S(1)} %shard_map.97.mine_ref), channel_id=1, source_target_pairs={{0,2},{1,3},{2,0},{3,1},{4,6},{5,7},{6,4},{7,5},{8,10},{9,11},{10,... | collective-permute-start | bytes 12296 | tf_op jit(solution)/shard_map/ppermute | solution.py:243
  37.7 3.7 %collective-permute-start.8 = (f32[8,128]{1,0:T(8,128)S(1)}, f32[8,128]{1,0:T(8,128)S(1)}, u32[]{:S(2)}, u32[]{:S(2)}) collective-permute-start(f32[8,128]{1,0:T(8,128)S(1)} %shard_map.97.mine_ref), channel_id=1, source_target_pairs={{0,1},{1,0},{2,3},{3,2},{4,5},{5,4},{6,7},{7,6},{8,9},{9,8},{10,11... | collective-permute-start | bytes 12296 | tf_op jit(solution)/shard_map/ppermute | solution.py:243
  42.2 12.2 %copy-start.2 = (f32[128,2048]{1,0:T(8,128)S(1)}, f32[128,2048]{1,0:T(8,128)}, u32[]{:S(2)}) copy-start(f32[128,2048]{1,0:T(8,128)} %peer_ref.1) | copy-start | bytes 3145732
  42.4 12.1 %copy-start = (f32[128,2048]{1,0:T(8,128)S(1)}, f32[128,2048]{1,0:T(8,128)}, u32[]{:S(2)}) copy-start(f32[128,2048]{1,0:T(8,128)} %global_ref.1) | copy-start | bytes 3145732
  42.4 12.1 %copy-start.1 = (f32[128,2048]{1,0:T(8,128)S(1)}, f32[128,2048]{1,0:T(8,128)}, u32[]{:S(2)}) copy-start(f32[128,2048]{1,0:T(8,128)} %momentum_ref.1) | copy-start | bytes 3145732
  42.4 7.8 %collective-permute-start.16 = (f16[16,4096]{1,0:T(8,128)(2,1)S(1)}, f16[16,4096]{1,0:T(8,128)(2,1)S(1)}, u32[]{:S(2)}, u32[]{:S(2)}) collective-permute-start(f16[16,4096]{1,0:T(8,128)(2,1)S(1)} %get-tuple-element.25), channel_id=1, source_target_pairs={{0,1},{1,0},{2,3},{3,2},{4,5},{5,4},{6,7},{7,6},{8,9},{9,8},{10,11... | collective-permute-start | bytes 393224 | tf_op jit(solution)/shard_map/ppermute | solution.py:243
  43.6 7.6 %collective-permute-start.15 = (f16[16,4096]{1,0:T(8,128)(2,1)S(1)}, f16[16,4096]{1,0:T(8,128)(2,1)S(1)}, u32[]{:S(2)}, u32[]{:S(2)}) collective-permute-start(f16[16,4096]{1,0:T(8,128)(2,1)S(1)} %get-tuple-element.26), channel_id=1, source_target_pairs={{0,2},{1,3},{2,0},{3,1},{4,6},{5,7},{6,4},{7,5},{8,10},{9,11},{10,... | collective-permute-start | bytes 393224 | tf_op jit(solution)/shard_map/ppermute | solution.py:243
  45.6 7.5 %collective-permute-start.14 = (f16[16,4096]{1,0:T(8,128)(2,1)S(1)}, f16[16,4096]{1,0:T(8,128)(2,1)S(1)}, u32[]{:S(2)}, u32[]{:S(2)}) collective-permute-start(f16[16,4096]{1,0:T(8,128)(2,1)S(1)} %get-tuple-element.27), channel_id=1, source_target_pairs={{0,3},{1,2},{2,1},{3,0},{4,7},{5,6},{6,5},{7,4},{8,11},{9,10},{10,... | collective-permute-start | bytes 393224 | tf_op jit(solution)/shard_map/ppermute | solution.py:243
  46.0 11.9 %collective-permute-start.11 = (f16[16,4096]{1,0:T(8,128)(2,1)S(1)}, f16[16,4096]{1,0:T(8,128)(2,1)S(1)}, u32[]{:S(2)}, u32[]{:S(2)}) collective-permute-start(f16[16,4096]{1,0:T(8,128)(2,1)S(1)} %get-tuple-element.24), channel_id=1, source_target_pairs={{0,3},{1,2},{2,1},{3,0},{4,7},{5,6},{6,5},{7,4},{8,11},{9,10},{10,... | collective-permute-start | bytes 393224 | tf_op jit(solution)/shard_map/ppermute | solution.py:243
  48.6 9.2 %collective-permute-start.13 = (f16[16,4096]{1,0:T(8,128)(2,1)S(1)}, f16[16,4096]{1,0:T(8,128)(2,1)S(1)}, u32[]{:S(2)}, u32[]{:S(2)}) collective-permute-start(f16[16,4096]{1,0:T(8,128)(2,1)S(1)} %get-tuple-element.28), channel_id=1, source_target_pairs={{0,1},{1,0},{2,3},{3,2},{4,5},{5,4},{6,7},{7,6},{8,9},{9,8},{10,11... | collective-permute-start | bytes 393224 | tf_op jit(solution)/shard_map/ppermute | solution.py:243
  50.2 7.7 %collective-permute-start.12 = (f16[16,4096]{1,0:T(8,128)(2,1)S(1)}, f16[16,4096]{1,0:T(8,128)(2,1)S(1)}, u32[]{:S(2)}, u32[]{:S(2)}) collective-permute-start(f16[16,4096]{1,0:T(8,128)(2,1)S(1)} %get-tuple-element.29), channel_id=1, source_target_pairs={{0,2},{1,3},{2,0},{3,1},{4,6},{5,7},{6,4},{7,5},{8,10},{9,11},{10,... | collective-permute-start | bytes 393224 | tf_op jit(solution)/shard_map/ppermute | solution.py:243
  53.2 7.3 %collective-permute-start.17 = (f16[16,4096]{1,0:T(8,128)(2,1)S(1)}, f16[16,4096]{1,0:T(8,128)(2,1)S(1)}, u32[]{:S(2)}, u32[]{:S(2)}) collective-permute-start(f16[16,4096]{1,0:T(8,128)(2,1)S(1)} %add_convert_fusion), channel_id=1, source_target_pairs={{0,4},{1,5},{2,6},{3,7},{4,0},{5,1},{6,2},{7,3},{8,12},{9,13},{10,... | collective-permute-start | bytes 393224 | tf_op jit(solution)/shard_map/ppermute | solution.py:243

commit v9 on v8

--- a/solution.py
+++ b/solution.py
@@ -159,38 +159,43 @@
     out_ref[...] = jnp.where(place == 0, top, jnp.where(place == 1, total, pick))
 
 
-def grad_kernel(first, one_ref, two_ref, near_ref, terms_ref):
+def grad_kernel(first, one_ref, two_ref, near_ref, *refs):
+    terms_ref = refs[-1]
+    tile = 1024
     both = jnp.concatenate([one_ref[...], two_ref[...]], axis=0)
-    turned = lax.dot_general(
-        near_ref[pl.ds(first, terms_ref.shape[1]), :], both, (((1,), (1,)), ((), ())),
-        preferred_element_type=jnp.float32,
-    )
-    terms_ref[...] = turned.T
-
-
-def join_kernel(members, scale, lines_ref, mine_ref, *refs):
-    *terms_refs, out_ref, loss_ref = refs
+    for place in range(0, terms_ref.shape[1], tile):
+        turned = lax.dot_general(
+            near_ref[pl.ds(first + place, tile), :], both, (((1,), (1,)), ((), ())),
+            preferred_element_type=jnp.float32,
+        )
+        terms_ref[:, pl.ds(place, tile)] = turned.T
+
+
+def join_kernel(scale, first, lines_ref, mine_ref, *refs):
+    *terms_refs, out_ref = refs
     rows = mine_ref.shape[1]
-    lines = lines_ref[...]
-    same = shared_order(lines, members)
-    loss = jnp.sum(same[0:1] + jnp.log(same[1:2]) - same[2:3], axis=1, keepdims=True) / rows
-    loss_ref[...] = jnp.broadcast_to(loss, loss_ref.shape)
-
-    top, total = lines[0:1], lines[1:2]
+    top, total = lines_ref[0:1, :], lines_ref[1:2, :]
     soft = as_columns(jnp.exp(mine_ref[0:1, :] - top) / (total * rows)) * scale
     hard = (jnp.exp(mine_ref[2:3, :] - top) / total - 1.0) / rows
     hard = as_columns(hard.astype(jnp.bfloat16).astype(jnp.float32)) * scale
 
-    near = rows // members * 4
-    chunk = min(near, rows - near, 64)
+    count = out_ref.shape[0]
+    chunk = min(count, 64)
     for place, terms_ref in enumerate(terms_refs):
         columns = pl.ds(place * terms_ref.shape[1], terms_ref.shape[1])
-        for first in range(0, rows, chunk):
-            at, other = (first, near) if first < near else (near + first, rows - near)
-            out_ref[pl.ds(first, chunk), columns] = (
-                soft[first : first + chunk] * terms_ref[pl.ds(at, chunk), :]
-                + hard[first : first + chunk] * terms_ref[pl.ds(at + other, chunk), :]
+        for i in range(0, count, chunk):
+            part = slice(first + i, first + i + chunk)
+            out_ref[pl.ds(i, chunk), columns] = (
+                soft[part] * terms_ref[pl.ds(2 * first + i, chunk), :]
+                + hard[part] * terms_ref[pl.ds(2 * first + count + i, chunk), :]
             )
+
+
+def loss_kernel(members, lines_ref, loss_ref):
+    rows = lines_ref.shape[1]
+    lines = shared_order(lines_ref[...], members)
+    loss = jnp.sum(lines[0:1] + jnp.log(lines[1:2]) - lines[2:3], axis=1, keepdims=True) / rows
+    loss_ref[...] = jnp.broadcast_to(loss, loss_ref.shape)
 
 
 def frag_kernel(rows_ref, digits_ref, lines_ref, one_ref, two_ref, head_ref, global_ref, momentum_ref,
@@ -267,9 +272,13 @@
     return jnp.concatenate(near, axis=0), far
 
 
-def scatter_sums(grads, own):
-    members = grads.shape[0] // own
-    blocks = [grads[i * own : (i + 1) * own] for i in range(members)]
+def scatter_sums(grads_near, grads_far, own):
+    blocks = [
+        grads[i * own : (i + 1) * own]
+        for grads in (grads_near, grads_far)
+        for i in range(grads.shape[0] // own)
+    ]
+    members = len(blocks)
 
     def moved(parts, step):
         value = jnp.concatenate([part.astype(SEND) for part in parts], axis=0)
@@ -316,28 +325,31 @@
 
     lines = mine
     for steps in [[step] for step in far_steps()] + [[1, 2, 3]]:
+        before = lines
         lines = call(
             functools.partial(merge_kernel, steps, members),
             [((8, rows), jnp.float32)], [lines] + [swap(lines, step) for step in steps],
         )[0]
 
-    cuts = 4
     terms = [
         call(
-            functools.partial(grad_kernel, i * depth // cuts),
-            [((2 * rows, depth // cuts), jnp.float32)], [both_near, both_far, near],
-            4 * rows * depth * width // cuts,
+            functools.partial(grad_kernel, first),
+            [((2 * rows, depth // 2), jnp.float32)], [both_near, both_far, near, *after],
+            2 * rows * depth * width,
         )[0]
-        for i in range(cuts)
+        for first, after in ((0, []), (depth // 2, [before]))
     ]
 
     scale = 2.0**14 * rows
-    grads, loss = call(
-        functools.partial(join_kernel, members, scale),
-        [((rows, depth), jnp.float32), ((8, LANES), jnp.float32)],
-        [lines, mine] + terms,
+    grads_far, grads_near = (
+        call(
+            functools.partial(join_kernel, scale, first),
+            [((count, depth), jnp.float32)], [lines, mine] + terms,
+        )[0]
+        for first, count in ((4 * own, rows - 4 * own), (0, 4 * own))
     )
-    hidden_grad = (scatter_sums(grads, own) * (1.0 / scale)).astype(jnp.bfloat16)
+    hidden_grad = (scatter_sums(grads_near, grads_far, own) * (1.0 / scale)).astype(jnp.bfloat16)
+    loss = call(functools.partial(loss_kernel, members), [((8, LANES), jnp.float32)], [lines])[0]
     new_global, new_momentum = frag_update(
         jnp.concatenate([rows_near, rows_far], axis=0), lines, [logits_near, logits_far], near,
         global_frag, momentum, peer_delta,

time: 61.4 us -> 56.8 us (0.925)
  starting transfers between devices: 26.8 us -> 23.7 us
  waiting for transfers between devices: 7.74 us -> 5.95 us
    ppermute x18, starting transfers between devices: 26.8 us -> 23.7 us  [swap(): lax.ppermute(value, AXIS, [(i, i ^ step) for i in range(lax.axis_size(AXI...]
    ppermute x18, waiting for transfers between devices: 7.74 us -> 5.95 us  [swap(): lax.ppermute(value, AXIS, [(i, i ^ step) for i in range(lax.axis_size(AXI...]
  transfers between devices with their start and end apart: 18 -> 18, of which waited for: 7 -> 5; matrix products, arithmetic and copies ran while one was open for 1% -> 2% of each run, Pallas kernels for 26% -> 33%
where the time goes in v9:
time: 56.8 us; the launch traced here: 56.6 us
  Pallas kernels  24.3 us (43%)
  starting transfers between devices  23.7 us (42%)
  waiting for transfers between devices  5.95 us (10%)
  other arithmetic  1.07 us (2%)
  between operations  0.82 us (1%)
  local copies, waits for them, and re-layouts  0.79 us (1%)
    ppermute x18, starting transfers between devices, swap(): lax.ppermute(value, AXIS, [(i, i ^ step) for i in range(lax.axis_size(AXI...  23.7 us
    pallas_call x11, Pallas kernels, call(): pl.pallas_call(kernel, out_shape=outs, in_specs=[pl.BlockSpec(memory_spac...  20.9 us
    ppermute x18, waiting for transfers between devices, swap(): lax.ppermute(value, AXIS, [(i, i ^ step) for i in range(lax.axis_size(AXI...  5.95 us
    pallas_call x1, Pallas kernels, frag_update(): pl.pallas_call(frag_kernel, grid=(width // TILE,), out_shape=[jax.ShapeDt...  3.36 us
  transfers between devices with their start and end apart: 18, of which 5 were waited for; matrix products, arithmetic and copies ran while one was open for 2% of the time, Pallas kernels for 33%

profile of v9, /device:TPU:0, one launch (start us, length us, event | category | flops | bytes accessed | tf_op | source)
XLA Modules:
  0.0 56.6 jit_solution(17544429123349342917)
XLA Ops:
  0.6 0.9 %shard_map.93 = bf16[16,4224]{1,0:T(8,128)(2,1)S(1)} custom-call(s32[16]{0:T(128)} %targets.1, bf16[16,4096]{1,0:T(8,128)(2,1)} %rows.1), custom_call_target="tpu_custom_call" | custom-call | bytes 131136 | tf_op jit(solution)/shard_map/pallas_call | solution.py:22
  1.6 4.1 %collective-permute-start = (bf16[16,4224]{1,0:T(8,128)(2,1)S(1)}, bf16[16,4224]{1,0:T(8,128)(2,1)S(1)}, u32[]{:S(2)}, u32[]{:S(2)}) collective-permute-start(bf16[16,4224]{1,0:T(8,128)(2,1)S(1)} %shard_map.93), channel_id=1, source_target_pairs={{0,4},{1,5},{2,6},{3,7},{4,0},{5,1},{6,2},{7,3},{8,12},{9,13},{10,... | collective-permute-start | bytes 405512 | tf_op jit(solution)/shard_map/ppermute | solution.py:248
  5.7 1.5 %collective-permute-start.4 = (bf16[16,4224]{1,0:T(8,128)(2,1)S(1)}, bf16[16,4224]{1,0:T(8,128)(2,1)S(1)}, u32[]{:S(2)}, u32[]{:S(2)}) collective-permute-start(bf16[16,4224]{1,0:T(8,128)(2,1)S(1)} %shard_map.93), channel_id=1, source_target_pairs={{0,1},{1,0},{2,3},{3,2},{4,5},{5,4},{6,7},{7,6},{8,9},{9,8},{10,11... | collective-permute-start | bytes 405512 | tf_op jit(solution)/shard_map/ppermute | solution.py:248
  7.2 1.6 %collective-permute-start.5 = (bf16[16,4224]{1,0:T(8,128)(2,1)S(1)}, bf16[16,4224]{1,0:T(8,128)(2,1)S(1)}, u32[]{:S(2)}, u32[]{:S(2)}) collective-permute-start(bf16[16,4224]{1,0:T(8,128)(2,1)S(1)} %shard_map.93), channel_id=1, source_target_pairs={{0,2},{1,3},{2,0},{3,1},{4,6},{5,7},{6,4},{7,5},{8,10},{9,11},{10,... | collective-permute-start | bytes 405512 | tf_op jit(solution)/shard_map/ppermute | solution.py:248
  9.2 5.9 %shard_map.94.near_ref.head_ref = bf16[4096,2048]{1,0:T(8,128)(2,1)S(1)} custom-call(bf16[4096,2048]{1,0:T(8,128)(2,1)} %source.1), custom_call_target="tpu_custom_call" | custom-call | bytes 16777216 | tf_op jit(solution)/shard_map/pallas_call | solution.py:22
  15.1 1.6 %collective-permute-start.1 = (bf16[16,4224]{1,0:T(8,128)(2,1)S(1)}, bf16[16,4224]{1,0:T(8,128)(2,1)S(1)}, u32[]{:S(2)}, u32[]{:S(2)}) collective-permute-start(bf16[16,4224]{1,0:T(8,128)(2,1)S(1)} %collective-permute-done), channel_id=1, source_target_pairs={{0,1},{1,0},{2,3},{3,2},{4,5},{5,4},{6,7},{7,6},{8,9},{9,8},{10,11... | collective-permute-start | bytes 405512 | tf_op jit(solution)/shard_map/ppermute | solution.py:248
  16.7 1.6 %collective-permute-start.2 = (bf16[16,4224]{1,0:T(8,128)(2,1)S(1)}, bf16[16,4224]{1,0:T(8,128)(2,1)S(1)}, u32[]{:S(2)}, u32[]{:S(2)}) collective-permute-start(bf16[16,4224]{1,0:T(8,128)(2,1)S(1)} %collective-permute-done), channel_id=1, source_target_pairs={{0,2},{1,3},{2,0},{3,1},{4,6},{5,7},{6,4},{7,5},{8,10},{9,11},{10,... | collective-permute-start | bytes 405512 | tf_op jit(solution)/shard_map/ppermute | solution.py:248
  18.8 3.8 %shard_map.95 = (f32[64,2048]{1,0:T(8,128)S(1)}, bf16[128,2048]{1,0:T(8,128)(2,1)S(1)}, f32[64,128]{1,0:T(8,128)S(1)}) custom-call(bf16[64,4224]{1,0:T(8,128)(2,1)S(1)} %pad_maximum_fusion.1.rows_ref, bf16[4096,2048]{1,0:T(8,128)(2,1)S(1)} %shard_map.94.near_ref.head_ref), custom_call_target="tpu_custom_call" | custom-call | flops 1073741824 | bytes 17317888 | tf_op jit(solution)/shard_map/pallas_call | solution.py:22
  22.5 1.7 %collective-permute-done.3 = bf16[16,4224]{1,0:T(8,128)(2,1)S(1)} collective-permute-done((bf16[16,4224]{1,0:T(8,128)(2,1)S(1)}, bf16[16,4224]{1,0:T(8,128)(2,1)S(1)}, u32[]{:S(2)}, u32[]{:S(2)}) %collective-permute-start.3) | collective-permute-done | bytes 135200 | tf_op jit(solution)/shard_map/ppermute | solution.py:248
  24.3 3.8 %shard_map.96 = (f32[64,2048]{1,0:T(8,128)S(1)}, bf16[128,2048]{1,0:T(8,128)(2,1)S(1)}, f32[8,128]{1,0:T(8,128)S(1)}) custom-call(bf16[64,4224]{1,0:T(8,128)(2,1)S(1)} %bitcast.6, bf16[4096,2048]{1,0:T(8,128)(2,1)S(1)} %shard_map.94.near_ref.head_ref, f32[64,128]{1,0:T(8,128)S(1)} %get-tuple-element.12.refs_0_), custom_call_target="tpu_custom_call" | custom-call | flops 1073741824 | bytes 17350656 | tf_op jit(solution)/shard_map/pallas_call | solution.py:22
  28.5 2.7 %shard_map.100.refs_0_ = f32[256,2048]{1,0:T(8,128)S(1)} custom-call(bf16[128,2048]{1,0:T(8,128)(2,1)S(1)} %get-tuple-element.14.one_ref, bf16[128,2048]{1,0:T(8,128)(2,1)S(1)} %get-tuple-element.15.two_ref, bf16[4096,2048]{1,0:T(8,128)(2,1)S(1)} %shard_map.94.near_ref.head_ref), custom_call_target="tpu_custom_call" | custom-call | flops 2147483648 | bytes 17825792 | tf_op jit(solution)/shard_map/pallas_call | solution.py:22
  31.2 1.4 %collective-permute-done.7.refs_0_ = f32[8,128]{1,0:T(8,128)S(1)} collective-permute-done((f32[8,128]{1,0:T(8,128)S(1)}, f32[8,128]{1,0:T(8,128)S(1)}, u32[]{:S(2)}, u32[]{:S(2)}) %collective-permute-start.7) | collective-permute-done | bytes 4128 | tf_op jit(solution)/shard_map/ppermute | solution.py:248
  32.7 1.8 %collective-permute-start.10 = (f32[8,128]{1,0:T(8,128)S(1)}, f32[8,128]{1,0:T(8,128)S(1)}, u32[]{:S(2)}, u32[]{:S(2)}) collective-permute-start(f32[8,128]{1,0:T(8,128)S(1)} %shard_map.97.mine_ref.refs_0_), channel_id=1, source_target_pairs={{0,3},{1,2},{2,1},{3,0},{4,7},{5,6},{6,5},{7,4},{8,11},{9,10},{10,... | collective-permute-start | bytes 12296 | tf_op jit(solution)/shard_map/ppermute | solution.py:248
  35.1 1.2 %collective-permute-start.9 = (f32[8,128]{1,0:T(8,128)S(1)}, f32[8,128]{1,0:T(8,128)S(1)}, u32[]{:S(2)}, u32[]{:S(2)}) collective-permute-start(f32[8,128]{1,0:T(8,128)S(1)} %shard_map.97.mine_ref.refs_0_), channel_id=1, source_target_pairs={{0,2},{1,3},{2,0},{3,1},{4,6},{5,7},{6,4},{7,5},{8,10},{9,11},{10,... | collective-permute-start | bytes 12296 | tf_op jit(solution)/shard_map/ppermute | solution.py:248
  36.3 2.7 %shard_map.101.refs_1_ = f32[256,2048]{1,0:T(8,128)S(1)} custom-call(bf16[128,2048]{1,0:T(8,128)(2,1)S(1)} %get-tuple-element.14.one_ref, bf16[128,2048]{1,0:T(8,128)(2,1)S(1)} %get-tuple-element.15.two_ref, bf16[4096,2048]{1,0:T(8,128)(2,1)S(1)} %shard_map.94.near_ref.head_ref, f32[8,128]{1,0:T(8,128)S(1)} %shard_map.97.mine_ref.refs_0_), custom_call_target="tpu_custom_call" | custom-call | flops 2147483648 | bytes 17829888 | tf_op jit(solution)/shard_map/pallas_call | solution.py:22
  39.9 1.8 %collective-permute-start.14 = (f16[16,4096]{1,0:T(8,128)(2,1)S(1)}, f16[16,4096]{1,0:T(8,128)(2,1)S(1)}, u32[]{:S(2)}, u32[]{:S(2)}) collective-permute-start(f16[16,4096]{1,0:T(8,128)(2,1)S(1)} %get-tuple-element.23), channel_id=1, source_target_pairs={{0,3},{1,2},{2,1},{3,0},{4,7},{5,6},{6,5},{7,4},{8,11},{9,10},{10,... | collective-permute-start | bytes 393224 | tf_op jit(solution)/shard_map/ppermute | solution.py:248
  41.8 0.9 %collective-permute-start.15 = (f16[16,4096]{1,0:T(8,128)(2,1)S(1)}, f16[16,4096]{1,0:T(8,128)(2,1)S(1)}, u32[]{:S(2)}, u32[]{:S(2)}) collective-permute-start(f16[16,4096]{1,0:T(8,128)(2,1)S(1)} %get-tuple-element.25), channel_id=1, source_target_pairs={{0,2},{1,3},{2,0},{3,1},{4,6},{5,7},{6,4},{7,5},{8,10},{9,11},{10,... | collective-permute-start | bytes 393224 | tf_op jit(solution)/shard_map/ppermute | solution.py:248
  42.6 0.9 %collective-permute-start.16 = (f16[16,4096]{1,0:T(8,128)(2,1)S(1)}, f16[16,4096]{1,0:T(8,128)(2,1)S(1)}, u32[]{:S(2)}, u32[]{:S(2)}) collective-permute-start(f16[16,4096]{1,0:T(8,128)(2,1)S(1)} %get-tuple-element.24), channel_id=1, source_target_pairs={{0,1},{1,0},{2,3},{3,2},{4,5},{5,4},{6,7},{7,6},{8,9},{9,8},{10,11... | collective-permute-start | bytes 393224 | tf_op jit(solution)/shard_map/ppermute | solution.py:248
  43.7 1.8 %collective-permute-start.11 = (f16[16,4096]{1,0:T(8,128)(2,1)S(1)}, f16[16,4096]{1,0:T(8,128)(2,1)S(1)}, u32[]{:S(2)}, u32[]{:S(2)}) collective-permute-start(f16[16,4096]{1,0:T(8,128)(2,1)S(1)} %get-tuple-element.20), channel_id=1, source_target_pairs={{0,3},{1,2},{2,1},{3,0},{4,7},{5,6},{6,5},{7,4},{8,11},{9,10},{10,... | collective-permute-start | bytes 393224 | tf_op jit(solution)/shard_map/ppermute | solution.py:248
  45.5 0.9 %collective-permute-start.12 = (f16[16,4096]{1,0:T(8,128)(2,1)S(1)}, f16[16,4096]{1,0:T(8,128)(2,1)S(1)}, u32[]{:S(2)}, u32[]{:S(2)}) collective-permute-start(f16[16,4096]{1,0:T(8,128)(2,1)S(1)} %get-tuple-element.22), channel_id=1, source_target_pairs={{0,2},{1,3},{2,0},{3,1},{4,6},{5,7},{6,4},{7,5},{8,10},{9,11},{10,... | collective-permute-start | bytes 393224 | tf_op jit(solution)/shard_map/ppermute | solution.py:248
  47.2 1.2 %collective-permute-done.15 = f16[16,4096]{1,0:T(8,128)(2,1)S(1)} collective-permute-done((f16[16,4096]{1,0:T(8,128)(2,1)S(1)}, f16[16,4096]{1,0:T(8,128)(2,1)S(1)}, u32[]{:S(2)}, u32[]{:S(2)}) %collective-permute-start.15) | collective-permute-done | bytes 131104 | tf_op jit(solution)/shard_map/ppermute | solution.py:248
  48.5 2.0 %collective-permute-start.17 = (f16[16,4096]{1,0:T(8,128)(2,1)S(1)}, f16[16,4096]{1,0:T(8,128)(2,1)S(1)}, u32[]{:S(2)}, u32[]{:S(2)}) collective-permute-start(f16[16,4096]{1,0:T(8,128)(2,1)S(1)} %fusion.2), channel_id=1, source_target_pairs={{0,4},{1,5},{2,6},{3,7},{4,0},{5,1},{6,2},{7,3},{8,12},{9,13},{10,... | collective-permute-start | bytes 393224 | tf_op jit(solution)/shard_map/ppermute | solution.py:248
  51.4 3.4 %shard_map.104 = (f32[128,2048]{1,0:T(8,128)}, f32[128,2048]{1,0:T(8,128)}) custom-call(bf16[128,4224]{1,0:T(8,128)(2,1)S(1)} %constant_dynamic-update-slice_fusion.rows_ref.digits_ref, bf16[128,4224]{1,0:T(8,128)(2,1)S(1)} %constant_dynamic-update-slice_fusion.rows_ref.digits_ref, f32[8,128]{1,0:T(8,128)S(1)} %shard_map.98.lines_ref, ...), custom_call_target="tpu_custom_call" | custom-call | flops 67108864 | bytes 6291456 | tf_op jit(solution)/shard_map/pallas_call | solution.py:224
  54.8 1.1 %collective-permute-done.17 = f16[16,4096]{1,0:T(8,128)(2,1)S(1)} collective-permute-done((f16[16,4096]{1,0:T(8,128)(2,1)S(1)}, f16[16,4096]{1,0:T(8,128)(2,1)S(1)}, u32[]{:S(2)}, u32[]{:S(2)}) %collective-permute-start.17) | collective-permute-done | bytes 131104 | tf_op jit(solution)/shard_map/ppermute | solution.py:248
  (44 shorter events, 5.6 us)
Async XLA Ops:
  1.6 13.5 %collective-permute-start = (bf16[16,4224]{1,0:T(8,128)(2,1)S(1)}, bf16[16,4224]{1,0:T(8,128)(2,1)S(1)}, u32[]{:S(2)}, u32[]{:S(2)}) collective-permute-start(bf16[16,4224]{1,0:T(8,128)(2,1)S(1)} %shard_map.93), channel_id=1, source_target_pairs={{0,4},{1,5},{2,6},{3,7},{4,0},{5,1},{6,2},{7,3},{8,12},{9,13},{10,... | collective-permute-start | bytes 405512 | tf_op jit(solution)/shard_map/ppermute | solution.py:248
  5.7 12.6 %collective-permute-start.4 = (bf16[16,4224]{1,0:T(8,128)(2,1)S(1)}, bf16[16,4224]{1,0:T(8,128)(2,1)S(1)}, u32[]{:S(2)}, u32[]{:S(2)}) collective-permute-start(bf16[16,4224]{1,0:T(8,128)(2,1)S(1)} %shard_map.93), channel_id=1, source_target_pairs={{0,1},{1,0},{2,3},{3,2},{4,5},{5,4},{6,7},{7,6},{8,9},{9,8},{10,11... | collective-permute-start | bytes 405512 | tf_op jit(solution)/shard_map/ppermute | solution.py:248
  7.2 11.5 %collective-permute-start.5 = (bf16[16,4224]{1,0:T(8,128)(2,1)S(1)}, bf16[16,4224]{1,0:T(8,128)(2,1)S(1)}, u32[]{:S(2)}, u32[]{:S(2)}) collective-permute-start(bf16[16,4224]{1,0:T(8,128)(2,1)S(1)} %shard_map.93), channel_id=1, source_target_pairs={{0,2},{1,3},{2,0},{3,1},{4,6},{5,7},{6,4},{7,5},{8,10},{9,11},{10,... | collective-permute-start | bytes 405512 | tf_op jit(solution)/shard_map/ppermute | solution.py:248
  8.8 9.9 %collective-permute-start.6 = (bf16[16,4224]{1,0:T(8,128)(2,1)S(1)}, bf16[16,4224]{1,0:T(8,128)(2,1)S(1)}, u32[]{:S(2)}, u32[]{:S(2)}) collective-permute-start(bf16[16,4224]{1,0:T(8,128)(2,1)S(1)} %shard_map.93), channel_id=1, source_target_pairs={{0,3},{1,2},{2,1},{3,0},{4,7},{5,6},{6,5},{7,4},{8,11},{9,10},{10,... | collective-permute-start | bytes 405512 | tf_op jit(solution)/shard_map/ppermute | solution.py:248
  15.1 7.4 %collective-permute-start.1 = (bf16[16,4224]{1,0:T(8,128)(2,1)S(1)}, bf16[16,4224]{1,0:T(8,128)(2,1)S(1)}, u32[]{:S(2)}, u32[]{:S(2)}) collective-permute-start(bf16[16,4224]{1,0:T(8,128)(2,1)S(1)} %collective-permute-done), channel_id=1, source_target_pairs={{0,1},{1,0},{2,3},{3,2},{4,5},{5,4},{6,7},{7,6},{8,9},{9,8},{10,11... | collective-permute-start | bytes 405512 | tf_op jit(solution)/shard_map/ppermute | solution.py:248
  16.7 5.9 %collective-permute-start.2 = (bf16[16,4224]{1,0:T(8,128)(2,1)S(1)}, bf16[16,4224]{1,0:T(8,128)(2,1)S(1)}, u32[]{:S(2)}, u32[]{:S(2)}) collective-permute-start(bf16[16,4224]{1,0:T(8,128)(2,1)S(1)} %collective-permute-done), channel_id=1, source_target_pairs={{0,2},{1,3},{2,0},{3,1},{4,6},{5,7},{6,4},{7,5},{8,10},{9,11},{10,... | collective-permute-start | bytes 405512 | tf_op jit(solution)/shard_map/ppermute | solution.py:248
  18.2 6.0 %collective-permute-start.3 = (bf16[16,4224]{1,0:T(8,128)(2,1)S(1)}, bf16[16,4224]{1,0:T(8,128)(2,1)S(1)}, u32[]{:S(2)}, u32[]{:S(2)}) collective-permute-start(bf16[16,4224]{1,0:T(8,128)(2,1)S(1)} %collective-permute-done), channel_id=1, source_target_pairs={{0,3},{1,2},{2,1},{3,0},{4,7},{5,6},{6,5},{7,4},{8,11},{9,10},{10,... | collective-permute-start | bytes 405512 | tf_op jit(solution)/shard_map/ppermute | solution.py:248
  28.1 4.5 %collective-permute-start.7 = (f32[8,128]{1,0:T(8,128)S(1)}, f32[8,128]{1,0:T(8,128)S(1)}, u32[]{:S(2)}, u32[]{:S(2)}) collective-permute-start(f32[8,128]{1,0:T(8,128)S(1)} %get-tuple-element.13.mine_ref), channel_id=1, source_target_pairs={{0,4},{1,5},{2,6},{3,7},{4,0},{5,1},{6,2},{7,3},{8,12},{9,13},{10,... | collective-permute-start | bytes 12296 | tf_op jit(solution)/shard_map/ppermute | solution.py:248
  32.7 6.2 %collective-permute-start.10 = (f32[8,128]{1,0:T(8,128)S(1)}, f32[8,128]{1,0:T(8,128)S(1)}, u32[]{:S(2)}, u32[]{:S(2)}) collective-permute-start(f32[8,128]{1,0:T(8,128)S(1)} %shard_map.97.mine_ref.refs_0_), channel_id=1, source_target_pairs={{0,3},{1,2},{2,1},{3,0},{4,7},{5,6},{6,5},{7,4},{8,11},{9,10},{10,... | collective-permute-start | bytes 12296 | tf_op jit(solution)/shard_map/ppermute | solution.py:248
  34.5 4.4 %collective-permute-start.8 = (f32[8,128]{1,0:T(8,128)S(1)}, f32[8,128]{1,0:T(8,128)S(1)}, u32[]{:S(2)}, u32[]{:S(2)}) collective-permute-start(f32[8,128]{1,0:T(8,128)S(1)} %shard_map.97.mine_ref.refs_0_), channel_id=1, source_target_pairs={{0,1},{1,0},{2,3},{3,2},{4,5},{5,4},{6,7},{7,6},{8,9},{9,8},{10,11... | collective-permute-start | bytes 12296 | tf_op jit(solution)/shard_map/ppermute | solution.py:248
  35.1 4.0 %collective-permute-start.9 = (f32[8,128]{1,0:T(8,128)S(1)}, f32[8,128]{1,0:T(8,128)S(1)}, u32[]{:S(2)}, u32[]{:S(2)}) collective-permute-start(f32[8,128]{1,0:T(8,128)S(1)} %shard_map.97.mine_ref.refs_0_), channel_id=1, source_target_pairs={{0,2},{1,3},{2,0},{3,1},{4,6},{5,7},{6,4},{7,5},{8,10},{9,11},{10,... | collective-permute-start | bytes 12296 | tf_op jit(solution)/shard_map/ppermute | solution.py:248
  39.9 6.8 %collective-permute-start.14 = (f16[16,4096]{1,0:T(8,128)(2,1)S(1)}, f16[16,4096]{1,0:T(8,128)(2,1)S(1)}, u32[]{:S(2)}, u32[]{:S(2)}) collective-permute-start(f16[16,4096]{1,0:T(8,128)(2,1)S(1)} %get-tuple-element.23), channel_id=1, source_target_pairs={{0,3},{1,2},{2,1},{3,0},{4,7},{5,6},{6,5},{7,4},{8,11},{9,10},{10,... | collective-permute-start | bytes 393224 | tf_op jit(solution)/shard_map/ppermute | solution.py:248
  41.8 6.7 %collective-permute-start.15 = (f16[16,4096]{1,0:T(8,128)(2,1)S(1)}, f16[16,4096]{1,0:T(8,128)(2,1)S(1)}, u32[]{:S(2)}, u32[]{:S(2)}) collective-permute-start(f16[16,4096]{1,0:T(8,128)(2,1)S(1)} %get-tuple-element.25), channel_id=1, source_target_pairs={{0,2},{1,3},{2,0},{3,1},{4,6},{5,7},{6,4},{7,5},{8,10},{9,11},{10,... | collective-permute-start | bytes 393224 | tf_op jit(solution)/shard_map/ppermute | solution.py:248
  42.6 5.8 %collective-permute-start.16 = (f16[16,4096]{1,0:T(8,128)(2,1)S(1)}, f16[16,4096]{1,0:T(8,128)(2,1)S(1)}, u32[]{:S(2)}, u32[]{:S(2)}) collective-permute-start(f16[16,4096]{1,0:T(8,128)(2,1)S(1)} %get-tuple-element.24), channel_id=1, source_target_pairs={{0,1},{1,0},{2,3},{3,2},{4,5},{5,4},{6,7},{7,6},{8,9},{9,8},{10,11... | collective-permute-start | bytes 393224 | tf_op jit(solution)/shard_map/ppermute | solution.py:248
  43.5 7.9 %copy-start.2 = (f32[128,2048]{1,0:T(8,128)S(1)}, f32[128,2048]{1,0:T(8,128)}, u32[]{:S(2)}) copy-start(f32[128,2048]{1,0:T(8,128)} %peer_ref.1) | copy-start | bytes 3145732
  43.6 7.8 %copy-start.1 = (f32[128,2048]{1,0:T(8,128)S(1)}, f32[128,2048]{1,0:T(8,128)}, u32[]{:S(2)}) copy-start(f32[128,2048]{1,0:T(8,128)} %momentum_ref.1) | copy-start | bytes 3145732
  43.7 7.8 %copy-start = (f32[128,2048]{1,0:T(8,128)S(1)}, f32[128,2048]{1,0:T(8,128)}, u32[]{:S(2)}) copy-start(f32[128,2048]{1,0:T(8,128)} %global_ref.1) | copy-start | bytes 3145732
  43.7 11.1 %collective-permute-start.11 = (f16[16,4096]{1,0:T(8,128)(2,1)S(1)}, f16[16,4096]{1,0:T(8,128)(2,1)S(1)}, u32[]{:S(2)}, u32[]{:S(2)}) collective-permute-start(f16[16,4096]{1,0:T(8,128)(2,1)S(1)} %get-tuple-element.20), channel_id=1, source_target_pairs={{0,3},{1,2},{2,1},{3,0},{4,7},{5,6},{6,5},{7,4},{8,11},{9,10},{10,... | collective-permute-start | bytes 393224 | tf_op jit(solution)/shard_map/ppermute | solution.py:248
  45.5 9.3 %collective-permute-start.12 = (f16[16,4096]{1,0:T(8,128)(2,1)S(1)}, f16[16,4096]{1,0:T(8,128)(2,1)S(1)}, u32[]{:S(2)}, u32[]{:S(2)}) collective-permute-start(f16[16,4096]{1,0:T(8,128)(2,1)S(1)} %get-tuple-element.22), channel_id=1, source_target_pairs={{0,2},{1,3},{2,0},{3,1},{4,6},{5,7},{6,4},{7,5},{8,10},{9,11},{10,... | collective-permute-start | bytes 393224 | tf_op jit(solution)/shard_map/ppermute | solution.py:248
  46.8 8.0 %collective-permute-start.13 = (f16[16,4096]{1,0:T(8,128)(2,1)S(1)}, f16[16,4096]{1,0:T(8,128)(2,1)S(1)}, u32[]{:S(2)}, u32[]{:S(2)}) collective-permute-start(f16[16,4096]{1,0:T(8,128)(2,1)S(1)} %get-tuple-element.21), channel_id=1, source_target_pairs={{0,1},{1,0},{2,3},{3,2},{4,5},{5,4},{6,7},{7,6},{8,9},{9,8},{10,11... | collective-permute-start | bytes 393224 | tf_op jit(solution)/shard_map/ppermute | solution.py:248
  48.5 7.3 %collective-permute-start.17 = (f16[16,4096]{1,0:T(8,128)(2,1)S(1)}, f16[16,4096]{1,0:T(8,128)(2,1)S(1)}, u32[]{:S(2)}, u32[]{:S(2)}) collective-permute-start(f16[16,4096]{1,0:T(8,128)(2,1)S(1)} %fusion.2), channel_id=1, source_target_pairs={{0,4},{1,5},{2,6},{3,7},{4,0},{5,1},{6,2},{7,3},{8,12},{9,13},{10,... | collective-permute-start | bytes 393224 | tf_op jit(solution)/shard_map/ppermute | solution.py:248

commit v10 on v9

--- a/solution.py
+++ b/solution.py
@@ -15,7 +15,7 @@
 VMEM = pl.BlockSpec(memory_space=pltpu.VMEM)
 
 
-def call(kernel, outs, operands, flops=0, scratch=(), sources=None, vmem=16 * 2**20):
+def call(kernel, outs, operands, flops=0, scratch=(), sources=None, vmem=16 * 2**20, aliases={}):
     outs = [pltpu.VMEM(shape, dtype) for shape, dtype in outs]
     places = sources or [pltpu.VMEM] * len(operands)
     moved = sum(x.size * x.dtype.itemsize for x in operands)
@@ -25,12 +25,17 @@
         in_specs=[pl.BlockSpec(memory_space=place) for place in places],
         out_specs=[VMEM] * len(outs),
         scratch_shapes=list(scratch),
+        input_output_aliases=aliases,
         compiler_params=pltpu.CompilerParams(vmem_limit_bytes=vmem),
         cost_estimate=pl.CostEstimate(flops=flops, bytes_accessed=moved, transcendentals=0),
     )(*[pltpu.with_memory_space_constraint(x, place) for x, place in zip(operands, places)])
 
 
-def load_kernel(source, target, sems):
+def late_sender():
+    return lax.rem(lax.axis_index("outer"), 2) == 1
+
+
+def load(source, target, sems):
     block = source.shape[0] // sems.shape[0]
     copies = []
     for i in range(sems.shape[0]):
@@ -42,18 +47,17 @@
         copy.wait()
 
 
-def resident(head):
-    return call(
-        load_kernel, [(head.shape, head.dtype)], [head],
-        scratch=[pltpu.SemaphoreType.DMA((4,))], sources=[pltpu.HBM],
-    )[0]
+def load_kernel(source, held, target, sems):
+    @pl.when(jnp.logical_not(late_sender()))
+    def _():
+        load(source, target, sems)
 
 
 TILE = 512
 WIDE = 1024
 
 
-def pack_kernel(targets, rows, out_ref, targets_ref, sems):
+def pack_kernel(targets, rows, head, out_ref, near_ref, targets_ref, sems, head_sems):
     own, depth = rows.shape
     ids_copy = pltpu.make_async_copy(targets, targets_ref, sems.at[0])
     rows_copy = pltpu.make_async_copy(rows, out_ref.at[:, pl.ds(0, depth)], sems.at[1])
@@ -68,6 +72,10 @@
     digits = jnp.where(lane == 0, ids // 256, ids % 256)
     out_ref[:, depth:] = digits.astype(jnp.float32).astype(jnp.bfloat16)
     rows_copy.wait()
+
+    @pl.when(late_sender())
+    def _():
+        load(head, near_ref, head_sems)
 
 
 def ids_of(digits):
@@ -302,13 +310,21 @@
     rows = own * members
     width = head.shape[1]
 
-    packed = call(
-        pack_kernel, [((own, depth + LANES), hidden.dtype)], [targets, hidden],
-        scratch=[pltpu.SMEM(targets.shape, targets.dtype), pltpu.SemaphoreType.DMA((2,))],
-        sources=[pltpu.HBM, pltpu.HBM],
+    packed, near = call(
+        pack_kernel, [((own, depth + LANES), hidden.dtype), (head.shape, head.dtype)],
+        [targets, hidden, head],
+        scratch=[
+            pltpu.SMEM(targets.shape, targets.dtype),
+            pltpu.SemaphoreType.DMA((2,)),
+            pltpu.SemaphoreType.DMA((4,)),
+        ],
+        sources=[pltpu.HBM] * 3,
+    )
+    rows_near, rows_far = gather_rows(packed)
+    near = call(
+        load_kernel, [(head.shape, head.dtype)], [head, near],
+        scratch=[pltpu.SemaphoreType.DMA((4,))], sources=[pltpu.HBM, pltpu.VMEM], aliases={1: 0},
     )[0]
-    rows_near, rows_far = gather_rows(packed)
-    near = resident(head)
 
     def part(held, *before):
         count = held.shape[0]

time: 56.8 us -> 60.9 us (1.072)
  waiting for transfers between devices: 5.95 us -> 9.13 us
  starting transfers between devices: 23.7 us -> 24.6 us
    ppermute x18, waiting for transfers between devices: 5.95 us -> 9.13 us  [swap(): lax.ppermute(value, AXIS, [(i, i ^ step) for i in range(lax.axis_size(AXI...]
    ppermute x18, starting transfers between devices: 23.7 us -> 24.6 us  [swap(): lax.ppermute(value, AXIS, [(i, i ^ step) for i in range(lax.axis_size(AXI...]
  transfers between devices with their start and end apart: 18 -> 18, of which waited for: 5 -> 7; matrix products, arithmetic and copies ran while one was open for 2% -> 1% of each run, Pallas kernels for 33% -> 31%
where the time goes in v10:
time: 60.9 us; the launch traced here: 60.7 us
  starting transfers between devices  24.6 us (40%)
  Pallas kernels  24.3 us (40%)
  waiting for transfers between devices  9.13 us (15%)
  other arithmetic  1.07 us (2%)
  between operations  0.81 us (1%)
  local copies, waits for them, and re-layouts  0.79 us (1%)
    ppermute x18, starting transfers between devices, swap(): lax.ppermute(value, AXIS, [(i, i ^ step) for i in range(lax.axis_size(AXI...  24.6 us
    pallas_call x11, Pallas kernels, call(): pl.pallas_call(kernel, out_shape=outs, in_specs=[pl.BlockSpec(memory_spac...  21 us
    ppermute x18, waiting for transfers between devices, swap(): lax.ppermute(value, AXIS, [(i, i ^ step) for i in range(lax.axis_size(AXI...  9.13 us
    pallas_call x1, Pallas kernels, frag_update(): pl.pallas_call(frag_kernel, grid=(width // TILE,), out_shape=[jax.ShapeDt...  3.36 us
  transfers between devices with their start and end apart: 18, of which 7 were waited for; matrix products, arithmetic and copies ran while one was open for 1% of the time, Pallas kernels for 31%

profile of v10, /device:TPU:0, one launch (start us, length us, event | category | flops | bytes accessed | tf_op | source)
XLA Modules:
  0.0 60.7 jit_solution(7810426766399385436)
XLA Ops:
  0.6 1.0 %shard_map.93 = (bf16[16,4224]{1,0:T(8,128)(2,1)S(1)}, bf16[4096,2048]{1,0:T(8,128)(2,1)S(1)}) custom-call(s32[16]{0:T(128)} %targets.1, bf16[16,4096]{1,0:T(8,128)(2,1)} %rows.1, bf16[4096,2048]{1,0:T(8,128)(2,1)} %source.1), custom_call_target="tpu_custom_call" | custom-call | bytes 16908352 | tf_op jit(solution)/shard_map/pallas_call | solution.py:22
  1.6 4.0 %collective-permute-start.6 = (bf16[16,4224]{1,0:T(8,128)(2,1)S(1)}, bf16[16,4224]{1,0:T(8,128)(2,1)S(1)}, u32[]{:S(2)}, u32[]{:S(2)}) collective-permute-start(bf16[16,4224]{1,0:T(8,128)(2,1)S(1)} %get-tuple-element.14), channel_id=1, source_target_pairs={{0,3},{1,2},{2,1},{3,0},{4,7},{5,6},{6,5},{7,4},{8,11},{9,10},{10,... | collective-permute-start | bytes 405512 | tf_op jit(solution)/shard_map/ppermute | solution.py:256
  6.3 2.9 %collective-permute-start = (bf16[16,4224]{1,0:T(8,128)(2,1)S(1)}, bf16[16,4224]{1,0:T(8,128)(2,1)S(1)}, u32[]{:S(2)}, u32[]{:S(2)}) collective-permute-start(bf16[16,4224]{1,0:T(8,128)(2,1)S(1)} %get-tuple-element.14), channel_id=1, source_target_pairs={{0,4},{1,5},{2,6},{3,7},{4,0},{5,1},{6,2},{7,3},{8,12},{9,13},{10,... | collective-permute-start | bytes 405512 | tf_op jit(solution)/shard_map/ppermute | solution.py:256
  9.2 5.9 %shard_map.94.near_ref.head_ref = bf16[4096,2048]{1,0:T(8,128)(2,1)S(1)} custom-call(bf16[4096,2048]{1,0:T(8,128)(2,1)} %source.1, bf16[4096,2048]{1,0:T(8,128)(2,1)S(1)} %get-tuple-element.15.held), custom_call_target="tpu_custom_call", output_to_operand_aliasing={{}: (1, {})} | custom-call | bytes 33554432 | tf_op jit(solution)/shard_map/pallas_call | solution.py:22
  15.1 2.6 %collective-permute-start.3 = (bf16[16,4224]{1,0:T(8,128)(2,1)S(1)}, bf16[16,4224]{1,0:T(8,128)(2,1)S(1)}, u32[]{:S(2)}, u32[]{:S(2)}) collective-permute-start(bf16[16,4224]{1,0:T(8,128)(2,1)S(1)} %collective-permute-done), channel_id=1, source_target_pairs={{0,3},{1,2},{2,1},{3,0},{4,7},{5,6},{6,5},{7,4},{8,11},{9,10},{10,... | collective-permute-start | bytes 405512 | tf_op jit(solution)/shard_map/ppermute | solution.py:256
  18.8 3.8 %shard_map.95 = (f32[64,2048]{1,0:T(8,128)S(1)}, bf16[128,2048]{1,0:T(8,128)(2,1)S(1)}, f32[64,128]{1,0:T(8,128)S(1)}) custom-call(bf16[64,4224]{1,0:T(8,128)(2,1)S(1)} %pad_maximum_fusion.1.rows_ref, bf16[4096,2048]{1,0:T(8,128)(2,1)S(1)} %shard_map.94.near_ref.head_ref), custom_call_target="tpu_custom_call" | custom-call | flops 1073741824 | bytes 17317888 | tf_op jit(solution)/shard_map/pallas_call | solution.py:22
  22.6 2.7 %collective-permute-done.2 = bf16[16,4224]{1,0:T(8,128)(2,1)S(1)} collective-permute-done((bf16[16,4224]{1,0:T(8,128)(2,1)S(1)}, bf16[16,4224]{1,0:T(8,128)(2,1)S(1)}, u32[]{:S(2)}, u32[]{:S(2)}) %collective-permute-start.2) | collective-permute-done | bytes 135200 | tf_op jit(solution)/shard_map/ppermute | solution.py:256
  25.4 3.8 %shard_map.96 = (f32[64,2048]{1,0:T(8,128)S(1)}, bf16[128,2048]{1,0:T(8,128)(2,1)S(1)}, f32[8,128]{1,0:T(8,128)S(1)}) custom-call(bf16[64,4224]{1,0:T(8,128)(2,1)S(1)} %bitcast.6, bf16[4096,2048]{1,0:T(8,128)(2,1)S(1)} %shard_map.94.near_ref.head_ref, f32[64,128]{1,0:T(8,128)S(1)} %get-tuple-element.16.refs_0_), custom_call_target="tpu_custom_call" | custom-call | flops 1073741824 | bytes 17350656 | tf_op jit(solution)/shard_map/pallas_call | solution.py:22
  29.2 0.7 %collective-permute-start.7 = (f32[8,128]{1,0:T(8,128)S(1)}, f32[8,128]{1,0:T(8,128)S(1)}, u32[]{:S(2)}, u32[]{:S(2)}) collective-permute-start(f32[8,128]{1,0:T(8,128)S(1)} %get-tuple-element.17.mine_ref), channel_id=1, source_target_pairs={{0,4},{1,5},{2,6},{3,7},{4,0},{5,1},{6,2},{7,3},{8,12},{9,13},{10,... | collective-permute-start | bytes 12296 | tf_op jit(solution)/shard_map/ppermute | solution.py:256
  29.9 2.7 %shard_map.100.refs_0_ = f32[256,2048]{1,0:T(8,128)S(1)} custom-call(bf16[128,2048]{1,0:T(8,128)(2,1)S(1)} %get-tuple-element.18.one_ref, bf16[128,2048]{1,0:T(8,128)(2,1)S(1)} %get-tuple-element.19.two_ref, bf16[4096,2048]{1,0:T(8,128)(2,1)S(1)} %shard_map.94.near_ref.head_ref), custom_call_target="tpu_custom_call" | custom-call | flops 2147483648 | bytes 17825792 | tf_op jit(solution)/shard_map/pallas_call | solution.py:22
  32.6 1.1 %collective-permute-done.7.refs_0_ = f32[8,128]{1,0:T(8,128)S(1)} collective-permute-done((f32[8,128]{1,0:T(8,128)S(1)}, f32[8,128]{1,0:T(8,128)S(1)}, u32[]{:S(2)}, u32[]{:S(2)}) %collective-permute-start.7) | collective-permute-done | bytes 4128 | tf_op jit(solution)/shard_map/ppermute | solution.py:256
  33.8 2.6 %collective-permute-start.10 = (f32[8,128]{1,0:T(8,128)S(1)}, f32[8,128]{1,0:T(8,128)S(1)}, u32[]{:S(2)}, u32[]{:S(2)}) collective-permute-start(f32[8,128]{1,0:T(8,128)S(1)} %shard_map.97.mine_ref.refs_0_), channel_id=1, source_target_pairs={{0,3},{1,2},{2,1},{3,0},{4,7},{5,6},{6,5},{7,4},{8,11},{9,10},{10,... | collective-permute-start | bytes 12296 | tf_op jit(solution)/shard_map/ppermute | solution.py:256
  37.4 2.7 %shard_map.101.refs_1_ = f32[256,2048]{1,0:T(8,128)S(1)} custom-call(bf16[128,2048]{1,0:T(8,128)(2,1)S(1)} %get-tuple-element.18.one_ref, bf16[128,2048]{1,0:T(8,128)(2,1)S(1)} %get-tuple-element.19.two_ref, bf16[4096,2048]{1,0:T(8,128)(2,1)S(1)} %shard_map.94.near_ref.head_ref, f32[8,128]{1,0:T(8,128)S(1)} %shard_map.97.mine_ref.refs_0_), custom_call_target="tpu_custom_call" | custom-call | flops 2147483648 | bytes 17829888 | tf_op jit(solution)/shard_map/pallas_call | solution.py:22
  41.5 2.2 %collective-permute-start.14 = (f16[16,4096]{1,0:T(8,128)(2,1)S(1)}, f16[16,4096]{1,0:T(8,128)(2,1)S(1)}, u32[]{:S(2)}, u32[]{:S(2)}) collective-permute-start(f16[16,4096]{1,0:T(8,128)(2,1)S(1)} %get-tuple-element.27), channel_id=1, source_target_pairs={{0,3},{1,2},{2,1},{3,0},{4,7},{5,6},{6,5},{7,4},{8,11},{9,10},{10,... | collective-permute-start | bytes 393224 | tf_op jit(solution)/shard_map/ppermute | solution.py:256
  43.7 0.9 %collective-permute-start.16 = (f16[16,4096]{1,0:T(8,128)(2,1)S(1)}, f16[16,4096]{1,0:T(8,128)(2,1)S(1)}, u32[]{:S(2)}, u32[]{:S(2)}) collective-permute-start(f16[16,4096]{1,0:T(8,128)(2,1)S(1)} %get-tuple-element.28), channel_id=1, source_target_pairs={{0,1},{1,0},{2,3},{3,2},{4,5},{5,4},{6,7},{7,6},{8,9},{9,8},{10,11... | collective-permute-start | bytes 393224 | tf_op jit(solution)/shard_map/ppermute | solution.py:256
  45.2 2.2 %collective-permute-start.11 = (f16[16,4096]{1,0:T(8,128)(2,1)S(1)}, f16[16,4096]{1,0:T(8,128)(2,1)S(1)}, u32[]{:S(2)}, u32[]{:S(2)}) collective-permute-start(f16[16,4096]{1,0:T(8,128)(2,1)S(1)} %get-tuple-element.24), channel_id=1, source_target_pairs={{0,3},{1,2},{2,1},{3,0},{4,7},{5,6},{6,5},{7,4},{8,11},{9,10},{10,... | collective-permute-start | bytes 393224 | tf_op jit(solution)/shard_map/ppermute | solution.py:256
  47.4 0.9 %collective-permute-start.13 = (f16[16,4096]{1,0:T(8,128)(2,1)S(1)}, f16[16,4096]{1,0:T(8,128)(2,1)S(1)}, u32[]{:S(2)}, u32[]{:S(2)}) collective-permute-start(f16[16,4096]{1,0:T(8,128)(2,1)S(1)} %get-tuple-element.25), channel_id=1, source_target_pairs={{0,1},{1,0},{2,3},{3,2},{4,5},{5,4},{6,7},{7,6},{8,9},{9,8},{10,11... | collective-permute-start | bytes 393224 | tf_op jit(solution)/shard_map/ppermute | solution.py:256
  48.2 0.7 %collective-permute-done.14 = f16[16,4096]{1,0:T(8,128)(2,1)S(1)} collective-permute-done((f16[16,4096]{1,0:T(8,128)(2,1)S(1)}, f16[16,4096]{1,0:T(8,128)(2,1)S(1)}, u32[]{:S(2)}, u32[]{:S(2)}) %collective-permute-start.14) | collective-permute-done | bytes 131104 | tf_op jit(solution)/shard_map/ppermute | solution.py:256
  49.0 1.6 %collective-permute-start.12 = (f16[16,4096]{1,0:T(8,128)(2,1)S(1)}, f16[16,4096]{1,0:T(8,128)(2,1)S(1)}, u32[]{:S(2)}, u32[]{:S(2)}) collective-permute-start(f16[16,4096]{1,0:T(8,128)(2,1)S(1)} %get-tuple-element.26), channel_id=1, source_target_pairs={{0,2},{1,3},{2,0},{3,1},{4,6},{5,7},{6,4},{7,5},{8,10},{9,11},{10,... | collective-permute-start | bytes 393224 | tf_op jit(solution)/shard_map/ppermute | solution.py:256
  50.6 1.9 %collective-permute-done.16 = f16[16,4096]{1,0:T(8,128)(2,1)S(1)} collective-permute-done((f16[16,4096]{1,0:T(8,128)(2,1)S(1)}, f16[16,4096]{1,0:T(8,128)(2,1)S(1)}, u32[]{:S(2)}, u32[]{:S(2)}) %collective-permute-start.16) | collective-permute-done | bytes 131104 | tf_op jit(solution)/shard_map/ppermute | solution.py:256
  52.6 0.9 %collective-permute-start.17 = (f16[16,4096]{1,0:T(8,128)(2,1)S(1)}, f16[16,4096]{1,0:T(8,128)(2,1)S(1)}, u32[]{:S(2)}, u32[]{:S(2)}) collective-permute-start(f16[16,4096]{1,0:T(8,128)(2,1)S(1)} %fusion.2), channel_id=1, source_target_pairs={{0,4},{1,5},{2,6},{3,7},{4,0},{5,1},{6,2},{7,3},{8,12},{9,13},{10,... | collective-permute-start | bytes 393224 | tf_op jit(solution)/shard_map/ppermute | solution.py:256
  54.4 3.4 %shard_map.104 = (f32[128,2048]{1,0:T(8,128)}, f32[128,2048]{1,0:T(8,128)}) custom-call(bf16[128,4224]{1,0:T(8,128)(2,1)S(1)} %constant_dynamic-update-slice_fusion.rows_ref.digits_ref, bf16[128,4224]{1,0:T(8,128)(2,1)S(1)} %constant_dynamic-update-slice_fusion.rows_ref.digits_ref, f32[8,128]{1,0:T(8,128)S(1)} %shard_map.98.lines_ref, ...), custom_call_target="tpu_custom_call" | custom-call | flops 67108864 | bytes 6291456 | tf_op jit(solution)/shard_map/pallas_call | solution.py:232
  57.8 2.2 %collective-permute-done.17 = f16[16,4096]{1,0:T(8,128)(2,1)S(1)} collective-permute-done((f16[16,4096]{1,0:T(8,128)(2,1)S(1)}, f16[16,4096]{1,0:T(8,128)(2,1)S(1)}, u32[]{:S(2)}, u32[]{:S(2)}) %collective-permute-start.17) | collective-permute-done | bytes 131104 | tf_op jit(solution)/shard_map/ppermute | solution.py:256
  59.9 0.7 %fusion.7 = bf16[16,4096]{1,0:T(8,128)(2,1)} fusion(f32[64,4096]{1,0:T(8,128)S(1)} %shard_map.102, f16[16,4096]{1,0:T(8,128)(2,1)S(1)} %collective-permute-done.17, f16[16,4096]{1,0:T(8,128)(2,1)S(1)} %collective-permute-done.13, f16[16,4096]{1,0:T(8,128)(2,1)S(1)} %collective-permute-done.12, f16[16,4096]{1,0:T(8,128)(2,1)S(1)} %collective-permute-done.11), kind=kLoop, calls=%fused_computation.11 | loop fusion | flops 655360 | bytes 917504 | tf_op jit(solution)/shard_map/convert_element_type | solution.py:367
  (44 shorter events, 5.8 us)
Async XLA Ops:
  1.6 17.1 %collective-permute-start.6 = (bf16[16,4224]{1,0:T(8,128)(2,1)S(1)}, bf16[16,4224]{1,0:T(8,128)(2,1)S(1)}, u32[]{:S(2)}, u32[]{:S(2)}) collective-permute-start(bf16[16,4224]{1,0:T(8,128)(2,1)S(1)} %get-tuple-element.14), channel_id=1, source_target_pairs={{0,3},{1,2},{2,1},{3,0},{4,7},{5,6},{6,5},{7,4},{8,11},{9,10},{10,... | collective-permute-start | bytes 405512 | tf_op jit(solution)/shard_map/ppermute | solution.py:256
  5.6 13.1 %collective-permute-start.5 = (bf16[16,4224]{1,0:T(8,128)(2,1)S(1)}, bf16[16,4224]{1,0:T(8,128)(2,1)S(1)}, u32[]{:S(2)}, u32[]{:S(2)}) collective-permute-start(bf16[16,4224]{1,0:T(8,128)(2,1)S(1)} %get-tuple-element.14), channel_id=1, source_target_pairs={{0,2},{1,3},{2,0},{3,1},{4,6},{5,7},{6,4},{7,5},{8,10},{9,11},{10,... | collective-permute-start | bytes 405512 | tf_op jit(solution)/shard_map/ppermute | solution.py:256
  6.1 12.1 %collective-permute-start.4 = (bf16[16,4224]{1,0:T(8,128)(2,1)S(1)}, bf16[16,4224]{1,0:T(8,128)(2,1)S(1)}, u32[]{:S(2)}, u32[]{:S(2)}) collective-permute-start(bf16[16,4224]{1,0:T(8,128)(2,1)S(1)} %get-tuple-element.14), channel_id=1, source_target_pairs={{0,1},{1,0},{2,3},{3,2},{4,5},{5,4},{6,7},{7,6},{8,9},{9,8},{10,11... | collective-permute-start | bytes 405512 | tf_op jit(solution)/shard_map/ppermute | solution.py:256
  6.3 8.8 %collective-permute-start = (bf16[16,4224]{1,0:T(8,128)(2,1)S(1)}, bf16[16,4224]{1,0:T(8,128)(2,1)S(1)}, u32[]{:S(2)}, u32[]{:S(2)}) collective-permute-start(bf16[16,4224]{1,0:T(8,128)(2,1)S(1)} %get-tuple-element.14), channel_id=1, source_target_pairs={{0,4},{1,5},{2,6},{3,7},{4,0},{5,1},{6,2},{7,3},{8,12},{9,13},{10,... | collective-permute-start | bytes 405512 | tf_op jit(solution)/shard_map/ppermute | solution.py:256
  15.1 7.4 %collective-permute-start.3 = (bf16[16,4224]{1,0:T(8,128)(2,1)S(1)}, bf16[16,4224]{1,0:T(8,128)(2,1)S(1)}, u32[]{:S(2)}, u32[]{:S(2)}) collective-permute-start(bf16[16,4224]{1,0:T(8,128)(2,1)S(1)} %collective-permute-done), channel_id=1, source_target_pairs={{0,3},{1,2},{2,1},{3,0},{4,7},{5,6},{6,5},{7,4},{8,11},{9,10},{10,... | collective-permute-start | bytes 405512 | tf_op jit(solution)/shard_map/ppermute | solution.py:256
  17.7 7.5 %collective-permute-start.2 = (bf16[16,4224]{1,0:T(8,128)(2,1)S(1)}, bf16[16,4224]{1,0:T(8,128)(2,1)S(1)}, u32[]{:S(2)}, u32[]{:S(2)}) collective-permute-start(bf16[16,4224]{1,0:T(8,128)(2,1)S(1)} %collective-permute-done), channel_id=1, source_target_pairs={{0,2},{1,3},{2,0},{3,1},{4,6},{5,7},{6,4},{7,5},{8,10},{9,11},{10,... | collective-permute-start | bytes 405512 | tf_op jit(solution)/shard_map/ppermute | solution.py:256
  18.2 7.2 %collective-permute-start.1 = (bf16[16,4224]{1,0:T(8,128)(2,1)S(1)}, bf16[16,4224]{1,0:T(8,128)(2,1)S(1)}, u32[]{:S(2)}, u32[]{:S(2)}) collective-permute-start(bf16[16,4224]{1,0:T(8,128)(2,1)S(1)} %collective-permute-done), channel_id=1, source_target_pairs={{0,1},{1,0},{2,3},{3,2},{4,5},{5,4},{6,7},{7,6},{8,9},{9,8},{10,11... | collective-permute-start | bytes 405512 | tf_op jit(solution)/shard_map/ppermute | solution.py:256
  29.2 4.5 %collective-permute-start.7 = (f32[8,128]{1,0:T(8,128)S(1)}, f32[8,128]{1,0:T(8,128)S(1)}, u32[]{:S(2)}, u32[]{:S(2)}) collective-permute-start(f32[8,128]{1,0:T(8,128)S(1)} %get-tuple-element.17.mine_ref), channel_id=1, source_target_pairs={{0,4},{1,5},{2,6},{3,7},{4,0},{5,1},{6,2},{7,3},{8,12},{9,13},{10,... | collective-permute-start | bytes 12296 | tf_op jit(solution)/shard_map/ppermute | solution.py:256
  33.8 6.2 %collective-permute-start.10 = (f32[8,128]{1,0:T(8,128)S(1)}, f32[8,128]{1,0:T(8,128)S(1)}, u32[]{:S(2)}, u32[]{:S(2)}) collective-permute-start(f32[8,128]{1,0:T(8,128)S(1)} %shard_map.97.mine_ref.refs_0_), channel_id=1, source_target_pairs={{0,3},{1,2},{2,1},{3,0},{4,7},{5,6},{6,5},{7,4},{8,11},{9,10},{10,... | collective-permute-start | bytes 12296 | tf_op jit(solution)/shard_map/ppermute | solution.py:256
  36.4 3.7 %collective-permute-start.9 = (f32[8,128]{1,0:T(8,128)S(1)}, f32[8,128]{1,0:T(8,128)S(1)}, u32[]{:S(2)}, u32[]{:S(2)}) collective-permute-start(f32[8,128]{1,0:T(8,128)S(1)} %shard_map.97.mine_ref.refs_0_), channel_id=1, source_target_pairs={{0,2},{1,3},{2,0},{3,1},{4,6},{5,7},{6,4},{7,5},{8,10},{9,11},{10,... | collective-permute-start | bytes 12296 | tf_op jit(solution)/shard_map/ppermute | solution.py:256
  36.9 3.6 %collective-permute-start.8 = (f32[8,128]{1,0:T(8,128)S(1)}, f32[8,128]{1,0:T(8,128)S(1)}, u32[]{:S(2)}, u32[]{:S(2)}) collective-permute-start(f32[8,128]{1,0:T(8,128)S(1)} %shard_map.97.mine_ref.refs_0_), channel_id=1, source_target_pairs={{0,1},{1,0},{2,3},{3,2},{4,5},{5,4},{6,7},{7,6},{8,9},{9,8},{10,11... | collective-permute-start | bytes 12296 | tf_op jit(solution)/shard_map/ppermute | solution.py:256
  41.4 13.0 %copy-start.2 = (f32[128,2048]{1,0:T(8,128)S(1)}, f32[128,2048]{1,0:T(8,128)}, u32[]{:S(2)}) copy-start(f32[128,2048]{1,0:T(8,128)} %peer_ref.1) | copy-start | bytes 3145732
  41.5 7.4 %collective-permute-start.14 = (f16[16,4096]{1,0:T(8,128)(2,1)S(1)}, f16[16,4096]{1,0:T(8,128)(2,1)S(1)}, u32[]{:S(2)}, u32[]{:S(2)}) collective-permute-start(f16[16,4096]{1,0:T(8,128)(2,1)S(1)} %get-tuple-element.27), channel_id=1, source_target_pairs={{0,3},{1,2},{2,1},{3,0},{4,7},{5,6},{6,5},{7,4},{8,11},{9,10},{10,... | collective-permute-start | bytes 393224 | tf_op jit(solution)/shard_map/ppermute | solution.py:256
  43.7 8.8 %collective-permute-start.16 = (f16[16,4096]{1,0:T(8,128)(2,1)S(1)}, f16[16,4096]{1,0:T(8,128)(2,1)S(1)}, u32[]{:S(2)}, u32[]{:S(2)}) collective-permute-start(f16[16,4096]{1,0:T(8,128)(2,1)S(1)} %get-tuple-element.28), channel_id=1, source_target_pairs={{0,1},{1,0},{2,3},{3,2},{4,5},{5,4},{6,7},{7,6},{8,9},{9,8},{10,11... | collective-permute-start | bytes 393224 | tf_op jit(solution)/shard_map/ppermute | solution.py:256
  44.6 7.9 %collective-permute-start.15 = (f16[16,4096]{1,0:T(8,128)(2,1)S(1)}, f16[16,4096]{1,0:T(8,128)(2,1)S(1)}, u32[]{:S(2)}, u32[]{:S(2)}) collective-permute-start(f16[16,4096]{1,0:T(8,128)(2,1)S(1)} %get-tuple-element.29), channel_id=1, source_target_pairs={{0,2},{1,3},{2,0},{3,1},{4,6},{5,7},{6,4},{7,5},{8,10},{9,11},{10,... | collective-permute-start | bytes 393224 | tf_op jit(solution)/shard_map/ppermute | solution.py:256
  45.1 9.3 %copy-start.1 = (f32[128,2048]{1,0:T(8,128)S(1)}, f32[128,2048]{1,0:T(8,128)}, u32[]{:S(2)}) copy-start(f32[128,2048]{1,0:T(8,128)} %momentum_ref.1) | copy-start | bytes 3145732
  45.1 9.2 %copy-start = (f32[128,2048]{1,0:T(8,128)S(1)}, f32[128,2048]{1,0:T(8,128)}, u32[]{:S(2)}) copy-start(f32[128,2048]{1,0:T(8,128)} %global_ref.1) | copy-start | bytes 3145732
  45.2 12.6 %collective-permute-start.11 = (f16[16,4096]{1,0:T(8,128)(2,1)S(1)}, f16[16,4096]{1,0:T(8,128)(2,1)S(1)}, u32[]{:S(2)}, u32[]{:S(2)}) collective-permute-start(f16[16,4096]{1,0:T(8,128)(2,1)S(1)} %get-tuple-element.24), channel_id=1, source_target_pairs={{0,3},{1,2},{2,1},{3,0},{4,7},{5,6},{6,5},{7,4},{8,11},{9,10},{10,... | collective-permute-start | bytes 393224 | tf_op jit(solution)/shard_map/ppermute | solution.py:256
  47.4 10.4 %collective-permute-start.13 = (f16[16,4096]{1,0:T(8,128)(2,1)S(1)}, f16[16,4096]{1,0:T(8,128)(2,1)S(1)}, u32[]{:S(2)}, u32[]{:S(2)}) collective-permute-start(f16[16,4096]{1,0:T(8,128)(2,1)S(1)} %get-tuple-element.25), channel_id=1, source_target_pairs={{0,1},{1,0},{2,3},{3,2},{4,5},{5,4},{6,7},{7,6},{8,9},{9,8},{10,11... | collective-permute-start | bytes 393224 | tf_op jit(solution)/shard_map/ppermute | solution.py:256
  49.0 8.8 %collective-permute-start.12 = (f16[16,4096]{1,0:T(8,128)(2,1)S(1)}, f16[16,4096]{1,0:T(8,128)(2,1)S(1)}, u32[]{:S(2)}, u32[]{:S(2)}) collective-permute-start(f16[16,4096]{1,0:T(8,128)(2,1)S(1)} %get-tuple-element.26), channel_id=1, source_target_pairs={{0,2},{1,3},{2,0},{3,1},{4,6},{5,7},{6,4},{7,5},{8,10},{9,11},{10,... | collective-permute-start | bytes 393224 | tf_op jit(solution)/shard_map/ppermute | solution.py:256
  52.6 7.3 %collective-permute-start.17 = (f16[16,4096]{1,0:T(8,128)(2,1)S(1)}, f16[16,4096]{1,0:T(8,128)(2,1)S(1)}, u32[]{:S(2)}, u32[]{:S(2)}) collective-permute-start(f16[16,4096]{1,0:T(8,128)(2,1)S(1)} %fusion.2), channel_id=1, source_target_pairs={{0,4},{1,5},{2,6},{3,7},{4,0},{5,1},{6,2},{7,3},{8,12},{9,13},{10,... | collective-permute-start | bytes 393224 | tf_op jit(solution)/shard_map/ppermute | solution.py:256

commit v11 on v9

--- a/solution.py
+++ b/solution.py
@@ -15,7 +15,7 @@
 VMEM = pl.BlockSpec(memory_space=pltpu.VMEM)
 
 
-def call(kernel, outs, operands, flops=0, scratch=(), sources=None, vmem=16 * 2**20):
+def call(kernel, outs, operands, flops=0, scratch=(), sources=None, vmem=16 * 2**20, aliases={}):
     outs = [pltpu.VMEM(shape, dtype) for shape, dtype in outs]
     places = sources or [pltpu.VMEM] * len(operands)
     moved = sum(x.size * x.dtype.itemsize for x in operands)
@@ -25,28 +25,28 @@
         in_specs=[pl.BlockSpec(memory_space=place) for place in places],
         out_specs=[VMEM] * len(outs),
         scratch_shapes=list(scratch),
+        input_output_aliases=aliases,
         compiler_params=pltpu.CompilerParams(vmem_limit_bytes=vmem),
         cost_estimate=pl.CostEstimate(flops=flops, bytes_accessed=moved, transcendentals=0),
     )(*[pltpu.with_memory_space_constraint(x, place) for x, place in zip(operands, places)])
 
 
-def load_kernel(source, target, sems):
+def head_copies(source, target, sems, half):
     block = source.shape[0] // sems.shape[0]
+    columns = pl.ds(half * (source.shape[1] // 2), source.shape[1] // 2)
     copies = []
     for i in range(sems.shape[0]):
         part = pl.ds(i * block, block)
-        copies.append(pltpu.make_async_copy(source.at[part], target.at[part], sems.at[i]))
+        copies.append(pltpu.make_async_copy(source.at[part, columns], target.at[part, columns], sems.at[i]))
+    return copies
+
+
+def load_kernel(head, near_ref, sems):
+    copies = head_copies(head, near_ref, sems, 0)
     for copy in copies:
         copy.start()
     for copy in copies:
         copy.wait()
-
-
-def resident(head):
-    return call(
-        load_kernel, [(head.shape, head.dtype)], [head],
-        scratch=[pltpu.SemaphoreType.DMA((4,))], sources=[pltpu.HBM],
-    )[0]
 
 
 TILE = 512
@@ -96,28 +96,28 @@
     return jnp.broadcast_to(line, (LANES, line.shape[1])).T[:, 0:1]
 
 
-def rows_kernel(rows_ref, near_ref, *refs):
-    before_ref, (logits_ref, both_ref, stats_ref) = (None, refs) if len(refs) == 3 else (refs[0], refs[1:4])
-    rows = rows_ref.shape[0]
-    depth, width = near_ref.shape
-
-    @pl.loop(0, width // WIDE)
+def logits_of(rows_ref, near_ref, logits_ref, first, count):
+    depth = near_ref.shape[0]
+
+    @pl.loop(0, count // WIDE)
     def _(i):
-        part = pl.ds(pl.multiple_of(i * WIDE, WIDE), WIDE)
+        part = pl.ds(pl.multiple_of(first + i * WIDE, WIDE), WIDE)
         logits_ref[:, part] = jnp.dot(
             rows_ref[:, :depth], near_ref[:, part], preferred_element_type=jnp.float32
         )
 
+
+def softmax_of(rows_ref, logits_ref, both_ref, columns_ref, first):
+    rows, width = logits_ref.shape
+    digits = rows_ref.shape[1] - LANES
     chunk = 32
     offset = lax.axis_index(AXIS) * width
-    columns_ref = stats_ref if before_ref is None else refs[4]
-    first = 0 if before_ref is None else before_ref.shape[0]
 
     @pl.loop(0, rows // chunk)
     def _(i):
         part = pl.ds(pl.multiple_of(i * chunk, chunk), chunk)
         logits = logits_ref[part, :]
-        ids = ids_of(rows_ref[part, depth:]) - offset
+        ids = ids_of(rows_ref[part, digits:]) - offset
         hit = lax.broadcasted_iota(jnp.int32, logits.shape, 1) == ids
         top = jnp.max(logits, axis=1, keepdims=True)
         raised = jnp.exp(logits - top)
@@ -130,9 +130,25 @@
         slot = pl.ds(pl.multiple_of(first + i * chunk, chunk), chunk)
         columns_ref[slot, :] = jnp.where(place == 0, top, jnp.where(place == 1, total, pick))
 
-    if before_ref is not None:
-        columns_ref[pl.ds(0, first), :] = before_ref[...]
-        stats_ref[...] = columns_ref[...].T[:8]
+
+def first_kernel(packed_ref, head, held_ref, near_ref, logits_ref, both_ref, columns_ref, sems):
+    half = near_ref.shape[1] // 2
+    copies = head_copies(head, near_ref, sems, 1)
+    for copy in copies:
+        copy.start()
+    logits_of(packed_ref, near_ref, logits_ref, 0, half)
+    for copy in copies:
+        copy.wait()
+    logits_of(packed_ref, near_ref, logits_ref, half, half)
+    softmax_of(packed_ref, logits_ref, both_ref, columns_ref, 0)
+
+
+def second_kernel(rows_ref, near_ref, before_ref, logits_ref, both_ref, lines_ref, columns_ref):
+    first = before_ref.shape[0]
+    logits_of(rows_ref, near_ref, logits_ref, 0, near_ref.shape[1])
+    softmax_of(rows_ref, logits_ref, both_ref, columns_ref, first)
+    columns_ref[pl.ds(0, first), :] = before_ref[...]
+    lines_ref[...] = columns_ref[...].T[:8]
 
 
 def merge_kernel(steps, members, mine_ref, *refs):
@@ -198,16 +214,18 @@
     loss_ref[...] = jnp.broadcast_to(loss, loss_ref.shape)
 
 
-def frag_kernel(rows_ref, digits_ref, lines_ref, one_ref, two_ref, head_ref, global_ref, momentum_ref,
-                peer_ref, new_global_ref, new_momentum_ref):
+def frag_kernel(rows_one_ref, rows_two_ref, ids_one_ref, ids_two_ref, lines_ref, one_ref, two_ref, head_ref,
+                global_ref, momentum_ref, peer_ref, new_global_ref, new_momentum_ref):
     logits = jnp.concatenate([one_ref[...], two_ref[...]], axis=0)
+    held = jnp.concatenate([rows_one_ref[...], rows_two_ref[...]], axis=0)
+    ids = jnp.concatenate([ids_of(ids_one_ref[...]), ids_of(ids_two_ref[...])], axis=0)
     rows, tile = logits.shape
     top, total = as_columns(lines_ref[0:1, :]), as_columns(lines_ref[1:2, :])
     offset = (lax.axis_index(AXIS) * pl.num_programs(0) + pl.program_id(0)) * tile
-    hit = lax.broadcasted_iota(jnp.int32, (rows, tile), 1) == ids_of(digits_ref[...]) - offset
+    hit = lax.broadcasted_iota(jnp.int32, (rows, tile), 1) == ids - offset
     shares = jnp.exp(logits - top) / total
     dlogits = ((shares - jnp.where(hit, 1.0, 0.0)) / rows).astype(jnp.bfloat16)
-    turned = rows_ref[...].astype(jnp.float32).T.astype(jnp.bfloat16)
+    turned = held.astype(jnp.float32).T.astype(jnp.bfloat16)
     frag_grad = jnp.dot(turned, dlogits, preferred_element_type=jnp.float32)
     local_frag = head_ref[...].astype(jnp.float32) - 1.0 * frag_grad
     pseudo = (global_ref[...] - local_frag + peer_ref[...]) / REPLICAS
@@ -216,20 +234,21 @@
     new_global_ref[...] = global_ref[...] - 0.7 * (pseudo + 0.9 * new_momentum)
 
 
-def frag_update(rows_all, lines, logits, near, global_frag, momentum, peer_delta):
-    rows = rows_all.shape[0]
+def frag_update(held, ids, lines, logits, near, global_frag, momentum, peer_delta):
+    rows = lines.shape[1]
     width = near.shape[1]
-    last = rows_all.shape[1] // LANES - 1
     tile = pl.BlockSpec((FRAG, TILE), lambda i: (0, i))
+
     return pl.pallas_call(
         frag_kernel,
         grid=(width // TILE,),
         out_shape=[jax.ShapeDtypeStruct((FRAG, width), jnp.float32)] * 2,
-        in_specs=[
-            pl.BlockSpec((rows, FRAG), lambda i: (0, 0)),
-            pl.BlockSpec((rows, LANES), lambda i: (0, last)),
-            pl.BlockSpec((8, rows), lambda i: (0, 0)),
+        in_specs=[pl.BlockSpec((x.shape[0], FRAG), lambda i: (0, 0)) for x in held]
+        + [
+            pl.BlockSpec((x.shape[0], LANES), lambda i, last=x.shape[1] // LANES - 1: (0, last))
+            for x in ids
         ]
+        + [pl.BlockSpec((8, rows), lambda i: (0, 0))]
         + [pl.BlockSpec((x.shape[0], TILE), lambda i: (0, i)) for x in logits]
         + [tile] * 4,
         out_specs=[tile, tile],
@@ -238,8 +257,7 @@
             flops=2 * rows * FRAG * width, bytes_accessed=24 * FRAG * width, transcendentals=0
         ),
     )(
-        rows_all, rows_all, lines,
-        *[pltpu.with_memory_space_constraint(x, pltpu.VMEM) for x in logits],
+        *held, *ids, lines, *[pltpu.with_memory_space_constraint(x, pltpu.VMEM) for x in logits],
         pltpu.with_memory_space_constraint(near, pltpu.VMEM), global_frag, momentum, peer_delta,
     )
 
@@ -260,16 +278,13 @@
 def gather_rows(packed):
     own = packed.shape[0]
     held = packed
-    for step in far_steps()[:1]:
-        held = jnp.concatenate([held, swap(held, step)], axis=0)
-    near = [packed] + [swap(packed, step) for step in (3, 2, 1)][::-1]
-    for step in far_steps()[1:]:
+    for step in far_steps():
         held = jnp.concatenate([held, swap(held, step)], axis=0)
     far = held[own:]
-    far = jnp.stack([far] + [swap(far, step) for step in (3, 2, 1)][::-1])
+    near = jnp.concatenate([packed] + [swap(packed, step) for step in (1, 2, 3)], axis=0)
+    far = jnp.stack([far] + [swap(far, step) for step in (1, 2, 3)])
     count = far.shape[1] // own
-    far = far.reshape(4, count, own, -1).swapaxes(0, 1).reshape(4 * count * own, -1)
-    return jnp.concatenate(near, axis=0), far
+    return near, far.reshape(4, count, own, -1).swapaxes(0, 1).reshape(4 * count * own, -1)
 
 
 def scatter_sums(grads_near, grads_far, own):
@@ -308,20 +323,27 @@
         sources=[pltpu.HBM, pltpu.HBM],
     )[0]
     rows_near, rows_far = gather_rows(packed)
-    near = resident(head)
-
-    def part(held, *before):
-        count = held.shape[0]
-        stats = (8, rows) if before else (count, LANES)
-        return call(
-            rows_kernel,
-            [((count, width), jnp.float32), ((2 * count, width), jnp.bfloat16), (stats, jnp.float32)],
-            [held, near, *before], 2 * count * depth * width,
-            scratch=[pltpu.VMEM((rows, LANES), jnp.float32)] if before else [],
-        )
-
-    logits_near, both_near, columns = part(rows_near)
-    logits_far, both_far, mine = part(rows_far, columns)
+    near = call(
+        load_kernel, [(head.shape, head.dtype)], [head],
+        scratch=[pltpu.SemaphoreType.DMA((4,))], sources=[pltpu.HBM],
+    )[0]
+
+    count = 4 * own
+    near, logits_near, both_near, columns = call(
+        first_kernel,
+        [(head.shape, head.dtype), ((count, width), jnp.float32), ((2 * count, width), jnp.bfloat16),
+         ((count, LANES), jnp.float32)],
+        [rows_near, head, near], 2 * count * depth * width,
+        scratch=[pltpu.SemaphoreType.DMA((4,))],
+        sources=[pltpu.VMEM, pltpu.HBM, pltpu.VMEM], aliases={2: 0},
+    )
+    count = rows - 4 * own
+    logits_far, both_far, mine = call(
+        second_kernel,
+        [((count, width), jnp.float32), ((2 * count, width), jnp.bfloat16), ((8, rows), jnp.float32)],
+        [rows_far, near, columns], 2 * count * depth * width,
+        scratch=[pltpu.VMEM((rows, LANES), jnp.float32)],
+    )
 
     lines = mine
     for steps in [[step] for step in far_steps()] + [[1, 2, 3]]:
@@ -351,7 +373,7 @@
     hidden_grad = (scatter_sums(grads_near, grads_far, own) * (1.0 / scale)).astype(jnp.bfloat16)
     loss = call(functools.partial(loss_kernel, members), [((8, LANES), jnp.float32)], [lines])[0]
     new_global, new_momentum = frag_update(
-        jnp.concatenate([rows_near, rows_far], axis=0), lines, [logits_near, logits_far], near,
+        [rows_near, rows_far], [rows_near, rows_far], lines, [logits_near, logits_far], near,
         global_frag, momentum, peer_delta,
     )
     return (loss[0, :1], hidden_grad, new_global, new_momentum)

time: 56.8 us -> 58.2 us (1.025)
  waiting for transfers between devices: 5.95 us -> 7.7 us
    ppermute x18, waiting for transfers between devices: 5.95 us -> 7.7 us  [swap(): lax.ppermute(value, AXIS, [(i, i ^ step) for i in range(lax.axis_size(AXI...]
  transfers between devices with their start and end apart: 18 -> 18, of which waited for: 5 -> 6; matrix products, arithmetic and copies ran while one was open for 2% -> 1% of each run, Pallas kernels for 33% -> 31%
where the time goes in v11:
time: 58.2 us; the launch traced here: 58 us
  starting transfers between devices  23.9 us (41%)
  Pallas kernels  23.8 us (41%)
  waiting for transfers between devices  7.7 us (13%)
  other arithmetic  1.07 us (2%)
  between operations  0.83 us (1%)
  local copies, waits for them, and re-layouts  0.68 us (1%)
    ppermute x18, starting transfers between devices, swap(): lax.ppermute(value, AXIS, [(i, i ^ step) for i in range(lax.axis_size(AXI...  23.9 us
    pallas_call x11, Pallas kernels, call(): pl.pallas_call(kernel, out_shape=outs, in_specs=[pl.BlockSpec(memory_spac...  20.4 us
    ppermute x18, waiting for transfers between devices, swap(): lax.ppermute(value, AXIS, [(i, i ^ step) for i in range(lax.axis_size(AXI...  7.7 us
    pallas_call x1, Pallas kernels, frag_update(): pl.pallas_call(frag_kernel, grid=(width // TILE,), out_shape=[jax.ShapeDt...  3.38 us
  transfers between devices with their start and end apart: 18, of which 6 were waited for; matrix products, arithmetic and copies ran while one was open for 1% of the time, Pallas kernels for 31%

profile of v11, /device:TPU:0, one launch (start us, length us, event | category | flops | bytes accessed | tf_op | source)
XLA Modules:
  0.0 58.0 jit_solution(14966776138264932995)
XLA Ops:
  0.6 0.9 %shard_map.93 = bf16[16,4224]{1,0:T(8,128)(2,1)S(1)} custom-call(s32[16]{0:T(128)} %targets.1, bf16[16,4096]{1,0:T(8,128)(2,1)} %rows.1), custom_call_target="tpu_custom_call" | custom-call | bytes 131136 | tf_op jit(solution)/shard_map/pallas_call | solution.py:22
  1.6 4.1 %collective-permute-start = (bf16[16,4224]{1,0:T(8,128)(2,1)S(1)}, bf16[16,4224]{1,0:T(8,128)(2,1)S(1)}, u32[]{:S(2)}, u32[]{:S(2)}) collective-permute-start(bf16[16,4224]{1,0:T(8,128)(2,1)S(1)} %shard_map.93), channel_id=1, source_target_pairs={{0,4},{1,5},{2,6},{3,7},{4,0},{5,1},{6,2},{7,3},{8,12},{9,13},{10,... | collective-permute-start | bytes 405512 | tf_op jit(solution)/shard_map/ppermute | solution.py:266
  5.7 2.5 %collective-permute-start.6 = (bf16[16,4224]{1,0:T(8,128)(2,1)S(1)}, bf16[16,4224]{1,0:T(8,128)(2,1)S(1)}, u32[]{:S(2)}, u32[]{:S(2)}) collective-permute-start(bf16[16,4224]{1,0:T(8,128)(2,1)S(1)} %shard_map.93), channel_id=1, source_target_pairs={{0,3},{1,2},{2,1},{3,0},{4,7},{5,6},{6,5},{7,4},{8,11},{9,10},{10,... | collective-permute-start | bytes 405512 | tf_op jit(solution)/shard_map/ppermute | solution.py:266
  9.2 3.5 %shard_map.94.held_ref = bf16[4096,2048]{1,0:T(8,128)(2,1)S(1)} custom-call(bf16[4096,2048]{1,0:T(8,128)(2,1)} %head.3), custom_call_target="tpu_custom_call" | custom-call | bytes 16777216 | tf_op jit(solution)/shard_map/pallas_call | solution.py:22
  12.7 2.6 %collective-permute-start.3 = (bf16[16,4224]{1,0:T(8,128)(2,1)S(1)}, bf16[16,4224]{1,0:T(8,128)(2,1)S(1)}, u32[]{:S(2)}, u32[]{:S(2)}) collective-permute-start(bf16[16,4224]{1,0:T(8,128)(2,1)S(1)} %collective-permute-done), channel_id=1, source_target_pairs={{0,3},{1,2},{2,1},{3,0},{4,7},{5,6},{6,5},{7,4},{8,11},{9,10},{10,... | collective-permute-start | bytes 405512 | tf_op jit(solution)/shard_map/ppermute | solution.py:266
  16.2 1.1 %collective-permute-done.5 = bf16[16,4224]{1,0:T(8,128)(2,1)S(1)} collective-permute-done((bf16[16,4224]{1,0:T(8,128)(2,1)S(1)}, bf16[16,4224]{1,0:T(8,128)(2,1)S(1)}, u32[]{:S(2)}, u32[]{:S(2)}) %collective-permute-start.5) | collective-permute-done | bytes 135200 | tf_op jit(solution)/shard_map/ppermute | solution.py:266
  17.4 5.7 %shard_map.95 = (bf16[4096,2048]{1,0:T(8,128)(2,1)S(1)}, f32[64,2048]{1,0:T(8,128)S(1)}, bf16[128,2048]{1,0:T(8,128)(2,1)S(1)}, f32[64,128]{1,0:T(8,128)S(1)}) custom-call(bf16[64,4224]{1,0:T(8,128)(2,1)S(1)} %pad_maximum_fusion.1.packed_ref.rows_one_ref.ids_one_ref, bf16[4096,2048]{1,0:T(8,128)(2,1)} %head.3, ...), custom_call_target="tpu_custom_call", output_to_operand_aliasing={{0}: (2, {})} | custom-call | flops 1073741824 | bytes 34095104 | tf_op jit(solution)/shard_map/pallas_call | solution.py:22
  23.2 3.7 %shard_map.96 = (f32[64,2048]{1,0:T(8,128)S(1)}, bf16[128,2048]{1,0:T(8,128)(2,1)S(1)}, f32[8,128]{1,0:T(8,128)S(1)}) custom-call(bf16[64,4224]{1,0:T(8,128)(2,1)S(1)} %bitcast.6, bf16[4096,2048]{1,0:T(8,128)(2,1)S(1)} %get-tuple-element.13.near_ref.head_ref, f32[64,128]{1,0:T(8,128)S(1)} %get-tuple-element.14.before_ref), custom_call_target="tpu_custom_call" | custom-call | flops 1073741824 | bytes 17350656 | tf_op jit(solution)/shard_map/pallas_call | solution.py:22
  27.8 2.7 %shard_map.100.refs_0_ = f32[256,2048]{1,0:T(8,128)S(1)} custom-call(bf16[128,2048]{1,0:T(8,128)(2,1)S(1)} %get-tuple-element.16.one_ref, bf16[128,2048]{1,0:T(8,128)(2,1)S(1)} %get-tuple-element.17.two_ref, bf16[4096,2048]{1,0:T(8,128)(2,1)S(1)} %get-tuple-element.13.near_ref.head_ref), custom_call_target="tpu_custom_call" | custom-call | flops 2147483648 | bytes 17825792 | tf_op jit(solution)/shard_map/pallas_call | solution.py:22
  30.5 1.0 %collective-permute-done.7.refs_0_ = f32[8,128]{1,0:T(8,128)S(1)} collective-permute-done((f32[8,128]{1,0:T(8,128)S(1)}, f32[8,128]{1,0:T(8,128)S(1)}, u32[]{:S(2)}, u32[]{:S(2)}) %collective-permute-start.7) | collective-permute-done | bytes 4128 | tf_op jit(solution)/shard_map/ppermute | solution.py:266
  31.6 1.7 %collective-permute-start.10 = (f32[8,128]{1,0:T(8,128)S(1)}, f32[8,128]{1,0:T(8,128)S(1)}, u32[]{:S(2)}, u32[]{:S(2)}) collective-permute-start(f32[8,128]{1,0:T(8,128)S(1)} %shard_map.97.mine_ref.refs_0_), channel_id=1, source_target_pairs={{0,3},{1,2},{2,1},{3,0},{4,7},{5,6},{6,5},{7,4},{8,11},{9,10},{10,... | collective-permute-start | bytes 12296 | tf_op jit(solution)/shard_map/ppermute | solution.py:266
  33.8 1.3 %collective-permute-start.8 = (f32[8,128]{1,0:T(8,128)S(1)}, f32[8,128]{1,0:T(8,128)S(1)}, u32[]{:S(2)}, u32[]{:S(2)}) collective-permute-start(f32[8,128]{1,0:T(8,128)S(1)} %shard_map.97.mine_ref.refs_0_), channel_id=1, source_target_pairs={{0,1},{1,0},{2,3},{3,2},{4,5},{5,4},{6,7},{7,6},{8,9},{9,8},{10,11... | collective-permute-start | bytes 12296 | tf_op jit(solution)/shard_map/ppermute | solution.py:266
  35.1 2.7 %shard_map.101.refs_1_ = f32[256,2048]{1,0:T(8,128)S(1)} custom-call(bf16[128,2048]{1,0:T(8,128)(2,1)S(1)} %get-tuple-element.16.one_ref, bf16[128,2048]{1,0:T(8,128)(2,1)S(1)} %get-tuple-element.17.two_ref, bf16[4096,2048]{1,0:T(8,128)(2,1)S(1)} %get-tuple-element.13.near_ref.head_ref, f32[8,128]{1,0:T(8,128)S(1)} %shard_map.97.mine_ref.refs_0_), custom_call_target="tpu_custom_call" | custom-call | flops 2147483648 | bytes 17829888 | tf_op jit(solution)/shard_map/pallas_call | solution.py:22
  38.9 1.7 %collective-permute-start.14 = (f16[16,4096]{1,0:T(8,128)(2,1)S(1)}, f16[16,4096]{1,0:T(8,128)(2,1)S(1)}, u32[]{:S(2)}, u32[]{:S(2)}) collective-permute-start(f16[16,4096]{1,0:T(8,128)(2,1)S(1)} %get-tuple-element.25), channel_id=1, source_target_pairs={{0,3},{1,2},{2,1},{3,0},{4,7},{5,6},{6,5},{7,4},{8,11},{9,10},{10,... | collective-permute-start | bytes 393224 | tf_op jit(solution)/shard_map/ppermute | solution.py:266
  40.6 0.9 %collective-permute-start.16 = (f16[16,4096]{1,0:T(8,128)(2,1)S(1)}, f16[16,4096]{1,0:T(8,128)(2,1)S(1)}, u32[]{:S(2)}, u32[]{:S(2)}) collective-permute-start(f16[16,4096]{1,0:T(8,128)(2,1)S(1)} %get-tuple-element.26), channel_id=1, source_target_pairs={{0,1},{1,0},{2,3},{3,2},{4,5},{5,4},{6,7},{7,6},{8,9},{9,8},{10,11... | collective-permute-start | bytes 393224 | tf_op jit(solution)/shard_map/ppermute | solution.py:266
  41.5 1.0 %collective-permute-start.15 = (f16[16,4096]{1,0:T(8,128)(2,1)S(1)}, f16[16,4096]{1,0:T(8,128)(2,1)S(1)}, u32[]{:S(2)}, u32[]{:S(2)}) collective-permute-start(f16[16,4096]{1,0:T(8,128)(2,1)S(1)} %get-tuple-element.27), channel_id=1, source_target_pairs={{0,2},{1,3},{2,0},{3,1},{4,6},{5,7},{6,4},{7,5},{8,10},{9,11},{10,... | collective-permute-start | bytes 393224 | tf_op jit(solution)/shard_map/ppermute | solution.py:266
  42.5 1.7 %collective-permute-start.11 = (f16[16,4096]{1,0:T(8,128)(2,1)S(1)}, f16[16,4096]{1,0:T(8,128)(2,1)S(1)}, u32[]{:S(2)}, u32[]{:S(2)}) collective-permute-start(f16[16,4096]{1,0:T(8,128)(2,1)S(1)} %get-tuple-element.22), channel_id=1, source_target_pairs={{0,3},{1,2},{2,1},{3,0},{4,7},{5,6},{6,5},{7,4},{8,11},{9,10},{10,... | collective-permute-start | bytes 393224 | tf_op jit(solution)/shard_map/ppermute | solution.py:266
  44.2 0.9 %collective-permute-start.13 = (f16[16,4096]{1,0:T(8,128)(2,1)S(1)}, f16[16,4096]{1,0:T(8,128)(2,1)S(1)}, u32[]{:S(2)}, u32[]{:S(2)}) collective-permute-start(f16[16,4096]{1,0:T(8,128)(2,1)S(1)} %get-tuple-element.23), channel_id=1, source_target_pairs={{0,1},{1,0},{2,3},{3,2},{4,5},{5,4},{6,7},{7,6},{8,9},{9,8},{10,11... | collective-permute-start | bytes 393224 | tf_op jit(solution)/shard_map/ppermute | solution.py:266
  45.1 1.1 %collective-permute-done.14 = f16[16,4096]{1,0:T(8,128)(2,1)S(1)} collective-permute-done((f16[16,4096]{1,0:T(8,128)(2,1)S(1)}, f16[16,4096]{1,0:T(8,128)(2,1)S(1)}, u32[]{:S(2)}, u32[]{:S(2)}) %collective-permute-start.14) | collective-permute-done | bytes 131104 | tf_op jit(solution)/shard_map/ppermute | solution.py:266
  46.2 1.2 %collective-permute-start.12 = (f16[16,4096]{1,0:T(8,128)(2,1)S(1)}, f16[16,4096]{1,0:T(8,128)(2,1)S(1)}, u32[]{:S(2)}, u32[]{:S(2)}) collective-permute-start(f16[16,4096]{1,0:T(8,128)(2,1)S(1)} %get-tuple-element.24), channel_id=1, source_target_pairs={{0,2},{1,3},{2,0},{3,1},{4,6},{5,7},{6,4},{7,5},{8,10},{9,11},{10,... | collective-permute-start | bytes 393224 | tf_op jit(solution)/shard_map/ppermute | solution.py:266
  47.4 1.9 %collective-permute-done.16 = f16[16,4096]{1,0:T(8,128)(2,1)S(1)} collective-permute-done((f16[16,4096]{1,0:T(8,128)(2,1)S(1)}, f16[16,4096]{1,0:T(8,128)(2,1)S(1)}, u32[]{:S(2)}, u32[]{:S(2)}) %collective-permute-start.16) | collective-permute-done | bytes 131104 | tf_op jit(solution)/shard_map/ppermute | solution.py:266
  49.9 1.1 %collective-permute-start.17 = (f16[16,4096]{1,0:T(8,128)(2,1)S(1)}, f16[16,4096]{1,0:T(8,128)(2,1)S(1)}, u32[]{:S(2)}, u32[]{:S(2)}) collective-permute-start(f16[16,4096]{1,0:T(8,128)(2,1)S(1)} %fusion.2), channel_id=1, source_target_pairs={{0,4},{1,5},{2,6},{3,7},{4,0},{5,1},{6,2},{7,3},{8,12},{9,13},{10,... | collective-permute-start | bytes 393224 | tf_op jit(solution)/shard_map/ppermute | solution.py:266
  51.9 3.4 %shard_map.104 = (f32[128,2048]{1,0:T(8,128)}, f32[128,2048]{1,0:T(8,128)}) custom-call(bf16[64,4224]{1,0:T(8,128)(2,1)S(1)} %pad_maximum_fusion.1.packed_ref.rows_one_ref.ids_one_ref, bf16[64,4224]{1,0:T(8,128)(2,1)S(1)} %bitcast.7, bf16[64,4224]{1,0:T(8,128)(2,1)S(1)} %pad_maximum_fusion.1.packed_ref.rows_one_ref.ids_one_ref, ...), custom_call_target="tpu_custom_call" | custom-call | flops 67108864 | bytes 6291456 | tf_op jit(solution)/shard_map/pallas_call | solution.py:242
  55.3 1.9 %collective-permute-done.17 = f16[16,4096]{1,0:T(8,128)(2,1)S(1)} collective-permute-done((f16[16,4096]{1,0:T(8,128)(2,1)S(1)}, f16[16,4096]{1,0:T(8,128)(2,1)S(1)}, u32[]{:S(2)}, u32[]{:S(2)}) %collective-permute-start.17) | collective-permute-done | bytes 131104 | tf_op jit(solution)/shard_map/ppermute | solution.py:266
  (39 shorter events, 6.8 us)
Async XLA Ops:
  1.6 11.1 %collective-permute-start = (bf16[16,4224]{1,0:T(8,128)(2,1)S(1)}, bf16[16,4224]{1,0:T(8,128)(2,1)S(1)}, u32[]{:S(2)}, u32[]{:S(2)}) collective-permute-start(bf16[16,4224]{1,0:T(8,128)(2,1)S(1)} %shard_map.93), channel_id=1, source_target_pairs={{0,4},{1,5},{2,6},{3,7},{4,0},{5,1},{6,2},{7,3},{8,12},{9,13},{10,... | collective-permute-start | bytes 405512 | tf_op jit(solution)/shard_map/ppermute | solution.py:266
  5.7 10.1 %collective-permute-start.6 = (bf16[16,4224]{1,0:T(8,128)(2,1)S(1)}, bf16[16,4224]{1,0:T(8,128)(2,1)S(1)}, u32[]{:S(2)}, u32[]{:S(2)}) collective-permute-start(bf16[16,4224]{1,0:T(8,128)(2,1)S(1)} %shard_map.93), channel_id=1, source_target_pairs={{0,3},{1,2},{2,1},{3,0},{4,7},{5,6},{6,5},{7,4},{8,11},{9,10},{10,... | collective-permute-start | bytes 405512 | tf_op jit(solution)/shard_map/ppermute | solution.py:266
  8.2 9.2 %collective-permute-start.5 = (bf16[16,4224]{1,0:T(8,128)(2,1)S(1)}, bf16[16,4224]{1,0:T(8,128)(2,1)S(1)}, u32[]{:S(2)}, u32[]{:S(2)}) collective-permute-start(bf16[16,4224]{1,0:T(8,128)(2,1)S(1)} %shard_map.93), channel_id=1, source_target_pairs={{0,2},{1,3},{2,0},{3,1},{4,6},{5,7},{6,4},{7,5},{8,10},{9,11},{10,... | collective-permute-start | bytes 405512 | tf_op jit(solution)/shard_map/ppermute | solution.py:266
  8.6 8.7 %collective-permute-start.4 = (bf16[16,4224]{1,0:T(8,128)(2,1)S(1)}, bf16[16,4224]{1,0:T(8,128)(2,1)S(1)}, u32[]{:S(2)}, u32[]{:S(2)}) collective-permute-start(bf16[16,4224]{1,0:T(8,128)(2,1)S(1)} %shard_map.93), channel_id=1, source_target_pairs={{0,1},{1,0},{2,3},{3,2},{4,5},{5,4},{6,7},{7,6},{8,9},{9,8},{10,11... | collective-permute-start | bytes 405512 | tf_op jit(solution)/shard_map/ppermute | solution.py:266
  12.7 10.4 %collective-permute-start.3 = (bf16[16,4224]{1,0:T(8,128)(2,1)S(1)}, bf16[16,4224]{1,0:T(8,128)(2,1)S(1)}, u32[]{:S(2)}, u32[]{:S(2)}) collective-permute-start(bf16[16,4224]{1,0:T(8,128)(2,1)S(1)} %collective-permute-done), channel_id=1, source_target_pairs={{0,3},{1,2},{2,1},{3,0},{4,7},{5,6},{6,5},{7,4},{8,11},{9,10},{10,... | collective-permute-start | bytes 405512 | tf_op jit(solution)/shard_map/ppermute | solution.py:266
  15.3 7.8 %collective-permute-start.2 = (bf16[16,4224]{1,0:T(8,128)(2,1)S(1)}, bf16[16,4224]{1,0:T(8,128)(2,1)S(1)}, u32[]{:S(2)}, u32[]{:S(2)}) collective-permute-start(bf16[16,4224]{1,0:T(8,128)(2,1)S(1)} %collective-permute-done), channel_id=1, source_target_pairs={{0,2},{1,3},{2,0},{3,1},{4,6},{5,7},{6,4},{7,5},{8,10},{9,11},{10,... | collective-permute-start | bytes 405512 | tf_op jit(solution)/shard_map/ppermute | solution.py:266
  15.7 7.4 %collective-permute-start.1 = (bf16[16,4224]{1,0:T(8,128)(2,1)S(1)}, bf16[16,4224]{1,0:T(8,128)(2,1)S(1)}, u32[]{:S(2)}, u32[]{:S(2)}) collective-permute-start(bf16[16,4224]{1,0:T(8,128)(2,1)S(1)} %collective-permute-done), channel_id=1, source_target_pairs={{0,1},{1,0},{2,3},{3,2},{4,5},{5,4},{6,7},{7,6},{8,9},{9,8},{10,11... | collective-permute-start | bytes 405512 | tf_op jit(solution)/shard_map/ppermute | solution.py:266
  26.9 4.5 %collective-permute-start.7 = (f32[8,128]{1,0:T(8,128)S(1)}, f32[8,128]{1,0:T(8,128)S(1)}, u32[]{:S(2)}, u32[]{:S(2)}) collective-permute-start(f32[8,128]{1,0:T(8,128)S(1)} %get-tuple-element.15.mine_ref), channel_id=1, source_target_pairs={{0,4},{1,5},{2,6},{3,7},{4,0},{5,1},{6,2},{7,3},{8,12},{9,13},{10,... | collective-permute-start | bytes 12296 | tf_op jit(solution)/shard_map/ppermute | solution.py:266
  31.6 6.2 %collective-permute-start.10 = (f32[8,128]{1,0:T(8,128)S(1)}, f32[8,128]{1,0:T(8,128)S(1)}, u32[]{:S(2)}, u32[]{:S(2)}) collective-permute-start(f32[8,128]{1,0:T(8,128)S(1)} %shard_map.97.mine_ref.refs_0_), channel_id=1, source_target_pairs={{0,3},{1,2},{2,1},{3,0},{4,7},{5,6},{6,5},{7,4},{8,11},{9,10},{10,... | collective-permute-start | bytes 12296 | tf_op jit(solution)/shard_map/ppermute | solution.py:266
  33.3 4.6 %collective-permute-start.9 = (f32[8,128]{1,0:T(8,128)S(1)}, f32[8,128]{1,0:T(8,128)S(1)}, u32[]{:S(2)}, u32[]{:S(2)}) collective-permute-start(f32[8,128]{1,0:T(8,128)S(1)} %shard_map.97.mine_ref.refs_0_), channel_id=1, source_target_pairs={{0,2},{1,3},{2,0},{3,1},{4,6},{5,7},{6,4},{7,5},{8,10},{9,11},{10,... | collective-permute-start | bytes 12296 | tf_op jit(solution)/shard_map/ppermute | solution.py:266
  33.8 4.0 %collective-permute-start.8 = (f32[8,128]{1,0:T(8,128)S(1)}, f32[8,128]{1,0:T(8,128)S(1)}, u32[]{:S(2)}, u32[]{:S(2)}) collective-permute-start(f32[8,128]{1,0:T(8,128)S(1)} %shard_map.97.mine_ref.refs_0_), channel_id=1, source_target_pairs={{0,1},{1,0},{2,3},{3,2},{4,5},{5,4},{6,7},{7,6},{8,9},{9,8},{10,11... | collective-permute-start | bytes 12296 | tf_op jit(solution)/shard_map/ppermute | solution.py:266
  38.7 13.2 %copy-start.2 = (f32[128,2048]{1,0:T(8,128)S(1)}, f32[128,2048]{1,0:T(8,128)}, u32[]{:S(2)}) copy-start(f32[128,2048]{1,0:T(8,128)} %peer_ref.1) | copy-start | bytes 3145732
  38.8 13.1 %copy-start = (f32[128,2048]{1,0:T(8,128)S(1)}, f32[128,2048]{1,0:T(8,128)}, u32[]{:S(2)}) copy-start(f32[128,2048]{1,0:T(8,128)} %global_ref.1) | copy-start | bytes 3145732
  38.8 13.1 %copy-start.1 = (f32[128,2048]{1,0:T(8,128)S(1)}, f32[128,2048]{1,0:T(8,128)}, u32[]{:S(2)}) copy-start(f32[128,2048]{1,0:T(8,128)} %momentum_ref.1) | copy-start | bytes 3145732
  38.9 7.4 %collective-permute-start.14 = (f16[16,4096]{1,0:T(8,128)(2,1)S(1)}, f16[16,4096]{1,0:T(8,128)(2,1)S(1)}, u32[]{:S(2)}, u32[]{:S(2)}) collective-permute-start(f16[16,4096]{1,0:T(8,128)(2,1)S(1)} %get-tuple-element.25), channel_id=1, source_target_pairs={{0,3},{1,2},{2,1},{3,0},{4,7},{5,6},{6,5},{7,4},{8,11},{9,10},{10,... | collective-permute-start | bytes 393224 | tf_op jit(solution)/shard_map/ppermute | solution.py:266
  40.6 8.7 %collective-permute-start.16 = (f16[16,4096]{1,0:T(8,128)(2,1)S(1)}, f16[16,4096]{1,0:T(8,128)(2,1)S(1)}, u32[]{:S(2)}, u32[]{:S(2)}) collective-permute-start(f16[16,4096]{1,0:T(8,128)(2,1)S(1)} %get-tuple-element.26), channel_id=1, source_target_pairs={{0,1},{1,0},{2,3},{3,2},{4,5},{5,4},{6,7},{7,6},{8,9},{9,8},{10,11... | collective-permute-start | bytes 393224 | tf_op jit(solution)/shard_map/ppermute | solution.py:266
  41.5 8.4 %collective-permute-start.15 = (f16[16,4096]{1,0:T(8,128)(2,1)S(1)}, f16[16,4096]{1,0:T(8,128)(2,1)S(1)}, u32[]{:S(2)}, u32[]{:S(2)}) collective-permute-start(f16[16,4096]{1,0:T(8,128)(2,1)S(1)} %get-tuple-element.27), channel_id=1, source_target_pairs={{0,2},{1,3},{2,0},{3,1},{4,6},{5,7},{6,4},{7,5},{8,10},{9,11},{10,... | collective-permute-start | bytes 393224 | tf_op jit(solution)/shard_map/ppermute | solution.py:266
  42.5 12.8 %collective-permute-start.11 = (f16[16,4096]{1,0:T(8,128)(2,1)S(1)}, f16[16,4096]{1,0:T(8,128)(2,1)S(1)}, u32[]{:S(2)}, u32[]{:S(2)}) collective-permute-start(f16[16,4096]{1,0:T(8,128)(2,1)S(1)} %get-tuple-element.22), channel_id=1, source_target_pairs={{0,3},{1,2},{2,1},{3,0},{4,7},{5,6},{6,5},{7,4},{8,11},{9,10},{10,... | collective-permute-start | bytes 393224 | tf_op jit(solution)/shard_map/ppermute | solution.py:266
  44.2 11.1 %collective-permute-start.13 = (f16[16,4096]{1,0:T(8,128)(2,1)S(1)}, f16[16,4096]{1,0:T(8,128)(2,1)S(1)}, u32[]{:S(2)}, u32[]{:S(2)}) collective-permute-start(f16[16,4096]{1,0:T(8,128)(2,1)S(1)} %get-tuple-element.23), channel_id=1, source_target_pairs={{0,1},{1,0},{2,3},{3,2},{4,5},{5,4},{6,7},{7,6},{8,9},{9,8},{10,11... | collective-permute-start | bytes 393224 | tf_op jit(solution)/shard_map/ppermute | solution.py:266
  46.2 9.1 %collective-permute-start.12 = (f16[16,4096]{1,0:T(8,128)(2,1)S(1)}, f16[16,4096]{1,0:T(8,128)(2,1)S(1)}, u32[]{:S(2)}, u32[]{:S(2)}) collective-permute-start(f16[16,4096]{1,0:T(8,128)(2,1)S(1)} %get-tuple-element.24), channel_id=1, source_target_pairs={{0,2},{1,3},{2,0},{3,1},{4,6},{5,7},{6,4},{7,5},{8,10},{9,11},{10,... | collective-permute-start | bytes 393224 | tf_op jit(solution)/shard_map/ppermute | solution.py:266
  49.9 7.3 %collective-permute-start.17 = (f16[16,4096]{1,0:T(8,128)(2,1)S(1)}, f16[16,4096]{1,0:T(8,128)(2,1)S(1)}, u32[]{:S(2)}, u32[]{:S(2)}) collective-permute-start(f16[16,4096]{1,0:T(8,128)(2,1)S(1)} %fusion.2), channel_id=1, source_target_pairs={{0,4},{1,5},{2,6},{3,7},{4,0},{5,1},{6,2},{7,3},{8,12},{9,13},{10,... | collective-permute-start | bytes 393224 | tf_op jit(solution)/shard_map/ppermute | solution.py:266

commit v12 on v11

--- a/solution.py
+++ b/solution.py
@@ -29,24 +29,6 @@
         compiler_params=pltpu.CompilerParams(vmem_limit_bytes=vmem),
         cost_estimate=pl.CostEstimate(flops=flops, bytes_accessed=moved, transcendentals=0),
     )(*[pltpu.with_memory_space_constraint(x, place) for x, place in zip(operands, places)])
-
-
-def head_copies(source, target, sems, half):
-    block = source.shape[0] // sems.shape[0]
-    columns = pl.ds(half * (source.shape[1] // 2), source.shape[1] // 2)
-    copies = []
-    for i in range(sems.shape[0]):
-        part = pl.ds(i * block, block)
-        copies.append(pltpu.make_async_copy(source.at[part, columns], target.at[part, columns], sems.at[i]))
-    return copies
-
-
-def load_kernel(head, near_ref, sems):
-    copies = head_copies(head, near_ref, sems, 0)
-    for copy in copies:
-        copy.start()
-    for copy in copies:
-        copy.wait()
 
 
 TILE = 512
@@ -131,15 +113,8 @@
         columns_ref[slot, :] = jnp.where(place == 0, top, jnp.where(place == 1, total, pick))
 
 
-def first_kernel(packed_ref, head, held_ref, near_ref, logits_ref, both_ref, columns_ref, sems):
-    half = near_ref.shape[1] // 2
-    copies = head_copies(head, near_ref, sems, 1)
-    for copy in copies:
-        copy.start()
-    logits_of(packed_ref, near_ref, logits_ref, 0, half)
-    for copy in copies:
-        copy.wait()
-    logits_of(packed_ref, near_ref, logits_ref, half, half)
+def first_kernel(packed_ref, near_ref, logits_ref, both_ref, columns_ref):
+    logits_of(packed_ref, near_ref, logits_ref, 0, near_ref.shape[1])
     softmax_of(packed_ref, logits_ref, both_ref, columns_ref, 0)
 
 
@@ -275,12 +250,17 @@
     return steps
 
 
-def gather_rows(packed):
+def relay_kernel(far_ref, near_ref, out_ref):
+    out_ref[...] = far_ref[...]
+
+
+def gather_rows(packed, near):
     own = packed.shape[0]
     held = packed
     for step in far_steps():
         held = jnp.concatenate([held, swap(held, step)], axis=0)
     far = held[own:]
+    far = call(relay_kernel, [(far.shape, far.dtype)], [far, near])[0]
     near = jnp.concatenate([packed] + [swap(packed, step) for step in (1, 2, 3)], axis=0)
     far = jnp.stack([far] + [swap(far, step) for step in (1, 2, 3)])
     count = far.shape[1] // own
@@ -322,20 +302,15 @@
         scratch=[pltpu.SMEM(targets.shape, targets.dtype), pltpu.SemaphoreType.DMA((2,))],
         sources=[pltpu.HBM, pltpu.HBM],
     )[0]
-    rows_near, rows_far = gather_rows(packed)
-    near = call(
-        load_kernel, [(head.shape, head.dtype)], [head],
-        scratch=[pltpu.SemaphoreType.DMA((4,))], sources=[pltpu.HBM],
-    )[0]
+    near = swap(head, 0)
+    rows_near, rows_far = gather_rows(packed, near)
 
     count = 4 * own
-    near, logits_near, both_near, columns = call(
+    logits_near, both_near, columns = call(
         first_kernel,
-        [(head.shape, head.dtype), ((count, width), jnp.float32), ((2 * count, width), jnp.bfloat16),
+        [((count, width), jnp.float32), ((2 * count, width), jnp.bfloat16),
          ((count, LANES), jnp.float32)],
-        [rows_near, head, near], 2 * count * depth * width,
-        scratch=[pltpu.SemaphoreType.DMA((4,))],
-        sources=[pltpu.VMEM, pltpu.HBM, pltpu.VMEM], aliases={2: 0},
+        [rows_near, near], 2 * count * depth * width,
     )
     count = rows - 4 * own
     logits_far, both_far, mine = call(

time: 58.2 us -> 62.3 us (1.070)
  starting transfers between devices: 23.9 us -> 31.7 us
  Pallas kernels: 23.8 us -> 18.3 us
  waiting for transfers between devices: 7.7 us -> 9.56 us
    ppermute x18 -> x19, starting transfers between devices: 23.9 us -> 31.7 us  [swap(): lax.ppermute(value, AXIS, [(i, i ^ step) for i in range(lax.axis_size(AXI...]
    pallas_call x11, Pallas kernels: 20.4 us -> 14.9 us  [call(): pl.pallas_call(kernel, out_shape=outs, in_specs=[pl.BlockSpec(memory_spac...]
    ppermute x18 -> x19, waiting for transfers between devices: 7.7 us -> 9.56 us  [swap(): lax.ppermute(value, AXIS, [(i, i ^ step) for i in range(lax.axis_size(AXI...]
  transfers between devices with their start and end apart: 18 -> 19, of which waited for: 6 -> 7; matrix products, arithmetic and copies ran while one was open for 1% -> 1% of each run, Pallas kernels for 31% -> 22%
where the time goes in v12:
time: 62.3 us; the launch traced here: 62.1 us
  starting transfers between devices  31.7 us (51%)
  Pallas kernels  18.3 us (29%)
  waiting for transfers between devices  9.56 us (15%)
  other arithmetic  1.07 us (2%)
  between operations  0.76 us (1%)
  local copies, waits for them, and re-layouts  0.67 us (1%)
    ppermute x19, starting transfers between devices, swap(): lax.ppermute(value, AXIS, [(i, i ^ step) for i in range(lax.axis_size(AXI...  31.7 us
    pallas_call x11, Pallas kernels, call(): pl.pallas_call(kernel, out_shape=outs, in_specs=[pl.BlockSpec(memory_spac...  14.9 us
    ppermute x19, waiting for transfers between devices, swap(): lax.ppermute(value, AXIS, [(i, i ^ step) for i in range(lax.axis_size(AXI...  9.56 us
    pallas_call x1, Pallas kernels, frag_update(): pl.pallas_call(frag_kernel, grid=(width // TILE,), out_shape=[jax.ShapeDt...  3.38 us
  transfers between devices with their start and end apart: 19, of which 7 were waited for; matrix products, arithmetic and copies ran while one was open for 1% of the time, Pallas kernels for 22%

profile of v12, /device:TPU:0, one launch (start us, length us, event | category | flops | bytes accessed | tf_op | source)
XLA Modules:
  0.0 62.1 jit_solution(1661747425551062949)
XLA Ops:
  0.6 5.8 %collective-permute-start.1 = (bf16[4096,2048]{1,0:T(8,128)(2,1)}, bf16[4096,2048]{1,0:T(8,128)(2,1)S(1)}, u32[]{:S(2)}, u32[]{:S(2)}) collective-permute-start(bf16[4096,2048]{1,0:T(8,128)(2,1)} %param.8), channel_id=1, source_target_pairs={{0,0},{1,1},{2,2},{3,3},{4,4},{5,5},{6,6},{7,7},{8,8},{9,9},{10,10... | collective-permute-start | bytes 50331656 | tf_op jit(solution)/shard_map/ppermute | solution.py:241
  6.4 0.9 %shard_map.93 = bf16[16,4224]{1,0:T(8,128)(2,1)S(1)} custom-call(s32[16]{0:T(128)} %targets.1, bf16[16,4096]{1,0:T(8,128)(2,1)} %rows.1), custom_call_target="tpu_custom_call" | custom-call | bytes 131136 | tf_op jit(solution)/shard_map/pallas_call | solution.py:22
  7.3 4.1 %collective-permute-start = (bf16[16,4224]{1,0:T(8,128)(2,1)S(1)}, bf16[16,4224]{1,0:T(8,128)(2,1)S(1)}, u32[]{:S(2)}, u32[]{:S(2)}) collective-permute-start(bf16[16,4224]{1,0:T(8,128)(2,1)S(1)} %shard_map.93), channel_id=1, source_target_pairs={{0,4},{1,5},{2,6},{3,7},{4,0},{5,1},{6,2},{7,3},{8,12},{9,13},{10,... | collective-permute-start | bytes 405512 | tf_op jit(solution)/shard_map/ppermute | solution.py:241
  11.4 1.5 %collective-permute-start.5 = (bf16[16,4224]{1,0:T(8,128)(2,1)S(1)}, bf16[16,4224]{1,0:T(8,128)(2,1)S(1)}, u32[]{:S(2)}, u32[]{:S(2)}) collective-permute-start(bf16[16,4224]{1,0:T(8,128)(2,1)S(1)} %shard_map.93), channel_id=1, source_target_pairs={{0,1},{1,0},{2,3},{3,2},{4,5},{5,4},{6,7},{7,6},{8,9},{9,8},{10,11... | collective-permute-start | bytes 405512 | tf_op jit(solution)/shard_map/ppermute | solution.py:241
  13.0 1.6 %collective-permute-start.6 = (bf16[16,4224]{1,0:T(8,128)(2,1)S(1)}, bf16[16,4224]{1,0:T(8,128)(2,1)S(1)}, u32[]{:S(2)}, u32[]{:S(2)}) collective-permute-start(bf16[16,4224]{1,0:T(8,128)(2,1)S(1)} %shard_map.93), channel_id=1, source_target_pairs={{0,2},{1,3},{2,0},{3,1},{4,6},{5,7},{6,4},{7,5},{8,10},{9,11},{10,... | collective-permute-start | bytes 405512 | tf_op jit(solution)/shard_map/ppermute | solution.py:241
  14.9 3.1 %collective-permute-done.far_ref = bf16[16,4224]{1,0:T(8,128)(2,1)S(1)} collective-permute-done((bf16[16,4224]{1,0:T(8,128)(2,1)S(1)}, bf16[16,4224]{1,0:T(8,128)(2,1)S(1)}, u32[]{:S(2)}, u32[]{:S(2)}) %collective-permute-start) | collective-permute-done | bytes 135200 | tf_op jit(solution)/shard_map/ppermute | solution.py:241
  18.0 1.6 %collective-permute-start.2 = (bf16[16,4224]{1,0:T(8,128)(2,1)S(1)}, bf16[16,4224]{1,0:T(8,128)(2,1)S(1)}, u32[]{:S(2)}, u32[]{:S(2)}) collective-permute-start(bf16[16,4224]{1,0:T(8,128)(2,1)S(1)} %shard_map.94), channel_id=1, source_target_pairs={{0,1},{1,0},{2,3},{3,2},{4,5},{5,4},{6,7},{7,6},{8,9},{9,8},{10,11... | collective-permute-start | bytes 405512 | tf_op jit(solution)/shard_map/ppermute | solution.py:241
  20.3 1.3 %collective-permute-start.4 = (bf16[16,4224]{1,0:T(8,128)(2,1)S(1)}, bf16[16,4224]{1,0:T(8,128)(2,1)S(1)}, u32[]{:S(2)}, u32[]{:S(2)}) collective-permute-start(bf16[16,4224]{1,0:T(8,128)(2,1)S(1)} %shard_map.94), channel_id=1, source_target_pairs={{0,3},{1,2},{2,1},{3,0},{4,7},{5,6},{6,5},{7,4},{8,11},{9,10},{10,... | collective-permute-start | bytes 405512 | tf_op jit(solution)/shard_map/ppermute | solution.py:241
  21.6 2.0 %collective-permute-done.7 = bf16[16,4224]{1,0:T(8,128)(2,1)S(1)} collective-permute-done((bf16[16,4224]{1,0:T(8,128)(2,1)S(1)}, bf16[16,4224]{1,0:T(8,128)(2,1)S(1)}, u32[]{:S(2)}, u32[]{:S(2)}) %collective-permute-start.7) | collective-permute-done | bytes 135200 | tf_op jit(solution)/shard_map/ppermute | solution.py:241
  23.6 3.7 %shard_map.95 = (f32[64,2048]{1,0:T(8,128)S(1)}, bf16[128,2048]{1,0:T(8,128)(2,1)S(1)}, f32[64,128]{1,0:T(8,128)S(1)}) custom-call(bf16[64,4224]{1,0:T(8,128)(2,1)S(1)} %pad_maximum_fusion.1.packed_ref.rows_one_ref.ids_one_ref, bf16[4096,2048]{1,0:T(8,128)(2,1)S(1)} %collective-permute-done.1.near_ref.head_ref), custom_call_target="tpu_custom_call" | custom-call | flops 1073741824 | bytes 17317888 | tf_op jit(solution)/shard_map/pallas_call | solution.py:22
  28.3 3.7 %shard_map.96 = (f32[64,2048]{1,0:T(8,128)S(1)}, bf16[128,2048]{1,0:T(8,128)(2,1)S(1)}, f32[8,128]{1,0:T(8,128)S(1)}) custom-call(bf16[64,4224]{1,0:T(8,128)(2,1)S(1)} %bitcast.6, bf16[4096,2048]{1,0:T(8,128)(2,1)S(1)} %collective-permute-done.1.near_ref.head_ref, f32[64,128]{1,0:T(8,128)S(1)} %get-tuple-element.12.before_ref), custom_call_target="tpu_custom_call" | custom-call | flops 1073741824 | bytes 17350656 | tf_op jit(solution)/shard_map/pallas_call | solution.py:22
  32.0 1.8 %collective-permute-start.8 = (f32[8,128]{1,0:T(8,128)S(1)}, f32[8,128]{1,0:T(8,128)S(1)}, u32[]{:S(2)}, u32[]{:S(2)}) collective-permute-start(f32[8,128]{1,0:T(8,128)S(1)} %get-tuple-element.13.mine_ref), channel_id=1, source_target_pairs={{0,4},{1,5},{2,6},{3,7},{4,0},{5,1},{6,2},{7,3},{8,12},{9,13},{10,... | collective-permute-start | bytes 12296 | tf_op jit(solution)/shard_map/ppermute | solution.py:241
  33.9 2.7 %shard_map.100.refs_0_ = f32[256,2048]{1,0:T(8,128)S(1)} custom-call(bf16[128,2048]{1,0:T(8,128)(2,1)S(1)} %get-tuple-element.14.one_ref, bf16[128,2048]{1,0:T(8,128)(2,1)S(1)} %get-tuple-element.15.two_ref, bf16[4096,2048]{1,0:T(8,128)(2,1)S(1)} %collective-permute-done.1.near_ref.head_ref), custom_call_target="tpu_custom_call" | custom-call | flops 2147483648 | bytes 17825792 | tf_op jit(solution)/shard_map/pallas_call | solution.py:22
  36.7 1.8 %collective-permute-start.10 = (f32[8,128]{1,0:T(8,128)S(1)}, f32[8,128]{1,0:T(8,128)S(1)}, u32[]{:S(2)}, u32[]{:S(2)}) collective-permute-start(f32[8,128]{1,0:T(8,128)S(1)} %shard_map.97.mine_ref.refs_0_), channel_id=1, source_target_pairs={{0,2},{1,3},{2,0},{3,1},{4,6},{5,7},{6,4},{7,5},{8,10},{9,11},{10,... | collective-permute-start | bytes 12296 | tf_op jit(solution)/shard_map/ppermute | solution.py:241
  38.4 1.2 %collective-permute-start.11 = (f32[8,128]{1,0:T(8,128)S(1)}, f32[8,128]{1,0:T(8,128)S(1)}, u32[]{:S(2)}, u32[]{:S(2)}) collective-permute-start(f32[8,128]{1,0:T(8,128)S(1)} %shard_map.97.mine_ref.refs_0_), channel_id=1, source_target_pairs={{0,3},{1,2},{2,1},{3,0},{4,7},{5,6},{6,5},{7,4},{8,11},{9,10},{10,... | collective-permute-start | bytes 12296 | tf_op jit(solution)/shard_map/ppermute | solution.py:241
  40.2 2.7 %shard_map.101.refs_1_ = f32[256,2048]{1,0:T(8,128)S(1)} custom-call(bf16[128,2048]{1,0:T(8,128)(2,1)S(1)} %get-tuple-element.14.one_ref, bf16[128,2048]{1,0:T(8,128)(2,1)S(1)} %get-tuple-element.15.two_ref, bf16[4096,2048]{1,0:T(8,128)(2,1)S(1)} %collective-permute-done.1.near_ref.head_ref, f32[8,128]{1,0:T(8,128)S(1)} %shard_map.97.mine_ref.refs_0_), custom_call_target="tpu_custom_call" | custom-call | flops 2147483648 | bytes 17829888 | tf_op jit(solution)/shard_map/pallas_call | solution.py:22
  44.2 2.4 %collective-permute-start.15 = (f16[16,4096]{1,0:T(8,128)(2,1)S(1)}, f16[16,4096]{1,0:T(8,128)(2,1)S(1)}, u32[]{:S(2)}, u32[]{:S(2)}) collective-permute-start(f16[16,4096]{1,0:T(8,128)(2,1)S(1)} %get-tuple-element.23), channel_id=1, source_target_pairs={{0,3},{1,2},{2,1},{3,0},{4,7},{5,6},{6,5},{7,4},{8,11},{9,10},{10,... | collective-permute-start | bytes 393224 | tf_op jit(solution)/shard_map/ppermute | solution.py:241
  47.9 2.4 %collective-permute-start.12 = (f16[16,4096]{1,0:T(8,128)(2,1)S(1)}, f16[16,4096]{1,0:T(8,128)(2,1)S(1)}, u32[]{:S(2)}, u32[]{:S(2)}) collective-permute-start(f16[16,4096]{1,0:T(8,128)(2,1)S(1)} %get-tuple-element.20), channel_id=1, source_target_pairs={{0,3},{1,2},{2,1},{3,0},{4,7},{5,6},{6,5},{7,4},{8,11},{9,10},{10,... | collective-permute-start | bytes 393224 | tf_op jit(solution)/shard_map/ppermute | solution.py:241
  50.6 0.9 %collective-permute-done.15 = f16[16,4096]{1,0:T(8,128)(2,1)S(1)} collective-permute-done((f16[16,4096]{1,0:T(8,128)(2,1)S(1)}, f16[16,4096]{1,0:T(8,128)(2,1)S(1)}, u32[]{:S(2)}, u32[]{:S(2)}) %collective-permute-start.15) | collective-permute-done | bytes 131104 | tf_op jit(solution)/shard_map/ppermute | solution.py:241
  51.5 1.2 %collective-permute-start.14 = (f16[16,4096]{1,0:T(8,128)(2,1)S(1)}, f16[16,4096]{1,0:T(8,128)(2,1)S(1)}, u32[]{:S(2)}, u32[]{:S(2)}) collective-permute-start(f16[16,4096]{1,0:T(8,128)(2,1)S(1)} %get-tuple-element.21), channel_id=1, source_target_pairs={{0,1},{1,0},{2,3},{3,2},{4,5},{5,4},{6,7},{7,6},{8,9},{9,8},{10,11... | collective-permute-start | bytes 393224 | tf_op jit(solution)/shard_map/ppermute | solution.py:241
  52.7 1.2 %collective-permute-done.16 = f16[16,4096]{1,0:T(8,128)(2,1)S(1)} collective-permute-done((f16[16,4096]{1,0:T(8,128)(2,1)S(1)}, f16[16,4096]{1,0:T(8,128)(2,1)S(1)}, u32[]{:S(2)}, u32[]{:S(2)}) %collective-permute-start.16) | collective-permute-done | bytes 131104 | tf_op jit(solution)/shard_map/ppermute | solution.py:241
  54.0 2.0 %collective-permute-start.18 = (f16[16,4096]{1,0:T(8,128)(2,1)S(1)}, f16[16,4096]{1,0:T(8,128)(2,1)S(1)}, u32[]{:S(2)}, u32[]{:S(2)}) collective-permute-start(f16[16,4096]{1,0:T(8,128)(2,1)S(1)} %fusion.2), channel_id=1, source_target_pairs={{0,4},{1,5},{2,6},{3,7},{4,0},{5,1},{6,2},{7,3},{8,12},{9,13},{10,... | collective-permute-start | bytes 393224 | tf_op jit(solution)/shard_map/ppermute | solution.py:241
  56.8 3.4 %shard_map.104 = (f32[128,2048]{1,0:T(8,128)}, f32[128,2048]{1,0:T(8,128)}) custom-call(bf16[64,4224]{1,0:T(8,128)(2,1)S(1)} %pad_maximum_fusion.1.packed_ref.rows_one_ref.ids_one_ref, bf16[64,4224]{1,0:T(8,128)(2,1)S(1)} %bitcast.7, bf16[64,4224]{1,0:T(8,128)(2,1)S(1)} %pad_maximum_fusion.1.packed_ref.rows_one_ref.ids_one_ref, ...), custom_call_target="tpu_custom_call" | custom-call | flops 67108864 | bytes 6291456 | tf_op jit(solution)/shard_map/pallas_call | solution.py:217
  60.2 1.1 %collective-permute-done.18 = f16[16,4096]{1,0:T(8,128)(2,1)S(1)} collective-permute-done((f16[16,4096]{1,0:T(8,128)(2,1)S(1)}, f16[16,4096]{1,0:T(8,128)(2,1)S(1)}, u32[]{:S(2)}, u32[]{:S(2)}) %collective-permute-start.18) | collective-permute-done | bytes 131104 | tf_op jit(solution)/shard_map/ppermute | solution.py:241
  (41 shorter events, 7.2 us)
Async XLA Ops:
  0.6 17.4 %collective-permute-start.1 = (bf16[4096,2048]{1,0:T(8,128)(2,1)}, bf16[4096,2048]{1,0:T(8,128)(2,1)S(1)}, u32[]{:S(2)}, u32[]{:S(2)}) collective-permute-start(bf16[4096,2048]{1,0:T(8,128)(2,1)} %param.8), channel_id=1, source_target_pairs={{0,0},{1,1},{2,2},{3,3},{4,4},{5,5},{6,6},{7,7},{8,8},{9,9},{10,10... | collective-permute-start | bytes 50331656 | tf_op jit(solution)/shard_map/ppermute | solution.py:241
  7.3 10.7 %collective-permute-start = (bf16[16,4224]{1,0:T(8,128)(2,1)S(1)}, bf16[16,4224]{1,0:T(8,128)(2,1)S(1)}, u32[]{:S(2)}, u32[]{:S(2)}) collective-permute-start(bf16[16,4224]{1,0:T(8,128)(2,1)S(1)} %shard_map.93), channel_id=1, source_target_pairs={{0,4},{1,5},{2,6},{3,7},{4,0},{5,1},{6,2},{7,3},{8,12},{9,13},{10,... | collective-permute-start | bytes 405512 | tf_op jit(solution)/shard_map/ppermute | solution.py:241
  11.4 8.9 %collective-permute-start.5 = (bf16[16,4224]{1,0:T(8,128)(2,1)S(1)}, bf16[16,4224]{1,0:T(8,128)(2,1)S(1)}, u32[]{:S(2)}, u32[]{:S(2)}) collective-permute-start(bf16[16,4224]{1,0:T(8,128)(2,1)S(1)} %shard_map.93), channel_id=1, source_target_pairs={{0,1},{1,0},{2,3},{3,2},{4,5},{5,4},{6,7},{7,6},{8,9},{9,8},{10,11... | collective-permute-start | bytes 405512 | tf_op jit(solution)/shard_map/ppermute | solution.py:241
  13.0 8.6 %collective-permute-start.6 = (bf16[16,4224]{1,0:T(8,128)(2,1)S(1)}, bf16[16,4224]{1,0:T(8,128)(2,1)S(1)}, u32[]{:S(2)}, u32[]{:S(2)}) collective-permute-start(bf16[16,4224]{1,0:T(8,128)(2,1)S(1)} %shard_map.93), channel_id=1, source_target_pairs={{0,2},{1,3},{2,0},{3,1},{4,6},{5,7},{6,4},{7,5},{8,10},{9,11},{10,... | collective-permute-start | bytes 405512 | tf_op jit(solution)/shard_map/ppermute | solution.py:241
  14.5 9.0 %collective-permute-start.7 = (bf16[16,4224]{1,0:T(8,128)(2,1)S(1)}, bf16[16,4224]{1,0:T(8,128)(2,1)S(1)}, u32[]{:S(2)}, u32[]{:S(2)}) collective-permute-start(bf16[16,4224]{1,0:T(8,128)(2,1)S(1)} %shard_map.93), channel_id=1, source_target_pairs={{0,3},{1,2},{2,1},{3,0},{4,7},{5,6},{6,5},{7,4},{8,11},{9,10},{10,... | collective-permute-start | bytes 405512 | tf_op jit(solution)/shard_map/ppermute | solution.py:241
  18.0 9.3 %collective-permute-start.2 = (bf16[16,4224]{1,0:T(8,128)(2,1)S(1)}, bf16[16,4224]{1,0:T(8,128)(2,1)S(1)}, u32[]{:S(2)}, u32[]{:S(2)}) collective-permute-start(bf16[16,4224]{1,0:T(8,128)(2,1)S(1)} %shard_map.94), channel_id=1, source_target_pairs={{0,1},{1,0},{2,3},{3,2},{4,5},{5,4},{6,7},{7,6},{8,9},{9,8},{10,11... | collective-permute-start | bytes 405512 | tf_op jit(solution)/shard_map/ppermute | solution.py:241
  19.7 7.7 %collective-permute-start.3 = (bf16[16,4224]{1,0:T(8,128)(2,1)S(1)}, bf16[16,4224]{1,0:T(8,128)(2,1)S(1)}, u32[]{:S(2)}, u32[]{:S(2)}) collective-permute-start(bf16[16,4224]{1,0:T(8,128)(2,1)S(1)} %shard_map.94), channel_id=1, source_target_pairs={{0,2},{1,3},{2,0},{3,1},{4,6},{5,7},{6,4},{7,5},{8,10},{9,11},{10,... | collective-permute-start | bytes 405512 | tf_op jit(solution)/shard_map/ppermute | solution.py:241
  20.3 7.9 %collective-permute-start.4 = (bf16[16,4224]{1,0:T(8,128)(2,1)S(1)}, bf16[16,4224]{1,0:T(8,128)(2,1)S(1)}, u32[]{:S(2)}, u32[]{:S(2)}) collective-permute-start(bf16[16,4224]{1,0:T(8,128)(2,1)S(1)} %shard_map.94), channel_id=1, source_target_pairs={{0,3},{1,2},{2,1},{3,0},{4,7},{5,6},{6,5},{7,4},{8,11},{9,10},{10,... | collective-permute-start | bytes 405512 | tf_op jit(solution)/shard_map/ppermute | solution.py:241
  32.0 4.5 %collective-permute-start.8 = (f32[8,128]{1,0:T(8,128)S(1)}, f32[8,128]{1,0:T(8,128)S(1)}, u32[]{:S(2)}, u32[]{:S(2)}) collective-permute-start(f32[8,128]{1,0:T(8,128)S(1)} %get-tuple-element.13.mine_ref), channel_id=1, source_target_pairs={{0,4},{1,5},{2,6},{3,7},{4,0},{5,1},{6,2},{7,3},{8,12},{9,13},{10,... | collective-permute-start | bytes 12296 | tf_op jit(solution)/shard_map/ppermute | solution.py:241
  36.7 6.2 %collective-permute-start.10 = (f32[8,128]{1,0:T(8,128)S(1)}, f32[8,128]{1,0:T(8,128)S(1)}, u32[]{:S(2)}, u32[]{:S(2)}) collective-permute-start(f32[8,128]{1,0:T(8,128)S(1)} %shard_map.97.mine_ref.refs_0_), channel_id=1, source_target_pairs={{0,2},{1,3},{2,0},{3,1},{4,6},{5,7},{6,4},{7,5},{8,10},{9,11},{10,... | collective-permute-start | bytes 12296 | tf_op jit(solution)/shard_map/ppermute | solution.py:241
  38.4 4.5 %collective-permute-start.11 = (f32[8,128]{1,0:T(8,128)S(1)}, f32[8,128]{1,0:T(8,128)S(1)}, u32[]{:S(2)}, u32[]{:S(2)}) collective-permute-start(f32[8,128]{1,0:T(8,128)S(1)} %shard_map.97.mine_ref.refs_0_), channel_id=1, source_target_pairs={{0,3},{1,2},{2,1},{3,0},{4,7},{5,6},{6,5},{7,4},{8,11},{9,10},{10,... | collective-permute-start | bytes 12296 | tf_op jit(solution)/shard_map/ppermute | solution.py:241
  39.7 3.6 %collective-permute-start.9 = (f32[8,128]{1,0:T(8,128)S(1)}, f32[8,128]{1,0:T(8,128)S(1)}, u32[]{:S(2)}, u32[]{:S(2)}) collective-permute-start(f32[8,128]{1,0:T(8,128)S(1)} %shard_map.97.mine_ref.refs_0_), channel_id=1, source_target_pairs={{0,1},{1,0},{2,3},{3,2},{4,5},{5,4},{6,7},{7,6},{8,9},{9,8},{10,11... | collective-permute-start | bytes 12296 | tf_op jit(solution)/shard_map/ppermute | solution.py:241
  44.2 7.3 %collective-permute-start.15 = (f16[16,4096]{1,0:T(8,128)(2,1)S(1)}, f16[16,4096]{1,0:T(8,128)(2,1)S(1)}, u32[]{:S(2)}, u32[]{:S(2)}) collective-permute-start(f16[16,4096]{1,0:T(8,128)(2,1)S(1)} %get-tuple-element.23), channel_id=1, source_target_pairs={{0,3},{1,2},{2,1},{3,0},{4,7},{5,6},{6,5},{7,4},{8,11},{9,10},{10,... | collective-permute-start | bytes 393224 | tf_op jit(solution)/shard_map/ppermute | solution.py:241
  46.6 7.3 %collective-permute-start.16 = (f16[16,4096]{1,0:T(8,128)(2,1)S(1)}, f16[16,4096]{1,0:T(8,128)(2,1)S(1)}, u32[]{:S(2)}, u32[]{:S(2)}) collective-permute-start(f16[16,4096]{1,0:T(8,128)(2,1)S(1)} %get-tuple-element.25), channel_id=1, source_target_pairs={{0,2},{1,3},{2,0},{3,1},{4,6},{5,7},{6,4},{7,5},{8,10},{9,11},{10,... | collective-permute-start | bytes 393224 | tf_op jit(solution)/shard_map/ppermute | solution.py:241
  46.9 7.0 %collective-permute-start.17 = (f16[16,4096]{1,0:T(8,128)(2,1)S(1)}, f16[16,4096]{1,0:T(8,128)(2,1)S(1)}, u32[]{:S(2)}, u32[]{:S(2)}) collective-permute-start(f16[16,4096]{1,0:T(8,128)(2,1)S(1)} %get-tuple-element.24), channel_id=1, source_target_pairs={{0,1},{1,0},{2,3},{3,2},{4,5},{5,4},{6,7},{7,6},{8,9},{9,8},{10,11... | collective-permute-start | bytes 393224 | tf_op jit(solution)/shard_map/ppermute | solution.py:241
  47.8 9.1 %copy-start.1 = (f32[128,2048]{1,0:T(8,128)S(1)}, f32[128,2048]{1,0:T(8,128)}, u32[]{:S(2)}) copy-start(f32[128,2048]{1,0:T(8,128)} %momentum_ref.1) | copy-start | bytes 3145732
  47.8 9.1 %copy-start.2 = (f32[128,2048]{1,0:T(8,128)S(1)}, f32[128,2048]{1,0:T(8,128)}, u32[]{:S(2)}) copy-start(f32[128,2048]{1,0:T(8,128)} %peer_ref.1) | copy-start | bytes 3145732
  47.8 9.0 %copy-start = (f32[128,2048]{1,0:T(8,128)S(1)}, f32[128,2048]{1,0:T(8,128)}, u32[]{:S(2)}) copy-start(f32[128,2048]{1,0:T(8,128)} %global_ref.1) | copy-start | bytes 3145732
  47.9 12.3 %collective-permute-start.12 = (f16[16,4096]{1,0:T(8,128)(2,1)S(1)}, f16[16,4096]{1,0:T(8,128)(2,1)S(1)}, u32[]{:S(2)}, u32[]{:S(2)}) collective-permute-start(f16[16,4096]{1,0:T(8,128)(2,1)S(1)} %get-tuple-element.20), channel_id=1, source_target_pairs={{0,3},{1,2},{2,1},{3,0},{4,7},{5,6},{6,5},{7,4},{8,11},{9,10},{10,... | collective-permute-start | bytes 393224 | tf_op jit(solution)/shard_map/ppermute | solution.py:241
  50.3 9.9 %collective-permute-start.13 = (f16[16,4096]{1,0:T(8,128)(2,1)S(1)}, f16[16,4096]{1,0:T(8,128)(2,1)S(1)}, u32[]{:S(2)}, u32[]{:S(2)}) collective-permute-start(f16[16,4096]{1,0:T(8,128)(2,1)S(1)} %get-tuple-element.22), channel_id=1, source_target_pairs={{0,2},{1,3},{2,0},{3,1},{4,6},{5,7},{6,4},{7,5},{8,10},{9,11},{10,... | collective-permute-start | bytes 393224 | tf_op jit(solution)/shard_map/ppermute | solution.py:241
  51.5 8.7 %collective-permute-start.14 = (f16[16,4096]{1,0:T(8,128)(2,1)S(1)}, f16[16,4096]{1,0:T(8,128)(2,1)S(1)}, u32[]{:S(2)}, u32[]{:S(2)}) collective-permute-start(f16[16,4096]{1,0:T(8,128)(2,1)S(1)} %get-tuple-element.21), channel_id=1, source_target_pairs={{0,1},{1,0},{2,3},{3,2},{4,5},{5,4},{6,7},{7,6},{8,9},{9,8},{10,11... | collective-permute-start | bytes 393224 | tf_op jit(solution)/shard_map/ppermute | solution.py:241
  54.0 7.3 %collective-permute-start.18 = (f16[16,4096]{1,0:T(8,128)(2,1)S(1)}, f16[16,4096]{1,0:T(8,128)(2,1)S(1)}, u32[]{:S(2)}, u32[]{:S(2)}) collective-permute-start(f16[16,4096]{1,0:T(8,128)(2,1)S(1)} %fusion.2), channel_id=1, source_target_pairs={{0,4},{1,5},{2,6},{3,7},{4,0},{5,1},{6,2},{7,3},{8,12},{9,13},{10,... | collective-permute-start | bytes 393224 | tf_op jit(solution)/shard_map/ppermute | solution.py:241

commit v13 on v11

--- a/solution.py
+++ b/solution.py
@@ -177,7 +177,7 @@
 
 def grad_kernel(first, one_ref, two_ref, near_ref, *refs):
     terms_ref = refs[-1]
-    tile = 1024
+    tile = min(terms_ref.shape[1], 2**20 // (one_ref.shape[0] + two_ref.shape[0]) // 2)
     both = jnp.concatenate([one_ref[...], two_ref[...]], axis=0)
     for place in range(0, terms_ref.shape[1], tile):
         turned = lax.dot_general(
@@ -197,6 +197,8 @@
 
     count = out_ref.shape[0]
     chunk = min(count, 64)
+    end = sum(terms_ref.shape[1] for terms_ref in terms_refs)
+    out_ref[:, end:] = jnp.zeros((count, out_ref.shape[1] - end), jnp.float32)
     for place, terms_ref in enumerate(terms_refs):
         columns = pl.ds(place * terms_ref.shape[1], terms_ref.shape[1])
         for i in range(0, count, chunk):
@@ -287,7 +289,7 @@
     return near, far.reshape(4, count, own, -1).swapaxes(0, 1).reshape(4 * count * own, -1)
 
 
-def scatter_sums(grads_near, grads_far, own):
+def scatter_sums(grads_near, grads_far, own, depth):
     blocks = [
         grads[i * own : (i + 1) * own]
         for grads in (grads_near, grads_far)
@@ -295,15 +297,15 @@
     ]
     members = len(blocks)
 
-    def moved(parts, step):
-        value = jnp.concatenate([part.astype(SEND) for part in parts], axis=0)
-        value = swap(value, step).astype(jnp.float32)
+    def moved(parts, step, longer=0):
+        value = jnp.concatenate([part[:, : depth + longer * LANES].astype(SEND) for part in parts], axis=0)
+        value = swap(value, step)[:, :depth].astype(jnp.float32)
         return [value[i * own : (i + 1) * own] for i in range(len(parts))]
 
-    sums = blocks[::4]
-    for part in (list(range(1, members // 4)), [0]):
-        for step in (3, 2, 1):
-            for i, value in zip(part, moved([blocks[4 * i + step] for i in part], step)):
+    sums = [block[:, :depth] for block in blocks[::4]]
+    for part, longer in ((list(range(1, members // 4)), (2, 1, 0)), ([0], (0, 1, 2))):
+        for step, more in zip((3, 2, 1), longer):
+            for i, value in zip(part, moved([blocks[4 * i + step] for i in part], step, more)):
                 sums[i] = sums[i] + value
     for step in far_steps()[::-1]:
         keep = len(sums) // 2
@@ -366,11 +368,11 @@
     grads_far, grads_near = (
         call(
             functools.partial(join_kernel, scale, first),
-            [((count, depth), jnp.float32)], [lines, mine] + terms,
+            [((count, depth + 2 * LANES), jnp.float32)], [lines, mine] + terms,
         )[0]
         for first, count in ((4 * own, rows - 4 * own), (0, 4 * own))
     )
-    hidden_grad = (scatter_sums(grads_near, grads_far, own) * (1.0 / scale)).astype(jnp.bfloat16)
+    hidden_grad = (scatter_sums(grads_near, grads_far, own, depth) * (1.0 / scale)).astype(jnp.bfloat16)
     loss = call(functools.partial(loss_kernel, members), [((8, LANES), jnp.float32)], [lines])[0]
     new_global, new_momentum = frag_update(
         [rows_near, rows_far], [rows_near, rows_far], lines, [logits_near, logits_far], near,

time: 58.2 us -> 57.8 us (level)
  transfers between devices with their start and end apart: 18 -> 18, of which waited for: 6 -> 4; matrix products, arithmetic and copies ran while one was open for 1% -> 1% of each run, Pallas kernels for 31% -> 32%
where the time goes in v13:
time: 57.8 us; the launch traced here: 57.6 us
  starting transfers between devices  24.2 us (42%)
  Pallas kernels  23.4 us (40%)
  waiting for transfers between devices  7.36 us (13%)
  other arithmetic  1.09 us (2%)
  between operations  0.86 us (1%)
  local copies, waits for them, and re-layouts  0.7 us (1%)
    ppermute x18, starting transfers between devices, swap(): lax.ppermute(value, AXIS, [(i, i ^ step) for i in range(lax.axis_size(AXI...  24.2 us
    pallas_call x11, Pallas kernels, call(): pl.pallas_call(kernel, out_shape=outs, in_specs=[pl.BlockSpec(memory_spac...  20 us
    ppermute x18, waiting for transfers between devices, swap(): lax.ppermute(value, AXIS, [(i, i ^ step) for i in range(lax.axis_size(AXI...  7.36 us
    pallas_call x1, Pallas kernels, frag_update(): pl.pallas_call(frag_kernel, grid=(width // TILE,), out_shape=[jax.ShapeDt...  3.38 us
  transfers between devices with their start and end apart: 18, of which 4 were waited for; matrix products, arithmetic and copies ran while one was open for 1% of the time, Pallas kernels for 32%

profile of v13, /device:TPU:0, one launch (start us, length us, event | category | flops | bytes accessed | tf_op | source)
XLA Modules:
  0.0 57.6 jit_solution(18149664307775921525)
XLA Ops:
  0.6 0.9 %shard_map.93 = bf16[16,4224]{1,0:T(8,128)(2,1)S(1)} custom-call(s32[16]{0:T(128)} %targets.1, bf16[16,4096]{1,0:T(8,128)(2,1)} %rows.1), custom_call_target="tpu_custom_call" | custom-call | bytes 131136 | tf_op jit(solution)/shard_map/pallas_call | solution.py:22
  1.6 4.1 %collective-permute-start = (bf16[16,4224]{1,0:T(8,128)(2,1)S(1)}, bf16[16,4224]{1,0:T(8,128)(2,1)S(1)}, u32[]{:S(2)}, u32[]{:S(2)}) collective-permute-start(bf16[16,4224]{1,0:T(8,128)(2,1)S(1)} %shard_map.93), channel_id=1, source_target_pairs={{0,4},{1,5},{2,6},{3,7},{4,0},{5,1},{6,2},{7,3},{8,12},{9,13},{10,... | collective-permute-start | bytes 405512 | tf_op jit(solution)/shard_map/ppermute | solution.py:268
  5.7 2.5 %collective-permute-start.6 = (bf16[16,4224]{1,0:T(8,128)(2,1)S(1)}, bf16[16,4224]{1,0:T(8,128)(2,1)S(1)}, u32[]{:S(2)}, u32[]{:S(2)}) collective-permute-start(bf16[16,4224]{1,0:T(8,128)(2,1)S(1)} %shard_map.93), channel_id=1, source_target_pairs={{0,3},{1,2},{2,1},{3,0},{4,7},{5,6},{6,5},{7,4},{8,11},{9,10},{10,... | collective-permute-start | bytes 405512 | tf_op jit(solution)/shard_map/ppermute | solution.py:268
  9.2 3.5 %shard_map.94.held_ref = bf16[4096,2048]{1,0:T(8,128)(2,1)S(1)} custom-call(bf16[4096,2048]{1,0:T(8,128)(2,1)} %head.3), custom_call_target="tpu_custom_call" | custom-call | bytes 16777216 | tf_op jit(solution)/shard_map/pallas_call | solution.py:22
  12.7 2.6 %collective-permute-start.3 = (bf16[16,4224]{1,0:T(8,128)(2,1)S(1)}, bf16[16,4224]{1,0:T(8,128)(2,1)S(1)}, u32[]{:S(2)}, u32[]{:S(2)}) collective-permute-start(bf16[16,4224]{1,0:T(8,128)(2,1)S(1)} %collective-permute-done), channel_id=1, source_target_pairs={{0,3},{1,2},{2,1},{3,0},{4,7},{5,6},{6,5},{7,4},{8,11},{9,10},{10,... | collective-permute-start | bytes 405512 | tf_op jit(solution)/shard_map/ppermute | solution.py:268
  16.2 1.1 %collective-permute-done.5 = bf16[16,4224]{1,0:T(8,128)(2,1)S(1)} collective-permute-done((bf16[16,4224]{1,0:T(8,128)(2,1)S(1)}, bf16[16,4224]{1,0:T(8,128)(2,1)S(1)}, u32[]{:S(2)}, u32[]{:S(2)}) %collective-permute-start.5) | collective-permute-done | bytes 135200 | tf_op jit(solution)/shard_map/ppermute | solution.py:268
  17.4 5.7 %shard_map.95 = (bf16[4096,2048]{1,0:T(8,128)(2,1)S(1)}, f32[64,2048]{1,0:T(8,128)S(1)}, bf16[128,2048]{1,0:T(8,128)(2,1)S(1)}, f32[64,128]{1,0:T(8,128)S(1)}) custom-call(bf16[64,4224]{1,0:T(8,128)(2,1)S(1)} %pad_maximum_fusion.1.packed_ref.rows_one_ref.ids_one_ref, bf16[4096,2048]{1,0:T(8,128)(2,1)} %head.3, ...), custom_call_target="tpu_custom_call", output_to_operand_aliasing={{0}: (2, {})} | custom-call | flops 1073741824 | bytes 34095104 | tf_op jit(solution)/shard_map/pallas_call | solution.py:22
  23.2 3.7 %shard_map.96 = (f32[64,2048]{1,0:T(8,128)S(1)}, bf16[128,2048]{1,0:T(8,128)(2,1)S(1)}, f32[8,128]{1,0:T(8,128)S(1)}) custom-call(bf16[64,4224]{1,0:T(8,128)(2,1)S(1)} %bitcast.6, bf16[4096,2048]{1,0:T(8,128)(2,1)S(1)} %get-tuple-element.13.near_ref.head_ref, f32[64,128]{1,0:T(8,128)S(1)} %get-tuple-element.14.before_ref), custom_call_target="tpu_custom_call" | custom-call | flops 1073741824 | bytes 17350656 | tf_op jit(solution)/shard_map/pallas_call | solution.py:22
  26.9 0.8 %collective-permute-start.7 = (f32[8,128]{1,0:T(8,128)S(1)}, f32[8,128]{1,0:T(8,128)S(1)}, u32[]{:S(2)}, u32[]{:S(2)}) collective-permute-start(f32[8,128]{1,0:T(8,128)S(1)} %get-tuple-element.15.mine_ref), channel_id=1, source_target_pairs={{0,4},{1,5},{2,6},{3,7},{4,0},{5,1},{6,2},{7,3},{8,12},{9,13},{10,... | collective-permute-start | bytes 12296 | tf_op jit(solution)/shard_map/ppermute | solution.py:268
  27.8 2.5 %shard_map.100.refs_0_ = f32[256,2048]{1,0:T(8,128)S(1)} custom-call(bf16[128,2048]{1,0:T(8,128)(2,1)S(1)} %get-tuple-element.16.one_ref, bf16[128,2048]{1,0:T(8,128)(2,1)S(1)} %get-tuple-element.17.two_ref, bf16[4096,2048]{1,0:T(8,128)(2,1)S(1)} %get-tuple-element.13.near_ref.head_ref), custom_call_target="tpu_custom_call" | custom-call | flops 2147483648 | bytes 17825792 | tf_op jit(solution)/shard_map/pallas_call | solution.py:22
  30.3 1.2 %collective-permute-done.7.refs_0_ = f32[8,128]{1,0:T(8,128)S(1)} collective-permute-done((f32[8,128]{1,0:T(8,128)S(1)}, f32[8,128]{1,0:T(8,128)S(1)}, u32[]{:S(2)}, u32[]{:S(2)}) %collective-permute-start.7) | collective-permute-done | bytes 4128 | tf_op jit(solution)/shard_map/ppermute | solution.py:268
  31.6 1.6 %collective-permute-start.10 = (f32[8,128]{1,0:T(8,128)S(1)}, f32[8,128]{1,0:T(8,128)S(1)}, u32[]{:S(2)}, u32[]{:S(2)}) collective-permute-start(f32[8,128]{1,0:T(8,128)S(1)} %shard_map.97.mine_ref.refs_0_), channel_id=1, source_target_pairs={{0,3},{1,2},{2,1},{3,0},{4,7},{5,6},{6,5},{7,4},{8,11},{9,10},{10,... | collective-permute-start | bytes 12296 | tf_op jit(solution)/shard_map/ppermute | solution.py:268
  33.8 1.3 %collective-permute-start.8 = (f32[8,128]{1,0:T(8,128)S(1)}, f32[8,128]{1,0:T(8,128)S(1)}, u32[]{:S(2)}, u32[]{:S(2)}) collective-permute-start(f32[8,128]{1,0:T(8,128)S(1)} %shard_map.97.mine_ref.refs_0_), channel_id=1, source_target_pairs={{0,1},{1,0},{2,3},{3,2},{4,5},{5,4},{6,7},{7,6},{8,9},{9,8},{10,11... | collective-permute-start | bytes 12296 | tf_op jit(solution)/shard_map/ppermute | solution.py:268
  35.1 2.5 %shard_map.101.refs_1_ = f32[256,2048]{1,0:T(8,128)S(1)} custom-call(bf16[128,2048]{1,0:T(8,128)(2,1)S(1)} %get-tuple-element.16.one_ref, bf16[128,2048]{1,0:T(8,128)(2,1)S(1)} %get-tuple-element.17.two_ref, bf16[4096,2048]{1,0:T(8,128)(2,1)S(1)} %get-tuple-element.13.near_ref.head_ref, f32[8,128]{1,0:T(8,128)S(1)} %shard_map.97.mine_ref.refs_0_), custom_call_target="tpu_custom_call" | custom-call | flops 2147483648 | bytes 17829888 | tf_op jit(solution)/shard_map/pallas_call | solution.py:22
  38.3 1.6 %collective-permute-start.14 = (f16[16,4352]{1,0:T(8,128)(2,1)S(1)}, f16[16,4352]{1,0:T(8,128)(2,1)S(1)}, u32[]{:S(2)}, u32[]{:S(2)}) collective-permute-start(f16[16,4352]{1,0:T(8,128)(2,1)S(1)} %slice.77), channel_id=1, source_target_pairs={{0,3},{1,2},{2,1},{3,0},{4,7},{5,6},{6,5},{7,4},{8,11},{9,10},{10,... | collective-permute-start | bytes 417800 | tf_op jit(solution)/shard_map/ppermute | solution.py:268
  39.9 1.0 %collective-permute-start.15 = (f16[16,4224]{1,0:T(8,128)(2,1)S(1)}, f16[16,4224]{1,0:T(8,128)(2,1)S(1)}, u32[]{:S(2)}, u32[]{:S(2)}) collective-permute-start(f16[16,4224]{1,0:T(8,128)(2,1)S(1)} %slice.79), channel_id=1, source_target_pairs={{0,2},{1,3},{2,0},{3,1},{4,6},{5,7},{6,4},{7,5},{8,10},{9,11},{10,... | collective-permute-start | bytes 405512 | tf_op jit(solution)/shard_map/ppermute | solution.py:268
  40.9 1.1 %collective-permute-start.16 = (f16[16,4096]{1,0:T(8,128)(2,1)S(1)}, f16[16,4096]{1,0:T(8,128)(2,1)S(1)}, u32[]{:S(2)}, u32[]{:S(2)}) collective-permute-start(f16[16,4096]{1,0:T(8,128)(2,1)S(1)} %slice.81), channel_id=1, source_target_pairs={{0,1},{1,0},{2,3},{3,2},{4,5},{5,4},{6,7},{7,6},{8,9},{9,8},{10,11... | collective-permute-start | bytes 393224 | tf_op jit(solution)/shard_map/ppermute | solution.py:268
  42.5 1.6 %collective-permute-start.11 = (f16[16,4096]{1,0:T(8,128)(2,1)S(1)}, f16[16,4096]{1,0:T(8,128)(2,1)S(1)}, u32[]{:S(2)}, u32[]{:S(2)}) collective-permute-start(f16[16,4096]{1,0:T(8,128)(2,1)S(1)} %slice.71), channel_id=1, source_target_pairs={{0,3},{1,2},{2,1},{3,0},{4,7},{5,6},{6,5},{7,4},{8,11},{9,10},{10,... | collective-permute-start | bytes 393224 | tf_op jit(solution)/shard_map/ppermute | solution.py:268
  44.1 1.0 %collective-permute-start.12 = (f16[16,4224]{1,0:T(8,128)(2,1)S(1)}, f16[16,4224]{1,0:T(8,128)(2,1)S(1)}, u32[]{:S(2)}, u32[]{:S(2)}) collective-permute-start(f16[16,4224]{1,0:T(8,128)(2,1)S(1)} %slice.72), channel_id=1, source_target_pairs={{0,2},{1,3},{2,0},{3,1},{4,6},{5,7},{6,4},{7,5},{8,10},{9,11},{10,... | collective-permute-start | bytes 405512 | tf_op jit(solution)/shard_map/ppermute | solution.py:268
  45.1 3.4 %collective-permute-done.16 = f16[16,4096]{1,0:T(8,128)(2,1)S(1)} collective-permute-done((f16[16,4096]{1,0:T(8,128)(2,1)S(1)}, f16[16,4096]{1,0:T(8,128)(2,1)S(1)}, u32[]{:S(2)}, u32[]{:S(2)}) %collective-permute-start.16) | collective-permute-done | bytes 131104 | tf_op jit(solution)/shard_map/ppermute | solution.py:268
  48.4 1.2 %collective-permute-start.13 = (f16[16,4352]{1,0:T(8,128)(2,1)S(1)}, f16[16,4352]{1,0:T(8,128)(2,1)S(1)}, u32[]{:S(2)}, u32[]{:S(2)}) collective-permute-start(f16[16,4352]{1,0:T(8,128)(2,1)S(1)} %slice.74), channel_id=1, source_target_pairs={{0,1},{1,0},{2,3},{3,2},{4,5},{5,4},{6,7},{7,6},{8,9},{9,8},{10,11... | collective-permute-start | bytes 417800 | tf_op jit(solution)/shard_map/ppermute | solution.py:268
  49.7 1.3 %collective-permute-start.17 = (f16[16,4096]{1,0:T(8,128)(2,1)S(1)}, f16[16,4096]{1,0:T(8,128)(2,1)S(1)}, u32[]{:S(2)}, u32[]{:S(2)}) collective-permute-start(f16[16,4096]{1,0:T(8,128)(2,1)S(1)} %fusion.2), channel_id=1, source_target_pairs={{0,4},{1,5},{2,6},{3,7},{4,0},{5,1},{6,2},{7,3},{8,12},{9,13},{10,... | collective-permute-start | bytes 393224 | tf_op jit(solution)/shard_map/ppermute | solution.py:268
  51.8 3.4 %shard_map.104 = (f32[128,2048]{1,0:T(8,128)}, f32[128,2048]{1,0:T(8,128)}) custom-call(bf16[64,4224]{1,0:T(8,128)(2,1)S(1)} %pad_maximum_fusion.1.packed_ref.rows_one_ref.ids_one_ref, bf16[64,4224]{1,0:T(8,128)(2,1)S(1)} %bitcast.7, bf16[64,4224]{1,0:T(8,128)(2,1)S(1)} %pad_maximum_fusion.1.packed_ref.rows_one_ref.ids_one_ref, ...), custom_call_target="tpu_custom_call" | custom-call | flops 67108864 | bytes 6291456 | tf_op jit(solution)/shard_map/pallas_call | solution.py:244
  55.2 1.7 %collective-permute-done.17 = f16[16,4096]{1,0:T(8,128)(2,1)S(1)} collective-permute-done((f16[16,4096]{1,0:T(8,128)(2,1)S(1)}, f16[16,4096]{1,0:T(8,128)(2,1)S(1)}, u32[]{:S(2)}, u32[]{:S(2)}) %collective-permute-start.17) | collective-permute-done | bytes 131104 | tf_op jit(solution)/shard_map/ppermute | solution.py:268
  (43 shorter events, 5.6 us)
Async XLA Ops:
  1.6 11.1 %collective-permute-start = (bf16[16,4224]{1,0:T(8,128)(2,1)S(1)}, bf16[16,4224]{1,0:T(8,128)(2,1)S(1)}, u32[]{:S(2)}, u32[]{:S(2)}) collective-permute-start(bf16[16,4224]{1,0:T(8,128)(2,1)S(1)} %shard_map.93), channel_id=1, source_target_pairs={{0,4},{1,5},{2,6},{3,7},{4,0},{5,1},{6,2},{7,3},{8,12},{9,13},{10,... | collective-permute-start | bytes 405512 | tf_op jit(solution)/shard_map/ppermute | solution.py:268
  5.7 10.1 %collective-permute-start.6 = (bf16[16,4224]{1,0:T(8,128)(2,1)S(1)}, bf16[16,4224]{1,0:T(8,128)(2,1)S(1)}, u32[]{:S(2)}, u32[]{:S(2)}) collective-permute-start(bf16[16,4224]{1,0:T(8,128)(2,1)S(1)} %shard_map.93), channel_id=1, source_target_pairs={{0,3},{1,2},{2,1},{3,0},{4,7},{5,6},{6,5},{7,4},{8,11},{9,10},{10,... | collective-permute-start | bytes 405512 | tf_op jit(solution)/shard_map/ppermute | solution.py:268
  8.2 9.2 %collective-permute-start.5 = (bf16[16,4224]{1,0:T(8,128)(2,1)S(1)}, bf16[16,4224]{1,0:T(8,128)(2,1)S(1)}, u32[]{:S(2)}, u32[]{:S(2)}) collective-permute-start(bf16[16,4224]{1,0:T(8,128)(2,1)S(1)} %shard_map.93), channel_id=1, source_target_pairs={{0,2},{1,3},{2,0},{3,1},{4,6},{5,7},{6,4},{7,5},{8,10},{9,11},{10,... | collective-permute-start | bytes 405512 | tf_op jit(solution)/shard_map/ppermute | solution.py:268
  8.6 8.7 %collective-permute-start.4 = (bf16[16,4224]{1,0:T(8,128)(2,1)S(1)}, bf16[16,4224]{1,0:T(8,128)(2,1)S(1)}, u32[]{:S(2)}, u32[]{:S(2)}) collective-permute-start(bf16[16,4224]{1,0:T(8,128)(2,1)S(1)} %shard_map.93), channel_id=1, source_target_pairs={{0,1},{1,0},{2,3},{3,2},{4,5},{5,4},{6,7},{7,6},{8,9},{9,8},{10,11... | collective-permute-start | bytes 405512 | tf_op jit(solution)/shard_map/ppermute | solution.py:268
  12.7 10.4 %collective-permute-start.3 = (bf16[16,4224]{1,0:T(8,128)(2,1)S(1)}, bf16[16,4224]{1,0:T(8,128)(2,1)S(1)}, u32[]{:S(2)}, u32[]{:S(2)}) collective-permute-start(bf16[16,4224]{1,0:T(8,128)(2,1)S(1)} %collective-permute-done), channel_id=1, source_target_pairs={{0,3},{1,2},{2,1},{3,0},{4,7},{5,6},{6,5},{7,4},{8,11},{9,10},{10,... | collective-permute-start | bytes 405512 | tf_op jit(solution)/shard_map/ppermute | solution.py:268
  15.3 7.8 %collective-permute-start.2 = (bf16[16,4224]{1,0:T(8,128)(2,1)S(1)}, bf16[16,4224]{1,0:T(8,128)(2,1)S(1)}, u32[]{:S(2)}, u32[]{:S(2)}) collective-permute-start(bf16[16,4224]{1,0:T(8,128)(2,1)S(1)} %collective-permute-done), channel_id=1, source_target_pairs={{0,2},{1,3},{2,0},{3,1},{4,6},{5,7},{6,4},{7,5},{8,10},{9,11},{10,... | collective-permute-start | bytes 405512 | tf_op jit(solution)/shard_map/ppermute | solution.py:268
  15.7 7.4 %collective-permute-start.1 = (bf16[16,4224]{1,0:T(8,128)(2,1)S(1)}, bf16[16,4224]{1,0:T(8,128)(2,1)S(1)}, u32[]{:S(2)}, u32[]{:S(2)}) collective-permute-start(bf16[16,4224]{1,0:T(8,128)(2,1)S(1)} %collective-permute-done), channel_id=1, source_target_pairs={{0,1},{1,0},{2,3},{3,2},{4,5},{5,4},{6,7},{7,6},{8,9},{9,8},{10,11... | collective-permute-start | bytes 405512 | tf_op jit(solution)/shard_map/ppermute | solution.py:268
  26.9 4.5 %collective-permute-start.7 = (f32[8,128]{1,0:T(8,128)S(1)}, f32[8,128]{1,0:T(8,128)S(1)}, u32[]{:S(2)}, u32[]{:S(2)}) collective-permute-start(f32[8,128]{1,0:T(8,128)S(1)} %get-tuple-element.15.mine_ref), channel_id=1, source_target_pairs={{0,4},{1,5},{2,6},{3,7},{4,0},{5,1},{6,2},{7,3},{8,12},{9,13},{10,... | collective-permute-start | bytes 12296 | tf_op jit(solution)/shard_map/ppermute | solution.py:268
  31.6 6.1 %collective-permute-start.10 = (f32[8,128]{1,0:T(8,128)S(1)}, f32[8,128]{1,0:T(8,128)S(1)}, u32[]{:S(2)}, u32[]{:S(2)}) collective-permute-start(f32[8,128]{1,0:T(8,128)S(1)} %shard_map.97.mine_ref.refs_0_), channel_id=1, source_target_pairs={{0,3},{1,2},{2,1},{3,0},{4,7},{5,6},{6,5},{7,4},{8,11},{9,10},{10,... | collective-permute-start | bytes 12296 | tf_op jit(solution)/shard_map/ppermute | solution.py:268
  33.2 4.5 %collective-permute-start.9 = (f32[8,128]{1,0:T(8,128)S(1)}, f32[8,128]{1,0:T(8,128)S(1)}, u32[]{:S(2)}, u32[]{:S(2)}) collective-permute-start(f32[8,128]{1,0:T(8,128)S(1)} %shard_map.97.mine_ref.refs_0_), channel_id=1, source_target_pairs={{0,2},{1,3},{2,0},{3,1},{4,6},{5,7},{6,4},{7,5},{8,10},{9,11},{10,... | collective-permute-start | bytes 12296 | tf_op jit(solution)/shard_map/ppermute | solution.py:268
  33.8 3.8 %collective-permute-start.8 = (f32[8,128]{1,0:T(8,128)S(1)}, f32[8,128]{1,0:T(8,128)S(1)}, u32[]{:S(2)}, u32[]{:S(2)}) collective-permute-start(f32[8,128]{1,0:T(8,128)S(1)} %shard_map.97.mine_ref.refs_0_), channel_id=1, source_target_pairs={{0,1},{1,0},{2,3},{3,2},{4,5},{5,4},{6,7},{7,6},{8,9},{9,8},{10,11... | collective-permute-start | bytes 12296 | tf_op jit(solution)/shard_map/ppermute | solution.py:268
  38.3 11.4 %collective-permute-start.14 = (f16[16,4352]{1,0:T(8,128)(2,1)S(1)}, f16[16,4352]{1,0:T(8,128)(2,1)S(1)}, u32[]{:S(2)}, u32[]{:S(2)}) collective-permute-start(f16[16,4352]{1,0:T(8,128)(2,1)S(1)} %slice.77), channel_id=1, source_target_pairs={{0,3},{1,2},{2,1},{3,0},{4,7},{5,6},{6,5},{7,4},{8,11},{9,10},{10,... | collective-permute-start | bytes 417800 | tf_op jit(solution)/shard_map/ppermute | solution.py:268
  39.9 9.7 %collective-permute-start.15 = (f16[16,4224]{1,0:T(8,128)(2,1)S(1)}, f16[16,4224]{1,0:T(8,128)(2,1)S(1)}, u32[]{:S(2)}, u32[]{:S(2)}) collective-permute-start(f16[16,4224]{1,0:T(8,128)(2,1)S(1)} %slice.79), channel_id=1, source_target_pairs={{0,2},{1,3},{2,0},{3,1},{4,6},{5,7},{6,4},{7,5},{8,10},{9,11},{10,... | collective-permute-start | bytes 405512 | tf_op jit(solution)/shard_map/ppermute | solution.py:268
  40.9 7.5 %collective-permute-start.16 = (f16[16,4096]{1,0:T(8,128)(2,1)S(1)}, f16[16,4096]{1,0:T(8,128)(2,1)S(1)}, u32[]{:S(2)}, u32[]{:S(2)}) collective-permute-start(f16[16,4096]{1,0:T(8,128)(2,1)S(1)} %slice.81), channel_id=1, source_target_pairs={{0,1},{1,0},{2,3},{3,2},{4,5},{5,4},{6,7},{7,6},{8,9},{9,8},{10,11... | collective-permute-start | bytes 393224 | tf_op jit(solution)/shard_map/ppermute | solution.py:268
  42.3 9.5 %copy-start.1 = (f32[128,2048]{1,0:T(8,128)S(1)}, f32[128,2048]{1,0:T(8,128)}, u32[]{:S(2)}) copy-start(f32[128,2048]{1,0:T(8,128)} %momentum_ref.1) | copy-start | bytes 3145732
  42.3 9.5 %copy-start.2 = (f32[128,2048]{1,0:T(8,128)S(1)}, f32[128,2048]{1,0:T(8,128)}, u32[]{:S(2)}) copy-start(f32[128,2048]{1,0:T(8,128)} %peer_ref.1) | copy-start | bytes 3145732
  42.4 9.4 %copy-start = (f32[128,2048]{1,0:T(8,128)S(1)}, f32[128,2048]{1,0:T(8,128)}, u32[]{:S(2)}) copy-start(f32[128,2048]{1,0:T(8,128)} %global_ref.1) | copy-start | bytes 3145732
  42.5 12.7 %collective-permute-start.11 = (f16[16,4096]{1,0:T(8,128)(2,1)S(1)}, f16[16,4096]{1,0:T(8,128)(2,1)S(1)}, u32[]{:S(2)}, u32[]{:S(2)}) collective-permute-start(f16[16,4096]{1,0:T(8,128)(2,1)S(1)} %slice.71), channel_id=1, source_target_pairs={{0,3},{1,2},{2,1},{3,0},{4,7},{5,6},{6,5},{7,4},{8,11},{9,10},{10,... | collective-permute-start | bytes 393224 | tf_op jit(solution)/shard_map/ppermute | solution.py:268
  44.1 11.0 %collective-permute-start.12 = (f16[16,4224]{1,0:T(8,128)(2,1)S(1)}, f16[16,4224]{1,0:T(8,128)(2,1)S(1)}, u32[]{:S(2)}, u32[]{:S(2)}) collective-permute-start(f16[16,4224]{1,0:T(8,128)(2,1)S(1)} %slice.72), channel_id=1, source_target_pairs={{0,2},{1,3},{2,0},{3,1},{4,6},{5,7},{6,4},{7,5},{8,10},{9,11},{10,... | collective-permute-start | bytes 405512 | tf_op jit(solution)/shard_map/ppermute | solution.py:268
  48.4 6.7 %collective-permute-start.13 = (f16[16,4352]{1,0:T(8,128)(2,1)S(1)}, f16[16,4352]{1,0:T(8,128)(2,1)S(1)}, u32[]{:S(2)}, u32[]{:S(2)}) collective-permute-start(f16[16,4352]{1,0:T(8,128)(2,1)S(1)} %slice.74), channel_id=1, source_target_pairs={{0,1},{1,0},{2,3},{3,2},{4,5},{5,4},{6,7},{7,6},{8,9},{9,8},{10,11... | collective-permute-start | bytes 417800 | tf_op jit(solution)/shard_map/ppermute | solution.py:268
  49.7 7.1 %collective-permute-start.17 = (f16[16,4096]{1,0:T(8,128)(2,1)S(1)}, f16[16,4096]{1,0:T(8,128)(2,1)S(1)}, u32[]{:S(2)}, u32[]{:S(2)}) collective-permute-start(f16[16,4096]{1,0:T(8,128)(2,1)S(1)} %fusion.2), channel_id=1, source_target_pairs={{0,4},{1,5},{2,6},{3,7},{4,0},{5,1},{6,2},{7,3},{8,12},{9,13},{10,... | collective-permute-start | bytes 393224 | tf_op jit(solution)/shard_map/ppermute | solution.py:268

commit v14 on v11

--- a/solution.py
+++ b/solution.py
@@ -110,7 +110,7 @@
 def softmax_of(rows_ref, logits_ref, both_ref, columns_ref, first):
     rows, width = logits_ref.shape
     digits = rows_ref.shape[1] - LANES
-    chunk = 32
+    chunk = 16
     offset = lax.axis_index(AXIS) * width
 
     @pl.loop(0, rows // chunk)
@@ -177,7 +177,7 @@
 
 def grad_kernel(first, one_ref, two_ref, near_ref, *refs):
     terms_ref = refs[-1]
-    tile = 1024
+    tile = min(terms_ref.shape[1], 2**20 // (one_ref.shape[0] + two_ref.shape[0]) // 2)
     both = jnp.concatenate([one_ref[...], two_ref[...]], axis=0)
     for place in range(0, terms_ref.shape[1], tile):
         turned = lax.dot_general(
@@ -187,7 +187,7 @@
         terms_ref[:, pl.ds(place, tile)] = turned.T
 
 
-def join_kernel(scale, first, lines_ref, mine_ref, *refs):
+def join_kernel(scale, first, head_rows, lines_ref, mine_ref, *refs):
     *terms_refs, out_ref = refs
     rows = mine_ref.shape[1]
     top, total = lines_ref[0:1, :], lines_ref[1:2, :]
@@ -195,15 +195,16 @@
     hard = (jnp.exp(mine_ref[2:3, :] - top) / total - 1.0) / rows
     hard = as_columns(hard.astype(jnp.bfloat16).astype(jnp.float32)) * scale
 
-    count = out_ref.shape[0]
-    chunk = min(count, 64)
+    chunk = 16
     for place, terms_ref in enumerate(terms_refs):
         columns = pl.ds(place * terms_ref.shape[1], terms_ref.shape[1])
-        for i in range(0, count, chunk):
-            part = slice(first + i, first + i + chunk)
+        for i in range(0, out_ref.shape[0], chunk):
+            at = first + i
+            part = slice(at, at + chunk)
+            held, other = (at, head_rows) if at < head_rows else (head_rows + at, rows - head_rows)
             out_ref[pl.ds(i, chunk), columns] = (
-                soft[part] * terms_ref[pl.ds(2 * first + i, chunk), :]
-                + hard[part] * terms_ref[pl.ds(2 * first + count + i, chunk), :]
+                soft[part] * terms_ref[pl.ds(held, chunk), :]
+                + hard[part] * terms_ref[pl.ds(held + other, chunk), :]
             )
 
 
@@ -281,10 +282,15 @@
     for step in far_steps():
         held = jnp.concatenate([held, swap(held, step)], axis=0)
     far = held[own:]
-    near = jnp.concatenate([packed] + [swap(packed, step) for step in (1, 2, 3)], axis=0)
-    far = jnp.stack([far] + [swap(far, step) for step in (1, 2, 3)])
-    count = far.shape[1] // own
-    return near, far.reshape(4, count, own, -1).swapaxes(0, 1).reshape(4 * count * own, -1)
+    count = far.shape[0] // own
+    z_near, y_near = swap(packed, 2), swap(packed, 1)
+    both = swap(jnp.concatenate([far, z_near], axis=0), 1)
+    parts = [far, both[: count * own], swap(far, 2), swap(far, 3)]
+    others = jnp.stack(parts).reshape(4, count, own, -1).swapaxes(0, 1).reshape(4 * count * own, -1)
+    return (
+        jnp.concatenate([packed, y_near, z_near], axis=0),
+        jnp.concatenate([both[count * own :], others], axis=0),
+    )
 
 
 def scatter_sums(grads_near, grads_far, own):
@@ -293,18 +299,20 @@
         for grads in (grads_near, grads_far)
         for i in range(grads.shape[0] // own)
     ]
-    members = len(blocks)
+    far = range(4, len(blocks), 4)
 
     def moved(parts, step):
         value = jnp.concatenate([part.astype(SEND) for part in parts], axis=0)
         value = swap(value, step).astype(jnp.float32)
         return [value[i * own : (i + 1) * own] for i in range(len(parts))]
 
-    sums = blocks[::4]
-    for part in (list(range(1, members // 4)), [0]):
-        for step in (3, 2, 1):
-            for i, value in zip(part, moved([blocks[4 * i + step] for i in part], step)):
-                sums[i] = sums[i] + value
+    *one, z_near = moved([blocks[i ^ 1] for i in far] + [blocks[3]], 1)
+    three = moved([blocks[i ^ 3] for i in far], 3)
+    two = moved([blocks[i ^ 2] for i in far], 2)
+    sums = [blocks[0]] + [blocks[i] + a + b + c for i, a, b, c in zip(far, one, two, three)]
+    y_near = moved([blocks[1]], 1)[0]
+    z_near = moved([blocks[2] + z_near], 2)[0]
+    sums[0] = sums[0] + y_near + z_near
     for step in far_steps()[::-1]:
         keep = len(sums) // 2
         sums = [a + b for a, b in zip(sums[:keep], moved(sums[keep:], step))]
@@ -328,7 +336,7 @@
         scratch=[pltpu.SemaphoreType.DMA((4,))], sources=[pltpu.HBM],
     )[0]
 
-    count = 4 * own
+    count = 3 * own
     near, logits_near, both_near, columns = call(
         first_kernel,
         [(head.shape, head.dtype), ((count, width), jnp.float32), ((2 * count, width), jnp.bfloat16),
@@ -337,7 +345,7 @@
         scratch=[pltpu.SemaphoreType.DMA((4,))],
         sources=[pltpu.VMEM, pltpu.HBM, pltpu.VMEM], aliases={2: 0},
     )
-    count = rows - 4 * own
+    count = rows - 3 * own
     logits_far, both_far, mine = call(
         second_kernel,
         [((count, width), jnp.float32), ((2 * count, width), jnp.bfloat16), ((8, rows), jnp.float32)],
@@ -365,10 +373,10 @@
     scale = 2.0**14 * rows
     grads_far, grads_near = (
         call(
-            functools.partial(join_kernel, scale, first),
+            functools.partial(join_kernel, scale, first, 3 * own),
             [((count, depth), jnp.float32)], [lines, mine] + terms,
         )[0]
-        for first, count in ((4 * own, rows - 4 * own), (0, 4 * own))
+        for first, count in ((2 * own, rows - 2 * own), (0, 2 * own))
     )
     hidden_grad = (scatter_sums(grads_near, grads_far, own) * (1.0 / scale)).astype(jnp.bfloat16)
     loss = call(functools.partial(loss_kernel, members), [((8, LANES), jnp.float32)], [lines])[0]

time: 58.2 us -> 61.9 us (1.064)
  waiting for transfers between devices: 7.7 us -> 11.5 us
    ppermute x18 -> x16, waiting for transfers between devices: 7.7 us -> 11.5 us  [swap(): lax.ppermute(value, AXIS, [(i, i ^ step) for i in range(lax.axis_size(AXI...]
    ppermute x18 -> x16, starting transfers between devices: 23.9 us -> 23.3 us  [swap(): lax.ppermute(value, AXIS, [(i, i ^ step) for i in range(lax.axis_size(AXI...]
  transfers between devices with their start and end apart: 18 -> 16, of which waited for: 6 -> 6; matrix products, arithmetic and copies ran while one was open for 1% -> 1% of each run, Pallas kernels for 31% -> 29%
where the time goes in v14:
time: 61.9 us; the launch traced here: 61.8 us
  Pallas kernels  24.3 us (39%)
  starting transfers between devices  23.3 us (38%)
  waiting for transfers between devices  11.5 us (19%)
  other arithmetic  1.22 us (2%)
  between operations  0.84 us (1%)
  local copies, waits for them, and re-layouts  0.65 us (1%)
    ppermute x16, starting transfers between devices, swap(): lax.ppermute(value, AXIS, [(i, i ^ step) for i in range(lax.axis_size(AXI...  23.3 us
    pallas_call x11, Pallas kernels, call(): pl.pallas_call(kernel, out_shape=outs, in_specs=[pl.BlockSpec(memory_spac...  20.9 us
    ppermute x16, waiting for transfers between devices, swap(): lax.ppermute(value, AXIS, [(i, i ^ step) for i in range(lax.axis_size(AXI...  11.5 us
    pallas_call x1, Pallas kernels, frag_update(): pl.pallas_call(frag_kernel, grid=(width // TILE,), out_shape=[jax.ShapeDt...  3.38 us
  transfers between devices with their start and end apart: 16, of which 6 were waited for; matrix products, arithmetic and copies ran while one was open for 1% of the time, Pallas kernels for 29%

profile of v14, /device:TPU:0, one launch (start us, length us, event | category | flops | bytes accessed | tf_op | source)
XLA Modules:
  0.0 61.8 jit_solution(13550069042527022555)
XLA Ops:
  0.6 0.9 %shard_map.93 = bf16[16,4224]{1,0:T(8,128)(2,1)S(1)} custom-call(s32[16]{0:T(128)} %targets.1, bf16[16,4096]{1,0:T(8,128)(2,1)} %rows.1), custom_call_target="tpu_custom_call" | custom-call | bytes 131136 | tf_op jit(solution)/shard_map/pallas_call | solution.py:22
  1.6 3.1 %collective-permute-start.1 = (bf16[16,4224]{1,0:T(8,128)(2,1)S(1)}, bf16[16,4224]{1,0:T(8,128)(2,1)S(1)}, u32[]{:S(2)}, u32[]{:S(2)}) collective-permute-start(bf16[16,4224]{1,0:T(8,128)(2,1)S(1)} %shard_map.93), channel_id=1, source_target_pairs={{0,2},{1,3},{2,0},{3,1},{4,6},{5,7},{6,4},{7,5},{8,10},{9,11},{10,... | collective-permute-start | bytes 405512 | tf_op jit(solution)/shard_map/ppermute | solution.py:267
  4.7 2.6 %collective-permute-start = (bf16[16,4224]{1,0:T(8,128)(2,1)S(1)}, bf16[16,4224]{1,0:T(8,128)(2,1)S(1)}, u32[]{:S(2)}, u32[]{:S(2)}) collective-permute-start(bf16[16,4224]{1,0:T(8,128)(2,1)S(1)} %shard_map.93), channel_id=1, source_target_pairs={{0,4},{1,5},{2,6},{3,7},{4,0},{5,1},{6,2},{7,3},{8,12},{9,13},{10,... | collective-permute-start | bytes 405512 | tf_op jit(solution)/shard_map/ppermute | solution.py:267
  7.2 1.5 %collective-permute-start.5 = (bf16[16,4224]{1,0:T(8,128)(2,1)S(1)}, bf16[16,4224]{1,0:T(8,128)(2,1)S(1)}, u32[]{:S(2)}, u32[]{:S(2)}) collective-permute-start(bf16[16,4224]{1,0:T(8,128)(2,1)S(1)} %shard_map.93), channel_id=1, source_target_pairs={{0,1},{1,0},{2,3},{3,2},{4,5},{5,4},{6,7},{7,6},{8,9},{9,8},{10,11... | collective-permute-start | bytes 405512 | tf_op jit(solution)/shard_map/ppermute | solution.py:267
  8.8 3.5 %shard_map.94.held_ref = bf16[4096,2048]{1,0:T(8,128)(2,1)S(1)} custom-call(bf16[4096,2048]{1,0:T(8,128)(2,1)} %head.3), custom_call_target="tpu_custom_call" | custom-call | bytes 16777216 | tf_op jit(solution)/shard_map/pallas_call | solution.py:22
  12.3 1.3 %collective-permute-done = bf16[16,4224]{1,0:T(8,128)(2,1)S(1)} collective-permute-done((bf16[16,4224]{1,0:T(8,128)(2,1)S(1)}, bf16[16,4224]{1,0:T(8,128)(2,1)S(1)}, u32[]{:S(2)}, u32[]{:S(2)}) %collective-permute-start) | collective-permute-done | bytes 135200 | tf_op jit(solution)/shard_map/ppermute | solution.py:267
  13.6 1.6 %collective-permute-start.2 = (bf16[32,4224]{1,0:T(8,128)(2,1)S(1)}, bf16[32,4224]{1,0:T(8,128)(2,1)S(1)}, u32[]{:S(2)}, u32[]{:S(2)}) collective-permute-start(bf16[32,4224]{1,0:T(8,128)(2,1)S(1)} %pad_maximum_fusion.3), channel_id=1, source_target_pairs={{0,1},{1,0},{2,3},{3,2},{4,5},{5,4},{6,7},{7,6},{8,9},{9,8},{10,11... | collective-permute-start | bytes 811016 | tf_op jit(solution)/shard_map/ppermute | solution.py:267
  15.5 1.6 %collective-permute-start.3 = (bf16[16,4224]{1,0:T(8,128)(2,1)S(1)}, bf16[16,4224]{1,0:T(8,128)(2,1)S(1)}, u32[]{:S(2)}, u32[]{:S(2)}) collective-permute-start(bf16[16,4224]{1,0:T(8,128)(2,1)S(1)} %collective-permute-done), channel_id=1, source_target_pairs={{0,2},{1,3},{2,0},{3,1},{4,6},{5,7},{6,4},{7,5},{8,10},{9,11},{10,... | collective-permute-start | bytes 405512 | tf_op jit(solution)/shard_map/ppermute | solution.py:267
  17.2 5.8 %shard_map.95 = (bf16[4096,2048]{1,0:T(8,128)(2,1)S(1)}, f32[48,2048]{1,0:T(8,128)S(1)}, bf16[96,2048]{1,0:T(8,128)(2,1)S(1)}, f32[48,128]{1,0:T(8,128)S(1)}) custom-call(bf16[48,4224]{1,0:T(8,128)(2,1)S(1)} %pad_maximum_fusion.2.packed_ref.rows_one_ref.ids_one_ref, bf16[4096,2048]{1,0:T(8,128)(2,1)} %head.3, ...), custom_call_target="tpu_custom_call", output_to_operand_aliasing={{0}: (2, {})} | custom-call | flops 805306368 | bytes 33959936 | tf_op jit(solution)/shard_map/pallas_call | solution.py:22
  23.2 4.5 %shard_map.96 = (f32[80,2048]{1,0:T(8,128)S(1)}, bf16[160,2048]{1,0:T(8,128)(2,1)S(1)}, f32[8,128]{1,0:T(8,128)S(1)}) custom-call(bf16[80,4224]{1,0:T(8,128)(2,1)S(1)} %pad_maximum_fusion.rows_ref.rows_two_ref.ids_two_ref, bf16[4096,2048]{1,0:T(8,128)(2,1)S(1)} %get-tuple-element.13.near_ref.head_ref, f32[48,128]{1,0:T(8,128)S(1)} %get-tuple-element.14.before_ref), custom_call_target="tpu_custom_call" | custom-call | flops 1342177280 | bytes 17477632 | tf_op jit(solution)/shard_map/pallas_call | solution.py:22
  27.7 1.5 %collective-permute-start.6 = (f32[8,128]{1,0:T(8,128)S(1)}, f32[8,128]{1,0:T(8,128)S(1)}, u32[]{:S(2)}, u32[]{:S(2)}) collective-permute-start(f32[8,128]{1,0:T(8,128)S(1)} %get-tuple-element.15.mine_ref), channel_id=1, source_target_pairs={{0,4},{1,5},{2,6},{3,7},{4,0},{5,1},{6,2},{7,3},{8,12},{9,13},{10,... | collective-permute-start | bytes 12296 | tf_op jit(solution)/shard_map/ppermute | solution.py:267
  29.1 2.5 %shard_map.100.refs_0_ = f32[256,2048]{1,0:T(8,128)S(1)} custom-call(bf16[96,2048]{1,0:T(8,128)(2,1)S(1)} %get-tuple-element.16.one_ref, bf16[160,2048]{1,0:T(8,128)(2,1)S(1)} %get-tuple-element.17.two_ref, bf16[4096,2048]{1,0:T(8,128)(2,1)S(1)} %get-tuple-element.13.near_ref.head_ref), custom_call_target="tpu_custom_call" | custom-call | flops 2147483648 | bytes 17825792 | tf_op jit(solution)/shard_map/pallas_call | solution.py:22
  32.3 2.9 %collective-permute-start.9 = (f32[8,128]{1,0:T(8,128)S(1)}, f32[8,128]{1,0:T(8,128)S(1)}, u32[]{:S(2)}, u32[]{:S(2)}) collective-permute-start(f32[8,128]{1,0:T(8,128)S(1)} %shard_map.97.mine_ref.refs_0_), channel_id=1, source_target_pairs={{0,3},{1,2},{2,1},{3,0},{4,7},{5,6},{6,5},{7,4},{8,11},{9,10},{10,... | collective-permute-start | bytes 12296 | tf_op jit(solution)/shard_map/ppermute | solution.py:267
  35.9 2.5 %shard_map.101.refs_1_ = f32[256,2048]{1,0:T(8,128)S(1)} custom-call(bf16[96,2048]{1,0:T(8,128)(2,1)S(1)} %get-tuple-element.16.one_ref, bf16[160,2048]{1,0:T(8,128)(2,1)S(1)} %get-tuple-element.17.two_ref, bf16[4096,2048]{1,0:T(8,128)(2,1)S(1)} %get-tuple-element.13.near_ref.head_ref, f32[8,128]{1,0:T(8,128)S(1)} %shard_map.97.mine_ref.refs_0_), custom_call_target="tpu_custom_call" | custom-call | flops 2147483648 | bytes 17829888 | tf_op jit(solution)/shard_map/pallas_call | solution.py:22
  39.9 1.9 %collective-permute-start.13 = (f16[16,4096]{1,0:T(8,128)(2,1)S(1)}, f16[16,4096]{1,0:T(8,128)(2,1)S(1)}, u32[]{:S(2)}, u32[]{:S(2)}) collective-permute-start(f16[16,4096]{1,0:T(8,128)(2,1)S(1)} %get-tuple-element.24), channel_id=1, source_target_pairs={{0,2},{1,3},{2,0},{3,1},{4,6},{5,7},{6,4},{7,5},{8,10},{9,11},{10,... | collective-permute-start | bytes 393224 | tf_op jit(solution)/shard_map/ppermute | solution.py:267
  41.9 0.6 collective-permute-start.14
  42.5 1.1 %collective-permute-start.11 = (f16[32,4096]{1,0:T(8,128)(2,1)S(1)}, f16[32,4096]{1,0:T(8,128)(2,1)S(1)}, u32[]{:S(2)}, u32[]{:S(2)}) collective-permute-start(f16[32,4096]{1,0:T(8,128)(2,1)S(1)} %pad_maximum_fusion.4), channel_id=1, source_target_pairs={{0,1},{1,0},{2,3},{3,2},{4,5},{5,4},{6,7},{7,6},{8,9},{9,8},{10,11... | collective-permute-start | bytes 786440 | tf_op jit(solution)/shard_map/ppermute | solution.py:267
  43.7 1.1 %collective-permute-start.10 = (f16[16,4096]{1,0:T(8,128)(2,1)S(1)}, f16[16,4096]{1,0:T(8,128)(2,1)S(1)}, u32[]{:S(2)}, u32[]{:S(2)}) collective-permute-start(f16[16,4096]{1,0:T(8,128)(2,1)S(1)} %slice_convert_fusion), channel_id=1, source_target_pairs={{0,1},{1,0},{2,3},{3,2},{4,5},{5,4},{6,7},{7,6},{8,9},{9,8},{10,11... | collective-permute-start | bytes 393224 | tf_op jit(solution)/shard_map/ppermute | solution.py:267
  44.7 7.4 %collective-permute-done.11 = f16[32,4096]{1,0:T(8,128)(2,1)S(1)} collective-permute-done((f16[32,4096]{1,0:T(8,128)(2,1)S(1)}, f16[32,4096]{1,0:T(8,128)(2,1)S(1)}, u32[]{:S(2)}, u32[]{:S(2)}) %collective-permute-start.11) | collective-permute-done | bytes 262176 | tf_op jit(solution)/shard_map/ppermute | solution.py:267
  52.2 1.8 %collective-permute-start.12 = (f16[16,4096]{1,0:T(8,128)(2,1)S(1)}, f16[16,4096]{1,0:T(8,128)(2,1)S(1)}, u32[]{:S(2)}, u32[]{:S(2)}) collective-permute-start(f16[16,4096]{1,0:T(8,128)(2,1)S(1)} %get-tuple-element.22), channel_id=1, source_target_pairs={{0,2},{1,3},{2,0},{3,1},{4,6},{5,7},{6,4},{7,5},{8,10},{9,11},{10,... | collective-permute-start | bytes 393224 | tf_op jit(solution)/shard_map/ppermute | solution.py:267
  54.0 1.1 %collective-permute-start.15 = (f16[16,4096]{1,0:T(8,128)(2,1)S(1)}, f16[16,4096]{1,0:T(8,128)(2,1)S(1)}, u32[]{:S(2)}, u32[]{:S(2)}) collective-permute-start(f16[16,4096]{1,0:T(8,128)(2,1)S(1)} %get-tuple-element.23), channel_id=1, source_target_pairs={{0,4},{1,5},{2,6},{3,7},{4,0},{5,1},{6,2},{7,3},{8,12},{9,13},{10,... | collective-permute-start | bytes 393224 | tf_op jit(solution)/shard_map/ppermute | solution.py:267
  56.0 3.4 %shard_map.104 = (f32[128,2048]{1,0:T(8,128)}, f32[128,2048]{1,0:T(8,128)}) custom-call(bf16[48,4224]{1,0:T(8,128)(2,1)S(1)} %pad_maximum_fusion.2.packed_ref.rows_one_ref.ids_one_ref, bf16[80,4224]{1,0:T(8,128)(2,1)S(1)} %pad_maximum_fusion.rows_ref.rows_two_ref.ids_two_ref, bf16[48,4224]{1,0:T(8,128)(2,1)S(1)} %pad_maximum_fusion.2.packed_ref.rows_one_ref.ids_one_ref, ...), custom_call_target="tpu_custom_call" | custom-call | flops 67108864 | bytes 6291456 | tf_op jit(solution)/shard_map/pallas_call | solution.py:243
  59.3 1.7 %collective-permute-done.15 = f16[16,4096]{1,0:T(8,128)(2,1)S(1)} collective-permute-done((f16[16,4096]{1,0:T(8,128)(2,1)S(1)}, f16[16,4096]{1,0:T(8,128)(2,1)S(1)}, u32[]{:S(2)}, u32[]{:S(2)}) %collective-permute-start.15) | collective-permute-done | bytes 131104 | tf_op jit(solution)/shard_map/ppermute | solution.py:267
  61.0 0.7 %fusion.7 = bf16[16,4096]{1,0:T(8,128)(2,1)} fusion(f32[32,4096]{1,0:T(8,128)S(1)} %shard_map.102, f16[16,4096]{1,0:T(8,128)(2,1)S(1)} %collective-permute-done.15, f16[16,4096]{1,0:T(8,128)(2,1)S(1)} %collective-permute-done.12, f16[16,4096]{1,0:T(8,128)(2,1)S(1)} %collective-permute-done.10), kind=kLoop, calls=%fused_computation.15 | loop fusion | flops 524288 | bytes 786432 | tf_op jit(solution)/shard_map/convert_element_type | solution.py:381
  (39 shorter events, 4.5 us)
Async XLA Ops:
  1.6 10.7 %collective-permute-start.1 = (bf16[16,4224]{1,0:T(8,128)(2,1)S(1)}, bf16[16,4224]{1,0:T(8,128)(2,1)S(1)}, u32[]{:S(2)}, u32[]{:S(2)}) collective-permute-start(bf16[16,4224]{1,0:T(8,128)(2,1)S(1)} %shard_map.93), channel_id=1, source_target_pairs={{0,2},{1,3},{2,0},{3,1},{4,6},{5,7},{6,4},{7,5},{8,10},{9,11},{10,... | collective-permute-start | bytes 405512 | tf_op jit(solution)/shard_map/ppermute | solution.py:267
  4.7 8.9 %collective-permute-start = (bf16[16,4224]{1,0:T(8,128)(2,1)S(1)}, bf16[16,4224]{1,0:T(8,128)(2,1)S(1)}, u32[]{:S(2)}, u32[]{:S(2)}) collective-permute-start(bf16[16,4224]{1,0:T(8,128)(2,1)S(1)} %shard_map.93), channel_id=1, source_target_pairs={{0,4},{1,5},{2,6},{3,7},{4,0},{5,1},{6,2},{7,3},{8,12},{9,13},{10,... | collective-permute-start | bytes 405512 | tf_op jit(solution)/shard_map/ppermute | solution.py:267
  7.2 9.9 %collective-permute-start.5 = (bf16[16,4224]{1,0:T(8,128)(2,1)S(1)}, bf16[16,4224]{1,0:T(8,128)(2,1)S(1)}, u32[]{:S(2)}, u32[]{:S(2)}) collective-permute-start(bf16[16,4224]{1,0:T(8,128)(2,1)S(1)} %shard_map.93), channel_id=1, source_target_pairs={{0,1},{1,0},{2,3},{3,2},{4,5},{5,4},{6,7},{7,6},{8,9},{9,8},{10,11... | collective-permute-start | bytes 405512 | tf_op jit(solution)/shard_map/ppermute | solution.py:267
  13.6 9.4 %collective-permute-start.2 = (bf16[32,4224]{1,0:T(8,128)(2,1)S(1)}, bf16[32,4224]{1,0:T(8,128)(2,1)S(1)}, u32[]{:S(2)}, u32[]{:S(2)}) collective-permute-start(bf16[32,4224]{1,0:T(8,128)(2,1)S(1)} %pad_maximum_fusion.3), channel_id=1, source_target_pairs={{0,1},{1,0},{2,3},{3,2},{4,5},{5,4},{6,7},{7,6},{8,9},{9,8},{10,11... | collective-permute-start | bytes 811016 | tf_op jit(solution)/shard_map/ppermute | solution.py:267
  15.2 7.9 %collective-permute-start.4 = (bf16[16,4224]{1,0:T(8,128)(2,1)S(1)}, bf16[16,4224]{1,0:T(8,128)(2,1)S(1)}, u32[]{:S(2)}, u32[]{:S(2)}) collective-permute-start(bf16[16,4224]{1,0:T(8,128)(2,1)S(1)} %collective-permute-done), channel_id=1, source_target_pairs={{0,3},{1,2},{2,1},{3,0},{4,7},{5,6},{6,5},{7,4},{8,11},{9,10},{10,... | collective-permute-start | bytes 405512 | tf_op jit(solution)/shard_map/ppermute | solution.py:267
  15.5 7.5 %collective-permute-start.3 = (bf16[16,4224]{1,0:T(8,128)(2,1)S(1)}, bf16[16,4224]{1,0:T(8,128)(2,1)S(1)}, u32[]{:S(2)}, u32[]{:S(2)}) collective-permute-start(bf16[16,4224]{1,0:T(8,128)(2,1)S(1)} %collective-permute-done), channel_id=1, source_target_pairs={{0,2},{1,3},{2,0},{3,1},{4,6},{5,7},{6,4},{7,5},{8,10},{9,11},{10,... | collective-permute-start | bytes 405512 | tf_op jit(solution)/shard_map/ppermute | solution.py:267
  27.7 4.6 %collective-permute-start.6 = (f32[8,128]{1,0:T(8,128)S(1)}, f32[8,128]{1,0:T(8,128)S(1)}, u32[]{:S(2)}, u32[]{:S(2)}) collective-permute-start(f32[8,128]{1,0:T(8,128)S(1)} %get-tuple-element.15.mine_ref), channel_id=1, source_target_pairs={{0,4},{1,5},{2,6},{3,7},{4,0},{5,1},{6,2},{7,3},{8,12},{9,13},{10,... | collective-permute-start | bytes 12296 | tf_op jit(solution)/shard_map/ppermute | solution.py:267
  32.3 6.1 %collective-permute-start.9 = (f32[8,128]{1,0:T(8,128)S(1)}, f32[8,128]{1,0:T(8,128)S(1)}, u32[]{:S(2)}, u32[]{:S(2)}) collective-permute-start(f32[8,128]{1,0:T(8,128)S(1)} %shard_map.97.mine_ref.refs_0_), channel_id=1, source_target_pairs={{0,3},{1,2},{2,1},{3,0},{4,7},{5,6},{6,5},{7,4},{8,11},{9,10},{10,... | collective-permute-start | bytes 12296 | tf_op jit(solution)/shard_map/ppermute | solution.py:267
  35.2 3.6 %collective-permute-start.8 = (f32[8,128]{1,0:T(8,128)S(1)}, f32[8,128]{1,0:T(8,128)S(1)}, u32[]{:S(2)}, u32[]{:S(2)}) collective-permute-start(f32[8,128]{1,0:T(8,128)S(1)} %shard_map.97.mine_ref.refs_0_), channel_id=1, source_target_pairs={{0,2},{1,3},{2,0},{3,1},{4,6},{5,7},{6,4},{7,5},{8,10},{9,11},{10,... | collective-permute-start | bytes 12296 | tf_op jit(solution)/shard_map/ppermute | solution.py:267
  35.3 3.6 %collective-permute-start.7 = (f32[8,128]{1,0:T(8,128)S(1)}, f32[8,128]{1,0:T(8,128)S(1)}, u32[]{:S(2)}, u32[]{:S(2)}) collective-permute-start(f32[8,128]{1,0:T(8,128)S(1)} %shard_map.97.mine_ref.refs_0_), channel_id=1, source_target_pairs={{0,1},{1,0},{2,3},{3,2},{4,5},{5,4},{6,7},{7,6},{8,9},{9,8},{10,11... | collective-permute-start | bytes 12296 | tf_op jit(solution)/shard_map/ppermute | solution.py:267
  39.8 16.1 %copy-start = (f32[128,2048]{1,0:T(8,128)S(1)}, f32[128,2048]{1,0:T(8,128)}, u32[]{:S(2)}) copy-start(f32[128,2048]{1,0:T(8,128)} %global_ref.1) | copy-start | bytes 3145732
  39.8 16.1 %copy-start.1 = (f32[128,2048]{1,0:T(8,128)S(1)}, f32[128,2048]{1,0:T(8,128)}, u32[]{:S(2)}) copy-start(f32[128,2048]{1,0:T(8,128)} %momentum_ref.1) | copy-start | bytes 3145732
  39.8 16.1 %copy-start.2 = (f32[128,2048]{1,0:T(8,128)S(1)}, f32[128,2048]{1,0:T(8,128)}, u32[]{:S(2)}) copy-start(f32[128,2048]{1,0:T(8,128)} %peer_ref.1) | copy-start | bytes 3145732
  39.9 12.2 %collective-permute-start.13 = (f16[16,4096]{1,0:T(8,128)(2,1)S(1)}, f16[16,4096]{1,0:T(8,128)(2,1)S(1)}, u32[]{:S(2)}, u32[]{:S(2)}) collective-permute-start(f16[16,4096]{1,0:T(8,128)(2,1)S(1)} %get-tuple-element.24), channel_id=1, source_target_pairs={{0,2},{1,3},{2,0},{3,1},{4,6},{5,7},{6,4},{7,5},{8,10},{9,11},{10,... | collective-permute-start | bytes 393224 | tf_op jit(solution)/shard_map/ppermute | solution.py:267
  41.9 10.3 %collective-permute-start.14 = (f16[16,4096]{1,0:T(8,128)(2,1)S(1)}, f16[16,4096]{1,0:T(8,128)(2,1)S(1)}, u32[]{:S(2)}, u32[]{:S(2)}) collective-permute-start(f16[16,4096]{1,0:T(8,128)(2,1)S(1)} %get-tuple-element.25), channel_id=1, source_target_pairs={{0,3},{1,2},{2,1},{3,0},{4,7},{5,6},{6,5},{7,4},{8,11},{9,10},{10,... | collective-permute-start | bytes 393224 | tf_op jit(solution)/shard_map/ppermute | solution.py:267
  42.5 9.6 %collective-permute-start.11 = (f16[32,4096]{1,0:T(8,128)(2,1)S(1)}, f16[32,4096]{1,0:T(8,128)(2,1)S(1)}, u32[]{:S(2)}, u32[]{:S(2)}) collective-permute-start(f16[32,4096]{1,0:T(8,128)(2,1)S(1)} %pad_maximum_fusion.4), channel_id=1, source_target_pairs={{0,1},{1,0},{2,3},{3,2},{4,5},{5,4},{6,7},{7,6},{8,9},{9,8},{10,11... | collective-permute-start | bytes 786440 | tf_op jit(solution)/shard_map/ppermute | solution.py:267
  43.7 15.7 %collective-permute-start.10 = (f16[16,4096]{1,0:T(8,128)(2,1)S(1)}, f16[16,4096]{1,0:T(8,128)(2,1)S(1)}, u32[]{:S(2)}, u32[]{:S(2)}) collective-permute-start(f16[16,4096]{1,0:T(8,128)(2,1)S(1)} %slice_convert_fusion), channel_id=1, source_target_pairs={{0,1},{1,0},{2,3},{3,2},{4,5},{5,4},{6,7},{7,6},{8,9},{9,8},{10,11... | collective-permute-start | bytes 393224 | tf_op jit(solution)/shard_map/ppermute | solution.py:267
  52.2 7.1 %collective-permute-start.12 = (f16[16,4096]{1,0:T(8,128)(2,1)S(1)}, f16[16,4096]{1,0:T(8,128)(2,1)S(1)}, u32[]{:S(2)}, u32[]{:S(2)}) collective-permute-start(f16[16,4096]{1,0:T(8,128)(2,1)S(1)} %get-tuple-element.22), channel_id=1, source_target_pairs={{0,2},{1,3},{2,0},{3,1},{4,6},{5,7},{6,4},{7,5},{8,10},{9,11},{10,... | collective-permute-start | bytes 393224 | tf_op jit(solution)/shard_map/ppermute | solution.py:267
  54.0 7.0 %collective-permute-start.15 = (f16[16,4096]{1,0:T(8,128)(2,1)S(1)}, f16[16,4096]{1,0:T(8,128)(2,1)S(1)}, u32[]{:S(2)}, u32[]{:S(2)}) collective-permute-start(f16[16,4096]{1,0:T(8,128)(2,1)S(1)} %get-tuple-element.23), channel_id=1, source_target_pairs={{0,4},{1,5},{2,6},{3,7},{4,0},{5,1},{6,2},{7,3},{8,12},{9,13},{10,... | collective-permute-start | bytes 393224 | tf_op jit(solution)/shard_map/ppermute | solution.py:267

commit v15 on v11

--- a/solution.py
+++ b/solution.py
@@ -177,7 +177,7 @@
 
 def grad_kernel(first, one_ref, two_ref, near_ref, *refs):
     terms_ref = refs[-1]
-    tile = 1024
+    tile = min(terms_ref.shape[1], 2**19 // (one_ref.shape[0] + two_ref.shape[0]))
     both = jnp.concatenate([one_ref[...], two_ref[...]], axis=0)
     for place in range(0, terms_ref.shape[1], tile):
         turned = lax.dot_general(
@@ -302,7 +302,7 @@
 
     sums = blocks[::4]
     for part in (list(range(1, members // 4)), [0]):
-        for step in (3, 2, 1):
+        for step in (3, 1, 2):
             for i, value in zip(part, moved([blocks[4 * i + step] for i in part], step)):
                 sums[i] = sums[i] + value
     for step in far_steps()[::-1]:

time: 58.2 us -> 57.8 us (level)
  waiting for transfers between devices: 7.7 us -> 8.8 us
  starting transfers between devices: 23.9 us -> 22.8 us
    ppermute x18, starting transfers between devices: 23.9 us -> 22.8 us  [swap(): lax.ppermute(value, AXIS, [(i, i ^ step) for i in range(lax.axis_size(AXI...]
    ppermute x18, waiting for transfers between devices: 7.7 us -> 8.8 us  [swap(): lax.ppermute(value, AXIS, [(i, i ^ step) for i in range(lax.axis_size(AXI...]
  transfers between devices with their start and end apart: 18 -> 18, of which waited for: 6 -> 5; matrix products, arithmetic and copies ran while one was open for 1% -> 1% of each run, Pallas kernels for 31% -> 31%
where the time goes in v15:
time: 57.8 us; the launch traced here: 57.7 us
  Pallas kernels  23.4 us (40%)
  starting transfers between devices  22.8 us (39%)
  waiting for transfers between devices  8.8 us (15%)
  other arithmetic  1.07 us (2%)
  between operations  0.84 us (1%)
  local copies, waits for them, and re-layouts  0.68 us (1%)
    ppermute x18, starting transfers between devices, swap(): lax.ppermute(value, AXIS, [(i, i ^ step) for i in range(lax.axis_size(AXI...  22.8 us
    pallas_call x11, Pallas kernels, call(): pl.pallas_call(kernel, out_shape=outs, in_specs=[pl.BlockSpec(memory_spac...  20 us
    ppermute x18, waiting for transfers between devices, swap(): lax.ppermute(value, AXIS, [(i, i ^ step) for i in range(lax.axis_size(AXI...  8.8 us
    pallas_call x1, Pallas kernels, frag_update(): pl.pallas_call(frag_kernel, grid=(width // TILE,), out_shape=[jax.ShapeDt...  3.38 us
  transfers between devices with their start and end apart: 18, of which 5 were waited for; matrix products, arithmetic and copies ran while one was open for 1% of the time, Pallas kernels for 31%

profile of v15, /device:TPU:0, one launch (start us, length us, event | category | flops | bytes accessed | tf_op | source)
XLA Modules:
  0.0 57.7 jit_solution(4543070179158786178)
XLA Ops:
  0.6 0.9 %shard_map.93 = bf16[16,4224]{1,0:T(8,128)(2,1)S(1)} custom-call(s32[16]{0:T(128)} %targets.1, bf16[16,4096]{1,0:T(8,128)(2,1)} %rows.1), custom_call_target="tpu_custom_call" | custom-call | bytes 131136 | tf_op jit(solution)/shard_map/pallas_call | solution.py:22
  1.6 4.1 %collective-permute-start = (bf16[16,4224]{1,0:T(8,128)(2,1)S(1)}, bf16[16,4224]{1,0:T(8,128)(2,1)S(1)}, u32[]{:S(2)}, u32[]{:S(2)}) collective-permute-start(bf16[16,4224]{1,0:T(8,128)(2,1)S(1)} %shard_map.93), channel_id=1, source_target_pairs={{0,4},{1,5},{2,6},{3,7},{4,0},{5,1},{6,2},{7,3},{8,12},{9,13},{10,... | collective-permute-start | bytes 405512 | tf_op jit(solution)/shard_map/ppermute | solution.py:266
  5.7 2.5 %collective-permute-start.6 = (bf16[16,4224]{1,0:T(8,128)(2,1)S(1)}, bf16[16,4224]{1,0:T(8,128)(2,1)S(1)}, u32[]{:S(2)}, u32[]{:S(2)}) collective-permute-start(bf16[16,4224]{1,0:T(8,128)(2,1)S(1)} %shard_map.93), channel_id=1, source_target_pairs={{0,3},{1,2},{2,1},{3,0},{4,7},{5,6},{6,5},{7,4},{8,11},{9,10},{10,... | collective-permute-start | bytes 405512 | tf_op jit(solution)/shard_map/ppermute | solution.py:266
  9.2 3.5 %shard_map.94.held_ref = bf16[4096,2048]{1,0:T(8,128)(2,1)S(1)} custom-call(bf16[4096,2048]{1,0:T(8,128)(2,1)} %head.3), custom_call_target="tpu_custom_call" | custom-call | bytes 16777216 | tf_op jit(solution)/shard_map/pallas_call | solution.py:22
  12.7 2.6 %collective-permute-start.3 = (bf16[16,4224]{1,0:T(8,128)(2,1)S(1)}, bf16[16,4224]{1,0:T(8,128)(2,1)S(1)}, u32[]{:S(2)}, u32[]{:S(2)}) collective-permute-start(bf16[16,4224]{1,0:T(8,128)(2,1)S(1)} %collective-permute-done), channel_id=1, source_target_pairs={{0,3},{1,2},{2,1},{3,0},{4,7},{5,6},{6,5},{7,4},{8,11},{9,10},{10,... | collective-permute-start | bytes 405512 | tf_op jit(solution)/shard_map/ppermute | solution.py:266
  16.2 1.1 %collective-permute-done.5 = bf16[16,4224]{1,0:T(8,128)(2,1)S(1)} collective-permute-done((bf16[16,4224]{1,0:T(8,128)(2,1)S(1)}, bf16[16,4224]{1,0:T(8,128)(2,1)S(1)}, u32[]{:S(2)}, u32[]{:S(2)}) %collective-permute-start.5) | collective-permute-done | bytes 135200 | tf_op jit(solution)/shard_map/ppermute | solution.py:266
  17.4 5.7 %shard_map.95 = (bf16[4096,2048]{1,0:T(8,128)(2,1)S(1)}, f32[64,2048]{1,0:T(8,128)S(1)}, bf16[128,2048]{1,0:T(8,128)(2,1)S(1)}, f32[64,128]{1,0:T(8,128)S(1)}) custom-call(bf16[64,4224]{1,0:T(8,128)(2,1)S(1)} %pad_maximum_fusion.1.packed_ref.rows_one_ref.ids_one_ref, bf16[4096,2048]{1,0:T(8,128)(2,1)} %head.3, ...), custom_call_target="tpu_custom_call", output_to_operand_aliasing={{0}: (2, {})} | custom-call | flops 1073741824 | bytes 34095104 | tf_op jit(solution)/shard_map/pallas_call | solution.py:22
  23.2 3.7 %shard_map.96 = (f32[64,2048]{1,0:T(8,128)S(1)}, bf16[128,2048]{1,0:T(8,128)(2,1)S(1)}, f32[8,128]{1,0:T(8,128)S(1)}) custom-call(bf16[64,4224]{1,0:T(8,128)(2,1)S(1)} %bitcast.6, bf16[4096,2048]{1,0:T(8,128)(2,1)S(1)} %get-tuple-element.13.near_ref.head_ref, f32[64,128]{1,0:T(8,128)S(1)} %get-tuple-element.14.before_ref), custom_call_target="tpu_custom_call" | custom-call | flops 1073741824 | bytes 17350656 | tf_op jit(solution)/shard_map/pallas_call | solution.py:22
  26.9 0.8 %collective-permute-start.7 = (f32[8,128]{1,0:T(8,128)S(1)}, f32[8,128]{1,0:T(8,128)S(1)}, u32[]{:S(2)}, u32[]{:S(2)}) collective-permute-start(f32[8,128]{1,0:T(8,128)S(1)} %get-tuple-element.15.mine_ref), channel_id=1, source_target_pairs={{0,4},{1,5},{2,6},{3,7},{4,0},{5,1},{6,2},{7,3},{8,12},{9,13},{10,... | collective-permute-start | bytes 12296 | tf_op jit(solution)/shard_map/ppermute | solution.py:266
  27.8 2.5 %shard_map.100.refs_0_ = f32[256,2048]{1,0:T(8,128)S(1)} custom-call(bf16[128,2048]{1,0:T(8,128)(2,1)S(1)} %get-tuple-element.16.one_ref, bf16[128,2048]{1,0:T(8,128)(2,1)S(1)} %get-tuple-element.17.two_ref, bf16[4096,2048]{1,0:T(8,128)(2,1)S(1)} %get-tuple-element.13.near_ref.head_ref), custom_call_target="tpu_custom_call" | custom-call | flops 2147483648 | bytes 17825792 | tf_op jit(solution)/shard_map/pallas_call | solution.py:22
  30.3 1.2 %collective-permute-done.7.refs_0_ = f32[8,128]{1,0:T(8,128)S(1)} collective-permute-done((f32[8,128]{1,0:T(8,128)S(1)}, f32[8,128]{1,0:T(8,128)S(1)}, u32[]{:S(2)}, u32[]{:S(2)}) %collective-permute-start.7) | collective-permute-done | bytes 4128 | tf_op jit(solution)/shard_map/ppermute | solution.py:266
  31.6 1.6 %collective-permute-start.10 = (f32[8,128]{1,0:T(8,128)S(1)}, f32[8,128]{1,0:T(8,128)S(1)}, u32[]{:S(2)}, u32[]{:S(2)}) collective-permute-start(f32[8,128]{1,0:T(8,128)S(1)} %shard_map.97.mine_ref.refs_0_), channel_id=1, source_target_pairs={{0,3},{1,2},{2,1},{3,0},{4,7},{5,6},{6,5},{7,4},{8,11},{9,10},{10,... | collective-permute-start | bytes 12296 | tf_op jit(solution)/shard_map/ppermute | solution.py:266
  33.8 1.3 %collective-permute-start.8 = (f32[8,128]{1,0:T(8,128)S(1)}, f32[8,128]{1,0:T(8,128)S(1)}, u32[]{:S(2)}, u32[]{:S(2)}) collective-permute-start(f32[8,128]{1,0:T(8,128)S(1)} %shard_map.97.mine_ref.refs_0_), channel_id=1, source_target_pairs={{0,1},{1,0},{2,3},{3,2},{4,5},{5,4},{6,7},{7,6},{8,9},{9,8},{10,11... | collective-permute-start | bytes 12296 | tf_op jit(solution)/shard_map/ppermute | solution.py:266
  35.1 2.5 %shard_map.101.refs_1_ = f32[256,2048]{1,0:T(8,128)S(1)} custom-call(bf16[128,2048]{1,0:T(8,128)(2,1)S(1)} %get-tuple-element.16.one_ref, bf16[128,2048]{1,0:T(8,128)(2,1)S(1)} %get-tuple-element.17.two_ref, bf16[4096,2048]{1,0:T(8,128)(2,1)S(1)} %get-tuple-element.13.near_ref.head_ref, f32[8,128]{1,0:T(8,128)S(1)} %shard_map.97.mine_ref.refs_0_), custom_call_target="tpu_custom_call" | custom-call | flops 2147483648 | bytes 17829888 | tf_op jit(solution)/shard_map/pallas_call | solution.py:22
  38.7 1.6 %collective-permute-start.14 = (f16[16,4096]{1,0:T(8,128)(2,1)S(1)}, f16[16,4096]{1,0:T(8,128)(2,1)S(1)}, u32[]{:S(2)}, u32[]{:S(2)}) collective-permute-start(f16[16,4096]{1,0:T(8,128)(2,1)S(1)} %get-tuple-element.25), channel_id=1, source_target_pairs={{0,3},{1,2},{2,1},{3,0},{4,7},{5,6},{6,5},{7,4},{8,11},{9,10},{10,... | collective-permute-start | bytes 393224 | tf_op jit(solution)/shard_map/ppermute | solution.py:266
  40.3 1.0 %collective-permute-start.16 = (f16[16,4096]{1,0:T(8,128)(2,1)S(1)}, f16[16,4096]{1,0:T(8,128)(2,1)S(1)}, u32[]{:S(2)}, u32[]{:S(2)}) collective-permute-start(f16[16,4096]{1,0:T(8,128)(2,1)S(1)} %get-tuple-element.26), channel_id=1, source_target_pairs={{0,2},{1,3},{2,0},{3,1},{4,6},{5,7},{6,4},{7,5},{8,10},{9,11},{10,... | collective-permute-start | bytes 393224 | tf_op jit(solution)/shard_map/ppermute | solution.py:266
  41.3 1.0 %collective-permute-start.15 = (f16[16,4096]{1,0:T(8,128)(2,1)S(1)}, f16[16,4096]{1,0:T(8,128)(2,1)S(1)}, u32[]{:S(2)}, u32[]{:S(2)}) collective-permute-start(f16[16,4096]{1,0:T(8,128)(2,1)S(1)} %get-tuple-element.27), channel_id=1, source_target_pairs={{0,1},{1,0},{2,3},{3,2},{4,5},{5,4},{6,7},{7,6},{8,9},{9,8},{10,11... | collective-permute-start | bytes 393224 | tf_op jit(solution)/shard_map/ppermute | solution.py:266
  42.3 1.6 %collective-permute-start.11 = (f16[16,4096]{1,0:T(8,128)(2,1)S(1)}, f16[16,4096]{1,0:T(8,128)(2,1)S(1)}, u32[]{:S(2)}, u32[]{:S(2)}) collective-permute-start(f16[16,4096]{1,0:T(8,128)(2,1)S(1)} %get-tuple-element.22), channel_id=1, source_target_pairs={{0,3},{1,2},{2,1},{3,0},{4,7},{5,6},{6,5},{7,4},{8,11},{9,10},{10,... | collective-permute-start | bytes 393224 | tf_op jit(solution)/shard_map/ppermute | solution.py:266
  43.9 1.0 %collective-permute-start.13 = (f16[16,4096]{1,0:T(8,128)(2,1)S(1)}, f16[16,4096]{1,0:T(8,128)(2,1)S(1)}, u32[]{:S(2)}, u32[]{:S(2)}) collective-permute-start(f16[16,4096]{1,0:T(8,128)(2,1)S(1)} %get-tuple-element.23), channel_id=1, source_target_pairs={{0,2},{1,3},{2,0},{3,1},{4,6},{5,7},{6,4},{7,5},{8,10},{9,11},{10,... | collective-permute-start | bytes 393224 | tf_op jit(solution)/shard_map/ppermute | solution.py:266
  44.9 1.2 %collective-permute-done.14 = f16[16,4096]{1,0:T(8,128)(2,1)S(1)} collective-permute-done((f16[16,4096]{1,0:T(8,128)(2,1)S(1)}, f16[16,4096]{1,0:T(8,128)(2,1)S(1)}, u32[]{:S(2)}, u32[]{:S(2)}) %collective-permute-start.14) | collective-permute-done | bytes 131104 | tf_op jit(solution)/shard_map/ppermute | solution.py:266
  46.1 1.1 %collective-permute-start.12 = (f16[16,4096]{1,0:T(8,128)(2,1)S(1)}, f16[16,4096]{1,0:T(8,128)(2,1)S(1)}, u32[]{:S(2)}, u32[]{:S(2)}) collective-permute-start(f16[16,4096]{1,0:T(8,128)(2,1)S(1)} %get-tuple-element.24), channel_id=1, source_target_pairs={{0,1},{1,0},{2,3},{3,2},{4,5},{5,4},{6,7},{7,6},{8,9},{9,8},{10,11... | collective-permute-start | bytes 393224 | tf_op jit(solution)/shard_map/ppermute | solution.py:266
  47.2 2.7 %collective-permute-done.16 = f16[16,4096]{1,0:T(8,128)(2,1)S(1)} collective-permute-done((f16[16,4096]{1,0:T(8,128)(2,1)S(1)}, f16[16,4096]{1,0:T(8,128)(2,1)S(1)}, u32[]{:S(2)}, u32[]{:S(2)}) %collective-permute-start.16) | collective-permute-done | bytes 131104 | tf_op jit(solution)/shard_map/ppermute | solution.py:266
  50.9 3.4 %shard_map.104 = (f32[128,2048]{1,0:T(8,128)}, f32[128,2048]{1,0:T(8,128)}) custom-call(bf16[64,4224]{1,0:T(8,128)(2,1)S(1)} %pad_maximum_fusion.1.packed_ref.rows_one_ref.ids_one_ref, bf16[64,4224]{1,0:T(8,128)(2,1)S(1)} %bitcast.7, bf16[64,4224]{1,0:T(8,128)(2,1)S(1)} %pad_maximum_fusion.1.packed_ref.rows_one_ref.ids_one_ref, ...), custom_call_target="tpu_custom_call" | custom-call | flops 67108864 | bytes 6291456 | tf_op jit(solution)/shard_map/pallas_call | solution.py:242
  54.3 2.6 %collective-permute-done.17 = f16[16,4096]{1,0:T(8,128)(2,1)S(1)} collective-permute-done((f16[16,4096]{1,0:T(8,128)(2,1)S(1)}, f16[16,4096]{1,0:T(8,128)(2,1)S(1)}, u32[]{:S(2)}, u32[]{:S(2)}) %collective-permute-start.17) | collective-permute-done | bytes 131104 | tf_op jit(solution)/shard_map/ppermute | solution.py:266
  (39 shorter events, 5.6 us)
Async XLA Ops:
  1.6 11.1 %collective-permute-start = (bf16[16,4224]{1,0:T(8,128)(2,1)S(1)}, bf16[16,4224]{1,0:T(8,128)(2,1)S(1)}, u32[]{:S(2)}, u32[]{:S(2)}) collective-permute-start(bf16[16,4224]{1,0:T(8,128)(2,1)S(1)} %shard_map.93), channel_id=1, source_target_pairs={{0,4},{1,5},{2,6},{3,7},{4,0},{5,1},{6,2},{7,3},{8,12},{9,13},{10,... | collective-permute-start | bytes 405512 | tf_op jit(solution)/shard_map/ppermute | solution.py:266
  5.7 10.1 %collective-permute-start.6 = (bf16[16,4224]{1,0:T(8,128)(2,1)S(1)}, bf16[16,4224]{1,0:T(8,128)(2,1)S(1)}, u32[]{:S(2)}, u32[]{:S(2)}) collective-permute-start(bf16[16,4224]{1,0:T(8,128)(2,1)S(1)} %shard_map.93), channel_id=1, source_target_pairs={{0,3},{1,2},{2,1},{3,0},{4,7},{5,6},{6,5},{7,4},{8,11},{9,10},{10,... | collective-permute-start | bytes 405512 | tf_op jit(solution)/shard_map/ppermute | solution.py:266
  8.2 9.2 %collective-permute-start.5 = (bf16[16,4224]{1,0:T(8,128)(2,1)S(1)}, bf16[16,4224]{1,0:T(8,128)(2,1)S(1)}, u32[]{:S(2)}, u32[]{:S(2)}) collective-permute-start(bf16[16,4224]{1,0:T(8,128)(2,1)S(1)} %shard_map.93), channel_id=1, source_target_pairs={{0,2},{1,3},{2,0},{3,1},{4,6},{5,7},{6,4},{7,5},{8,10},{9,11},{10,... | collective-permute-start | bytes 405512 | tf_op jit(solution)/shard_map/ppermute | solution.py:266
  8.6 8.7 %collective-permute-start.4 = (bf16[16,4224]{1,0:T(8,128)(2,1)S(1)}, bf16[16,4224]{1,0:T(8,128)(2,1)S(1)}, u32[]{:S(2)}, u32[]{:S(2)}) collective-permute-start(bf16[16,4224]{1,0:T(8,128)(2,1)S(1)} %shard_map.93), channel_id=1, source_target_pairs={{0,1},{1,0},{2,3},{3,2},{4,5},{5,4},{6,7},{7,6},{8,9},{9,8},{10,11... | collective-permute-start | bytes 405512 | tf_op jit(solution)/shard_map/ppermute | solution.py:266
  12.7 10.4 %collective-permute-start.3 = (bf16[16,4224]{1,0:T(8,128)(2,1)S(1)}, bf16[16,4224]{1,0:T(8,128)(2,1)S(1)}, u32[]{:S(2)}, u32[]{:S(2)}) collective-permute-start(bf16[16,4224]{1,0:T(8,128)(2,1)S(1)} %collective-permute-done), channel_id=1, source_target_pairs={{0,3},{1,2},{2,1},{3,0},{4,7},{5,6},{6,5},{7,4},{8,11},{9,10},{10,... | collective-permute-start | bytes 405512 | tf_op jit(solution)/shard_map/ppermute | solution.py:266
  15.3 7.8 %collective-permute-start.2 = (bf16[16,4224]{1,0:T(8,128)(2,1)S(1)}, bf16[16,4224]{1,0:T(8,128)(2,1)S(1)}, u32[]{:S(2)}, u32[]{:S(2)}) collective-permute-start(bf16[16,4224]{1,0:T(8,128)(2,1)S(1)} %collective-permute-done), channel_id=1, source_target_pairs={{0,2},{1,3},{2,0},{3,1},{4,6},{5,7},{6,4},{7,5},{8,10},{9,11},{10,... | collective-permute-start | bytes 405512 | tf_op jit(solution)/shard_map/ppermute | solution.py:266
  15.7 7.4 %collective-permute-start.1 = (bf16[16,4224]{1,0:T(8,128)(2,1)S(1)}, bf16[16,4224]{1,0:T(8,128)(2,1)S(1)}, u32[]{:S(2)}, u32[]{:S(2)}) collective-permute-start(bf16[16,4224]{1,0:T(8,128)(2,1)S(1)} %collective-permute-done), channel_id=1, source_target_pairs={{0,1},{1,0},{2,3},{3,2},{4,5},{5,4},{6,7},{7,6},{8,9},{9,8},{10,11... | collective-permute-start | bytes 405512 | tf_op jit(solution)/shard_map/ppermute | solution.py:266
  26.9 4.5 %collective-permute-start.7 = (f32[8,128]{1,0:T(8,128)S(1)}, f32[8,128]{1,0:T(8,128)S(1)}, u32[]{:S(2)}, u32[]{:S(2)}) collective-permute-start(f32[8,128]{1,0:T(8,128)S(1)} %get-tuple-element.15.mine_ref), channel_id=1, source_target_pairs={{0,4},{1,5},{2,6},{3,7},{4,0},{5,1},{6,2},{7,3},{8,12},{9,13},{10,... | collective-permute-start | bytes 12296 | tf_op jit(solution)/shard_map/ppermute | solution.py:266
  31.6 6.1 %collective-permute-start.10 = (f32[8,128]{1,0:T(8,128)S(1)}, f32[8,128]{1,0:T(8,128)S(1)}, u32[]{:S(2)}, u32[]{:S(2)}) collective-permute-start(f32[8,128]{1,0:T(8,128)S(1)} %shard_map.97.mine_ref.refs_0_), channel_id=1, source_target_pairs={{0,3},{1,2},{2,1},{3,0},{4,7},{5,6},{6,5},{7,4},{8,11},{9,10},{10,... | collective-permute-start | bytes 12296 | tf_op jit(solution)/shard_map/ppermute | solution.py:266
  33.2 4.5 %collective-permute-start.9 = (f32[8,128]{1,0:T(8,128)S(1)}, f32[8,128]{1,0:T(8,128)S(1)}, u32[]{:S(2)}, u32[]{:S(2)}) collective-permute-start(f32[8,128]{1,0:T(8,128)S(1)} %shard_map.97.mine_ref.refs_0_), channel_id=1, source_target_pairs={{0,2},{1,3},{2,0},{3,1},{4,6},{5,7},{6,4},{7,5},{8,10},{9,11},{10,... | collective-permute-start | bytes 12296 | tf_op jit(solution)/shard_map/ppermute | solution.py:266
  33.8 3.8 %collective-permute-start.8 = (f32[8,128]{1,0:T(8,128)S(1)}, f32[8,128]{1,0:T(8,128)S(1)}, u32[]{:S(2)}, u32[]{:S(2)}) collective-permute-start(f32[8,128]{1,0:T(8,128)S(1)} %shard_map.97.mine_ref.refs_0_), channel_id=1, source_target_pairs={{0,1},{1,0},{2,3},{3,2},{4,5},{5,4},{6,7},{7,6},{8,9},{9,8},{10,11... | collective-permute-start | bytes 12296 | tf_op jit(solution)/shard_map/ppermute | solution.py:266
  38.5 12.4 %copy-start.2 = (f32[128,2048]{1,0:T(8,128)S(1)}, f32[128,2048]{1,0:T(8,128)}, u32[]{:S(2)}) copy-start(f32[128,2048]{1,0:T(8,128)} %peer_ref.1) | copy-start | bytes 3145732
  38.6 12.3 %copy-start = (f32[128,2048]{1,0:T(8,128)S(1)}, f32[128,2048]{1,0:T(8,128)}, u32[]{:S(2)}) copy-start(f32[128,2048]{1,0:T(8,128)} %global_ref.1) | copy-start | bytes 3145732
  38.6 12.3 %copy-start.1 = (f32[128,2048]{1,0:T(8,128)S(1)}, f32[128,2048]{1,0:T(8,128)}, u32[]{:S(2)}) copy-start(f32[128,2048]{1,0:T(8,128)} %momentum_ref.1) | copy-start | bytes 3145732
  38.7 7.4 %collective-permute-start.14 = (f16[16,4096]{1,0:T(8,128)(2,1)S(1)}, f16[16,4096]{1,0:T(8,128)(2,1)S(1)}, u32[]{:S(2)}, u32[]{:S(2)}) collective-permute-start(f16[16,4096]{1,0:T(8,128)(2,1)S(1)} %get-tuple-element.25), channel_id=1, source_target_pairs={{0,3},{1,2},{2,1},{3,0},{4,7},{5,6},{6,5},{7,4},{8,11},{9,10},{10,... | collective-permute-start | bytes 393224 | tf_op jit(solution)/shard_map/ppermute | solution.py:266
  40.3 9.6 %collective-permute-start.16 = (f16[16,4096]{1,0:T(8,128)(2,1)S(1)}, f16[16,4096]{1,0:T(8,128)(2,1)S(1)}, u32[]{:S(2)}, u32[]{:S(2)}) collective-permute-start(f16[16,4096]{1,0:T(8,128)(2,1)S(1)} %get-tuple-element.26), channel_id=1, source_target_pairs={{0,2},{1,3},{2,0},{3,1},{4,6},{5,7},{6,4},{7,5},{8,10},{9,11},{10,... | collective-permute-start | bytes 393224 | tf_op jit(solution)/shard_map/ppermute | solution.py:266
  41.3 8.6 %collective-permute-start.15 = (f16[16,4096]{1,0:T(8,128)(2,1)S(1)}, f16[16,4096]{1,0:T(8,128)(2,1)S(1)}, u32[]{:S(2)}, u32[]{:S(2)}) collective-permute-start(f16[16,4096]{1,0:T(8,128)(2,1)S(1)} %get-tuple-element.27), channel_id=1, source_target_pairs={{0,1},{1,0},{2,3},{3,2},{4,5},{5,4},{6,7},{7,6},{8,9},{9,8},{10,11... | collective-permute-start | bytes 393224 | tf_op jit(solution)/shard_map/ppermute | solution.py:266
  42.3 11.9 %collective-permute-start.11 = (f16[16,4096]{1,0:T(8,128)(2,1)S(1)}, f16[16,4096]{1,0:T(8,128)(2,1)S(1)}, u32[]{:S(2)}, u32[]{:S(2)}) collective-permute-start(f16[16,4096]{1,0:T(8,128)(2,1)S(1)} %get-tuple-element.22), channel_id=1, source_target_pairs={{0,3},{1,2},{2,1},{3,0},{4,7},{5,6},{6,5},{7,4},{8,11},{9,10},{10,... | collective-permute-start | bytes 393224 | tf_op jit(solution)/shard_map/ppermute | solution.py:266
  43.9 10.3 %collective-permute-start.13 = (f16[16,4096]{1,0:T(8,128)(2,1)S(1)}, f16[16,4096]{1,0:T(8,128)(2,1)S(1)}, u32[]{:S(2)}, u32[]{:S(2)}) collective-permute-start(f16[16,4096]{1,0:T(8,128)(2,1)S(1)} %get-tuple-element.23), channel_id=1, source_target_pairs={{0,2},{1,3},{2,0},{3,1},{4,6},{5,7},{6,4},{7,5},{8,10},{9,11},{10,... | collective-permute-start | bytes 393224 | tf_op jit(solution)/shard_map/ppermute | solution.py:266
  46.1 8.2 %collective-permute-start.12 = (f16[16,4096]{1,0:T(8,128)(2,1)S(1)}, f16[16,4096]{1,0:T(8,128)(2,1)S(1)}, u32[]{:S(2)}, u32[]{:S(2)}) collective-permute-start(f16[16,4096]{1,0:T(8,128)(2,1)S(1)} %get-tuple-element.24), channel_id=1, source_target_pairs={{0,1},{1,0},{2,3},{3,2},{4,5},{5,4},{6,7},{7,6},{8,9},{9,8},{10,11... | collective-permute-start | bytes 393224 | tf_op jit(solution)/shard_map/ppermute | solution.py:266
  50.0 6.9 %collective-permute-start.17 = (f16[16,4096]{1,0:T(8,128)(2,1)S(1)}, f16[16,4096]{1,0:T(8,128)(2,1)S(1)}, u32[]{:S(2)}, u32[]{:S(2)}) collective-permute-start(f16[16,4096]{1,0:T(8,128)(2,1)S(1)} %fusion.2), channel_id=1, source_target_pairs={{0,4},{1,5},{2,6},{3,7},{4,0},{5,1},{6,2},{7,3},{8,12},{9,13},{10,... | collective-permute-start | bytes 393224 | tf_op jit(solution)/shard_map/ppermute | solution.py:266

commit v16 on v15

--- a/solution.py
+++ b/solution.py
@@ -83,7 +83,7 @@
 
 
 def shared_order(value, members):
-    me = lax.axis_index(AXIS)
+    me = my_label()
     step = 1
     while step < members:
         swapped = swap_blocks(value, value.shape[1] // members * step)
@@ -154,7 +154,7 @@
 def merge_kernel(steps, members, mine_ref, *refs):
     *other_refs, out_ref = refs
     block = mine_ref.shape[1] // members
-    me = lax.axis_index(AXIS)
+    me = my_label()
     groups = [mine_ref[...]]
     for step, other_ref in zip(steps, other_refs):
         other, bit = other_ref[...], 1
@@ -262,8 +262,22 @@
     )
 
 
+def turned(label):
+    return label // 4 * 4 + label % 2 * 2 + label // 2 % 2
+
+
+def my_label():
+    me = lax.axis_index(AXIS)
+    return jnp.where(lax.rem(lax.axis_index("outer"), 2) == 1, turned(me), me)
+
+
 def swap(value, step):
-    return lax.ppermute(value, AXIS, [(i, i ^ step) for i in range(lax.axis_size(AXIS))])
+    members = lax.axis_size(AXIS)
+    pairs = []
+    for outer in range(lax.axis_size("outer")):
+        flip = turned(step) if outer % 2 else step
+        pairs += [(outer * members + i, outer * members + (i ^ flip)) for i in range(members)]
+    return lax.ppermute(value, ("outer", AXIS), pairs)
 
 
 def far_steps():

time: 57.8 us -> 57.4 us (level)
  waiting for transfers between devices: 8.8 us -> 8.01 us
    ppermute x18, waiting for transfers between devices: 8.8 us -> 8.01 us  [swap(): return lax.ppermute(value, ('outer', AXIS), pairs)]
where the time goes in v16:
time: 57.4 us; the launch traced here: 57.2 us
  Pallas kernels  23.4 us (41%)
  starting transfers between devices  23.2 us (40%)
  waiting for transfers between devices  8.01 us (14%)
  other arithmetic  1.07 us (2%)
  between operations  0.84 us (1%)
  local copies, waits for them, and re-layouts  0.68 us (1%)
    ppermute x18, starting transfers between devices, swap(): return lax.ppermute(value, ('outer', AXIS), pairs)  23.2 us
    pallas_call x11, Pallas kernels, call(): pl.pallas_call(kernel, out_shape=outs, in_specs=[pl.BlockSpec(memory_spac...  20 us
    ppermute x18, waiting for transfers between devices, swap(): return lax.ppermute(value, ('outer', AXIS), pairs)  8.01 us
    pallas_call x1, Pallas kernels, frag_update(): pl.pallas_call(frag_kernel, grid=(width // TILE,), out_shape=[jax.ShapeDt...  3.38 us
  transfers between devices with their start and end apart: 18, of which 5 were waited for; matrix products, arithmetic and copies ran while one was open for 1% of the time, Pallas kernels for 31%

profile of v16, /device:TPU:0, one launch (start us, length us, event | category | flops | bytes accessed | tf_op | source)
XLA Modules:
  0.0 57.2 jit_solution(1068243931653380996)
XLA Ops:
  0.6 0.9 %shard_map.93 = bf16[16,4224]{1,0:T(8,128)(2,1)S(1)} custom-call(s32[16]{0:T(128)} %targets.1, bf16[16,4096]{1,0:T(8,128)(2,1)} %rows.1), custom_call_target="tpu_custom_call" | custom-call | bytes 131136 | tf_op jit(solution)/shard_map/pallas_call | solution.py:22
  1.6 4.1 %collective-permute-start = (bf16[16,4224]{1,0:T(8,128)(2,1)S(1)}, bf16[16,4224]{1,0:T(8,128)(2,1)S(1)}, u32[]{:S(2)}, u32[]{:S(2)}) collective-permute-start(bf16[16,4224]{1,0:T(8,128)(2,1)S(1)} %shard_map.93), channel_id=1, source_target_pairs={{0,4},{1,5},{2,6},{3,7},{4,0},{5,1},{6,2},{7,3},{8,12},{9,13},{10,... | collective-permute-start | bytes 405512 | tf_op jit(solution)/shard_map/ppermute | solution.py:280
  5.7 2.5 %collective-permute-start.6 = (bf16[16,4224]{1,0:T(8,128)(2,1)S(1)}, bf16[16,4224]{1,0:T(8,128)(2,1)S(1)}, u32[]{:S(2)}, u32[]{:S(2)}) collective-permute-start(bf16[16,4224]{1,0:T(8,128)(2,1)S(1)} %shard_map.93), channel_id=1, source_target_pairs={{0,3},{1,2},{2,1},{3,0},{4,7},{5,6},{6,5},{7,4},{8,11},{9,10},{10,... | collective-permute-start | bytes 405512 | tf_op jit(solution)/shard_map/ppermute | solution.py:280
  9.2 3.5 %shard_map.94.held_ref = bf16[4096,2048]{1,0:T(8,128)(2,1)S(1)} custom-call(bf16[4096,2048]{1,0:T(8,128)(2,1)} %head.3), custom_call_target="tpu_custom_call" | custom-call | bytes 16777216 | tf_op jit(solution)/shard_map/pallas_call | solution.py:22
  12.7 2.6 %collective-permute-start.3 = (bf16[16,4224]{1,0:T(8,128)(2,1)S(1)}, bf16[16,4224]{1,0:T(8,128)(2,1)S(1)}, u32[]{:S(2)}, u32[]{:S(2)}) collective-permute-start(bf16[16,4224]{1,0:T(8,128)(2,1)S(1)} %collective-permute-done), channel_id=1, source_target_pairs={{0,3},{1,2},{2,1},{3,0},{4,7},{5,6},{6,5},{7,4},{8,11},{9,10},{10,... | collective-permute-start | bytes 405512 | tf_op jit(solution)/shard_map/ppermute | solution.py:280
  16.2 1.1 %collective-permute-done.5 = bf16[16,4224]{1,0:T(8,128)(2,1)S(1)} collective-permute-done((bf16[16,4224]{1,0:T(8,128)(2,1)S(1)}, bf16[16,4224]{1,0:T(8,128)(2,1)S(1)}, u32[]{:S(2)}, u32[]{:S(2)}) %collective-permute-start.5) | collective-permute-done | bytes 135200 | tf_op jit(solution)/shard_map/ppermute | solution.py:280
  17.4 5.7 %shard_map.95 = (bf16[4096,2048]{1,0:T(8,128)(2,1)S(1)}, f32[64,2048]{1,0:T(8,128)S(1)}, bf16[128,2048]{1,0:T(8,128)(2,1)S(1)}, f32[64,128]{1,0:T(8,128)S(1)}) custom-call(bf16[64,4224]{1,0:T(8,128)(2,1)S(1)} %pad_maximum_fusion.1.packed_ref.rows_one_ref.ids_one_ref, bf16[4096,2048]{1,0:T(8,128)(2,1)} %head.3, ...), custom_call_target="tpu_custom_call", output_to_operand_aliasing={{0}: (2, {})} | custom-call | flops 1073741824 | bytes 34095104 | tf_op jit(solution)/shard_map/pallas_call | solution.py:22
  23.2 3.7 %shard_map.96 = (f32[64,2048]{1,0:T(8,128)S(1)}, bf16[128,2048]{1,0:T(8,128)(2,1)S(1)}, f32[8,128]{1,0:T(8,128)S(1)}) custom-call(bf16[64,4224]{1,0:T(8,128)(2,1)S(1)} %bitcast.6, bf16[4096,2048]{1,0:T(8,128)(2,1)S(1)} %get-tuple-element.13.near_ref.head_ref, f32[64,128]{1,0:T(8,128)S(1)} %get-tuple-element.14.before_ref), custom_call_target="tpu_custom_call" | custom-call | flops 1073741824 | bytes 17350656 | tf_op jit(solution)/shard_map/pallas_call | solution.py:22
  26.9 0.8 %collective-permute-start.7 = (f32[8,128]{1,0:T(8,128)S(1)}, f32[8,128]{1,0:T(8,128)S(1)}, u32[]{:S(2)}, u32[]{:S(2)}) collective-permute-start(f32[8,128]{1,0:T(8,128)S(1)} %get-tuple-element.15.mine_ref), channel_id=1, source_target_pairs={{0,4},{1,5},{2,6},{3,7},{4,0},{5,1},{6,2},{7,3},{8,12},{9,13},{10,... | collective-permute-start | bytes 12296 | tf_op jit(solution)/shard_map/ppermute | solution.py:280
  27.8 2.5 %shard_map.100.refs_0_ = f32[256,2048]{1,0:T(8,128)S(1)} custom-call(bf16[128,2048]{1,0:T(8,128)(2,1)S(1)} %get-tuple-element.16.one_ref, bf16[128,2048]{1,0:T(8,128)(2,1)S(1)} %get-tuple-element.17.two_ref, bf16[4096,2048]{1,0:T(8,128)(2,1)S(1)} %get-tuple-element.13.near_ref.head_ref), custom_call_target="tpu_custom_call" | custom-call | flops 2147483648 | bytes 17825792 | tf_op jit(solution)/shard_map/pallas_call | solution.py:22
  30.3 1.2 %collective-permute-done.7.refs_0_ = f32[8,128]{1,0:T(8,128)S(1)} collective-permute-done((f32[8,128]{1,0:T(8,128)S(1)}, f32[8,128]{1,0:T(8,128)S(1)}, u32[]{:S(2)}, u32[]{:S(2)}) %collective-permute-start.7) | collective-permute-done | bytes 4128 | tf_op jit(solution)/shard_map/ppermute | solution.py:280
  31.6 1.6 %collective-permute-start.10 = (f32[8,128]{1,0:T(8,128)S(1)}, f32[8,128]{1,0:T(8,128)S(1)}, u32[]{:S(2)}, u32[]{:S(2)}) collective-permute-start(f32[8,128]{1,0:T(8,128)S(1)} %shard_map.97.mine_ref.refs_0_), channel_id=1, source_target_pairs={{0,3},{1,2},{2,1},{3,0},{4,7},{5,6},{6,5},{7,4},{8,11},{9,10},{10,... | collective-permute-start | bytes 12296 | tf_op jit(solution)/shard_map/ppermute | solution.py:280
  33.5 1.6 %collective-permute-start.8 = (f32[8,128]{1,0:T(8,128)S(1)}, f32[8,128]{1,0:T(8,128)S(1)}, u32[]{:S(2)}, u32[]{:S(2)}) collective-permute-start(f32[8,128]{1,0:T(8,128)S(1)} %shard_map.97.mine_ref.refs_0_), channel_id=1, source_target_pairs={{0,1},{1,0},{2,3},{3,2},{4,5},{5,4},{6,7},{7,6},{8,10},{9,11},{10,... | collective-permute-start | bytes 12296 | tf_op jit(solution)/shard_map/ppermute | solution.py:280
  35.1 2.5 %shard_map.101.refs_1_ = f32[256,2048]{1,0:T(8,128)S(1)} custom-call(bf16[128,2048]{1,0:T(8,128)(2,1)S(1)} %get-tuple-element.16.one_ref, bf16[128,2048]{1,0:T(8,128)(2,1)S(1)} %get-tuple-element.17.two_ref, bf16[4096,2048]{1,0:T(8,128)(2,1)S(1)} %get-tuple-element.13.near_ref.head_ref, f32[8,128]{1,0:T(8,128)S(1)} %shard_map.97.mine_ref.refs_0_), custom_call_target="tpu_custom_call" | custom-call | flops 2147483648 | bytes 17829888 | tf_op jit(solution)/shard_map/pallas_call | solution.py:22
  38.7 1.6 %collective-permute-start.14 = (f16[16,4096]{1,0:T(8,128)(2,1)S(1)}, f16[16,4096]{1,0:T(8,128)(2,1)S(1)}, u32[]{:S(2)}, u32[]{:S(2)}) collective-permute-start(f16[16,4096]{1,0:T(8,128)(2,1)S(1)} %get-tuple-element.25), channel_id=1, source_target_pairs={{0,3},{1,2},{2,1},{3,0},{4,7},{5,6},{6,5},{7,4},{8,11},{9,10},{10,... | collective-permute-start | bytes 393224 | tf_op jit(solution)/shard_map/ppermute | solution.py:280
  40.3 1.0 %collective-permute-start.16 = (f16[16,4096]{1,0:T(8,128)(2,1)S(1)}, f16[16,4096]{1,0:T(8,128)(2,1)S(1)}, u32[]{:S(2)}, u32[]{:S(2)}) collective-permute-start(f16[16,4096]{1,0:T(8,128)(2,1)S(1)} %get-tuple-element.26), channel_id=1, source_target_pairs={{0,2},{1,3},{2,0},{3,1},{4,6},{5,7},{6,4},{7,5},{8,9},{9,8},{10,11... | collective-permute-start | bytes 393224 | tf_op jit(solution)/shard_map/ppermute | solution.py:280
  41.3 1.0 %collective-permute-start.15 = (f16[16,4096]{1,0:T(8,128)(2,1)S(1)}, f16[16,4096]{1,0:T(8,128)(2,1)S(1)}, u32[]{:S(2)}, u32[]{:S(2)}) collective-permute-start(f16[16,4096]{1,0:T(8,128)(2,1)S(1)} %get-tuple-element.27), channel_id=1, source_target_pairs={{0,1},{1,0},{2,3},{3,2},{4,5},{5,4},{6,7},{7,6},{8,10},{9,11},{10,... | collective-permute-start | bytes 393224 | tf_op jit(solution)/shard_map/ppermute | solution.py:280
  42.3 1.6 %collective-permute-start.11 = (f16[16,4096]{1,0:T(8,128)(2,1)S(1)}, f16[16,4096]{1,0:T(8,128)(2,1)S(1)}, u32[]{:S(2)}, u32[]{:S(2)}) collective-permute-start(f16[16,4096]{1,0:T(8,128)(2,1)S(1)} %get-tuple-element.22), channel_id=1, source_target_pairs={{0,3},{1,2},{2,1},{3,0},{4,7},{5,6},{6,5},{7,4},{8,11},{9,10},{10,... | collective-permute-start | bytes 393224 | tf_op jit(solution)/shard_map/ppermute | solution.py:280
  43.9 1.0 %collective-permute-start.13 = (f16[16,4096]{1,0:T(8,128)(2,1)S(1)}, f16[16,4096]{1,0:T(8,128)(2,1)S(1)}, u32[]{:S(2)}, u32[]{:S(2)}) collective-permute-start(f16[16,4096]{1,0:T(8,128)(2,1)S(1)} %get-tuple-element.23), channel_id=1, source_target_pairs={{0,2},{1,3},{2,0},{3,1},{4,6},{5,7},{6,4},{7,5},{8,9},{9,8},{10,11... | collective-permute-start | bytes 393224 | tf_op jit(solution)/shard_map/ppermute | solution.py:280
  44.9 1.2 %collective-permute-done.14 = f16[16,4096]{1,0:T(8,128)(2,1)S(1)} collective-permute-done((f16[16,4096]{1,0:T(8,128)(2,1)S(1)}, f16[16,4096]{1,0:T(8,128)(2,1)S(1)}, u32[]{:S(2)}, u32[]{:S(2)}) %collective-permute-start.14) | collective-permute-done | bytes 131104 | tf_op jit(solution)/shard_map/ppermute | solution.py:280
  46.1 1.0 %collective-permute-start.12 = (f16[16,4096]{1,0:T(8,128)(2,1)S(1)}, f16[16,4096]{1,0:T(8,128)(2,1)S(1)}, u32[]{:S(2)}, u32[]{:S(2)}) collective-permute-start(f16[16,4096]{1,0:T(8,128)(2,1)S(1)} %get-tuple-element.24), channel_id=1, source_target_pairs={{0,1},{1,0},{2,3},{3,2},{4,5},{5,4},{6,7},{7,6},{8,10},{9,11},{10,... | collective-permute-start | bytes 393224 | tf_op jit(solution)/shard_map/ppermute | solution.py:280
  47.2 2.2 %collective-permute-done.16 = f16[16,4096]{1,0:T(8,128)(2,1)S(1)} collective-permute-done((f16[16,4096]{1,0:T(8,128)(2,1)S(1)}, f16[16,4096]{1,0:T(8,128)(2,1)S(1)}, u32[]{:S(2)}, u32[]{:S(2)}) %collective-permute-start.16) | collective-permute-done | bytes 131104 | tf_op jit(solution)/shard_map/ppermute | solution.py:280
  50.8 3.4 %shard_map.104 = (f32[128,2048]{1,0:T(8,128)}, f32[128,2048]{1,0:T(8,128)}) custom-call(bf16[64,4224]{1,0:T(8,128)(2,1)S(1)} %pad_maximum_fusion.1.packed_ref.rows_one_ref.ids_one_ref, bf16[64,4224]{1,0:T(8,128)(2,1)S(1)} %bitcast.7, bf16[64,4224]{1,0:T(8,128)(2,1)S(1)} %pad_maximum_fusion.1.packed_ref.rows_one_ref.ids_one_ref, ...), custom_call_target="tpu_custom_call" | custom-call | flops 67108864 | bytes 6291456 | tf_op jit(solution)/shard_map/pallas_call | solution.py:242
  54.2 2.2 %collective-permute-done.17 = f16[16,4096]{1,0:T(8,128)(2,1)S(1)} collective-permute-done((f16[16,4096]{1,0:T(8,128)(2,1)S(1)}, f16[16,4096]{1,0:T(8,128)(2,1)S(1)}, u32[]{:S(2)}, u32[]{:S(2)}) %collective-permute-start.17) | collective-permute-done | bytes 131104 | tf_op jit(solution)/shard_map/ppermute | solution.py:280
  (39 shorter events, 5.7 us)
Async XLA Ops:
  1.6 11.1 %collective-permute-start = (bf16[16,4224]{1,0:T(8,128)(2,1)S(1)}, bf16[16,4224]{1,0:T(8,128)(2,1)S(1)}, u32[]{:S(2)}, u32[]{:S(2)}) collective-permute-start(bf16[16,4224]{1,0:T(8,128)(2,1)S(1)} %shard_map.93), channel_id=1, source_target_pairs={{0,4},{1,5},{2,6},{3,7},{4,0},{5,1},{6,2},{7,3},{8,12},{9,13},{10,... | collective-permute-start | bytes 405512 | tf_op jit(solution)/shard_map/ppermute | solution.py:280
  5.7 10.1 %collective-permute-start.6 = (bf16[16,4224]{1,0:T(8,128)(2,1)S(1)}, bf16[16,4224]{1,0:T(8,128)(2,1)S(1)}, u32[]{:S(2)}, u32[]{:S(2)}) collective-permute-start(bf16[16,4224]{1,0:T(8,128)(2,1)S(1)} %shard_map.93), channel_id=1, source_target_pairs={{0,3},{1,2},{2,1},{3,0},{4,7},{5,6},{6,5},{7,4},{8,11},{9,10},{10,... | collective-permute-start | bytes 405512 | tf_op jit(solution)/shard_map/ppermute | solution.py:280
  8.2 9.2 %collective-permute-start.5 = (bf16[16,4224]{1,0:T(8,128)(2,1)S(1)}, bf16[16,4224]{1,0:T(8,128)(2,1)S(1)}, u32[]{:S(2)}, u32[]{:S(2)}) collective-permute-start(bf16[16,4224]{1,0:T(8,128)(2,1)S(1)} %shard_map.93), channel_id=1, source_target_pairs={{0,2},{1,3},{2,0},{3,1},{4,6},{5,7},{6,4},{7,5},{8,9},{9,8},{10,11... | collective-permute-start | bytes 405512 | tf_op jit(solution)/shard_map/ppermute | solution.py:280
  8.6 8.7 %collective-permute-start.4 = (bf16[16,4224]{1,0:T(8,128)(2,1)S(1)}, bf16[16,4224]{1,0:T(8,128)(2,1)S(1)}, u32[]{:S(2)}, u32[]{:S(2)}) collective-permute-start(bf16[16,4224]{1,0:T(8,128)(2,1)S(1)} %shard_map.93), channel_id=1, source_target_pairs={{0,1},{1,0},{2,3},{3,2},{4,5},{5,4},{6,7},{7,6},{8,10},{9,11},{10,... | collective-permute-start | bytes 405512 | tf_op jit(solution)/shard_map/ppermute | solution.py:280
  12.7 10.4 %collective-permute-start.3 = (bf16[16,4224]{1,0:T(8,128)(2,1)S(1)}, bf16[16,4224]{1,0:T(8,128)(2,1)S(1)}, u32[]{:S(2)}, u32[]{:S(2)}) collective-permute-start(bf16[16,4224]{1,0:T(8,128)(2,1)S(1)} %collective-permute-done), channel_id=1, source_target_pairs={{0,3},{1,2},{2,1},{3,0},{4,7},{5,6},{6,5},{7,4},{8,11},{9,10},{10,... | collective-permute-start | bytes 405512 | tf_op jit(solution)/shard_map/ppermute | solution.py:280
  15.3 7.8 %collective-permute-start.2 = (bf16[16,4224]{1,0:T(8,128)(2,1)S(1)}, bf16[16,4224]{1,0:T(8,128)(2,1)S(1)}, u32[]{:S(2)}, u32[]{:S(2)}) collective-permute-start(bf16[16,4224]{1,0:T(8,128)(2,1)S(1)} %collective-permute-done), channel_id=1, source_target_pairs={{0,2},{1,3},{2,0},{3,1},{4,6},{5,7},{6,4},{7,5},{8,9},{9,8},{10,11... | collective-permute-start | bytes 405512 | tf_op jit(solution)/shard_map/ppermute | solution.py:280
  15.7 7.4 %collective-permute-start.1 = (bf16[16,4224]{1,0:T(8,128)(2,1)S(1)}, bf16[16,4224]{1,0:T(8,128)(2,1)S(1)}, u32[]{:S(2)}, u32[]{:S(2)}) collective-permute-start(bf16[16,4224]{1,0:T(8,128)(2,1)S(1)} %collective-permute-done), channel_id=1, source_target_pairs={{0,1},{1,0},{2,3},{3,2},{4,5},{5,4},{6,7},{7,6},{8,10},{9,11},{10,... | collective-permute-start | bytes 405512 | tf_op jit(solution)/shard_map/ppermute | solution.py:280
  26.9 4.5 %collective-permute-start.7 = (f32[8,128]{1,0:T(8,128)S(1)}, f32[8,128]{1,0:T(8,128)S(1)}, u32[]{:S(2)}, u32[]{:S(2)}) collective-permute-start(f32[8,128]{1,0:T(8,128)S(1)} %get-tuple-element.15.mine_ref), channel_id=1, source_target_pairs={{0,4},{1,5},{2,6},{3,7},{4,0},{5,1},{6,2},{7,3},{8,12},{9,13},{10,... | collective-permute-start | bytes 12296 | tf_op jit(solution)/shard_map/ppermute | solution.py:280
  31.6 6.1 %collective-permute-start.10 = (f32[8,128]{1,0:T(8,128)S(1)}, f32[8,128]{1,0:T(8,128)S(1)}, u32[]{:S(2)}, u32[]{:S(2)}) collective-permute-start(f32[8,128]{1,0:T(8,128)S(1)} %shard_map.97.mine_ref.refs_0_), channel_id=1, source_target_pairs={{0,3},{1,2},{2,1},{3,0},{4,7},{5,6},{6,5},{7,4},{8,11},{9,10},{10,... | collective-permute-start | bytes 12296 | tf_op jit(solution)/shard_map/ppermute | solution.py:280
  33.2 4.5 %collective-permute-start.9 = (f32[8,128]{1,0:T(8,128)S(1)}, f32[8,128]{1,0:T(8,128)S(1)}, u32[]{:S(2)}, u32[]{:S(2)}) collective-permute-start(f32[8,128]{1,0:T(8,128)S(1)} %shard_map.97.mine_ref.refs_0_), channel_id=1, source_target_pairs={{0,2},{1,3},{2,0},{3,1},{4,6},{5,7},{6,4},{7,5},{8,9},{9,8},{10,11... | collective-permute-start | bytes 12296 | tf_op jit(solution)/shard_map/ppermute | solution.py:280
  33.5 4.2 %collective-permute-start.8 = (f32[8,128]{1,0:T(8,128)S(1)}, f32[8,128]{1,0:T(8,128)S(1)}, u32[]{:S(2)}, u32[]{:S(2)}) collective-permute-start(f32[8,128]{1,0:T(8,128)S(1)} %shard_map.97.mine_ref.refs_0_), channel_id=1, source_target_pairs={{0,1},{1,0},{2,3},{3,2},{4,5},{5,4},{6,7},{7,6},{8,10},{9,11},{10,... | collective-permute-start | bytes 12296 | tf_op jit(solution)/shard_map/ppermute | solution.py:280
  38.5 12.3 %copy-start.2 = (f32[128,2048]{1,0:T(8,128)S(1)}, f32[128,2048]{1,0:T(8,128)}, u32[]{:S(2)}) copy-start(f32[128,2048]{1,0:T(8,128)} %peer_ref.1) | copy-start | bytes 3145732
  38.6 12.2 %copy-start = (f32[128,2048]{1,0:T(8,128)S(1)}, f32[128,2048]{1,0:T(8,128)}, u32[]{:S(2)}) copy-start(f32[128,2048]{1,0:T(8,128)} %global_ref.1) | copy-start | bytes 3145732
  38.6 12.2 %copy-start.1 = (f32[128,2048]{1,0:T(8,128)S(1)}, f32[128,2048]{1,0:T(8,128)}, u32[]{:S(2)}) copy-start(f32[128,2048]{1,0:T(8,128)} %momentum_ref.1) | copy-start | bytes 3145732
  38.7 7.4 %collective-permute-start.14 = (f16[16,4096]{1,0:T(8,128)(2,1)S(1)}, f16[16,4096]{1,0:T(8,128)(2,1)S(1)}, u32[]{:S(2)}, u32[]{:S(2)}) collective-permute-start(f16[16,4096]{1,0:T(8,128)(2,1)S(1)} %get-tuple-element.25), channel_id=1, source_target_pairs={{0,3},{1,2},{2,1},{3,0},{4,7},{5,6},{6,5},{7,4},{8,11},{9,10},{10,... | collective-permute-start | bytes 393224 | tf_op jit(solution)/shard_map/ppermute | solution.py:280
  40.3 9.1 %collective-permute-start.16 = (f16[16,4096]{1,0:T(8,128)(2,1)S(1)}, f16[16,4096]{1,0:T(8,128)(2,1)S(1)}, u32[]{:S(2)}, u32[]{:S(2)}) collective-permute-start(f16[16,4096]{1,0:T(8,128)(2,1)S(1)} %get-tuple-element.26), channel_id=1, source_target_pairs={{0,2},{1,3},{2,0},{3,1},{4,6},{5,7},{6,4},{7,5},{8,9},{9,8},{10,11... | collective-permute-start | bytes 393224 | tf_op jit(solution)/shard_map/ppermute | solution.py:280
  41.3 8.1 %collective-permute-start.15 = (f16[16,4096]{1,0:T(8,128)(2,1)S(1)}, f16[16,4096]{1,0:T(8,128)(2,1)S(1)}, u32[]{:S(2)}, u32[]{:S(2)}) collective-permute-start(f16[16,4096]{1,0:T(8,128)(2,1)S(1)} %get-tuple-element.27), channel_id=1, source_target_pairs={{0,1},{1,0},{2,3},{3,2},{4,5},{5,4},{6,7},{7,6},{8,10},{9,11},{10,... | collective-permute-start | bytes 393224 | tf_op jit(solution)/shard_map/ppermute | solution.py:280
  42.3 11.9 %collective-permute-start.11 = (f16[16,4096]{1,0:T(8,128)(2,1)S(1)}, f16[16,4096]{1,0:T(8,128)(2,1)S(1)}, u32[]{:S(2)}, u32[]{:S(2)}) collective-permute-start(f16[16,4096]{1,0:T(8,128)(2,1)S(1)} %get-tuple-element.22), channel_id=1, source_target_pairs={{0,3},{1,2},{2,1},{3,0},{4,7},{5,6},{6,5},{7,4},{8,11},{9,10},{10,... | collective-permute-start | bytes 393224 | tf_op jit(solution)/shard_map/ppermute | solution.py:280
  43.9 10.3 %collective-permute-start.13 = (f16[16,4096]{1,0:T(8,128)(2,1)S(1)}, f16[16,4096]{1,0:T(8,128)(2,1)S(1)}, u32[]{:S(2)}, u32[]{:S(2)}) collective-permute-start(f16[16,4096]{1,0:T(8,128)(2,1)S(1)} %get-tuple-element.23), channel_id=1, source_target_pairs={{0,2},{1,3},{2,0},{3,1},{4,6},{5,7},{6,4},{7,5},{8,9},{9,8},{10,11... | collective-permute-start | bytes 393224 | tf_op jit(solution)/shard_map/ppermute | solution.py:280
  46.1 8.1 %collective-permute-start.12 = (f16[16,4096]{1,0:T(8,128)(2,1)S(1)}, f16[16,4096]{1,0:T(8,128)(2,1)S(1)}, u32[]{:S(2)}, u32[]{:S(2)}) collective-permute-start(f16[16,4096]{1,0:T(8,128)(2,1)S(1)} %get-tuple-element.24), channel_id=1, source_target_pairs={{0,1},{1,0},{2,3},{3,2},{4,5},{5,4},{6,7},{7,6},{8,10},{9,11},{10,... | collective-permute-start | bytes 393224 | tf_op jit(solution)/shard_map/ppermute | solution.py:280
  49.5 7.0 %collective-permute-start.17 = (f16[16,4096]{1,0:T(8,128)(2,1)S(1)}, f16[16,4096]{1,0:T(8,128)(2,1)S(1)}, u32[]{:S(2)}, u32[]{:S(2)}) collective-permute-start(f16[16,4096]{1,0:T(8,128)(2,1)S(1)} %fusion.2), channel_id=1, source_target_pairs={{0,4},{1,5},{2,6},{3,7},{4,0},{5,1},{6,2},{7,3},{8,12},{9,13},{10,... | collective-permute-start | bytes 393224 | tf_op jit(solution)/shard_map/ppermute | solution.py:280

commit v17 on v9

--- a/solution.py
+++ b/solution.py
@@ -83,7 +83,7 @@
 
 
 def shared_order(value, members):
-    me = lax.axis_index(AXIS)
+    me = my_label()
     step = 1
     while step < members:
         swapped = swap_blocks(value, value.shape[1] // members * step)
@@ -138,7 +138,7 @@
 def merge_kernel(steps, members, mine_ref, *refs):
     *other_refs, out_ref = refs
     block = mine_ref.shape[1] // members
-    me = lax.axis_index(AXIS)
+    me = my_label()
     groups = [mine_ref[...]]
     for step, other_ref in zip(steps, other_refs):
         other, bit = other_ref[...], 1
@@ -161,7 +161,7 @@
 
 def grad_kernel(first, one_ref, two_ref, near_ref, *refs):
     terms_ref = refs[-1]
-    tile = 1024
+    tile = min(terms_ref.shape[1], 2**19 // (one_ref.shape[0] + two_ref.shape[0]))
     both = jnp.concatenate([one_ref[...], two_ref[...]], axis=0)
     for place in range(0, terms_ref.shape[1], tile):
         turned = lax.dot_general(
@@ -244,8 +244,22 @@
     )
 
 
+def turned(label):
+    return label // 4 * 4 + label % 2 * 2 + label // 2 % 2
+
+
+def my_label():
+    me = lax.axis_index(AXIS)
+    return jnp.where(lax.rem(lax.axis_index("outer"), 2) == 1, turned(me), me)
+
+
 def swap(value, step):
-    return lax.ppermute(value, AXIS, [(i, i ^ step) for i in range(lax.axis_size(AXIS))])
+    members = lax.axis_size(AXIS)
+    pairs = []
+    for outer in range(lax.axis_size("outer")):
+        flip = turned(step) if outer % 2 else step
+        pairs += [(outer * members + i, outer * members + (i ^ flip)) for i in range(members)]
+    return lax.ppermute(value, ("outer", AXIS), pairs)
 
 
 def far_steps():

time: 56.8 us -> 57.4 us (1.011)
  waiting for transfers between devices: 5.95 us -> 7.46 us
  starting transfers between devices: 23.7 us -> 23.1 us
    ppermute x18, waiting for transfers between devices: 5.95 us -> 7.46 us  [swap(): return lax.ppermute(value, ('outer', AXIS), pairs)]
    ppermute x18, starting transfers between devices: 23.7 us -> 23.1 us  [swap(): return lax.ppermute(value, ('outer', AXIS), pairs)]
  transfers between devices with their start and end apart: 18 -> 18, of which waited for: 5 -> 4; matrix products, arithmetic and copies ran while one was open for 2% -> 2% of each run, Pallas kernels for 33% -> 32%
where the time goes in v17:
time: 57.4 us; the launch traced here: 57.2 us
  Pallas kernels  23.9 us (42%)
  starting transfers between devices  23.1 us (40%)
  waiting for transfers between devices  7.46 us (13%)
  other arithmetic  1.07 us (2%)
  between operations  0.82 us (1%)
  local copies, waits for them, and re-layouts  0.79 us (1%)
    ppermute x18, starting transfers between devices, swap(): return lax.ppermute(value, ('outer', AXIS), pairs)  23.1 us
    pallas_call x11, Pallas kernels, call(): pl.pallas_call(kernel, out_shape=outs, in_specs=[pl.BlockSpec(memory_spac...  20.6 us
    ppermute x18, waiting for transfers between devices, swap(): return lax.ppermute(value, ('outer', AXIS), pairs)  7.46 us
    pallas_call x1, Pallas kernels, frag_update(): pl.pallas_call(frag_kernel, grid=(width // TILE,), out_shape=[jax.ShapeDt...  3.36 us
  transfers between devices with their start and end apart: 18, of which 4 were waited for; matrix products, arithmetic and copies ran while one was open for 2% of the time, Pallas kernels for 32%

profile of v17, /device:TPU:0, one launch (start us, length us, event | category | flops | bytes accessed | tf_op | source)
XLA Modules:
  0.0 57.2 jit_solution(15884141995860361374)
XLA Ops:
  1.6 4.1 %collective-permute-start = (bf16[16,4224]{1,0:T(8,128)(2,1)S(1)}, bf16[16,4224]{1,0:T(8,128)(2,1)S(1)}, u32[]{:S(2)}, u32[]{:S(2)}) collective-permute-start(bf16[16,4224]{1,0:T(8,128)(2,1)S(1)} %shard_map.93), channel_id=1, source_target_pairs={{0,4},{1,5},{2,6},{3,7},{4,0},{5,1},{6,2},{7,3},{8,12},{9,13},{10,... | collective-permute-start | bytes 405512 | tf_op jit(solution)/shard_map/ppermute | solution.py:262
  5.7 1.5 %collective-permute-start.4 = (bf16[16,4224]{1,0:T(8,128)(2,1)S(1)}, bf16[16,4224]{1,0:T(8,128)(2,1)S(1)}, u32[]{:S(2)}, u32[]{:S(2)}) collective-permute-start(bf16[16,4224]{1,0:T(8,128)(2,1)S(1)} %shard_map.93), channel_id=1, source_target_pairs={{0,1},{1,0},{2,3},{3,2},{4,5},{5,4},{6,7},{7,6},{8,10},{9,11},{10,... | collective-permute-start | bytes 405512 | tf_op jit(solution)/shard_map/ppermute | solution.py:262
  7.2 1.6 %collective-permute-start.5 = (bf16[16,4224]{1,0:T(8,128)(2,1)S(1)}, bf16[16,4224]{1,0:T(8,128)(2,1)S(1)}, u32[]{:S(2)}, u32[]{:S(2)}) collective-permute-start(bf16[16,4224]{1,0:T(8,128)(2,1)S(1)} %shard_map.93), channel_id=1, source_target_pairs={{0,2},{1,3},{2,0},{3,1},{4,6},{5,7},{6,4},{7,5},{8,9},{9,8},{10,11... | collective-permute-start | bytes 405512 | tf_op jit(solution)/shard_map/ppermute | solution.py:262
  9.2 5.9 %shard_map.94.near_ref.head_ref = bf16[4096,2048]{1,0:T(8,128)(2,1)S(1)} custom-call(bf16[4096,2048]{1,0:T(8,128)(2,1)} %source.1), custom_call_target="tpu_custom_call" | custom-call | bytes 16777216 | tf_op jit(solution)/shard_map/pallas_call | solution.py:22
  15.1 1.6 %collective-permute-start.1 = (bf16[16,4224]{1,0:T(8,128)(2,1)S(1)}, bf16[16,4224]{1,0:T(8,128)(2,1)S(1)}, u32[]{:S(2)}, u32[]{:S(2)}) collective-permute-start(bf16[16,4224]{1,0:T(8,128)(2,1)S(1)} %collective-permute-done), channel_id=1, source_target_pairs={{0,1},{1,0},{2,3},{3,2},{4,5},{5,4},{6,7},{7,6},{8,10},{9,11},{10,... | collective-permute-start | bytes 405512 | tf_op jit(solution)/shard_map/ppermute | solution.py:262
  16.7 1.6 %collective-permute-start.2 = (bf16[16,4224]{1,0:T(8,128)(2,1)S(1)}, bf16[16,4224]{1,0:T(8,128)(2,1)S(1)}, u32[]{:S(2)}, u32[]{:S(2)}) collective-permute-start(bf16[16,4224]{1,0:T(8,128)(2,1)S(1)} %collective-permute-done), channel_id=1, source_target_pairs={{0,2},{1,3},{2,0},{3,1},{4,6},{5,7},{6,4},{7,5},{8,9},{9,8},{10,11... | collective-permute-start | bytes 405512 | tf_op jit(solution)/shard_map/ppermute | solution.py:262
  18.8 3.8 %shard_map.95 = (f32[64,2048]{1,0:T(8,128)S(1)}, bf16[128,2048]{1,0:T(8,128)(2,1)S(1)}, f32[64,128]{1,0:T(8,128)S(1)}) custom-call(bf16[64,4224]{1,0:T(8,128)(2,1)S(1)} %pad_maximum_fusion.1.rows_ref, bf16[4096,2048]{1,0:T(8,128)(2,1)S(1)} %shard_map.94.near_ref.head_ref), custom_call_target="tpu_custom_call" | custom-call | flops 1073741824 | bytes 17317888 | tf_op jit(solution)/shard_map/pallas_call | solution.py:22
  22.5 1.7 %collective-permute-done.3 = bf16[16,4224]{1,0:T(8,128)(2,1)S(1)} collective-permute-done((bf16[16,4224]{1,0:T(8,128)(2,1)S(1)}, bf16[16,4224]{1,0:T(8,128)(2,1)S(1)}, u32[]{:S(2)}, u32[]{:S(2)}) %collective-permute-start.3) | collective-permute-done | bytes 135200 | tf_op jit(solution)/shard_map/ppermute | solution.py:262
  24.3 3.8 %shard_map.96 = (f32[64,2048]{1,0:T(8,128)S(1)}, bf16[128,2048]{1,0:T(8,128)(2,1)S(1)}, f32[8,128]{1,0:T(8,128)S(1)}) custom-call(bf16[64,4224]{1,0:T(8,128)(2,1)S(1)} %bitcast.6, bf16[4096,2048]{1,0:T(8,128)(2,1)S(1)} %shard_map.94.near_ref.head_ref, f32[64,128]{1,0:T(8,128)S(1)} %get-tuple-element.12.refs_0_), custom_call_target="tpu_custom_call" | custom-call | flops 1073741824 | bytes 17350656 | tf_op jit(solution)/shard_map/pallas_call | solution.py:22
  28.5 2.5 %shard_map.100.refs_0_ = f32[256,2048]{1,0:T(8,128)S(1)} custom-call(bf16[128,2048]{1,0:T(8,128)(2,1)S(1)} %get-tuple-element.14.one_ref, bf16[128,2048]{1,0:T(8,128)(2,1)S(1)} %get-tuple-element.15.two_ref, bf16[4096,2048]{1,0:T(8,128)(2,1)S(1)} %shard_map.94.near_ref.head_ref), custom_call_target="tpu_custom_call" | custom-call | flops 2147483648 | bytes 17825792 | tf_op jit(solution)/shard_map/pallas_call | solution.py:22
  31.0 1.6 %collective-permute-done.7.refs_0_ = f32[8,128]{1,0:T(8,128)S(1)} collective-permute-done((f32[8,128]{1,0:T(8,128)S(1)}, f32[8,128]{1,0:T(8,128)S(1)}, u32[]{:S(2)}, u32[]{:S(2)}) %collective-permute-start.7) | collective-permute-done | bytes 4128 | tf_op jit(solution)/shard_map/ppermute | solution.py:262
  32.7 1.4 %collective-permute-start.10 = (f32[8,128]{1,0:T(8,128)S(1)}, f32[8,128]{1,0:T(8,128)S(1)}, u32[]{:S(2)}, u32[]{:S(2)}) collective-permute-start(f32[8,128]{1,0:T(8,128)S(1)} %shard_map.97.mine_ref.refs_0_), channel_id=1, source_target_pairs={{0,3},{1,2},{2,1},{3,0},{4,7},{5,6},{6,5},{7,4},{8,11},{9,10},{10,... | collective-permute-start | bytes 12296 | tf_op jit(solution)/shard_map/ppermute | solution.py:262
  34.9 1.4 %collective-permute-start.9 = (f32[8,128]{1,0:T(8,128)S(1)}, f32[8,128]{1,0:T(8,128)S(1)}, u32[]{:S(2)}, u32[]{:S(2)}) collective-permute-start(f32[8,128]{1,0:T(8,128)S(1)} %shard_map.97.mine_ref.refs_0_), channel_id=1, source_target_pairs={{0,2},{1,3},{2,0},{3,1},{4,6},{5,7},{6,4},{7,5},{8,9},{9,8},{10,11... | collective-permute-start | bytes 12296 | tf_op jit(solution)/shard_map/ppermute | solution.py:262
  36.3 2.5 %shard_map.101.refs_1_ = f32[256,2048]{1,0:T(8,128)S(1)} custom-call(bf16[128,2048]{1,0:T(8,128)(2,1)S(1)} %get-tuple-element.14.one_ref, bf16[128,2048]{1,0:T(8,128)(2,1)S(1)} %get-tuple-element.15.two_ref, bf16[4096,2048]{1,0:T(8,128)(2,1)S(1)} %shard_map.94.near_ref.head_ref, f32[8,128]{1,0:T(8,128)S(1)} %shard_map.97.mine_ref.refs_0_), custom_call_target="tpu_custom_call" | custom-call | flops 2147483648 | bytes 17829888 | tf_op jit(solution)/shard_map/pallas_call | solution.py:22
  39.8 1.4 %collective-permute-start.14 = (f16[16,4096]{1,0:T(8,128)(2,1)S(1)}, f16[16,4096]{1,0:T(8,128)(2,1)S(1)}, u32[]{:S(2)}, u32[]{:S(2)}) collective-permute-start(f16[16,4096]{1,0:T(8,128)(2,1)S(1)} %get-tuple-element.23), channel_id=1, source_target_pairs={{0,3},{1,2},{2,1},{3,0},{4,7},{5,6},{6,5},{7,4},{8,11},{9,10},{10,... | collective-permute-start | bytes 393224 | tf_op jit(solution)/shard_map/ppermute | solution.py:262
  41.2 1.0 %collective-permute-start.15 = (f16[16,4096]{1,0:T(8,128)(2,1)S(1)}, f16[16,4096]{1,0:T(8,128)(2,1)S(1)}, u32[]{:S(2)}, u32[]{:S(2)}) collective-permute-start(f16[16,4096]{1,0:T(8,128)(2,1)S(1)} %get-tuple-element.25), channel_id=1, source_target_pairs={{0,2},{1,3},{2,0},{3,1},{4,6},{5,7},{6,4},{7,5},{8,9},{9,8},{10,11... | collective-permute-start | bytes 393224 | tf_op jit(solution)/shard_map/ppermute | solution.py:262
  42.2 1.1 %collective-permute-start.16 = (f16[16,4096]{1,0:T(8,128)(2,1)S(1)}, f16[16,4096]{1,0:T(8,128)(2,1)S(1)}, u32[]{:S(2)}, u32[]{:S(2)}) collective-permute-start(f16[16,4096]{1,0:T(8,128)(2,1)S(1)} %get-tuple-element.24), channel_id=1, source_target_pairs={{0,1},{1,0},{2,3},{3,2},{4,5},{5,4},{6,7},{7,6},{8,10},{9,11},{10,... | collective-permute-start | bytes 393224 | tf_op jit(solution)/shard_map/ppermute | solution.py:262
  43.5 1.4 %collective-permute-start.11 = (f16[16,4096]{1,0:T(8,128)(2,1)S(1)}, f16[16,4096]{1,0:T(8,128)(2,1)S(1)}, u32[]{:S(2)}, u32[]{:S(2)}) collective-permute-start(f16[16,4096]{1,0:T(8,128)(2,1)S(1)} %get-tuple-element.20), channel_id=1, source_target_pairs={{0,3},{1,2},{2,1},{3,0},{4,7},{5,6},{6,5},{7,4},{8,11},{9,10},{10,... | collective-permute-start | bytes 393224 | tf_op jit(solution)/shard_map/ppermute | solution.py:262
  44.9 1.0 %collective-permute-start.12 = (f16[16,4096]{1,0:T(8,128)(2,1)S(1)}, f16[16,4096]{1,0:T(8,128)(2,1)S(1)}, u32[]{:S(2)}, u32[]{:S(2)}) collective-permute-start(f16[16,4096]{1,0:T(8,128)(2,1)S(1)} %get-tuple-element.22), channel_id=1, source_target_pairs={{0,2},{1,3},{2,0},{3,1},{4,6},{5,7},{6,4},{7,5},{8,9},{9,8},{10,11... | collective-permute-start | bytes 393224 | tf_op jit(solution)/shard_map/ppermute | solution.py:262
  46.0 2.0 %collective-permute-done.14 = f16[16,4096]{1,0:T(8,128)(2,1)S(1)} collective-permute-done((f16[16,4096]{1,0:T(8,128)(2,1)S(1)}, f16[16,4096]{1,0:T(8,128)(2,1)S(1)}, u32[]{:S(2)}, u32[]{:S(2)}) %collective-permute-start.14) | collective-permute-done | bytes 131104 | tf_op jit(solution)/shard_map/ppermute | solution.py:262
  48.0 1.1 %collective-permute-start.13 = (f16[16,4096]{1,0:T(8,128)(2,1)S(1)}, f16[16,4096]{1,0:T(8,128)(2,1)S(1)}, u32[]{:S(2)}, u32[]{:S(2)}) collective-permute-start(f16[16,4096]{1,0:T(8,128)(2,1)S(1)} %get-tuple-element.21), channel_id=1, source_target_pairs={{0,1},{1,0},{2,3},{3,2},{4,5},{5,4},{6,7},{7,6},{8,10},{9,11},{10,... | collective-permute-start | bytes 393224 | tf_op jit(solution)/shard_map/ppermute | solution.py:262
  49.1 1.0 %collective-permute-start.17 = (f16[16,4096]{1,0:T(8,128)(2,1)S(1)}, f16[16,4096]{1,0:T(8,128)(2,1)S(1)}, u32[]{:S(2)}, u32[]{:S(2)}) collective-permute-start(f16[16,4096]{1,0:T(8,128)(2,1)S(1)} %fusion.2), channel_id=1, source_target_pairs={{0,4},{1,5},{2,6},{3,7},{4,0},{5,1},{6,2},{7,3},{8,12},{9,13},{10,... | collective-permute-start | bytes 393224 | tf_op jit(solution)/shard_map/ppermute | solution.py:262
  51.0 3.4 %shard_map.104 = (f32[128,2048]{1,0:T(8,128)}, f32[128,2048]{1,0:T(8,128)}) custom-call(bf16[128,4224]{1,0:T(8,128)(2,1)S(1)} %constant_dynamic-update-slice_fusion.rows_ref.digits_ref, bf16[128,4224]{1,0:T(8,128)(2,1)S(1)} %constant_dynamic-update-slice_fusion.rows_ref.digits_ref, f32[8,128]{1,0:T(8,128)S(1)} %shard_map.98.lines_ref, ...), custom_call_target="tpu_custom_call" | custom-call | flops 67108864 | bytes 6291456 | tf_op jit(solution)/shard_map/pallas_call | solution.py:224
  54.4 2.1 %collective-permute-done.17 = f16[16,4096]{1,0:T(8,128)(2,1)S(1)} collective-permute-done((f16[16,4096]{1,0:T(8,128)(2,1)S(1)}, f16[16,4096]{1,0:T(8,128)(2,1)S(1)}, u32[]{:S(2)}, u32[]{:S(2)}) %collective-permute-start.17) | collective-permute-done | bytes 131104 | tf_op jit(solution)/shard_map/ppermute | solution.py:262
  (44 shorter events, 5.8 us)
Async XLA Ops:
  1.6 13.5 %collective-permute-start = (bf16[16,4224]{1,0:T(8,128)(2,1)S(1)}, bf16[16,4224]{1,0:T(8,128)(2,1)S(1)}, u32[]{:S(2)}, u32[]{:S(2)}) collective-permute-start(bf16[16,4224]{1,0:T(8,128)(2,1)S(1)} %shard_map.93), channel_id=1, source_target_pairs={{0,4},{1,5},{2,6},{3,7},{4,0},{5,1},{6,2},{7,3},{8,12},{9,13},{10,... | collective-permute-start | bytes 405512 | tf_op jit(solution)/shard_map/ppermute | solution.py:262
  5.7 12.6 %collective-permute-start.4 = (bf16[16,4224]{1,0:T(8,128)(2,1)S(1)}, bf16[16,4224]{1,0:T(8,128)(2,1)S(1)}, u32[]{:S(2)}, u32[]{:S(2)}) collective-permute-start(bf16[16,4224]{1,0:T(8,128)(2,1)S(1)} %shard_map.93), channel_id=1, source_target_pairs={{0,1},{1,0},{2,3},{3,2},{4,5},{5,4},{6,7},{7,6},{8,10},{9,11},{10,... | collective-permute-start | bytes 405512 | tf_op jit(solution)/shard_map/ppermute | solution.py:262
  7.2 11.5 %collective-permute-start.5 = (bf16[16,4224]{1,0:T(8,128)(2,1)S(1)}, bf16[16,4224]{1,0:T(8,128)(2,1)S(1)}, u32[]{:S(2)}, u32[]{:S(2)}) collective-permute-start(bf16[16,4224]{1,0:T(8,128)(2,1)S(1)} %shard_map.93), channel_id=1, source_target_pairs={{0,2},{1,3},{2,0},{3,1},{4,6},{5,7},{6,4},{7,5},{8,9},{9,8},{10,11... | collective-permute-start | bytes 405512 | tf_op jit(solution)/shard_map/ppermute | solution.py:262
  8.8 9.9 %collective-permute-start.6 = (bf16[16,4224]{1,0:T(8,128)(2,1)S(1)}, bf16[16,4224]{1,0:T(8,128)(2,1)S(1)}, u32[]{:S(2)}, u32[]{:S(2)}) collective-permute-start(bf16[16,4224]{1,0:T(8,128)(2,1)S(1)} %shard_map.93), channel_id=1, source_target_pairs={{0,3},{1,2},{2,1},{3,0},{4,7},{5,6},{6,5},{7,4},{8,11},{9,10},{10,... | collective-permute-start | bytes 405512 | tf_op jit(solution)/shard_map/ppermute | solution.py:262
  15.1 7.4 %collective-permute-start.1 = (bf16[16,4224]{1,0:T(8,128)(2,1)S(1)}, bf16[16,4224]{1,0:T(8,128)(2,1)S(1)}, u32[]{:S(2)}, u32[]{:S(2)}) collective-permute-start(bf16[16,4224]{1,0:T(8,128)(2,1)S(1)} %collective-permute-done), channel_id=1, source_target_pairs={{0,1},{1,0},{2,3},{3,2},{4,5},{5,4},{6,7},{7,6},{8,10},{9,11},{10,... | collective-permute-start | bytes 405512 | tf_op jit(solution)/shard_map/ppermute | solution.py:262
  16.7 5.9 %collective-permute-start.2 = (bf16[16,4224]{1,0:T(8,128)(2,1)S(1)}, bf16[16,4224]{1,0:T(8,128)(2,1)S(1)}, u32[]{:S(2)}, u32[]{:S(2)}) collective-permute-start(bf16[16,4224]{1,0:T(8,128)(2,1)S(1)} %collective-permute-done), channel_id=1, source_target_pairs={{0,2},{1,3},{2,0},{3,1},{4,6},{5,7},{6,4},{7,5},{8,9},{9,8},{10,11... | collective-permute-start | bytes 405512 | tf_op jit(solution)/shard_map/ppermute | solution.py:262
  18.2 6.0 %collective-permute-start.3 = (bf16[16,4224]{1,0:T(8,128)(2,1)S(1)}, bf16[16,4224]{1,0:T(8,128)(2,1)S(1)}, u32[]{:S(2)}, u32[]{:S(2)}) collective-permute-start(bf16[16,4224]{1,0:T(8,128)(2,1)S(1)} %collective-permute-done), channel_id=1, source_target_pairs={{0,3},{1,2},{2,1},{3,0},{4,7},{5,6},{6,5},{7,4},{8,11},{9,10},{10,... | collective-permute-start | bytes 405512 | tf_op jit(solution)/shard_map/ppermute | solution.py:262
  28.1 4.6 %collective-permute-start.7 = (f32[8,128]{1,0:T(8,128)S(1)}, f32[8,128]{1,0:T(8,128)S(1)}, u32[]{:S(2)}, u32[]{:S(2)}) collective-permute-start(f32[8,128]{1,0:T(8,128)S(1)} %get-tuple-element.13.mine_ref), channel_id=1, source_target_pairs={{0,4},{1,5},{2,6},{3,7},{4,0},{5,1},{6,2},{7,3},{8,12},{9,13},{10,... | collective-permute-start | bytes 12296 | tf_op jit(solution)/shard_map/ppermute | solution.py:262
  32.7 6.1 %collective-permute-start.10 = (f32[8,128]{1,0:T(8,128)S(1)}, f32[8,128]{1,0:T(8,128)S(1)}, u32[]{:S(2)}, u32[]{:S(2)}) collective-permute-start(f32[8,128]{1,0:T(8,128)S(1)} %shard_map.97.mine_ref.refs_0_), channel_id=1, source_target_pairs={{0,3},{1,2},{2,1},{3,0},{4,7},{5,6},{6,5},{7,4},{8,11},{9,10},{10,... | collective-permute-start | bytes 12296 | tf_op jit(solution)/shard_map/ppermute | solution.py:262
  34.1 4.7 %collective-permute-start.8 = (f32[8,128]{1,0:T(8,128)S(1)}, f32[8,128]{1,0:T(8,128)S(1)}, u32[]{:S(2)}, u32[]{:S(2)}) collective-permute-start(f32[8,128]{1,0:T(8,128)S(1)} %shard_map.97.mine_ref.refs_0_), channel_id=1, source_target_pairs={{0,1},{1,0},{2,3},{3,2},{4,5},{5,4},{6,7},{7,6},{8,10},{9,11},{10,... | collective-permute-start | bytes 12296 | tf_op jit(solution)/shard_map/ppermute | solution.py:262
  34.9 4.0 %collective-permute-start.9 = (f32[8,128]{1,0:T(8,128)S(1)}, f32[8,128]{1,0:T(8,128)S(1)}, u32[]{:S(2)}, u32[]{:S(2)}) collective-permute-start(f32[8,128]{1,0:T(8,128)S(1)} %shard_map.97.mine_ref.refs_0_), channel_id=1, source_target_pairs={{0,2},{1,3},{2,0},{3,1},{4,6},{5,7},{6,4},{7,5},{8,9},{9,8},{10,11... | collective-permute-start | bytes 12296 | tf_op jit(solution)/shard_map/ppermute | solution.py:262
  39.8 8.2 %collective-permute-start.14 = (f16[16,4096]{1,0:T(8,128)(2,1)S(1)}, f16[16,4096]{1,0:T(8,128)(2,1)S(1)}, u32[]{:S(2)}, u32[]{:S(2)}) collective-permute-start(f16[16,4096]{1,0:T(8,128)(2,1)S(1)} %get-tuple-element.23), channel_id=1, source_target_pairs={{0,3},{1,2},{2,1},{3,0},{4,7},{5,6},{6,5},{7,4},{8,11},{9,10},{10,... | collective-permute-start | bytes 393224 | tf_op jit(solution)/shard_map/ppermute | solution.py:262
  41.2 7.8 %collective-permute-start.15 = (f16[16,4096]{1,0:T(8,128)(2,1)S(1)}, f16[16,4096]{1,0:T(8,128)(2,1)S(1)}, u32[]{:S(2)}, u32[]{:S(2)}) collective-permute-start(f16[16,4096]{1,0:T(8,128)(2,1)S(1)} %get-tuple-element.25), channel_id=1, source_target_pairs={{0,2},{1,3},{2,0},{3,1},{4,6},{5,7},{6,4},{7,5},{8,9},{9,8},{10,11... | collective-permute-start | bytes 393224 | tf_op jit(solution)/shard_map/ppermute | solution.py:262
  42.2 6.8 %collective-permute-start.16 = (f16[16,4096]{1,0:T(8,128)(2,1)S(1)}, f16[16,4096]{1,0:T(8,128)(2,1)S(1)}, u32[]{:S(2)}, u32[]{:S(2)}) collective-permute-start(f16[16,4096]{1,0:T(8,128)(2,1)S(1)} %get-tuple-element.24), channel_id=1, source_target_pairs={{0,1},{1,0},{2,3},{3,2},{4,5},{5,4},{6,7},{7,6},{8,10},{9,11},{10,... | collective-permute-start | bytes 393224 | tf_op jit(solution)/shard_map/ppermute | solution.py:262
  43.3 7.7 %copy-start.2 = (f32[128,2048]{1,0:T(8,128)S(1)}, f32[128,2048]{1,0:T(8,128)}, u32[]{:S(2)}) copy-start(f32[128,2048]{1,0:T(8,128)} %peer_ref.1) | copy-start | bytes 3145732
  43.4 7.6 %copy-start.1 = (f32[128,2048]{1,0:T(8,128)S(1)}, f32[128,2048]{1,0:T(8,128)}, u32[]{:S(2)}) copy-start(f32[128,2048]{1,0:T(8,128)} %momentum_ref.1) | copy-start | bytes 3145732
  43.5 7.5 %copy-start = (f32[128,2048]{1,0:T(8,128)S(1)}, f32[128,2048]{1,0:T(8,128)}, u32[]{:S(2)}) copy-start(f32[128,2048]{1,0:T(8,128)} %global_ref.1) | copy-start | bytes 3145732
  43.5 10.9 %collective-permute-start.11 = (f16[16,4096]{1,0:T(8,128)(2,1)S(1)}, f16[16,4096]{1,0:T(8,128)(2,1)S(1)}, u32[]{:S(2)}, u32[]{:S(2)}) collective-permute-start(f16[16,4096]{1,0:T(8,128)(2,1)S(1)} %get-tuple-element.20), channel_id=1, source_target_pairs={{0,3},{1,2},{2,1},{3,0},{4,7},{5,6},{6,5},{7,4},{8,11},{9,10},{10,... | collective-permute-start | bytes 393224 | tf_op jit(solution)/shard_map/ppermute | solution.py:262
  44.9 9.5 %collective-permute-start.12 = (f16[16,4096]{1,0:T(8,128)(2,1)S(1)}, f16[16,4096]{1,0:T(8,128)(2,1)S(1)}, u32[]{:S(2)}, u32[]{:S(2)}) collective-permute-start(f16[16,4096]{1,0:T(8,128)(2,1)S(1)} %get-tuple-element.22), channel_id=1, source_target_pairs={{0,2},{1,3},{2,0},{3,1},{4,6},{5,7},{6,4},{7,5},{8,9},{9,8},{10,11... | collective-permute-start | bytes 393224 | tf_op jit(solution)/shard_map/ppermute | solution.py:262
  48.0 6.4 %collective-permute-start.13 = (f16[16,4096]{1,0:T(8,128)(2,1)S(1)}, f16[16,4096]{1,0:T(8,128)(2,1)S(1)}, u32[]{:S(2)}, u32[]{:S(2)}) collective-permute-start(f16[16,4096]{1,0:T(8,128)(2,1)S(1)} %get-tuple-element.21), channel_id=1, source_target_pairs={{0,1},{1,0},{2,3},{3,2},{4,5},{5,4},{6,7},{7,6},{8,10},{9,11},{10,... | collective-permute-start | bytes 393224 | tf_op jit(solution)/shard_map/ppermute | solution.py:262
  49.1 7.3 %collective-permute-start.17 = (f16[16,4096]{1,0:T(8,128)(2,1)S(1)}, f16[16,4096]{1,0:T(8,128)(2,1)S(1)}, u32[]{:S(2)}, u32[]{:S(2)}) collective-permute-start(f16[16,4096]{1,0:T(8,128)(2,1)S(1)} %fusion.2), channel_id=1, source_target_pairs={{0,4},{1,5},{2,6},{3,7},{4,0},{5,1},{6,2},{7,3},{8,12},{9,13},{10,... | collective-permute-start | bytes 393224 | tf_op jit(solution)/shard_map/ppermute | solution.py:262

commit v18 on v15

--- a/solution.py
+++ b/solution.py
@@ -31,18 +31,21 @@
     )(*[pltpu.with_memory_space_constraint(x, place) for x, place in zip(operands, places)])
 
 
-def head_copies(source, target, sems, half):
-    block = source.shape[0] // sems.shape[0]
-    columns = pl.ds(half * (source.shape[1] // 2), source.shape[1] // 2)
+PARTS = 8
+AHEAD = 6
+
+
+def head_copies(source, target, sems, first, last):
+    width = source.shape[1] // PARTS
     copies = []
-    for i in range(sems.shape[0]):
-        part = pl.ds(i * block, block)
-        copies.append(pltpu.make_async_copy(source.at[part, columns], target.at[part, columns], sems.at[i]))
+    for part in range(first, last):
+        columns = pl.ds(part * width, width)
+        copies.append(pltpu.make_async_copy(source.at[:, columns], target.at[:, columns], sems.at[part]))
     return copies
 
 
 def load_kernel(head, near_ref, sems):
-    copies = head_copies(head, near_ref, sems, 0)
+    copies = head_copies(head, near_ref, sems, 0, AHEAD)
     for copy in copies:
         copy.start()
     for copy in copies:
@@ -96,15 +99,14 @@
     return jnp.broadcast_to(line, (LANES, line.shape[1])).T[:, 0:1]
 
 
-def logits_of(rows_ref, near_ref, logits_ref, first, count):
+def logits_of(rows_ref, near_ref, logits_ref, first, last):
     depth = near_ref.shape[0]
-
-    @pl.loop(0, count // WIDE)
-    def _(i):
-        part = pl.ds(pl.multiple_of(first + i * WIDE, WIDE), WIDE)
+    while first < last:
+        part = pl.ds(first, min(WIDE, last - first))
         logits_ref[:, part] = jnp.dot(
             rows_ref[:, :depth], near_ref[:, part], preferred_element_type=jnp.float32
         )
+        first += WIDE
 
 
 def softmax_of(rows_ref, logits_ref, both_ref, columns_ref, first):
@@ -132,14 +134,15 @@
 
 
 def first_kernel(packed_ref, head, held_ref, near_ref, logits_ref, both_ref, columns_ref, sems):
-    half = near_ref.shape[1] // 2
-    copies = head_copies(head, near_ref, sems, 1)
+    width = near_ref.shape[1]
+    there = width // PARTS * AHEAD
+    copies = head_copies(head, near_ref, sems, AHEAD, PARTS)
     for copy in copies:
         copy.start()
-    logits_of(packed_ref, near_ref, logits_ref, 0, half)
+    logits_of(packed_ref, near_ref, logits_ref, 0, there)
     for copy in copies:
         copy.wait()
-    logits_of(packed_ref, near_ref, logits_ref, half, half)
+    logits_of(packed_ref, near_ref, logits_ref, there, width)
     softmax_of(packed_ref, logits_ref, both_ref, columns_ref, 0)
 
 
@@ -325,7 +328,7 @@
     rows_near, rows_far = gather_rows(packed)
     near = call(
         load_kernel, [(head.shape, head.dtype)], [head],
-        scratch=[pltpu.SemaphoreType.DMA((4,))], sources=[pltpu.HBM],
+        scratch=[pltpu.SemaphoreType.DMA((PARTS,))], sources=[pltpu.HBM],
     )[0]
 
     count = 4 * own
@@ -334,7 +337,7 @@
         [(head.shape, head.dtype), ((count, width), jnp.float32), ((2 * count, width), jnp.bfloat16),
          ((count, LANES), jnp.float32)],
         [rows_near, head, near], 2 * count * depth * width,
-        scratch=[pltpu.SemaphoreType.DMA((4,))],
+        scratch=[pltpu.SemaphoreType.DMA((PARTS,))],
         sources=[pltpu.VMEM, pltpu.HBM, pltpu.VMEM], aliases={2: 0},
     )
     count = rows - 4 * own

time: 57.8 us -> 57.4 us (level)
  starting transfers between devices: 22.8 us -> 23.8 us
  waiting for transfers between devices: 8.8 us -> 7.96 us
    ppermute x18, starting transfers between devices: 22.8 us -> 23.8 us  [swap(): lax.ppermute(value, AXIS, [(i, i ^ step) for i in range(lax.axis_size(AXI...]
    ppermute x18, waiting for transfers between devices: 8.8 us -> 7.96 us  [swap(): lax.ppermute(value, AXIS, [(i, i ^ step) for i in range(lax.axis_size(AXI...]
  transfers between devices with their start and end apart: 18 -> 18, of which waited for: 5 -> 6; matrix products, arithmetic and copies ran while one was open for 1% -> 1% of each run, Pallas kernels for 31% -> 31%
where the time goes in v18:
time: 57.4 us; the launch traced here: 57.3 us
  starting transfers between devices  23.8 us (41%)
  Pallas kernels  22.9 us (40%)
  waiting for transfers between devices  7.96 us (14%)
  other arithmetic  1.07 us (2%)
  between operations  0.8 us (1%)
  local copies, waits for them, and re-layouts  0.68 us (1%)
    ppermute x18, starting transfers between devices, swap(): lax.ppermute(value, AXIS, [(i, i ^ step) for i in range(lax.axis_size(AXI...  23.8 us
    pallas_call x11, Pallas kernels, call(): pl.pallas_call(kernel, out_shape=outs, in_specs=[pl.BlockSpec(memory_spac...  19.5 us
    ppermute x18, waiting for transfers between devices, swap(): lax.ppermute(value, AXIS, [(i, i ^ step) for i in range(lax.axis_size(AXI...  7.96 us
    pallas_call x1, Pallas kernels, frag_update(): pl.pallas_call(frag_kernel, grid=(width // TILE,), out_shape=[jax.ShapeDt...  3.38 us
  transfers between devices with their start and end apart: 18, of which 6 were waited for; matrix products, arithmetic and copies ran while one was open for 1% of the time, Pallas kernels for 31%

profile of v18, /device:TPU:0, one launch (start us, length us, event | category | flops | bytes accessed | tf_op | source)
XLA Modules:
  0.0 57.3 jit_solution(14429141764696979306)
XLA Ops:
  0.6 0.9 %shard_map.93 = bf16[16,4224]{1,0:T(8,128)(2,1)S(1)} custom-call(s32[16]{0:T(128)} %targets.1, bf16[16,4096]{1,0:T(8,128)(2,1)} %rows.1), custom_call_target="tpu_custom_call" | custom-call | bytes 131136 | tf_op jit(solution)/shard_map/pallas_call | solution.py:22
  1.6 4.1 %collective-permute-start = (bf16[16,4224]{1,0:T(8,128)(2,1)S(1)}, bf16[16,4224]{1,0:T(8,128)(2,1)S(1)}, u32[]{:S(2)}, u32[]{:S(2)}) collective-permute-start(bf16[16,4224]{1,0:T(8,128)(2,1)S(1)} %shard_map.93), channel_id=1, source_target_pairs={{0,4},{1,5},{2,6},{3,7},{4,0},{5,1},{6,2},{7,3},{8,12},{9,13},{10,... | collective-permute-start | bytes 405512 | tf_op jit(solution)/shard_map/ppermute | solution.py:269
  5.7 2.5 %collective-permute-start.6 = (bf16[16,4224]{1,0:T(8,128)(2,1)S(1)}, bf16[16,4224]{1,0:T(8,128)(2,1)S(1)}, u32[]{:S(2)}, u32[]{:S(2)}) collective-permute-start(bf16[16,4224]{1,0:T(8,128)(2,1)S(1)} %shard_map.93), channel_id=1, source_target_pairs={{0,3},{1,2},{2,1},{3,0},{4,7},{5,6},{6,5},{7,4},{8,11},{9,10},{10,... | collective-permute-start | bytes 405512 | tf_op jit(solution)/shard_map/ppermute | solution.py:269
  9.2 4.8 %shard_map.94.held_ref = bf16[4096,2048]{1,0:T(8,128)(2,1)S(1)} custom-call(bf16[4096,2048]{1,0:T(8,128)(2,1)} %head.3), custom_call_target="tpu_custom_call" | custom-call | bytes 16777216 | tf_op jit(solution)/shard_map/pallas_call | solution.py:22
  14.0 2.6 %collective-permute-start.3 = (bf16[16,4224]{1,0:T(8,128)(2,1)S(1)}, bf16[16,4224]{1,0:T(8,128)(2,1)S(1)}, u32[]{:S(2)}, u32[]{:S(2)}) collective-permute-start(bf16[16,4224]{1,0:T(8,128)(2,1)S(1)} %collective-permute-done), channel_id=1, source_target_pairs={{0,3},{1,2},{2,1},{3,0},{4,7},{5,6},{6,5},{7,4},{8,11},{9,10},{10,... | collective-permute-start | bytes 405512 | tf_op jit(solution)/shard_map/ppermute | solution.py:269
  17.0 0.5 collective-permute-start.1
  17.6 4.0 %shard_map.95 = (bf16[4096,2048]{1,0:T(8,128)(2,1)S(1)}, f32[64,2048]{1,0:T(8,128)S(1)}, bf16[128,2048]{1,0:T(8,128)(2,1)S(1)}, f32[64,128]{1,0:T(8,128)S(1)}) custom-call(bf16[64,4224]{1,0:T(8,128)(2,1)S(1)} %pad_maximum_fusion.1.packed_ref.rows_one_ref.ids_one_ref, bf16[4096,2048]{1,0:T(8,128)(2,1)} %head.3, ...), custom_call_target="tpu_custom_call", output_to_operand_aliasing={{0}: (2, {})} | custom-call | flops 1073741824 | bytes 34095104 | tf_op jit(solution)/shard_map/pallas_call | solution.py:22
  21.6 0.5 collective-permute-done.2
  22.2 3.6 %shard_map.96 = (f32[64,2048]{1,0:T(8,128)S(1)}, bf16[128,2048]{1,0:T(8,128)(2,1)S(1)}, f32[8,128]{1,0:T(8,128)S(1)}) custom-call(bf16[64,4224]{1,0:T(8,128)(2,1)S(1)} %bitcast.6, bf16[4096,2048]{1,0:T(8,128)(2,1)S(1)} %get-tuple-element.13.near_ref.head_ref, f32[64,128]{1,0:T(8,128)S(1)} %get-tuple-element.14.before_ref), custom_call_target="tpu_custom_call" | custom-call | flops 1073741824 | bytes 17350656 | tf_op jit(solution)/shard_map/pallas_call | solution.py:22
  25.8 1.8 %collective-permute-start.7 = (f32[8,128]{1,0:T(8,128)S(1)}, f32[8,128]{1,0:T(8,128)S(1)}, u32[]{:S(2)}, u32[]{:S(2)}) collective-permute-start(f32[8,128]{1,0:T(8,128)S(1)} %get-tuple-element.15.mine_ref), channel_id=1, source_target_pairs={{0,4},{1,5},{2,6},{3,7},{4,0},{5,1},{6,2},{7,3},{8,12},{9,13},{10,... | collective-permute-start | bytes 12296 | tf_op jit(solution)/shard_map/ppermute | solution.py:269
  27.7 2.5 %shard_map.100.refs_0_ = f32[256,2048]{1,0:T(8,128)S(1)} custom-call(bf16[128,2048]{1,0:T(8,128)(2,1)S(1)} %get-tuple-element.16.one_ref, bf16[128,2048]{1,0:T(8,128)(2,1)S(1)} %get-tuple-element.17.two_ref, bf16[4096,2048]{1,0:T(8,128)(2,1)S(1)} %get-tuple-element.13.near_ref.head_ref), custom_call_target="tpu_custom_call" | custom-call | flops 2147483648 | bytes 17825792 | tf_op jit(solution)/shard_map/pallas_call | solution.py:22
  30.5 2.5 %collective-permute-start.10 = (f32[8,128]{1,0:T(8,128)S(1)}, f32[8,128]{1,0:T(8,128)S(1)}, u32[]{:S(2)}, u32[]{:S(2)}) collective-permute-start(f32[8,128]{1,0:T(8,128)S(1)} %shard_map.97.mine_ref.refs_0_), channel_id=1, source_target_pairs={{0,3},{1,2},{2,1},{3,0},{4,7},{5,6},{6,5},{7,4},{8,11},{9,10},{10,... | collective-permute-start | bytes 12296 | tf_op jit(solution)/shard_map/ppermute | solution.py:269
  33.4 0.6 %collective-permute-start.8 = (f32[8,128]{1,0:T(8,128)S(1)}, f32[8,128]{1,0:T(8,128)S(1)}, u32[]{:S(2)}, u32[]{:S(2)}) collective-permute-start(f32[8,128]{1,0:T(8,128)S(1)} %shard_map.97.mine_ref.refs_0_), channel_id=1, source_target_pairs={{0,1},{1,0},{2,3},{3,2},{4,5},{5,4},{6,7},{7,6},{8,9},{9,8},{10,11... | collective-permute-start | bytes 12296 | tf_op jit(solution)/shard_map/ppermute | solution.py:269
  34.0 2.5 %shard_map.101.refs_1_ = f32[256,2048]{1,0:T(8,128)S(1)} custom-call(bf16[128,2048]{1,0:T(8,128)(2,1)S(1)} %get-tuple-element.16.one_ref, bf16[128,2048]{1,0:T(8,128)(2,1)S(1)} %get-tuple-element.17.two_ref, bf16[4096,2048]{1,0:T(8,128)(2,1)S(1)} %get-tuple-element.13.near_ref.head_ref, f32[8,128]{1,0:T(8,128)S(1)} %shard_map.97.mine_ref.refs_0_), custom_call_target="tpu_custom_call" | custom-call | flops 2147483648 | bytes 17829888 | tf_op jit(solution)/shard_map/pallas_call | solution.py:22
  38.0 2.1 %collective-permute-start.14 = (f16[16,4096]{1,0:T(8,128)(2,1)S(1)}, f16[16,4096]{1,0:T(8,128)(2,1)S(1)}, u32[]{:S(2)}, u32[]{:S(2)}) collective-permute-start(f16[16,4096]{1,0:T(8,128)(2,1)S(1)} %get-tuple-element.25), channel_id=1, source_target_pairs={{0,3},{1,2},{2,1},{3,0},{4,7},{5,6},{6,5},{7,4},{8,11},{9,10},{10,... | collective-permute-start | bytes 393224 | tf_op jit(solution)/shard_map/ppermute | solution.py:269
  40.6 1.0 %collective-permute-start.15 = (f16[16,4096]{1,0:T(8,128)(2,1)S(1)}, f16[16,4096]{1,0:T(8,128)(2,1)S(1)}, u32[]{:S(2)}, u32[]{:S(2)}) collective-permute-start(f16[16,4096]{1,0:T(8,128)(2,1)S(1)} %get-tuple-element.27), channel_id=1, source_target_pairs={{0,1},{1,0},{2,3},{3,2},{4,5},{5,4},{6,7},{7,6},{8,9},{9,8},{10,11... | collective-permute-start | bytes 393224 | tf_op jit(solution)/shard_map/ppermute | solution.py:269
  41.7 2.1 %collective-permute-start.11 = (f16[16,4096]{1,0:T(8,128)(2,1)S(1)}, f16[16,4096]{1,0:T(8,128)(2,1)S(1)}, u32[]{:S(2)}, u32[]{:S(2)}) collective-permute-start(f16[16,4096]{1,0:T(8,128)(2,1)S(1)} %get-tuple-element.22), channel_id=1, source_target_pairs={{0,3},{1,2},{2,1},{3,0},{4,7},{5,6},{6,5},{7,4},{8,11},{9,10},{10,... | collective-permute-start | bytes 393224 | tf_op jit(solution)/shard_map/ppermute | solution.py:269
  44.2 1.4 %collective-permute-done.14 = f16[16,4096]{1,0:T(8,128)(2,1)S(1)} collective-permute-done((f16[16,4096]{1,0:T(8,128)(2,1)S(1)}, f16[16,4096]{1,0:T(8,128)(2,1)S(1)}, u32[]{:S(2)}, u32[]{:S(2)}) %collective-permute-start.14) | collective-permute-done | bytes 131104 | tf_op jit(solution)/shard_map/ppermute | solution.py:269
  45.5 0.8 %collective-permute-start.12 = (f16[16,4096]{1,0:T(8,128)(2,1)S(1)}, f16[16,4096]{1,0:T(8,128)(2,1)S(1)}, u32[]{:S(2)}, u32[]{:S(2)}) collective-permute-start(f16[16,4096]{1,0:T(8,128)(2,1)S(1)} %get-tuple-element.24), channel_id=1, source_target_pairs={{0,1},{1,0},{2,3},{3,2},{4,5},{5,4},{6,7},{7,6},{8,9},{9,8},{10,11... | collective-permute-start | bytes 393224 | tf_op jit(solution)/shard_map/ppermute | solution.py:269
  46.4 2.7 %collective-permute-done.16 = f16[16,4096]{1,0:T(8,128)(2,1)S(1)} collective-permute-done((f16[16,4096]{1,0:T(8,128)(2,1)S(1)}, f16[16,4096]{1,0:T(8,128)(2,1)S(1)}, u32[]{:S(2)}, u32[]{:S(2)}) %collective-permute-start.16) | collective-permute-done | bytes 131104 | tf_op jit(solution)/shard_map/ppermute | solution.py:269
  49.9 0.5 slice.33
  50.4 3.4 %shard_map.104 = (f32[128,2048]{1,0:T(8,128)}, f32[128,2048]{1,0:T(8,128)}) custom-call(bf16[64,4224]{1,0:T(8,128)(2,1)S(1)} %pad_maximum_fusion.1.packed_ref.rows_one_ref.ids_one_ref, bf16[64,4224]{1,0:T(8,128)(2,1)S(1)} %bitcast.7, bf16[64,4224]{1,0:T(8,128)(2,1)S(1)} %pad_maximum_fusion.1.packed_ref.rows_one_ref.ids_one_ref, ...), custom_call_target="tpu_custom_call" | custom-call | flops 67108864 | bytes 6291456 | tf_op jit(solution)/shard_map/pallas_call | solution.py:245
  53.8 2.7 %collective-permute-done.17 = f16[16,4096]{1,0:T(8,128)(2,1)S(1)} collective-permute-done((f16[16,4096]{1,0:T(8,128)(2,1)S(1)}, f16[16,4096]{1,0:T(8,128)(2,1)S(1)}, u32[]{:S(2)}, u32[]{:S(2)}) %collective-permute-start.17) | collective-permute-done | bytes 131104 | tf_op jit(solution)/shard_map/ppermute | solution.py:269
  56.5 0.8 %fusion.7 = bf16[16,4096]{1,0:T(8,128)(2,1)} fusion(f32[64,4096]{1,0:T(8,128)S(1)} %shard_map.102, f16[16,4096]{1,0:T(8,128)(2,1)S(1)} %collective-permute-done.17, f16[16,4096]{1,0:T(8,128)(2,1)S(1)} %collective-permute-done.13, f16[16,4096]{1,0:T(8,128)(2,1)S(1)} %collective-permute-done.12, f16[16,4096]{1,0:T(8,128)(2,1)S(1)} %collective-permute-done.11), kind=kLoop, calls=%fused_computation.11 | loop fusion | flops 655360 | bytes 917504 | tf_op jit(solution)/shard_map/convert_element_type | solution.py:376
  (39 shorter events, 5.4 us)
Async XLA Ops:
  1.6 12.4 %collective-permute-start = (bf16[16,4224]{1,0:T(8,128)(2,1)S(1)}, bf16[16,4224]{1,0:T(8,128)(2,1)S(1)}, u32[]{:S(2)}, u32[]{:S(2)}) collective-permute-start(bf16[16,4224]{1,0:T(8,128)(2,1)S(1)} %shard_map.93), channel_id=1, source_target_pairs={{0,4},{1,5},{2,6},{3,7},{4,0},{5,1},{6,2},{7,3},{8,12},{9,13},{10,... | collective-permute-start | bytes 405512 | tf_op jit(solution)/shard_map/ppermute | solution.py:269
  5.7 11.4 %collective-permute-start.6 = (bf16[16,4224]{1,0:T(8,128)(2,1)S(1)}, bf16[16,4224]{1,0:T(8,128)(2,1)S(1)}, u32[]{:S(2)}, u32[]{:S(2)}) collective-permute-start(bf16[16,4224]{1,0:T(8,128)(2,1)S(1)} %shard_map.93), channel_id=1, source_target_pairs={{0,3},{1,2},{2,1},{3,0},{4,7},{5,6},{6,5},{7,4},{8,11},{9,10},{10,... | collective-permute-start | bytes 405512 | tf_op jit(solution)/shard_map/ppermute | solution.py:269
  8.2 9.3 %collective-permute-start.5 = (bf16[16,4224]{1,0:T(8,128)(2,1)S(1)}, bf16[16,4224]{1,0:T(8,128)(2,1)S(1)}, u32[]{:S(2)}, u32[]{:S(2)}) collective-permute-start(bf16[16,4224]{1,0:T(8,128)(2,1)S(1)} %shard_map.93), channel_id=1, source_target_pairs={{0,2},{1,3},{2,0},{3,1},{4,6},{5,7},{6,4},{7,5},{8,10},{9,11},{10,... | collective-permute-start | bytes 405512 | tf_op jit(solution)/shard_map/ppermute | solution.py:269
  8.6 8.9 %collective-permute-start.4 = (bf16[16,4224]{1,0:T(8,128)(2,1)S(1)}, bf16[16,4224]{1,0:T(8,128)(2,1)S(1)}, u32[]{:S(2)}, u32[]{:S(2)}) collective-permute-start(bf16[16,4224]{1,0:T(8,128)(2,1)S(1)} %shard_map.93), channel_id=1, source_target_pairs={{0,1},{1,0},{2,3},{3,2},{4,5},{5,4},{6,7},{7,6},{8,9},{9,8},{10,11... | collective-permute-start | bytes 405512 | tf_op jit(solution)/shard_map/ppermute | solution.py:269
  14.0 7.6 %collective-permute-start.3 = (bf16[16,4224]{1,0:T(8,128)(2,1)S(1)}, bf16[16,4224]{1,0:T(8,128)(2,1)S(1)}, u32[]{:S(2)}, u32[]{:S(2)}) collective-permute-start(bf16[16,4224]{1,0:T(8,128)(2,1)S(1)} %collective-permute-done), channel_id=1, source_target_pairs={{0,3},{1,2},{2,1},{3,0},{4,7},{5,6},{6,5},{7,4},{8,11},{9,10},{10,... | collective-permute-start | bytes 405512 | tf_op jit(solution)/shard_map/ppermute | solution.py:269
  16.6 5.5 %collective-permute-start.2 = (bf16[16,4224]{1,0:T(8,128)(2,1)S(1)}, bf16[16,4224]{1,0:T(8,128)(2,1)S(1)}, u32[]{:S(2)}, u32[]{:S(2)}) collective-permute-start(bf16[16,4224]{1,0:T(8,128)(2,1)S(1)} %collective-permute-done), channel_id=1, source_target_pairs={{0,2},{1,3},{2,0},{3,1},{4,6},{5,7},{6,4},{7,5},{8,10},{9,11},{10,... | collective-permute-start | bytes 405512 | tf_op jit(solution)/shard_map/ppermute | solution.py:269
  17.0 5.1 %collective-permute-start.1 = (bf16[16,4224]{1,0:T(8,128)(2,1)S(1)}, bf16[16,4224]{1,0:T(8,128)(2,1)S(1)}, u32[]{:S(2)}, u32[]{:S(2)}) collective-permute-start(bf16[16,4224]{1,0:T(8,128)(2,1)S(1)} %collective-permute-done), channel_id=1, source_target_pairs={{0,1},{1,0},{2,3},{3,2},{4,5},{5,4},{6,7},{7,6},{8,9},{9,8},{10,11... | collective-permute-start | bytes 405512 | tf_op jit(solution)/shard_map/ppermute | solution.py:269
  25.8 4.5 %collective-permute-start.7 = (f32[8,128]{1,0:T(8,128)S(1)}, f32[8,128]{1,0:T(8,128)S(1)}, u32[]{:S(2)}, u32[]{:S(2)}) collective-permute-start(f32[8,128]{1,0:T(8,128)S(1)} %get-tuple-element.15.mine_ref), channel_id=1, source_target_pairs={{0,4},{1,5},{2,6},{3,7},{4,0},{5,1},{6,2},{7,3},{8,12},{9,13},{10,... | collective-permute-start | bytes 12296 | tf_op jit(solution)/shard_map/ppermute | solution.py:269
  30.5 6.1 %collective-permute-start.10 = (f32[8,128]{1,0:T(8,128)S(1)}, f32[8,128]{1,0:T(8,128)S(1)}, u32[]{:S(2)}, u32[]{:S(2)}) collective-permute-start(f32[8,128]{1,0:T(8,128)S(1)} %shard_map.97.mine_ref.refs_0_), channel_id=1, source_target_pairs={{0,3},{1,2},{2,1},{3,0},{4,7},{5,6},{6,5},{7,4},{8,11},{9,10},{10,... | collective-permute-start | bytes 12296 | tf_op jit(solution)/shard_map/ppermute | solution.py:269
  33.0 3.6 %collective-permute-start.9 = (f32[8,128]{1,0:T(8,128)S(1)}, f32[8,128]{1,0:T(8,128)S(1)}, u32[]{:S(2)}, u32[]{:S(2)}) collective-permute-start(f32[8,128]{1,0:T(8,128)S(1)} %shard_map.97.mine_ref.refs_0_), channel_id=1, source_target_pairs={{0,2},{1,3},{2,0},{3,1},{4,6},{5,7},{6,4},{7,5},{8,10},{9,11},{10,... | collective-permute-start | bytes 12296 | tf_op jit(solution)/shard_map/ppermute | solution.py:269
  33.4 3.6 %collective-permute-start.8 = (f32[8,128]{1,0:T(8,128)S(1)}, f32[8,128]{1,0:T(8,128)S(1)}, u32[]{:S(2)}, u32[]{:S(2)}) collective-permute-start(f32[8,128]{1,0:T(8,128)S(1)} %shard_map.97.mine_ref.refs_0_), channel_id=1, source_target_pairs={{0,1},{1,0},{2,3},{3,2},{4,5},{5,4},{6,7},{7,6},{8,9},{9,8},{10,11... | collective-permute-start | bytes 12296 | tf_op jit(solution)/shard_map/ppermute | solution.py:269
  37.9 12.6 %copy-start.2 = (f32[128,2048]{1,0:T(8,128)S(1)}, f32[128,2048]{1,0:T(8,128)}, u32[]{:S(2)}) copy-start(f32[128,2048]{1,0:T(8,128)} %peer_ref.1) | copy-start | bytes 3145732
  37.9 12.5 %copy-start = (f32[128,2048]{1,0:T(8,128)S(1)}, f32[128,2048]{1,0:T(8,128)}, u32[]{:S(2)}) copy-start(f32[128,2048]{1,0:T(8,128)} %global_ref.1) | copy-start | bytes 3145732
  38.0 12.5 %copy-start.1 = (f32[128,2048]{1,0:T(8,128)S(1)}, f32[128,2048]{1,0:T(8,128)}, u32[]{:S(2)}) copy-start(f32[128,2048]{1,0:T(8,128)} %momentum_ref.1) | copy-start | bytes 3145732
  38.0 7.5 %collective-permute-start.14 = (f16[16,4096]{1,0:T(8,128)(2,1)S(1)}, f16[16,4096]{1,0:T(8,128)(2,1)S(1)}, u32[]{:S(2)}, u32[]{:S(2)}) collective-permute-start(f16[16,4096]{1,0:T(8,128)(2,1)S(1)} %get-tuple-element.25), channel_id=1, source_target_pairs={{0,3},{1,2},{2,1},{3,0},{4,7},{5,6},{6,5},{7,4},{8,11},{9,10},{10,... | collective-permute-start | bytes 393224 | tf_op jit(solution)/shard_map/ppermute | solution.py:269
  40.1 9.0 %collective-permute-start.16 = (f16[16,4096]{1,0:T(8,128)(2,1)S(1)}, f16[16,4096]{1,0:T(8,128)(2,1)S(1)}, u32[]{:S(2)}, u32[]{:S(2)}) collective-permute-start(f16[16,4096]{1,0:T(8,128)(2,1)S(1)} %get-tuple-element.26), channel_id=1, source_target_pairs={{0,2},{1,3},{2,0},{3,1},{4,6},{5,7},{6,4},{7,5},{8,10},{9,11},{10,... | collective-permute-start | bytes 393224 | tf_op jit(solution)/shard_map/ppermute | solution.py:269
  40.6 8.5 %collective-permute-start.15 = (f16[16,4096]{1,0:T(8,128)(2,1)S(1)}, f16[16,4096]{1,0:T(8,128)(2,1)S(1)}, u32[]{:S(2)}, u32[]{:S(2)}) collective-permute-start(f16[16,4096]{1,0:T(8,128)(2,1)S(1)} %get-tuple-element.27), channel_id=1, source_target_pairs={{0,1},{1,0},{2,3},{3,2},{4,5},{5,4},{6,7},{7,6},{8,9},{9,8},{10,11... | collective-permute-start | bytes 393224 | tf_op jit(solution)/shard_map/ppermute | solution.py:269
  41.7 12.1 %collective-permute-start.11 = (f16[16,4096]{1,0:T(8,128)(2,1)S(1)}, f16[16,4096]{1,0:T(8,128)(2,1)S(1)}, u32[]{:S(2)}, u32[]{:S(2)}) collective-permute-start(f16[16,4096]{1,0:T(8,128)(2,1)S(1)} %get-tuple-element.22), channel_id=1, source_target_pairs={{0,3},{1,2},{2,1},{3,0},{4,7},{5,6},{6,5},{7,4},{8,11},{9,10},{10,... | collective-permute-start | bytes 393224 | tf_op jit(solution)/shard_map/ppermute | solution.py:269
  43.8 10.1 %collective-permute-start.13 = (f16[16,4096]{1,0:T(8,128)(2,1)S(1)}, f16[16,4096]{1,0:T(8,128)(2,1)S(1)}, u32[]{:S(2)}, u32[]{:S(2)}) collective-permute-start(f16[16,4096]{1,0:T(8,128)(2,1)S(1)} %get-tuple-element.23), channel_id=1, source_target_pairs={{0,2},{1,3},{2,0},{3,1},{4,6},{5,7},{6,4},{7,5},{8,10},{9,11},{10,... | collective-permute-start | bytes 393224 | tf_op jit(solution)/shard_map/ppermute | solution.py:269
  45.5 8.3 %collective-permute-start.12 = (f16[16,4096]{1,0:T(8,128)(2,1)S(1)}, f16[16,4096]{1,0:T(8,128)(2,1)S(1)}, u32[]{:S(2)}, u32[]{:S(2)}) collective-permute-start(f16[16,4096]{1,0:T(8,128)(2,1)S(1)} %get-tuple-element.24), channel_id=1, source_target_pairs={{0,1},{1,0},{2,3},{3,2},{4,5},{5,4},{6,7},{7,6},{8,9},{9,8},{10,11... | collective-permute-start | bytes 393224 | tf_op jit(solution)/shard_map/ppermute | solution.py:269
  49.2 7.3 %collective-permute-start.17 = (f16[16,4096]{1,0:T(8,128)(2,1)S(1)}, f16[16,4096]{1,0:T(8,128)(2,1)S(1)}, u32[]{:S(2)}, u32[]{:S(2)}) collective-permute-start(f16[16,4096]{1,0:T(8,128)(2,1)S(1)} %fusion.2), channel_id=1, source_target_pairs={{0,4},{1,5},{2,6},{3,7},{4,0},{5,1},{6,2},{7,3},{8,12},{9,13},{10,... | collective-permute-start | bytes 393224 | tf_op jit(solution)/shard_map/ppermute | solution.py:269

commit v19 on v18

--- a/solution.py
+++ b/solution.py
@@ -303,11 +303,15 @@
         value = swap(value, step).astype(jnp.float32)
         return [value[i * own : (i + 1) * own] for i in range(len(parts))]
 
-    sums = blocks[::4]
-    for part in (list(range(1, members // 4)), [0]):
-        for step in (3, 1, 2):
-            for i, value in zip(part, moved([blocks[4 * i + step] for i in part], step)):
-                sums[i] = sums[i] + value
+    far = range(4, members, 4)
+    three = moved([blocks[i ^ 3] for i in far], 3)
+    two = moved([blocks[i ^ 2] for i in far], 2)
+    one = moved([blocks[i ^ 1] for i in far], 1)
+    relayed = moved([blocks[3]], 1)[0]
+    y_near = moved([blocks[1]], 1)[0]
+    z_near = moved([blocks[2] + relayed], 2)[0]
+    sums = [blocks[0] + z_near + y_near]
+    sums += [blocks[i] + a + b + c for i, a, b, c in zip(far, three, one, two)]
     for step in far_steps()[::-1]:
         keep = len(sums) // 2
         sums = [a + b for a, b in zip(sums[:keep], moved(sums[keep:], step))]

time: 57.4 us -> 56.5 us (0.984)
  waiting for transfers between devices: 7.96 us -> 5.62 us
  starting transfers between devices: 23.8 us -> 25.3 us
    ppermute x18, waiting for transfers between devices: 7.96 us -> 5.62 us  [swap(): lax.ppermute(value, AXIS, [(i, i ^ step) for i in range(lax.axis_size(AXI...]
    ppermute x18, starting transfers between devices: 23.8 us -> 25.3 us  [swap(): lax.ppermute(value, AXIS, [(i, i ^ step) for i in range(lax.axis_size(AXI...]
  transfers between devices with their start and end apart: 18 -> 18, of which waited for: 6 -> 7; matrix products, arithmetic and copies ran while one was open for 1% -> 1% of each run, Pallas kernels for 31% -> 31%
where the time goes in v19:
time: 56.5 us; the launch traced here: 56.4 us
  starting transfers between devices  25.3 us (45%)
  Pallas kernels  22.9 us (41%)
  waiting for transfers between devices  5.62 us (10%)
  other arithmetic  1.1 us (2%)
  between operations  0.79 us (1%)
  local copies, waits for them, and re-layouts  0.65 us (1%)
    ppermute x18, starting transfers between devices, swap(): lax.ppermute(value, AXIS, [(i, i ^ step) for i in range(lax.axis_size(AXI...  25.3 us
    pallas_call x11, Pallas kernels, call(): pl.pallas_call(kernel, out_shape=outs, in_specs=[pl.BlockSpec(memory_spac...  19.5 us
    ppermute x18, waiting for transfers between devices, swap(): lax.ppermute(value, AXIS, [(i, i ^ step) for i in range(lax.axis_size(AXI...  5.62 us
    pallas_call x1, Pallas kernels, frag_update(): pl.pallas_call(frag_kernel, grid=(width // TILE,), out_shape=[jax.ShapeDt...  3.38 us
  transfers between devices with their start and end apart: 18, of which 7 were waited for; matrix products, arithmetic and copies ran while one was open for 1% of the time, Pallas kernels for 31%

profile of v19, /device:TPU:0, one launch (start us, length us, event | category | flops | bytes accessed | tf_op | source)
XLA Modules:
  0.0 56.4 jit_solution(9824441312908131133)
XLA Ops:
  0.6 0.9 %shard_map.93 = bf16[16,4224]{1,0:T(8,128)(2,1)S(1)} custom-call(s32[16]{0:T(128)} %targets.1, bf16[16,4096]{1,0:T(8,128)(2,1)} %rows.1), custom_call_target="tpu_custom_call" | custom-call | bytes 131136 | tf_op jit(solution)/shard_map/pallas_call | solution.py:22
  1.6 4.1 %collective-permute-start = (bf16[16,4224]{1,0:T(8,128)(2,1)S(1)}, bf16[16,4224]{1,0:T(8,128)(2,1)S(1)}, u32[]{:S(2)}, u32[]{:S(2)}) collective-permute-start(bf16[16,4224]{1,0:T(8,128)(2,1)S(1)} %shard_map.93), channel_id=1, source_target_pairs={{0,4},{1,5},{2,6},{3,7},{4,0},{5,1},{6,2},{7,3},{8,12},{9,13},{10,... | collective-permute-start | bytes 405512 | tf_op jit(solution)/shard_map/ppermute | solution.py:269
  5.7 2.5 %collective-permute-start.6 = (bf16[16,4224]{1,0:T(8,128)(2,1)S(1)}, bf16[16,4224]{1,0:T(8,128)(2,1)S(1)}, u32[]{:S(2)}, u32[]{:S(2)}) collective-permute-start(bf16[16,4224]{1,0:T(8,128)(2,1)S(1)} %shard_map.93), channel_id=1, source_target_pairs={{0,3},{1,2},{2,1},{3,0},{4,7},{5,6},{6,5},{7,4},{8,11},{9,10},{10,... | collective-permute-start | bytes 405512 | tf_op jit(solution)/shard_map/ppermute | solution.py:269
  9.2 4.8 %shard_map.94.held_ref = bf16[4096,2048]{1,0:T(8,128)(2,1)S(1)} custom-call(bf16[4096,2048]{1,0:T(8,128)(2,1)} %head.3), custom_call_target="tpu_custom_call" | custom-call | bytes 16777216 | tf_op jit(solution)/shard_map/pallas_call | solution.py:22
  14.0 2.6 %collective-permute-start.3 = (bf16[16,4224]{1,0:T(8,128)(2,1)S(1)}, bf16[16,4224]{1,0:T(8,128)(2,1)S(1)}, u32[]{:S(2)}, u32[]{:S(2)}) collective-permute-start(bf16[16,4224]{1,0:T(8,128)(2,1)S(1)} %collective-permute-done), channel_id=1, source_target_pairs={{0,3},{1,2},{2,1},{3,0},{4,7},{5,6},{6,5},{7,4},{8,11},{9,10},{10,... | collective-permute-start | bytes 405512 | tf_op jit(solution)/shard_map/ppermute | solution.py:269
  17.6 4.0 %shard_map.95 = (bf16[4096,2048]{1,0:T(8,128)(2,1)S(1)}, f32[64,2048]{1,0:T(8,128)S(1)}, bf16[128,2048]{1,0:T(8,128)(2,1)S(1)}, f32[64,128]{1,0:T(8,128)S(1)}) custom-call(bf16[64,4224]{1,0:T(8,128)(2,1)S(1)} %pad_maximum_fusion.1.packed_ref.rows_one_ref.ids_one_ref, bf16[4096,2048]{1,0:T(8,128)(2,1)} %head.3, ...), custom_call_target="tpu_custom_call", output_to_operand_aliasing={{0}: (2, {})} | custom-call | flops 1073741824 | bytes 34095104 | tf_op jit(solution)/shard_map/pallas_call | solution.py:22
  22.2 3.6 %shard_map.96 = (f32[64,2048]{1,0:T(8,128)S(1)}, bf16[128,2048]{1,0:T(8,128)(2,1)S(1)}, f32[8,128]{1,0:T(8,128)S(1)}) custom-call(bf16[64,4224]{1,0:T(8,128)(2,1)S(1)} %bitcast.6, bf16[4096,2048]{1,0:T(8,128)(2,1)S(1)} %get-tuple-element.13.near_ref.head_ref, f32[64,128]{1,0:T(8,128)S(1)} %get-tuple-element.14.before_ref), custom_call_target="tpu_custom_call" | custom-call | flops 1073741824 | bytes 17350656 | tf_op jit(solution)/shard_map/pallas_call | solution.py:22
  25.8 1.8 %collective-permute-start.7 = (f32[8,128]{1,0:T(8,128)S(1)}, f32[8,128]{1,0:T(8,128)S(1)}, u32[]{:S(2)}, u32[]{:S(2)}) collective-permute-start(f32[8,128]{1,0:T(8,128)S(1)} %get-tuple-element.15.mine_ref), channel_id=1, source_target_pairs={{0,4},{1,5},{2,6},{3,7},{4,0},{5,1},{6,2},{7,3},{8,12},{9,13},{10,... | collective-permute-start | bytes 12296 | tf_op jit(solution)/shard_map/ppermute | solution.py:269
  27.7 2.5 %shard_map.100.refs_0_ = f32[256,2048]{1,0:T(8,128)S(1)} custom-call(bf16[128,2048]{1,0:T(8,128)(2,1)S(1)} %get-tuple-element.16.one_ref, bf16[128,2048]{1,0:T(8,128)(2,1)S(1)} %get-tuple-element.17.two_ref, bf16[4096,2048]{1,0:T(8,128)(2,1)S(1)} %get-tuple-element.13.near_ref.head_ref), custom_call_target="tpu_custom_call" | custom-call | flops 2147483648 | bytes 17825792 | tf_op jit(solution)/shard_map/pallas_call | solution.py:22
  30.5 2.5 %collective-permute-start.10 = (f32[8,128]{1,0:T(8,128)S(1)}, f32[8,128]{1,0:T(8,128)S(1)}, u32[]{:S(2)}, u32[]{:S(2)}) collective-permute-start(f32[8,128]{1,0:T(8,128)S(1)} %shard_map.97.mine_ref.refs_0_), channel_id=1, source_target_pairs={{0,3},{1,2},{2,1},{3,0},{4,7},{5,6},{6,5},{7,4},{8,11},{9,10},{10,... | collective-permute-start | bytes 12296 | tf_op jit(solution)/shard_map/ppermute | solution.py:269
  33.4 0.6 %collective-permute-start.8 = (f32[8,128]{1,0:T(8,128)S(1)}, f32[8,128]{1,0:T(8,128)S(1)}, u32[]{:S(2)}, u32[]{:S(2)}) collective-permute-start(f32[8,128]{1,0:T(8,128)S(1)} %shard_map.97.mine_ref.refs_0_), channel_id=1, source_target_pairs={{0,1},{1,0},{2,3},{3,2},{4,5},{5,4},{6,7},{7,6},{8,9},{9,8},{10,11... | collective-permute-start | bytes 12296 | tf_op jit(solution)/shard_map/ppermute | solution.py:269
  34.0 2.5 %shard_map.101.refs_1_ = f32[256,2048]{1,0:T(8,128)S(1)} custom-call(bf16[128,2048]{1,0:T(8,128)(2,1)S(1)} %get-tuple-element.16.one_ref, bf16[128,2048]{1,0:T(8,128)(2,1)S(1)} %get-tuple-element.17.two_ref, bf16[4096,2048]{1,0:T(8,128)(2,1)S(1)} %get-tuple-element.13.near_ref.head_ref, f32[8,128]{1,0:T(8,128)S(1)} %shard_map.97.mine_ref.refs_0_), custom_call_target="tpu_custom_call" | custom-call | flops 2147483648 | bytes 17829888 | tf_op jit(solution)/shard_map/pallas_call | solution.py:22
  37.9 2.1 %collective-permute-start.14 = (f16[16,4096]{1,0:T(8,128)(2,1)S(1)}, f16[16,4096]{1,0:T(8,128)(2,1)S(1)}, u32[]{:S(2)}, u32[]{:S(2)}) collective-permute-start(f16[16,4096]{1,0:T(8,128)(2,1)S(1)} %get-tuple-element.24), channel_id=1, source_target_pairs={{0,3},{1,2},{2,1},{3,0},{4,7},{5,6},{6,5},{7,4},{8,11},{9,10},{10,... | collective-permute-start | bytes 393224 | tf_op jit(solution)/shard_map/ppermute | solution.py:269
  40.5 1.0 %collective-permute-start.15 = (f16[16,4096]{1,0:T(8,128)(2,1)S(1)}, f16[16,4096]{1,0:T(8,128)(2,1)S(1)}, u32[]{:S(2)}, u32[]{:S(2)}) collective-permute-start(f16[16,4096]{1,0:T(8,128)(2,1)S(1)} %get-tuple-element.26), channel_id=1, source_target_pairs={{0,1},{1,0},{2,3},{3,2},{4,5},{5,4},{6,7},{7,6},{8,9},{9,8},{10,11... | collective-permute-start | bytes 393224 | tf_op jit(solution)/shard_map/ppermute | solution.py:269
  41.6 1.1 %collective-permute-start.11 = (f16[16,4096]{1,0:T(8,128)(2,1)S(1)}, f16[16,4096]{1,0:T(8,128)(2,1)S(1)}, u32[]{:S(2)}, u32[]{:S(2)}) collective-permute-start(f16[16,4096]{1,0:T(8,128)(2,1)S(1)} %get-tuple-element.22), channel_id=1, source_target_pairs={{0,1},{1,0},{2,3},{3,2},{4,5},{5,4},{6,7},{7,6},{8,9},{9,8},{10,11... | collective-permute-start | bytes 393224 | tf_op jit(solution)/shard_map/ppermute | solution.py:269
  42.7 1.0 %collective-permute-start.13 = (f16[16,4096]{1,0:T(8,128)(2,1)S(1)}, f16[16,4096]{1,0:T(8,128)(2,1)S(1)}, u32[]{:S(2)}, u32[]{:S(2)}) collective-permute-start(f16[16,4096]{1,0:T(8,128)(2,1)S(1)} %get-tuple-element.23), channel_id=1, source_target_pairs={{0,1},{1,0},{2,3},{3,2},{4,5},{5,4},{6,7},{7,6},{8,9},{9,8},{10,11... | collective-permute-start | bytes 393224 | tf_op jit(solution)/shard_map/ppermute | solution.py:269
  44.2 1.3 %collective-permute-done.16 = f16[16,4096]{1,0:T(8,128)(2,1)S(1)} collective-permute-done((f16[16,4096]{1,0:T(8,128)(2,1)S(1)}, f16[16,4096]{1,0:T(8,128)(2,1)S(1)}, u32[]{:S(2)}, u32[]{:S(2)}) %collective-permute-start.16) | collective-permute-done | bytes 131104 | tf_op jit(solution)/shard_map/ppermute | solution.py:269
  45.4 1.6 %collective-permute-done.15 = f16[16,4096]{1,0:T(8,128)(2,1)S(1)} collective-permute-done((f16[16,4096]{1,0:T(8,128)(2,1)S(1)}, f16[16,4096]{1,0:T(8,128)(2,1)S(1)}, u32[]{:S(2)}, u32[]{:S(2)}) %collective-permute-start.15) | collective-permute-done | bytes 131104 | tf_op jit(solution)/shard_map/ppermute | solution.py:269
  47.1 1.5 %collective-permute-start.17 = (f16[16,4096]{1,0:T(8,128)(2,1)S(1)}, f16[16,4096]{1,0:T(8,128)(2,1)S(1)}, u32[]{:S(2)}, u32[]{:S(2)}) collective-permute-start(f16[16,4096]{1,0:T(8,128)(2,1)S(1)} %fusion.2), channel_id=1, source_target_pairs={{0,4},{1,5},{2,6},{3,7},{4,0},{5,1},{6,2},{7,3},{8,12},{9,13},{10,... | collective-permute-start | bytes 393224 | tf_op jit(solution)/shard_map/ppermute | solution.py:269
  48.6 1.1 %collective-permute-done.11 = f16[16,4096]{1,0:T(8,128)(2,1)S(1)} collective-permute-done((f16[16,4096]{1,0:T(8,128)(2,1)S(1)}, f16[16,4096]{1,0:T(8,128)(2,1)S(1)}, u32[]{:S(2)}, u32[]{:S(2)}) %collective-permute-start.11) | collective-permute-done | bytes 131104 | tf_op jit(solution)/shard_map/ppermute | solution.py:269
  49.7 1.7 %collective-permute-start.12 = (f16[16,4096]{1,0:T(8,128)(2,1)S(1)}, f16[16,4096]{1,0:T(8,128)(2,1)S(1)}, u32[]{:S(2)}, u32[]{:S(2)}) collective-permute-start(f16[16,4096]{1,0:T(8,128)(2,1)S(1)} %fusion.3), channel_id=1, source_target_pairs={{0,2},{1,3},{2,0},{3,1},{4,6},{5,7},{6,4},{7,5},{8,10},{9,11},{10,... | collective-permute-start | bytes 393224 | tf_op jit(solution)/shard_map/ppermute | solution.py:269
  51.7 0.5 slice.32
  52.2 3.4 %shard_map.104 = (f32[128,2048]{1,0:T(8,128)}, f32[128,2048]{1,0:T(8,128)}) custom-call(bf16[64,4224]{1,0:T(8,128)(2,1)S(1)} %pad_maximum_fusion.1.packed_ref.rows_one_ref.ids_one_ref, bf16[64,4224]{1,0:T(8,128)(2,1)S(1)} %bitcast.7, bf16[64,4224]{1,0:T(8,128)(2,1)S(1)} %pad_maximum_fusion.1.packed_ref.rows_one_ref.ids_one_ref, ...), custom_call_target="tpu_custom_call" | custom-call | flops 67108864 | bytes 6291456 | tf_op jit(solution)/shard_map/pallas_call | solution.py:245
  55.6 0.7 %fusion.7 = bf16[16,4096]{1,0:T(8,128)(2,1)} fusion(f32[64,4096]{1,0:T(8,128)S(1)} %shard_map.102, f16[16,4096]{1,0:T(8,128)(2,1)S(1)} %collective-permute-done.17, f16[16,4096]{1,0:T(8,128)(2,1)S(1)} %collective-permute-done.13, f16[16,4096]{1,0:T(8,128)(2,1)S(1)} %collective-permute-done.12), kind=kLoop, calls=%fused_computation.12 | loop fusion | flops 524288 | bytes 786432 | tf_op jit(solution)/shard_map/convert_element_type | solution.py:380
  (40 shorter events, 6.1 us)
Async XLA Ops:
  1.6 12.4 %collective-permute-start = (bf16[16,4224]{1,0:T(8,128)(2,1)S(1)}, bf16[16,4224]{1,0:T(8,128)(2,1)S(1)}, u32[]{:S(2)}, u32[]{:S(2)}) collective-permute-start(bf16[16,4224]{1,0:T(8,128)(2,1)S(1)} %shard_map.93), channel_id=1, source_target_pairs={{0,4},{1,5},{2,6},{3,7},{4,0},{5,1},{6,2},{7,3},{8,12},{9,13},{10,... | collective-permute-start | bytes 405512 | tf_op jit(solution)/shard_map/ppermute | solution.py:269
  5.7 11.4 %collective-permute-start.6 = (bf16[16,4224]{1,0:T(8,128)(2,1)S(1)}, bf16[16,4224]{1,0:T(8,128)(2,1)S(1)}, u32[]{:S(2)}, u32[]{:S(2)}) collective-permute-start(bf16[16,4224]{1,0:T(8,128)(2,1)S(1)} %shard_map.93), channel_id=1, source_target_pairs={{0,3},{1,2},{2,1},{3,0},{4,7},{5,6},{6,5},{7,4},{8,11},{9,10},{10,... | collective-permute-start | bytes 405512 | tf_op jit(solution)/shard_map/ppermute | solution.py:269
  8.2 9.3 %collective-permute-start.5 = (bf16[16,4224]{1,0:T(8,128)(2,1)S(1)}, bf16[16,4224]{1,0:T(8,128)(2,1)S(1)}, u32[]{:S(2)}, u32[]{:S(2)}) collective-permute-start(bf16[16,4224]{1,0:T(8,128)(2,1)S(1)} %shard_map.93), channel_id=1, source_target_pairs={{0,2},{1,3},{2,0},{3,1},{4,6},{5,7},{6,4},{7,5},{8,10},{9,11},{10,... | collective-permute-start | bytes 405512 | tf_op jit(solution)/shard_map/ppermute | solution.py:269
  8.6 8.9 %collective-permute-start.4 = (bf16[16,4224]{1,0:T(8,128)(2,1)S(1)}, bf16[16,4224]{1,0:T(8,128)(2,1)S(1)}, u32[]{:S(2)}, u32[]{:S(2)}) collective-permute-start(bf16[16,4224]{1,0:T(8,128)(2,1)S(1)} %shard_map.93), channel_id=1, source_target_pairs={{0,1},{1,0},{2,3},{3,2},{4,5},{5,4},{6,7},{7,6},{8,9},{9,8},{10,11... | collective-permute-start | bytes 405512 | tf_op jit(solution)/shard_map/ppermute | solution.py:269
  14.0 7.6 %collective-permute-start.3 = (bf16[16,4224]{1,0:T(8,128)(2,1)S(1)}, bf16[16,4224]{1,0:T(8,128)(2,1)S(1)}, u32[]{:S(2)}, u32[]{:S(2)}) collective-permute-start(bf16[16,4224]{1,0:T(8,128)(2,1)S(1)} %collective-permute-done), channel_id=1, source_target_pairs={{0,3},{1,2},{2,1},{3,0},{4,7},{5,6},{6,5},{7,4},{8,11},{9,10},{10,... | collective-permute-start | bytes 405512 | tf_op jit(solution)/shard_map/ppermute | solution.py:269
  16.6 5.5 %collective-permute-start.2 = (bf16[16,4224]{1,0:T(8,128)(2,1)S(1)}, bf16[16,4224]{1,0:T(8,128)(2,1)S(1)}, u32[]{:S(2)}, u32[]{:S(2)}) collective-permute-start(bf16[16,4224]{1,0:T(8,128)(2,1)S(1)} %collective-permute-done), channel_id=1, source_target_pairs={{0,2},{1,3},{2,0},{3,1},{4,6},{5,7},{6,4},{7,5},{8,10},{9,11},{10,... | collective-permute-start | bytes 405512 | tf_op jit(solution)/shard_map/ppermute | solution.py:269
  17.0 5.1 %collective-permute-start.1 = (bf16[16,4224]{1,0:T(8,128)(2,1)S(1)}, bf16[16,4224]{1,0:T(8,128)(2,1)S(1)}, u32[]{:S(2)}, u32[]{:S(2)}) collective-permute-start(bf16[16,4224]{1,0:T(8,128)(2,1)S(1)} %collective-permute-done), channel_id=1, source_target_pairs={{0,1},{1,0},{2,3},{3,2},{4,5},{5,4},{6,7},{7,6},{8,9},{9,8},{10,11... | collective-permute-start | bytes 405512 | tf_op jit(solution)/shard_map/ppermute | solution.py:269
  25.8 4.5 %collective-permute-start.7 = (f32[8,128]{1,0:T(8,128)S(1)}, f32[8,128]{1,0:T(8,128)S(1)}, u32[]{:S(2)}, u32[]{:S(2)}) collective-permute-start(f32[8,128]{1,0:T(8,128)S(1)} %get-tuple-element.15.mine_ref), channel_id=1, source_target_pairs={{0,4},{1,5},{2,6},{3,7},{4,0},{5,1},{6,2},{7,3},{8,12},{9,13},{10,... | collective-permute-start | bytes 12296 | tf_op jit(solution)/shard_map/ppermute | solution.py:269
  30.5 6.1 %collective-permute-start.10 = (f32[8,128]{1,0:T(8,128)S(1)}, f32[8,128]{1,0:T(8,128)S(1)}, u32[]{:S(2)}, u32[]{:S(2)}) collective-permute-start(f32[8,128]{1,0:T(8,128)S(1)} %shard_map.97.mine_ref.refs_0_), channel_id=1, source_target_pairs={{0,3},{1,2},{2,1},{3,0},{4,7},{5,6},{6,5},{7,4},{8,11},{9,10},{10,... | collective-permute-start | bytes 12296 | tf_op jit(solution)/shard_map/ppermute | solution.py:269
  33.0 3.6 %collective-permute-start.9 = (f32[8,128]{1,0:T(8,128)S(1)}, f32[8,128]{1,0:T(8,128)S(1)}, u32[]{:S(2)}, u32[]{:S(2)}) collective-permute-start(f32[8,128]{1,0:T(8,128)S(1)} %shard_map.97.mine_ref.refs_0_), channel_id=1, source_target_pairs={{0,2},{1,3},{2,0},{3,1},{4,6},{5,7},{6,4},{7,5},{8,10},{9,11},{10,... | collective-permute-start | bytes 12296 | tf_op jit(solution)/shard_map/ppermute | solution.py:269
  33.4 3.6 %collective-permute-start.8 = (f32[8,128]{1,0:T(8,128)S(1)}, f32[8,128]{1,0:T(8,128)S(1)}, u32[]{:S(2)}, u32[]{:S(2)}) collective-permute-start(f32[8,128]{1,0:T(8,128)S(1)} %shard_map.97.mine_ref.refs_0_), channel_id=1, source_target_pairs={{0,1},{1,0},{2,3},{3,2},{4,5},{5,4},{6,7},{7,6},{8,9},{9,8},{10,11... | collective-permute-start | bytes 12296 | tf_op jit(solution)/shard_map/ppermute | solution.py:269
  37.9 6.2 %collective-permute-start.14 = (f16[16,4096]{1,0:T(8,128)(2,1)S(1)}, f16[16,4096]{1,0:T(8,128)(2,1)S(1)}, u32[]{:S(2)}, u32[]{:S(2)}) collective-permute-start(f16[16,4096]{1,0:T(8,128)(2,1)S(1)} %get-tuple-element.24), channel_id=1, source_target_pairs={{0,3},{1,2},{2,1},{3,0},{4,7},{5,6},{6,5},{7,4},{8,11},{9,10},{10,... | collective-permute-start | bytes 393224 | tf_op jit(solution)/shard_map/ppermute | solution.py:269
  40.0 5.4 %collective-permute-start.16 = (f16[16,4096]{1,0:T(8,128)(2,1)S(1)}, f16[16,4096]{1,0:T(8,128)(2,1)S(1)}, u32[]{:S(2)}, u32[]{:S(2)}) collective-permute-start(f16[16,4096]{1,0:T(8,128)(2,1)S(1)} %get-tuple-element.25), channel_id=1, source_target_pairs={{0,2},{1,3},{2,0},{3,1},{4,6},{5,7},{6,4},{7,5},{8,10},{9,11},{10,... | collective-permute-start | bytes 393224 | tf_op jit(solution)/shard_map/ppermute | solution.py:269
  40.5 6.6 %collective-permute-start.15 = (f16[16,4096]{1,0:T(8,128)(2,1)S(1)}, f16[16,4096]{1,0:T(8,128)(2,1)S(1)}, u32[]{:S(2)}, u32[]{:S(2)}) collective-permute-start(f16[16,4096]{1,0:T(8,128)(2,1)S(1)} %get-tuple-element.26), channel_id=1, source_target_pairs={{0,1},{1,0},{2,3},{3,2},{4,5},{5,4},{6,7},{7,6},{8,9},{9,8},{10,11... | collective-permute-start | bytes 393224 | tf_op jit(solution)/shard_map/ppermute | solution.py:269
  41.5 10.7 %copy-start.1 = (f32[128,2048]{1,0:T(8,128)S(1)}, f32[128,2048]{1,0:T(8,128)}, u32[]{:S(2)}) copy-start(f32[128,2048]{1,0:T(8,128)} %momentum_ref.1) | copy-start | bytes 3145732
  41.5 10.7 %copy-start.2 = (f32[128,2048]{1,0:T(8,128)S(1)}, f32[128,2048]{1,0:T(8,128)}, u32[]{:S(2)}) copy-start(f32[128,2048]{1,0:T(8,128)} %peer_ref.1) | copy-start | bytes 3145732
  41.6 10.7 %copy-start = (f32[128,2048]{1,0:T(8,128)S(1)}, f32[128,2048]{1,0:T(8,128)}, u32[]{:S(2)}) copy-start(f32[128,2048]{1,0:T(8,128)} %global_ref.1) | copy-start | bytes 3145732
  41.6 8.0 %collective-permute-start.11 = (f16[16,4096]{1,0:T(8,128)(2,1)S(1)}, f16[16,4096]{1,0:T(8,128)(2,1)S(1)}, u32[]{:S(2)}, u32[]{:S(2)}) collective-permute-start(f16[16,4096]{1,0:T(8,128)(2,1)S(1)} %get-tuple-element.22), channel_id=1, source_target_pairs={{0,1},{1,0},{2,3},{3,2},{4,5},{5,4},{6,7},{7,6},{8,9},{9,8},{10,11... | collective-permute-start | bytes 393224 | tf_op jit(solution)/shard_map/ppermute | solution.py:269
  42.7 12.9 %collective-permute-start.13 = (f16[16,4096]{1,0:T(8,128)(2,1)S(1)}, f16[16,4096]{1,0:T(8,128)(2,1)S(1)}, u32[]{:S(2)}, u32[]{:S(2)}) collective-permute-start(f16[16,4096]{1,0:T(8,128)(2,1)S(1)} %get-tuple-element.23), channel_id=1, source_target_pairs={{0,1},{1,0},{2,3},{3,2},{4,5},{5,4},{6,7},{7,6},{8,9},{9,8},{10,11... | collective-permute-start | bytes 393224 | tf_op jit(solution)/shard_map/ppermute | solution.py:269
  47.1 8.5 %collective-permute-start.17 = (f16[16,4096]{1,0:T(8,128)(2,1)S(1)}, f16[16,4096]{1,0:T(8,128)(2,1)S(1)}, u32[]{:S(2)}, u32[]{:S(2)}) collective-permute-start(f16[16,4096]{1,0:T(8,128)(2,1)S(1)} %fusion.2), channel_id=1, source_target_pairs={{0,4},{1,5},{2,6},{3,7},{4,0},{5,1},{6,2},{7,3},{8,12},{9,13},{10,... | collective-permute-start | bytes 393224 | tf_op jit(solution)/shard_map/ppermute | solution.py:269
  49.7 5.9 %collective-permute-start.12 = (f16[16,4096]{1,0:T(8,128)(2,1)S(1)}, f16[16,4096]{1,0:T(8,128)(2,1)S(1)}, u32[]{:S(2)}, u32[]{:S(2)}) collective-permute-start(f16[16,4096]{1,0:T(8,128)(2,1)S(1)} %fusion.3), channel_id=1, source_target_pairs={{0,2},{1,3},{2,0},{3,1},{4,6},{5,7},{6,4},{7,5},{8,10},{9,11},{10,... | collective-permute-start | bytes 393224 | tf_op jit(solution)/shard_map/ppermute | solution.py:269

commit v20 on v19

--- a/solution.py
+++ b/solution.py
@@ -52,7 +52,7 @@
         copy.wait()
 
 
-TILE = 512
+TILE = 1024
 WIDE = 1024
 
 
@@ -210,24 +210,23 @@
             )
 
 
-def loss_kernel(members, lines_ref, loss_ref):
-    rows = lines_ref.shape[1]
-    lines = shared_order(lines_ref[...], members)
-    loss = jnp.sum(lines[0:1] + jnp.log(lines[1:2]) - lines[2:3], axis=1, keepdims=True) / rows
-    loss_ref[...] = jnp.broadcast_to(loss, loss_ref.shape)
-
-
-def frag_kernel(rows_one_ref, rows_two_ref, ids_one_ref, ids_two_ref, lines_ref, one_ref, two_ref, head_ref,
-                global_ref, momentum_ref, peer_ref, new_global_ref, new_momentum_ref):
+def frag_kernel(members, rows_one_ref, rows_two_ref, ids_one_ref, ids_two_ref, lines_ref, one_ref, two_ref, head_ref,
+                global_ref, momentum_ref, peer_ref, new_global_ref, new_momentum_ref, loss_ref):
     logits = jnp.concatenate([one_ref[...], two_ref[...]], axis=0)
     held = jnp.concatenate([rows_one_ref[...], rows_two_ref[...]], axis=0)
     ids = jnp.concatenate([ids_of(ids_one_ref[...]), ids_of(ids_two_ref[...])], axis=0)
     rows, tile = logits.shape
-    top, total = as_columns(lines_ref[0:1, :]), as_columns(lines_ref[1:2, :])
+
+    @pl.when(pl.program_id(0) == 0)
+    def _():
+        lines = shared_order(lines_ref[...], members)
+        loss_ref[0] = jnp.sum(lines[0:1] + jnp.log(lines[1:2]) - lines[2:3]) / rows
+
+    top, share = as_columns(lines_ref[0:1, :]), as_columns(1.0 / lines_ref[1:2, :])
     offset = (lax.axis_index(AXIS) * pl.num_programs(0) + pl.program_id(0)) * tile
     hit = lax.broadcasted_iota(jnp.int32, (rows, tile), 1) == ids - offset
-    shares = jnp.exp(logits - top) / total
-    dlogits = ((shares - jnp.where(hit, 1.0, 0.0)) / rows).astype(jnp.bfloat16)
+    shares = jnp.exp(logits - top) * share
+    dlogits = ((shares - jnp.where(hit, 1.0, 0.0)) * (1.0 / rows)).astype(jnp.bfloat16)
     turned = held.astype(jnp.float32).T.astype(jnp.bfloat16)
     frag_grad = jnp.dot(turned, dlogits, preferred_element_type=jnp.float32)
     local_frag = head_ref[...].astype(jnp.float32) - 1.0 * frag_grad
@@ -237,15 +236,16 @@
     new_global_ref[...] = global_ref[...] - 0.7 * (pseudo + 0.9 * new_momentum)
 
 
-def frag_update(held, ids, lines, logits, near, global_frag, momentum, peer_delta):
+def frag_update(members, held, ids, lines, logits, near, global_frag, momentum, peer_delta):
     rows = lines.shape[1]
     width = near.shape[1]
     tile = pl.BlockSpec((FRAG, TILE), lambda i: (0, i))
 
     return pl.pallas_call(
-        frag_kernel,
+        functools.partial(frag_kernel, members),
         grid=(width // TILE,),
-        out_shape=[jax.ShapeDtypeStruct((FRAG, width), jnp.float32)] * 2,
+        out_shape=[jax.ShapeDtypeStruct((FRAG, width), jnp.float32)] * 2
+        + [jax.ShapeDtypeStruct((1,), jnp.float32)],
         in_specs=[pl.BlockSpec((x.shape[0], FRAG), lambda i: (0, 0)) for x in held]
         + [
             pl.BlockSpec((x.shape[0], LANES), lambda i, last=x.shape[1] // LANES - 1: (0, last))
@@ -254,7 +254,7 @@
         + [pl.BlockSpec((8, rows), lambda i: (0, 0))]
         + [pl.BlockSpec((x.shape[0], TILE), lambda i: (0, i)) for x in logits]
         + [tile] * 4,
-        out_specs=[tile, tile],
+        out_specs=[tile, tile, pl.BlockSpec(memory_space=pltpu.SMEM)],
         compiler_params=pltpu.CompilerParams(vmem_limit_bytes=16 * 2**20),
         cost_estimate=pl.CostEstimate(
             flops=2 * rows * FRAG * width, bytes_accessed=24 * FRAG * width, transcendentals=0
@@ -378,12 +378,11 @@
         for first, count in ((4 * own, rows - 4 * own), (0, 4 * own))
     )
     hidden_grad = (scatter_sums(grads_near, grads_far, own) * (1.0 / scale)).astype(jnp.bfloat16)
-    loss = call(functools.partial(loss_kernel, members), [((8, LANES), jnp.float32)], [lines])[0]
-    new_global, new_momentum = frag_update(
-        [rows_near, rows_far], [rows_near, rows_far], lines, [logits_near, logits_far], near,
+    new_global, new_momentum, loss = frag_update(
+        members, [rows_near, rows_far], [rows_near, rows_far], lines, [logits_near, logits_far], near,
         global_frag, momentum, peer_delta,
     )
-    return (loss[0, :1], hidden_grad, new_global, new_momentum)
+    return (loss, hidden_grad, new_global, new_momentum)
 
 
 def solution(mesh):

time: 56.5 us -> 56.1 us (level)
  waiting for transfers between devices: 5.62 us -> 6.27 us
  Pallas kernels: 22.9 us -> 22.3 us
    ppermute x18, waiting for transfers between devices: 5.62 us -> 6.27 us  [swap(): lax.ppermute(value, AXIS, [(i, i ^ step) for i in range(lax.axis_size(AXI...]
    pallas_call x11 -> x10, Pallas kernels: 19.5 us -> 19.2 us  [call(): pl.pallas_call(kernel, out_shape=outs, in_specs=[pl.BlockSpec(memory_spac...]
  transfers between devices with their start and end apart: 18 -> 18, of which waited for: 7 -> 9; matrix products, arithmetic and copies ran while one was open for 1% -> 0% of each run, Pallas kernels for 31% -> 30%
where the time goes in v20:
time: 56.1 us; the launch traced here: 55.9 us
  starting transfers between devices  25.3 us (45%)
  Pallas kernels  22.3 us (40%)
  waiting for transfers between devices  6.27 us (11%)
  other arithmetic  1.1 us (2%)
  between operations  0.78 us (1%)
    ppermute x18, starting transfers between devices, swap(): lax.ppermute(value, AXIS, [(i, i ^ step) for i in range(lax.axis_size(AXI...  25.3 us
    pallas_call x10, Pallas kernels, call(): pl.pallas_call(kernel, out_shape=outs, in_specs=[pl.BlockSpec(memory_spac...  19.2 us
    ppermute x18, waiting for transfers between devices, swap(): lax.ppermute(value, AXIS, [(i, i ^ step) for i in range(lax.axis_size(AXI...  6.27 us
    pallas_call x1, Pallas kernels, frag_update(): pl.pallas_call(functools.partial(frag_kernel, members), grid=(width // TI...  3.08 us
  transfers between devices with their start and end apart: 18, of which 9 were waited for; matrix products, arithmetic and copies ran while one was open for 0% of the time, Pallas kernels for 30%

profile of v20, /device:TPU:0, one launch (start us, length us, event | category | flops | bytes accessed | tf_op | source)
XLA Modules:
  0.0 55.9 jit_solution(10988322258416504929)
XLA Ops:
  0.6 0.9 %shard_map.93 = bf16[16,4224]{1,0:T(8,128)(2,1)S(1)} custom-call(s32[16]{0:T(128)} %targets.1, bf16[16,4096]{1,0:T(8,128)(2,1)} %rows.1), custom_call_target="tpu_custom_call" | custom-call | bytes 131136 | tf_op jit(solution)/shard_map/pallas_call | solution.py:22
  1.6 4.1 %collective-permute-start.3 = (bf16[16,4224]{1,0:T(8,128)(2,1)S(1)}, bf16[16,4224]{1,0:T(8,128)(2,1)S(1)}, u32[]{:S(2)}, u32[]{:S(2)}) collective-permute-start(bf16[16,4224]{1,0:T(8,128)(2,1)S(1)} %shard_map.93), channel_id=1, source_target_pairs={{0,4},{1,5},{2,6},{3,7},{4,0},{5,1},{6,2},{7,3},{8,12},{9,13},{10,... | collective-permute-start | bytes 405512 | tf_op jit(solution)/shard_map/ppermute | solution.py:269
  5.7 2.5 %collective-permute-start.2 = (bf16[16,4224]{1,0:T(8,128)(2,1)S(1)}, bf16[16,4224]{1,0:T(8,128)(2,1)S(1)}, u32[]{:S(2)}, u32[]{:S(2)}) collective-permute-start(bf16[16,4224]{1,0:T(8,128)(2,1)S(1)} %shard_map.93), channel_id=1, source_target_pairs={{0,3},{1,2},{2,1},{3,0},{4,7},{5,6},{6,5},{7,4},{8,11},{9,10},{10,... | collective-permute-start | bytes 405512 | tf_op jit(solution)/shard_map/ppermute | solution.py:269
  9.2 4.8 %shard_map.94.held_ref = bf16[4096,2048]{1,0:T(8,128)(2,1)S(1)} custom-call(bf16[4096,2048]{1,0:T(8,128)(2,1)} %head.3), custom_call_target="tpu_custom_call" | custom-call | bytes 16777216 | tf_op jit(solution)/shard_map/pallas_call | solution.py:22
  14.0 2.6 %collective-permute-start.6 = (bf16[16,4224]{1,0:T(8,128)(2,1)S(1)}, bf16[16,4224]{1,0:T(8,128)(2,1)S(1)}, u32[]{:S(2)}, u32[]{:S(2)}) collective-permute-start(bf16[16,4224]{1,0:T(8,128)(2,1)S(1)} %collective-permute-done.3), channel_id=1, source_target_pairs={{0,3},{1,2},{2,1},{3,0},{4,7},{5,6},{6,5},{7,4},{8,11},{9,10},{10,... | collective-permute-start | bytes 405512 | tf_op jit(solution)/shard_map/ppermute | solution.py:269
  17.6 4.0 %shard_map.95 = (bf16[4096,2048]{1,0:T(8,128)(2,1)S(1)}, f32[64,2048]{1,0:T(8,128)S(1)}, bf16[128,2048]{1,0:T(8,128)(2,1)S(1)}, f32[64,128]{1,0:T(8,128)S(1)}) custom-call(bf16[64,4224]{1,0:T(8,128)(2,1)S(1)} %pad_maximum_fusion.packed_ref.rows_one_ref.ids_one_ref, bf16[4096,2048]{1,0:T(8,128)(2,1)} %head.3, ...), custom_call_target="tpu_custom_call", output_to_operand_aliasing={{0}: (2, {})} | custom-call | flops 1073741824 | bytes 34095104 | tf_op jit(solution)/shard_map/pallas_call | solution.py:22
  22.2 3.6 %shard_map.96 = (f32[64,2048]{1,0:T(8,128)S(1)}, bf16[128,2048]{1,0:T(8,128)(2,1)S(1)}, f32[8,128]{1,0:T(8,128)S(1)}) custom-call(bf16[64,4224]{1,0:T(8,128)(2,1)S(1)} %bitcast.5, bf16[4096,2048]{1,0:T(8,128)(2,1)S(1)} %get-tuple-element.14.near_ref.head_ref, f32[64,128]{1,0:T(8,128)S(1)} %get-tuple-element.15.before_ref), custom_call_target="tpu_custom_call" | custom-call | flops 1073741824 | bytes 17350656 | tf_op jit(solution)/shard_map/pallas_call | solution.py:22
  25.8 1.8 %collective-permute-start.7 = (f32[8,128]{1,0:T(8,128)S(1)}, f32[8,128]{1,0:T(8,128)S(1)}, u32[]{:S(2)}, u32[]{:S(2)}) collective-permute-start(f32[8,128]{1,0:T(8,128)S(1)} %get-tuple-element.16.mine_ref), channel_id=1, source_target_pairs={{0,4},{1,5},{2,6},{3,7},{4,0},{5,1},{6,2},{7,3},{8,12},{9,13},{10,... | collective-permute-start | bytes 12296 | tf_op jit(solution)/shard_map/ppermute | solution.py:269
  27.7 2.5 %shard_map.100.refs_0_ = f32[256,2048]{1,0:T(8,128)S(1)} custom-call(bf16[128,2048]{1,0:T(8,128)(2,1)S(1)} %get-tuple-element.20.one_ref, bf16[128,2048]{1,0:T(8,128)(2,1)S(1)} %get-tuple-element.21.two_ref, bf16[4096,2048]{1,0:T(8,128)(2,1)S(1)} %get-tuple-element.14.near_ref.head_ref), custom_call_target="tpu_custom_call" | custom-call | flops 2147483648 | bytes 17825792 | tf_op jit(solution)/shard_map/pallas_call | solution.py:22
  30.5 2.5 %collective-permute-start.10 = (f32[8,128]{1,0:T(8,128)S(1)}, f32[8,128]{1,0:T(8,128)S(1)}, u32[]{:S(2)}, u32[]{:S(2)}) collective-permute-start(f32[8,128]{1,0:T(8,128)S(1)} %shard_map.97.mine_ref.refs_0_), channel_id=1, source_target_pairs={{0,3},{1,2},{2,1},{3,0},{4,7},{5,6},{6,5},{7,4},{8,11},{9,10},{10,... | collective-permute-start | bytes 12296 | tf_op jit(solution)/shard_map/ppermute | solution.py:269
  33.4 0.6 %collective-permute-start.8 = (f32[8,128]{1,0:T(8,128)S(1)}, f32[8,128]{1,0:T(8,128)S(1)}, u32[]{:S(2)}, u32[]{:S(2)}) collective-permute-start(f32[8,128]{1,0:T(8,128)S(1)} %shard_map.97.mine_ref.refs_0_), channel_id=1, source_target_pairs={{0,1},{1,0},{2,3},{3,2},{4,5},{5,4},{6,7},{7,6},{8,9},{9,8},{10,11... | collective-permute-start | bytes 12296 | tf_op jit(solution)/shard_map/ppermute | solution.py:269
  34.0 2.5 %shard_map.101.refs_1_ = f32[256,2048]{1,0:T(8,128)S(1)} custom-call(bf16[128,2048]{1,0:T(8,128)(2,1)S(1)} %get-tuple-element.20.one_ref, bf16[128,2048]{1,0:T(8,128)(2,1)S(1)} %get-tuple-element.21.two_ref, bf16[4096,2048]{1,0:T(8,128)(2,1)S(1)} %get-tuple-element.14.near_ref.head_ref, f32[8,128]{1,0:T(8,128)S(1)} %shard_map.97.mine_ref.refs_0_), custom_call_target="tpu_custom_call" | custom-call | flops 2147483648 | bytes 17829888 | tf_op jit(solution)/shard_map/pallas_call | solution.py:22
  37.9 2.1 %collective-permute-start.14 = (f16[16,4096]{1,0:T(8,128)(2,1)S(1)}, f16[16,4096]{1,0:T(8,128)(2,1)S(1)}, u32[]{:S(2)}, u32[]{:S(2)}) collective-permute-start(f16[16,4096]{1,0:T(8,128)(2,1)S(1)} %get-tuple-element.26), channel_id=1, source_target_pairs={{0,3},{1,2},{2,1},{3,0},{4,7},{5,6},{6,5},{7,4},{8,11},{9,10},{10,... | collective-permute-start | bytes 393224 | tf_op jit(solution)/shard_map/ppermute | solution.py:269
  40.5 1.0 %collective-permute-start.15 = (f16[16,4096]{1,0:T(8,128)(2,1)S(1)}, f16[16,4096]{1,0:T(8,128)(2,1)S(1)}, u32[]{:S(2)}, u32[]{:S(2)}) collective-permute-start(f16[16,4096]{1,0:T(8,128)(2,1)S(1)} %get-tuple-element.28), channel_id=1, source_target_pairs={{0,1},{1,0},{2,3},{3,2},{4,5},{5,4},{6,7},{7,6},{8,9},{9,8},{10,11... | collective-permute-start | bytes 393224 | tf_op jit(solution)/shard_map/ppermute | solution.py:269
  41.6 1.1 %collective-permute-start.11 = (f16[16,4096]{1,0:T(8,128)(2,1)S(1)}, f16[16,4096]{1,0:T(8,128)(2,1)S(1)}, u32[]{:S(2)}, u32[]{:S(2)}) collective-permute-start(f16[16,4096]{1,0:T(8,128)(2,1)S(1)} %get-tuple-element.24), channel_id=1, source_target_pairs={{0,1},{1,0},{2,3},{3,2},{4,5},{5,4},{6,7},{7,6},{8,9},{9,8},{10,11... | collective-permute-start | bytes 393224 | tf_op jit(solution)/shard_map/ppermute | solution.py:269
  42.7 1.0 %collective-permute-start.13 = (f16[16,4096]{1,0:T(8,128)(2,1)S(1)}, f16[16,4096]{1,0:T(8,128)(2,1)S(1)}, u32[]{:S(2)}, u32[]{:S(2)}) collective-permute-start(f16[16,4096]{1,0:T(8,128)(2,1)S(1)} %get-tuple-element.25), channel_id=1, source_target_pairs={{0,1},{1,0},{2,3},{3,2},{4,5},{5,4},{6,7},{7,6},{8,9},{9,8},{10,11... | collective-permute-start | bytes 393224 | tf_op jit(solution)/shard_map/ppermute | solution.py:269
  44.2 1.3 %collective-permute-done.16 = f16[16,4096]{1,0:T(8,128)(2,1)S(1)} collective-permute-done((f16[16,4096]{1,0:T(8,128)(2,1)S(1)}, f16[16,4096]{1,0:T(8,128)(2,1)S(1)}, u32[]{:S(2)}, u32[]{:S(2)}) %collective-permute-start.16) | collective-permute-done | bytes 131104 | tf_op jit(solution)/shard_map/ppermute | solution.py:269
  45.4 1.6 %collective-permute-done.15 = f16[16,4096]{1,0:T(8,128)(2,1)S(1)} collective-permute-done((f16[16,4096]{1,0:T(8,128)(2,1)S(1)}, f16[16,4096]{1,0:T(8,128)(2,1)S(1)}, u32[]{:S(2)}, u32[]{:S(2)}) %collective-permute-start.15) | collective-permute-done | bytes 131104 | tf_op jit(solution)/shard_map/ppermute | solution.py:269
  47.1 1.5 %collective-permute-start.17 = (f16[16,4096]{1,0:T(8,128)(2,1)S(1)}, f16[16,4096]{1,0:T(8,128)(2,1)S(1)}, u32[]{:S(2)}, u32[]{:S(2)}) collective-permute-start(f16[16,4096]{1,0:T(8,128)(2,1)S(1)} %fusion.2), channel_id=1, source_target_pairs={{0,4},{1,5},{2,6},{3,7},{4,0},{5,1},{6,2},{7,3},{8,12},{9,13},{10,... | collective-permute-start | bytes 393224 | tf_op jit(solution)/shard_map/ppermute | solution.py:269
  48.6 1.1 %collective-permute-done.11 = f16[16,4096]{1,0:T(8,128)(2,1)S(1)} collective-permute-done((f16[16,4096]{1,0:T(8,128)(2,1)S(1)}, f16[16,4096]{1,0:T(8,128)(2,1)S(1)}, u32[]{:S(2)}, u32[]{:S(2)}) %collective-permute-start.11) | collective-permute-done | bytes 131104 | tf_op jit(solution)/shard_map/ppermute | solution.py:269
  49.7 1.7 %collective-permute-start.12 = (f16[16,4096]{1,0:T(8,128)(2,1)S(1)}, f16[16,4096]{1,0:T(8,128)(2,1)S(1)}, u32[]{:S(2)}, u32[]{:S(2)}) collective-permute-start(f16[16,4096]{1,0:T(8,128)(2,1)S(1)} %fusion.3), channel_id=1, source_target_pairs={{0,2},{1,3},{2,0},{3,1},{4,6},{5,7},{6,4},{7,5},{8,10},{9,11},{10,... | collective-permute-start | bytes 393224 | tf_op jit(solution)/shard_map/ppermute | solution.py:269
  51.4 3.1 %shard_map.99 = (f32[128,2048]{1,0:T(8,128)}, f32[128,2048]{1,0:T(8,128)}, f32[1]{0:T(128)}) custom-call(bf16[64,4224]{1,0:T(8,128)(2,1)S(1)} %pad_maximum_fusion.packed_ref.rows_one_ref.ids_one_ref, bf16[64,4224]{1,0:T(8,128)(2,1)S(1)} %bitcast.6, bf16[64,4224]{1,0:T(8,128)(2,1)S(1)} %pad_maximum_fusion.packed_ref.rows_one_ref.ids_one_ref, ...), custom_call_target="tpu_custom_call" | custom-call | flops 67108864 | bytes 6291456 | tf_op jit(solution)/shard_map/pallas_call | solution.py:244
  54.6 0.6 %collective-permute-done.12 = f16[16,4096]{1,0:T(8,128)(2,1)S(1)} collective-permute-done((f16[16,4096]{1,0:T(8,128)(2,1)S(1)}, f16[16,4096]{1,0:T(8,128)(2,1)S(1)}, u32[]{:S(2)}, u32[]{:S(2)}) %collective-permute-start.12) | collective-permute-done | bytes 131104 | tf_op jit(solution)/shard_map/ppermute | solution.py:269
  55.2 0.7 %fusion.7 = bf16[16,4096]{1,0:T(8,128)(2,1)} fusion(f32[64,4096]{1,0:T(8,128)S(1)} %shard_map.102, f16[16,4096]{1,0:T(8,128)(2,1)S(1)} %collective-permute-done.17, f16[16,4096]{1,0:T(8,128)(2,1)S(1)} %collective-permute-done.13, f16[16,4096]{1,0:T(8,128)(2,1)S(1)} %collective-permute-done.12), kind=kLoop, calls=%fused_computation.12 | loop fusion | flops 524288 | bytes 786432 | tf_op jit(solution)/shard_map/convert_element_type | solution.py:380
  (38 shorter events, 5.8 us)
Async XLA Ops:
  1.6 12.4 %collective-permute-start.3 = (bf16[16,4224]{1,0:T(8,128)(2,1)S(1)}, bf16[16,4224]{1,0:T(8,128)(2,1)S(1)}, u32[]{:S(2)}, u32[]{:S(2)}) collective-permute-start(bf16[16,4224]{1,0:T(8,128)(2,1)S(1)} %shard_map.93), channel_id=1, source_target_pairs={{0,4},{1,5},{2,6},{3,7},{4,0},{5,1},{6,2},{7,3},{8,12},{9,13},{10,... | collective-permute-start | bytes 405512 | tf_op jit(solution)/shard_map/ppermute | solution.py:269
  5.7 11.4 %collective-permute-start.2 = (bf16[16,4224]{1,0:T(8,128)(2,1)S(1)}, bf16[16,4224]{1,0:T(8,128)(2,1)S(1)}, u32[]{:S(2)}, u32[]{:S(2)}) collective-permute-start(bf16[16,4224]{1,0:T(8,128)(2,1)S(1)} %shard_map.93), channel_id=1, source_target_pairs={{0,3},{1,2},{2,1},{3,0},{4,7},{5,6},{6,5},{7,4},{8,11},{9,10},{10,... | collective-permute-start | bytes 405512 | tf_op jit(solution)/shard_map/ppermute | solution.py:269
  8.2 9.3 %collective-permute-start.1 = (bf16[16,4224]{1,0:T(8,128)(2,1)S(1)}, bf16[16,4224]{1,0:T(8,128)(2,1)S(1)}, u32[]{:S(2)}, u32[]{:S(2)}) collective-permute-start(bf16[16,4224]{1,0:T(8,128)(2,1)S(1)} %shard_map.93), channel_id=1, source_target_pairs={{0,2},{1,3},{2,0},{3,1},{4,6},{5,7},{6,4},{7,5},{8,10},{9,11},{10,... | collective-permute-start | bytes 405512 | tf_op jit(solution)/shard_map/ppermute | solution.py:269
  8.6 8.9 %collective-permute-start = (bf16[16,4224]{1,0:T(8,128)(2,1)S(1)}, bf16[16,4224]{1,0:T(8,128)(2,1)S(1)}, u32[]{:S(2)}, u32[]{:S(2)}) collective-permute-start(bf16[16,4224]{1,0:T(8,128)(2,1)S(1)} %shard_map.93), channel_id=1, source_target_pairs={{0,1},{1,0},{2,3},{3,2},{4,5},{5,4},{6,7},{7,6},{8,9},{9,8},{10,11... | collective-permute-start | bytes 405512 | tf_op jit(solution)/shard_map/ppermute | solution.py:269
  14.0 7.6 %collective-permute-start.6 = (bf16[16,4224]{1,0:T(8,128)(2,1)S(1)}, bf16[16,4224]{1,0:T(8,128)(2,1)S(1)}, u32[]{:S(2)}, u32[]{:S(2)}) collective-permute-start(bf16[16,4224]{1,0:T(8,128)(2,1)S(1)} %collective-permute-done.3), channel_id=1, source_target_pairs={{0,3},{1,2},{2,1},{3,0},{4,7},{5,6},{6,5},{7,4},{8,11},{9,10},{10,... | collective-permute-start | bytes 405512 | tf_op jit(solution)/shard_map/ppermute | solution.py:269
  16.6 5.5 %collective-permute-start.5 = (bf16[16,4224]{1,0:T(8,128)(2,1)S(1)}, bf16[16,4224]{1,0:T(8,128)(2,1)S(1)}, u32[]{:S(2)}, u32[]{:S(2)}) collective-permute-start(bf16[16,4224]{1,0:T(8,128)(2,1)S(1)} %collective-permute-done.3), channel_id=1, source_target_pairs={{0,2},{1,3},{2,0},{3,1},{4,6},{5,7},{6,4},{7,5},{8,10},{9,11},{10,... | collective-permute-start | bytes 405512 | tf_op jit(solution)/shard_map/ppermute | solution.py:269
  17.0 5.1 %collective-permute-start.4 = (bf16[16,4224]{1,0:T(8,128)(2,1)S(1)}, bf16[16,4224]{1,0:T(8,128)(2,1)S(1)}, u32[]{:S(2)}, u32[]{:S(2)}) collective-permute-start(bf16[16,4224]{1,0:T(8,128)(2,1)S(1)} %collective-permute-done.3), channel_id=1, source_target_pairs={{0,1},{1,0},{2,3},{3,2},{4,5},{5,4},{6,7},{7,6},{8,9},{9,8},{10,11... | collective-permute-start | bytes 405512 | tf_op jit(solution)/shard_map/ppermute | solution.py:269
  25.8 4.5 %collective-permute-start.7 = (f32[8,128]{1,0:T(8,128)S(1)}, f32[8,128]{1,0:T(8,128)S(1)}, u32[]{:S(2)}, u32[]{:S(2)}) collective-permute-start(f32[8,128]{1,0:T(8,128)S(1)} %get-tuple-element.16.mine_ref), channel_id=1, source_target_pairs={{0,4},{1,5},{2,6},{3,7},{4,0},{5,1},{6,2},{7,3},{8,12},{9,13},{10,... | collective-permute-start | bytes 12296 | tf_op jit(solution)/shard_map/ppermute | solution.py:269
  30.5 6.1 %collective-permute-start.10 = (f32[8,128]{1,0:T(8,128)S(1)}, f32[8,128]{1,0:T(8,128)S(1)}, u32[]{:S(2)}, u32[]{:S(2)}) collective-permute-start(f32[8,128]{1,0:T(8,128)S(1)} %shard_map.97.mine_ref.refs_0_), channel_id=1, source_target_pairs={{0,3},{1,2},{2,1},{3,0},{4,7},{5,6},{6,5},{7,4},{8,11},{9,10},{10,... | collective-permute-start | bytes 12296 | tf_op jit(solution)/shard_map/ppermute | solution.py:269
  33.0 3.6 %collective-permute-start.9 = (f32[8,128]{1,0:T(8,128)S(1)}, f32[8,128]{1,0:T(8,128)S(1)}, u32[]{:S(2)}, u32[]{:S(2)}) collective-permute-start(f32[8,128]{1,0:T(8,128)S(1)} %shard_map.97.mine_ref.refs_0_), channel_id=1, source_target_pairs={{0,2},{1,3},{2,0},{3,1},{4,6},{5,7},{6,4},{7,5},{8,10},{9,11},{10,... | collective-permute-start | bytes 12296 | tf_op jit(solution)/shard_map/ppermute | solution.py:269
  33.4 3.6 %collective-permute-start.8 = (f32[8,128]{1,0:T(8,128)S(1)}, f32[8,128]{1,0:T(8,128)S(1)}, u32[]{:S(2)}, u32[]{:S(2)}) collective-permute-start(f32[8,128]{1,0:T(8,128)S(1)} %shard_map.97.mine_ref.refs_0_), channel_id=1, source_target_pairs={{0,1},{1,0},{2,3},{3,2},{4,5},{5,4},{6,7},{7,6},{8,9},{9,8},{10,11... | collective-permute-start | bytes 12296 | tf_op jit(solution)/shard_map/ppermute | solution.py:269
  37.9 6.2 %collective-permute-start.14 = (f16[16,4096]{1,0:T(8,128)(2,1)S(1)}, f16[16,4096]{1,0:T(8,128)(2,1)S(1)}, u32[]{:S(2)}, u32[]{:S(2)}) collective-permute-start(f16[16,4096]{1,0:T(8,128)(2,1)S(1)} %get-tuple-element.26), channel_id=1, source_target_pairs={{0,3},{1,2},{2,1},{3,0},{4,7},{5,6},{6,5},{7,4},{8,11},{9,10},{10,... | collective-permute-start | bytes 393224 | tf_op jit(solution)/shard_map/ppermute | solution.py:269
  40.0 5.4 %collective-permute-start.16 = (f16[16,4096]{1,0:T(8,128)(2,1)S(1)}, f16[16,4096]{1,0:T(8,128)(2,1)S(1)}, u32[]{:S(2)}, u32[]{:S(2)}) collective-permute-start(f16[16,4096]{1,0:T(8,128)(2,1)S(1)} %get-tuple-element.27), channel_id=1, source_target_pairs={{0,2},{1,3},{2,0},{3,1},{4,6},{5,7},{6,4},{7,5},{8,10},{9,11},{10,... | collective-permute-start | bytes 393224 | tf_op jit(solution)/shard_map/ppermute | solution.py:269
  40.5 6.6 %collective-permute-start.15 = (f16[16,4096]{1,0:T(8,128)(2,1)S(1)}, f16[16,4096]{1,0:T(8,128)(2,1)S(1)}, u32[]{:S(2)}, u32[]{:S(2)}) collective-permute-start(f16[16,4096]{1,0:T(8,128)(2,1)S(1)} %get-tuple-element.28), channel_id=1, source_target_pairs={{0,1},{1,0},{2,3},{3,2},{4,5},{5,4},{6,7},{7,6},{8,9},{9,8},{10,11... | collective-permute-start | bytes 393224 | tf_op jit(solution)/shard_map/ppermute | solution.py:269
  41.5 9.9 %copy-start.1 = (f32[128,2048]{1,0:T(8,128)S(1)}, f32[128,2048]{1,0:T(8,128)}, u32[]{:S(2)}) copy-start(f32[128,2048]{1,0:T(8,128)} %momentum_ref.1) | copy-start | bytes 3145732
  41.5 9.9 %copy-start.2 = (f32[128,2048]{1,0:T(8,128)S(1)}, f32[128,2048]{1,0:T(8,128)}, u32[]{:S(2)}) copy-start(f32[128,2048]{1,0:T(8,128)} %peer_ref.1) | copy-start | bytes 3145732
  41.6 9.9 %copy-start = (f32[128,2048]{1,0:T(8,128)S(1)}, f32[128,2048]{1,0:T(8,128)}, u32[]{:S(2)}) copy-start(f32[128,2048]{1,0:T(8,128)} %global_ref.1) | copy-start | bytes 3145732
  41.6 8.0 %collective-permute-start.11 = (f16[16,4096]{1,0:T(8,128)(2,1)S(1)}, f16[16,4096]{1,0:T(8,128)(2,1)S(1)}, u32[]{:S(2)}, u32[]{:S(2)}) collective-permute-start(f16[16,4096]{1,0:T(8,128)(2,1)S(1)} %get-tuple-element.24), channel_id=1, source_target_pairs={{0,1},{1,0},{2,3},{3,2},{4,5},{5,4},{6,7},{7,6},{8,9},{9,8},{10,11... | collective-permute-start | bytes 393224 | tf_op jit(solution)/shard_map/ppermute | solution.py:269
  42.7 11.8 %collective-permute-start.13 = (f16[16,4096]{1,0:T(8,128)(2,1)S(1)}, f16[16,4096]{1,0:T(8,128)(2,1)S(1)}, u32[]{:S(2)}, u32[]{:S(2)}) collective-permute-start(f16[16,4096]{1,0:T(8,128)(2,1)S(1)} %get-tuple-element.25), channel_id=1, source_target_pairs={{0,1},{1,0},{2,3},{3,2},{4,5},{5,4},{6,7},{7,6},{8,9},{9,8},{10,11... | collective-permute-start | bytes 393224 | tf_op jit(solution)/shard_map/ppermute | solution.py:269
  47.1 7.4 %collective-permute-start.17 = (f16[16,4096]{1,0:T(8,128)(2,1)S(1)}, f16[16,4096]{1,0:T(8,128)(2,1)S(1)}, u32[]{:S(2)}, u32[]{:S(2)}) collective-permute-start(f16[16,4096]{1,0:T(8,128)(2,1)S(1)} %fusion.2), channel_id=1, source_target_pairs={{0,4},{1,5},{2,6},{3,7},{4,0},{5,1},{6,2},{7,3},{8,12},{9,13},{10,... | collective-permute-start | bytes 393224 | tf_op jit(solution)/shard_map/ppermute | solution.py:269
  49.7 5.4 %collective-permute-start.12 = (f16[16,4096]{1,0:T(8,128)(2,1)S(1)}, f16[16,4096]{1,0:T(8,128)(2,1)S(1)}, u32[]{:S(2)}, u32[]{:S(2)}) collective-permute-start(f16[16,4096]{1,0:T(8,128)(2,1)S(1)} %fusion.3), channel_id=1, source_target_pairs={{0,2},{1,3},{2,0},{3,1},{4,6},{5,7},{6,4},{7,5},{8,10},{9,11},{10,... | collective-permute-start | bytes 393224 | tf_op jit(solution)/shard_map/ppermute | solution.py:269

commit v21 on v20

--- a/solution.py
+++ b/solution.py
@@ -86,7 +86,7 @@
 
 
 def shared_order(value, members):
-    me = lax.axis_index(AXIS)
+    me = my_label()
     step = 1
     while step < members:
         swapped = swap_blocks(value, value.shape[1] // members * step)
@@ -157,7 +157,7 @@
 def merge_kernel(steps, members, mine_ref, *refs):
     *other_refs, out_ref = refs
     block = mine_ref.shape[1] // members
-    me = lax.axis_index(AXIS)
+    me = my_label()
     groups = [mine_ref[...]]
     for step, other_ref in zip(steps, other_refs):
         other, bit = other_ref[...], 1
@@ -265,8 +265,22 @@
     )
 
 
+def turned(label):
+    return label // 4 * 4 + label % 2 * 2 + label // 2 % 2
+
+
+def my_label():
+    me = lax.axis_index(AXIS)
+    return jnp.where(lax.rem(lax.axis_index("outer"), 2) == 1, turned(me), me)
+
+
 def swap(value, step):
-    return lax.ppermute(value, AXIS, [(i, i ^ step) for i in range(lax.axis_size(AXIS))])
+    members = lax.axis_size(AXIS)
+    pairs = []
+    for outer in range(lax.axis_size("outer")):
+        flip = turned(step) if outer % 2 else step
+        pairs += [(outer * members + i, outer * members + (i ^ flip)) for i in range(members)]
+    return lax.ppermute(value, ("outer", AXIS), pairs)
 
 
 def far_steps():

time: 56.1 us -> 57 us (1.016)
  waiting for transfers between devices: 6.27 us -> 8.08 us
  starting transfers between devices: 25.3 us -> 24.4 us
    ppermute x18, waiting for transfers between devices: 6.27 us -> 8.08 us  [swap(): return lax.ppermute(value, ('outer', AXIS), pairs)]
    ppermute x18, starting transfers between devices: 25.3 us -> 24.4 us  [swap(): return lax.ppermute(value, ('outer', AXIS), pairs)]
  transfers between devices with their start and end apart: 18 -> 18, of which waited for: 9 -> 7; matrix products, arithmetic and copies ran while one was open for 0% -> 0% of each run, Pallas kernels for 30% -> 30%
where the time goes in v21:
time: 57 us; the launch traced here: 56.8 us
  starting transfers between devices  24.4 us (43%)
  Pallas kernels  22.3 us (39%)
  waiting for transfers between devices  8.08 us (14%)
  other arithmetic  1.1 us (2%)
  between operations  0.8 us (1%)
    ppermute x18, starting transfers between devices, swap(): return lax.ppermute(value, ('outer', AXIS), pairs)  24.4 us
    pallas_call x10, Pallas kernels, call(): pl.pallas_call(kernel, out_shape=outs, in_specs=[pl.BlockSpec(memory_spac...  19.2 us
    ppermute x18, waiting for transfers between devices, swap(): return lax.ppermute(value, ('outer', AXIS), pairs)  8.08 us
    pallas_call x1, Pallas kernels, frag_update(): pl.pallas_call(functools.partial(frag_kernel, members), grid=(width // TI...  3.1 us
  transfers between devices with their start and end apart: 18, of which 7 were waited for; matrix products, arithmetic and copies ran while one was open for 0% of the time, Pallas kernels for 30%

profile of v21, /device:TPU:0, one launch (start us, length us, event | category | flops | bytes accessed | tf_op | source)
XLA Modules:
  0.0 56.8 jit_solution(722243793598182534)
XLA Ops:
  0.6 0.9 %shard_map.93 = bf16[16,4224]{1,0:T(8,128)(2,1)S(1)} custom-call(s32[16]{0:T(128)} %targets.1, bf16[16,4096]{1,0:T(8,128)(2,1)} %rows.1), custom_call_target="tpu_custom_call" | custom-call | bytes 131136 | tf_op jit(solution)/shard_map/pallas_call | solution.py:22
  1.6 4.1 %collective-permute-start.3 = (bf16[16,4224]{1,0:T(8,128)(2,1)S(1)}, bf16[16,4224]{1,0:T(8,128)(2,1)S(1)}, u32[]{:S(2)}, u32[]{:S(2)}) collective-permute-start(bf16[16,4224]{1,0:T(8,128)(2,1)S(1)} %shard_map.93), channel_id=1, source_target_pairs={{0,4},{1,5},{2,6},{3,7},{4,0},{5,1},{6,2},{7,3},{8,12},{9,13},{10,... | collective-permute-start | bytes 405512 | tf_op jit(solution)/shard_map/ppermute | solution.py:283
  5.7 2.5 %collective-permute-start.2 = (bf16[16,4224]{1,0:T(8,128)(2,1)S(1)}, bf16[16,4224]{1,0:T(8,128)(2,1)S(1)}, u32[]{:S(2)}, u32[]{:S(2)}) collective-permute-start(bf16[16,4224]{1,0:T(8,128)(2,1)S(1)} %shard_map.93), channel_id=1, source_target_pairs={{0,3},{1,2},{2,1},{3,0},{4,7},{5,6},{6,5},{7,4},{8,11},{9,10},{10,... | collective-permute-start | bytes 405512 | tf_op jit(solution)/shard_map/ppermute | solution.py:283
  9.2 4.8 %shard_map.94.held_ref = bf16[4096,2048]{1,0:T(8,128)(2,1)S(1)} custom-call(bf16[4096,2048]{1,0:T(8,128)(2,1)} %head.3), custom_call_target="tpu_custom_call" | custom-call | bytes 16777216 | tf_op jit(solution)/shard_map/pallas_call | solution.py:22
  14.0 2.6 %collective-permute-start.6 = (bf16[16,4224]{1,0:T(8,128)(2,1)S(1)}, bf16[16,4224]{1,0:T(8,128)(2,1)S(1)}, u32[]{:S(2)}, u32[]{:S(2)}) collective-permute-start(bf16[16,4224]{1,0:T(8,128)(2,1)S(1)} %collective-permute-done.3), channel_id=1, source_target_pairs={{0,3},{1,2},{2,1},{3,0},{4,7},{5,6},{6,5},{7,4},{8,11},{9,10},{10,... | collective-permute-start | bytes 405512 | tf_op jit(solution)/shard_map/ppermute | solution.py:283
  17.6 4.0 %shard_map.95 = (bf16[4096,2048]{1,0:T(8,128)(2,1)S(1)}, f32[64,2048]{1,0:T(8,128)S(1)}, bf16[128,2048]{1,0:T(8,128)(2,1)S(1)}, f32[64,128]{1,0:T(8,128)S(1)}) custom-call(bf16[64,4224]{1,0:T(8,128)(2,1)S(1)} %pad_maximum_fusion.packed_ref.rows_one_ref.ids_one_ref, bf16[4096,2048]{1,0:T(8,128)(2,1)} %head.3, ...), custom_call_target="tpu_custom_call", output_to_operand_aliasing={{0}: (2, {})} | custom-call | flops 1073741824 | bytes 34095104 | tf_op jit(solution)/shard_map/pallas_call | solution.py:22
  21.6 0.6 %collective-permute-done.5 = bf16[16,4224]{1,0:T(8,128)(2,1)S(1)} collective-permute-done((bf16[16,4224]{1,0:T(8,128)(2,1)S(1)}, bf16[16,4224]{1,0:T(8,128)(2,1)S(1)}, u32[]{:S(2)}, u32[]{:S(2)}) %collective-permute-start.5) | collective-permute-done | bytes 135200 | tf_op jit(solution)/shard_map/ppermute | solution.py:283
  22.4 3.6 %shard_map.96 = (f32[64,2048]{1,0:T(8,128)S(1)}, bf16[128,2048]{1,0:T(8,128)(2,1)S(1)}, f32[8,128]{1,0:T(8,128)S(1)}) custom-call(bf16[64,4224]{1,0:T(8,128)(2,1)S(1)} %bitcast.5, bf16[4096,2048]{1,0:T(8,128)(2,1)S(1)} %get-tuple-element.14.near_ref.head_ref, f32[64,128]{1,0:T(8,128)S(1)} %get-tuple-element.15.before_ref), custom_call_target="tpu_custom_call" | custom-call | flops 1073741824 | bytes 17350656 | tf_op jit(solution)/shard_map/pallas_call | solution.py:22
  26.0 1.6 %collective-permute-start.7 = (f32[8,128]{1,0:T(8,128)S(1)}, f32[8,128]{1,0:T(8,128)S(1)}, u32[]{:S(2)}, u32[]{:S(2)}) collective-permute-start(f32[8,128]{1,0:T(8,128)S(1)} %get-tuple-element.16.mine_ref), channel_id=1, source_target_pairs={{0,4},{1,5},{2,6},{3,7},{4,0},{5,1},{6,2},{7,3},{8,12},{9,13},{10,... | collective-permute-start | bytes 12296 | tf_op jit(solution)/shard_map/ppermute | solution.py:283
  27.7 2.5 %shard_map.100.refs_0_ = f32[256,2048]{1,0:T(8,128)S(1)} custom-call(bf16[128,2048]{1,0:T(8,128)(2,1)S(1)} %get-tuple-element.20.one_ref, bf16[128,2048]{1,0:T(8,128)(2,1)S(1)} %get-tuple-element.21.two_ref, bf16[4096,2048]{1,0:T(8,128)(2,1)S(1)} %get-tuple-element.14.near_ref.head_ref), custom_call_target="tpu_custom_call" | custom-call | flops 2147483648 | bytes 17825792 | tf_op jit(solution)/shard_map/pallas_call | solution.py:22
  30.6 2.2 %collective-permute-start.10 = (f32[8,128]{1,0:T(8,128)S(1)}, f32[8,128]{1,0:T(8,128)S(1)}, u32[]{:S(2)}, u32[]{:S(2)}) collective-permute-start(f32[8,128]{1,0:T(8,128)S(1)} %shard_map.97.mine_ref.refs_0_), channel_id=1, source_target_pairs={{0,3},{1,2},{2,1},{3,0},{4,7},{5,6},{6,5},{7,4},{8,11},{9,10},{10,... | collective-permute-start | bytes 12296 | tf_op jit(solution)/shard_map/ppermute | solution.py:283
  32.9 0.5 collective-permute-start.9
  33.4 0.8 %collective-permute-start.8 = (f32[8,128]{1,0:T(8,128)S(1)}, f32[8,128]{1,0:T(8,128)S(1)}, u32[]{:S(2)}, u32[]{:S(2)}) collective-permute-start(f32[8,128]{1,0:T(8,128)S(1)} %shard_map.97.mine_ref.refs_0_), channel_id=1, source_target_pairs={{0,1},{1,0},{2,3},{3,2},{4,5},{5,4},{6,7},{7,6},{8,10},{9,11},{10,... | collective-permute-start | bytes 12296 | tf_op jit(solution)/shard_map/ppermute | solution.py:283
  34.2 2.5 %shard_map.101.refs_1_ = f32[256,2048]{1,0:T(8,128)S(1)} custom-call(bf16[128,2048]{1,0:T(8,128)(2,1)S(1)} %get-tuple-element.20.one_ref, bf16[128,2048]{1,0:T(8,128)(2,1)S(1)} %get-tuple-element.21.two_ref, bf16[4096,2048]{1,0:T(8,128)(2,1)S(1)} %get-tuple-element.14.near_ref.head_ref, f32[8,128]{1,0:T(8,128)S(1)} %shard_map.97.mine_ref.refs_0_), custom_call_target="tpu_custom_call" | custom-call | flops 2147483648 | bytes 17829888 | tf_op jit(solution)/shard_map/pallas_call | solution.py:22
  37.9 2.0 %collective-permute-start.14 = (f16[16,4096]{1,0:T(8,128)(2,1)S(1)}, f16[16,4096]{1,0:T(8,128)(2,1)S(1)}, u32[]{:S(2)}, u32[]{:S(2)}) collective-permute-start(f16[16,4096]{1,0:T(8,128)(2,1)S(1)} %get-tuple-element.26), channel_id=1, source_target_pairs={{0,3},{1,2},{2,1},{3,0},{4,7},{5,6},{6,5},{7,4},{8,11},{9,10},{10,... | collective-permute-start | bytes 393224 | tf_op jit(solution)/shard_map/ppermute | solution.py:283
  40.5 1.0 %collective-permute-start.15 = (f16[16,4096]{1,0:T(8,128)(2,1)S(1)}, f16[16,4096]{1,0:T(8,128)(2,1)S(1)}, u32[]{:S(2)}, u32[]{:S(2)}) collective-permute-start(f16[16,4096]{1,0:T(8,128)(2,1)S(1)} %get-tuple-element.28), channel_id=1, source_target_pairs={{0,1},{1,0},{2,3},{3,2},{4,5},{5,4},{6,7},{7,6},{8,10},{9,11},{10,... | collective-permute-start | bytes 393224 | tf_op jit(solution)/shard_map/ppermute | solution.py:283
  41.6 1.1 %collective-permute-start.11 = (f16[16,4096]{1,0:T(8,128)(2,1)S(1)}, f16[16,4096]{1,0:T(8,128)(2,1)S(1)}, u32[]{:S(2)}, u32[]{:S(2)}) collective-permute-start(f16[16,4096]{1,0:T(8,128)(2,1)S(1)} %get-tuple-element.24), channel_id=1, source_target_pairs={{0,1},{1,0},{2,3},{3,2},{4,5},{5,4},{6,7},{7,6},{8,10},{9,11},{10,... | collective-permute-start | bytes 393224 | tf_op jit(solution)/shard_map/ppermute | solution.py:283
  42.7 1.0 %collective-permute-start.13 = (f16[16,4096]{1,0:T(8,128)(2,1)S(1)}, f16[16,4096]{1,0:T(8,128)(2,1)S(1)}, u32[]{:S(2)}, u32[]{:S(2)}) collective-permute-start(f16[16,4096]{1,0:T(8,128)(2,1)S(1)} %get-tuple-element.25), channel_id=1, source_target_pairs={{0,1},{1,0},{2,3},{3,2},{4,5},{5,4},{6,7},{7,6},{8,10},{9,11},{10,... | collective-permute-start | bytes 393224 | tf_op jit(solution)/shard_map/ppermute | solution.py:283
  43.7 1.6 %collective-permute-done.14 = f16[16,4096]{1,0:T(8,128)(2,1)S(1)} collective-permute-done((f16[16,4096]{1,0:T(8,128)(2,1)S(1)}, f16[16,4096]{1,0:T(8,128)(2,1)S(1)}, u32[]{:S(2)}, u32[]{:S(2)}) %collective-permute-start.14) | collective-permute-done | bytes 131104 | tf_op jit(solution)/shard_map/ppermute | solution.py:283
  45.3 3.7 %collective-permute-done.16 = f16[16,4096]{1,0:T(8,128)(2,1)S(1)} collective-permute-done((f16[16,4096]{1,0:T(8,128)(2,1)S(1)}, f16[16,4096]{1,0:T(8,128)(2,1)S(1)}, u32[]{:S(2)}, u32[]{:S(2)}) %collective-permute-start.16) | collective-permute-done | bytes 131104 | tf_op jit(solution)/shard_map/ppermute | solution.py:283
  49.3 2.3 %collective-permute-start.12 = (f16[16,4096]{1,0:T(8,128)(2,1)S(1)}, f16[16,4096]{1,0:T(8,128)(2,1)S(1)}, u32[]{:S(2)}, u32[]{:S(2)}) collective-permute-start(f16[16,4096]{1,0:T(8,128)(2,1)S(1)} %fusion.3), channel_id=1, source_target_pairs={{0,2},{1,3},{2,0},{3,1},{4,6},{5,7},{6,4},{7,5},{8,9},{9,8},{10,11... | collective-permute-start | bytes 393224 | tf_op jit(solution)/shard_map/ppermute | solution.py:283
  51.6 3.1 %shard_map.99 = (f32[128,2048]{1,0:T(8,128)}, f32[128,2048]{1,0:T(8,128)}, f32[1]{0:T(128)}) custom-call(bf16[64,4224]{1,0:T(8,128)(2,1)S(1)} %pad_maximum_fusion.packed_ref.rows_one_ref.ids_one_ref, bf16[64,4224]{1,0:T(8,128)(2,1)S(1)} %bitcast.6, bf16[64,4224]{1,0:T(8,128)(2,1)S(1)} %pad_maximum_fusion.packed_ref.rows_one_ref.ids_one_ref, ...), custom_call_target="tpu_custom_call" | custom-call | flops 67108864 | bytes 6291456 | tf_op jit(solution)/shard_map/pallas_call | solution.py:244
  54.7 1.3 %collective-permute-done.17 = f16[16,4096]{1,0:T(8,128)(2,1)S(1)} collective-permute-done((f16[16,4096]{1,0:T(8,128)(2,1)S(1)}, f16[16,4096]{1,0:T(8,128)(2,1)S(1)}, u32[]{:S(2)}, u32[]{:S(2)}) %collective-permute-start.17) | collective-permute-done | bytes 131104 | tf_op jit(solution)/shard_map/ppermute | solution.py:283
  56.1 0.7 %fusion.7 = bf16[16,4096]{1,0:T(8,128)(2,1)} fusion(f32[64,4096]{1,0:T(8,128)S(1)} %shard_map.102, f16[16,4096]{1,0:T(8,128)(2,1)S(1)} %collective-permute-done.17, f16[16,4096]{1,0:T(8,128)(2,1)S(1)} %collective-permute-done.13, f16[16,4096]{1,0:T(8,128)(2,1)S(1)} %collective-permute-done.12), kind=kLoop, calls=%fused_computation.12 | loop fusion | flops 524288 | bytes 786432 | tf_op jit(solution)/shard_map/convert_element_type | solution.py:394
  (38 shorter events, 4.7 us)
Async XLA Ops:
  1.6 12.4 %collective-permute-start.3 = (bf16[16,4224]{1,0:T(8,128)(2,1)S(1)}, bf16[16,4224]{1,0:T(8,128)(2,1)S(1)}, u32[]{:S(2)}, u32[]{:S(2)}) collective-permute-start(bf16[16,4224]{1,0:T(8,128)(2,1)S(1)} %shard_map.93), channel_id=1, source_target_pairs={{0,4},{1,5},{2,6},{3,7},{4,0},{5,1},{6,2},{7,3},{8,12},{9,13},{10,... | collective-permute-start | bytes 405512 | tf_op jit(solution)/shard_map/ppermute | solution.py:283
  5.7 11.4 %collective-permute-start.2 = (bf16[16,4224]{1,0:T(8,128)(2,1)S(1)}, bf16[16,4224]{1,0:T(8,128)(2,1)S(1)}, u32[]{:S(2)}, u32[]{:S(2)}) collective-permute-start(bf16[16,4224]{1,0:T(8,128)(2,1)S(1)} %shard_map.93), channel_id=1, source_target_pairs={{0,3},{1,2},{2,1},{3,0},{4,7},{5,6},{6,5},{7,4},{8,11},{9,10},{10,... | collective-permute-start | bytes 405512 | tf_op jit(solution)/shard_map/ppermute | solution.py:283
  8.2 9.3 %collective-permute-start.1 = (bf16[16,4224]{1,0:T(8,128)(2,1)S(1)}, bf16[16,4224]{1,0:T(8,128)(2,1)S(1)}, u32[]{:S(2)}, u32[]{:S(2)}) collective-permute-start(bf16[16,4224]{1,0:T(8,128)(2,1)S(1)} %shard_map.93), channel_id=1, source_target_pairs={{0,2},{1,3},{2,0},{3,1},{4,6},{5,7},{6,4},{7,5},{8,9},{9,8},{10,11... | collective-permute-start | bytes 405512 | tf_op jit(solution)/shard_map/ppermute | solution.py:283
  8.6 8.9 %collective-permute-start = (bf16[16,4224]{1,0:T(8,128)(2,1)S(1)}, bf16[16,4224]{1,0:T(8,128)(2,1)S(1)}, u32[]{:S(2)}, u32[]{:S(2)}) collective-permute-start(bf16[16,4224]{1,0:T(8,128)(2,1)S(1)} %shard_map.93), channel_id=1, source_target_pairs={{0,1},{1,0},{2,3},{3,2},{4,5},{5,4},{6,7},{7,6},{8,10},{9,11},{10,... | collective-permute-start | bytes 405512 | tf_op jit(solution)/shard_map/ppermute | solution.py:283
  14.0 7.6 %collective-permute-start.6 = (bf16[16,4224]{1,0:T(8,128)(2,1)S(1)}, bf16[16,4224]{1,0:T(8,128)(2,1)S(1)}, u32[]{:S(2)}, u32[]{:S(2)}) collective-permute-start(bf16[16,4224]{1,0:T(8,128)(2,1)S(1)} %collective-permute-done.3), channel_id=1, source_target_pairs={{0,3},{1,2},{2,1},{3,0},{4,7},{5,6},{6,5},{7,4},{8,11},{9,10},{10,... | collective-permute-start | bytes 405512 | tf_op jit(solution)/shard_map/ppermute | solution.py:283
  16.6 5.6 %collective-permute-start.5 = (bf16[16,4224]{1,0:T(8,128)(2,1)S(1)}, bf16[16,4224]{1,0:T(8,128)(2,1)S(1)}, u32[]{:S(2)}, u32[]{:S(2)}) collective-permute-start(bf16[16,4224]{1,0:T(8,128)(2,1)S(1)} %collective-permute-done.3), channel_id=1, source_target_pairs={{0,2},{1,3},{2,0},{3,1},{4,6},{5,7},{6,4},{7,5},{8,9},{9,8},{10,11... | collective-permute-start | bytes 405512 | tf_op jit(solution)/shard_map/ppermute | solution.py:283
  17.0 5.3 %collective-permute-start.4 = (bf16[16,4224]{1,0:T(8,128)(2,1)S(1)}, bf16[16,4224]{1,0:T(8,128)(2,1)S(1)}, u32[]{:S(2)}, u32[]{:S(2)}) collective-permute-start(bf16[16,4224]{1,0:T(8,128)(2,1)S(1)} %collective-permute-done.3), channel_id=1, source_target_pairs={{0,1},{1,0},{2,3},{3,2},{4,5},{5,4},{6,7},{7,6},{8,10},{9,11},{10,... | collective-permute-start | bytes 405512 | tf_op jit(solution)/shard_map/ppermute | solution.py:283
  26.0 4.5 %collective-permute-start.7 = (f32[8,128]{1,0:T(8,128)S(1)}, f32[8,128]{1,0:T(8,128)S(1)}, u32[]{:S(2)}, u32[]{:S(2)}) collective-permute-start(f32[8,128]{1,0:T(8,128)S(1)} %get-tuple-element.16.mine_ref), channel_id=1, source_target_pairs={{0,4},{1,5},{2,6},{3,7},{4,0},{5,1},{6,2},{7,3},{8,12},{9,13},{10,... | collective-permute-start | bytes 12296 | tf_op jit(solution)/shard_map/ppermute | solution.py:283
  30.6 6.1 %collective-permute-start.10 = (f32[8,128]{1,0:T(8,128)S(1)}, f32[8,128]{1,0:T(8,128)S(1)}, u32[]{:S(2)}, u32[]{:S(2)}) collective-permute-start(f32[8,128]{1,0:T(8,128)S(1)} %shard_map.97.mine_ref.refs_0_), channel_id=1, source_target_pairs={{0,3},{1,2},{2,1},{3,0},{4,7},{5,6},{6,5},{7,4},{8,11},{9,10},{10,... | collective-permute-start | bytes 12296 | tf_op jit(solution)/shard_map/ppermute | solution.py:283
  32.9 3.8 %collective-permute-start.9 = (f32[8,128]{1,0:T(8,128)S(1)}, f32[8,128]{1,0:T(8,128)S(1)}, u32[]{:S(2)}, u32[]{:S(2)}) collective-permute-start(f32[8,128]{1,0:T(8,128)S(1)} %shard_map.97.mine_ref.refs_0_), channel_id=1, source_target_pairs={{0,2},{1,3},{2,0},{3,1},{4,6},{5,7},{6,4},{7,5},{8,9},{9,8},{10,11... | collective-permute-start | bytes 12296 | tf_op jit(solution)/shard_map/ppermute | solution.py:283
  33.4 3.6 %collective-permute-start.8 = (f32[8,128]{1,0:T(8,128)S(1)}, f32[8,128]{1,0:T(8,128)S(1)}, u32[]{:S(2)}, u32[]{:S(2)}) collective-permute-start(f32[8,128]{1,0:T(8,128)S(1)} %shard_map.97.mine_ref.refs_0_), channel_id=1, source_target_pairs={{0,1},{1,0},{2,3},{3,2},{4,5},{5,4},{6,7},{7,6},{8,10},{9,11},{10,... | collective-permute-start | bytes 12296 | tf_op jit(solution)/shard_map/ppermute | solution.py:283
  37.9 7.4 %collective-permute-start.14 = (f16[16,4096]{1,0:T(8,128)(2,1)S(1)}, f16[16,4096]{1,0:T(8,128)(2,1)S(1)}, u32[]{:S(2)}, u32[]{:S(2)}) collective-permute-start(f16[16,4096]{1,0:T(8,128)(2,1)S(1)} %get-tuple-element.26), channel_id=1, source_target_pairs={{0,3},{1,2},{2,1},{3,0},{4,7},{5,6},{6,5},{7,4},{8,11},{9,10},{10,... | collective-permute-start | bytes 393224 | tf_op jit(solution)/shard_map/ppermute | solution.py:283
  39.9 9.1 %collective-permute-start.16 = (f16[16,4096]{1,0:T(8,128)(2,1)S(1)}, f16[16,4096]{1,0:T(8,128)(2,1)S(1)}, u32[]{:S(2)}, u32[]{:S(2)}) collective-permute-start(f16[16,4096]{1,0:T(8,128)(2,1)S(1)} %get-tuple-element.27), channel_id=1, source_target_pairs={{0,2},{1,3},{2,0},{3,1},{4,6},{5,7},{6,4},{7,5},{8,9},{9,8},{10,11... | collective-permute-start | bytes 393224 | tf_op jit(solution)/shard_map/ppermute | solution.py:283
  40.5 8.6 %collective-permute-start.15 = (f16[16,4096]{1,0:T(8,128)(2,1)S(1)}, f16[16,4096]{1,0:T(8,128)(2,1)S(1)}, u32[]{:S(2)}, u32[]{:S(2)}) collective-permute-start(f16[16,4096]{1,0:T(8,128)(2,1)S(1)} %get-tuple-element.28), channel_id=1, source_target_pairs={{0,1},{1,0},{2,3},{3,2},{4,5},{5,4},{6,7},{7,6},{8,10},{9,11},{10,... | collective-permute-start | bytes 393224 | tf_op jit(solution)/shard_map/ppermute | solution.py:283
  41.5 10.1 %copy-start.1 = (f32[128,2048]{1,0:T(8,128)S(1)}, f32[128,2048]{1,0:T(8,128)}, u32[]{:S(2)}) copy-start(f32[128,2048]{1,0:T(8,128)} %momentum_ref.1) | copy-start | bytes 3145732
  41.5 10.1 %copy-start.2 = (f32[128,2048]{1,0:T(8,128)S(1)}, f32[128,2048]{1,0:T(8,128)}, u32[]{:S(2)}) copy-start(f32[128,2048]{1,0:T(8,128)} %peer_ref.1) | copy-start | bytes 3145732
  41.6 10.0 %copy-start = (f32[128,2048]{1,0:T(8,128)S(1)}, f32[128,2048]{1,0:T(8,128)}, u32[]{:S(2)}) copy-start(f32[128,2048]{1,0:T(8,128)} %global_ref.1) | copy-start | bytes 3145732
  41.6 7.6 %collective-permute-start.11 = (f16[16,4096]{1,0:T(8,128)(2,1)S(1)}, f16[16,4096]{1,0:T(8,128)(2,1)S(1)}, u32[]{:S(2)}, u32[]{:S(2)}) collective-permute-start(f16[16,4096]{1,0:T(8,128)(2,1)S(1)} %get-tuple-element.24), channel_id=1, source_target_pairs={{0,1},{1,0},{2,3},{3,2},{4,5},{5,4},{6,7},{7,6},{8,10},{9,11},{10,... | collective-permute-start | bytes 393224 | tf_op jit(solution)/shard_map/ppermute | solution.py:283
  42.7 12.0 %collective-permute-start.13 = (f16[16,4096]{1,0:T(8,128)(2,1)S(1)}, f16[16,4096]{1,0:T(8,128)(2,1)S(1)}, u32[]{:S(2)}, u32[]{:S(2)}) collective-permute-start(f16[16,4096]{1,0:T(8,128)(2,1)S(1)} %get-tuple-element.25), channel_id=1, source_target_pairs={{0,1},{1,0},{2,3},{3,2},{4,5},{5,4},{6,7},{7,6},{8,10},{9,11},{10,... | collective-permute-start | bytes 393224 | tf_op jit(solution)/shard_map/ppermute | solution.py:283
  49.1 6.9 %collective-permute-start.17 = (f16[16,4096]{1,0:T(8,128)(2,1)S(1)}, f16[16,4096]{1,0:T(8,128)(2,1)S(1)}, u32[]{:S(2)}, u32[]{:S(2)}) collective-permute-start(f16[16,4096]{1,0:T(8,128)(2,1)S(1)} %fusion.2), channel_id=1, source_target_pairs={{0,4},{1,5},{2,6},{3,7},{4,0},{5,1},{6,2},{7,3},{8,12},{9,13},{10,... | collective-permute-start | bytes 393224 | tf_op jit(solution)/shard_map/ppermute | solution.py:283
  49.3 6.8 %collective-permute-start.12 = (f16[16,4096]{1,0:T(8,128)(2,1)S(1)}, f16[16,4096]{1,0:T(8,128)(2,1)S(1)}, u32[]{:S(2)}, u32[]{:S(2)}) collective-permute-start(f16[16,4096]{1,0:T(8,128)(2,1)S(1)} %fusion.3), channel_id=1, source_target_pairs={{0,2},{1,3},{2,0},{3,1},{4,6},{5,7},{6,4},{7,5},{8,9},{9,8},{10,11... | collective-permute-start | bytes 393224 | tf_op jit(solution)/shard_map/ppermute | solution.py:283

commit v22 on v20

--- a/solution.py
+++ b/solution.py
@@ -32,7 +32,7 @@
 
 
 PARTS = 8
-AHEAD = 6
+AHEAD = 5
 
 
 def head_copies(source, target, sems, first, last):
@@ -311,7 +311,7 @@
     y_near = moved([blocks[1]], 1)[0]
     z_near = moved([blocks[2] + relayed], 2)[0]
     sums = [blocks[0] + z_near + y_near]
-    sums += [blocks[i] + a + b + c for i, a, b, c in zip(far, three, one, two)]
+    sums += [blocks[i] + a + b + c for i, a, b, c in zip(far, three, two, one)]
     for step in far_steps()[::-1]:
         keep = len(sums) // 2
         sums = [a + b for a, b in zip(sums[:keep], moved(sums[keep:], step))]

time: 56.1 us -> 56.5 us (level)
  Pallas kernels: 22.3 us -> 22.9 us
    pallas_call x10, Pallas kernels: 19.2 us -> 19.8 us  [call(): pl.pallas_call(kernel, out_shape=outs, in_specs=[pl.BlockSpec(memory_spac...]
  transfers between devices with their start and end apart: 18 -> 18, of which waited for: 9 -> 8; matrix products, arithmetic and copies ran while one was open for 0% -> 0% of each run, Pallas kernels for 30% -> 31%
where the time goes in v22:
time: 56.5 us; the launch traced here: 56.4 us
  starting transfers between devices  25.2 us (45%)
  Pallas kernels  22.9 us (41%)
  waiting for transfers between devices  6.23 us (11%)
  other arithmetic  1.1 us (2%)
  between operations  0.8 us (1%)
    ppermute x18, starting transfers between devices, swap(): lax.ppermute(value, AXIS, [(i, i ^ step) for i in range(lax.axis_size(AXI...  25.2 us
    pallas_call x10, Pallas kernels, call(): pl.pallas_call(kernel, out_shape=outs, in_specs=[pl.BlockSpec(memory_spac...  19.8 us
    ppermute x18, waiting for transfers between devices, swap(): lax.ppermute(value, AXIS, [(i, i ^ step) for i in range(lax.axis_size(AXI...  6.23 us
    pallas_call x1, Pallas kernels, frag_update(): pl.pallas_call(functools.partial(frag_kernel, members), grid=(width // TI...  3.08 us
  transfers between devices with their start and end apart: 18, of which 8 were waited for; matrix products, arithmetic and copies ran while one was open for 0% of the time, Pallas kernels for 31%

profile of v22, /device:TPU:0, one launch (start us, length us, event | category | flops | bytes accessed | tf_op | source)
XLA Modules:
  0.0 56.4 jit_solution(14489260465078869081)
XLA Ops:
  0.6 0.9 %shard_map.93 = bf16[16,4224]{1,0:T(8,128)(2,1)S(1)} custom-call(s32[16]{0:T(128)} %targets.1, bf16[16,4096]{1,0:T(8,128)(2,1)} %rows.1), custom_call_target="tpu_custom_call" | custom-call | bytes 131136 | tf_op jit(solution)/shard_map/pallas_call | solution.py:22
  1.6 4.1 %collective-permute-start.3 = (bf16[16,4224]{1,0:T(8,128)(2,1)S(1)}, bf16[16,4224]{1,0:T(8,128)(2,1)S(1)}, u32[]{:S(2)}, u32[]{:S(2)}) collective-permute-start(bf16[16,4224]{1,0:T(8,128)(2,1)S(1)} %shard_map.93), channel_id=1, source_target_pairs={{0,4},{1,5},{2,6},{3,7},{4,0},{5,1},{6,2},{7,3},{8,12},{9,13},{10,... | collective-permute-start | bytes 405512 | tf_op jit(solution)/shard_map/ppermute | solution.py:269
  5.7 2.5 %collective-permute-start.2 = (bf16[16,4224]{1,0:T(8,128)(2,1)S(1)}, bf16[16,4224]{1,0:T(8,128)(2,1)S(1)}, u32[]{:S(2)}, u32[]{:S(2)}) collective-permute-start(bf16[16,4224]{1,0:T(8,128)(2,1)S(1)} %shard_map.93), channel_id=1, source_target_pairs={{0,3},{1,2},{2,1},{3,0},{4,7},{5,6},{6,5},{7,4},{8,11},{9,10},{10,... | collective-permute-start | bytes 405512 | tf_op jit(solution)/shard_map/ppermute | solution.py:269
  9.2 4.2 %shard_map.94.held_ref = bf16[4096,2048]{1,0:T(8,128)(2,1)S(1)} custom-call(bf16[4096,2048]{1,0:T(8,128)(2,1)} %head.3), custom_call_target="tpu_custom_call" | custom-call | bytes 16777216 | tf_op jit(solution)/shard_map/pallas_call | solution.py:22
  13.4 2.6 %collective-permute-start.6 = (bf16[16,4224]{1,0:T(8,128)(2,1)S(1)}, bf16[16,4224]{1,0:T(8,128)(2,1)S(1)}, u32[]{:S(2)}, u32[]{:S(2)}) collective-permute-start(bf16[16,4224]{1,0:T(8,128)(2,1)S(1)} %collective-permute-done.3), channel_id=1, source_target_pairs={{0,3},{1,2},{2,1},{3,0},{4,7},{5,6},{6,5},{7,4},{8,11},{9,10},{10,... | collective-permute-start | bytes 405512 | tf_op jit(solution)/shard_map/ppermute | solution.py:269
  16.4 0.5 collective-permute-start.4
  17.0 5.2 %shard_map.95 = (bf16[4096,2048]{1,0:T(8,128)(2,1)S(1)}, f32[64,2048]{1,0:T(8,128)S(1)}, bf16[128,2048]{1,0:T(8,128)(2,1)S(1)}, f32[64,128]{1,0:T(8,128)S(1)}) custom-call(bf16[64,4224]{1,0:T(8,128)(2,1)S(1)} %pad_maximum_fusion.packed_ref.rows_one_ref.ids_one_ref, bf16[4096,2048]{1,0:T(8,128)(2,1)} %head.3, ...), custom_call_target="tpu_custom_call", output_to_operand_aliasing={{0}: (2, {})} | custom-call | flops 1073741824 | bytes 34095104 | tf_op jit(solution)/shard_map/pallas_call | solution.py:22
  22.3 3.6 %shard_map.96 = (f32[64,2048]{1,0:T(8,128)S(1)}, bf16[128,2048]{1,0:T(8,128)(2,1)S(1)}, f32[8,128]{1,0:T(8,128)S(1)}) custom-call(bf16[64,4224]{1,0:T(8,128)(2,1)S(1)} %bitcast.5, bf16[4096,2048]{1,0:T(8,128)(2,1)S(1)} %get-tuple-element.14.near_ref.head_ref, f32[64,128]{1,0:T(8,128)S(1)} %get-tuple-element.15.before_ref), custom_call_target="tpu_custom_call" | custom-call | flops 1073741824 | bytes 17350656 | tf_op jit(solution)/shard_map/pallas_call | solution.py:22
  25.9 1.8 %collective-permute-start.7 = (f32[8,128]{1,0:T(8,128)S(1)}, f32[8,128]{1,0:T(8,128)S(1)}, u32[]{:S(2)}, u32[]{:S(2)}) collective-permute-start(f32[8,128]{1,0:T(8,128)S(1)} %get-tuple-element.16.mine_ref), channel_id=1, source_target_pairs={{0,4},{1,5},{2,6},{3,7},{4,0},{5,1},{6,2},{7,3},{8,12},{9,13},{10,... | collective-permute-start | bytes 12296 | tf_op jit(solution)/shard_map/ppermute | solution.py:269
  27.7 2.5 %shard_map.100.refs_0_ = f32[256,2048]{1,0:T(8,128)S(1)} custom-call(bf16[128,2048]{1,0:T(8,128)(2,1)S(1)} %get-tuple-element.20.one_ref, bf16[128,2048]{1,0:T(8,128)(2,1)S(1)} %get-tuple-element.21.two_ref, bf16[4096,2048]{1,0:T(8,128)(2,1)S(1)} %get-tuple-element.14.near_ref.head_ref), custom_call_target="tpu_custom_call" | custom-call | flops 2147483648 | bytes 17825792 | tf_op jit(solution)/shard_map/pallas_call | solution.py:22
  30.5 2.6 %collective-permute-start.10 = (f32[8,128]{1,0:T(8,128)S(1)}, f32[8,128]{1,0:T(8,128)S(1)}, u32[]{:S(2)}, u32[]{:S(2)}) collective-permute-start(f32[8,128]{1,0:T(8,128)S(1)} %shard_map.97.mine_ref.refs_0_), channel_id=1, source_target_pairs={{0,3},{1,2},{2,1},{3,0},{4,7},{5,6},{6,5},{7,4},{8,11},{9,10},{10,... | collective-permute-start | bytes 12296 | tf_op jit(solution)/shard_map/ppermute | solution.py:269
  34.1 2.5 %shard_map.101.refs_1_ = f32[256,2048]{1,0:T(8,128)S(1)} custom-call(bf16[128,2048]{1,0:T(8,128)(2,1)S(1)} %get-tuple-element.20.one_ref, bf16[128,2048]{1,0:T(8,128)(2,1)S(1)} %get-tuple-element.21.two_ref, bf16[4096,2048]{1,0:T(8,128)(2,1)S(1)} %get-tuple-element.14.near_ref.head_ref, f32[8,128]{1,0:T(8,128)S(1)} %shard_map.97.mine_ref.refs_0_), custom_call_target="tpu_custom_call" | custom-call | flops 2147483648 | bytes 17829888 | tf_op jit(solution)/shard_map/pallas_call | solution.py:22
  38.1 2.1 %collective-permute-start.14 = (f16[16,4096]{1,0:T(8,128)(2,1)S(1)}, f16[16,4096]{1,0:T(8,128)(2,1)S(1)}, u32[]{:S(2)}, u32[]{:S(2)}) collective-permute-start(f16[16,4096]{1,0:T(8,128)(2,1)S(1)} %get-tuple-element.26), channel_id=1, source_target_pairs={{0,3},{1,2},{2,1},{3,0},{4,7},{5,6},{6,5},{7,4},{8,11},{9,10},{10,... | collective-permute-start | bytes 393224 | tf_op jit(solution)/shard_map/ppermute | solution.py:269
  40.2 1.0 %collective-permute-start.16 = (f16[16,4096]{1,0:T(8,128)(2,1)S(1)}, f16[16,4096]{1,0:T(8,128)(2,1)S(1)}, u32[]{:S(2)}, u32[]{:S(2)}) collective-permute-start(f16[16,4096]{1,0:T(8,128)(2,1)S(1)} %get-tuple-element.27), channel_id=1, source_target_pairs={{0,1},{1,0},{2,3},{3,2},{4,5},{5,4},{6,7},{7,6},{8,9},{9,8},{10,11... | collective-permute-start | bytes 393224 | tf_op jit(solution)/shard_map/ppermute | solution.py:269
  41.8 1.1 %collective-permute-start.11 = (f16[16,4096]{1,0:T(8,128)(2,1)S(1)}, f16[16,4096]{1,0:T(8,128)(2,1)S(1)}, u32[]{:S(2)}, u32[]{:S(2)}) collective-permute-start(f16[16,4096]{1,0:T(8,128)(2,1)S(1)} %get-tuple-element.24), channel_id=1, source_target_pairs={{0,1},{1,0},{2,3},{3,2},{4,5},{5,4},{6,7},{7,6},{8,9},{9,8},{10,11... | collective-permute-start | bytes 393224 | tf_op jit(solution)/shard_map/ppermute | solution.py:269
  42.8 1.0 %collective-permute-start.13 = (f16[16,4096]{1,0:T(8,128)(2,1)S(1)}, f16[16,4096]{1,0:T(8,128)(2,1)S(1)}, u32[]{:S(2)}, u32[]{:S(2)}) collective-permute-start(f16[16,4096]{1,0:T(8,128)(2,1)S(1)} %get-tuple-element.25), channel_id=1, source_target_pairs={{0,1},{1,0},{2,3},{3,2},{4,5},{5,4},{6,7},{7,6},{8,9},{9,8},{10,11... | collective-permute-start | bytes 393224 | tf_op jit(solution)/shard_map/ppermute | solution.py:269
  43.9 1.5 %collective-permute-done.14 = f16[16,4096]{1,0:T(8,128)(2,1)S(1)} collective-permute-done((f16[16,4096]{1,0:T(8,128)(2,1)S(1)}, f16[16,4096]{1,0:T(8,128)(2,1)S(1)}, u32[]{:S(2)}, u32[]{:S(2)}) %collective-permute-start.14) | collective-permute-done | bytes 131104 | tf_op jit(solution)/shard_map/ppermute | solution.py:269
  45.3 2.1 %collective-permute-done.16 = f16[16,4096]{1,0:T(8,128)(2,1)S(1)} collective-permute-done((f16[16,4096]{1,0:T(8,128)(2,1)S(1)}, f16[16,4096]{1,0:T(8,128)(2,1)S(1)}, u32[]{:S(2)}, u32[]{:S(2)}) %collective-permute-start.16) | collective-permute-done | bytes 131104 | tf_op jit(solution)/shard_map/ppermute | solution.py:269
  47.5 1.6 %collective-permute-start.17 = (f16[16,4096]{1,0:T(8,128)(2,1)S(1)}, f16[16,4096]{1,0:T(8,128)(2,1)S(1)}, u32[]{:S(2)}, u32[]{:S(2)}) collective-permute-start(f16[16,4096]{1,0:T(8,128)(2,1)S(1)} %fusion.2), channel_id=1, source_target_pairs={{0,4},{1,5},{2,6},{3,7},{4,0},{5,1},{6,2},{7,3},{8,12},{9,13},{10,... | collective-permute-start | bytes 393224 | tf_op jit(solution)/shard_map/ppermute | solution.py:269
  49.7 1.5 %collective-permute-start.12 = (f16[16,4096]{1,0:T(8,128)(2,1)S(1)}, f16[16,4096]{1,0:T(8,128)(2,1)S(1)}, u32[]{:S(2)}, u32[]{:S(2)}) collective-permute-start(f16[16,4096]{1,0:T(8,128)(2,1)S(1)} %fusion.3), channel_id=1, source_target_pairs={{0,2},{1,3},{2,0},{3,1},{4,6},{5,7},{6,4},{7,5},{8,10},{9,11},{10,... | collective-permute-start | bytes 393224 | tf_op jit(solution)/shard_map/ppermute | solution.py:269
  51.2 3.1 %shard_map.99 = (f32[128,2048]{1,0:T(8,128)}, f32[128,2048]{1,0:T(8,128)}, f32[1]{0:T(128)}) custom-call(bf16[64,4224]{1,0:T(8,128)(2,1)S(1)} %pad_maximum_fusion.packed_ref.rows_one_ref.ids_one_ref, bf16[64,4224]{1,0:T(8,128)(2,1)S(1)} %bitcast.6, bf16[64,4224]{1,0:T(8,128)(2,1)S(1)} %pad_maximum_fusion.packed_ref.rows_one_ref.ids_one_ref, ...), custom_call_target="tpu_custom_call" | custom-call | flops 67108864 | bytes 6291456 | tf_op jit(solution)/shard_map/pallas_call | solution.py:244
  54.3 0.7 %collective-permute-done.17 = f16[16,4096]{1,0:T(8,128)(2,1)S(1)} collective-permute-done((f16[16,4096]{1,0:T(8,128)(2,1)S(1)}, f16[16,4096]{1,0:T(8,128)(2,1)S(1)}, u32[]{:S(2)}, u32[]{:S(2)}) %collective-permute-start.17) | collective-permute-done | bytes 131104 | tf_op jit(solution)/shard_map/ppermute | solution.py:269
  55.0 0.6 %collective-permute-done.12 = f16[16,4096]{1,0:T(8,128)(2,1)S(1)} collective-permute-done((f16[16,4096]{1,0:T(8,128)(2,1)S(1)}, f16[16,4096]{1,0:T(8,128)(2,1)S(1)}, u32[]{:S(2)}, u32[]{:S(2)}) %collective-permute-start.12) | collective-permute-done | bytes 131104 | tf_op jit(solution)/shard_map/ppermute | solution.py:269
  55.6 0.7 %fusion.7 = bf16[16,4096]{1,0:T(8,128)(2,1)} fusion(f32[64,4096]{1,0:T(8,128)S(1)} %shard_map.102, f16[16,4096]{1,0:T(8,128)(2,1)S(1)} %collective-permute-done.17, f16[16,4096]{1,0:T(8,128)(2,1)S(1)} %collective-permute-done.13, f16[16,4096]{1,0:T(8,128)(2,1)S(1)} %collective-permute-done.12), kind=kLoop, calls=%fused_computation.12 | loop fusion | flops 524288 | bytes 786432 | tf_op jit(solution)/shard_map/convert_element_type | solution.py:380
  (38 shorter events, 5.5 us)
Async XLA Ops:
  1.6 11.8 %collective-permute-start.3 = (bf16[16,4224]{1,0:T(8,128)(2,1)S(1)}, bf16[16,4224]{1,0:T(8,128)(2,1)S(1)}, u32[]{:S(2)}, u32[]{:S(2)}) collective-permute-start(bf16[16,4224]{1,0:T(8,128)(2,1)S(1)} %shard_map.93), channel_id=1, source_target_pairs={{0,4},{1,5},{2,6},{3,7},{4,0},{5,1},{6,2},{7,3},{8,12},{9,13},{10,... | collective-permute-start | bytes 405512 | tf_op jit(solution)/shard_map/ppermute | solution.py:269
  5.7 10.8 %collective-permute-start.2 = (bf16[16,4224]{1,0:T(8,128)(2,1)S(1)}, bf16[16,4224]{1,0:T(8,128)(2,1)S(1)}, u32[]{:S(2)}, u32[]{:S(2)}) collective-permute-start(bf16[16,4224]{1,0:T(8,128)(2,1)S(1)} %shard_map.93), channel_id=1, source_target_pairs={{0,3},{1,2},{2,1},{3,0},{4,7},{5,6},{6,5},{7,4},{8,11},{9,10},{10,... | collective-permute-start | bytes 405512 | tf_op jit(solution)/shard_map/ppermute | solution.py:269
  8.2 8.7 %collective-permute-start.1 = (bf16[16,4224]{1,0:T(8,128)(2,1)S(1)}, bf16[16,4224]{1,0:T(8,128)(2,1)S(1)}, u32[]{:S(2)}, u32[]{:S(2)}) collective-permute-start(bf16[16,4224]{1,0:T(8,128)(2,1)S(1)} %shard_map.93), channel_id=1, source_target_pairs={{0,2},{1,3},{2,0},{3,1},{4,6},{5,7},{6,4},{7,5},{8,10},{9,11},{10,... | collective-permute-start | bytes 405512 | tf_op jit(solution)/shard_map/ppermute | solution.py:269
  8.6 8.3 %collective-permute-start = (bf16[16,4224]{1,0:T(8,128)(2,1)S(1)}, bf16[16,4224]{1,0:T(8,128)(2,1)S(1)}, u32[]{:S(2)}, u32[]{:S(2)}) collective-permute-start(bf16[16,4224]{1,0:T(8,128)(2,1)S(1)} %shard_map.93), channel_id=1, source_target_pairs={{0,1},{1,0},{2,3},{3,2},{4,5},{5,4},{6,7},{7,6},{8,9},{9,8},{10,11... | collective-permute-start | bytes 405512 | tf_op jit(solution)/shard_map/ppermute | solution.py:269
  13.4 8.8 %collective-permute-start.6 = (bf16[16,4224]{1,0:T(8,128)(2,1)S(1)}, bf16[16,4224]{1,0:T(8,128)(2,1)S(1)}, u32[]{:S(2)}, u32[]{:S(2)}) collective-permute-start(bf16[16,4224]{1,0:T(8,128)(2,1)S(1)} %collective-permute-done.3), channel_id=1, source_target_pairs={{0,3},{1,2},{2,1},{3,0},{4,7},{5,6},{6,5},{7,4},{8,11},{9,10},{10,... | collective-permute-start | bytes 405512 | tf_op jit(solution)/shard_map/ppermute | solution.py:269
  16.0 6.2 %collective-permute-start.5 = (bf16[16,4224]{1,0:T(8,128)(2,1)S(1)}, bf16[16,4224]{1,0:T(8,128)(2,1)S(1)}, u32[]{:S(2)}, u32[]{:S(2)}) collective-permute-start(bf16[16,4224]{1,0:T(8,128)(2,1)S(1)} %collective-permute-done.3), channel_id=1, source_target_pairs={{0,2},{1,3},{2,0},{3,1},{4,6},{5,7},{6,4},{7,5},{8,10},{9,11},{10,... | collective-permute-start | bytes 405512 | tf_op jit(solution)/shard_map/ppermute | solution.py:269
  16.4 5.8 %collective-permute-start.4 = (bf16[16,4224]{1,0:T(8,128)(2,1)S(1)}, bf16[16,4224]{1,0:T(8,128)(2,1)S(1)}, u32[]{:S(2)}, u32[]{:S(2)}) collective-permute-start(bf16[16,4224]{1,0:T(8,128)(2,1)S(1)} %collective-permute-done.3), channel_id=1, source_target_pairs={{0,1},{1,0},{2,3},{3,2},{4,5},{5,4},{6,7},{7,6},{8,9},{9,8},{10,11... | collective-permute-start | bytes 405512 | tf_op jit(solution)/shard_map/ppermute | solution.py:269
  25.9 4.5 %collective-permute-start.7 = (f32[8,128]{1,0:T(8,128)S(1)}, f32[8,128]{1,0:T(8,128)S(1)}, u32[]{:S(2)}, u32[]{:S(2)}) collective-permute-start(f32[8,128]{1,0:T(8,128)S(1)} %get-tuple-element.16.mine_ref), channel_id=1, source_target_pairs={{0,4},{1,5},{2,6},{3,7},{4,0},{5,1},{6,2},{7,3},{8,12},{9,13},{10,... | collective-permute-start | bytes 12296 | tf_op jit(solution)/shard_map/ppermute | solution.py:269
  30.5 6.1 %collective-permute-start.10 = (f32[8,128]{1,0:T(8,128)S(1)}, f32[8,128]{1,0:T(8,128)S(1)}, u32[]{:S(2)}, u32[]{:S(2)}) collective-permute-start(f32[8,128]{1,0:T(8,128)S(1)} %shard_map.97.mine_ref.refs_0_), channel_id=1, source_target_pairs={{0,3},{1,2},{2,1},{3,0},{4,7},{5,6},{6,5},{7,4},{8,11},{9,10},{10,... | collective-permute-start | bytes 12296 | tf_op jit(solution)/shard_map/ppermute | solution.py:269
  33.1 3.6 %collective-permute-start.9 = (f32[8,128]{1,0:T(8,128)S(1)}, f32[8,128]{1,0:T(8,128)S(1)}, u32[]{:S(2)}, u32[]{:S(2)}) collective-permute-start(f32[8,128]{1,0:T(8,128)S(1)} %shard_map.97.mine_ref.refs_0_), channel_id=1, source_target_pairs={{0,2},{1,3},{2,0},{3,1},{4,6},{5,7},{6,4},{7,5},{8,10},{9,11},{10,... | collective-permute-start | bytes 12296 | tf_op jit(solution)/shard_map/ppermute | solution.py:269
  33.6 3.6 %collective-permute-start.8 = (f32[8,128]{1,0:T(8,128)S(1)}, f32[8,128]{1,0:T(8,128)S(1)}, u32[]{:S(2)}, u32[]{:S(2)}) collective-permute-start(f32[8,128]{1,0:T(8,128)S(1)} %shard_map.97.mine_ref.refs_0_), channel_id=1, source_target_pairs={{0,1},{1,0},{2,3},{3,2},{4,5},{5,4},{6,7},{7,6},{8,9},{9,8},{10,11... | collective-permute-start | bytes 12296 | tf_op jit(solution)/shard_map/ppermute | solution.py:269
  38.1 7.2 %collective-permute-start.14 = (f16[16,4096]{1,0:T(8,128)(2,1)S(1)}, f16[16,4096]{1,0:T(8,128)(2,1)S(1)}, u32[]{:S(2)}, u32[]{:S(2)}) collective-permute-start(f16[16,4096]{1,0:T(8,128)(2,1)S(1)} %get-tuple-element.26), channel_id=1, source_target_pairs={{0,3},{1,2},{2,1},{3,0},{4,7},{5,6},{6,5},{7,4},{8,11},{9,10},{10,... | collective-permute-start | bytes 393224 | tf_op jit(solution)/shard_map/ppermute | solution.py:269
  40.2 7.3 %collective-permute-start.16 = (f16[16,4096]{1,0:T(8,128)(2,1)S(1)}, f16[16,4096]{1,0:T(8,128)(2,1)S(1)}, u32[]{:S(2)}, u32[]{:S(2)}) collective-permute-start(f16[16,4096]{1,0:T(8,128)(2,1)S(1)} %get-tuple-element.27), channel_id=1, source_target_pairs={{0,1},{1,0},{2,3},{3,2},{4,5},{5,4},{6,7},{7,6},{8,9},{9,8},{10,11... | collective-permute-start | bytes 393224 | tf_op jit(solution)/shard_map/ppermute | solution.py:269
  41.2 6.3 %collective-permute-start.15 = (f16[16,4096]{1,0:T(8,128)(2,1)S(1)}, f16[16,4096]{1,0:T(8,128)(2,1)S(1)}, u32[]{:S(2)}, u32[]{:S(2)}) collective-permute-start(f16[16,4096]{1,0:T(8,128)(2,1)S(1)} %get-tuple-element.28), channel_id=1, source_target_pairs={{0,2},{1,3},{2,0},{3,1},{4,6},{5,7},{6,4},{7,5},{8,10},{9,11},{10,... | collective-permute-start | bytes 393224 | tf_op jit(solution)/shard_map/ppermute | solution.py:269
  41.6 9.6 %copy-start.1 = (f32[128,2048]{1,0:T(8,128)S(1)}, f32[128,2048]{1,0:T(8,128)}, u32[]{:S(2)}) copy-start(f32[128,2048]{1,0:T(8,128)} %momentum_ref.1) | copy-start | bytes 3145732
  41.7 9.6 %copy-start.2 = (f32[128,2048]{1,0:T(8,128)S(1)}, f32[128,2048]{1,0:T(8,128)}, u32[]{:S(2)}) copy-start(f32[128,2048]{1,0:T(8,128)} %peer_ref.1) | copy-start | bytes 3145732
  41.7 9.5 %copy-start = (f32[128,2048]{1,0:T(8,128)S(1)}, f32[128,2048]{1,0:T(8,128)}, u32[]{:S(2)}) copy-start(f32[128,2048]{1,0:T(8,128)} %global_ref.1) | copy-start | bytes 3145732
  41.8 7.9 %collective-permute-start.11 = (f16[16,4096]{1,0:T(8,128)(2,1)S(1)}, f16[16,4096]{1,0:T(8,128)(2,1)S(1)}, u32[]{:S(2)}, u32[]{:S(2)}) collective-permute-start(f16[16,4096]{1,0:T(8,128)(2,1)S(1)} %get-tuple-element.24), channel_id=1, source_target_pairs={{0,1},{1,0},{2,3},{3,2},{4,5},{5,4},{6,7},{7,6},{8,9},{9,8},{10,11... | collective-permute-start | bytes 393224 | tf_op jit(solution)/shard_map/ppermute | solution.py:269
  42.8 11.5 %collective-permute-start.13 = (f16[16,4096]{1,0:T(8,128)(2,1)S(1)}, f16[16,4096]{1,0:T(8,128)(2,1)S(1)}, u32[]{:S(2)}, u32[]{:S(2)}) collective-permute-start(f16[16,4096]{1,0:T(8,128)(2,1)S(1)} %get-tuple-element.25), channel_id=1, source_target_pairs={{0,1},{1,0},{2,3},{3,2},{4,5},{5,4},{6,7},{7,6},{8,9},{9,8},{10,11... | collective-permute-start | bytes 393224 | tf_op jit(solution)/shard_map/ppermute | solution.py:269
  47.5 7.4 %collective-permute-start.17 = (f16[16,4096]{1,0:T(8,128)(2,1)S(1)}, f16[16,4096]{1,0:T(8,128)(2,1)S(1)}, u32[]{:S(2)}, u32[]{:S(2)}) collective-permute-start(f16[16,4096]{1,0:T(8,128)(2,1)S(1)} %fusion.2), channel_id=1, source_target_pairs={{0,4},{1,5},{2,6},{3,7},{4,0},{5,1},{6,2},{7,3},{8,12},{9,13},{10,... | collective-permute-start | bytes 393224 | tf_op jit(solution)/shard_map/ppermute | solution.py:269
  49.7 5.9 %collective-permute-start.12 = (f16[16,4096]{1,0:T(8,128)(2,1)S(1)}, f16[16,4096]{1,0:T(8,128)(2,1)S(1)}, u32[]{:S(2)}, u32[]{:S(2)}) collective-permute-start(f16[16,4096]{1,0:T(8,128)(2,1)S(1)} %fusion.3), channel_id=1, source_target_pairs={{0,2},{1,3},{2,0},{3,1},{4,6},{5,7},{6,4},{7,5},{8,10},{9,11},{10,... | collective-permute-start | bytes 393224 | tf_op jit(solution)/shard_map/ppermute | solution.py:269

commit v23 on v20

--- a/solution.py
+++ b/solution.py
@@ -53,7 +53,7 @@
 
 
 TILE = 1024
-WIDE = 1024
+WIDE = 2048
 
 
 def pack_kernel(targets, rows, out_ref, targets_ref, sems):
@@ -180,34 +180,32 @@
 
 def grad_kernel(first, one_ref, two_ref, near_ref, *refs):
     terms_ref = refs[-1]
-    tile = min(terms_ref.shape[1], 2**19 // (one_ref.shape[0] + two_ref.shape[0]))
-    both = jnp.concatenate([one_ref[...], two_ref[...]], axis=0)
-    for place in range(0, terms_ref.shape[1], tile):
-        turned = lax.dot_general(
+    one, two = one_ref.shape[0] // 2, two_ref.shape[0] // 2
+    both = jnp.concatenate([one_ref[:one], two_ref[:two], one_ref[one:], two_ref[two:]], axis=0)
+    tile = min(terms_ref.shape[0], 2**19 // both.shape[0])
+    for place in range(0, terms_ref.shape[0], tile):
+        terms_ref[pl.ds(place, tile), :] = lax.dot_general(
             near_ref[pl.ds(first + place, tile), :], both, (((1,), (1,)), ((), ())),
             preferred_element_type=jnp.float32,
         )
-        terms_ref[:, pl.ds(place, tile)] = turned.T
-
-
-def join_kernel(scale, first, lines_ref, mine_ref, *refs):
-    *terms_refs, out_ref = refs
+
+
+def join_kernel(scale, lines_ref, mine_ref, *refs):
+    *terms_refs, far_ref, near_ref = refs
     rows = mine_ref.shape[1]
+    near = near_ref.shape[0]
     top, total = lines_ref[0:1, :], lines_ref[1:2, :]
-    soft = as_columns(jnp.exp(mine_ref[0:1, :] - top) / (total * rows)) * scale
+    soft = jnp.exp(mine_ref[0:1, :] - top) / (total * rows) * scale
     hard = (jnp.exp(mine_ref[2:3, :] - top) / total - 1.0) / rows
-    hard = as_columns(hard.astype(jnp.bfloat16).astype(jnp.float32)) * scale
-
-    count = out_ref.shape[0]
-    chunk = min(count, 64)
+    hard = hard.astype(jnp.bfloat16).astype(jnp.float32) * scale
+    tile = 512
     for place, terms_ref in enumerate(terms_refs):
-        columns = pl.ds(place * terms_ref.shape[1], terms_ref.shape[1])
-        for i in range(0, count, chunk):
-            part = slice(first + i, first + i + chunk)
-            out_ref[pl.ds(i, chunk), columns] = (
-                soft[part] * terms_ref[pl.ds(2 * first + i, chunk), :]
-                + hard[part] * terms_ref[pl.ds(2 * first + count + i, chunk), :]
-            )
+        for first in range(0, terms_ref.shape[0], tile):
+            part = pl.ds(first, tile)
+            value = (soft * terms_ref[part, :rows] + hard * terms_ref[part, rows:]).T
+            columns = pl.ds(place * terms_ref.shape[0] + first, tile)
+            near_ref[:, columns] = value[:near]
+            far_ref[:, columns] = value[near:]
 
 
 def frag_kernel(members, rows_one_ref, rows_two_ref, ids_one_ref, ids_two_ref, lines_ref, one_ref, two_ref, head_ref,
@@ -363,19 +361,17 @@
     terms = [
         call(
             functools.partial(grad_kernel, first),
-            [((2 * rows, depth // 2), jnp.float32)], [both_near, both_far, near, *after],
+            [((depth // 2, 2 * rows), jnp.float32)], [both_near, both_far, near, *after],
             2 * rows * depth * width,
         )[0]
         for first, after in ((0, []), (depth // 2, [before]))
     ]
 
     scale = 2.0**14 * rows
-    grads_far, grads_near = (
-        call(
-            functools.partial(join_kernel, scale, first),
-            [((count, depth), jnp.float32)], [lines, mine] + terms,
-        )[0]
-        for first, count in ((4 * own, rows - 4 * own), (0, 4 * own))
+    grads_far, grads_near = call(
+        functools.partial(join_kernel, scale),
+        [((rows - 4 * own, depth), jnp.float32), ((4 * own, depth), jnp.float32)],
+        [lines, mine] + terms,
     )
     hidden_grad = (scatter_sums(grads_near, grads_far, own) * (1.0 / scale)).astype(jnp.bfloat16)
     new_global, new_momentum, loss = frag_update(

time: 56.1 us -> 55.9 us (level)
    pallas_call x10 -> x9, Pallas kernels: 19.2 us -> 19.2 us  [call(): pl.pallas_call(kernel, out_shape=outs, in_specs=[pl.BlockSpec(memory_spac...]
where the time goes in v23:
time: 55.9 us; the launch traced here: 55.7 us
  starting transfers between devices  25.5 us (46%)
  Pallas kernels  22.3 us (40%)
  waiting for transfers between devices  6.01 us (11%)
  other arithmetic  1.09 us (2%)
  between operations  0.78 us (1%)
    ppermute x18, starting transfers between devices, swap(): lax.ppermute(value, AXIS, [(i, i ^ step) for i in range(lax.axis_size(AXI...  25.5 us
    pallas_call x9, Pallas kernels, call(): pl.pallas_call(kernel, out_shape=outs, in_specs=[pl.BlockSpec(memory_spac...  19.2 us
    ppermute x18, waiting for transfers between devices, swap(): lax.ppermute(value, AXIS, [(i, i ^ step) for i in range(lax.axis_size(AXI...  6.01 us
    pallas_call x1, Pallas kernels, frag_update(): pl.pallas_call(functools.partial(frag_kernel, members), grid=(width // TI...  3.08 us
  transfers between devices with their start and end apart: 18, of which 9 were waited for; matrix products, arithmetic and copies ran while one was open for 0% of the time, Pallas kernels for 30%

profile of v23, /device:TPU:0, one launch (start us, length us, event | category | flops | bytes accessed | tf_op | source)
XLA Modules:
  0.0 55.7 jit_solution(11760966840762361116)
XLA Ops:
  0.6 0.9 %shard_map.93 = bf16[16,4224]{1,0:T(8,128)(2,1)S(1)} custom-call(s32[16]{0:T(128)} %targets.1, bf16[16,4096]{1,0:T(8,128)(2,1)} %rows.1), custom_call_target="tpu_custom_call" | custom-call | bytes 131136 | tf_op jit(solution)/shard_map/pallas_call | solution.py:22
  1.6 4.1 %collective-permute-start.3 = (bf16[16,4224]{1,0:T(8,128)(2,1)S(1)}, bf16[16,4224]{1,0:T(8,128)(2,1)S(1)}, u32[]{:S(2)}, u32[]{:S(2)}) collective-permute-start(bf16[16,4224]{1,0:T(8,128)(2,1)S(1)} %shard_map.93), channel_id=1, source_target_pairs={{0,4},{1,5},{2,6},{3,7},{4,0},{5,1},{6,2},{7,3},{8,12},{9,13},{10,... | collective-permute-start | bytes 405512 | tf_op jit(solution)/shard_map/ppermute | solution.py:267
  5.7 2.5 %collective-permute-start.2 = (bf16[16,4224]{1,0:T(8,128)(2,1)S(1)}, bf16[16,4224]{1,0:T(8,128)(2,1)S(1)}, u32[]{:S(2)}, u32[]{:S(2)}) collective-permute-start(bf16[16,4224]{1,0:T(8,128)(2,1)S(1)} %shard_map.93), channel_id=1, source_target_pairs={{0,3},{1,2},{2,1},{3,0},{4,7},{5,6},{6,5},{7,4},{8,11},{9,10},{10,... | collective-permute-start | bytes 405512 | tf_op jit(solution)/shard_map/ppermute | solution.py:267
  9.2 4.8 %shard_map.94.held_ref = bf16[4096,2048]{1,0:T(8,128)(2,1)S(1)} custom-call(bf16[4096,2048]{1,0:T(8,128)(2,1)} %head.3), custom_call_target="tpu_custom_call" | custom-call | bytes 16777216 | tf_op jit(solution)/shard_map/pallas_call | solution.py:22
  14.0 2.6 %collective-permute-start.6 = (bf16[16,4224]{1,0:T(8,128)(2,1)S(1)}, bf16[16,4224]{1,0:T(8,128)(2,1)S(1)}, u32[]{:S(2)}, u32[]{:S(2)}) collective-permute-start(bf16[16,4224]{1,0:T(8,128)(2,1)S(1)} %collective-permute-done.3), channel_id=1, source_target_pairs={{0,3},{1,2},{2,1},{3,0},{4,7},{5,6},{6,5},{7,4},{8,11},{9,10},{10,... | collective-permute-start | bytes 405512 | tf_op jit(solution)/shard_map/ppermute | solution.py:267
  17.6 4.0 %shard_map.95 = (bf16[4096,2048]{1,0:T(8,128)(2,1)S(1)}, f32[64,2048]{1,0:T(8,128)S(1)}, bf16[128,2048]{1,0:T(8,128)(2,1)S(1)}, f32[64,128]{1,0:T(8,128)S(1)}) custom-call(bf16[64,4224]{1,0:T(8,128)(2,1)S(1)} %pad_maximum_fusion.packed_ref.rows_one_ref.ids_one_ref, bf16[4096,2048]{1,0:T(8,128)(2,1)} %head.3, ...), custom_call_target="tpu_custom_call", output_to_operand_aliasing={{0}: (2, {})} | custom-call | flops 1073741824 | bytes 34095104 | tf_op jit(solution)/shard_map/pallas_call | solution.py:22
  22.2 3.7 %shard_map.96 = (f32[64,2048]{1,0:T(8,128)S(1)}, bf16[128,2048]{1,0:T(8,128)(2,1)S(1)}, f32[8,128]{1,0:T(8,128)S(1)}) custom-call(bf16[64,4224]{1,0:T(8,128)(2,1)S(1)} %bitcast.5, bf16[4096,2048]{1,0:T(8,128)(2,1)S(1)} %get-tuple-element.16.near_ref.head_ref, f32[64,128]{1,0:T(8,128)S(1)} %get-tuple-element.17.before_ref), custom_call_target="tpu_custom_call" | custom-call | flops 1073741824 | bytes 17350656 | tf_op jit(solution)/shard_map/pallas_call | solution.py:22
  25.9 1.8 %collective-permute-start.7 = (f32[8,128]{1,0:T(8,128)S(1)}, f32[8,128]{1,0:T(8,128)S(1)}, u32[]{:S(2)}, u32[]{:S(2)}) collective-permute-start(f32[8,128]{1,0:T(8,128)S(1)} %get-tuple-element.18.mine_ref), channel_id=1, source_target_pairs={{0,4},{1,5},{2,6},{3,7},{4,0},{5,1},{6,2},{7,3},{8,12},{9,13},{10,... | collective-permute-start | bytes 12296 | tf_op jit(solution)/shard_map/ppermute | solution.py:267
  27.7 2.5 %shard_map.100.refs_0_ = f32[2048,256]{1,0:T(8,128)S(1)} custom-call(bf16[128,2048]{1,0:T(8,128)(2,1)S(1)} %get-tuple-element.22.one_ref, bf16[128,2048]{1,0:T(8,128)(2,1)S(1)} %get-tuple-element.23.two_ref, bf16[4096,2048]{1,0:T(8,128)(2,1)S(1)} %get-tuple-element.16.near_ref.head_ref), custom_call_target="tpu_custom_call" | custom-call | flops 2147483648 | bytes 17825792 | tf_op jit(solution)/shard_map/pallas_call | solution.py:22
  30.5 2.5 %collective-permute-start.10 = (f32[8,128]{1,0:T(8,128)S(1)}, f32[8,128]{1,0:T(8,128)S(1)}, u32[]{:S(2)}, u32[]{:S(2)}) collective-permute-start(f32[8,128]{1,0:T(8,128)S(1)} %shard_map.97.mine_ref.refs_0_), channel_id=1, source_target_pairs={{0,3},{1,2},{2,1},{3,0},{4,7},{5,6},{6,5},{7,4},{8,11},{9,10},{10,... | collective-permute-start | bytes 12296 | tf_op jit(solution)/shard_map/ppermute | solution.py:267
  33.5 0.6 %collective-permute-start.8 = (f32[8,128]{1,0:T(8,128)S(1)}, f32[8,128]{1,0:T(8,128)S(1)}, u32[]{:S(2)}, u32[]{:S(2)}) collective-permute-start(f32[8,128]{1,0:T(8,128)S(1)} %shard_map.97.mine_ref.refs_0_), channel_id=1, source_target_pairs={{0,1},{1,0},{2,3},{3,2},{4,5},{5,4},{6,7},{7,6},{8,9},{9,8},{10,11... | collective-permute-start | bytes 12296 | tf_op jit(solution)/shard_map/ppermute | solution.py:267
  34.0 2.5 %shard_map.101.refs_1_ = f32[2048,256]{1,0:T(8,128)S(1)} custom-call(bf16[128,2048]{1,0:T(8,128)(2,1)S(1)} %get-tuple-element.22.one_ref, bf16[128,2048]{1,0:T(8,128)(2,1)S(1)} %get-tuple-element.23.two_ref, bf16[4096,2048]{1,0:T(8,128)(2,1)S(1)} %get-tuple-element.16.near_ref.head_ref, f32[8,128]{1,0:T(8,128)S(1)} %shard_map.97.mine_ref.refs_0_), custom_call_target="tpu_custom_call" | custom-call | flops 2147483648 | bytes 17829888 | tf_op jit(solution)/shard_map/pallas_call | solution.py:22
  37.2 0.6 %shard_map.102 = (f32[64,4096]{1,0:T(8,128)S(1)}, f32[64,4096]{1,0:T(8,128)S(1)}) custom-call(f32[8,128]{1,0:T(8,128)S(1)} %shard_map.98.lines_ref, f32[8,128]{1,0:T(8,128)S(1)} %get-tuple-element.18.mine_ref, f32[2048,256]{1,0:T(8,128)S(1)} %shard_map.100.refs_0_, f32[2048,256]{1,0:T(8,128)S(1)} %shard_map.101.refs_1_), custom_call_target="tpu_custom_call" | custom-call | bytes 4202496 | tf_op jit(solution)/shard_map/pallas_call | solution.py:22
  38.0 2.0 %collective-permute-start.14 = (f16[16,4096]{1,0:T(8,128)(2,1)S(1)}, f16[16,4096]{1,0:T(8,128)(2,1)S(1)}, u32[]{:S(2)}, u32[]{:S(2)}) collective-permute-start(f16[16,4096]{1,0:T(8,128)(2,1)S(1)} %get-tuple-element.30), channel_id=1, source_target_pairs={{0,3},{1,2},{2,1},{3,0},{4,7},{5,6},{6,5},{7,4},{8,11},{9,10},{10,... | collective-permute-start | bytes 393224 | tf_op jit(solution)/shard_map/ppermute | solution.py:267
  40.4 1.1 %collective-permute-start.15 = (f16[16,4096]{1,0:T(8,128)(2,1)S(1)}, f16[16,4096]{1,0:T(8,128)(2,1)S(1)}, u32[]{:S(2)}, u32[]{:S(2)}) collective-permute-start(f16[16,4096]{1,0:T(8,128)(2,1)S(1)} %get-tuple-element.32), channel_id=1, source_target_pairs={{0,1},{1,0},{2,3},{3,2},{4,5},{5,4},{6,7},{7,6},{8,9},{9,8},{10,11... | collective-permute-start | bytes 393224 | tf_op jit(solution)/shard_map/ppermute | solution.py:267
  41.7 1.0 %collective-permute-start.11 = (f16[16,4096]{1,0:T(8,128)(2,1)S(1)}, f16[16,4096]{1,0:T(8,128)(2,1)S(1)}, u32[]{:S(2)}, u32[]{:S(2)}) collective-permute-start(f16[16,4096]{1,0:T(8,128)(2,1)S(1)} %get-tuple-element.28), channel_id=1, source_target_pairs={{0,1},{1,0},{2,3},{3,2},{4,5},{5,4},{6,7},{7,6},{8,9},{9,8},{10,11... | collective-permute-start | bytes 393224 | tf_op jit(solution)/shard_map/ppermute | solution.py:267
  42.7 1.1 %collective-permute-start.13 = (f16[16,4096]{1,0:T(8,128)(2,1)S(1)}, f16[16,4096]{1,0:T(8,128)(2,1)S(1)}, u32[]{:S(2)}, u32[]{:S(2)}) collective-permute-start(f16[16,4096]{1,0:T(8,128)(2,1)S(1)} %get-tuple-element.29), channel_id=1, source_target_pairs={{0,1},{1,0},{2,3},{3,2},{4,5},{5,4},{6,7},{7,6},{8,9},{9,8},{10,11... | collective-permute-start | bytes 393224 | tf_op jit(solution)/shard_map/ppermute | solution.py:267
  44.1 1.3 %collective-permute-done.16 = f16[16,4096]{1,0:T(8,128)(2,1)S(1)} collective-permute-done((f16[16,4096]{1,0:T(8,128)(2,1)S(1)}, f16[16,4096]{1,0:T(8,128)(2,1)S(1)}, u32[]{:S(2)}, u32[]{:S(2)}) %collective-permute-start.16) | collective-permute-done | bytes 131104 | tf_op jit(solution)/shard_map/ppermute | solution.py:267
  45.4 1.6 %collective-permute-done.15 = f16[16,4096]{1,0:T(8,128)(2,1)S(1)} collective-permute-done((f16[16,4096]{1,0:T(8,128)(2,1)S(1)}, f16[16,4096]{1,0:T(8,128)(2,1)S(1)}, u32[]{:S(2)}, u32[]{:S(2)}) %collective-permute-start.15) | collective-permute-done | bytes 131104 | tf_op jit(solution)/shard_map/ppermute | solution.py:267
  47.0 1.5 %collective-permute-start.17 = (f16[16,4096]{1,0:T(8,128)(2,1)S(1)}, f16[16,4096]{1,0:T(8,128)(2,1)S(1)}, u32[]{:S(2)}, u32[]{:S(2)}) collective-permute-start(f16[16,4096]{1,0:T(8,128)(2,1)S(1)} %add_convert_fusion), channel_id=1, source_target_pairs={{0,4},{1,5},{2,6},{3,7},{4,0},{5,1},{6,2},{7,3},{8,12},{9,13},{10,... | collective-permute-start | bytes 393224 | tf_op jit(solution)/shard_map/ppermute | solution.py:267
  48.6 1.0 %collective-permute-done.11 = f16[16,4096]{1,0:T(8,128)(2,1)S(1)} collective-permute-done((f16[16,4096]{1,0:T(8,128)(2,1)S(1)}, f16[16,4096]{1,0:T(8,128)(2,1)S(1)}, u32[]{:S(2)}, u32[]{:S(2)}) %collective-permute-start.11) | collective-permute-done | bytes 131104 | tf_op jit(solution)/shard_map/ppermute | solution.py:267
  49.6 1.8 %collective-permute-start.12 = (f16[16,4096]{1,0:T(8,128)(2,1)S(1)}, f16[16,4096]{1,0:T(8,128)(2,1)S(1)}, u32[]{:S(2)}, u32[]{:S(2)}) collective-permute-start(f16[16,4096]{1,0:T(8,128)(2,1)S(1)} %add_convert_fusion.1), channel_id=1, source_target_pairs={{0,2},{1,3},{2,0},{3,1},{4,6},{5,7},{6,4},{7,5},{8,10},{9,11},{10,... | collective-permute-start | bytes 393224 | tf_op jit(solution)/shard_map/ppermute | solution.py:267
  51.4 3.1 %shard_map.99 = (f32[128,2048]{1,0:T(8,128)}, f32[128,2048]{1,0:T(8,128)}, f32[1]{0:T(128)}) custom-call(bf16[64,4224]{1,0:T(8,128)(2,1)S(1)} %pad_maximum_fusion.packed_ref.rows_one_ref.ids_one_ref, bf16[64,4224]{1,0:T(8,128)(2,1)S(1)} %bitcast.6, bf16[64,4224]{1,0:T(8,128)(2,1)S(1)} %pad_maximum_fusion.packed_ref.rows_one_ref.ids_one_ref, ...), custom_call_target="tpu_custom_call" | custom-call | flops 67108864 | bytes 6291456 | tf_op jit(solution)/shard_map/pallas_call | solution.py:242
  55.0 0.7 %multiply_convert_fusion = bf16[16,4096]{1,0:T(8,128)(2,1)} fusion(f16[16,4096]{1,0:T(8,128)(2,1)S(1)} %collective-permute-done.17, f16[16,4096]{1,0:T(8,128)(2,1)S(1)} %collective-permute-done.13, f16[16,4096]{1,0:T(8,128)(2,1)S(1)} %collective-permute-done.12, f32[64,4096]{1,0:T(8,128)S(1)} %get-tuple-element.24), kind=kLoop, calls=%fused_computation.2 | loop fusion | flops 524288 | bytes 786432 | tf_op jit(solution)/shard_map/convert_element_type | solution.py:376
  (37 shorter events, 5.7 us)
Async XLA Ops:
  1.6 12.4 %collective-permute-start.3 = (bf16[16,4224]{1,0:T(8,128)(2,1)S(1)}, bf16[16,4224]{1,0:T(8,128)(2,1)S(1)}, u32[]{:S(2)}, u32[]{:S(2)}) collective-permute-start(bf16[16,4224]{1,0:T(8,128)(2,1)S(1)} %shard_map.93), channel_id=1, source_target_pairs={{0,4},{1,5},{2,6},{3,7},{4,0},{5,1},{6,2},{7,3},{8,12},{9,13},{10,... | collective-permute-start | bytes 405512 | tf_op jit(solution)/shard_map/ppermute | solution.py:267
  5.7 11.4 %collective-permute-start.2 = (bf16[16,4224]{1,0:T(8,128)(2,1)S(1)}, bf16[16,4224]{1,0:T(8,128)(2,1)S(1)}, u32[]{:S(2)}, u32[]{:S(2)}) collective-permute-start(bf16[16,4224]{1,0:T(8,128)(2,1)S(1)} %shard_map.93), channel_id=1, source_target_pairs={{0,3},{1,2},{2,1},{3,0},{4,7},{5,6},{6,5},{7,4},{8,11},{9,10},{10,... | collective-permute-start | bytes 405512 | tf_op jit(solution)/shard_map/ppermute | solution.py:267
  8.2 9.3 %collective-permute-start.1 = (bf16[16,4224]{1,0:T(8,128)(2,1)S(1)}, bf16[16,4224]{1,0:T(8,128)(2,1)S(1)}, u32[]{:S(2)}, u32[]{:S(2)}) collective-permute-start(bf16[16,4224]{1,0:T(8,128)(2,1)S(1)} %shard_map.93), channel_id=1, source_target_pairs={{0,2},{1,3},{2,0},{3,1},{4,6},{5,7},{6,4},{7,5},{8,10},{9,11},{10,... | collective-permute-start | bytes 405512 | tf_op jit(solution)/shard_map/ppermute | solution.py:267
  8.6 8.9 %collective-permute-start = (bf16[16,4224]{1,0:T(8,128)(2,1)S(1)}, bf16[16,4224]{1,0:T(8,128)(2,1)S(1)}, u32[]{:S(2)}, u32[]{:S(2)}) collective-permute-start(bf16[16,4224]{1,0:T(8,128)(2,1)S(1)} %shard_map.93), channel_id=1, source_target_pairs={{0,1},{1,0},{2,3},{3,2},{4,5},{5,4},{6,7},{7,6},{8,9},{9,8},{10,11... | collective-permute-start | bytes 405512 | tf_op jit(solution)/shard_map/ppermute | solution.py:267
  14.0 7.6 %collective-permute-start.6 = (bf16[16,4224]{1,0:T(8,128)(2,1)S(1)}, bf16[16,4224]{1,0:T(8,128)(2,1)S(1)}, u32[]{:S(2)}, u32[]{:S(2)}) collective-permute-start(bf16[16,4224]{1,0:T(8,128)(2,1)S(1)} %collective-permute-done.3), channel_id=1, source_target_pairs={{0,3},{1,2},{2,1},{3,0},{4,7},{5,6},{6,5},{7,4},{8,11},{9,10},{10,... | collective-permute-start | bytes 405512 | tf_op jit(solution)/shard_map/ppermute | solution.py:267
  16.6 5.5 %collective-permute-start.5 = (bf16[16,4224]{1,0:T(8,128)(2,1)S(1)}, bf16[16,4224]{1,0:T(8,128)(2,1)S(1)}, u32[]{:S(2)}, u32[]{:S(2)}) collective-permute-start(bf16[16,4224]{1,0:T(8,128)(2,1)S(1)} %collective-permute-done.3), channel_id=1, source_target_pairs={{0,2},{1,3},{2,0},{3,1},{4,6},{5,7},{6,4},{7,5},{8,10},{9,11},{10,... | collective-permute-start | bytes 405512 | tf_op jit(solution)/shard_map/ppermute | solution.py:267
  17.0 5.1 %collective-permute-start.4 = (bf16[16,4224]{1,0:T(8,128)(2,1)S(1)}, bf16[16,4224]{1,0:T(8,128)(2,1)S(1)}, u32[]{:S(2)}, u32[]{:S(2)}) collective-permute-start(bf16[16,4224]{1,0:T(8,128)(2,1)S(1)} %collective-permute-done.3), channel_id=1, source_target_pairs={{0,1},{1,0},{2,3},{3,2},{4,5},{5,4},{6,7},{7,6},{8,9},{9,8},{10,11... | collective-permute-start | bytes 405512 | tf_op jit(solution)/shard_map/ppermute | solution.py:267
  25.9 4.5 %collective-permute-start.7 = (f32[8,128]{1,0:T(8,128)S(1)}, f32[8,128]{1,0:T(8,128)S(1)}, u32[]{:S(2)}, u32[]{:S(2)}) collective-permute-start(f32[8,128]{1,0:T(8,128)S(1)} %get-tuple-element.18.mine_ref), channel_id=1, source_target_pairs={{0,4},{1,5},{2,6},{3,7},{4,0},{5,1},{6,2},{7,3},{8,12},{9,13},{10,... | collective-permute-start | bytes 12296 | tf_op jit(solution)/shard_map/ppermute | solution.py:267
  30.5 6.0 %collective-permute-start.10 = (f32[8,128]{1,0:T(8,128)S(1)}, f32[8,128]{1,0:T(8,128)S(1)}, u32[]{:S(2)}, u32[]{:S(2)}) collective-permute-start(f32[8,128]{1,0:T(8,128)S(1)} %shard_map.97.mine_ref.refs_0_), channel_id=1, source_target_pairs={{0,3},{1,2},{2,1},{3,0},{4,7},{5,6},{6,5},{7,4},{8,11},{9,10},{10,... | collective-permute-start | bytes 12296 | tf_op jit(solution)/shard_map/ppermute | solution.py:267
  33.0 3.6 %collective-permute-start.9 = (f32[8,128]{1,0:T(8,128)S(1)}, f32[8,128]{1,0:T(8,128)S(1)}, u32[]{:S(2)}, u32[]{:S(2)}) collective-permute-start(f32[8,128]{1,0:T(8,128)S(1)} %shard_map.97.mine_ref.refs_0_), channel_id=1, source_target_pairs={{0,2},{1,3},{2,0},{3,1},{4,6},{5,7},{6,4},{7,5},{8,10},{9,11},{10,... | collective-permute-start | bytes 12296 | tf_op jit(solution)/shard_map/ppermute | solution.py:267
  33.5 3.6 %collective-permute-start.8 = (f32[8,128]{1,0:T(8,128)S(1)}, f32[8,128]{1,0:T(8,128)S(1)}, u32[]{:S(2)}, u32[]{:S(2)}) collective-permute-start(f32[8,128]{1,0:T(8,128)S(1)} %shard_map.97.mine_ref.refs_0_), channel_id=1, source_target_pairs={{0,1},{1,0},{2,3},{3,2},{4,5},{5,4},{6,7},{7,6},{8,9},{9,8},{10,11... | collective-permute-start | bytes 12296 | tf_op jit(solution)/shard_map/ppermute | solution.py:267
  38.0 6.1 %collective-permute-start.14 = (f16[16,4096]{1,0:T(8,128)(2,1)S(1)}, f16[16,4096]{1,0:T(8,128)(2,1)S(1)}, u32[]{:S(2)}, u32[]{:S(2)}) collective-permute-start(f16[16,4096]{1,0:T(8,128)(2,1)S(1)} %get-tuple-element.30), channel_id=1, source_target_pairs={{0,3},{1,2},{2,1},{3,0},{4,7},{5,6},{6,5},{7,4},{8,11},{9,10},{10,... | collective-permute-start | bytes 393224 | tf_op jit(solution)/shard_map/ppermute | solution.py:267
  40.0 5.4 %collective-permute-start.16 = (f16[16,4096]{1,0:T(8,128)(2,1)S(1)}, f16[16,4096]{1,0:T(8,128)(2,1)S(1)}, u32[]{:S(2)}, u32[]{:S(2)}) collective-permute-start(f16[16,4096]{1,0:T(8,128)(2,1)S(1)} %get-tuple-element.31), channel_id=1, source_target_pairs={{0,2},{1,3},{2,0},{3,1},{4,6},{5,7},{6,4},{7,5},{8,10},{9,11},{10,... | collective-permute-start | bytes 393224 | tf_op jit(solution)/shard_map/ppermute | solution.py:267
  40.4 6.5 %collective-permute-start.15 = (f16[16,4096]{1,0:T(8,128)(2,1)S(1)}, f16[16,4096]{1,0:T(8,128)(2,1)S(1)}, u32[]{:S(2)}, u32[]{:S(2)}) collective-permute-start(f16[16,4096]{1,0:T(8,128)(2,1)S(1)} %get-tuple-element.32), channel_id=1, source_target_pairs={{0,1},{1,0},{2,3},{3,2},{4,5},{5,4},{6,7},{7,6},{8,9},{9,8},{10,11... | collective-permute-start | bytes 393224 | tf_op jit(solution)/shard_map/ppermute | solution.py:267
  41.5 9.9 %copy-start.1 = (f32[128,2048]{1,0:T(8,128)S(1)}, f32[128,2048]{1,0:T(8,128)}, u32[]{:S(2)}) copy-start(f32[128,2048]{1,0:T(8,128)} %momentum_ref.1) | copy-start | bytes 3145732
  41.5 9.9 %copy-start.2 = (f32[128,2048]{1,0:T(8,128)S(1)}, f32[128,2048]{1,0:T(8,128)}, u32[]{:S(2)}) copy-start(f32[128,2048]{1,0:T(8,128)} %peer_ref.1) | copy-start | bytes 3145732
  41.6 9.8 %copy-start = (f32[128,2048]{1,0:T(8,128)S(1)}, f32[128,2048]{1,0:T(8,128)}, u32[]{:S(2)}) copy-start(f32[128,2048]{1,0:T(8,128)} %global_ref.1) | copy-start | bytes 3145732
  41.7 7.9 %collective-permute-start.11 = (f16[16,4096]{1,0:T(8,128)(2,1)S(1)}, f16[16,4096]{1,0:T(8,128)(2,1)S(1)}, u32[]{:S(2)}, u32[]{:S(2)}) collective-permute-start(f16[16,4096]{1,0:T(8,128)(2,1)S(1)} %get-tuple-element.28), channel_id=1, source_target_pairs={{0,1},{1,0},{2,3},{3,2},{4,5},{5,4},{6,7},{7,6},{8,9},{9,8},{10,11... | collective-permute-start | bytes 393224 | tf_op jit(solution)/shard_map/ppermute | solution.py:267
  42.7 11.8 %collective-permute-start.13 = (f16[16,4096]{1,0:T(8,128)(2,1)S(1)}, f16[16,4096]{1,0:T(8,128)(2,1)S(1)}, u32[]{:S(2)}, u32[]{:S(2)}) collective-permute-start(f16[16,4096]{1,0:T(8,128)(2,1)S(1)} %get-tuple-element.29), channel_id=1, source_target_pairs={{0,1},{1,0},{2,3},{3,2},{4,5},{5,4},{6,7},{7,6},{8,9},{9,8},{10,11... | collective-permute-start | bytes 393224 | tf_op jit(solution)/shard_map/ppermute | solution.py:267
  47.0 7.5 %collective-permute-start.17 = (f16[16,4096]{1,0:T(8,128)(2,1)S(1)}, f16[16,4096]{1,0:T(8,128)(2,1)S(1)}, u32[]{:S(2)}, u32[]{:S(2)}) collective-permute-start(f16[16,4096]{1,0:T(8,128)(2,1)S(1)} %add_convert_fusion), channel_id=1, source_target_pairs={{0,4},{1,5},{2,6},{3,7},{4,0},{5,1},{6,2},{7,3},{8,12},{9,13},{10,... | collective-permute-start | bytes 393224 | tf_op jit(solution)/shard_map/ppermute | solution.py:267
  49.6 5.4 %collective-permute-start.12 = (f16[16,4096]{1,0:T(8,128)(2,1)S(1)}, f16[16,4096]{1,0:T(8,128)(2,1)S(1)}, u32[]{:S(2)}, u32[]{:S(2)}) collective-permute-start(f16[16,4096]{1,0:T(8,128)(2,1)S(1)} %add_convert_fusion.1), channel_id=1, source_target_pairs={{0,2},{1,3},{2,0},{3,1},{4,6},{5,7},{6,4},{7,5},{8,10},{9,11},{10,... | collective-permute-start | bytes 393224 | tf_op jit(solution)/shard_map/ppermute | solution.py:267

commit v24 on v23

--- a/solution.py
+++ b/solution.py
@@ -196,7 +196,7 @@
     near = near_ref.shape[0]
     top, total = lines_ref[0:1, :], lines_ref[1:2, :]
     soft = jnp.exp(mine_ref[0:1, :] - top) / (total * rows) * scale
-    hard = (jnp.exp(mine_ref[2:3, :] - top) / total - 1.0) / rows
+    hard = (jnp.exp(jnp.minimum(mine_ref[2:3, :] - top, 0.0)) / total - 1.0) / rows
     hard = hard.astype(jnp.bfloat16).astype(jnp.float32) * scale
     tile = 512
     for place, terms_ref in enumerate(terms_refs):

time: 55.9 us -> 55.9 us (level)
  no operation moved by 1% of the time
where the time goes in v24:
time: 55.9 us; the launch traced here: 55.7 us
  starting transfers between devices  25.5 us (46%)
  Pallas kernels  22.3 us (40%)
  waiting for transfers between devices  6.01 us (11%)
  other arithmetic  1.09 us (2%)
  between operations  0.78 us (1%)
    ppermute x18, starting transfers between devices, swap(): lax.ppermute(value, AXIS, [(i, i ^ step) for i in range(lax.axis_size(AXI...  25.5 us
    pallas_call x9, Pallas kernels, call(): pl.pallas_call(kernel, out_shape=outs, in_specs=[pl.BlockSpec(memory_spac...  19.2 us
    ppermute x18, waiting for transfers between devices, swap(): lax.ppermute(value, AXIS, [(i, i ^ step) for i in range(lax.axis_size(AXI...  6.01 us
    pallas_call x1, Pallas kernels, frag_update(): pl.pallas_call(functools.partial(frag_kernel, members), grid=(width // TI...  3.08 us
  transfers between devices with their start and end apart: 18, of which 9 were waited for; matrix products, arithmetic and copies ran while one was open for 0% of the time, Pallas kernels for 30%

profile of v24, /device:TPU:0, one launch (start us, length us, event | category | flops | bytes accessed | tf_op | source)
XLA Modules:
  0.0 55.7 jit_solution(8133653648105525469)
XLA Ops:
  0.6 0.9 %shard_map.93 = bf16[16,4224]{1,0:T(8,128)(2,1)S(1)} custom-call(s32[16]{0:T(128)} %targets.1, bf16[16,4096]{1,0:T(8,128)(2,1)} %rows.1), custom_call_target="tpu_custom_call" | custom-call | bytes 131136 | tf_op jit(solution)/shard_map/pallas_call | solution.py:22
  1.6 4.1 %collective-permute-start.3 = (bf16[16,4224]{1,0:T(8,128)(2,1)S(1)}, bf16[16,4224]{1,0:T(8,128)(2,1)S(1)}, u32[]{:S(2)}, u32[]{:S(2)}) collective-permute-start(bf16[16,4224]{1,0:T(8,128)(2,1)S(1)} %shard_map.93), channel_id=1, source_target_pairs={{0,4},{1,5},{2,6},{3,7},{4,0},{5,1},{6,2},{7,3},{8,12},{9,13},{10,... | collective-permute-start | bytes 405512 | tf_op jit(solution)/shard_map/ppermute | solution.py:267
  5.7 2.5 %collective-permute-start.2 = (bf16[16,4224]{1,0:T(8,128)(2,1)S(1)}, bf16[16,4224]{1,0:T(8,128)(2,1)S(1)}, u32[]{:S(2)}, u32[]{:S(2)}) collective-permute-start(bf16[16,4224]{1,0:T(8,128)(2,1)S(1)} %shard_map.93), channel_id=1, source_target_pairs={{0,3},{1,2},{2,1},{3,0},{4,7},{5,6},{6,5},{7,4},{8,11},{9,10},{10,... | collective-permute-start | bytes 405512 | tf_op jit(solution)/shard_map/ppermute | solution.py:267
  9.2 4.8 %shard_map.94.held_ref = bf16[4096,2048]{1,0:T(8,128)(2,1)S(1)} custom-call(bf16[4096,2048]{1,0:T(8,128)(2,1)} %head.3), custom_call_target="tpu_custom_call" | custom-call | bytes 16777216 | tf_op jit(solution)/shard_map/pallas_call | solution.py:22
  14.0 2.6 %collective-permute-start.6 = (bf16[16,4224]{1,0:T(8,128)(2,1)S(1)}, bf16[16,4224]{1,0:T(8,128)(2,1)S(1)}, u32[]{:S(2)}, u32[]{:S(2)}) collective-permute-start(bf16[16,4224]{1,0:T(8,128)(2,1)S(1)} %collective-permute-done.3), channel_id=1, source_target_pairs={{0,3},{1,2},{2,1},{3,0},{4,7},{5,6},{6,5},{7,4},{8,11},{9,10},{10,... | collective-permute-start | bytes 405512 | tf_op jit(solution)/shard_map/ppermute | solution.py:267
  17.6 4.0 %shard_map.95 = (bf16[4096,2048]{1,0:T(8,128)(2,1)S(1)}, f32[64,2048]{1,0:T(8,128)S(1)}, bf16[128,2048]{1,0:T(8,128)(2,1)S(1)}, f32[64,128]{1,0:T(8,128)S(1)}) custom-call(bf16[64,4224]{1,0:T(8,128)(2,1)S(1)} %pad_maximum_fusion.packed_ref.rows_one_ref.ids_one_ref, bf16[4096,2048]{1,0:T(8,128)(2,1)} %head.3, ...), custom_call_target="tpu_custom_call", output_to_operand_aliasing={{0}: (2, {})} | custom-call | flops 1073741824 | bytes 34095104 | tf_op jit(solution)/shard_map/pallas_call | solution.py:22
  22.2 3.7 %shard_map.96 = (f32[64,2048]{1,0:T(8,128)S(1)}, bf16[128,2048]{1,0:T(8,128)(2,1)S(1)}, f32[8,128]{1,0:T(8,128)S(1)}) custom-call(bf16[64,4224]{1,0:T(8,128)(2,1)S(1)} %bitcast.5, bf16[4096,2048]{1,0:T(8,128)(2,1)S(1)} %get-tuple-element.16.near_ref.head_ref, f32[64,128]{1,0:T(8,128)S(1)} %get-tuple-element.17.before_ref), custom_call_target="tpu_custom_call" | custom-call | flops 1073741824 | bytes 17350656 | tf_op jit(solution)/shard_map/pallas_call | solution.py:22
  25.9 1.8 %collective-permute-start.7 = (f32[8,128]{1,0:T(8,128)S(1)}, f32[8,128]{1,0:T(8,128)S(1)}, u32[]{:S(2)}, u32[]{:S(2)}) collective-permute-start(f32[8,128]{1,0:T(8,128)S(1)} %get-tuple-element.18.mine_ref), channel_id=1, source_target_pairs={{0,4},{1,5},{2,6},{3,7},{4,0},{5,1},{6,2},{7,3},{8,12},{9,13},{10,... | collective-permute-start | bytes 12296 | tf_op jit(solution)/shard_map/ppermute | solution.py:267
  27.7 2.5 %shard_map.100.refs_0_ = f32[2048,256]{1,0:T(8,128)S(1)} custom-call(bf16[128,2048]{1,0:T(8,128)(2,1)S(1)} %get-tuple-element.22.one_ref, bf16[128,2048]{1,0:T(8,128)(2,1)S(1)} %get-tuple-element.23.two_ref, bf16[4096,2048]{1,0:T(8,128)(2,1)S(1)} %get-tuple-element.16.near_ref.head_ref), custom_call_target="tpu_custom_call" | custom-call | flops 2147483648 | bytes 17825792 | tf_op jit(solution)/shard_map/pallas_call | solution.py:22
  30.5 2.5 %collective-permute-start.10 = (f32[8,128]{1,0:T(8,128)S(1)}, f32[8,128]{1,0:T(8,128)S(1)}, u32[]{:S(2)}, u32[]{:S(2)}) collective-permute-start(f32[8,128]{1,0:T(8,128)S(1)} %shard_map.97.mine_ref.refs_0_), channel_id=1, source_target_pairs={{0,3},{1,2},{2,1},{3,0},{4,7},{5,6},{6,5},{7,4},{8,11},{9,10},{10,... | collective-permute-start | bytes 12296 | tf_op jit(solution)/shard_map/ppermute | solution.py:267
  33.5 0.6 %collective-permute-start.8 = (f32[8,128]{1,0:T(8,128)S(1)}, f32[8,128]{1,0:T(8,128)S(1)}, u32[]{:S(2)}, u32[]{:S(2)}) collective-permute-start(f32[8,128]{1,0:T(8,128)S(1)} %shard_map.97.mine_ref.refs_0_), channel_id=1, source_target_pairs={{0,1},{1,0},{2,3},{3,2},{4,5},{5,4},{6,7},{7,6},{8,9},{9,8},{10,11... | collective-permute-start | bytes 12296 | tf_op jit(solution)/shard_map/ppermute | solution.py:267
  34.0 2.5 %shard_map.101.refs_1_ = f32[2048,256]{1,0:T(8,128)S(1)} custom-call(bf16[128,2048]{1,0:T(8,128)(2,1)S(1)} %get-tuple-element.22.one_ref, bf16[128,2048]{1,0:T(8,128)(2,1)S(1)} %get-tuple-element.23.two_ref, bf16[4096,2048]{1,0:T(8,128)(2,1)S(1)} %get-tuple-element.16.near_ref.head_ref, f32[8,128]{1,0:T(8,128)S(1)} %shard_map.97.mine_ref.refs_0_), custom_call_target="tpu_custom_call" | custom-call | flops 2147483648 | bytes 17829888 | tf_op jit(solution)/shard_map/pallas_call | solution.py:22
  37.2 0.6 %shard_map.102 = (f32[64,4096]{1,0:T(8,128)S(1)}, f32[64,4096]{1,0:T(8,128)S(1)}) custom-call(f32[8,128]{1,0:T(8,128)S(1)} %shard_map.98.lines_ref, f32[8,128]{1,0:T(8,128)S(1)} %get-tuple-element.18.mine_ref, f32[2048,256]{1,0:T(8,128)S(1)} %shard_map.100.refs_0_, f32[2048,256]{1,0:T(8,128)S(1)} %shard_map.101.refs_1_), custom_call_target="tpu_custom_call" | custom-call | bytes 4202496 | tf_op jit(solution)/shard_map/pallas_call | solution.py:22
  38.0 2.0 %collective-permute-start.14 = (f16[16,4096]{1,0:T(8,128)(2,1)S(1)}, f16[16,4096]{1,0:T(8,128)(2,1)S(1)}, u32[]{:S(2)}, u32[]{:S(2)}) collective-permute-start(f16[16,4096]{1,0:T(8,128)(2,1)S(1)} %get-tuple-element.30), channel_id=1, source_target_pairs={{0,3},{1,2},{2,1},{3,0},{4,7},{5,6},{6,5},{7,4},{8,11},{9,10},{10,... | collective-permute-start | bytes 393224 | tf_op jit(solution)/shard_map/ppermute | solution.py:267
  40.4 1.1 %collective-permute-start.15 = (f16[16,4096]{1,0:T(8,128)(2,1)S(1)}, f16[16,4096]{1,0:T(8,128)(2,1)S(1)}, u32[]{:S(2)}, u32[]{:S(2)}) collective-permute-start(f16[16,4096]{1,0:T(8,128)(2,1)S(1)} %get-tuple-element.32), channel_id=1, source_target_pairs={{0,1},{1,0},{2,3},{3,2},{4,5},{5,4},{6,7},{7,6},{8,9},{9,8},{10,11... | collective-permute-start | bytes 393224 | tf_op jit(solution)/shard_map/ppermute | solution.py:267
  41.7 1.0 %collective-permute-start.11 = (f16[16,4096]{1,0:T(8,128)(2,1)S(1)}, f16[16,4096]{1,0:T(8,128)(2,1)S(1)}, u32[]{:S(2)}, u32[]{:S(2)}) collective-permute-start(f16[16,4096]{1,0:T(8,128)(2,1)S(1)} %get-tuple-element.28), channel_id=1, source_target_pairs={{0,1},{1,0},{2,3},{3,2},{4,5},{5,4},{6,7},{7,6},{8,9},{9,8},{10,11... | collective-permute-start | bytes 393224 | tf_op jit(solution)/shard_map/ppermute | solution.py:267
  42.7 1.1 %collective-permute-start.13 = (f16[16,4096]{1,0:T(8,128)(2,1)S(1)}, f16[16,4096]{1,0:T(8,128)(2,1)S(1)}, u32[]{:S(2)}, u32[]{:S(2)}) collective-permute-start(f16[16,4096]{1,0:T(8,128)(2,1)S(1)} %get-tuple-element.29), channel_id=1, source_target_pairs={{0,1},{1,0},{2,3},{3,2},{4,5},{5,4},{6,7},{7,6},{8,9},{9,8},{10,11... | collective-permute-start | bytes 393224 | tf_op jit(solution)/shard_map/ppermute | solution.py:267
  44.1 1.3 %collective-permute-done.16 = f16[16,4096]{1,0:T(8,128)(2,1)S(1)} collective-permute-done((f16[16,4096]{1,0:T(8,128)(2,1)S(1)}, f16[16,4096]{1,0:T(8,128)(2,1)S(1)}, u32[]{:S(2)}, u32[]{:S(2)}) %collective-permute-start.16) | collective-permute-done | bytes 131104 | tf_op jit(solution)/shard_map/ppermute | solution.py:267
  45.4 1.6 %collective-permute-done.15 = f16[16,4096]{1,0:T(8,128)(2,1)S(1)} collective-permute-done((f16[16,4096]{1,0:T(8,128)(2,1)S(1)}, f16[16,4096]{1,0:T(8,128)(2,1)S(1)}, u32[]{:S(2)}, u32[]{:S(2)}) %collective-permute-start.15) | collective-permute-done | bytes 131104 | tf_op jit(solution)/shard_map/ppermute | solution.py:267
  47.0 1.5 %collective-permute-start.17 = (f16[16,4096]{1,0:T(8,128)(2,1)S(1)}, f16[16,4096]{1,0:T(8,128)(2,1)S(1)}, u32[]{:S(2)}, u32[]{:S(2)}) collective-permute-start(f16[16,4096]{1,0:T(8,128)(2,1)S(1)} %add_convert_fusion), channel_id=1, source_target_pairs={{0,4},{1,5},{2,6},{3,7},{4,0},{5,1},{6,2},{7,3},{8,12},{9,13},{10,... | collective-permute-start | bytes 393224 | tf_op jit(solution)/shard_map/ppermute | solution.py:267
  48.6 1.0 %collective-permute-done.11 = f16[16,4096]{1,0:T(8,128)(2,1)S(1)} collective-permute-done((f16[16,4096]{1,0:T(8,128)(2,1)S(1)}, f16[16,4096]{1,0:T(8,128)(2,1)S(1)}, u32[]{:S(2)}, u32[]{:S(2)}) %collective-permute-start.11) | collective-permute-done | bytes 131104 | tf_op jit(solution)/shard_map/ppermute | solution.py:267
  49.6 1.8 %collective-permute-start.12 = (f16[16,4096]{1,0:T(8,128)(2,1)S(1)}, f16[16,4096]{1,0:T(8,128)(2,1)S(1)}, u32[]{:S(2)}, u32[]{:S(2)}) collective-permute-start(f16[16,4096]{1,0:T(8,128)(2,1)S(1)} %add_convert_fusion.1), channel_id=1, source_target_pairs={{0,2},{1,3},{2,0},{3,1},{4,6},{5,7},{6,4},{7,5},{8,10},{9,11},{10,... | collective-permute-start | bytes 393224 | tf_op jit(solution)/shard_map/ppermute | solution.py:267
  51.4 3.1 %shard_map.99 = (f32[128,2048]{1,0:T(8,128)}, f32[128,2048]{1,0:T(8,128)}, f32[1]{0:T(128)}) custom-call(bf16[64,4224]{1,0:T(8,128)(2,1)S(1)} %pad_maximum_fusion.packed_ref.rows_one_ref.ids_one_ref, bf16[64,4224]{1,0:T(8,128)(2,1)S(1)} %bitcast.6, bf16[64,4224]{1,0:T(8,128)(2,1)S(1)} %pad_maximum_fusion.packed_ref.rows_one_ref.ids_one_ref, ...), custom_call_target="tpu_custom_call" | custom-call | flops 67108864 | bytes 6291456 | tf_op jit(solution)/shard_map/pallas_call | solution.py:242
  55.0 0.7 %multiply_convert_fusion = bf16[16,4096]{1,0:T(8,128)(2,1)} fusion(f16[16,4096]{1,0:T(8,128)(2,1)S(1)} %collective-permute-done.17, f16[16,4096]{1,0:T(8,128)(2,1)S(1)} %collective-permute-done.13, f16[16,4096]{1,0:T(8,128)(2,1)S(1)} %collective-permute-done.12, f32[64,4096]{1,0:T(8,128)S(1)} %get-tuple-element.24), kind=kLoop, calls=%fused_computation.2 | loop fusion | flops 524288 | bytes 786432 | tf_op jit(solution)/shard_map/convert_element_type | solution.py:376
  (37 shorter events, 5.7 us)
Async XLA Ops:
  1.6 12.4 %collective-permute-start.3 = (bf16[16,4224]{1,0:T(8,128)(2,1)S(1)}, bf16[16,4224]{1,0:T(8,128)(2,1)S(1)}, u32[]{:S(2)}, u32[]{:S(2)}) collective-permute-start(bf16[16,4224]{1,0:T(8,128)(2,1)S(1)} %shard_map.93), channel_id=1, source_target_pairs={{0,4},{1,5},{2,6},{3,7},{4,0},{5,1},{6,2},{7,3},{8,12},{9,13},{10,... | collective-permute-start | bytes 405512 | tf_op jit(solution)/shard_map/ppermute | solution.py:267
  5.7 11.4 %collective-permute-start.2 = (bf16[16,4224]{1,0:T(8,128)(2,1)S(1)}, bf16[16,4224]{1,0:T(8,128)(2,1)S(1)}, u32[]{:S(2)}, u32[]{:S(2)}) collective-permute-start(bf16[16,4224]{1,0:T(8,128)(2,1)S(1)} %shard_map.93), channel_id=1, source_target_pairs={{0,3},{1,2},{2,1},{3,0},{4,7},{5,6},{6,5},{7,4},{8,11},{9,10},{10,... | collective-permute-start | bytes 405512 | tf_op jit(solution)/shard_map/ppermute | solution.py:267
  8.2 9.3 %collective-permute-start.1 = (bf16[16,4224]{1,0:T(8,128)(2,1)S(1)}, bf16[16,4224]{1,0:T(8,128)(2,1)S(1)}, u32[]{:S(2)}, u32[]{:S(2)}) collective-permute-start(bf16[16,4224]{1,0:T(8,128)(2,1)S(1)} %shard_map.93), channel_id=1, source_target_pairs={{0,2},{1,3},{2,0},{3,1},{4,6},{5,7},{6,4},{7,5},{8,10},{9,11},{10,... | collective-permute-start | bytes 405512 | tf_op jit(solution)/shard_map/ppermute | solution.py:267
  8.6 8.9 %collective-permute-start = (bf16[16,4224]{1,0:T(8,128)(2,1)S(1)}, bf16[16,4224]{1,0:T(8,128)(2,1)S(1)}, u32[]{:S(2)}, u32[]{:S(2)}) collective-permute-start(bf16[16,4224]{1,0:T(8,128)(2,1)S(1)} %shard_map.93), channel_id=1, source_target_pairs={{0,1},{1,0},{2,3},{3,2},{4,5},{5,4},{6,7},{7,6},{8,9},{9,8},{10,11... | collective-permute-start | bytes 405512 | tf_op jit(solution)/shard_map/ppermute | solution.py:267
  14.0 7.6 %collective-permute-start.6 = (bf16[16,4224]{1,0:T(8,128)(2,1)S(1)}, bf16[16,4224]{1,0:T(8,128)(2,1)S(1)}, u32[]{:S(2)}, u32[]{:S(2)}) collective-permute-start(bf16[16,4224]{1,0:T(8,128)(2,1)S(1)} %collective-permute-done.3), channel_id=1, source_target_pairs={{0,3},{1,2},{2,1},{3,0},{4,7},{5,6},{6,5},{7,4},{8,11},{9,10},{10,... | collective-permute-start | bytes 405512 | tf_op jit(solution)/shard_map/ppermute | solution.py:267
  16.6 5.5 %collective-permute-start.5 = (bf16[16,4224]{1,0:T(8,128)(2,1)S(1)}, bf16[16,4224]{1,0:T(8,128)(2,1)S(1)}, u32[]{:S(2)}, u32[]{:S(2)}) collective-permute-start(bf16[16,4224]{1,0:T(8,128)(2,1)S(1)} %collective-permute-done.3), channel_id=1, source_target_pairs={{0,2},{1,3},{2,0},{3,1},{4,6},{5,7},{6,4},{7,5},{8,10},{9,11},{10,... | collective-permute-start | bytes 405512 | tf_op jit(solution)/shard_map/ppermute | solution.py:267
  17.0 5.1 %collective-permute-start.4 = (bf16[16,4224]{1,0:T(8,128)(2,1)S(1)}, bf16[16,4224]{1,0:T(8,128)(2,1)S(1)}, u32[]{:S(2)}, u32[]{:S(2)}) collective-permute-start(bf16[16,4224]{1,0:T(8,128)(2,1)S(1)} %collective-permute-done.3), channel_id=1, source_target_pairs={{0,1},{1,0},{2,3},{3,2},{4,5},{5,4},{6,7},{7,6},{8,9},{9,8},{10,11... | collective-permute-start | bytes 405512 | tf_op jit(solution)/shard_map/ppermute | solution.py:267
  25.9 4.5 %collective-permute-start.7 = (f32[8,128]{1,0:T(8,128)S(1)}, f32[8,128]{1,0:T(8,128)S(1)}, u32[]{:S(2)}, u32[]{:S(2)}) collective-permute-start(f32[8,128]{1,0:T(8,128)S(1)} %get-tuple-element.18.mine_ref), channel_id=1, source_target_pairs={{0,4},{1,5},{2,6},{3,7},{4,0},{5,1},{6,2},{7,3},{8,12},{9,13},{10,... | collective-permute-start | bytes 12296 | tf_op jit(solution)/shard_map/ppermute | solution.py:267
  30.5 6.0 %collective-permute-start.10 = (f32[8,128]{1,0:T(8,128)S(1)}, f32[8,128]{1,0:T(8,128)S(1)}, u32[]{:S(2)}, u32[]{:S(2)}) collective-permute-start(f32[8,128]{1,0:T(8,128)S(1)} %shard_map.97.mine_ref.refs_0_), channel_id=1, source_target_pairs={{0,3},{1,2},{2,1},{3,0},{4,7},{5,6},{6,5},{7,4},{8,11},{9,10},{10,... | collective-permute-start | bytes 12296 | tf_op jit(solution)/shard_map/ppermute | solution.py:267
  33.0 3.6 %collective-permute-start.9 = (f32[8,128]{1,0:T(8,128)S(1)}, f32[8,128]{1,0:T(8,128)S(1)}, u32[]{:S(2)}, u32[]{:S(2)}) collective-permute-start(f32[8,128]{1,0:T(8,128)S(1)} %shard_map.97.mine_ref.refs_0_), channel_id=1, source_target_pairs={{0,2},{1,3},{2,0},{3,1},{4,6},{5,7},{6,4},{7,5},{8,10},{9,11},{10,... | collective-permute-start | bytes 12296 | tf_op jit(solution)/shard_map/ppermute | solution.py:267
  33.5 3.6 %collective-permute-start.8 = (f32[8,128]{1,0:T(8,128)S(1)}, f32[8,128]{1,0:T(8,128)S(1)}, u32[]{:S(2)}, u32[]{:S(2)}) collective-permute-start(f32[8,128]{1,0:T(8,128)S(1)} %shard_map.97.mine_ref.refs_0_), channel_id=1, source_target_pairs={{0,1},{1,0},{2,3},{3,2},{4,5},{5,4},{6,7},{7,6},{8,9},{9,8},{10,11... | collective-permute-start | bytes 12296 | tf_op jit(solution)/shard_map/ppermute | solution.py:267
  38.0 6.1 %collective-permute-start.14 = (f16[16,4096]{1,0:T(8,128)(2,1)S(1)}, f16[16,4096]{1,0:T(8,128)(2,1)S(1)}, u32[]{:S(2)}, u32[]{:S(2)}) collective-permute-start(f16[16,4096]{1,0:T(8,128)(2,1)S(1)} %get-tuple-element.30), channel_id=1, source_target_pairs={{0,3},{1,2},{2,1},{3,0},{4,7},{5,6},{6,5},{7,4},{8,11},{9,10},{10,... | collective-permute-start | bytes 393224 | tf_op jit(solution)/shard_map/ppermute | solution.py:267
  40.0 5.4 %collective-permute-start.16 = (f16[16,4096]{1,0:T(8,128)(2,1)S(1)}, f16[16,4096]{1,0:T(8,128)(2,1)S(1)}, u32[]{:S(2)}, u32[]{:S(2)}) collective-permute-start(f16[16,4096]{1,0:T(8,128)(2,1)S(1)} %get-tuple-element.31), channel_id=1, source_target_pairs={{0,2},{1,3},{2,0},{3,1},{4,6},{5,7},{6,4},{7,5},{8,10},{9,11},{10,... | collective-permute-start | bytes 393224 | tf_op jit(solution)/shard_map/ppermute | solution.py:267
  40.4 6.5 %collective-permute-start.15 = (f16[16,4096]{1,0:T(8,128)(2,1)S(1)}, f16[16,4096]{1,0:T(8,128)(2,1)S(1)}, u32[]{:S(2)}, u32[]{:S(2)}) collective-permute-start(f16[16,4096]{1,0:T(8,128)(2,1)S(1)} %get-tuple-element.32), channel_id=1, source_target_pairs={{0,1},{1,0},{2,3},{3,2},{4,5},{5,4},{6,7},{7,6},{8,9},{9,8},{10,11... | collective-permute-start | bytes 393224 | tf_op jit(solution)/shard_map/ppermute | solution.py:267
  41.5 9.9 %copy-start.1 = (f32[128,2048]{1,0:T(8,128)S(1)}, f32[128,2048]{1,0:T(8,128)}, u32[]{:S(2)}) copy-start(f32[128,2048]{1,0:T(8,128)} %momentum_ref.1) | copy-start | bytes 3145732
  41.5 9.9 %copy-start.2 = (f32[128,2048]{1,0:T(8,128)S(1)}, f32[128,2048]{1,0:T(8,128)}, u32[]{:S(2)}) copy-start(f32[128,2048]{1,0:T(8,128)} %peer_ref.1) | copy-start | bytes 3145732
  41.6 9.8 %copy-start = (f32[128,2048]{1,0:T(8,128)S(1)}, f32[128,2048]{1,0:T(8,128)}, u32[]{:S(2)}) copy-start(f32[128,2048]{1,0:T(8,128)} %global_ref.1) | copy-start | bytes 3145732
  41.7 7.9 %collective-permute-start.11 = (f16[16,4096]{1,0:T(8,128)(2,1)S(1)}, f16[16,4096]{1,0:T(8,128)(2,1)S(1)}, u32[]{:S(2)}, u32[]{:S(2)}) collective-permute-start(f16[16,4096]{1,0:T(8,128)(2,1)S(1)} %get-tuple-element.28), channel_id=1, source_target_pairs={{0,1},{1,0},{2,3},{3,2},{4,5},{5,4},{6,7},{7,6},{8,9},{9,8},{10,11... | collective-permute-start | bytes 393224 | tf_op jit(solution)/shard_map/ppermute | solution.py:267
  42.7 11.8 %collective-permute-start.13 = (f16[16,4096]{1,0:T(8,128)(2,1)S(1)}, f16[16,4096]{1,0:T(8,128)(2,1)S(1)}, u32[]{:S(2)}, u32[]{:S(2)}) collective-permute-start(f16[16,4096]{1,0:T(8,128)(2,1)S(1)} %get-tuple-element.29), channel_id=1, source_target_pairs={{0,1},{1,0},{2,3},{3,2},{4,5},{5,4},{6,7},{7,6},{8,9},{9,8},{10,11... | collective-permute-start | bytes 393224 | tf_op jit(solution)/shard_map/ppermute | solution.py:267
  47.0 7.5 %collective-permute-start.17 = (f16[16,4096]{1,0:T(8,128)(2,1)S(1)}, f16[16,4096]{1,0:T(8,128)(2,1)S(1)}, u32[]{:S(2)}, u32[]{:S(2)}) collective-permute-start(f16[16,4096]{1,0:T(8,128)(2,1)S(1)} %add_convert_fusion), channel_id=1, source_target_pairs={{0,4},{1,5},{2,6},{3,7},{4,0},{5,1},{6,2},{7,3},{8,12},{9,13},{10,... | collective-permute-start | bytes 393224 | tf_op jit(solution)/shard_map/ppermute | solution.py:267
  49.6 5.4 %collective-permute-start.12 = (f16[16,4096]{1,0:T(8,128)(2,1)S(1)}, f16[16,4096]{1,0:T(8,128)(2,1)S(1)}, u32[]{:S(2)}, u32[]{:S(2)}) collective-permute-start(f16[16,4096]{1,0:T(8,128)(2,1)S(1)} %add_convert_fusion.1), channel_id=1, source_target_pairs={{0,2},{1,3},{2,0},{3,1},{4,6},{5,7},{6,4},{7,5},{8,10},{9,11},{10,... | collective-permute-start | bytes 393224 | tf_op jit(solution)/shard_map/ppermute | solution.py:267

commit v25 on v24

--- a/solution.py
+++ b/solution.py
@@ -309,7 +309,7 @@
     y_near = moved([blocks[1]], 1)[0]
     z_near = moved([blocks[2] + relayed], 2)[0]
     sums = [blocks[0] + z_near + y_near]
-    sums += [blocks[i] + a + b + c for i, a, b, c in zip(far, three, one, two)]
+    sums += [blocks[i] + a + b + c for i, a, b, c in zip(far, one, two, three)]
     for step in far_steps()[::-1]:
         keep = len(sums) // 2
         sums = [a + b for a, b in zip(sums[:keep], moved(sums[keep:], step))]

time: 55.9 us -> 55.4 us (level)
  waiting for transfers between devices: 6.01 us -> 5.37 us
    ppermute x18, waiting for transfers between devices: 6.01 us -> 5.37 us  [swap(): lax.ppermute(value, AXIS, [(i, i ^ step) for i in range(lax.axis_size(AXI...]
  transfers between devices with their start and end apart: 18 -> 18, of which waited for: 9 -> 7; matrix products, arithmetic and copies ran while one was open for 0% -> 0% of each run, Pallas kernels for 30% -> 30%
where the time goes in v25:
time: 55.4 us; the launch traced here: 55.2 us
  starting transfers between devices  25.6 us (46%)
  Pallas kernels  22.3 us (40%)
  waiting for transfers between devices  5.37 us (10%)
  other arithmetic  1.09 us (2%)
  between operations  0.78 us (1%)
    ppermute x18, starting transfers between devices, swap(): lax.ppermute(value, AXIS, [(i, i ^ step) for i in range(lax.axis_size(AXI...  25.6 us
    pallas_call x9, Pallas kernels, call(): pl.pallas_call(kernel, out_shape=outs, in_specs=[pl.BlockSpec(memory_spac...  19.2 us
    ppermute x18, waiting for transfers between devices, swap(): lax.ppermute(value, AXIS, [(i, i ^ step) for i in range(lax.axis_size(AXI...  5.37 us
    pallas_call x1, Pallas kernels, frag_update(): pl.pallas_call(functools.partial(frag_kernel, members), grid=(width // TI...  3.08 us
  transfers between devices with their start and end apart: 18, of which 7 were waited for; matrix products, arithmetic and copies ran while one was open for 0% of the time, Pallas kernels for 30%

profile of v25, /device:TPU:0, one launch (start us, length us, event | category | flops | bytes accessed | tf_op | source)
XLA Modules:
  0.0 55.2 jit_solution(13456093534751298671)
XLA Ops:
  0.6 0.9 %shard_map.93 = bf16[16,4224]{1,0:T(8,128)(2,1)S(1)} custom-call(s32[16]{0:T(128)} %targets.1, bf16[16,4096]{1,0:T(8,128)(2,1)} %rows.1), custom_call_target="tpu_custom_call" | custom-call | bytes 131136 | tf_op jit(solution)/shard_map/pallas_call | solution.py:22
  1.6 4.1 %collective-permute-start.3 = (bf16[16,4224]{1,0:T(8,128)(2,1)S(1)}, bf16[16,4224]{1,0:T(8,128)(2,1)S(1)}, u32[]{:S(2)}, u32[]{:S(2)}) collective-permute-start(bf16[16,4224]{1,0:T(8,128)(2,1)S(1)} %shard_map.93), channel_id=1, source_target_pairs={{0,4},{1,5},{2,6},{3,7},{4,0},{5,1},{6,2},{7,3},{8,12},{9,13},{10,... | collective-permute-start | bytes 405512 | tf_op jit(solution)/shard_map/ppermute | solution.py:267
  5.7 2.5 %collective-permute-start.2 = (bf16[16,4224]{1,0:T(8,128)(2,1)S(1)}, bf16[16,4224]{1,0:T(8,128)(2,1)S(1)}, u32[]{:S(2)}, u32[]{:S(2)}) collective-permute-start(bf16[16,4224]{1,0:T(8,128)(2,1)S(1)} %shard_map.93), channel_id=1, source_target_pairs={{0,3},{1,2},{2,1},{3,0},{4,7},{5,6},{6,5},{7,4},{8,11},{9,10},{10,... | collective-permute-start | bytes 405512 | tf_op jit(solution)/shard_map/ppermute | solution.py:267
  9.2 4.8 %shard_map.94.held_ref = bf16[4096,2048]{1,0:T(8,128)(2,1)S(1)} custom-call(bf16[4096,2048]{1,0:T(8,128)(2,1)} %head.3), custom_call_target="tpu_custom_call" | custom-call | bytes 16777216 | tf_op jit(solution)/shard_map/pallas_call | solution.py:22
  14.0 2.6 %collective-permute-start.6 = (bf16[16,4224]{1,0:T(8,128)(2,1)S(1)}, bf16[16,4224]{1,0:T(8,128)(2,1)S(1)}, u32[]{:S(2)}, u32[]{:S(2)}) collective-permute-start(bf16[16,4224]{1,0:T(8,128)(2,1)S(1)} %collective-permute-done.3), channel_id=1, source_target_pairs={{0,3},{1,2},{2,1},{3,0},{4,7},{5,6},{6,5},{7,4},{8,11},{9,10},{10,... | collective-permute-start | bytes 405512 | tf_op jit(solution)/shard_map/ppermute | solution.py:267
  17.0 0.5 collective-permute-start.4
  17.6 4.0 %shard_map.95 = (bf16[4096,2048]{1,0:T(8,128)(2,1)S(1)}, f32[64,2048]{1,0:T(8,128)S(1)}, bf16[128,2048]{1,0:T(8,128)(2,1)S(1)}, f32[64,128]{1,0:T(8,128)S(1)}) custom-call(bf16[64,4224]{1,0:T(8,128)(2,1)S(1)} %pad_maximum_fusion.packed_ref.rows_one_ref.ids_one_ref, bf16[4096,2048]{1,0:T(8,128)(2,1)} %head.3, ...), custom_call_target="tpu_custom_call", output_to_operand_aliasing={{0}: (2, {})} | custom-call | flops 1073741824 | bytes 34095104 | tf_op jit(solution)/shard_map/pallas_call | solution.py:22
  22.2 3.7 %shard_map.96 = (f32[64,2048]{1,0:T(8,128)S(1)}, bf16[128,2048]{1,0:T(8,128)(2,1)S(1)}, f32[8,128]{1,0:T(8,128)S(1)}) custom-call(bf16[64,4224]{1,0:T(8,128)(2,1)S(1)} %bitcast.5, bf16[4096,2048]{1,0:T(8,128)(2,1)S(1)} %get-tuple-element.16.near_ref.head_ref, f32[64,128]{1,0:T(8,128)S(1)} %get-tuple-element.17.before_ref), custom_call_target="tpu_custom_call" | custom-call | flops 1073741824 | bytes 17350656 | tf_op jit(solution)/shard_map/pallas_call | solution.py:22
  25.9 1.8 %collective-permute-start.7 = (f32[8,128]{1,0:T(8,128)S(1)}, f32[8,128]{1,0:T(8,128)S(1)}, u32[]{:S(2)}, u32[]{:S(2)}) collective-permute-start(f32[8,128]{1,0:T(8,128)S(1)} %get-tuple-element.18.mine_ref), channel_id=1, source_target_pairs={{0,4},{1,5},{2,6},{3,7},{4,0},{5,1},{6,2},{7,3},{8,12},{9,13},{10,... | collective-permute-start | bytes 12296 | tf_op jit(solution)/shard_map/ppermute | solution.py:267
  27.7 2.5 %shard_map.100.refs_0_ = f32[2048,256]{1,0:T(8,128)S(1)} custom-call(bf16[128,2048]{1,0:T(8,128)(2,1)S(1)} %get-tuple-element.22.one_ref, bf16[128,2048]{1,0:T(8,128)(2,1)S(1)} %get-tuple-element.23.two_ref, bf16[4096,2048]{1,0:T(8,128)(2,1)S(1)} %get-tuple-element.16.near_ref.head_ref), custom_call_target="tpu_custom_call" | custom-call | flops 2147483648 | bytes 17825792 | tf_op jit(solution)/shard_map/pallas_call | solution.py:22
  30.5 2.5 %collective-permute-start.10 = (f32[8,128]{1,0:T(8,128)S(1)}, f32[8,128]{1,0:T(8,128)S(1)}, u32[]{:S(2)}, u32[]{:S(2)}) collective-permute-start(f32[8,128]{1,0:T(8,128)S(1)} %shard_map.97.mine_ref.refs_0_), channel_id=1, source_target_pairs={{0,3},{1,2},{2,1},{3,0},{4,7},{5,6},{6,5},{7,4},{8,11},{9,10},{10,... | collective-permute-start | bytes 12296 | tf_op jit(solution)/shard_map/ppermute | solution.py:267
  33.5 0.6 %collective-permute-start.8 = (f32[8,128]{1,0:T(8,128)S(1)}, f32[8,128]{1,0:T(8,128)S(1)}, u32[]{:S(2)}, u32[]{:S(2)}) collective-permute-start(f32[8,128]{1,0:T(8,128)S(1)} %shard_map.97.mine_ref.refs_0_), channel_id=1, source_target_pairs={{0,1},{1,0},{2,3},{3,2},{4,5},{5,4},{6,7},{7,6},{8,9},{9,8},{10,11... | collective-permute-start | bytes 12296 | tf_op jit(solution)/shard_map/ppermute | solution.py:267
  34.0 2.5 %shard_map.101.refs_1_ = f32[2048,256]{1,0:T(8,128)S(1)} custom-call(bf16[128,2048]{1,0:T(8,128)(2,1)S(1)} %get-tuple-element.22.one_ref, bf16[128,2048]{1,0:T(8,128)(2,1)S(1)} %get-tuple-element.23.two_ref, bf16[4096,2048]{1,0:T(8,128)(2,1)S(1)} %get-tuple-element.16.near_ref.head_ref, f32[8,128]{1,0:T(8,128)S(1)} %shard_map.97.mine_ref.refs_0_), custom_call_target="tpu_custom_call" | custom-call | flops 2147483648 | bytes 17829888 | tf_op jit(solution)/shard_map/pallas_call | solution.py:22
  37.2 0.6 %shard_map.102 = (f32[64,4096]{1,0:T(8,128)S(1)}, f32[64,4096]{1,0:T(8,128)S(1)}) custom-call(f32[8,128]{1,0:T(8,128)S(1)} %shard_map.98.lines_ref, f32[8,128]{1,0:T(8,128)S(1)} %get-tuple-element.18.mine_ref, f32[2048,256]{1,0:T(8,128)S(1)} %shard_map.100.refs_0_, f32[2048,256]{1,0:T(8,128)S(1)} %shard_map.101.refs_1_), custom_call_target="tpu_custom_call" | custom-call | bytes 4202496 | tf_op jit(solution)/shard_map/pallas_call | solution.py:22
  38.0 1.0 %collective-permute-start.14 = (f16[16,4096]{1,0:T(8,128)(2,1)S(1)}, f16[16,4096]{1,0:T(8,128)(2,1)S(1)}, u32[]{:S(2)}, u32[]{:S(2)}) collective-permute-start(f16[16,4096]{1,0:T(8,128)(2,1)S(1)} %get-tuple-element.30), channel_id=1, source_target_pairs={{0,1},{1,0},{2,3},{3,2},{4,5},{5,4},{6,7},{7,6},{8,9},{9,8},{10,11... | collective-permute-start | bytes 393224 | tf_op jit(solution)/shard_map/ppermute | solution.py:267
  39.0 2.1 %collective-permute-start.16 = (f16[16,4096]{1,0:T(8,128)(2,1)S(1)}, f16[16,4096]{1,0:T(8,128)(2,1)S(1)}, u32[]{:S(2)}, u32[]{:S(2)}) collective-permute-start(f16[16,4096]{1,0:T(8,128)(2,1)S(1)} %get-tuple-element.31), channel_id=1, source_target_pairs={{0,3},{1,2},{2,1},{3,0},{4,7},{5,6},{6,5},{7,4},{8,11},{9,10},{10,... | collective-permute-start | bytes 393224 | tf_op jit(solution)/shard_map/ppermute | solution.py:267
  41.7 1.0 %collective-permute-start.11 = (f16[16,4096]{1,0:T(8,128)(2,1)S(1)}, f16[16,4096]{1,0:T(8,128)(2,1)S(1)}, u32[]{:S(2)}, u32[]{:S(2)}) collective-permute-start(f16[16,4096]{1,0:T(8,128)(2,1)S(1)} %get-tuple-element.28), channel_id=1, source_target_pairs={{0,1},{1,0},{2,3},{3,2},{4,5},{5,4},{6,7},{7,6},{8,9},{9,8},{10,11... | collective-permute-start | bytes 393224 | tf_op jit(solution)/shard_map/ppermute | solution.py:267
  42.7 1.1 %collective-permute-start.13 = (f16[16,4096]{1,0:T(8,128)(2,1)S(1)}, f16[16,4096]{1,0:T(8,128)(2,1)S(1)}, u32[]{:S(2)}, u32[]{:S(2)}) collective-permute-start(f16[16,4096]{1,0:T(8,128)(2,1)S(1)} %get-tuple-element.29), channel_id=1, source_target_pairs={{0,1},{1,0},{2,3},{3,2},{4,5},{5,4},{6,7},{7,6},{8,9},{9,8},{10,11... | collective-permute-start | bytes 393224 | tf_op jit(solution)/shard_map/ppermute | solution.py:267
  43.8 2.7 %collective-permute-done.14 = f16[16,4096]{1,0:T(8,128)(2,1)S(1)} collective-permute-done((f16[16,4096]{1,0:T(8,128)(2,1)S(1)}, f16[16,4096]{1,0:T(8,128)(2,1)S(1)}, u32[]{:S(2)}, u32[]{:S(2)}) %collective-permute-start.14) | collective-permute-done | bytes 131104 | tf_op jit(solution)/shard_map/ppermute | solution.py:267
  46.6 1.6 %collective-permute-start.17 = (f16[16,4096]{1,0:T(8,128)(2,1)S(1)}, f16[16,4096]{1,0:T(8,128)(2,1)S(1)}, u32[]{:S(2)}, u32[]{:S(2)}) collective-permute-start(f16[16,4096]{1,0:T(8,128)(2,1)S(1)} %add_convert_fusion), channel_id=1, source_target_pairs={{0,4},{1,5},{2,6},{3,7},{4,0},{5,1},{6,2},{7,3},{8,12},{9,13},{10,... | collective-permute-start | bytes 393224 | tf_op jit(solution)/shard_map/ppermute | solution.py:267
  48.2 1.1 %collective-permute-done.11 = f16[16,4096]{1,0:T(8,128)(2,1)S(1)} collective-permute-done((f16[16,4096]{1,0:T(8,128)(2,1)S(1)}, f16[16,4096]{1,0:T(8,128)(2,1)S(1)}, u32[]{:S(2)}, u32[]{:S(2)}) %collective-permute-start.11) | collective-permute-done | bytes 131104 | tf_op jit(solution)/shard_map/ppermute | solution.py:267
  49.3 1.8 %collective-permute-start.12 = (f16[16,4096]{1,0:T(8,128)(2,1)S(1)}, f16[16,4096]{1,0:T(8,128)(2,1)S(1)}, u32[]{:S(2)}, u32[]{:S(2)}) collective-permute-start(f16[16,4096]{1,0:T(8,128)(2,1)S(1)} %add_convert_fusion.1), channel_id=1, source_target_pairs={{0,2},{1,3},{2,0},{3,1},{4,6},{5,7},{6,4},{7,5},{8,10},{9,11},{10,... | collective-permute-start | bytes 393224 | tf_op jit(solution)/shard_map/ppermute | solution.py:267
  51.1 3.1 %shard_map.99 = (f32[128,2048]{1,0:T(8,128)}, f32[128,2048]{1,0:T(8,128)}, f32[1]{0:T(128)}) custom-call(bf16[64,4224]{1,0:T(8,128)(2,1)S(1)} %pad_maximum_fusion.packed_ref.rows_one_ref.ids_one_ref, bf16[64,4224]{1,0:T(8,128)(2,1)S(1)} %bitcast.6, bf16[64,4224]{1,0:T(8,128)(2,1)S(1)} %pad_maximum_fusion.packed_ref.rows_one_ref.ids_one_ref, ...), custom_call_target="tpu_custom_call" | custom-call | flops 67108864 | bytes 6291456 | tf_op jit(solution)/shard_map/pallas_call | solution.py:242
  54.5 0.7 %multiply_convert_fusion = bf16[16,4096]{1,0:T(8,128)(2,1)} fusion(f16[16,4096]{1,0:T(8,128)(2,1)S(1)} %collective-permute-done.17, f16[16,4096]{1,0:T(8,128)(2,1)S(1)} %collective-permute-done.13, f16[16,4096]{1,0:T(8,128)(2,1)S(1)} %collective-permute-done.12, f32[64,4096]{1,0:T(8,128)S(1)} %get-tuple-element.24), kind=kLoop, calls=%fused_computation.2 | loop fusion | flops 524288 | bytes 786432 | tf_op jit(solution)/shard_map/convert_element_type | solution.py:376
  (37 shorter events, 4.6 us)
Async XLA Ops:
  1.6 12.4 %collective-permute-start.3 = (bf16[16,4224]{1,0:T(8,128)(2,1)S(1)}, bf16[16,4224]{1,0:T(8,128)(2,1)S(1)}, u32[]{:S(2)}, u32[]{:S(2)}) collective-permute-start(bf16[16,4224]{1,0:T(8,128)(2,1)S(1)} %shard_map.93), channel_id=1, source_target_pairs={{0,4},{1,5},{2,6},{3,7},{4,0},{5,1},{6,2},{7,3},{8,12},{9,13},{10,... | collective-permute-start | bytes 405512 | tf_op jit(solution)/shard_map/ppermute | solution.py:267
  5.7 11.4 %collective-permute-start.2 = (bf16[16,4224]{1,0:T(8,128)(2,1)S(1)}, bf16[16,4224]{1,0:T(8,128)(2,1)S(1)}, u32[]{:S(2)}, u32[]{:S(2)}) collective-permute-start(bf16[16,4224]{1,0:T(8,128)(2,1)S(1)} %shard_map.93), channel_id=1, source_target_pairs={{0,3},{1,2},{2,1},{3,0},{4,7},{5,6},{6,5},{7,4},{8,11},{9,10},{10,... | collective-permute-start | bytes 405512 | tf_op jit(solution)/shard_map/ppermute | solution.py:267
  8.2 9.3 %collective-permute-start.1 = (bf16[16,4224]{1,0:T(8,128)(2,1)S(1)}, bf16[16,4224]{1,0:T(8,128)(2,1)S(1)}, u32[]{:S(2)}, u32[]{:S(2)}) collective-permute-start(bf16[16,4224]{1,0:T(8,128)(2,1)S(1)} %shard_map.93), channel_id=1, source_target_pairs={{0,2},{1,3},{2,0},{3,1},{4,6},{5,7},{6,4},{7,5},{8,10},{9,11},{10,... | collective-permute-start | bytes 405512 | tf_op jit(solution)/shard_map/ppermute | solution.py:267
  8.6 8.9 %collective-permute-start = (bf16[16,4224]{1,0:T(8,128)(2,1)S(1)}, bf16[16,4224]{1,0:T(8,128)(2,1)S(1)}, u32[]{:S(2)}, u32[]{:S(2)}) collective-permute-start(bf16[16,4224]{1,0:T(8,128)(2,1)S(1)} %shard_map.93), channel_id=1, source_target_pairs={{0,1},{1,0},{2,3},{3,2},{4,5},{5,4},{6,7},{7,6},{8,9},{9,8},{10,11... | collective-permute-start | bytes 405512 | tf_op jit(solution)/shard_map/ppermute | solution.py:267
  14.0 7.6 %collective-permute-start.6 = (bf16[16,4224]{1,0:T(8,128)(2,1)S(1)}, bf16[16,4224]{1,0:T(8,128)(2,1)S(1)}, u32[]{:S(2)}, u32[]{:S(2)}) collective-permute-start(bf16[16,4224]{1,0:T(8,128)(2,1)S(1)} %collective-permute-done.3), channel_id=1, source_target_pairs={{0,3},{1,2},{2,1},{3,0},{4,7},{5,6},{6,5},{7,4},{8,11},{9,10},{10,... | collective-permute-start | bytes 405512 | tf_op jit(solution)/shard_map/ppermute | solution.py:267
  16.6 5.5 %collective-permute-start.5 = (bf16[16,4224]{1,0:T(8,128)(2,1)S(1)}, bf16[16,4224]{1,0:T(8,128)(2,1)S(1)}, u32[]{:S(2)}, u32[]{:S(2)}) collective-permute-start(bf16[16,4224]{1,0:T(8,128)(2,1)S(1)} %collective-permute-done.3), channel_id=1, source_target_pairs={{0,2},{1,3},{2,0},{3,1},{4,6},{5,7},{6,4},{7,5},{8,10},{9,11},{10,... | collective-permute-start | bytes 405512 | tf_op jit(solution)/shard_map/ppermute | solution.py:267
  17.0 5.1 %collective-permute-start.4 = (bf16[16,4224]{1,0:T(8,128)(2,1)S(1)}, bf16[16,4224]{1,0:T(8,128)(2,1)S(1)}, u32[]{:S(2)}, u32[]{:S(2)}) collective-permute-start(bf16[16,4224]{1,0:T(8,128)(2,1)S(1)} %collective-permute-done.3), channel_id=1, source_target_pairs={{0,1},{1,0},{2,3},{3,2},{4,5},{5,4},{6,7},{7,6},{8,9},{9,8},{10,11... | collective-permute-start | bytes 405512 | tf_op jit(solution)/shard_map/ppermute | solution.py:267
  25.9 4.5 %collective-permute-start.7 = (f32[8,128]{1,0:T(8,128)S(1)}, f32[8,128]{1,0:T(8,128)S(1)}, u32[]{:S(2)}, u32[]{:S(2)}) collective-permute-start(f32[8,128]{1,0:T(8,128)S(1)} %get-tuple-element.18.mine_ref), channel_id=1, source_target_pairs={{0,4},{1,5},{2,6},{3,7},{4,0},{5,1},{6,2},{7,3},{8,12},{9,13},{10,... | collective-permute-start | bytes 12296 | tf_op jit(solution)/shard_map/ppermute | solution.py:267
  30.5 6.0 %collective-permute-start.10 = (f32[8,128]{1,0:T(8,128)S(1)}, f32[8,128]{1,0:T(8,128)S(1)}, u32[]{:S(2)}, u32[]{:S(2)}) collective-permute-start(f32[8,128]{1,0:T(8,128)S(1)} %shard_map.97.mine_ref.refs_0_), channel_id=1, source_target_pairs={{0,3},{1,2},{2,1},{3,0},{4,7},{5,6},{6,5},{7,4},{8,11},{9,10},{10,... | collective-permute-start | bytes 12296 | tf_op jit(solution)/shard_map/ppermute | solution.py:267
  33.0 3.6 %collective-permute-start.9 = (f32[8,128]{1,0:T(8,128)S(1)}, f32[8,128]{1,0:T(8,128)S(1)}, u32[]{:S(2)}, u32[]{:S(2)}) collective-permute-start(f32[8,128]{1,0:T(8,128)S(1)} %shard_map.97.mine_ref.refs_0_), channel_id=1, source_target_pairs={{0,2},{1,3},{2,0},{3,1},{4,6},{5,7},{6,4},{7,5},{8,10},{9,11},{10,... | collective-permute-start | bytes 12296 | tf_op jit(solution)/shard_map/ppermute | solution.py:267
  33.5 3.6 %collective-permute-start.8 = (f32[8,128]{1,0:T(8,128)S(1)}, f32[8,128]{1,0:T(8,128)S(1)}, u32[]{:S(2)}, u32[]{:S(2)}) collective-permute-start(f32[8,128]{1,0:T(8,128)S(1)} %shard_map.97.mine_ref.refs_0_), channel_id=1, source_target_pairs={{0,1},{1,0},{2,3},{3,2},{4,5},{5,4},{6,7},{7,6},{8,9},{9,8},{10,11... | collective-permute-start | bytes 12296 | tf_op jit(solution)/shard_map/ppermute | solution.py:267
  38.0 8.5 %collective-permute-start.14 = (f16[16,4096]{1,0:T(8,128)(2,1)S(1)}, f16[16,4096]{1,0:T(8,128)(2,1)S(1)}, u32[]{:S(2)}, u32[]{:S(2)}) collective-permute-start(f16[16,4096]{1,0:T(8,128)(2,1)S(1)} %get-tuple-element.30), channel_id=1, source_target_pairs={{0,1},{1,0},{2,3},{3,2},{4,5},{5,4},{6,7},{7,6},{8,9},{9,8},{10,11... | collective-permute-start | bytes 393224 | tf_op jit(solution)/shard_map/ppermute | solution.py:267
  39.0 7.5 %collective-permute-start.16 = (f16[16,4096]{1,0:T(8,128)(2,1)S(1)}, f16[16,4096]{1,0:T(8,128)(2,1)S(1)}, u32[]{:S(2)}, u32[]{:S(2)}) collective-permute-start(f16[16,4096]{1,0:T(8,128)(2,1)S(1)} %get-tuple-element.31), channel_id=1, source_target_pairs={{0,3},{1,2},{2,1},{3,0},{4,7},{5,6},{6,5},{7,4},{8,11},{9,10},{10,... | collective-permute-start | bytes 393224 | tf_op jit(solution)/shard_map/ppermute | solution.py:267
  41.1 5.4 %collective-permute-start.15 = (f16[16,4096]{1,0:T(8,128)(2,1)S(1)}, f16[16,4096]{1,0:T(8,128)(2,1)S(1)}, u32[]{:S(2)}, u32[]{:S(2)}) collective-permute-start(f16[16,4096]{1,0:T(8,128)(2,1)S(1)} %get-tuple-element.32), channel_id=1, source_target_pairs={{0,2},{1,3},{2,0},{3,1},{4,6},{5,7},{6,4},{7,5},{8,10},{9,11},{10,... | collective-permute-start | bytes 393224 | tf_op jit(solution)/shard_map/ppermute | solution.py:267
  41.5 9.6 %copy-start.1 = (f32[128,2048]{1,0:T(8,128)S(1)}, f32[128,2048]{1,0:T(8,128)}, u32[]{:S(2)}) copy-start(f32[128,2048]{1,0:T(8,128)} %momentum_ref.1) | copy-start | bytes 3145732
  41.5 9.6 %copy-start.2 = (f32[128,2048]{1,0:T(8,128)S(1)}, f32[128,2048]{1,0:T(8,128)}, u32[]{:S(2)}) copy-start(f32[128,2048]{1,0:T(8,128)} %peer_ref.1) | copy-start | bytes 3145732
  41.6 9.5 %copy-start = (f32[128,2048]{1,0:T(8,128)S(1)}, f32[128,2048]{1,0:T(8,128)}, u32[]{:S(2)}) copy-start(f32[128,2048]{1,0:T(8,128)} %global_ref.1) | copy-start | bytes 3145732
  41.7 7.6 %collective-permute-start.11 = (f16[16,4096]{1,0:T(8,128)(2,1)S(1)}, f16[16,4096]{1,0:T(8,128)(2,1)S(1)}, u32[]{:S(2)}, u32[]{:S(2)}) collective-permute-start(f16[16,4096]{1,0:T(8,128)(2,1)S(1)} %get-tuple-element.28), channel_id=1, source_target_pairs={{0,1},{1,0},{2,3},{3,2},{4,5},{5,4},{6,7},{7,6},{8,9},{9,8},{10,11... | collective-permute-start | bytes 393224 | tf_op jit(solution)/shard_map/ppermute | solution.py:267
  42.7 11.6 %collective-permute-start.13 = (f16[16,4096]{1,0:T(8,128)(2,1)S(1)}, f16[16,4096]{1,0:T(8,128)(2,1)S(1)}, u32[]{:S(2)}, u32[]{:S(2)}) collective-permute-start(f16[16,4096]{1,0:T(8,128)(2,1)S(1)} %get-tuple-element.29), channel_id=1, source_target_pairs={{0,1},{1,0},{2,3},{3,2},{4,5},{5,4},{6,7},{7,6},{8,9},{9,8},{10,11... | collective-permute-start | bytes 393224 | tf_op jit(solution)/shard_map/ppermute | solution.py:267
  46.6 7.7 %collective-permute-start.17 = (f16[16,4096]{1,0:T(8,128)(2,1)S(1)}, f16[16,4096]{1,0:T(8,128)(2,1)S(1)}, u32[]{:S(2)}, u32[]{:S(2)}) collective-permute-start(f16[16,4096]{1,0:T(8,128)(2,1)S(1)} %add_convert_fusion), channel_id=1, source_target_pairs={{0,4},{1,5},{2,6},{3,7},{4,0},{5,1},{6,2},{7,3},{8,12},{9,13},{10,... | collective-permute-start | bytes 393224 | tf_op jit(solution)/shard_map/ppermute | solution.py:267
  49.3 5.2 %collective-permute-start.12 = (f16[16,4096]{1,0:T(8,128)(2,1)S(1)}, f16[16,4096]{1,0:T(8,128)(2,1)S(1)}, u32[]{:S(2)}, u32[]{:S(2)}) collective-permute-start(f16[16,4096]{1,0:T(8,128)(2,1)S(1)} %add_convert_fusion.1), channel_id=1, source_target_pairs={{0,2},{1,3},{2,0},{3,1},{4,6},{5,7},{6,4},{7,5},{8,10},{9,11},{10,... | collective-permute-start | bytes 393224 | tf_op jit(solution)/shard_map/ppermute | solution.py:267

commit v26 on v25

--- a/solution.py
+++ b/solution.py
@@ -309,7 +309,7 @@
     y_near = moved([blocks[1]], 1)[0]
     z_near = moved([blocks[2] + relayed], 2)[0]
     sums = [blocks[0] + z_near + y_near]
-    sums += [blocks[i] + a + b + c for i, a, b, c in zip(far, one, two, three)]
+    sums += [blocks[i] + a + b + c for i, a, b, c in zip(far, one, three, two)]
     for step in far_steps()[::-1]:
         keep = len(sums) // 2
         sums = [a + b for a, b in zip(sums[:keep], moved(sums[keep:], step))]

time: 55.4 us -> 56.4 us (1.018)
  waiting for transfers between devices: 5.37 us -> 6.71 us
    ppermute x18, waiting for transfers between devices: 5.37 us -> 6.71 us  [swap(): lax.ppermute(value, AXIS, [(i, i ^ step) for i in range(lax.axis_size(AXI...]
  transfers between devices with their start and end apart: 18 -> 18, of which waited for: 7 -> 8; matrix products, arithmetic and copies ran while one was open for 0% -> 0% of each run, Pallas kernels for 30% -> 30%
where the time goes in v26:
time: 56.4 us; the launch traced here: 56.3 us
  starting transfers between devices  25.3 us (45%)
  Pallas kernels  22.3 us (40%)
  waiting for transfers between devices  6.71 us (12%)
  other arithmetic  1.09 us (2%)
  between operations  0.78 us (1%)
    ppermute x18, starting transfers between devices, swap(): lax.ppermute(value, AXIS, [(i, i ^ step) for i in range(lax.axis_size(AXI...  25.3 us
    pallas_call x9, Pallas kernels, call(): pl.pallas_call(kernel, out_shape=outs, in_specs=[pl.BlockSpec(memory_spac...  19.2 us
    ppermute x18, waiting for transfers between devices, swap(): lax.ppermute(value, AXIS, [(i, i ^ step) for i in range(lax.axis_size(AXI...  6.71 us
    pallas_call x1, Pallas kernels, frag_update(): pl.pallas_call(functools.partial(frag_kernel, members), grid=(width // TI...  3.08 us
  transfers between devices with their start and end apart: 18, of which 8 were waited for; matrix products, arithmetic and copies ran while one was open for 0% of the time, Pallas kernels for 30%

profile of v26, /device:TPU:0, one launch (start us, length us, event | category | flops | bytes accessed | tf_op | source)
XLA Modules:
  0.0 56.3 jit_solution(15580698271149187293)
XLA Ops:
  0.6 0.9 %shard_map.93 = bf16[16,4224]{1,0:T(8,128)(2,1)S(1)} custom-call(s32[16]{0:T(128)} %targets.1, bf16[16,4096]{1,0:T(8,128)(2,1)} %rows.1), custom_call_target="tpu_custom_call" | custom-call | bytes 131136 | tf_op jit(solution)/shard_map/pallas_call | solution.py:22
  1.6 4.1 %collective-permute-start.3 = (bf16[16,4224]{1,0:T(8,128)(2,1)S(1)}, bf16[16,4224]{1,0:T(8,128)(2,1)S(1)}, u32[]{:S(2)}, u32[]{:S(2)}) collective-permute-start(bf16[16,4224]{1,0:T(8,128)(2,1)S(1)} %shard_map.93), channel_id=1, source_target_pairs={{0,4},{1,5},{2,6},{3,7},{4,0},{5,1},{6,2},{7,3},{8,12},{9,13},{10,... | collective-permute-start | bytes 405512 | tf_op jit(solution)/shard_map/ppermute | solution.py:267
  5.7 2.5 %collective-permute-start.2 = (bf16[16,4224]{1,0:T(8,128)(2,1)S(1)}, bf16[16,4224]{1,0:T(8,128)(2,1)S(1)}, u32[]{:S(2)}, u32[]{:S(2)}) collective-permute-start(bf16[16,4224]{1,0:T(8,128)(2,1)S(1)} %shard_map.93), channel_id=1, source_target_pairs={{0,3},{1,2},{2,1},{3,0},{4,7},{5,6},{6,5},{7,4},{8,11},{9,10},{10,... | collective-permute-start | bytes 405512 | tf_op jit(solution)/shard_map/ppermute | solution.py:267
  9.2 4.8 %shard_map.94.held_ref = bf16[4096,2048]{1,0:T(8,128)(2,1)S(1)} custom-call(bf16[4096,2048]{1,0:T(8,128)(2,1)} %head.3), custom_call_target="tpu_custom_call" | custom-call | bytes 16777216 | tf_op jit(solution)/shard_map/pallas_call | solution.py:22
  14.0 2.6 %collective-permute-start.6 = (bf16[16,4224]{1,0:T(8,128)(2,1)S(1)}, bf16[16,4224]{1,0:T(8,128)(2,1)S(1)}, u32[]{:S(2)}, u32[]{:S(2)}) collective-permute-start(bf16[16,4224]{1,0:T(8,128)(2,1)S(1)} %collective-permute-done.3), channel_id=1, source_target_pairs={{0,3},{1,2},{2,1},{3,0},{4,7},{5,6},{6,5},{7,4},{8,11},{9,10},{10,... | collective-permute-start | bytes 405512 | tf_op jit(solution)/shard_map/ppermute | solution.py:267
  17.6 4.0 %shard_map.95 = (bf16[4096,2048]{1,0:T(8,128)(2,1)S(1)}, f32[64,2048]{1,0:T(8,128)S(1)}, bf16[128,2048]{1,0:T(8,128)(2,1)S(1)}, f32[64,128]{1,0:T(8,128)S(1)}) custom-call(bf16[64,4224]{1,0:T(8,128)(2,1)S(1)} %pad_maximum_fusion.packed_ref.rows_one_ref.ids_one_ref, bf16[4096,2048]{1,0:T(8,128)(2,1)} %head.3, ...), custom_call_target="tpu_custom_call", output_to_operand_aliasing={{0}: (2, {})} | custom-call | flops 1073741824 | bytes 34095104 | tf_op jit(solution)/shard_map/pallas_call | solution.py:22
  22.2 3.7 %shard_map.96 = (f32[64,2048]{1,0:T(8,128)S(1)}, bf16[128,2048]{1,0:T(8,128)(2,1)S(1)}, f32[8,128]{1,0:T(8,128)S(1)}) custom-call(bf16[64,4224]{1,0:T(8,128)(2,1)S(1)} %bitcast.5, bf16[4096,2048]{1,0:T(8,128)(2,1)S(1)} %get-tuple-element.16.near_ref.head_ref, f32[64,128]{1,0:T(8,128)S(1)} %get-tuple-element.17.before_ref), custom_call_target="tpu_custom_call" | custom-call | flops 1073741824 | bytes 17350656 | tf_op jit(solution)/shard_map/pallas_call | solution.py:22
  25.9 1.8 %collective-permute-start.7 = (f32[8,128]{1,0:T(8,128)S(1)}, f32[8,128]{1,0:T(8,128)S(1)}, u32[]{:S(2)}, u32[]{:S(2)}) collective-permute-start(f32[8,128]{1,0:T(8,128)S(1)} %get-tuple-element.18.mine_ref), channel_id=1, source_target_pairs={{0,4},{1,5},{2,6},{3,7},{4,0},{5,1},{6,2},{7,3},{8,12},{9,13},{10,... | collective-permute-start | bytes 12296 | tf_op jit(solution)/shard_map/ppermute | solution.py:267
  27.7 2.5 %shard_map.100.refs_0_ = f32[2048,256]{1,0:T(8,128)S(1)} custom-call(bf16[128,2048]{1,0:T(8,128)(2,1)S(1)} %get-tuple-element.22.one_ref, bf16[128,2048]{1,0:T(8,128)(2,1)S(1)} %get-tuple-element.23.two_ref, bf16[4096,2048]{1,0:T(8,128)(2,1)S(1)} %get-tuple-element.16.near_ref.head_ref), custom_call_target="tpu_custom_call" | custom-call | flops 2147483648 | bytes 17825792 | tf_op jit(solution)/shard_map/pallas_call | solution.py:22
  30.5 2.5 %collective-permute-start.10 = (f32[8,128]{1,0:T(8,128)S(1)}, f32[8,128]{1,0:T(8,128)S(1)}, u32[]{:S(2)}, u32[]{:S(2)}) collective-permute-start(f32[8,128]{1,0:T(8,128)S(1)} %shard_map.97.mine_ref.refs_0_), channel_id=1, source_target_pairs={{0,3},{1,2},{2,1},{3,0},{4,7},{5,6},{6,5},{7,4},{8,11},{9,10},{10,... | collective-permute-start | bytes 12296 | tf_op jit(solution)/shard_map/ppermute | solution.py:267
  34.0 2.5 %shard_map.101.refs_1_ = f32[2048,256]{1,0:T(8,128)S(1)} custom-call(bf16[128,2048]{1,0:T(8,128)(2,1)S(1)} %get-tuple-element.22.one_ref, bf16[128,2048]{1,0:T(8,128)(2,1)S(1)} %get-tuple-element.23.two_ref, bf16[4096,2048]{1,0:T(8,128)(2,1)S(1)} %get-tuple-element.16.near_ref.head_ref, f32[8,128]{1,0:T(8,128)S(1)} %shard_map.97.mine_ref.refs_0_), custom_call_target="tpu_custom_call" | custom-call | flops 2147483648 | bytes 17829888 | tf_op jit(solution)/shard_map/pallas_call | solution.py:22
  37.2 0.6 %shard_map.102 = (f32[64,4096]{1,0:T(8,128)S(1)}, f32[64,4096]{1,0:T(8,128)S(1)}) custom-call(f32[8,128]{1,0:T(8,128)S(1)} %shard_map.98.lines_ref, f32[8,128]{1,0:T(8,128)S(1)} %get-tuple-element.18.mine_ref, f32[2048,256]{1,0:T(8,128)S(1)} %shard_map.100.refs_0_, f32[2048,256]{1,0:T(8,128)S(1)} %shard_map.101.refs_1_), custom_call_target="tpu_custom_call" | custom-call | bytes 4202496 | tf_op jit(solution)/shard_map/pallas_call | solution.py:22
  38.0 1.0 %collective-permute-start.14 = (f16[16,4096]{1,0:T(8,128)(2,1)S(1)}, f16[16,4096]{1,0:T(8,128)(2,1)S(1)}, u32[]{:S(2)}, u32[]{:S(2)}) collective-permute-start(f16[16,4096]{1,0:T(8,128)(2,1)S(1)} %get-tuple-element.30), channel_id=1, source_target_pairs={{0,1},{1,0},{2,3},{3,2},{4,5},{5,4},{6,7},{7,6},{8,9},{9,8},{10,11... | collective-permute-start | bytes 393224 | tf_op jit(solution)/shard_map/ppermute | solution.py:267
  39.0 1.6 %collective-permute-start.16 = (f16[16,4096]{1,0:T(8,128)(2,1)S(1)}, f16[16,4096]{1,0:T(8,128)(2,1)S(1)}, u32[]{:S(2)}, u32[]{:S(2)}) collective-permute-start(f16[16,4096]{1,0:T(8,128)(2,1)S(1)} %get-tuple-element.31), channel_id=1, source_target_pairs={{0,2},{1,3},{2,0},{3,1},{4,6},{5,7},{6,4},{7,5},{8,10},{9,11},{10,... | collective-permute-start | bytes 393224 | tf_op jit(solution)/shard_map/ppermute | solution.py:267
  40.6 1.0 %collective-permute-start.15 = (f16[16,4096]{1,0:T(8,128)(2,1)S(1)}, f16[16,4096]{1,0:T(8,128)(2,1)S(1)}, u32[]{:S(2)}, u32[]{:S(2)}) collective-permute-start(f16[16,4096]{1,0:T(8,128)(2,1)S(1)} %get-tuple-element.32), channel_id=1, source_target_pairs={{0,3},{1,2},{2,1},{3,0},{4,7},{5,6},{6,5},{7,4},{8,11},{9,10},{10,... | collective-permute-start | bytes 393224 | tf_op jit(solution)/shard_map/ppermute | solution.py:267
  41.7 1.0 %collective-permute-start.11 = (f16[16,4096]{1,0:T(8,128)(2,1)S(1)}, f16[16,4096]{1,0:T(8,128)(2,1)S(1)}, u32[]{:S(2)}, u32[]{:S(2)}) collective-permute-start(f16[16,4096]{1,0:T(8,128)(2,1)S(1)} %get-tuple-element.28), channel_id=1, source_target_pairs={{0,1},{1,0},{2,3},{3,2},{4,5},{5,4},{6,7},{7,6},{8,9},{9,8},{10,11... | collective-permute-start | bytes 393224 | tf_op jit(solution)/shard_map/ppermute | solution.py:267
  42.7 1.1 %collective-permute-start.13 = (f16[16,4096]{1,0:T(8,128)(2,1)S(1)}, f16[16,4096]{1,0:T(8,128)(2,1)S(1)}, u32[]{:S(2)}, u32[]{:S(2)}) collective-permute-start(f16[16,4096]{1,0:T(8,128)(2,1)S(1)} %get-tuple-element.29), channel_id=1, source_target_pairs={{0,1},{1,0},{2,3},{3,2},{4,5},{5,4},{6,7},{7,6},{8,9},{9,8},{10,11... | collective-permute-start | bytes 393224 | tf_op jit(solution)/shard_map/ppermute | solution.py:267
  43.8 3.4 %collective-permute-done.14 = f16[16,4096]{1,0:T(8,128)(2,1)S(1)} collective-permute-done((f16[16,4096]{1,0:T(8,128)(2,1)S(1)}, f16[16,4096]{1,0:T(8,128)(2,1)S(1)}, u32[]{:S(2)}, u32[]{:S(2)}) %collective-permute-start.14) | collective-permute-done | bytes 131104 | tf_op jit(solution)/shard_map/ppermute | solution.py:267
  47.2 1.7 %collective-permute-start.17 = (f16[16,4096]{1,0:T(8,128)(2,1)S(1)}, f16[16,4096]{1,0:T(8,128)(2,1)S(1)}, u32[]{:S(2)}, u32[]{:S(2)}) collective-permute-start(f16[16,4096]{1,0:T(8,128)(2,1)S(1)} %add_convert_fusion), channel_id=1, source_target_pairs={{0,4},{1,5},{2,6},{3,7},{4,0},{5,1},{6,2},{7,3},{8,12},{9,13},{10,... | collective-permute-start | bytes 393224 | tf_op jit(solution)/shard_map/ppermute | solution.py:267
  48.9 1.0 %collective-permute-done.11 = f16[16,4096]{1,0:T(8,128)(2,1)S(1)} collective-permute-done((f16[16,4096]{1,0:T(8,128)(2,1)S(1)}, f16[16,4096]{1,0:T(8,128)(2,1)S(1)}, u32[]{:S(2)}, u32[]{:S(2)}) %collective-permute-start.11) | collective-permute-done | bytes 131104 | tf_op jit(solution)/shard_map/ppermute | solution.py:267
  50.0 1.5 %collective-permute-start.12 = (f16[16,4096]{1,0:T(8,128)(2,1)S(1)}, f16[16,4096]{1,0:T(8,128)(2,1)S(1)}, u32[]{:S(2)}, u32[]{:S(2)}) collective-permute-start(f16[16,4096]{1,0:T(8,128)(2,1)S(1)} %add_convert_fusion.1), channel_id=1, source_target_pairs={{0,2},{1,3},{2,0},{3,1},{4,6},{5,7},{6,4},{7,5},{8,10},{9,11},{10,... | collective-permute-start | bytes 393224 | tf_op jit(solution)/shard_map/ppermute | solution.py:267
  51.5 3.1 %shard_map.99 = (f32[128,2048]{1,0:T(8,128)}, f32[128,2048]{1,0:T(8,128)}, f32[1]{0:T(128)}) custom-call(bf16[64,4224]{1,0:T(8,128)(2,1)S(1)} %pad_maximum_fusion.packed_ref.rows_one_ref.ids_one_ref, bf16[64,4224]{1,0:T(8,128)(2,1)S(1)} %bitcast.6, bf16[64,4224]{1,0:T(8,128)(2,1)S(1)} %pad_maximum_fusion.packed_ref.rows_one_ref.ids_one_ref, ...), custom_call_target="tpu_custom_call" | custom-call | flops 67108864 | bytes 6291456 | tf_op jit(solution)/shard_map/pallas_call | solution.py:242
  54.7 0.8 %collective-permute-done.12 = f16[16,4096]{1,0:T(8,128)(2,1)S(1)} collective-permute-done((f16[16,4096]{1,0:T(8,128)(2,1)S(1)}, f16[16,4096]{1,0:T(8,128)(2,1)S(1)}, u32[]{:S(2)}, u32[]{:S(2)}) %collective-permute-start.12) | collective-permute-done | bytes 131104 | tf_op jit(solution)/shard_map/ppermute | solution.py:267
  55.5 0.7 %multiply_convert_fusion = bf16[16,4096]{1,0:T(8,128)(2,1)} fusion(f16[16,4096]{1,0:T(8,128)(2,1)S(1)} %collective-permute-done.17, f16[16,4096]{1,0:T(8,128)(2,1)S(1)} %collective-permute-done.13, f16[16,4096]{1,0:T(8,128)(2,1)S(1)} %collective-permute-done.12, f32[64,4096]{1,0:T(8,128)S(1)} %get-tuple-element.24), kind=kLoop, calls=%fused_computation.2 | loop fusion | flops 524288 | bytes 786432 | tf_op jit(solution)/shard_map/convert_element_type | solution.py:376
  (37 shorter events, 5.1 us)
Async XLA Ops:
  1.6 12.4 %collective-permute-start.3 = (bf16[16,4224]{1,0:T(8,128)(2,1)S(1)}, bf16[16,4224]{1,0:T(8,128)(2,1)S(1)}, u32[]{:S(2)}, u32[]{:S(2)}) collective-permute-start(bf16[16,4224]{1,0:T(8,128)(2,1)S(1)} %shard_map.93), channel_id=1, source_target_pairs={{0,4},{1,5},{2,6},{3,7},{4,0},{5,1},{6,2},{7,3},{8,12},{9,13},{10,... | collective-permute-start | bytes 405512 | tf_op jit(solution)/shard_map/ppermute | solution.py:267
  5.7 11.4 %collective-permute-start.2 = (bf16[16,4224]{1,0:T(8,128)(2,1)S(1)}, bf16[16,4224]{1,0:T(8,128)(2,1)S(1)}, u32[]{:S(2)}, u32[]{:S(2)}) collective-permute-start(bf16[16,4224]{1,0:T(8,128)(2,1)S(1)} %shard_map.93), channel_id=1, source_target_pairs={{0,3},{1,2},{2,1},{3,0},{4,7},{5,6},{6,5},{7,4},{8,11},{9,10},{10,... | collective-permute-start | bytes 405512 | tf_op jit(solution)/shard_map/ppermute | solution.py:267
  8.2 9.3 %collective-permute-start.1 = (bf16[16,4224]{1,0:T(8,128)(2,1)S(1)}, bf16[16,4224]{1,0:T(8,128)(2,1)S(1)}, u32[]{:S(2)}, u32[]{:S(2)}) collective-permute-start(bf16[16,4224]{1,0:T(8,128)(2,1)S(1)} %shard_map.93), channel_id=1, source_target_pairs={{0,2},{1,3},{2,0},{3,1},{4,6},{5,7},{6,4},{7,5},{8,10},{9,11},{10,... | collective-permute-start | bytes 405512 | tf_op jit(solution)/shard_map/ppermute | solution.py:267
  8.6 8.9 %collective-permute-start = (bf16[16,4224]{1,0:T(8,128)(2,1)S(1)}, bf16[16,4224]{1,0:T(8,128)(2,1)S(1)}, u32[]{:S(2)}, u32[]{:S(2)}) collective-permute-start(bf16[16,4224]{1,0:T(8,128)(2,1)S(1)} %shard_map.93), channel_id=1, source_target_pairs={{0,1},{1,0},{2,3},{3,2},{4,5},{5,4},{6,7},{7,6},{8,9},{9,8},{10,11... | collective-permute-start | bytes 405512 | tf_op jit(solution)/shard_map/ppermute | solution.py:267
  14.0 7.6 %collective-permute-start.6 = (bf16[16,4224]{1,0:T(8,128)(2,1)S(1)}, bf16[16,4224]{1,0:T(8,128)(2,1)S(1)}, u32[]{:S(2)}, u32[]{:S(2)}) collective-permute-start(bf16[16,4224]{1,0:T(8,128)(2,1)S(1)} %collective-permute-done.3), channel_id=1, source_target_pairs={{0,3},{1,2},{2,1},{3,0},{4,7},{5,6},{6,5},{7,4},{8,11},{9,10},{10,... | collective-permute-start | bytes 405512 | tf_op jit(solution)/shard_map/ppermute | solution.py:267
  16.6 5.5 %collective-permute-start.5 = (bf16[16,4224]{1,0:T(8,128)(2,1)S(1)}, bf16[16,4224]{1,0:T(8,128)(2,1)S(1)}, u32[]{:S(2)}, u32[]{:S(2)}) collective-permute-start(bf16[16,4224]{1,0:T(8,128)(2,1)S(1)} %collective-permute-done.3), channel_id=1, source_target_pairs={{0,2},{1,3},{2,0},{3,1},{4,6},{5,7},{6,4},{7,5},{8,10},{9,11},{10,... | collective-permute-start | bytes 405512 | tf_op jit(solution)/shard_map/ppermute | solution.py:267
  17.0 5.1 %collective-permute-start.4 = (bf16[16,4224]{1,0:T(8,128)(2,1)S(1)}, bf16[16,4224]{1,0:T(8,128)(2,1)S(1)}, u32[]{:S(2)}, u32[]{:S(2)}) collective-permute-start(bf16[16,4224]{1,0:T(8,128)(2,1)S(1)} %collective-permute-done.3), channel_id=1, source_target_pairs={{0,1},{1,0},{2,3},{3,2},{4,5},{5,4},{6,7},{7,6},{8,9},{9,8},{10,11... | collective-permute-start | bytes 405512 | tf_op jit(solution)/shard_map/ppermute | solution.py:267
  25.9 4.5 %collective-permute-start.7 = (f32[8,128]{1,0:T(8,128)S(1)}, f32[8,128]{1,0:T(8,128)S(1)}, u32[]{:S(2)}, u32[]{:S(2)}) collective-permute-start(f32[8,128]{1,0:T(8,128)S(1)} %get-tuple-element.18.mine_ref), channel_id=1, source_target_pairs={{0,4},{1,5},{2,6},{3,7},{4,0},{5,1},{6,2},{7,3},{8,12},{9,13},{10,... | collective-permute-start | bytes 12296 | tf_op jit(solution)/shard_map/ppermute | solution.py:267
  30.5 6.0 %collective-permute-start.10 = (f32[8,128]{1,0:T(8,128)S(1)}, f32[8,128]{1,0:T(8,128)S(1)}, u32[]{:S(2)}, u32[]{:S(2)}) collective-permute-start(f32[8,128]{1,0:T(8,128)S(1)} %shard_map.97.mine_ref.refs_0_), channel_id=1, source_target_pairs={{0,3},{1,2},{2,1},{3,0},{4,7},{5,6},{6,5},{7,4},{8,11},{9,10},{10,... | collective-permute-start | bytes 12296 | tf_op jit(solution)/shard_map/ppermute | solution.py:267
  33.0 3.6 %collective-permute-start.9 = (f32[8,128]{1,0:T(8,128)S(1)}, f32[8,128]{1,0:T(8,128)S(1)}, u32[]{:S(2)}, u32[]{:S(2)}) collective-permute-start(f32[8,128]{1,0:T(8,128)S(1)} %shard_map.97.mine_ref.refs_0_), channel_id=1, source_target_pairs={{0,2},{1,3},{2,0},{3,1},{4,6},{5,7},{6,4},{7,5},{8,10},{9,11},{10,... | collective-permute-start | bytes 12296 | tf_op jit(solution)/shard_map/ppermute | solution.py:267
  33.5 3.6 %collective-permute-start.8 = (f32[8,128]{1,0:T(8,128)S(1)}, f32[8,128]{1,0:T(8,128)S(1)}, u32[]{:S(2)}, u32[]{:S(2)}) collective-permute-start(f32[8,128]{1,0:T(8,128)S(1)} %shard_map.97.mine_ref.refs_0_), channel_id=1, source_target_pairs={{0,1},{1,0},{2,3},{3,2},{4,5},{5,4},{6,7},{7,6},{8,9},{9,8},{10,11... | collective-permute-start | bytes 12296 | tf_op jit(solution)/shard_map/ppermute | solution.py:267
  38.0 9.2 %collective-permute-start.14 = (f16[16,4096]{1,0:T(8,128)(2,1)S(1)}, f16[16,4096]{1,0:T(8,128)(2,1)S(1)}, u32[]{:S(2)}, u32[]{:S(2)}) collective-permute-start(f16[16,4096]{1,0:T(8,128)(2,1)S(1)} %get-tuple-element.30), channel_id=1, source_target_pairs={{0,1},{1,0},{2,3},{3,2},{4,5},{5,4},{6,7},{7,6},{8,9},{9,8},{10,11... | collective-permute-start | bytes 393224 | tf_op jit(solution)/shard_map/ppermute | solution.py:267
  39.0 8.2 %collective-permute-start.16 = (f16[16,4096]{1,0:T(8,128)(2,1)S(1)}, f16[16,4096]{1,0:T(8,128)(2,1)S(1)}, u32[]{:S(2)}, u32[]{:S(2)}) collective-permute-start(f16[16,4096]{1,0:T(8,128)(2,1)S(1)} %get-tuple-element.31), channel_id=1, source_target_pairs={{0,2},{1,3},{2,0},{3,1},{4,6},{5,7},{6,4},{7,5},{8,10},{9,11},{10,... | collective-permute-start | bytes 393224 | tf_op jit(solution)/shard_map/ppermute | solution.py:267
  40.6 6.6 %collective-permute-start.15 = (f16[16,4096]{1,0:T(8,128)(2,1)S(1)}, f16[16,4096]{1,0:T(8,128)(2,1)S(1)}, u32[]{:S(2)}, u32[]{:S(2)}) collective-permute-start(f16[16,4096]{1,0:T(8,128)(2,1)S(1)} %get-tuple-element.32), channel_id=1, source_target_pairs={{0,3},{1,2},{2,1},{3,0},{4,7},{5,6},{6,5},{7,4},{8,11},{9,10},{10,... | collective-permute-start | bytes 393224 | tf_op jit(solution)/shard_map/ppermute | solution.py:267
  41.5 9.9 %copy-start.1 = (f32[128,2048]{1,0:T(8,128)S(1)}, f32[128,2048]{1,0:T(8,128)}, u32[]{:S(2)}) copy-start(f32[128,2048]{1,0:T(8,128)} %momentum_ref.1) | copy-start | bytes 3145732
  41.5 9.9 %copy-start.2 = (f32[128,2048]{1,0:T(8,128)S(1)}, f32[128,2048]{1,0:T(8,128)}, u32[]{:S(2)}) copy-start(f32[128,2048]{1,0:T(8,128)} %peer_ref.1) | copy-start | bytes 3145732
  41.6 9.9 %copy-start = (f32[128,2048]{1,0:T(8,128)S(1)}, f32[128,2048]{1,0:T(8,128)}, u32[]{:S(2)}) copy-start(f32[128,2048]{1,0:T(8,128)} %global_ref.1) | copy-start | bytes 3145732
  41.7 8.3 %collective-permute-start.11 = (f16[16,4096]{1,0:T(8,128)(2,1)S(1)}, f16[16,4096]{1,0:T(8,128)(2,1)S(1)}, u32[]{:S(2)}, u32[]{:S(2)}) collective-permute-start(f16[16,4096]{1,0:T(8,128)(2,1)S(1)} %get-tuple-element.28), channel_id=1, source_target_pairs={{0,1},{1,0},{2,3},{3,2},{4,5},{5,4},{6,7},{7,6},{8,9},{9,8},{10,11... | collective-permute-start | bytes 393224 | tf_op jit(solution)/shard_map/ppermute | solution.py:267
  42.7 11.9 %collective-permute-start.13 = (f16[16,4096]{1,0:T(8,128)(2,1)S(1)}, f16[16,4096]{1,0:T(8,128)(2,1)S(1)}, u32[]{:S(2)}, u32[]{:S(2)}) collective-permute-start(f16[16,4096]{1,0:T(8,128)(2,1)S(1)} %get-tuple-element.29), channel_id=1, source_target_pairs={{0,1},{1,0},{2,3},{3,2},{4,5},{5,4},{6,7},{7,6},{8,9},{9,8},{10,11... | collective-permute-start | bytes 393224 | tf_op jit(solution)/shard_map/ppermute | solution.py:267
  47.2 7.4 %collective-permute-start.17 = (f16[16,4096]{1,0:T(8,128)(2,1)S(1)}, f16[16,4096]{1,0:T(8,128)(2,1)S(1)}, u32[]{:S(2)}, u32[]{:S(2)}) collective-permute-start(f16[16,4096]{1,0:T(8,128)(2,1)S(1)} %add_convert_fusion), channel_id=1, source_target_pairs={{0,4},{1,5},{2,6},{3,7},{4,0},{5,1},{6,2},{7,3},{8,12},{9,13},{10,... | collective-permute-start | bytes 393224 | tf_op jit(solution)/shard_map/ppermute | solution.py:267
  50.0 5.5 %collective-permute-start.12 = (f16[16,4096]{1,0:T(8,128)(2,1)S(1)}, f16[16,4096]{1,0:T(8,128)(2,1)S(1)}, u32[]{:S(2)}, u32[]{:S(2)}) collective-permute-start(f16[16,4096]{1,0:T(8,128)(2,1)S(1)} %add_convert_fusion.1), channel_id=1, source_target_pairs={{0,2},{1,3},{2,0},{3,1},{4,6},{5,7},{6,4},{7,5},{8,10},{9,11},{10,... | collective-permute-start | bytes 393224 | tf_op jit(solution)/shard_map/ppermute | solution.py:267
